TPU v7x, 32 devices: a whole 2x2x4 slice. The times are simulated.
32 devices in a mesh: parts: 2 (over y), group: 4 (over z), ingroup: 2 (over x), dp: 2 (over core).
Axes of the slice: x: 2, y: 2, z: 4, core: 2. Of those that a mesh axis runs over, the one named last changes fastest.
Arguments:
- tokens: bfloat16 [4096, 1024], P(('parts', 'group', 'ingroup', 'dp')), parts along dimension 0, may hold values from -6 to 6
- upstream: bfloat16 [4096, 1024], P(('parts', 'group', 'ingroup', 'dp')), parts along dimension 0, may hold values from -6 to 6
- expert_ids: int32 [4096, 8], P(('parts', 'group', 'ingroup', 'dp')), parts along dimension 0, may hold values from 0 to 31, as said below
- gate_fixed: int32 [4096, 8], P(('parts', 'group', 'ingroup', 'dp')), parts along dimension 0, may hold values from 1 to 65535
- slots: int32 [4096, 8], P(('parts', 'group', 'ingroup', 'dp')), parts along dimension 0, may hold values from 0 to 48, as said below
- w_gate: bfloat16 [32, 1024, 256], P(('group', 'ingroup')), may hold values from -0.1875 to 0.1875
- w_up: bfloat16 [32, 1024, 256], P(('group', 'ingroup')), may hold values from -0.1875 to 0.1875
- w_down: bfloat16 [32, 256, 1024], P(('group', 'ingroup')), may hold values from -0.375 to 0.375
Outputs:
- grad_tokens: bfloat16 [4096, 1024], P(('parts', 'group', 'ingroup', 'dp')), parts along dimension 0
- grad_gate: bfloat16 [64, 1024, 256], P(('parts', 'group', 'ingroup'), 'dp'), parts along dimension 0
- grad_up: bfloat16 [64, 1024, 256], P(('parts', 'group', 'ingroup'), 'dp'), parts along dimension 0
- grad_down: bfloat16 [64, 256, 1024], P(('parts', 'group', 'ingroup'), None, 'dp'), parts along dimension 0
There are 2 independent parts, one for each index of `parts`. A program takes and returns all parts, laid end to end along the dimension named above; an argument that names none is the same for every part. Nothing has to cross between parts.
Inputs may be any that keep to these rules, and one draw needn't show every extreme that they name: `expert_ids`: each token's 8 ids differ. The choices k with one value of k // 2 lie in one expert group (expert e belongs to group e // 8), and the 4 groups of a token differ. In every block of 128 rows at most 128 tokens have choices in one group, and some group has exactly 128 of them. In every block one expert, the same in all blocks, is chosen by 48 + 1 tokens or more. `slots`: within a block of 128 rows, the choices of one expert are numbered 0, 1, 2, ... in the order of tokens and then of k; numbers from 48 on are given as 48 (dropped). Some expert reaches 48 in every block.
All inputs are finite; a program needn't handle non-finite values.
Results may differ from a plain program's by a relative error of at most 0.0085.
Values may be sent and summed in bfloat16 or wider, within the bound.
No kernel may reach another device: no remote copies, remote signals or barrier semaphores. Data moves between devices by JAX's collectives and lax.ppermute only.
A program may use at most 128 MiB of HBM per device.

v0:
```python
import jax
import jax.numpy as jnp
from jax import lax
from jax.sharding import PartitionSpec as P

GROUPS_TOK = 4


def gated_parts(pre_gate):
    logistic = jax.nn.sigmoid(pre_gate)
    return (pre_gate * logistic, logistic * (1.0 + pre_gate * (1.0 - logistic)))


def per_device(tokens, upstream, expert_ids, gate_fixed, slots, w_gate, w_up, w_down):
    local_experts = w_gate.shape[0]
    n_group = lax.axis_size("group")
    n_ingroup = lax.axis_size("ingroup")
    owners = n_group * n_ingroup
    experts_all = local_experts * owners
    tok_rows = expert_ids.shape[0]
    top_count = expert_ids.shape[1]
    groups_tok = GROUPS_TOK
    per_group = top_count // groups_tok
    width = tokens.shape[1]
    capacity = max(2, 3 * tok_rows * top_count // (2 * experts_all))
    slot_rows = experts_all * capacity
    group_size = local_experts * n_ingroup
    group_ids = expert_ids[:, ::per_group] // group_size
    usable = slots < capacity
    target = jnp.where(usable, expert_ids * capacity + slots, slot_rows)
    member = ((expert_ids // group_size)[:, None, :] == group_ids[:, :, None]) & usable[:, None, :]
    shape_flat = (owners, local_experts, capacity, width)
    gates = gate_fixed.astype(jnp.float32) / 65536.0
    scaled = (
        (gates[:, :, None] * upstream.astype(jnp.float32)[:, None, :])
        .astype(jnp.bfloat16)
        .reshape(-1, width)
    )
    copies = jnp.broadcast_to(tokens[:, None, :], (tok_rows, top_count, width)).reshape(-1, width)
    flat_target = target.reshape(-1)
    empty = jnp.zeros((slot_rows + 1, width), jnp.bfloat16)
    x_send = empty.at[flat_target].set(copies)[:slot_rows]
    s_send = empty.at[flat_target].set(scaled)[:slot_rows]
    x_recv, s_recv = (
        lax.all_to_all(
            x_send.reshape(shape_flat),
            ("group", "ingroup"),
            split_axis=0,
            concat_axis=0,
            tiled=True,
        ),
        lax.all_to_all(
            s_send.reshape(shape_flat),
            ("group", "ingroup"),
            split_axis=0,
            concat_axis=0,
            tiled=True,
        ),
    )
    pre_gate = jnp.einsum("secd,edf->secf", x_recv, w_gate, preferred_element_type=jnp.float32)
    pre_up = jnp.einsum("secd,edf->secf", x_recv, w_up, preferred_element_type=jnp.float32)
    active, slope = gated_parts(pre_gate)
    hidden = (active * pre_up).astype(jnp.bfloat16)
    grad_hidden = jnp.einsum("secd,efd->secf", s_recv, w_down, preferred_element_type=jnp.float32)
    grad_gate_pre = (grad_hidden * pre_up * slope).astype(jnp.bfloat16)
    grad_up_pre = (grad_hidden * active).astype(jnp.bfloat16)
    rows_back = (
        jnp.einsum("secf,edf->secd", grad_gate_pre, w_gate, preferred_element_type=jnp.float32)
        + jnp.einsum("secf,edf->secd", grad_up_pre, w_up, preferred_element_type=jnp.float32)
    ).astype(jnp.bfloat16)
    part_gate = jnp.einsum(
        "secd,secf->edf", x_recv, grad_gate_pre, preferred_element_type=jnp.float32
    )
    part_up = jnp.einsum("secd,secf->edf", x_recv, grad_up_pre, preferred_element_type=jnp.float32)
    part_down = jnp.einsum("secf,secd->efd", hidden, s_recv, preferred_element_type=jnp.float32)
    summed_gate, summed_up, summed_down = (
        lax.psum_scatter(part_gate, "dp", scatter_dimension=1, tiled=True),
        lax.psum_scatter(part_up, "dp", scatter_dimension=1, tiled=True),
        lax.psum_scatter(part_down, "dp", scatter_dimension=2, tiled=True),
    )
    returned = lax.all_to_all(
        rows_back, ("group", "ingroup"), split_axis=0, concat_axis=0, tiled=True
    )
    padded = jnp.concatenate(
        [returned.reshape(slot_rows, width), jnp.zeros((1, width), jnp.bfloat16)], axis=0
    )
    picked = padded[target.reshape(-1)].reshape(tok_rows, top_count, width)
    group_part = jnp.einsum(
        "tjk,tkd->tjd", member.astype(jnp.bfloat16), picked, preferred_element_type=jnp.float32
    ).astype(jnp.bfloat16)
    grad_tokens = jnp.sum(group_part.astype(jnp.float32), axis=1).astype(jnp.bfloat16)
    return (
        grad_tokens,
        summed_gate.astype(jnp.bfloat16),
        summed_up.astype(jnp.bfloat16),
        summed_down.astype(jnp.bfloat16),
    )


def solution(mesh):
    in_specs = (
        P(("parts", "group", "ingroup", "dp"), None),
        P(("parts", "group", "ingroup", "dp"), None),
        P(("parts", "group", "ingroup", "dp"), None),
        P(("parts", "group", "ingroup", "dp"), None),
        P(("parts", "group", "ingroup", "dp"), None),
        P(("group", "ingroup"), None, None),
        P(("group", "ingroup"), None, None),
        P(("group", "ingroup"), None, None),
    )
    out_specs = (
        P(("parts", "group", "ingroup", "dp"), None),
        P(("parts", "group", "ingroup"), "dp", None),
        P(("parts", "group", "ingroup"), "dp", None),
        P(("parts", "group", "ingroup"), None, "dp"),
    )
    return jax.shard_map(
        per_device, mesh=mesh, in_specs=in_specs, out_specs=out_specs, check_vma=False
    )
```

profile of v0, /device:TPU:0, one launch (start us, length us, event | category | flops | bytes accessed | tf_op | source)
XLA Modules:
  0.0 307.3 jit_solution(15485739888821113986)
XLA Ops:
  7.2 0.0 copy-start
  7.2 0.9 add_select_fusion
  8.0 0.1 copy.26
  8.1 0.1 reshape.65
  8.3 7.7 %scatter_custom_fusion.1 = bf16[1537,1024]{1,0:T(8,128)(2,1)} fusion(s32[1024]{0:T(1024)S(1)} %bitcast.97, bf16[]{:T(256)} %constant.37.clone.1, bf16[128,1024]{1,0:T(8,128)(2,1)} %param.8), kind=kCustom, calls=%fused_computation.27 | custom fusion | bytes 3409922 | tf_op jit(solution)/shard_map/scatter | solution.py:42
  16.0 3.9 %slice.15 = bf16[1536,1024]{1,0:T(8,128)(2,1)} slice(bf16[1537,1024]{1,0:T(8,128)(2,1)} %scatter_custom_fusion.1), slice={[0:1536], [0:1024]} | slice | bytes 6291456 | tf_op jit(solution)/shard_map/slice | solution.py:42
  19.9 0.0 copy-start.6
  19.9 0.0 copy-start.3
  19.9 7.4 %all-to-all-start.1 = ((bf16[8,4,48,1024]{3,2,1,0:T(8,128)(2,1)}), bf16[8,4,48,1024]{3,2,1,0:T(8,128)(2,1)}, u32[]{:S(2)}, u32[]{:S(2)}) async-start(bf16[8,4,48,1024]{3,2,1,0:T(8,128)(2,1)} %bitcast.95), calls=%async_computation.1 | async-start | bytes 6291456 | tf_op jit(solution)/shard_map/all_to_all | solution.py:45
  27.3 0.0 copy-done.6
  27.3 0.1 copy.27
  27.4 0.1 mul.43
  27.5 0.0 copy-done.3
  27.5 7.8 %scatter_custom_fusion = bf16[1537,1024]{1,0:T(8,128)(2,1)} fusion(s32[1024]{0:T(1024)S(1)} %bitcast.98, f32[128,1024]{1,0:T(8,128)S(1)} %convert_element_type.41, f32[1024]{0:T(1024)S(1)} %mul.43, bf16[]{:T(256)} %constant.37.clone.1), kind=kCustom, calls=%fused_computation.18 | custom fusion | flops 2097152 | bytes 3676162 | tf_op jit(solution)/shard_map/scatter | solution.py:43
  35.3 3.9 %slice.14 = bf16[1536,1024]{1,0:T(8,128)(2,1)} slice(bf16[1537,1024]{1,0:T(8,128)(2,1)} %scatter_custom_fusion), slice={[0:1536], [0:1024]} | slice | bytes 6291456 | tf_op jit(solution)/shard_map/slice | solution.py:43
  39.2 58.9 %all-to-all-done.1 = bf16[8,4,48,1024]{3,2,1,0:T(8,128)(2,1)} async-done(((bf16[8,4,48,1024]{3,2,1,0:T(8,128)(2,1)}), bf16[8,4,48,1024]{3,2,1,0:T(8,128)(2,1)}, u32[]{:S(2)}, u32[]{:S(2)}) %all-to-all-start.1) | async-done | bytes 3145760 | tf_op jit(solution)/shard_map/all_to_all | solution.py:45
  98.1 4.4 %all-to-all-start = ((bf16[8,4,48,1024]{3,2,1,0:T(8,128)(2,1)}), bf16[8,4,48,1024]{3,2,1,0:T(8,128)(2,1)}, u32[]{:S(2)}, u32[]{:S(2)}) async-start(bf16[8,4,48,1024]{3,2,1,0:T(8,128)(2,1)} %bitcast.96), calls=%async_computation | async-start | bytes 6291456 | tf_op jit(solution)/shard_map/all_to_all | solution.py:52
  102.5 0.2 reduce-scatter.8.cloned.1.call-start
  102.7 0.0 copy-done
  102.8 0.0 copy-start.1
  102.8 4.2 %fusion.2 = f32[4,8,48,256]{3,2,1,0:T(8,128)} fusion(bf16[8,4,48,1024]{3,2,1,0:T(8,128)(2,1)} %all-to-all-done.1, bf16[4,1024,256]{2,1,0:T(8,128)(2,1)S(1)} %copy-done), kind=kOutput, calls=%fused_computation.7 | convolution fusion | flops 805306368 | bytes 6815744 | tf_op jit(solution)/shard_map/secd,edf->secf/dot_general | solution.py:60
  106.9 0.0 copy-done.1
  107.0 4.0 %fusion.4 = f32[4,8,48,256]{3,2,1,0:T(8,128)} fusion(bf16[8,4,48,1024]{3,2,1,0:T(8,128)(2,1)} %all-to-all-done.1, bf16[4,1024,256]{2,1,0:T(8,128)(2,1)S(1)} %copy-done.1), kind=kOutput, calls=%fused_computation.9 | convolution fusion | flops 805306368 | bytes 6815744 | tf_op jit(solution)/shard_map/secd,edf->secf/dot_general | solution.py:61
  111.0 61.7 %all-to-all-done = bf16[8,4,48,1024]{3,2,1,0:T(8,128)(2,1)} async-done(((bf16[8,4,48,1024]{3,2,1,0:T(8,128)(2,1)}), bf16[8,4,48,1024]{3,2,1,0:T(8,128)(2,1)}, u32[]{:S(2)}, u32[]{:S(2)}) %all-to-all-start) | async-done | bytes 3145760 | tf_op jit(solution)/shard_map/all_to_all | solution.py:52
  172.7 6.1 %fusion.10 = f32[4,256,1024]{2,1,0:T(8,128)} fusion(bf16[8,4,48,1024]{3,2,1,0:T(8,128)(2,1)} %all-to-all-done, f32[4,8,48,256]{3,2,1,0:T(8,128)} %fusion.4, f32[4,8,48,256]{3,2,1,0:T(8,128)} %fusion.2), kind=kOutput, calls=%fused_computation.15 | convolution fusion | flops 807665664 | bytes 10485760 | tf_op jit(solution)/shard_map/secf,secd->efd/dot_general | solution.py:75
  178.8 0.0 reduce-scatter.8.cloned.1.call-update
  178.8 0.0 reduce-scatter.6.cloned.1.call-start
  178.9 5.8 %fusion.37 = (bf16[8,4,48,256]{3,2,0,1:T(8,128)(2,1)S(1)}, bf16[8,4,48,256]{3,2,0,1:T(8,128)(2,1)}) fusion(f32[4,8,48,256]{3,2,1,0:T(8,128)} %fusion.2, f32[4,8,48,256]{3,2,1,0:T(8,128)} %fusion.4, bf16[4,256,1024]{2,1,0:T(8,128)(2,1)} %param.15, bf16[8,4,48,1024]{3,2,1,0:T(8,128)(2,1)} %all-to-all-done), kind=kOutput, calls=%fused_computation.47 | convolution fusion | flops 810418176 | bytes 9961472 | tf_op jit(solution)/shard_map/secd,efd->secf/dot_general | solution.py:64
  184.7 5.4 %convolution_bitcast_fusion = f32[4,1024,256]{2,1,0:T(8,128)} fusion(bf16[8,4,48,1024]{3,2,1,0:T(8,128)(2,1)} %all-to-all-done.1, bf16[8,4,48,256]{3,2,0,1:T(8,128)(2,1)S(1)} %get-tuple-element.4), kind=kOutput, calls=%fused_computation.16 | convolution fusion | flops 805306368 | bytes 8126464 | tf_op jit(solution)/shard_map/secd,secf->edf/dot_general | solution.py:74
  190.1 0.0 reduce-scatter.6.cloned.1.call-update
  190.1 0.0 reduce-scatter.4.cloned.1.call-start
  190.2 5.5 %convolution_bitcast_fusion.1 = f32[4,1024,256]{2,1,0:T(8,128)} fusion(bf16[8,4,48,1024]{3,2,1,0:T(8,128)(2,1)} %all-to-all-done.1, bf16[8,4,48,256]{3,2,0,1:T(8,128)(2,1)} %get-tuple-element.5), kind=kOutput, calls=%fused_computation.17 | convolution fusion | flops 805306368 | bytes 8126464 | tf_op jit(solution)/shard_map/secd,secf->edf/dot_general | solution.py:71
  195.7 0.0 reduce-scatter.4.cloned.1.call-update
  195.7 0.0 copy-start.2
  195.8 2.3 fusion.15
  198.1 0.0 copy-done.2
  198.1 1.1 fusion.1
  199.2 1.9 copy.31
  201.1 0.0 copy-start.5
  201.1 0.0 copy-start.4
  201.1 5.0 %all-to-all-start.2 = ((bf16[8,4,48,1024]{3,2,1,0:T(8,128)(2,1)}), bf16[8,4,48,1024]{3,2,1,0:T(8,128)(2,1)}, u32[]{:S(2)}, u32[]{:S(2)}) async-start(bf16[8,4,48,1024]{3,2,1,0:T(8,128)(2,1)} %copy.31), calls=%async_computation.2 | async-start | bytes 6291456 | tf_op jit(solution)/shard_map/all_to_all | solution.py:81
  206.1 0.0 copy-done.5
  206.1 0.0 copy-done.4
  206.1 0.1 copy.25
  206.2 0.1 copy.23
  206.3 0.1 copy.24
  206.5 70.2 %all-to-all-done.2 = bf16[8,4,48,1024]{3,2,1,0:T(8,128)(2,1)} async-done(((bf16[8,4,48,1024]{3,2,1,0:T(8,128)(2,1)}), bf16[8,4,48,1024]{3,2,1,0:T(8,128)(2,1)}, u32[]{:S(2)}, u32[]{:S(2)}) %all-to-all-start.2) | async-done | bytes 3145760 | tf_op jit(solution)/shard_map/all_to_all | solution.py:81
  276.7 3.8 %concatenate.3 = bf16[1537,1024]{1,0:T(8,128)(2,1)} pad(bf16[1536,1024]{1,0:T(8,128)(2,1)} %bitcast.16, bf16[]{:T(256)} %constant.37.clone.1), padding=0_1x0_0 | pad | bytes 6293506 | tf_op jit(solution)/shard_map/concatenate | solution.py:84
  280.5 8.3 %gather_fusion = bf16[1024,1024]{1,0:T(8,128)(2,1)} fusion(bf16[1537,1024]{1,0:T(8,128)(2,1)} %concatenate.3, s32[1024]{0:T(1024)S(1)} %broadcast_clamp_fusion), kind=kCustom, calls=%fused_computation | custom fusion | bytes 4198400 | tf_op jit(solution)/shard_map/gather | solution.py:87
  288.9 3.9 %fusion.41 = bf16[128,1024]{1,0:T(8,128)(2,1)} fusion(bf16[1024,1024]{1,0:T(8,128)(2,1)} %gather_fusion, s32[128,4]{1,0:T(8,128)S(1)} %copy.24, s32[128,8]{1,0:T(8,128)S(1)} %copy.23, pred[128,8]{1,0:T(8,128)(4,1)S(1)} %copy.25), kind=kOutput, calls=%fused_computation.49 | convolution fusion | flops 9314304 | bytes 2366464 | tf_op jit(solution)/shard_map/tjk,tkd->tjd/dot_general | solution.py:88
  292.7 0.0 reduce-scatter.8.cloned.1.call-done
  292.7 2.7 convert_element_type.51
  295.4 0.0 reduce-scatter.6.cloned.1.call-done
  295.4 2.7 convert_element_type.49
  298.1 0.0 reduce-scatter.4.cloned.1.call-done
  298.1 2.7 convert_element_type.48
  (7 shorter events, 0.1 us)
Async XLA Ops:
  7.2 95.6 %copy-start = (bf16[4,1024,256]{2,1,0:T(8,128)(2,1)S(1)}, bf16[4,1024,256]{2,1,0:T(8,128)(2,1)}, u32[]{:S(2)}) copy-start(bf16[4,1024,256]{2,1,0:T(8,128)(2,1)} %param.13) | copy-start | bytes 6291460
  19.9 7.4 %copy-start.6 = (s32[128,8]{0,1:T(8,128)S(1)}, s32[128,8]{0,1:T(8,128)}, u32[]{:S(2)}) copy-start(s32[128,8]{0,1:T(8,128)} %param.11) | copy-start | bytes 12292
  19.9 7.6 %copy-start.3 = (bf16[128,1024]{1,0:T(8,128)(2,1)S(1)}, bf16[128,1024]{1,0:T(8,128)(2,1)}, u32[]{:S(2)}) copy-start(bf16[128,1024]{1,0:T(8,128)(2,1)} %param.9) | copy-start | bytes 786436
  19.9 78.2 %all-to-all-start.1 = ((bf16[8,4,48,1024]{3,2,1,0:T(8,128)(2,1)}), bf16[8,4,48,1024]{3,2,1,0:T(8,128)(2,1)}, u32[]{:S(2)}, u32[]{:S(2)}) async-start(bf16[8,4,48,1024]{3,2,1,0:T(8,128)(2,1)} %bitcast.95), calls=%async_computation.1 | async-start | bytes 6291456 | tf_op jit(solution)/shard_map/all_to_all | solution.py:45
  98.1 74.6 %all-to-all-start = ((bf16[8,4,48,1024]{3,2,1,0:T(8,128)(2,1)}), bf16[8,4,48,1024]{3,2,1,0:T(8,128)(2,1)}, u32[]{:S(2)}, u32[]{:S(2)}) async-start(bf16[8,4,48,1024]{3,2,1,0:T(8,128)(2,1)} %bitcast.96), calls=%async_computation | async-start | bytes 6291456 | tf_op jit(solution)/shard_map/all_to_all | solution.py:52
  102.5 190.2 %reduce-scatter.8.cloned.1.call-start = ((), (), s32[]{:S(2)}) async-start(), calls=%async_computation.8 | async-start | bytes 6291456 | tf_op jit(solution)/shard_map/reduce_scatter | solution.py:79
  102.8 4.2 %copy-start.1 = (bf16[4,1024,256]{2,1,0:T(8,128)(2,1)S(1)}, bf16[4,1024,256]{2,1,0:T(8,128)(2,1)}, u32[]{:S(2)}) copy-start(bf16[4,1024,256]{2,1,0:T(8,128)(2,1)} %param.14) | copy-start | bytes 6291460
  178.8 116.6 %reduce-scatter.6.cloned.1.call-start = ((), (), s32[]{:S(2)}) async-start(), calls=%async_computation.7 | async-start | bytes 6291456 | tf_op jit(solution)/shard_map/reduce_scatter | solution.py:78
  190.1 107.9 %reduce-scatter.4.cloned.1.call-start = ((), (), s32[]{:S(2)}) async-start(), calls=%async_computation.6 | async-start | bytes 6291456 | tf_op jit(solution)/shard_map/reduce_scatter | solution.py:77
  195.7 2.3 copy-start.2
  201.1 5.0 %copy-start.5 = (s32[128,8]{0,1:T(8,128)S(1)}, s32[128,8]{0,1:T(8,128)}, u32[]{:S(2)}) copy-start(s32[128,8]{0,1:T(8,128)} %param.10) | copy-start | bytes 12292
  201.1 5.0 %copy-start.4 = (s32[128,8]{0,1:T(8,128)S(1)}, s32[128,8]{0,1:T(8,128)}, u32[]{:S(2)}) copy-start(s32[128,8]{0,1:T(8,128)} %param.12) | copy-start | bytes 12292
  201.1 75.6 %all-to-all-start.2 = ((bf16[8,4,48,1024]{3,2,1,0:T(8,128)(2,1)}), bf16[8,4,48,1024]{3,2,1,0:T(8,128)(2,1)}, u32[]{:S(2)}, u32[]{:S(2)}) async-start(bf16[8,4,48,1024]{3,2,1,0:T(8,128)(2,1)} %copy.31), calls=%async_computation.2 | async-start | bytes 6291456 | tf_op jit(solution)/shard_map/all_to_all | solution.py:81
Sparse Core Ops, SparseCore 0:
  179.0 11.1 reduce-scatter.7
  192.5 13.3 reduce-scatter.5
  208.2 13.3 reduce-scatter.3
where the time goes:
time: 308 us; the launch traced here: 307 us
  waiting for transfers between devices  191 us (62%)
  matrix products  38.3 us (12%)
  local copies, waits for them, and re-layouts  30.4 us (10%)
  starting transfers between devices  17.1 us (6%)
  other arithmetic  16.7 us (5%)
  between operations  13.9 us (5%)
    all_to_all x1, waiting for transfers between devices, per_device(): lax.all_to_all(rows_back, ('group', 'ingroup'), split_axis=0, concat_axis...  70.2 us
    all_to_all x1, waiting for transfers between devices, per_device(): lax.all_to_all(s_send.reshape(shape_flat), ('group', 'ingroup'), split_ax...  61.7 us
    all_to_all x1, waiting for transfers between devices, per_device(): lax.all_to_all(x_send.reshape(shape_flat), ('group', 'ingroup'), split_ax...  58.9 us
    gather x1, local copies, waits for them, and re-layouts, per_device(): picked = padded[target.reshape(-1)].reshape(tok_rows, top_count, width)  8.32 us
    scatter x1, other arithmetic, per_device(): s_send = empty.at[flat_target].set(scaled)[:slot_rows]  7.77 us
    scatter x1, local copies, waits for them, and re-layouts, per_device(): x_send = empty.at[flat_target].set(copies)[:slot_rows]  7.73 us
    all_to_all x1, starting transfers between devices, per_device(): lax.all_to_all(x_send.reshape(shape_flat), ('group', 'ingroup'), split_ax...  7.38 us
  transfers between devices with their start and end apart: 6, of which 3 were waited for; matrix products, arithmetic and copies ran while one was open for 21% of the time, Pallas kernels for 0%

commit v1 on v0

v1 whole, which is shorter than its diff:
```python
import functools

import jax
import jax.numpy as jnp
from jax import lax
from jax.experimental import pallas as pl
from jax.experimental.pallas import tpu as pltpu
from jax.sharding import PartitionSpec as P

GROUPS_TOK = 4
ROUTE_ROWS = 16
VMEM_LIMIT = 48 * 1024 * 1024


def dot(a, b, contract):
    return lax.dot_general(a, b, ((contract[:1], contract[1:]), ((), ())), preferred_element_type=jnp.float32)


def gated_parts(pre_gate):
    logistic = jax.nn.sigmoid(pre_gate)
    return (pre_gate * logistic, logistic * (1.0 + pre_gate * (1.0 - logistic)))


def partner(z, k, size):
    return z ^ k if size & (size - 1) == 0 else (k - z) % size


def route_keys(route, first_expert, local_experts, capacity, rows, offset, tok_rows, per_group):
    expert = route[0:1, :].astype(jnp.int32) - first_expert
    slot = route[1:2, :].astype(jnp.int32)
    gate = (route[2:3, :] * 256.0 + route[3:4, :]) / 65536.0
    valid = (expert >= 0) & (expert < local_experts) & (slot < capacity)
    key = jnp.where(valid, expert * rows + offset + slot, -1)
    gate = jnp.where(valid, gate, 0.0)
    width = tok_rows * per_group
    key_out, gate_out = key[:, :width], gate[:, :width]
    for j in range(1, route.shape[1] // width):
        key_out = jnp.maximum(key_out, key[:, j * width : (j + 1) * width])
        gate_out = jnp.maximum(gate_out, gate[:, j * width : (j + 1) * width])
    return key_out, gate_out


def chunk_kernel(n_blocks, tok_rows, capacity, rows, per_group, first_ref, *refs):
    payloads = refs[:n_blocks]
    w_gate, w_up, w_down = refs[n_blocks : n_blocks + 3]
    parts = refs[n_blocks + 3 : 2 * n_blocks + 3]
    x_out, s_out, h_out = refs[2 * n_blocks + 3 : 2 * n_blocks + 6]
    x_all, u_all, key_all, gate_all, hot_all, back_all = refs[2 * n_blocks + 6 :]
    e = pl.program_id(0)
    local_experts = pl.num_programs(0)
    n_tok = n_blocks * tok_rows
    ff = w_gate.shape[2]

    @pl.when(e == 0)
    def _():
        for b in range(n_blocks):
            rows_b = slice(b * tok_rows, (b + 1) * tok_rows)
            x_all[rows_b, :] = payloads[b][:tok_rows, :]
            u_all[rows_b, :] = payloads[b][tok_rows : 2 * tok_rows, :]
            route = payloads[b][2 * tok_rows : 2 * tok_rows + ROUTE_ROWS, :].astype(jnp.float32)
            key, gate = route_keys(
                route, first_ref[0], local_experts, capacity, rows, b * capacity, tok_rows, per_group
            )
            for i in range(per_group):
                cols = slice(i * tok_rows, (i + 1) * tok_rows)
                key_all[i : i + 1, rows_b] = key[:, cols]
                gate_all[i : i + 1, rows_b] = gate[:, cols]

    place = lax.broadcasted_iota(jnp.int32, (rows, n_tok), 0) + e * rows
    hot = jnp.zeros((rows, n_tok), jnp.float32)
    gate_hot = jnp.zeros((rows, n_tok), jnp.float32)
    for i in range(per_group):
        match = place == key_all[i : i + 1, :]
        hot = jnp.where(match, 1.0, hot)
        gate_hot = jnp.where(match, gate_all[i : i + 1, :], gate_hot)
    hot = hot.astype(jnp.bfloat16)
    row_gate = jnp.sum(gate_hot, axis=1, keepdims=True)
    here = pl.ds(pl.multiple_of(e * rows, rows), rows)
    hot_all[here, :] = hot
    x_rows = dot(hot, x_all[...], (1, 0)).astype(jnp.bfloat16)
    s_rows = (dot(hot, u_all[...], (1, 0)) * row_gate).astype(jnp.bfloat16)
    x_out[0] = x_rows
    s_out[0] = s_rows
    pre_gate = dot(x_rows, w_gate[0], (1, 0))
    pre_up = dot(x_rows, w_up[0], (1, 0))
    grad_hidden = dot(s_rows, w_down[0], (1, 1))
    active, slope = gated_parts(pre_gate)
    grad_gate_pre = (grad_hidden * pre_up * slope).astype(jnp.bfloat16)
    grad_up_pre = (grad_hidden * active).astype(jnp.bfloat16)
    h_out[0, :, :ff] = grad_gate_pre
    h_out[0, :, ff : 2 * ff] = grad_up_pre
    h_out[0, :, 2 * ff :] = (active * pre_up).astype(jnp.bfloat16)
    back = dot(grad_gate_pre, w_gate[0], (1, 1)) + dot(grad_up_pre, w_up[0], (1, 1))
    back_all[here, :] = back.astype(jnp.bfloat16)

    @pl.when(e == local_experts - 1)
    def _():
        summed = dot(hot_all[...], back_all[...], (0, 0)).astype(jnp.bfloat16)
        for b in range(n_blocks):
            parts[b][...] = summed[b * tok_rows : (b + 1) * tok_rows, :]


def chunk_call(payloads, first_expert, w_gate, w_up, w_down, tok_rows, capacity, rows, per_group):
    n_blocks = len(payloads)
    n_tok = n_blocks * tok_rows
    experts, width, ff = w_gate.shape
    whole = lambda shape: pl.BlockSpec(shape, lambda e, first: (0, 0))
    per_expert = lambda shape: pl.BlockSpec((1,) + shape, lambda e, first: (e, 0, 0))
    flops = 2 * experts * rows * width * (5 * ff + 3 * n_tok)
    return pl.pallas_call(
        functools.partial(chunk_kernel, n_blocks, tok_rows, capacity, rows, per_group),
        grid_spec=pltpu.PrefetchScalarGridSpec(
            num_scalar_prefetch=1,
            grid=(experts,),
            in_specs=[whole(payloads[0].shape)] * n_blocks
            + [per_expert((width, ff)), per_expert((width, ff)), per_expert((ff, width))],
            out_specs=[whole((tok_rows, width))] * n_blocks
            + [per_expert((rows, width)), per_expert((rows, width)), per_expert((rows, 3 * ff))],
            scratch_shapes=[
                pltpu.VMEM((n_tok, width), jnp.bfloat16),
                pltpu.VMEM((n_tok, width), jnp.bfloat16),
                pltpu.VMEM((per_group, n_tok), jnp.int32),
                pltpu.VMEM((per_group, n_tok), jnp.float32),
                pltpu.VMEM((experts * rows, n_tok), jnp.bfloat16),
                pltpu.VMEM((experts * rows, width), jnp.bfloat16),
            ],
        ),
        out_shape=[jax.ShapeDtypeStruct((tok_rows, width), jnp.bfloat16)] * n_blocks
        + [
            jax.ShapeDtypeStruct((experts, rows, width), jnp.bfloat16),
            jax.ShapeDtypeStruct((experts, rows, width), jnp.bfloat16),
            jax.ShapeDtypeStruct((experts, rows, 3 * ff), jnp.bfloat16),
        ],
        compiler_params=pltpu.CompilerParams(vmem_limit_bytes=VMEM_LIMIT),
        cost_estimate=pl.CostEstimate(
            flops=flops, bytes_accessed=6 * experts * width * ff + 8 * n_tok * width, transcendentals=0
        ),
        name="chunk",
    )(first_expert, *payloads, w_gate, w_up, w_down)


def halves_of(n, ff, refs):
    cat = lambda part: jnp.concatenate([ref[0] for ref in part], axis=0)
    x_rows, s_rows, hid = cat(refs[:n]), cat(refs[n : 2 * n]), cat(refs[2 * n : 3 * n])
    return dot(x_rows, hid[:, : 2 * ff], (0, 0)), dot(hid[:, 2 * ff :], s_rows, (0, 0))


def send_kernel(n, ff, half_ref, *refs):
    gate_up, down = halves_of(n, ff, refs)
    out = refs[3 * n]
    depth = gate_up.shape[0]
    out[0, :depth, :] = gate_up.astype(jnp.bfloat16)
    out[0, depth:, :] = down.astype(jnp.bfloat16)


def keep_kernel(n, ff, half_ref, *refs):
    gate_up, down = halves_of(n, ff, refs)
    got = refs[3 * n]
    out_gate, out_up, out_down = refs[3 * n + 1 :]
    depth = gate_up.shape[0]
    gate_up = gate_up + got[0, :depth, :].astype(jnp.float32)
    out_gate[0] = gate_up[:, :ff].astype(jnp.bfloat16)
    out_up[0] = gate_up[:, ff:].astype(jnp.bfloat16)
    out_down[0] = (down + got[0, depth:, :].astype(jnp.float32)).astype(jnp.bfloat16)


def weight_call(half, x_rows, s_rows, hids, got=None):
    n = len(x_rows)
    experts, rows, width = x_rows[0].shape
    ff = hids[0].shape[2] // 3
    depth = width // 2
    piece = lambda shape: pl.BlockSpec((1,) + shape, lambda e, half: (e, 0, 0))
    split = pl.BlockSpec((1, rows, depth), lambda e, half: (e, 0, half[0]))
    in_specs = [split] * (2 * n) + [piece((rows, 3 * ff))] * n
    operands = [*x_rows, *s_rows, *hids]
    packed = (depth + ff, depth)
    if got is None:
        kernel = send_kernel
        out_specs = piece(packed)
        out_shape = jax.ShapeDtypeStruct((experts,) + packed, jnp.bfloat16)
    else:
        kernel = keep_kernel
        in_specs = in_specs + [piece(packed)]
        operands = operands + [got]
        shapes = [(depth, ff), (depth, ff), (ff, depth)]
        out_specs = [piece(s) for s in shapes]
        out_shape = [jax.ShapeDtypeStruct((experts,) + s, jnp.bfloat16) for s in shapes]
    return pl.pallas_call(
        functools.partial(kernel, n, ff),
        grid_spec=pltpu.PrefetchScalarGridSpec(
            num_scalar_prefetch=1, grid=(experts,), in_specs=in_specs, out_specs=out_specs
        ),
        out_shape=out_shape,
        compiler_params=pltpu.CompilerParams(vmem_limit_bytes=VMEM_LIMIT),
        cost_estimate=pl.CostEstimate(
            flops=2 * experts * n * rows * 3 * ff * depth,
            bytes_accessed=2 * experts * (n * rows * (width + 3 * ff) + 3 * ff * depth),
            transcendentals=0,
        ),
        name="weight_grads",
    )(half, *operands)


def per_device(tokens, upstream, expert_ids, gate_fixed, slots, w_gate, w_up, w_down):
    local_experts = w_gate.shape[0]
    n_group = lax.axis_size("group")
    n_ingroup = lax.axis_size("ingroup")
    experts_all = local_experts * n_group * n_ingroup
    tok_rows, top_count = expert_ids.shape
    width = tokens.shape[1]
    per_group = top_count // GROUPS_TOK
    capacity = max(2, 3 * tok_rows * top_count // (2 * experts_all))
    rows = -(-n_ingroup * capacity // 16) * 16
    z, x, core = (lax.axis_index(a) for a in ("group", "ingroup", "dp"))
    first_expert = ((z * n_ingroup + x) * local_experts).astype(jnp.int32).reshape(1)

    route = jnp.stack([expert_ids.T, slots.T, (gate_fixed // 256).T, (gate_fixed % 256).T])
    route = route.reshape(-1, width).astype(jnp.bfloat16)
    route = jnp.pad(route, ((0, ROUTE_ROWS - route.shape[0]), (0, 0)))
    own = jnp.concatenate([tokens, upstream, route], axis=0)

    ups, downs = {0: own}, {0: own}
    for s in range(1, n_group):
        ups[s] = lax.ppermute(ups[s - 1], "group", [(i, i + 1) for i in range(s - 1, n_group - 1)])
        downs[s] = lax.ppermute(downs[s - 1], "group", [(i, i - 1) for i in range(1, n_group - s + 1)])

    chunks = []
    for k in range(n_group):
        if k == 0:
            column = own
        else:
            offsets = [i - partner(i, k, n_group) for i in range(n_group)]
            kinds = sorted(set(offsets))
            column = None
            for off in kinds:
                case = ups[off] if off >= 0 else downs[-off]
                picks = functools.reduce(jnp.logical_or, [z == i for i in range(n_group) if offsets[i] == off])
                column = case if column is None else jnp.where(picks, case, column)
        blocks = [column] + [
            lax.ppermute(column, "ingroup", [(i, (i + s) % n_ingroup) for i in range(n_ingroup)])
            for s in range(1, n_ingroup)
        ]
        chunks.append(
            chunk_call(blocks, first_expert, w_gate, w_up, w_down, tok_rows, capacity, rows, per_group)
        )

    x_rows, s_rows, hids = ([c[n_ingroup + i] for c in chunks] for i in range(3))
    half = core.astype(jnp.int32).reshape(1)
    to_send = weight_call(1 - half, x_rows, s_rows, hids)
    got = lax.ppermute(to_send, "dp", [(0, 1), (1, 0)])

    total = jnp.zeros((tok_rows, width), jnp.float32)
    for k in range(n_group):
        parts = chunks[k][:n_ingroup]
        group_part = parts[0].astype(jnp.float32)
        for s in range(1, n_ingroup):
            back = lax.ppermute(parts[s], "ingroup", [(i, (i - s) % n_ingroup) for i in range(n_ingroup)])
            group_part = group_part + back.astype(jnp.float32)
        group_part = group_part.astype(jnp.bfloat16)
        if k > 0:
            group_part = lax.ppermute(
                group_part, "group", [(i, partner(i, k, n_group)) for i in range(n_group)]
            )
        total = total + group_part.astype(jnp.float32)
    grad_tokens = total.astype(jnp.bfloat16)

    grad_gate, grad_up, grad_down = weight_call(half, x_rows, s_rows, hids, got)
    return grad_tokens, grad_gate, grad_up, grad_down


def solution(mesh):
    rows_spec = P(("parts", "group", "ingroup", "dp"), None)
    weight_spec = P(("group", "ingroup"), None, None)
    out_specs = (
        rows_spec,
        P(("parts", "group", "ingroup"), "dp", None),
        P(("parts", "group", "ingroup"), "dp", None),
        P(("parts", "group", "ingroup"), None, "dp"),
    )
    return jax.shard_map(
        per_device,
        mesh=mesh,
        in_specs=(rows_spec,) * 5 + (weight_spec,) * 3,
        out_specs=out_specs,
        check_vma=False,
    )
```

time: 308 us -> 148 us (0.48)
  waiting for transfers between devices: 191 us -> 61.9 us
  Pallas kernels: 0 us -> 39.3 us
  matrix products: 38.3 us -> 0 us
  local copies, waits for them, and re-layouts: 30.4 us -> 5.23 us
  starting transfers between devices: 17.1 us -> 31.9 us
  between operations: 13.9 us -> 0.83 us
  other arithmetic: 16.7 us -> 7.91 us
    all_to_all x3 -> x0, waiting for transfers between devices: 191 us -> none  [the longest x1 70.2 us: per_device(): lax.all_to_all(rows_back, ('group', 'ingroup'), split_axis=0, concat_axis...]
    ppermute x0 -> x18, waiting for transfers between devices: none -> 61.9 us  [the longest x3 32.7 us: per_device(): lax.ppermute(downs[s - 1], 'group', [(i, i - 1) for i in range(1, n_group...]
    pallas_call x0 -> x6, Pallas kernels: none -> 39.3 us  [the longest x4 28.5 us: chunk_call(): pl.pallas_call(functools.partial(chunk_kernel, n_blocks, tok_rows, capaci...]
    dot_general x9 -> x0, matrix products: 38.3 us -> none  [the longest x1 6.1 us: per_device(): jnp.einsum('secf,secd->efd', hidden, s_recv, preferred_element_type=jnp.f...]
    ppermute x0 -> x18, starting transfers between devices: none -> 31.9 us  [the longest x3 11.3 us: per_device(): lax.ppermute(group_part, 'group', [(i, partner(i, k, n_group)) for i in r...]
    all_to_all x3 -> x0, starting transfers between devices: 16.8 us -> none  [the longest x1 7.38 us: per_device(): lax.all_to_all(x_send.reshape(shape_flat), ('group', 'ingroup'), split_ax...]
    gather x1 -> x0, local copies, waits for them, and re-layouts: 8.32 us -> none  [per_device(): picked = padded[target.reshape(-1)].reshape(tok_rows, top_count, width)]
    slice x3 -> x0, local copies, waits for them, and re-layouts: 7.81 us -> none  [the longest x1 3.91 us: per_device(): s_send = empty.at[flat_target].set(scaled)[:slot_rows]]
  transfers between devices with their start and end apart: 6 -> 18, of which waited for: 3 -> 11; matrix products, arithmetic and copies ran while one was open for 21% -> 3% of each run, Pallas kernels for 0% -> 14%
where the time goes in v1:
time: 148 us; the launch traced here: 147 us
  waiting for transfers between devices  61.9 us (42%)
  Pallas kernels  39.3 us (27%)
  starting transfers between devices  31.9 us (22%)
  other arithmetic  7.91 us (5%)
  local copies, waits for them, and re-layouts  5.23 us (4%)
    ppermute x3, waiting for transfers between devices, per_device(): lax.ppermute(downs[s - 1], 'group', [(i, i - 1) for i in range(1, n_group...  32.7 us
    pallas_call x4, Pallas kernels, chunk_call(): pl.pallas_call(functools.partial(chunk_kernel, n_blocks, tok_rows, capaci...  28.5 us
    ppermute x4, waiting for transfers between devices, per_device(): lax.ppermute(parts[s], 'ingroup', [(i, (i - s) % n_ingroup) for i in rang...  13.3 us
    ppermute x3, starting transfers between devices, per_device(): lax.ppermute(group_part, 'group', [(i, partner(i, k, n_group)) for i in r...  11.3 us
    pallas_call x2, Pallas kernels, weight_call(): pl.pallas_call(functools.partial(kernel, n, ff), grid_spec=pltpu.Prefetch...  10.8 us
    ppermute x3, starting transfers between devices, per_device(): lax.ppermute(ups[s - 1], 'group', [(i, i + 1) for i in range(s - 1, n_gro...  8.55 us
    ppermute x4, waiting for transfers between devices, per_device(): lax.ppermute(column, 'ingroup', [(i, (i + s) % n_ingroup) for i in range(...  8.01 us
    ppermute x3, waiting for transfers between devices, per_device(): lax.ppermute(group_part, 'group', [(i, partner(i, k, n_group)) for i in r...  7.85 us
  transfers between devices with their start and end apart: 18, of which 11 were waited for; matrix products, arithmetic and copies ran while one was open for 3% of the time, Pallas kernels for 14%

profile of v1, /device:TPU:0, one launch (start us, length us, event | category | flops | bytes accessed | tf_op | source)
XLA Modules:
  0.0 147.0 jit_solution(8076927181296724938)
XLA Ops:
  0.6 0.7 convert_bitcast_fusion.1
  1.3 0.7 convert_bitcast_fusion
  2.0 0.7 fusion.12
  2.8 1.1 pad_maximum_fusion.refs_0_
  3.8 1.3 collective-permute-start.3
  5.1 5.6 %collective-permute-start.2 = (bf16[272,1024]{1,0:T(8,128)(2,1)S(1)}, bf16[272,1024]{1,0:T(8,128)(2,1)S(1)}, u32[]{:S(2)}, u32[]{:S(2)}) collective-permute-start(bf16[272,1024]{1,0:T(8,128)(2,1)S(1)} %pad_maximum_fusion.refs_0_), channel_id=1, source_target_pairs={{0,4},{4,8},{8,12},{1,5},{5,9},{9,13},{2,6},{6,10},{10,14},{3,7},{... | collective-permute-start | bytes 1671176 | tf_op jit(solution)/shard_map/ppermute | solution.py:224
  10.7 10.7 %collective-permute-done.3 = bf16[272,1024]{1,0:T(8,128)(2,1)S(1)} collective-permute-done((bf16[272,1024]{1,0:T(8,128)(2,1)S(1)}, bf16[272,1024]{1,0:T(8,128)(2,1)S(1)}, u32[]{:S(2)}, u32[]{:S(2)}) %collective-permute-start.3) | collective-permute-done | bytes 557088 | tf_op jit(solution)/shard_map/ppermute | solution.py:225
  21.4 1.3 collective-permute-start.8
  22.7 0.0 collective-permute-done.2
  22.7 0.0 copy-start.7
  22.7 1.5 %collective-permute-start.7 = (bf16[272,1024]{1,0:T(8,128)(2,1)S(1)}, bf16[272,1024]{1,0:T(8,128)(2,1)}, u32[]{:S(2)}, u32[]{:S(2)}) collective-permute-start(bf16[272,1024]{1,0:T(8,128)(2,1)S(1)} %collective-permute-done.2), channel_id=1, source_target_pairs={{4,8},{8,12},{5,9},{9,13},{6,10},{10,14},{7,11},{11,15},{20,24},{2... | collective-permute-start | bytes 1671176 | tf_op jit(solution)/shard_map/ppermute | solution.py:224
  24.2 13.0 %collective-permute-done.8 = bf16[272,1024]{1,0:T(8,128)(2,1)} collective-permute-done((bf16[272,1024]{1,0:T(8,128)(2,1)S(1)}, bf16[272,1024]{1,0:T(8,128)(2,1)}, u32[]{:S(2)}, u32[]{:S(2)}) %collective-permute-start.8) | collective-permute-done | bytes 557088 | tf_op jit(solution)/shard_map/ppermute | solution.py:225
  37.2 1.3 collective-permute-start.13
  38.5 0.0 collective-permute-done.7
  38.5 0.0 copy-done.6
  38.5 1.5 %collective-permute-start.12 = (bf16[272,1024]{1,0:T(8,128)(2,1)}, bf16[272,1024]{1,0:T(8,128)(2,1)}, u32[]{:S(2)}, u32[]{:S(2)}) collective-permute-start(bf16[272,1024]{1,0:T(8,128)(2,1)} %collective-permute-done.7), channel_id=1, source_target_pairs={{8,12},{9,13},{10,14},{11,15},{24,28},{25,29},{26,30},{27,31}} | collective-permute-start | bytes 1671176 | tf_op jit(solution)/shard_map/ppermute | solution.py:224
  40.0 0.0 copy-done.7
  40.0 1.3 collective-permute-start
  41.3 1.1 broadcast_select_fusion.refs_0_
  42.4 0.0 copy-start
  42.5 0.8 collective-permute-start.9
  43.2 9.1 %collective-permute-done.13 = bf16[272,1024]{1,0:T(8,128)(2,1)} collective-permute-done((bf16[272,1024]{1,0:T(8,128)(2,1)}, bf16[272,1024]{1,0:T(8,128)(2,1)}, u32[]{:S(2)}, u32[]{:S(2)}) %collective-permute-start.13) | collective-permute-done | bytes 557088 | tf_op jit(solution)/shard_map/ppermute | solution.py:225
  52.3 0.0 collective-permute-done.12
  52.3 2.5 %broadcast_select_fusion.1 = (bf16[272,1024]{1,0:T(8,128)(2,1)}, bf16[272,1024]{1,0:T(8,128)(2,1)}) fusion(bf16[272,1024]{1,0:T(8,128)(2,1)} %copy-done.7, bf16[272,1024]{1,0:T(8,128)(2,1)} %copy-done.6, pred[]{:T(512)S(6)} %or.6, bf16[272,1024]{1,0:T(8,128)(2,1)} %collective-permute-done.12, bf16[272,1024]{1,0:T(8,128)(2,1)} %collective-permute-done.13, ...), kind=kLoop, calls=%fused_computation.3 | loop fusion | flops 1114112 | bytes 3342340 | tf_op jit(solution)/shard_map/jit(_where)/select_n | solution.py:238
  54.8 1.0 collective-permute-start.14
  55.8 1.0 collective-permute-start.4
  56.8 0.0 collective-permute-done.refs_1_
  56.8 0.0 copy-done
  56.8 7.0 %chunk.4 = (bf16[128,1024]{1,0:T(8,128)(2,1)S(1)}, bf16[128,1024]{1,0:T(8,128)(2,1)S(1)}, bf16[4,96,1024]{2,1,0:T(8,128)(2,1)S(1)}, bf16[4,96,1024]{2,1,0:T(8,128)(2,1)S(1)}, bf16[4,96,768]{2,1,0:T(8,128)(2,1)S(1)}) custom-call(s32[1]{0:T(128)} %bitcast.first_ref, bf16[272,1024]{1,0:T(8,128)(2,1)S(1)} %pad_maximum_fusion.refs_0_, ...), custom_call_target="tpu_custom_call" | custom-call | flops 1610612736 | bytes 8388608 | tf_op jit(solution)/shard_map/chunk/pallas_call | solution.py:110
  63.9 0.0 copy-start.1
  63.9 0.9 copy-done.1
  64.7 2.9 %collective-permute-done.9.refs_1_ = bf16[272,1024]{1,0:T(8,128)(2,1)} collective-permute-done((bf16[272,1024]{1,0:T(8,128)(2,1)S(1)}, bf16[272,1024]{1,0:T(8,128)(2,1)}, u32[]{:S(2)}, u32[]{:S(2)}) %collective-permute-start.9) | collective-permute-done | bytes 557088 | tf_op jit(solution)/shard_map/ppermute | solution.py:240
  67.6 7.0 %chunk.6 = (bf16[128,1024]{1,0:T(8,128)(2,1)S(1)}, bf16[128,1024]{1,0:T(8,128)(2,1)S(1)}, bf16[4,96,1024]{2,1,0:T(8,128)(2,1)S(1)}, bf16[4,96,1024]{2,1,0:T(8,128)(2,1)S(1)}, bf16[4,96,768]{2,1,0:T(8,128)(2,1)S(1)}) custom-call(s32[1]{0:T(128)} %bitcast.first_ref, bf16[272,1024]{1,0:T(8,128)(2,1)S(1)} %broadcast_select_fusion.refs_0_, ...), custom_call_target="tpu_custom_call" | custom-call | flops 1610612736 | bytes 8388608 | tf_op jit(solution)/shard_map/chunk/pallas_call | solution.py:110
  74.6 0.0 copy-start.2
  74.6 0.9 copy-done.2
  75.5 4.0 %collective-permute-done.14.refs_1_ = bf16[272,1024]{1,0:T(8,128)(2,1)} collective-permute-done((bf16[272,1024]{1,0:T(8,128)(2,1)}, bf16[272,1024]{1,0:T(8,128)(2,1)}, u32[]{:S(2)}, u32[]{:S(2)}) %collective-permute-start.14) | collective-permute-done | bytes 557088 | tf_op jit(solution)/shard_map/ppermute | solution.py:240
  79.5 7.2 %chunk.7 = (bf16[128,1024]{1,0:T(8,128)(2,1)S(1)}, bf16[128,1024]{1,0:T(8,128)(2,1)S(1)}, bf16[4,96,1024]{2,1,0:T(8,128)(2,1)S(1)}, bf16[4,96,1024]{2,1,0:T(8,128)(2,1)S(1)}, bf16[4,96,768]{2,1,0:T(8,128)(2,1)S(1)}) custom-call(s32[1]{0:T(128)} %bitcast.first_ref, bf16[272,1024]{1,0:T(8,128)(2,1)} %get-tuple-element.51.refs_0_, ...), custom_call_target="tpu_custom_call" | custom-call | flops 1610612736 | bytes 8388608 | tf_op jit(solution)/shard_map/chunk/pallas_call | solution.py:110
  86.8 0.9 copy-done.3
  87.7 1.1 collective-permute-done.4.refs_1_
  88.8 7.2 %chunk.5 = (bf16[128,1024]{1,0:T(8,128)(2,1)S(1)}, bf16[128,1024]{1,0:T(8,128)(2,1)S(1)}, bf16[4,96,1024]{2,1,0:T(8,128)(2,1)S(1)}, bf16[4,96,1024]{2,1,0:T(8,128)(2,1)S(1)}, bf16[4,96,768]{2,1,0:T(8,128)(2,1)S(1)}) custom-call(s32[1]{0:T(128)} %bitcast.first_ref, bf16[272,1024]{1,0:T(8,128)(2,1)} %get-tuple-element.50.refs_0_, ...), custom_call_target="tpu_custom_call" | custom-call | flops 1610612736 | bytes 8388608 | tf_op jit(solution)/shard_map/chunk/pallas_call | solution.py:110
  96.0 0.9 copy-done.4
  96.9 5.2 %weight_grads.2 = bf16[4,768,512]{2,1,0:T(8,128)(2,1)} custom-call(s32[1]{0:T(128)S(6)} %sub.10.half_ref, bf16[4,96,1024]{2,1,0:T(8,128)(2,1)S(1)} %get-tuple-element.35.refs_0_, bf16[4,96,1024]{2,1,0:T(8,128)(2,1)S(1)} %get-tuple-element.36.refs_1_, bf16[4,96,1024]{2,1,0:T(8,128)(2,1)S(1)} %get-tuple-element.37.refs_2_, ...), custom_call_target="tpu_custom_call" | custom-call | flops 1207959552 | bytes 8650752 | tf_op jit(solution)/shard_map/weight_grads/pallas_call | solution.py:188
  102.2 0.0 collective-permute-start.17
  102.2 1.0 collective-permute-start.10
  103.2 1.0 collective-permute-start.15
  104.2 1.0 collective-permute-start.1
  105.2 1.0 collective-permute-start.5
  106.2 5.0 %collective-permute-done.10 = bf16[128,1024]{1,0:T(8,128)(2,1)S(1)} collective-permute-done((bf16[128,1024]{1,0:T(8,128)(2,1)S(1)}, bf16[128,1024]{1,0:T(8,128)(2,1)S(1)}, u32[]{:S(2)}, u32[]{:S(2)}) %collective-permute-start.10) | collective-permute-done | bytes 262176 | tf_op jit(solution)/shard_map/ppermute | solution.py:257
  111.3 0.1 add_convert_fusion.2
  111.3 4.9 %collective-permute-start.11 = (bf16[128,1024]{1,0:T(8,128)(2,1)S(1)}, bf16[128,1024]{1,0:T(8,128)(2,1)S(1)}, u32[]{:S(2)}, u32[]{:S(2)}) collective-permute-start(bf16[128,1024]{1,0:T(8,128)(2,1)S(1)} %add_convert_fusion.2), channel_id=1, source_target_pairs={{0,8},{4,12},{8,0},{12,4},{1,9},{5,13},{9,1},{13,5},{2,10},{6,14},... | collective-permute-start | bytes 786440 | tf_op jit(solution)/shard_map/ppermute | solution.py:261
  116.2 0.7 collective-permute-done.15
  116.9 0.1 add_convert_fusion.1
  117.0 3.2 %collective-permute-start.16 = (bf16[128,1024]{1,0:T(8,128)(2,1)S(1)}, bf16[128,1024]{1,0:T(8,128)(2,1)S(1)}, u32[]{:S(2)}, u32[]{:S(2)}) collective-permute-start(bf16[128,1024]{1,0:T(8,128)(2,1)S(1)} %add_convert_fusion.1), channel_id=1, source_target_pairs={{0,12},{4,8},{8,4},{12,0},{1,13},{5,9},{9,5},{13,1},{2,14},{6,10},... | collective-permute-start | bytes 786440 | tf_op jit(solution)/shard_map/ppermute | solution.py:261
  120.2 7.5 %collective-permute-done.5 = bf16[128,1024]{1,0:T(8,128)(2,1)S(1)} collective-permute-done((bf16[128,1024]{1,0:T(8,128)(2,1)S(1)}, bf16[128,1024]{1,0:T(8,128)(2,1)S(1)}, u32[]{:S(2)}, u32[]{:S(2)}) %collective-permute-start.5) | collective-permute-done | bytes 262176 | tf_op jit(solution)/shard_map/ppermute | solution.py:257
  127.7 0.1 add_convert_fusion.3
  127.8 3.2 %collective-permute-start.6 = (bf16[128,1024]{1,0:T(8,128)(2,1)S(1)}, bf16[128,1024]{1,0:T(8,128)(2,1)S(1)}, u32[]{:S(2)}, u32[]{:S(2)}) collective-permute-start(bf16[128,1024]{1,0:T(8,128)(2,1)S(1)} %add_convert_fusion.3), channel_id=1, source_target_pairs={{0,4},{4,0},{8,12},{12,8},{1,5},{5,1},{9,13},{13,9},{2,6},{6,2},{1... | collective-permute-start | bytes 786440 | tf_op jit(solution)/shard_map/ppermute | solution.py:261
  131.0 0.0 collective-permute-done.1
  131.0 2.8 %collective-permute-done.11 = bf16[128,1024]{1,0:T(8,128)(2,1)S(1)} collective-permute-done((bf16[128,1024]{1,0:T(8,128)(2,1)S(1)}, bf16[128,1024]{1,0:T(8,128)(2,1)S(1)}, u32[]{:S(2)}, u32[]{:S(2)}) %collective-permute-start.11) | collective-permute-done | bytes 262176 | tf_op jit(solution)/shard_map/ppermute | solution.py:261
  133.8 0.0 collective-permute-done.16
  133.8 5.1 %collective-permute-done.6 = bf16[128,1024]{1,0:T(8,128)(2,1)S(1)} collective-permute-done((bf16[128,1024]{1,0:T(8,128)(2,1)S(1)}, bf16[128,1024]{1,0:T(8,128)(2,1)S(1)}, u32[]{:S(2)}, u32[]{:S(2)}) %collective-permute-start.6) | collective-permute-done | bytes 262176 | tf_op jit(solution)/shard_map/ppermute | solution.py:261
  138.9 0.9 add_convert_fusion
  139.8 0.0 collective-permute-done.17.refs_12_
  139.8 1.6 %copy-done.5 = bf16[4,768,512]{2,1,0:T(8,128)(2,1)} copy-done((bf16[4,768,512]{2,1,0:T(8,128)(2,1)}, bf16[4,768,512]{2,1,0:T(8,128)(2,1)S(1)}, u32[]{:S(2)}) %copy-start.5) | copy-done | bytes 3145752
  141.4 5.6 %weight_grads.3 = (bf16[4,512,256]{2,1,0:T(8,128)(2,1)}, bf16[4,512,256]{2,1,0:T(8,128)(2,1)}, bf16[4,256,512]{2,1,0:T(8,128)(2,1)}) custom-call(s32[1]{0:T(128)} %bitcast.5.half_ref, bf16[4,96,1024]{2,1,0:T(8,128)(2,1)S(1)} %get-tuple-element.35.refs_0_, bf16[4,96,1024]{2,1,0:T(8,128)(2,1)S(1)} %get-tuple-element.36.refs_1_, ...), custom_call_target="tpu_custom_call" | custom-call | flops 1207959552 | bytes 8650752 | tf_op jit(solution)/shard_map/weight_grads/pallas_call | solution.py:188
  (7 shorter events, 0.1 us)
Async XLA Ops:
  3.8 17.5 %collective-permute-start.3 = (bf16[272,1024]{1,0:T(8,128)(2,1)S(1)}, bf16[272,1024]{1,0:T(8,128)(2,1)S(1)}, u32[]{:S(2)}, u32[]{:S(2)}) collective-permute-start(bf16[272,1024]{1,0:T(8,128)(2,1)S(1)} %pad_maximum_fusion.refs_0_), channel_id=1, source_target_pairs={{4,0},{8,4},{12,8},{5,1},{9,5},{13,9},{6,2},{10,6},{14,10},{7,3},{... | collective-permute-start | bytes 1671176 | tf_op jit(solution)/shard_map/ppermute | solution.py:225
  5.1 17.5 %collective-permute-start.2 = (bf16[272,1024]{1,0:T(8,128)(2,1)S(1)}, bf16[272,1024]{1,0:T(8,128)(2,1)S(1)}, u32[]{:S(2)}, u32[]{:S(2)}) collective-permute-start(bf16[272,1024]{1,0:T(8,128)(2,1)S(1)} %pad_maximum_fusion.refs_0_), channel_id=1, source_target_pairs={{0,4},{4,8},{8,12},{1,5},{5,9},{9,13},{2,6},{6,10},{10,14},{3,7},{... | collective-permute-start | bytes 1671176 | tf_op jit(solution)/shard_map/ppermute | solution.py:224
  21.4 17.1 %copy-start.6 = (bf16[272,1024]{1,0:T(8,128)(2,1)}, bf16[272,1024]{1,0:T(8,128)(2,1)S(1)}, u32[]{:S(2)}) copy-start(bf16[272,1024]{1,0:T(8,128)(2,1)S(1)} %collective-permute-done.3) | copy-start | bytes 1671172
  21.4 15.8 %collective-permute-start.8 = (bf16[272,1024]{1,0:T(8,128)(2,1)S(1)}, bf16[272,1024]{1,0:T(8,128)(2,1)}, u32[]{:S(2)}, u32[]{:S(2)}) collective-permute-start(bf16[272,1024]{1,0:T(8,128)(2,1)S(1)} %collective-permute-done.3), channel_id=1, source_target_pairs={{4,0},{8,4},{5,1},{9,5},{6,2},{10,6},{7,3},{11,7},{20,16},{24,20},... | collective-permute-start | bytes 1671176 | tf_op jit(solution)/shard_map/ppermute | solution.py:225
  22.7 17.3 %copy-start.7 = (bf16[272,1024]{1,0:T(8,128)(2,1)}, bf16[272,1024]{1,0:T(8,128)(2,1)S(1)}, u32[]{:S(2)}) copy-start(bf16[272,1024]{1,0:T(8,128)(2,1)S(1)} %collective-permute-done.2) | copy-start | bytes 1671172
  22.7 15.8 %collective-permute-start.7 = (bf16[272,1024]{1,0:T(8,128)(2,1)S(1)}, bf16[272,1024]{1,0:T(8,128)(2,1)}, u32[]{:S(2)}, u32[]{:S(2)}) collective-permute-start(bf16[272,1024]{1,0:T(8,128)(2,1)S(1)} %collective-permute-done.2), channel_id=1, source_target_pairs={{4,8},{8,12},{5,9},{9,13},{6,10},{10,14},{7,11},{11,15},{20,24},{2... | collective-permute-start | bytes 1671176 | tf_op jit(solution)/shard_map/ppermute | solution.py:224
  37.2 15.1 %collective-permute-start.13 = (bf16[272,1024]{1,0:T(8,128)(2,1)}, bf16[272,1024]{1,0:T(8,128)(2,1)}, u32[]{:S(2)}, u32[]{:S(2)}) collective-permute-start(bf16[272,1024]{1,0:T(8,128)(2,1)} %collective-permute-done.8), channel_id=1, source_target_pairs={{4,0},{5,1},{6,2},{7,3},{20,16},{21,17},{22,18},{23,19}} | collective-permute-start | bytes 1671176 | tf_op jit(solution)/shard_map/ppermute | solution.py:225
  38.5 13.8 %collective-permute-start.12 = (bf16[272,1024]{1,0:T(8,128)(2,1)}, bf16[272,1024]{1,0:T(8,128)(2,1)}, u32[]{:S(2)}, u32[]{:S(2)}) collective-permute-start(bf16[272,1024]{1,0:T(8,128)(2,1)} %collective-permute-done.7), channel_id=1, source_target_pairs={{8,12},{9,13},{10,14},{11,15},{24,28},{25,29},{26,30},{27,31}} | collective-permute-start | bytes 1671176 | tf_op jit(solution)/shard_map/ppermute | solution.py:224
  40.0 16.8 %collective-permute-start = (bf16[272,1024]{1,0:T(8,128)(2,1)S(1)}, bf16[272,1024]{1,0:T(8,128)(2,1)}, u32[]{:S(2)}, u32[]{:S(2)}) collective-permute-start(bf16[272,1024]{1,0:T(8,128)(2,1)S(1)} %pad_maximum_fusion.refs_0_), channel_id=1, source_target_pairs={{0,2},{2,0},{1,3},{3,1},{4,6},{6,4},{5,7},{7,5},{8,10},{10,8},{9,1... | collective-permute-start | bytes 1671176 | tf_op jit(solution)/shard_map/ppermute | solution.py:240
  42.4 14.4 %copy-start = (bf16[4,1024,256]{2,1,0:T(8,128)(2,1)S(1)}, bf16[4,1024,256]{2,1,0:T(8,128)(2,1)}, u32[]{:S(2)}) copy-start(bf16[4,1024,256]{2,1,0:T(8,128)(2,1)} %refs_2_.7) | copy-start | bytes 6291460
  42.5 25.1 %collective-permute-start.9 = (bf16[272,1024]{1,0:T(8,128)(2,1)S(1)}, bf16[272,1024]{1,0:T(8,128)(2,1)}, u32[]{:S(2)}, u32[]{:S(2)}) collective-permute-start(bf16[272,1024]{1,0:T(8,128)(2,1)S(1)} %broadcast_select_fusion.refs_0_), channel_id=1, source_target_pairs={{0,2},{2,0},{1,3},{3,1},{4,6},{6,4},{5,7},{7,5},{8,10},{10,8},{9,1... | collective-permute-start | bytes 1671176 | tf_op jit(solution)/shard_map/ppermute | solution.py:240
  54.8 24.8 %collective-permute-start.14 = (bf16[272,1024]{1,0:T(8,128)(2,1)}, bf16[272,1024]{1,0:T(8,128)(2,1)}, u32[]{:S(2)}, u32[]{:S(2)}) collective-permute-start(bf16[272,1024]{1,0:T(8,128)(2,1)} %get-tuple-element.51.refs_0_), channel_id=1, source_target_pairs={{0,2},{2,0},{1,3},{3,1},{4,6},{6,4},{5,7},{7,5},{8,10},{10,8},{9,1... | collective-permute-start | bytes 1671176 | tf_op jit(solution)/shard_map/ppermute | solution.py:240
  55.8 33.0 %collective-permute-start.4 = (bf16[272,1024]{1,0:T(8,128)(2,1)}, bf16[272,1024]{1,0:T(8,128)(2,1)}, u32[]{:S(2)}, u32[]{:S(2)}) collective-permute-start(bf16[272,1024]{1,0:T(8,128)(2,1)} %get-tuple-element.50.refs_0_), channel_id=1, source_target_pairs={{0,2},{2,0},{1,3},{3,1},{4,6},{6,4},{5,7},{7,5},{8,10},{10,8},{9,1... | collective-permute-start | bytes 1671176 | tf_op jit(solution)/shard_map/ppermute | solution.py:240
  63.9 0.9 copy-start.1
  74.6 0.9 copy-start.2
  86.7 0.9 copy-start.3
  96.0 0.9 copy-start.4
  102.2 37.6 %collective-permute-start.17 = (bf16[4,768,512]{2,1,0:T(8,128)(2,1)}, bf16[4,768,512]{2,1,0:T(8,128)(2,1)S(1)}, u32[]{:S(2)}, u32[]{:S(2)}) collective-permute-start(bf16[4,768,512]{2,1,0:T(8,128)(2,1)} %weight_grads.2), channel_id=1, source_target_pairs={{0,1},{1,0},{2,3},{3,2},{4,5},{5,4},{6,7},{7,6},{8,9},{9,8},{10,11... | collective-permute-start | bytes 9437192 | tf_op jit(solution)/shard_map/ppermute | solution.py:250
  102.2 9.1 %collective-permute-start.10 = (bf16[128,1024]{1,0:T(8,128)(2,1)S(1)}, bf16[128,1024]{1,0:T(8,128)(2,1)S(1)}, u32[]{:S(2)}, u32[]{:S(2)}) collective-permute-start(bf16[128,1024]{1,0:T(8,128)(2,1)S(1)} %get-tuple-element.32), channel_id=1, source_target_pairs={{0,2},{2,0},{1,3},{3,1},{4,6},{6,4},{5,7},{7,5},{8,10},{10,8},{9,1... | collective-permute-start | bytes 786440 | tf_op jit(solution)/shard_map/ppermute | solution.py:257
  103.2 13.7 %collective-permute-start.15 = (bf16[128,1024]{1,0:T(8,128)(2,1)S(1)}, bf16[128,1024]{1,0:T(8,128)(2,1)S(1)}, u32[]{:S(2)}, u32[]{:S(2)}) collective-permute-start(bf16[128,1024]{1,0:T(8,128)(2,1)S(1)} %get-tuple-element.34), channel_id=1, source_target_pairs={{0,2},{2,0},{1,3},{3,1},{4,6},{6,4},{5,7},{7,5},{8,10},{10,8},{9,1... | collective-permute-start | bytes 786440 | tf_op jit(solution)/shard_map/ppermute | solution.py:257
  104.2 26.8 %collective-permute-start.1 = (bf16[128,1024]{1,0:T(8,128)(2,1)S(1)}, bf16[128,1024]{1,0:T(8,128)(2,1)S(1)}, u32[]{:S(2)}, u32[]{:S(2)}) collective-permute-start(bf16[128,1024]{1,0:T(8,128)(2,1)S(1)} %get-tuple-element.28), channel_id=1, source_target_pairs={{0,2},{2,0},{1,3},{3,1},{4,6},{6,4},{5,7},{7,5},{8,10},{10,8},{9,1... | collective-permute-start | bytes 786440 | tf_op jit(solution)/shard_map/ppermute | solution.py:257
  105.2 22.5 %collective-permute-start.5 = (bf16[128,1024]{1,0:T(8,128)(2,1)S(1)}, bf16[128,1024]{1,0:T(8,128)(2,1)S(1)}, u32[]{:S(2)}, u32[]{:S(2)}) collective-permute-start(bf16[128,1024]{1,0:T(8,128)(2,1)S(1)} %get-tuple-element.30), channel_id=1, source_target_pairs={{0,2},{2,0},{1,3},{3,1},{4,6},{6,4},{5,7},{7,5},{8,10},{10,8},{9,1... | collective-permute-start | bytes 786440 | tf_op jit(solution)/shard_map/ppermute | solution.py:257
  111.3 22.5 %collective-permute-start.11 = (bf16[128,1024]{1,0:T(8,128)(2,1)S(1)}, bf16[128,1024]{1,0:T(8,128)(2,1)S(1)}, u32[]{:S(2)}, u32[]{:S(2)}) collective-permute-start(bf16[128,1024]{1,0:T(8,128)(2,1)S(1)} %add_convert_fusion.2), channel_id=1, source_target_pairs={{0,8},{4,12},{8,0},{12,4},{1,9},{5,13},{9,1},{13,5},{2,10},{6,14},... | collective-permute-start | bytes 786440 | tf_op jit(solution)/shard_map/ppermute | solution.py:261
  117.0 16.9 %collective-permute-start.16 = (bf16[128,1024]{1,0:T(8,128)(2,1)S(1)}, bf16[128,1024]{1,0:T(8,128)(2,1)S(1)}, u32[]{:S(2)}, u32[]{:S(2)}) collective-permute-start(bf16[128,1024]{1,0:T(8,128)(2,1)S(1)} %add_convert_fusion.1), channel_id=1, source_target_pairs={{0,12},{4,8},{8,4},{12,0},{1,13},{5,9},{9,5},{13,1},{2,14},{6,10},... | collective-permute-start | bytes 786440 | tf_op jit(solution)/shard_map/ppermute | solution.py:261
  127.8 11.1 %collective-permute-start.6 = (bf16[128,1024]{1,0:T(8,128)(2,1)S(1)}, bf16[128,1024]{1,0:T(8,128)(2,1)S(1)}, u32[]{:S(2)}, u32[]{:S(2)}) collective-permute-start(bf16[128,1024]{1,0:T(8,128)(2,1)S(1)} %add_convert_fusion.3), channel_id=1, source_target_pairs={{0,4},{4,0},{8,12},{12,8},{1,5},{5,1},{9,13},{13,9},{2,6},{6,2},{1... | collective-permute-start | bytes 786440 | tf_op jit(solution)/shard_map/ppermute | solution.py:261
  139.8 1.6 %copy-start.5 = (bf16[4,768,512]{2,1,0:T(8,128)(2,1)}, bf16[4,768,512]{2,1,0:T(8,128)(2,1)S(1)}, u32[]{:S(2)}) copy-start(bf16[4,768,512]{2,1,0:T(8,128)(2,1)S(1)} %collective-permute-done.17.refs_12_) | copy-start | bytes 9437188

commit v2 on v1

--- a/solution.py
+++ b/solution.py
@@ -9,7 +9,7 @@
 
 GROUPS_TOK = 4
 ROUTE_ROWS = 16
-VMEM_LIMIT = 48 * 1024 * 1024
+VMEM_LIMIT = 24 * 1024 * 1024
 
 
 def dot(a, b, contract):
@@ -25,27 +25,61 @@
     return z ^ k if size & (size - 1) == 0 else (k - z) % size
 
 
+def pack_kernel(tokens, upstream, expert_ids, slots, gate_fixed, out, sem):
+    top_count, tok_rows = expert_ids.shape
+    copies = [
+        pltpu.make_async_copy(src, out.at[pl.ds(i * tok_rows, tok_rows), :], sem.at[i])
+        for i, src in enumerate((tokens, upstream))
+    ]
+    for copy in copies:
+        copy.start()
+    gate = gate_fixed[...]
+    out[2 * tok_rows :, :] = jnp.zeros((ROUTE_ROWS, out.shape[1]), jnp.bfloat16)
+    for i, field in enumerate((expert_ids[...], slots[...], gate >> 8, gate & 255)):
+        field = jnp.concatenate([field.astype(jnp.float32), jnp.zeros((ROUTE_ROWS - top_count, tok_rows), jnp.float32)], axis=0)
+        out[2 * tok_rows :, i * tok_rows : (i + 1) * tok_rows] = field.astype(jnp.bfloat16)
+    for copy in copies:
+        copy.wait()
+
+
+def pack_call(tokens, upstream, expert_ids, slots, gate_fixed):
+    tok_rows, width = tokens.shape
+    vmem = pl.BlockSpec(memory_space=pltpu.VMEM)
+    return pl.pallas_call(
+        pack_kernel,
+        in_specs=[pl.BlockSpec(memory_space=pltpu.HBM)] * 2 + [vmem] * 3,
+        out_specs=vmem,
+        out_shape=jax.ShapeDtypeStruct((2 * tok_rows + ROUTE_ROWS, width), jnp.bfloat16),
+        scratch_shapes=[pltpu.SemaphoreType.DMA((2,))],
+        compiler_params=pltpu.CompilerParams(vmem_limit_bytes=VMEM_LIMIT),
+        name="pack",
+    )(tokens, upstream, expert_ids.T, slots.T, gate_fixed.T)
+
+
 def route_keys(route, first_expert, local_experts, capacity, rows, offset, tok_rows, per_group):
-    expert = route[0:1, :].astype(jnp.int32) - first_expert
-    slot = route[1:2, :].astype(jnp.int32)
-    gate = (route[2:3, :] * 256.0 + route[3:4, :]) / 65536.0
+    field = lambda i: route[:, i * tok_rows : (i + 1) * tok_rows]
+    expert = field(0).astype(jnp.int32) - first_expert
+    slot = field(1).astype(jnp.int32)
+    gate = (field(2) * 256.0 + field(3)) / 65536.0
     valid = (expert >= 0) & (expert < local_experts) & (slot < capacity)
     key = jnp.where(valid, expert * rows + offset + slot, -1)
     gate = jnp.where(valid, gate, 0.0)
-    width = tok_rows * per_group
-    key_out, gate_out = key[:, :width], gate[:, :width]
-    for j in range(1, route.shape[1] // width):
-        key_out = jnp.maximum(key_out, key[:, j * width : (j + 1) * width])
-        gate_out = jnp.maximum(gate_out, gate[:, j * width : (j + 1) * width])
-    return key_out, gate_out
-
-
-def chunk_kernel(n_blocks, tok_rows, capacity, rows, per_group, first_ref, *refs):
+    pairs = []
+    for i in range(per_group):
+        key_out, gate_out = key[i : i + 1, :], gate[i : i + 1, :]
+        for j in range(i + per_group, route.shape[0], per_group):
+            key_out = jnp.maximum(key_out, key[j : j + 1, :])
+            gate_out = jnp.maximum(gate_out, gate[j : j + 1, :])
+        pairs.append((key_out, gate_out))
+    return pairs
+
+
+def chunk_kernel(n_blocks, tok_rows, capacity, rows, top_count, per_group, first_ref, *refs):
     payloads = refs[:n_blocks]
     w_gate, w_up, w_down = refs[n_blocks : n_blocks + 3]
-    parts = refs[n_blocks + 3 : 2 * n_blocks + 3]
-    x_out, s_out, h_out = refs[2 * n_blocks + 3 : 2 * n_blocks + 6]
-    x_all, u_all, key_all, gate_all, hot_all, back_all = refs[2 * n_blocks + 6 :]
+    n_parts = len(refs) - n_blocks - 12
+    parts = refs[n_blocks + 3 : n_blocks + 3 + n_parts]
+    x_out, s_out, h_out, x_all, u_all, key_all, gate_all, hot_all, back_all = refs[-9:]
     e = pl.program_id(0)
     local_experts = pl.num_programs(0)
     n_tok = n_blocks * tok_rows
@@ -57,14 +91,13 @@
             rows_b = slice(b * tok_rows, (b + 1) * tok_rows)
             x_all[rows_b, :] = payloads[b][:tok_rows, :]
             u_all[rows_b, :] = payloads[b][tok_rows : 2 * tok_rows, :]
-            route = payloads[b][2 * tok_rows : 2 * tok_rows + ROUTE_ROWS, :].astype(jnp.float32)
-            key, gate = route_keys(
+            route = payloads[b][2 * tok_rows : 2 * tok_rows + ROUTE_ROWS, :].astype(jnp.float32)[:top_count]
+            pairs = route_keys(
                 route, first_ref[0], local_experts, capacity, rows, b * capacity, tok_rows, per_group
             )
-            for i in range(per_group):
-                cols = slice(i * tok_rows, (i + 1) * tok_rows)
-                key_all[i : i + 1, rows_b] = key[:, cols]
-                gate_all[i : i + 1, rows_b] = gate[:, cols]
+            for i, (key, gate) in enumerate(pairs):
+                key_all[i : i + 1, rows_b] = key
+                gate_all[i : i + 1, rows_b] = gate
 
     place = lax.broadcasted_iota(jnp.int32, (rows, n_tok), 0) + e * rows
     hot = jnp.zeros((rows, n_tok), jnp.float32)
@@ -96,25 +129,28 @@
     @pl.when(e == local_experts - 1)
     def _():
         summed = dot(hot_all[...], back_all[...], (0, 0)).astype(jnp.bfloat16)
-        for b in range(n_blocks):
-            parts[b][...] = summed[b * tok_rows : (b + 1) * tok_rows, :]
-
-
-def chunk_call(payloads, first_expert, w_gate, w_up, w_down, tok_rows, capacity, rows, per_group):
+        start = 0
+        for part in parts:
+            part[...] = summed[start : start + part.shape[0], :]
+            start += part.shape[0]
+
+
+def chunk_call(payloads, first_expert, w_gate, w_up, w_down, tok_rows, capacity, rows, top_count, per_group, joined):
     n_blocks = len(payloads)
     n_tok = n_blocks * tok_rows
     experts, width, ff = w_gate.shape
+    part_shapes = [(n_tok, width)] if joined else [(tok_rows, width), (n_tok - tok_rows, width)]
     whole = lambda shape: pl.BlockSpec(shape, lambda e, first: (0, 0))
     per_expert = lambda shape: pl.BlockSpec((1,) + shape, lambda e, first: (e, 0, 0))
     flops = 2 * experts * rows * width * (5 * ff + 3 * n_tok)
     return pl.pallas_call(
-        functools.partial(chunk_kernel, n_blocks, tok_rows, capacity, rows, per_group),
+        functools.partial(chunk_kernel, n_blocks, tok_rows, capacity, rows, top_count, per_group),
         grid_spec=pltpu.PrefetchScalarGridSpec(
             num_scalar_prefetch=1,
             grid=(experts,),
             in_specs=[whole(payloads[0].shape)] * n_blocks
             + [per_expert((width, ff)), per_expert((width, ff)), per_expert((ff, width))],
-            out_specs=[whole((tok_rows, width))] * n_blocks
+            out_specs=[whole(shape) for shape in part_shapes]
             + [per_expert((rows, width)), per_expert((rows, width)), per_expert((rows, 3 * ff))],
             scratch_shapes=[
                 pltpu.VMEM((n_tok, width), jnp.bfloat16),
@@ -125,7 +161,7 @@
                 pltpu.VMEM((experts * rows, width), jnp.bfloat16),
             ],
         ),
-        out_shape=[jax.ShapeDtypeStruct((tok_rows, width), jnp.bfloat16)] * n_blocks
+        out_shape=[jax.ShapeDtypeStruct(shape, jnp.bfloat16) for shape in part_shapes]
         + [
             jax.ShapeDtypeStruct((experts, rows, width), jnp.bfloat16),
             jax.ShapeDtypeStruct((experts, rows, width), jnp.bfloat16),
@@ -201,6 +237,32 @@
     )(half, *operands)
 
 
+def pass_steps(size):
+    steps = [{} for _ in range(size - 1)]
+    for z in range(size):
+        for k in range(1, size):
+            block = partner(z, k, size)
+            via = z + (1 if block > z else -1)
+            held = next(j for j in range(size) if partner(via, j, size) == block)
+            steps[abs(block - z) - 1].setdefault((held, k), []).append((via, z))
+    return steps
+
+
+def merge(pieces, z):
+    out = pieces[0][0]
+    for piece, places in pieces[1:]:
+        out = jnp.where(functools.reduce(jnp.logical_or, [z == i for i in places]), piece, out)
+    return out
+
+
+def piece_of(pieces, pairs, z):
+    sources = {a for a, _ in pairs}
+    for piece, places in pieces:
+        if sources <= set(places):
+            return piece
+    return merge(pieces, z)
+
+
 def per_device(tokens, upstream, expert_ids, gate_fixed, slots, w_gate, w_up, w_down):
     local_experts = w_gate.shape[0]
     n_group = lax.axis_size("group")
@@ -214,56 +276,74 @@
     z, x, core = (lax.axis_index(a) for a in ("group", "ingroup", "dp"))
     first_expert = ((z * n_ingroup + x) * local_experts).astype(jnp.int32).reshape(1)
 
-    route = jnp.stack([expert_ids.T, slots.T, (gate_fixed // 256).T, (gate_fixed % 256).T])
-    route = route.reshape(-1, width).astype(jnp.bfloat16)
-    route = jnp.pad(route, ((0, ROUTE_ROWS - route.shape[0]), (0, 0)))
-    own = jnp.concatenate([tokens, upstream, route], axis=0)
-
-    ups, downs = {0: own}, {0: own}
-    for s in range(1, n_group):
-        ups[s] = lax.ppermute(ups[s - 1], "group", [(i, i + 1) for i in range(s - 1, n_group - 1)])
-        downs[s] = lax.ppermute(downs[s - 1], "group", [(i, i - 1) for i in range(1, n_group - s + 1)])
-
-    chunks = []
-    for k in range(n_group):
-        if k == 0:
-            column = own
-        else:
-            offsets = [i - partner(i, k, n_group) for i in range(n_group)]
-            kinds = sorted(set(offsets))
-            column = None
-            for off in kinds:
-                case = ups[off] if off >= 0 else downs[-off]
-                picks = functools.reduce(jnp.logical_or, [z == i for i in range(n_group) if offsets[i] == off])
-                column = case if column is None else jnp.where(picks, case, column)
-        blocks = [column] + [
-            lax.ppermute(column, "ingroup", [(i, (i + s) % n_ingroup) for i in range(n_ingroup)])
+    own = pack_call(tokens, upstream, expert_ids, slots, gate_fixed)
+    swap = lambda k: [(i, partner(i, k, n_group)) for i in range(n_group)]
+    shift = lambda s: [(i, (i + s) % n_ingroup) for i in range(n_ingroup)]
+    spread = lambda column: [column] + [lax.ppermute(column, "ingroup", shift(s)) for s in range(1, n_ingroup)]
+    steps = pass_steps(n_group)
+
+    pieces = {0: [(own, range(n_group))]}
+    ready = {0: 0}
+    for step, table in enumerate(steps, 1):
+        ready.update({k: step for _, k in table})
+    wide = lambda v: v.astype(jnp.float32)
+
+    def across(others):
+        return [
+            lax.ppermute(others[(s - 1) * tok_rows : s * tok_rows], "ingroup", [(b, a) for a, b in shift(s)])
             for s in range(1, n_ingroup)
         ]
-        chunks.append(
-            chunk_call(blocks, first_expert, w_gate, w_up, w_down, tok_rows, capacity, rows, per_group)
+
+    half = core.astype(jnp.int32).reshape(1)
+    blocks, chunks, backs, near, to_send = {}, {}, {}, None, None
+    for wave in range(1, n_group + 2):
+        table = steps[wave - 1] if wave < n_group else {}
+        moved = [
+            lax.ppermute(piece_of(pieces[a], pairs, z), "group", pairs) for (a, b), pairs in table.items()
+        ]
+        new = [k for k in ready if ready[k] == wave - 1]
+        spreads = [spread(merge(pieces[k], z)) for k in new]
+        sums = []
+        if wave == n_group + 1:
+            other = (wide(chunks[0][1]) + wide(near[tok_rows:])).astype(jnp.bfloat16)
+            sums = {k: across(other if k == 0 else chunks[k][1]) for k in chunks if k != 1}
+        elif near is None and 1 in chunks:
+            near = lax.ppermute(chunks[1][0], "group", swap(1))
+        here = [k for k in ready if ready[k] == wave - 2]
+        done = [
+            chunk_call(
+                blocks[k], first_expert, w_gate, w_up, w_down, tok_rows, capacity, rows, top_count, per_group, k == 1
+            )
+            for k in here
+        ]
+        if wave == n_group + 1:
+            all_chunks = {**chunks, **dict(zip(here, done))}
+            kept = [[all_chunks[k][i] for k in range(n_group)] for i in (-3, -2, -1)]
+            to_send = weight_call(1 - half, *kept)
+        moved, spreads, done, near, sums, to_send = lax.optimization_barrier(
+            (moved, spreads, done, near, sums, to_send)
         )
-
-    x_rows, s_rows, hids = ([c[n_ingroup + i] for c in chunks] for i in range(3))
-    half = core.astype(jnp.int32).reshape(1)
-    to_send = weight_call(1 - half, x_rows, s_rows, hids)
+        for (a, b), pairs, piece in zip(table.keys(), table.values(), moved):
+            pieces.setdefault(b, []).append((piece, [to for _, to in pairs]))
+        blocks.update(zip(new, spreads))
+        chunks.update(zip(here, done))
+
     got = lax.ppermute(to_send, "dp", [(0, 1), (1, 0)])
-
-    total = jnp.zeros((tok_rows, width), jnp.float32)
-    for k in range(n_group):
-        parts = chunks[k][:n_ingroup]
-        group_part = parts[0].astype(jnp.float32)
-        for s in range(1, n_ingroup):
-            back = lax.ppermute(parts[s], "ingroup", [(i, (i - s) % n_ingroup) for i in range(n_ingroup)])
-            group_part = group_part + back.astype(jnp.float32)
-        group_part = group_part.astype(jnp.bfloat16)
-        if k > 0:
-            group_part = lax.ppermute(
-                group_part, "group", [(i, partner(i, k, n_group)) for i in range(n_group)]
-            )
-        total = total + group_part.astype(jnp.float32)
+    total = wide(chunks[0][0]) + wide(near[:tok_rows])
+    for back in sums[0]:
+        total = total + wide(back)
+    last = {k: across(chunks[k][1]) for k in here}
+    sent = {}
+    for k in range(2, n_group):
+        group_part = wide(chunks[k][0])
+        for back in last[k] if k in last else sums[k]:
+            group_part = group_part + wide(back)
+        sent[k] = lax.ppermute(group_part.astype(jnp.bfloat16), "group", swap(k))
+    for k in range(2, n_group):
+        total = total + wide(sent[k])
     grad_tokens = total.astype(jnp.bfloat16)
 
+    x_rows, s_rows, hids = ([chunks[k][i] for k in range(n_group)] for i in (-3, -2, -1))
     grad_gate, grad_up, grad_down = weight_call(half, x_rows, s_rows, hids, got)
     return grad_tokens, grad_gate, grad_up, grad_down
 

time: 148 us -> 125 us (0.84)
  the two profiles are of different devices: /device:TPU:0 before, /device:TPU:12 now
where the time goes in v2:
time: 125 us; the launch traced here: 124 us
  waiting for transfers between devices  37.7 us (30%)
  Pallas kernels  33.9 us (27%)
  local copies, waits for them, and re-layouts  23.7 us (19%)
  starting transfers between devices  20.8 us (17%)
  other arithmetic  6.87 us (5%)
    pallas_call x4, Pallas kernels, chunk_call(): pl.pallas_call(functools.partial(chunk_kernel, n_blocks, tok_rows, capaci...  27.1 us
    unnamed x60, local copies, waits for them, and re-layouts  23.7 us
    ppermute x2, waiting for transfers between devices, per_device(): sent[k] = lax.ppermute(group_part.astype(jnp.bfloat16), 'group', swap(k))  16.4 us
    ppermute x5, starting transfers between devices, per_device(): lax.ppermute(piece_of(pieces[a], pairs, z), 'group', pairs)  11.6 us
    ppermute x4, waiting for transfers between devices, per_device(): lax.ppermute(column, 'ingroup', shift(s))  9.59 us
    ppermute x3, waiting for transfers between devices, across(): lax.ppermute(others[(s - 1) * tok_rows:s * tok_rows], 'ingroup', [(b, a)...  6.8 us
    pallas_call x2, Pallas kernels, weight_call(): pl.pallas_call(functools.partial(kernel, n, ff), grid_spec=pltpu.Prefetch...  6.7 us
    ppermute x4, starting transfers between devices, per_device(): lax.ppermute(column, 'ingroup', shift(s))  4.11 us
  transfers between devices with their start and end apart: 16, of which 8 were waited for; matrix products, arithmetic and copies ran while one was open for 2% of the time, Pallas kernels for 24%

profile of v2, /device:TPU:12, one launch (start us, length us, event | category | flops | bytes accessed | tf_op | source)
XLA Modules:
  0.0 123.8 jit_solution(15404659176872565455)
XLA Ops:
  0.6 0.9 copy-done.23
  1.6 0.9 copy-done.24
  2.5 0.7 copy-done.27
  3.2 0.7 copy-done.28
  3.9 0.7 copy-done.29
  4.6 0.1 pack.1.refs_0_
  4.7 1.6 %collective-permute-start.2 = (bf16[272,1024]{1,0:T(8,128)(2,1)S(1)}, bf16[272,1024]{1,0:T(8,128)(2,1)S(1)}, u32[]{:S(2)}, u32[]{:S(2)}) collective-permute-start(bf16[272,1024]{1,0:T(8,128)(2,1)S(1)} %pack.1.refs_0_), channel_id=1, source_target_pairs={{0,2},{2,0},{1,3},{3,1},{4,6},{6,4},{5,7},{7,5},{8,10},{10,8},{9,1... | collective-permute-start | bytes 1671176 | tf_op jit(solution)/shard_map/ppermute | solution.py:282
  6.2 3.5 %collective-permute-start.1 = (bf16[272,1024]{1,0:T(8,128)(2,1)S(1)}, bf16[272,1024]{1,0:T(8,128)(2,1)}, u32[]{:S(2)}, u32[]{:S(2)}) collective-permute-start(bf16[272,1024]{1,0:T(8,128)(2,1)S(1)} %pack.1.refs_0_), channel_id=1, source_target_pairs={{8,4},{4,8},{9,5},{5,9},{10,6},{6,10},{11,7},{7,11},{24,20},{20,24... | collective-permute-start | bytes 1671176 | tf_op jit(solution)/shard_map/ppermute | solution.py:302
  9.7 0.1 collective-permute-start
  9.8 0.0 copy-start.17
  9.8 0.8 copy-done.17
  10.6 8.5 %collective-permute-done.2.refs_1_ = bf16[272,1024]{1,0:T(8,128)(2,1)S(1)} collective-permute-done((bf16[272,1024]{1,0:T(8,128)(2,1)S(1)}, bf16[272,1024]{1,0:T(8,128)(2,1)S(1)}, u32[]{:S(2)}, u32[]{:S(2)}) %collective-permute-start.2) | collective-permute-done | bytes 557088 | tf_op jit(solution)/shard_map/ppermute | solution.py:282
  19.1 0.8 copy-done.19
  19.9 2.4 %collective-permute-done.1 = bf16[272,1024]{1,0:T(8,128)(2,1)} collective-permute-done((bf16[272,1024]{1,0:T(8,128)(2,1)S(1)}, bf16[272,1024]{1,0:T(8,128)(2,1)}, u32[]{:S(2)}, u32[]{:S(2)}) %collective-permute-start.1) | collective-permute-done | bytes 557088 | tf_op jit(solution)/shard_map/ppermute | solution.py:302
  22.3 1.4 %collective-permute-done.refs_0_ = bf16[272,1024]{1,0:T(8,128)(2,1)} collective-permute-done((bf16[272,1024]{1,0:T(8,128)(2,1)S(1)}, bf16[272,1024]{1,0:T(8,128)(2,1)}, u32[]{:S(2)}, u32[]{:S(2)}) %collective-permute-start) | collective-permute-done | bytes 557088 | tf_op jit(solution)/shard_map/ppermute | solution.py:302
  23.7 3.0 %collective-permute-start.3 = (bf16[272,1024]{1,0:T(8,128)(2,1)}, bf16[272,1024]{1,0:T(8,128)(2,1)}, u32[]{:S(2)}, u32[]{:S(2)}) collective-permute-start(bf16[272,1024]{1,0:T(8,128)(2,1)} %collective-permute-done.1), channel_id=1, source_target_pairs={{4,0},{8,12},{5,1},{9,13},{6,2},{10,14},{7,3},{11,15},{20,16},{24,... | collective-permute-start | bytes 1671176 | tf_op jit(solution)/shard_map/ppermute | solution.py:302
  26.7 0.5 collective-permute-start.5
  27.2 3.0 %collective-permute-start.4 = (bf16[272,1024]{1,0:T(8,128)(2,1)}, bf16[272,1024]{1,0:T(8,128)(2,1)}, u32[]{:S(2)}, u32[]{:S(2)}) collective-permute-start(bf16[272,1024]{1,0:T(8,128)(2,1)} %collective-permute-done.refs_0_), channel_id=1, source_target_pairs={{8,4},{4,8},{9,5},{5,9},{10,6},{6,10},{11,7},{7,11},{24,20},{20,24... | collective-permute-start | bytes 1671176 | tf_op jit(solution)/shard_map/ppermute | solution.py:302
  30.2 0.0 copy-start
  30.2 1.6 %copy-done = bf16[4,1024,256]{2,1,0:T(8,128)(2,1)S(1)} copy-done((bf16[4,1024,256]{2,1,0:T(8,128)(2,1)S(1)}, bf16[4,1024,256]{2,1,0:T(8,128)(2,1)}, u32[]{:S(2)}) %copy-start) | copy-done | bytes 2097176
  31.8 1.6 %copy-done.2 = bf16[4,1024,256]{2,1,0:T(8,128)(2,1)S(1)} copy-done((bf16[4,1024,256]{2,1,0:T(8,128)(2,1)S(1)}, bf16[4,1024,256]{2,1,0:T(8,128)(2,1)}, u32[]{:S(2)}) %copy-start.2) | copy-done | bytes 2097176
  33.4 1.6 %copy-done.6 = bf16[4,256,1024]{2,1,0:T(8,128)(2,1)S(1)} copy-done((bf16[4,256,1024]{2,1,0:T(8,128)(2,1)S(1)}, bf16[4,256,1024]{2,1,0:T(8,128)(2,1)}, u32[]{:S(2)}) %copy-start.6) | copy-done | bytes 2097176
  35.0 1.1 copy-done.18
  36.0 1.1 copy-done.20
  37.1 5.6 %chunk.4 = (bf16[128,1024]{1,0:T(8,128)(2,1)S(1)}, bf16[128,1024]{1,0:T(8,128)(2,1)S(1)}, bf16[4,96,1024]{2,1,0:T(8,128)(2,1)S(1)}, bf16[4,96,1024]{2,1,0:T(8,128)(2,1)S(1)}, bf16[4,96,768]{2,1,0:T(8,128)(2,1)S(1)}) custom-call(s32[1]{0:T(128)} %bitcast.3.first_ref, bf16[272,1024]{1,0:T(8,128)(2,1)S(1)} %copy-done.18, bf16[272,1024]{1,0:T(8,128)(2,1)S(1)} %copy-done.20, ...), custom_call_target="tpu_custom_call" | custom-call | flops 1610612736 | bytes 8388608 | tf_op jit(solution)/shard_map/chunk/pallas_call | solution.py:146
  42.7 0.0 copy-start.9
  42.7 0.9 copy-done.9
  43.6 0.7 copy-done.21
  44.3 0.7 copy-done.25
  45.0 1.9 %broadcast_select_fusion.refs_0_ = bf16[272,1024]{1,0:T(8,128)(2,1)} fusion(bf16[272,1024]{1,0:T(8,128)(2,1)} %collective-permute-done.4, bf16[272,1024]{1,0:T(8,128)(2,1)} %collective-permute-done.3, pred[]{:T(512)S(6)} %or.7), kind=kLoop, calls=%fused_computation | loop fusion | flops 278528 | bytes 1671169 | tf_op jit(solution)/shard_map/jit(_where)/select_n | solution.py:254
  46.9 1.5 %collective-permute-start.7 = (bf16[272,1024]{1,0:T(8,128)(2,1)}, bf16[272,1024]{1,0:T(8,128)(2,1)}, u32[]{:S(2)}, u32[]{:S(2)}) collective-permute-start(bf16[272,1024]{1,0:T(8,128)(2,1)} %broadcast_select_fusion.refs_0_), channel_id=1, source_target_pairs={{0,2},{2,0},{1,3},{3,1},{4,6},{6,4},{5,7},{7,5},{8,10},{10,8},{9,1... | collective-permute-start | bytes 1671176 | tf_op jit(solution)/shard_map/ppermute | solution.py:282
  48.4 2.1 %collective-permute-start.6 = (bf16[272,1024]{1,0:T(8,128)(2,1)}, bf16[272,1024]{1,0:T(8,128)(2,1)}, u32[]{:S(2)}, u32[]{:S(2)}) collective-permute-start(bf16[272,1024]{1,0:T(8,128)(2,1)} %collective-permute-done.4), channel_id=1, source_target_pairs={{4,0},{8,12},{5,1},{9,13},{6,2},{10,14},{7,3},{11,15},{20,16},{24,... | collective-permute-start | bytes 1671176 | tf_op jit(solution)/shard_map/ppermute | solution.py:302
  50.5 1.6 %copy-done.3 = bf16[4,1024,256]{2,1,0:T(8,128)(2,1)S(1)} copy-done((bf16[4,1024,256]{2,1,0:T(8,128)(2,1)S(1)}, bf16[4,1024,256]{2,1,0:T(8,128)(2,1)}, u32[]{:S(2)}) %copy-start.3) | copy-done | bytes 2097176
  52.1 1.6 %copy-done.7 = bf16[4,256,1024]{2,1,0:T(8,128)(2,1)S(1)} copy-done((bf16[4,256,1024]{2,1,0:T(8,128)(2,1)S(1)}, bf16[4,256,1024]{2,1,0:T(8,128)(2,1)}, u32[]{:S(2)}) %copy-start.7) | copy-done | bytes 2097176
  53.7 7.7 %chunk.5 = (bf16[256,1024]{1,0:T(8,128)(2,1)}, bf16[4,96,1024]{2,1,0:T(8,128)(2,1)S(1)}, bf16[4,96,1024]{2,1,0:T(8,128)(2,1)S(1)}, bf16[4,96,768]{2,1,0:T(8,128)(2,1)S(1)}) custom-call(s32[1]{0:T(128)} %bitcast.3.first_ref, bf16[272,1024]{1,0:T(8,128)(2,1)} %collective-permute-done.refs_0_, bf16[272,1024]{1,0:T(8,128)(2,1)} %collective-permute-done.5.refs_1_, ...), custom_call_target="tpu_custom_call" | custom-call | flops 1610612736 | bytes 8388608 | tf_op jit(solution)/shard_map/chunk/pallas_call | solution.py:146
  61.3 0.9 copy-done.11
  62.2 0.9 copy-done.13
  63.1 0.8 copy-done.15
  63.9 1.9 %broadcast_select_fusion.1.refs_0_ = bf16[272,1024]{1,0:T(8,128)(2,1)} fusion(bf16[272,1024]{1,0:T(8,128)(2,1)} %collective-permute-done.6, bf16[272,1024]{1,0:T(8,128)(2,1)} %collective-permute-done.1, pred[]{:T(512)S(6)} %or.6), kind=kLoop, calls=%fused_computation.1 | loop fusion | flops 278528 | bytes 1671169 | tf_op jit(solution)/shard_map/jit(_where)/select_n | solution.py:254
  65.9 0.5 collective-permute-start.8
  66.4 1.6 %copy-done.4 = bf16[4,1024,256]{2,1,0:T(8,128)(2,1)S(1)} copy-done((bf16[4,1024,256]{2,1,0:T(8,128)(2,1)S(1)}, bf16[4,1024,256]{2,1,0:T(8,128)(2,1)}, u32[]{:S(2)}) %copy-start.4) | copy-done | bytes 2097176
  68.0 1.6 %copy-done.8 = bf16[4,256,1024]{2,1,0:T(8,128)(2,1)S(1)} copy-done((bf16[4,256,1024]{2,1,0:T(8,128)(2,1)S(1)}, bf16[4,256,1024]{2,1,0:T(8,128)(2,1)}, u32[]{:S(2)}) %copy-start.8) | copy-done | bytes 2097176
  69.6 7.0 %chunk.6 = (bf16[128,1024]{1,0:T(8,128)(2,1)S(1)}, bf16[128,1024]{1,0:T(8,128)(2,1)S(1)}, bf16[4,96,1024]{2,1,0:T(8,128)(2,1)S(1)}, bf16[4,96,1024]{2,1,0:T(8,128)(2,1)S(1)}, bf16[4,96,768]{2,1,0:T(8,128)(2,1)S(1)}) custom-call(s32[1]{0:T(128)} %bitcast.3.first_ref, bf16[272,1024]{1,0:T(8,128)(2,1)} %broadcast_select_fusion.refs_0_, ...), custom_call_target="tpu_custom_call" | custom-call | flops 1610612736 | bytes 8388608 | tf_op jit(solution)/shard_map/chunk/pallas_call | solution.py:146
  76.6 1.2 collective-permute-done.9
  77.8 1.1 collective-permute-done.8.refs_1_
  78.9 0.4 collective-permute-start.11
  79.3 1.0 add_convert_fusion.3
  80.3 0.0 copy-start.10
  80.3 0.0 copy-start.12
  80.3 0.0 copy-start.14
  80.3 1.7 %collective-permute-start.10 = (bf16[128,1024]{1,0:T(8,128)(2,1)S(1)}, bf16[128,1024]{1,0:T(8,128)(2,1)S(1)}, u32[]{:S(2)}, u32[]{:S(2)}) collective-permute-start(bf16[128,1024]{1,0:T(8,128)(2,1)S(1)} %add_convert_fusion.3), channel_id=1, source_target_pairs={{2,0},{0,2},{3,1},{1,3},{6,4},{4,6},{7,5},{5,7},{10,8},{8,10},{11,... | collective-permute-start | bytes 786440 | tf_op jit(solution)/shard_map/ppermute | solution.py:293
  82.0 6.8 %chunk.7 = (bf16[128,1024]{1,0:T(8,128)(2,1)S(1)}, bf16[128,1024]{1,0:T(8,128)(2,1)S(1)}, bf16[4,96,1024]{2,1,0:T(8,128)(2,1)S(1)}, bf16[4,96,1024]{2,1,0:T(8,128)(2,1)S(1)}, bf16[4,96,768]{2,1,0:T(8,128)(2,1)S(1)}) custom-call(s32[1]{0:T(128)} %bitcast.3.first_ref, bf16[272,1024]{1,0:T(8,128)(2,1)} %broadcast_select_fusion.1.refs_0_, ...), custom_call_target="tpu_custom_call" | custom-call | flops 1610612736 | bytes 8388608 | tf_op jit(solution)/shard_map/chunk/pallas_call | solution.py:146
  88.9 3.0 %weight_grads.2 = bf16[4,768,512]{2,1,0:T(8,128)(2,1)S(1)} custom-call(s32[1]{0:T(128)S(6)} %sub.3.half_ref, bf16[4,96,1024]{2,1,0:T(8,128)(2,1)S(1)} %get-tuple-element.100.refs_0_, bf16[4,96,1024]{2,1,0:T(8,128)(2,1)S(1)} %copy-done.12, bf16[4,96,1024]{2,1,0:T(8,128)(2,1)S(1)} %get-tuple-element.102.refs_2_, ...), custom_call_target="tpu_custom_call" | custom-call | flops 1207959552 | bytes 8650752 | tf_op jit(solution)/shard_map/weight_grads/pallas_call | solution.py:224
  91.9 0.1 collective-permute-start.15
  92.0 0.7 collective-permute-start.13
  92.8 0.1 add_convert_fusion.2
  92.8 1.1 collective-permute-start.12
  94.0 6.8 %collective-permute-done.13 = bf16[128,1024]{1,0:T(8,128)(2,1)S(1)} collective-permute-done((bf16[128,1024]{1,0:T(8,128)(2,1)S(1)}, bf16[128,1024]{1,0:T(8,128)(2,1)S(1)}, u32[]{:S(2)}, u32[]{:S(2)}) %collective-permute-start.13) | collective-permute-done | bytes 262176 | tf_op jit(solution)/shard_map/ppermute | solution.py:293
  100.7 0.1 add_convert_fusion.1
  100.8 1.0 collective-permute-start.14
  101.8 10.0 %collective-permute-done.12 = bf16[128,1024]{1,0:T(8,128)(2,1)S(1)} collective-permute-done((bf16[128,1024]{1,0:T(8,128)(2,1)S(1)}, bf16[128,1024]{1,0:T(8,128)(2,1)S(1)}, u32[]{:S(2)}, u32[]{:S(2)}) %collective-permute-start.12) | collective-permute-done | bytes 262176 | tf_op jit(solution)/shard_map/ppermute | solution.py:341
  111.9 6.4 %collective-permute-done.14 = bf16[128,1024]{1,0:T(8,128)(2,1)S(1)} collective-permute-done((bf16[128,1024]{1,0:T(8,128)(2,1)S(1)}, bf16[128,1024]{1,0:T(8,128)(2,1)S(1)}, u32[]{:S(2)}, u32[]{:S(2)}) %collective-permute-start.14) | collective-permute-done | bytes 262176 | tf_op jit(solution)/shard_map/ppermute | solution.py:341
  118.2 1.9 %add_convert_fusion = bf16[128,1024]{1,0:T(8,128)(2,1)} fusion(bf16[128,1024]{1,0:T(8,128)(2,1)S(1)} %collective-permute-done.14, bf16[128,1024]{1,0:T(8,128)(2,1)S(1)} %collective-permute-done.12, bf16[128,1024]{1,0:T(8,128)(2,1)S(1)} %collective-permute-done.10, bf16[128,1024]{1,0:T(8,128)(2,1)S(1)} %copy-done.26, bf16[256,1024]{1,0:T(8,128)(2,1)} %collective-permute-done.9), kind=kLoop, calls=%fused_computation.2 | loop fusion | flops 1310720 | bytes 1572864 | tf_op jit(solution)/shard_map/convert_element_type | solution.py:344
  120.1 3.7 %weight_grads.3 = (bf16[4,512,256]{2,1,0:T(8,128)(2,1)}, bf16[4,512,256]{2,1,0:T(8,128)(2,1)}, bf16[4,256,512]{2,1,0:T(8,128)(2,1)}) custom-call(s32[1]{0:T(128)} %bitcast.4.half_ref, bf16[4,96,1024]{2,1,0:T(8,128)(2,1)S(1)} %get-tuple-element.100.refs_0_, bf16[4,96,1024]{2,1,0:T(8,128)(2,1)S(1)} %copy-done.12, ...), custom_call_target="tpu_custom_call" | custom-call | flops 1207959552 | bytes 8650752 | tf_op jit(solution)/shard_map/weight_grads/pallas_call | solution.py:224
  (41 shorter events, 0.1 us)
Async XLA Ops:
  0.6 1.0 copy-start.23
  1.6 0.9 copy-start.24
  2.5 0.7 copy-start.27
  3.2 0.7 copy-start.28
  3.9 0.7 copy-start.29
  4.7 14.4 %collective-permute-start.2 = (bf16[272,1024]{1,0:T(8,128)(2,1)S(1)}, bf16[272,1024]{1,0:T(8,128)(2,1)S(1)}, u32[]{:S(2)}, u32[]{:S(2)}) collective-permute-start(bf16[272,1024]{1,0:T(8,128)(2,1)S(1)} %pack.1.refs_0_), channel_id=1, source_target_pairs={{0,2},{2,0},{1,3},{3,1},{4,6},{6,4},{5,7},{7,5},{8,10},{10,8},{9,1... | collective-permute-start | bytes 1671176 | tf_op jit(solution)/shard_map/ppermute | solution.py:282
  6.2 16.1 %collective-permute-start.1 = (bf16[272,1024]{1,0:T(8,128)(2,1)S(1)}, bf16[272,1024]{1,0:T(8,128)(2,1)}, u32[]{:S(2)}, u32[]{:S(2)}) collective-permute-start(bf16[272,1024]{1,0:T(8,128)(2,1)S(1)} %pack.1.refs_0_), channel_id=1, source_target_pairs={{8,4},{4,8},{9,5},{5,9},{10,6},{6,10},{11,7},{7,11},{24,20},{20,24... | collective-permute-start | bytes 1671176 | tf_op jit(solution)/shard_map/ppermute | solution.py:302
  9.7 14.0 %collective-permute-start = (bf16[272,1024]{1,0:T(8,128)(2,1)S(1)}, bf16[272,1024]{1,0:T(8,128)(2,1)}, u32[]{:S(2)}, u32[]{:S(2)}) collective-permute-start(bf16[272,1024]{1,0:T(8,128)(2,1)S(1)} %pack.1.refs_0_), channel_id=1, source_target_pairs={{4,0},{0,4},{12,8},{8,12},{5,1},{1,5},{13,9},{9,13},{6,2},{2,6},{1... | collective-permute-start | bytes 1671176 | tf_op jit(solution)/shard_map/ppermute | solution.py:302
  9.8 0.8 copy-start.17
  19.1 0.8 copy-start.19
  23.7 21.3 %collective-permute-start.3 = (bf16[272,1024]{1,0:T(8,128)(2,1)}, bf16[272,1024]{1,0:T(8,128)(2,1)}, u32[]{:S(2)}, u32[]{:S(2)}) collective-permute-start(bf16[272,1024]{1,0:T(8,128)(2,1)} %collective-permute-done.1), channel_id=1, source_target_pairs={{4,0},{8,12},{5,1},{9,13},{6,2},{10,14},{7,3},{11,15},{20,16},{24,... | collective-permute-start | bytes 1671176 | tf_op jit(solution)/shard_map/ppermute | solution.py:302
  26.7 18.3 %collective-permute-start.5 = (bf16[272,1024]{1,0:T(8,128)(2,1)}, bf16[272,1024]{1,0:T(8,128)(2,1)}, u32[]{:S(2)}, u32[]{:S(2)}) collective-permute-start(bf16[272,1024]{1,0:T(8,128)(2,1)} %collective-permute-done.refs_0_), channel_id=1, source_target_pairs={{0,2},{2,0},{1,3},{3,1},{4,6},{6,4},{5,7},{7,5},{8,10},{10,8},{9,1... | collective-permute-start | bytes 1671176 | tf_op jit(solution)/shard_map/ppermute | solution.py:282
  27.2 17.8 %collective-permute-start.4 = (bf16[272,1024]{1,0:T(8,128)(2,1)}, bf16[272,1024]{1,0:T(8,128)(2,1)}, u32[]{:S(2)}, u32[]{:S(2)}) collective-permute-start(bf16[272,1024]{1,0:T(8,128)(2,1)} %collective-permute-done.refs_0_), channel_id=1, source_target_pairs={{8,4},{4,8},{9,5},{5,9},{10,6},{6,10},{11,7},{7,11},{24,20},{20,24... | collective-permute-start | bytes 1671176 | tf_op jit(solution)/shard_map/ppermute | solution.py:302
  30.2 1.6 %copy-start = (bf16[4,1024,256]{2,1,0:T(8,128)(2,1)S(1)}, bf16[4,1024,256]{2,1,0:T(8,128)(2,1)}, u32[]{:S(2)}) copy-start(bf16[4,1024,256]{2,1,0:T(8,128)(2,1)} %refs_2_.7) | copy-start | bytes 6291460
  31.8 1.6 %copy-start.2 = (bf16[4,1024,256]{2,1,0:T(8,128)(2,1)S(1)}, bf16[4,1024,256]{2,1,0:T(8,128)(2,1)}, u32[]{:S(2)}) copy-start(bf16[4,1024,256]{2,1,0:T(8,128)(2,1)} %refs_3_.7) | copy-start | bytes 6291460
  33.4 1.6 %copy-start.6 = (bf16[4,256,1024]{2,1,0:T(8,128)(2,1)S(1)}, bf16[4,256,1024]{2,1,0:T(8,128)(2,1)}, u32[]{:S(2)}) copy-start(bf16[4,256,1024]{2,1,0:T(8,128)(2,1)} %refs_4_.7) | copy-start | bytes 6291460
  35.0 1.1 copy-start.18
  36.0 1.1 copy-start.20
  37.1 13.4 %copy-start.1 = (bf16[4,1024,256]{2,1,0:T(8,128)(2,1)S(1)}, bf16[4,1024,256]{2,1,0:T(8,128)(2,1)}, u32[]{:S(2)}) copy-start(bf16[4,1024,256]{2,1,0:T(8,128)(2,1)} %refs_2_.7) | copy-start | bytes 6291460
  42.7 0.9 copy-start.9
  43.6 0.7 copy-start.21
  44.3 0.7 copy-start.25
  46.9 17.0 %collective-permute-start.7 = (bf16[272,1024]{1,0:T(8,128)(2,1)}, bf16[272,1024]{1,0:T(8,128)(2,1)}, u32[]{:S(2)}, u32[]{:S(2)}) collective-permute-start(bf16[272,1024]{1,0:T(8,128)(2,1)} %broadcast_select_fusion.refs_0_), channel_id=1, source_target_pairs={{0,2},{2,0},{1,3},{3,1},{4,6},{6,4},{5,7},{7,5},{8,10},{10,8},{9,1... | collective-permute-start | bytes 1671176 | tf_op jit(solution)/shard_map/ppermute | solution.py:282
  48.4 15.5 %collective-permute-start.6 = (bf16[272,1024]{1,0:T(8,128)(2,1)}, bf16[272,1024]{1,0:T(8,128)(2,1)}, u32[]{:S(2)}, u32[]{:S(2)}) collective-permute-start(bf16[272,1024]{1,0:T(8,128)(2,1)} %collective-permute-done.4), channel_id=1, source_target_pairs={{4,0},{8,12},{5,1},{9,13},{6,2},{10,14},{7,3},{11,15},{20,16},{24,... | collective-permute-start | bytes 1671176 | tf_op jit(solution)/shard_map/ppermute | solution.py:302
  50.5 1.6 %copy-start.3 = (bf16[4,1024,256]{2,1,0:T(8,128)(2,1)S(1)}, bf16[4,1024,256]{2,1,0:T(8,128)(2,1)}, u32[]{:S(2)}) copy-start(bf16[4,1024,256]{2,1,0:T(8,128)(2,1)} %refs_3_.7) | copy-start | bytes 6291460
  52.1 1.6 %copy-start.7 = (bf16[4,256,1024]{2,1,0:T(8,128)(2,1)S(1)}, bf16[4,256,1024]{2,1,0:T(8,128)(2,1)}, u32[]{:S(2)}) copy-start(bf16[4,256,1024]{2,1,0:T(8,128)(2,1)} %refs_4_.7) | copy-start | bytes 6291460
  61.3 0.9 copy-start.11
  62.2 0.9 copy-start.13
  63.1 0.8 copy-start.15
  65.9 13.0 %collective-permute-start.8 = (bf16[272,1024]{1,0:T(8,128)(2,1)}, bf16[272,1024]{1,0:T(8,128)(2,1)}, u32[]{:S(2)}, u32[]{:S(2)}) collective-permute-start(bf16[272,1024]{1,0:T(8,128)(2,1)} %broadcast_select_fusion.1.refs_0_), channel_id=1, source_target_pairs={{0,2},{2,0},{1,3},{3,1},{4,6},{6,4},{5,7},{7,5},{8,10},{10,8},{9,1... | collective-permute-start | bytes 1671176 | tf_op jit(solution)/shard_map/ppermute | solution.py:282
  66.4 11.4 %collective-permute-start.9 = (bf16[256,1024]{1,0:T(8,128)(2,1)}, bf16[256,1024]{1,0:T(8,128)(2,1)}, u32[]{:S(2)}, u32[]{:S(2)}) collective-permute-start(bf16[256,1024]{1,0:T(8,128)(2,1)} %get-tuple-element.89), channel_id=1, source_target_pairs={{0,4},{4,0},{8,12},{12,8},{1,5},{5,1},{9,13},{13,9},{2,6},{6,2},{1... | collective-permute-start | bytes 1572872 | tf_op jit(solution)/shard_map/ppermute | solution.py:311
  66.4 1.6 %copy-start.4 = (bf16[4,1024,256]{2,1,0:T(8,128)(2,1)S(1)}, bf16[4,1024,256]{2,1,0:T(8,128)(2,1)}, u32[]{:S(2)}) copy-start(bf16[4,1024,256]{2,1,0:T(8,128)(2,1)} %refs_3_.7) | copy-start | bytes 6291460
  68.0 1.6 %copy-start.8 = (bf16[4,256,1024]{2,1,0:T(8,128)(2,1)S(1)}, bf16[4,256,1024]{2,1,0:T(8,128)(2,1)}, u32[]{:S(2)}) copy-start(bf16[4,256,1024]{2,1,0:T(8,128)(2,1)} %refs_4_.7) | copy-start | bytes 6291460
  69.6 9.7 %copy-start.22 = (bf16[128,1024]{1,0:T(8,128)(2,1)S(1)}, bf16[128,1024]{1,0:T(8,128)(2,1)}, u32[]{:S(2)}) copy-start(bf16[128,1024]{1,0:T(8,128)(2,1)} %copy-done.21) | copy-start | bytes 786436
  69.6 12.4 %copy-start.5 = (bf16[4,1024,256]{2,1,0:T(8,128)(2,1)S(1)}, bf16[4,1024,256]{2,1,0:T(8,128)(2,1)}, u32[]{:S(2)}) copy-start(bf16[4,1024,256]{2,1,0:T(8,128)(2,1)} %refs_3_.7) | copy-start | bytes 6291460
  78.9 13.1 %collective-permute-start.11 = (bf16[128,1024]{1,0:T(8,128)(2,1)S(1)}, bf16[128,1024]{1,0:T(8,128)(2,1)S(1)}, u32[]{:S(2)}, u32[]{:S(2)}) collective-permute-start(bf16[128,1024]{1,0:T(8,128)(2,1)S(1)} %get-tuple-element.99), channel_id=1, source_target_pairs={{2,0},{0,2},{3,1},{1,3},{6,4},{4,6},{7,5},{5,7},{10,8},{8,10},{11,... | collective-permute-start | bytes 786440 | tf_op jit(solution)/shard_map/ppermute | solution.py:293
  80.3 8.6 %copy-start.10 = (bf16[4,96,1024]{2,1,0:T(8,128)(2,1)S(1)}, bf16[4,96,1024]{2,1,0:T(8,128)(2,1)}, u32[]{:S(2)}) copy-start(bf16[4,96,1024]{2,1,0:T(8,128)(2,1)} %copy-done.9) | copy-start | bytes 2359300
  80.3 8.6 %copy-start.12 = (bf16[4,96,1024]{2,1,0:T(8,128)(2,1)S(1)}, bf16[4,96,1024]{2,1,0:T(8,128)(2,1)}, u32[]{:S(2)}) copy-start(bf16[4,96,1024]{2,1,0:T(8,128)(2,1)} %copy-done.11) | copy-start | bytes 2359300
  80.3 8.6 %copy-start.14 = (bf16[4,96,1024]{2,1,0:T(8,128)(2,1)S(1)}, bf16[4,96,1024]{2,1,0:T(8,128)(2,1)}, u32[]{:S(2)}) copy-start(bf16[4,96,1024]{2,1,0:T(8,128)(2,1)} %copy-done.13) | copy-start | bytes 2359300
  80.3 8.6 %copy-start.16 = (bf16[4,96,768]{2,1,0:T(8,128)(2,1)S(1)}, bf16[4,96,768]{2,1,0:T(8,128)(2,1)}, u32[]{:S(2)}) copy-start(bf16[4,96,768]{2,1,0:T(8,128)(2,1)} %copy-done.15) | copy-start | bytes 1769476
  80.3 11.6 %collective-permute-start.10 = (bf16[128,1024]{1,0:T(8,128)(2,1)S(1)}, bf16[128,1024]{1,0:T(8,128)(2,1)S(1)}, u32[]{:S(2)}, u32[]{:S(2)}) collective-permute-start(bf16[128,1024]{1,0:T(8,128)(2,1)S(1)} %add_convert_fusion.3), channel_id=1, source_target_pairs={{2,0},{0,2},{3,1},{1,3},{6,4},{4,6},{7,5},{5,7},{10,8},{8,10},{11,... | collective-permute-start | bytes 786440 | tf_op jit(solution)/shard_map/ppermute | solution.py:293
  88.9 29.3 %copy-start.26 = (bf16[128,1024]{1,0:T(8,128)(2,1)S(1)}, bf16[128,1024]{1,0:T(8,128)(2,1)}, u32[]{:S(2)}) copy-start(bf16[128,1024]{1,0:T(8,128)(2,1)} %copy-done.25) | copy-start | bytes 786436
  91.9 28.2 %collective-permute-start.15 = (bf16[4,768,512]{2,1,0:T(8,128)(2,1)S(1)}, bf16[4,768,512]{2,1,0:T(8,128)(2,1)S(1)}, u32[]{:S(2)}, u32[]{:S(2)}) collective-permute-start(bf16[4,768,512]{2,1,0:T(8,128)(2,1)S(1)} %weight_grads.2), channel_id=1, source_target_pairs={{0,1},{1,0},{2,3},{3,2},{4,5},{5,4},{6,7},{7,6},{8,9},{9,8},{10,11... | collective-permute-start | bytes 9437192 | tf_op jit(solution)/shard_map/ppermute | solution.py:331
  92.0 8.7 %collective-permute-start.13 = (bf16[128,1024]{1,0:T(8,128)(2,1)S(1)}, bf16[128,1024]{1,0:T(8,128)(2,1)S(1)}, u32[]{:S(2)}, u32[]{:S(2)}) collective-permute-start(bf16[128,1024]{1,0:T(8,128)(2,1)S(1)} %get-tuple-element.114), channel_id=1, source_target_pairs={{2,0},{0,2},{3,1},{1,3},{6,4},{4,6},{7,5},{5,7},{10,8},{8,10},{11,... | collective-permute-start | bytes 786440 | tf_op jit(solution)/shard_map/ppermute | solution.py:293
  92.8 19.0 %collective-permute-start.12 = (bf16[128,1024]{1,0:T(8,128)(2,1)S(1)}, bf16[128,1024]{1,0:T(8,128)(2,1)S(1)}, u32[]{:S(2)}, u32[]{:S(2)}) collective-permute-start(bf16[128,1024]{1,0:T(8,128)(2,1)S(1)} %add_convert_fusion.2), channel_id=1, source_target_pairs={{0,8},{4,12},{8,0},{12,4},{1,9},{5,13},{9,1},{13,5},{2,10},{6,14},... | collective-permute-start | bytes 786440 | tf_op jit(solution)/shard_map/ppermute | solution.py:341
  100.8 17.4 %collective-permute-start.14 = (bf16[128,1024]{1,0:T(8,128)(2,1)S(1)}, bf16[128,1024]{1,0:T(8,128)(2,1)S(1)}, u32[]{:S(2)}, u32[]{:S(2)}) collective-permute-start(bf16[128,1024]{1,0:T(8,128)(2,1)S(1)} %add_convert_fusion.1), channel_id=1, source_target_pairs={{0,12},{4,8},{8,4},{12,0},{1,13},{5,9},{9,5},{13,1},{2,14},{6,10},... | collective-permute-start | bytes 786440 | tf_op jit(solution)/shard_map/ppermute | solution.py:341

commit v3 on v1

--- a/solution.py
+++ b/solution.py
@@ -8,12 +8,15 @@
 from jax.sharding import PartitionSpec as P
 
 GROUPS_TOK = 4
-ROUTE_ROWS = 16
-VMEM_LIMIT = 48 * 1024 * 1024
+VMEM_LIMIT = 24 * 1024 * 1024
 
 
 def dot(a, b, contract):
     return lax.dot_general(a, b, ((contract[:1], contract[1:]), ((), ())), preferred_element_type=jnp.float32)
+
+
+def in_hbm(v):
+    return pltpu.with_memory_space_constraint(v, pltpu.HBM)
 
 
 def gated_parts(pre_gate):
@@ -25,27 +28,29 @@
     return z ^ k if size & (size - 1) == 0 else (k - z) % size
 
 
-def route_keys(route, first_expert, local_experts, capacity, rows, offset, tok_rows, per_group):
-    expert = route[0:1, :].astype(jnp.int32) - first_expert
-    slot = route[1:2, :].astype(jnp.int32)
-    gate = (route[2:3, :] * 256.0 + route[3:4, :]) / 65536.0
+def route_keys(route, first_expert, local_experts, capacity, rows, offset, top_count, per_group):
+    expert = route[:top_count] - first_expert
+    slot = route[top_count : 2 * top_count]
+    gate = route[2 * top_count :].astype(jnp.float32) / 65536.0
     valid = (expert >= 0) & (expert < local_experts) & (slot < capacity)
     key = jnp.where(valid, expert * rows + offset + slot, -1)
     gate = jnp.where(valid, gate, 0.0)
-    width = tok_rows * per_group
-    key_out, gate_out = key[:, :width], gate[:, :width]
-    for j in range(1, route.shape[1] // width):
-        key_out = jnp.maximum(key_out, key[:, j * width : (j + 1) * width])
-        gate_out = jnp.maximum(gate_out, gate[:, j * width : (j + 1) * width])
-    return key_out, gate_out
-
-
-def chunk_kernel(n_blocks, tok_rows, capacity, rows, per_group, first_ref, *refs):
-    payloads = refs[:n_blocks]
-    w_gate, w_up, w_down = refs[n_blocks : n_blocks + 3]
-    parts = refs[n_blocks + 3 : 2 * n_blocks + 3]
-    x_out, s_out, h_out = refs[2 * n_blocks + 3 : 2 * n_blocks + 6]
-    x_all, u_all, key_all, gate_all, hot_all, back_all = refs[2 * n_blocks + 6 :]
+    pairs = []
+    for i in range(per_group):
+        key_out, gate_out = key[i : i + 1, :], gate[i : i + 1, :]
+        for j in range(i + per_group, top_count, per_group):
+            key_out = jnp.maximum(key_out, key[j : j + 1, :])
+            gate_out = jnp.maximum(gate_out, gate[j : j + 1, :])
+        pairs.append((key_out, gate_out))
+    return pairs
+
+
+def chunk_kernel(n_blocks, tok_rows, capacity, rows, top_count, per_group, where_ref, *refs):
+    tokens, upstream, routes = (refs[i * n_blocks : (i + 1) * n_blocks] for i in range(3))
+    w_gate, w_up, w_down = refs[3 * n_blocks : 3 * n_blocks + 3]
+    n_parts = len(refs) - 3 * n_blocks - 12
+    parts = refs[3 * n_blocks + 3 : 3 * n_blocks + 3 + n_parts]
+    x_out, s_out, h_out, x_all, u_all, key_all, gate_all, hot_all, back_all = refs[-9:]
     e = pl.program_id(0)
     local_experts = pl.num_programs(0)
     n_tok = n_blocks * tok_rows
@@ -55,16 +60,14 @@
     def _():
         for b in range(n_blocks):
             rows_b = slice(b * tok_rows, (b + 1) * tok_rows)
-            x_all[rows_b, :] = payloads[b][:tok_rows, :]
-            u_all[rows_b, :] = payloads[b][tok_rows : 2 * tok_rows, :]
-            route = payloads[b][2 * tok_rows : 2 * tok_rows + ROUTE_ROWS, :].astype(jnp.float32)
-            key, gate = route_keys(
-                route, first_ref[0], local_experts, capacity, rows, b * capacity, tok_rows, per_group
+            x_all[rows_b, :] = tokens[b][0]
+            u_all[rows_b, :] = upstream[b][0]
+            pairs = route_keys(
+                routes[b][0], where_ref[0], local_experts, capacity, rows, b * capacity, top_count, per_group
             )
-            for i in range(per_group):
-                cols = slice(i * tok_rows, (i + 1) * tok_rows)
-                key_all[i : i + 1, rows_b] = key[:, cols]
-                gate_all[i : i + 1, rows_b] = gate[:, cols]
+            for i, (key, gate) in enumerate(pairs):
+                key_all[i : i + 1, rows_b] = key
+                gate_all[i : i + 1, rows_b] = gate
 
     place = lax.broadcasted_iota(jnp.int32, (rows, n_tok), 0) + e * rows
     hot = jnp.zeros((rows, n_tok), jnp.float32)
@@ -96,25 +99,32 @@
     @pl.when(e == local_experts - 1)
     def _():
         summed = dot(hot_all[...], back_all[...], (0, 0)).astype(jnp.bfloat16)
-        for b in range(n_blocks):
-            parts[b][...] = summed[b * tok_rows : (b + 1) * tok_rows, :]
-
-
-def chunk_call(payloads, first_expert, w_gate, w_up, w_down, tok_rows, capacity, rows, per_group):
-    n_blocks = len(payloads)
+        start = 0
+        for part in parts:
+            part[...] = summed[start : start + part.shape[0], :]
+            start += part.shape[0]
+
+
+def chunk_call(tokens, upstream, routes, where, weights, capacity, rows, per_group, joined):
+    n_blocks = where.shape[0] - 1
+    tok_rows, width = tokens.shape[1:]
+    top_count = routes.shape[1] // 3
     n_tok = n_blocks * tok_rows
-    experts, width, ff = w_gate.shape
-    whole = lambda shape: pl.BlockSpec(shape, lambda e, first: (0, 0))
-    per_expert = lambda shape: pl.BlockSpec((1,) + shape, lambda e, first: (e, 0, 0))
-    flops = 2 * experts * rows * width * (5 * ff + 3 * n_tok)
+    experts, _, ff = weights[0].shape
+    part_shapes = [(n_tok, width)] if joined else [(tok_rows, width), (n_tok - tok_rows, width)]
+    whole = lambda shape: pl.BlockSpec(shape, lambda e, where: (0, 0))
+    per_expert = lambda shape: pl.BlockSpec((1,) + shape, lambda e, where: (e, 0, 0))
+    picked = lambda shape: [
+        pl.BlockSpec((1,) + shape[1:], lambda e, where, b=b: (where[b + 1], 0, 0)) for b in range(n_blocks)
+    ]
     return pl.pallas_call(
-        functools.partial(chunk_kernel, n_blocks, tok_rows, capacity, rows, per_group),
+        functools.partial(chunk_kernel, n_blocks, tok_rows, capacity, rows, top_count, per_group),
         grid_spec=pltpu.PrefetchScalarGridSpec(
             num_scalar_prefetch=1,
             grid=(experts,),
-            in_specs=[whole(payloads[0].shape)] * n_blocks
+            in_specs=picked(tokens.shape) + picked(upstream.shape) + picked(routes.shape)
             + [per_expert((width, ff)), per_expert((width, ff)), per_expert((ff, width))],
-            out_specs=[whole((tok_rows, width))] * n_blocks
+            out_specs=[whole(shape) for shape in part_shapes]
             + [per_expert((rows, width)), per_expert((rows, width)), per_expert((rows, 3 * ff))],
             scratch_shapes=[
                 pltpu.VMEM((n_tok, width), jnp.bfloat16),
@@ -125,7 +135,7 @@
                 pltpu.VMEM((experts * rows, width), jnp.bfloat16),
             ],
         ),
-        out_shape=[jax.ShapeDtypeStruct((tok_rows, width), jnp.bfloat16)] * n_blocks
+        out_shape=[jax.ShapeDtypeStruct(shape, jnp.bfloat16) for shape in part_shapes]
         + [
             jax.ShapeDtypeStruct((experts, rows, width), jnp.bfloat16),
             jax.ShapeDtypeStruct((experts, rows, width), jnp.bfloat16),
@@ -133,10 +143,12 @@
         ],
         compiler_params=pltpu.CompilerParams(vmem_limit_bytes=VMEM_LIMIT),
         cost_estimate=pl.CostEstimate(
-            flops=flops, bytes_accessed=6 * experts * width * ff + 8 * n_tok * width, transcendentals=0
+            flops=2 * experts * rows * width * (5 * ff + 3 * n_tok),
+            bytes_accessed=6 * experts * width * ff + 8 * n_tok * width,
+            transcendentals=0,
         ),
         name="chunk",
-    )(first_expert, *payloads, w_gate, w_up, w_down)
+    )(where, *[in_hbm(v) for v in (tokens, upstream, routes) for _ in range(n_blocks)], *weights)
 
 
 def halves_of(n, ff, refs):
@@ -212,56 +224,63 @@
     capacity = max(2, 3 * tok_rows * top_count // (2 * experts_all))
     rows = -(-n_ingroup * capacity // 16) * 16
     z, x, core = (lax.axis_index(a) for a in ("group", "ingroup", "dp"))
-    first_expert = ((z * n_ingroup + x) * local_experts).astype(jnp.int32).reshape(1)
-
-    route = jnp.stack([expert_ids.T, slots.T, (gate_fixed // 256).T, (gate_fixed % 256).T])
-    route = route.reshape(-1, width).astype(jnp.bfloat16)
-    route = jnp.pad(route, ((0, ROUTE_ROWS - route.shape[0]), (0, 0)))
-    own = jnp.concatenate([tokens, upstream, route], axis=0)
-
-    ups, downs = {0: own}, {0: own}
-    for s in range(1, n_group):
-        ups[s] = lax.ppermute(ups[s - 1], "group", [(i, i + 1) for i in range(s - 1, n_group - 1)])
-        downs[s] = lax.ppermute(downs[s - 1], "group", [(i, i - 1) for i in range(1, n_group - s + 1)])
-
-    chunks = []
-    for k in range(n_group):
-        if k == 0:
-            column = own
-        else:
-            offsets = [i - partner(i, k, n_group) for i in range(n_group)]
-            kinds = sorted(set(offsets))
-            column = None
-            for off in kinds:
-                case = ups[off] if off >= 0 else downs[-off]
-                picks = functools.reduce(jnp.logical_or, [z == i for i in range(n_group) if offsets[i] == off])
-                column = case if column is None else jnp.where(picks, case, column)
-        blocks = [column] + [
-            lax.ppermute(column, "ingroup", [(i, (i + s) % n_ingroup) for i in range(n_ingroup)])
+    first_expert = (z * n_ingroup + x) * local_experts
+    weights = [in_hbm(w) for w in (w_gate, w_up, w_down)]
+    wide = lambda v: v.astype(jnp.float32)
+    tie = lambda *trees: lax.optimization_barrier(trees)
+    swap = lambda k: [(i, partner(i, k, n_group)) for i in range(n_group)]
+
+    gather = lambda v: lax.all_gather(v, ("group", "ingroup"))
+    routes = gather(jnp.concatenate([expert_ids.T, slots.T, gate_fixed.T], axis=0))
+    tokens, upstream = gather(tokens), gather(upstream)
+
+    def chunk(k):
+        column = partner(z, k, n_group) * n_ingroup
+        where = [first_expert] + [column + (x - s) % n_ingroup for s in range(n_ingroup)]
+        where = jnp.stack(where).astype(jnp.int32)
+        return chunk_call(tokens, upstream, routes, where, weights, capacity, rows, per_group, k == 1)
+
+    def across(others):
+        return [
+            lax.ppermute(
+                others[(s - 1) * tok_rows : s * tok_rows], "ingroup", [(i, (i - s) % n_ingroup) for i in range(n_ingroup)]
+            )
             for s in range(1, n_ingroup)
         ]
-        chunks.append(
-            chunk_call(blocks, first_expert, w_gate, w_up, w_down, tok_rows, capacity, rows, per_group)
-        )
-
-    x_rows, s_rows, hids = ([c[n_ingroup + i] for c in chunks] for i in range(3))
+
+    def homeward(k):
+        group_part = wide(chunks[k][0])
+        for back in backs[k]:
+            group_part = group_part + wide(back)
+        return lax.ppermute(group_part.astype(jnp.bfloat16), "group", swap(k))
+
+    chunks, backs, sent = {}, {}, {}
+    chunks[1] = chunk(1)
+    chunks[1], tokens = tie(chunks[1], tokens)
+    near = lax.ppermute(chunks[1][0], "group", swap(1))
+    for k in range(2, n_group):
+        chunks[k] = chunk(k)
+        if k > 2:
+            chunks[k], backs[k - 1], tokens = tie(chunks[k], backs[k - 1], tokens)
+            sent[k - 1] = homeward(k - 1)
+        else:
+            chunks[k], tokens = tie(chunks[k], tokens)
+        backs[k] = across(chunks[k][1])
+    chunks[0] = chunk(0)
+    last = n_group - 1
+    chunks[0], near, backs[last] = tie(chunks[0], near, backs[last])
+    backs[0] = across((wide(chunks[0][1]) + wide(near[tok_rows:])).astype(jnp.bfloat16))
+    sent[last] = homeward(last)
+
+    x_rows, s_rows, hids = ([chunks[k][i] for k in range(n_group)] for i in (-3, -2, -1))
     half = core.astype(jnp.int32).reshape(1)
     to_send = weight_call(1 - half, x_rows, s_rows, hids)
     got = lax.ppermute(to_send, "dp", [(0, 1), (1, 0)])
-
-    total = jnp.zeros((tok_rows, width), jnp.float32)
-    for k in range(n_group):
-        parts = chunks[k][:n_ingroup]
-        group_part = parts[0].astype(jnp.float32)
-        for s in range(1, n_ingroup):
-            back = lax.ppermute(parts[s], "ingroup", [(i, (i - s) % n_ingroup) for i in range(n_ingroup)])
-            group_part = group_part + back.astype(jnp.float32)
-        group_part = group_part.astype(jnp.bfloat16)
-        if k > 0:
-            group_part = lax.ppermute(
-                group_part, "group", [(i, partner(i, k, n_group)) for i in range(n_group)]
-            )
-        total = total + group_part.astype(jnp.float32)
+    total = wide(chunks[0][0]) + wide(near[:tok_rows])
+    for back in backs[0]:
+        total = total + wide(back)
+    for k in range(2, n_group):
+        total = total + wide(sent[k])
     grad_tokens = total.astype(jnp.bfloat16)
 
     grad_gate, grad_up, grad_down = weight_call(half, x_rows, s_rows, hids, got)

time: 148 us -> 196 us (1.32); the launches traced: 147 us -> 192 us
  blocking collectives: 0 us -> 34.4 us
  starting transfers between devices: 31.9 us -> 7.32 us
  waiting for transfers between devices: 61.9 us -> 85.1 us
  between operations: 0.83 us -> 14.2 us
  other arithmetic: 7.91 us -> 4.92 us
    all_gather x0 -> x2, waiting for transfers between devices: none -> 68.5 us  [per_device(): gather = lambda v: lax.all_gather(v, ('group', 'ingroup'))]
    ppermute x17 -> x6, waiting for transfers between devices: 61.9 us -> 15.2 us  [the longest x2 15.2 us: homeward(): return lax.ppermute(group_part.astype(jnp.bfloat16), 'group', swap(k))]
    all_gather x0 -> x1, blocking collectives: none -> 34.4 us  [per_device(): gather = lambda v: lax.all_gather(v, ('group', 'ingroup'))]
    ppermute x17 -> x6, starting transfers between devices: 31.9 us -> 7.17 us  [the longest x2 3.04 us: homeward(): return lax.ppermute(group_part.astype(jnp.bfloat16), 'group', swap(k))]
    pallas_call x4, Pallas kernels: 28.5 us -> 34.4 us  [chunk_call(): pl.pallas_call(functools.partial(chunk_kernel, n_blocks, tok_rows, capaci...]
    pallas_call x2, Pallas kernels: 10.8 us -> 6.7 us  [weight_call(): pl.pallas_call(functools.partial(kernel, n, ff), grid_spec=pltpu.Prefetch...]
    select_n x2 -> x0, other arithmetic: 3.61 us -> none  [per_device(): column = case if column is None else jnp.where(picks, case, column)]
    unnamed x3 -> x0, other arithmetic: 2.08 us -> none
  transfers between devices with their start and end apart: 18 -> 9, of which waited for: 11 -> 3; matrix products, arithmetic and copies ran while one was open for 3% -> 3% of each run, Pallas kernels for 14% -> 13%
where the time goes in v3:
time: 196 us; the launch traced here: 192 us
  waiting for transfers between devices  85.1 us (43%)
  Pallas kernels  41.1 us (21%)
  blocking collectives  34.4 us (18%)
  between operations  14.2 us (7%)
  starting transfers between devices  7.32 us (4%)
  other arithmetic  4.92 us (3%)
  local copies, waits for them, and re-layouts  4.86 us (2%)
    all_gather x2, waiting for transfers between devices, per_device(): gather = lambda v: lax.all_gather(v, ('group', 'ingroup'))  68.5 us
    all_gather x1, blocking collectives, per_device(): gather = lambda v: lax.all_gather(v, ('group', 'ingroup'))  34.4 us
    pallas_call x4, Pallas kernels, chunk_call(): pl.pallas_call(functools.partial(chunk_kernel, n_blocks, tok_rows, capaci...  34.4 us
    ppermute x2, waiting for transfers between devices, homeward(): return lax.ppermute(group_part.astype(jnp.bfloat16), 'group', swap(k))  15.2 us
    pallas_call x2, Pallas kernels, weight_call(): pl.pallas_call(functools.partial(kernel, n, ff), grid_spec=pltpu.Prefetch...  6.7 us
    unnamed x28, local copies, waits for them, and re-layouts  4.86 us
  transfers between devices with their start and end apart: 9, of which 3 were waited for; matrix products, arithmetic and copies ran while one was open for 3% of the time, Pallas kernels for 13%

profile of v3, /device:TPU:0, one launch (start us, length us, event | category | flops | bytes accessed | tf_op | source)
XLA Modules:
  0.0 192.0 jit_solution(2927677348175931658)
XLA Ops:
  7.2 0.0 all-gather.6.cloned.1.call-start
  7.2 0.7 all-gather.6.cloned.1.call-update
  7.9 0.0 all-gather.8.cloned.1.call-start
  7.9 0.7 all-gather.8.cloned.1.call-update
  8.7 0.7 pad_add_fusion
  9.4 34.4 %all-gather.2 = s32[192,128]{1,0:T(8,128)} all-gather(s32[24,128]{1,0:T(8,128)S(1)} %pad_add_fusion), channel_id=4, replica_groups=mesh['parts'=2,'group'=4,'ingroup'=2,'dp'=2] {'group','ingroup'}, dimensions={0}, use_global_device_ids=true | all-gather | bytes 110592 | tf_op jit(solution)/shard_map/all_gather | solution.py:233
  43.9 0.1 pad_add_fusion.3.where_ref
  43.9 0.1 pad_add_fusion.4.where_ref
  44.0 18.5 %all-gather.6.cloned.1.call-done = bf16[1024,1024]{1,0:T(8,128)(2,1)} async-done(((bf16[128,1024]{1,0:T(8,128)(2,1)}), bf16[1024,1024]{1,0:T(8,128)(2,1)}) %all-gather.6.cloned.1.call-update) | async-done | bytes 2097168 | tf_op jit(solution)/shard_map/all_gather | solution.py:233
  62.5 50.0 %all-gather.8.cloned.1.call-done = bf16[1024,1024]{1,0:T(8,128)(2,1)} async-done(((bf16[128,1024]{1,0:T(8,128)(2,1)}), bf16[1024,1024]{1,0:T(8,128)(2,1)}) %all-gather.8.cloned.1.call-update) | async-done | bytes 2097168 | tf_op jit(solution)/shard_map/all_gather | solution.py:233
  112.5 8.9 %chunk.4 = (bf16[256,1024]{1,0:T(8,128)(2,1)}, bf16[4,96,1024]{2,1,0:T(8,128)(2,1)S(1)}, bf16[4,96,1024]{2,1,0:T(8,128)(2,1)S(1)}, bf16[4,96,768]{2,1,0:T(8,128)(2,1)S(1)}) custom-call(s32[3]{0:T(128)S(1)} %pad_add_fusion.4.where_ref, bf16[8,128,1024]{2,1,0:T(8,128)(2,1)} %bitcast.16, bf16[8,128,1024]{2,1,0:T(8,128)(2,1)} %bitcast.17, ...), custom_call_target="tpu_custom_call" | custom-call | flops 1610612736 | bytes 8388608 | tf_op jit(solution)/shard_map/chunk/pallas_call | solution.py:120
  121.4 0.0 copy-start.4
  121.4 1.5 collective-permute-start.1
  122.9 8.2 %chunk.5 = (bf16[128,1024]{1,0:T(8,128)(2,1)S(1)}, bf16[128,1024]{1,0:T(8,128)(2,1)S(1)}, bf16[4,96,1024]{2,1,0:T(8,128)(2,1)S(1)}, bf16[4,96,1024]{2,1,0:T(8,128)(2,1)S(1)}, bf16[4,96,768]{2,1,0:T(8,128)(2,1)S(1)}) custom-call(s32[3]{0:T(128)S(1)} %pad_add_fusion.3.where_ref, bf16[8,128,1024]{2,1,0:T(8,128)(2,1)} %bitcast.18, ...), custom_call_target="tpu_custom_call" | custom-call | flops 1610612736 | bytes 8388608 | tf_op jit(solution)/shard_map/chunk/pallas_call | solution.py:120
  131.1 0.0 copy-done.4
  131.1 0.0 copy-start.6
  131.1 0.8 copy-done.6
  131.9 0.6 collective-permute-start
  132.5 0.1 pad_add_fusion.1
  132.6 8.8 %chunk.6 = (bf16[128,1024]{1,0:T(8,128)(2,1)S(1)}, bf16[128,1024]{1,0:T(8,128)(2,1)}, bf16[4,96,1024]{2,1,0:T(8,128)(2,1)S(1)}, bf16[4,96,1024]{2,1,0:T(8,128)(2,1)S(1)}, bf16[4,96,768]{2,1,0:T(8,128)(2,1)S(1)}) custom-call(s32[3]{0:T(128)S(1)} %get-tuple-element.99.where_ref, bf16[8,128,1024]{2,1,0:T(8,128)(2,1)} %bitcast.20, ...), custom_call_target="tpu_custom_call" | custom-call | flops 1610612736 | bytes 8388608 | tf_op jit(solution)/shard_map/chunk/pallas_call | solution.py:120
  141.4 0.0 copy-start
  141.4 0.9 copy-done
  142.3 0.0 copy-start.2
  142.3 0.9 copy-done.2
  143.2 0.0 copy-start.8
  143.2 0.8 copy-done.8
  144.0 0.0 copy-start.10
  144.0 0.7 copy-done.10
  144.7 0.0 collective-permute-done
  144.7 0.0 copy-start.12
  144.7 0.7 copy-done.12
  145.4 1.5 collective-permute-start.2
  146.9 0.0 copy-start.1
  146.9 0.0 copy-start.3
  146.9 0.0 copy-start.5
  146.9 0.0 copy-start.7
  146.9 0.0 copy-start.9
  146.9 8.5 %chunk.7 = (bf16[128,1024]{1,0:T(8,128)(2,1)S(1)}, bf16[128,1024]{1,0:T(8,128)(2,1)S(1)}, bf16[4,96,1024]{2,1,0:T(8,128)(2,1)S(1)}, bf16[4,96,1024]{2,1,0:T(8,128)(2,1)S(1)}, bf16[4,96,768]{2,1,0:T(8,128)(2,1)S(1)}) custom-call(s32[3]{0:T(128)S(1)} %get-tuple-element.98.where_ref, bf16[8,128,1024]{2,1,0:T(8,128)(2,1)} %bitcast.22, ...), custom_call_target="tpu_custom_call" | custom-call | flops 1610612736 | bytes 8388608 | tf_op jit(solution)/shard_map/chunk/pallas_call | solution.py:120
  155.4 0.0 collective-permute-done.1
  155.4 0.0 collective-permute-done.2
  155.4 0.0 copy-done.1
  155.4 0.0 copy-done.3
  155.4 0.0 copy-done.5
  155.4 0.0 copy-done.7
  155.5 0.0 copy-done.9
  155.5 0.0 copy-start.13
  155.5 0.0 copy-start.11
  155.5 3.0 %weight_grads.2 = bf16[4,768,512]{2,1,0:T(8,128)(2,1)S(1)} custom-call(s32[1]{0:T(128)S(6)} %sub.10.half_ref, bf16[4,96,1024]{2,1,0:T(8,128)(2,1)S(1)} %get-tuple-element.83.refs_0_, bf16[4,96,1024]{2,1,0:T(8,128)(2,1)S(1)} %get-tuple-element.84.refs_1_, bf16[4,96,1024]{2,1,0:T(8,128)(2,1)S(1)} %get-tuple-element.85.refs_2_, ...), custom_call_target="tpu_custom_call" | custom-call | flops 1207959552 | bytes 8650752 | tf_op jit(solution)/shard_map/weight_grads/pallas_call | solution.py:200
  158.5 0.1 collective-permute-start.6
  158.6 0.0 copy-done.13
  158.6 0.1 add_convert_fusion.2
  158.6 1.0 collective-permute-start.4
  159.6 1.0 add_convert_fusion.3
  160.6 0.6 collective-permute-start.3
  161.2 0.0 copy-done.11
  161.2 1.0 add_convert_fusion.1
  162.3 2.1 %collective-permute-start.5 = (bf16[128,1024]{1,0:T(8,128)(2,1)S(1)}, bf16[128,1024]{1,0:T(8,128)(2,1)S(1)}, u32[]{:S(2)}, u32[]{:S(2)}) collective-permute-start(bf16[128,1024]{1,0:T(8,128)(2,1)S(1)} %add_convert_fusion.1), channel_id=1, source_target_pairs={{0,12},{4,8},{8,4},{12,0},{1,13},{5,9},{9,5},{13,1},{2,14},{6,10},... | collective-permute-start | bytes 786440 | tf_op jit(solution)/shard_map/ppermute | solution.py:255
  164.3 15.2 %collective-permute-done.4 = bf16[128,1024]{1,0:T(8,128)(2,1)S(1)} collective-permute-done((bf16[128,1024]{1,0:T(8,128)(2,1)S(1)}, bf16[128,1024]{1,0:T(8,128)(2,1)S(1)}, u32[]{:S(2)}, u32[]{:S(2)}) %collective-permute-start.4) | collective-permute-done | bytes 262176 | tf_op jit(solution)/shard_map/ppermute | solution.py:255
  179.6 0.0 collective-permute-done.3
  179.6 0.0 collective-permute-done.5
  179.6 1.9 add_convert_fusion
  181.4 0.0 collective-permute-done.6.refs_12_
  181.4 3.7 %weight_grads.3 = (bf16[4,512,256]{2,1,0:T(8,128)(2,1)}, bf16[4,512,256]{2,1,0:T(8,128)(2,1)}, bf16[4,256,512]{2,1,0:T(8,128)(2,1)}) custom-call(s32[1]{0:T(128)} %bitcast.15.half_ref, bf16[4,96,1024]{2,1,0:T(8,128)(2,1)S(1)} %get-tuple-element.83.refs_0_, bf16[4,96,1024]{2,1,0:T(8,128)(2,1)S(1)} %get-tuple-element.84.refs_1_, ...), custom_call_target="tpu_custom_call" | custom-call | flops 1207959552 | bytes 8650752 | tf_op jit(solution)/shard_map/weight_grads/pallas_call | solution.py:200
Async XLA Ops:
  7.2 55.3 %all-gather.6.cloned.1.call-start = ((), (), s32[]{:S(2)}) async-start(), calls=%async_computation | async-start | bytes 2359296 | tf_op jit(solution)/shard_map/all_gather | solution.py:233
  7.9 104.6 %all-gather.8.cloned.1.call-start = ((), (), s32[]{:S(2)}) async-start(), calls=%async_computation.1 | async-start | bytes 2359296 | tf_op jit(solution)/shard_map/all_gather | solution.py:233
  121.4 9.7 %copy-start.4 = (bf16[4,96,768]{2,1,0:T(8,128)(2,1)}, bf16[4,96,768]{2,1,0:T(8,128)(2,1)S(1)}, u32[]{:S(2)}) copy-start(bf16[4,96,768]{2,1,0:T(8,128)(2,1)S(1)} %get-tuple-element.92.refs_9_) | copy-start | bytes 1769476
  121.4 34.0 %collective-permute-start.1 = (bf16[256,1024]{1,0:T(8,128)(2,1)}, bf16[256,1024]{1,0:T(8,128)(2,1)}, u32[]{:S(2)}, u32[]{:S(2)}) collective-permute-start(bf16[256,1024]{1,0:T(8,128)(2,1)} %get-tuple-element.74), channel_id=1, source_target_pairs={{0,4},{4,0},{8,12},{12,8},{1,5},{5,1},{9,13},{13,9},{2,6},{6,2},{1... | collective-permute-start | bytes 1572872 | tf_op jit(solution)/shard_map/ppermute | solution.py:260
  131.1 0.8 copy-start.6
  131.9 12.8 %collective-permute-start = (bf16[128,1024]{1,0:T(8,128)(2,1)S(1)}, bf16[128,1024]{1,0:T(8,128)(2,1)S(1)}, u32[]{:S(2)}, u32[]{:S(2)}) collective-permute-start(bf16[128,1024]{1,0:T(8,128)(2,1)S(1)} %get-tuple-element.67), channel_id=1, source_target_pairs={{0,2},{2,0},{1,3},{3,1},{4,6},{6,4},{5,7},{7,5},{8,10},{10,8},{9,1... | collective-permute-start | bytes 786440 | tf_op jit(solution)/shard_map/ppermute | solution.py:245
  141.4 0.9 copy-start
  142.3 0.9 copy-start.2
  143.2 0.8 copy-start.8
  144.0 0.7 copy-start.10
  144.7 0.7 copy-start.12
  145.4 10.0 %collective-permute-start.2 = (bf16[128,1024]{1,0:T(8,128)(2,1)}, bf16[128,1024]{1,0:T(8,128)(2,1)}, u32[]{:S(2)}, u32[]{:S(2)}) collective-permute-start(bf16[128,1024]{1,0:T(8,128)(2,1)} %get-tuple-element.75), channel_id=1, source_target_pairs={{0,2},{2,0},{1,3},{3,1},{4,6},{6,4},{5,7},{7,5},{8,10},{10,8},{9,1... | collective-permute-start | bytes 786440 | tf_op jit(solution)/shard_map/ppermute | solution.py:245
  146.9 8.5 %copy-start.1 = (bf16[4,96,1024]{2,1,0:T(8,128)(2,1)S(1)}, bf16[4,96,1024]{2,1,0:T(8,128)(2,1)}, u32[]{:S(2)}) copy-start(bf16[4,96,1024]{2,1,0:T(8,128)(2,1)} %copy-done) | copy-start | bytes 2359300
  146.9 8.5 %copy-start.3 = (bf16[4,96,1024]{2,1,0:T(8,128)(2,1)S(1)}, bf16[4,96,1024]{2,1,0:T(8,128)(2,1)}, u32[]{:S(2)}) copy-start(bf16[4,96,1024]{2,1,0:T(8,128)(2,1)} %copy-done.2) | copy-start | bytes 2359300
  146.9 8.5 %copy-start.5 = (bf16[4,96,768]{2,1,0:T(8,128)(2,1)S(1)}, bf16[4,96,768]{2,1,0:T(8,128)(2,1)}, u32[]{:S(2)}) copy-start(bf16[4,96,768]{2,1,0:T(8,128)(2,1)} %copy-done.4) | copy-start | bytes 1769476
  146.9 8.5 %copy-start.7 = (bf16[4,96,768]{2,1,0:T(8,128)(2,1)S(1)}, bf16[4,96,768]{2,1,0:T(8,128)(2,1)}, u32[]{:S(2)}) copy-start(bf16[4,96,768]{2,1,0:T(8,128)(2,1)} %copy-done.6) | copy-start | bytes 1769476
  146.9 8.5 %copy-start.9 = (bf16[4,96,768]{2,1,0:T(8,128)(2,1)S(1)}, bf16[4,96,768]{2,1,0:T(8,128)(2,1)}, u32[]{:S(2)}) copy-start(bf16[4,96,768]{2,1,0:T(8,128)(2,1)} %copy-done.8) | copy-start | bytes 1769476
  155.5 3.1 %copy-start.13 = (bf16[128,1024]{1,0:T(8,128)(2,1)S(1)}, bf16[128,1024]{1,0:T(8,128)(2,1)}, u32[]{:S(2)}) copy-start(bf16[128,1024]{1,0:T(8,128)(2,1)} %copy-done.12) | copy-start | bytes 786436
  155.5 5.8 %copy-start.11 = (bf16[128,1024]{1,0:T(8,128)(2,1)S(1)}, bf16[128,1024]{1,0:T(8,128)(2,1)}, u32[]{:S(2)}) copy-start(bf16[128,1024]{1,0:T(8,128)(2,1)} %copy-done.10) | copy-start | bytes 786436
  158.5 23.0 %collective-permute-start.6 = (bf16[4,768,512]{2,1,0:T(8,128)(2,1)S(1)}, bf16[4,768,512]{2,1,0:T(8,128)(2,1)S(1)}, u32[]{:S(2)}, u32[]{:S(2)}) collective-permute-start(bf16[4,768,512]{2,1,0:T(8,128)(2,1)S(1)} %weight_grads.2), channel_id=1, source_target_pairs={{0,1},{1,0},{2,3},{3,2},{4,5},{5,4},{6,7},{7,6},{8,9},{9,8},{10,11... | collective-permute-start | bytes 9437192 | tf_op jit(solution)/shard_map/ppermute | solution.py:278
  158.6 20.9 %collective-permute-start.4 = (bf16[128,1024]{1,0:T(8,128)(2,1)S(1)}, bf16[128,1024]{1,0:T(8,128)(2,1)S(1)}, u32[]{:S(2)}, u32[]{:S(2)}) collective-permute-start(bf16[128,1024]{1,0:T(8,128)(2,1)S(1)} %add_convert_fusion.2), channel_id=1, source_target_pairs={{0,8},{4,12},{8,0},{12,4},{1,9},{5,13},{9,1},{13,5},{2,10},{6,14},... | collective-permute-start | bytes 786440 | tf_op jit(solution)/shard_map/ppermute | solution.py:255
  160.6 18.9 %collective-permute-start.3 = (bf16[128,1024]{1,0:T(8,128)(2,1)S(1)}, bf16[128,1024]{1,0:T(8,128)(2,1)S(1)}, u32[]{:S(2)}, u32[]{:S(2)}) collective-permute-start(bf16[128,1024]{1,0:T(8,128)(2,1)S(1)} %add_convert_fusion.3), channel_id=1, source_target_pairs={{0,2},{2,0},{1,3},{3,1},{4,6},{6,4},{5,7},{7,5},{8,10},{10,8},{9,1... | collective-permute-start | bytes 786440 | tf_op jit(solution)/shard_map/ppermute | solution.py:245
  162.3 17.3 %collective-permute-start.5 = (bf16[128,1024]{1,0:T(8,128)(2,1)S(1)}, bf16[128,1024]{1,0:T(8,128)(2,1)S(1)}, u32[]{:S(2)}, u32[]{:S(2)}) collective-permute-start(bf16[128,1024]{1,0:T(8,128)(2,1)S(1)} %add_convert_fusion.1), channel_id=1, source_target_pairs={{0,12},{4,8},{8,4},{12,0},{1,13},{5,9},{9,5},{13,1},{2,14},{6,10},... | collective-permute-start | bytes 786440 | tf_op jit(solution)/shard_map/ppermute | solution.py:255
Sparse Core Ops, SparseCore 0:
  10.1 52.3 all-gather.5
  64.6 47.8 all-gather.7

commit v4 on v3

v4 whole, which is shorter than its diff:
```python
import functools

import jax
import jax.numpy as jnp
from jax import lax
from jax.experimental import pallas as pl
from jax.experimental.pallas import tpu as pltpu
from jax.sharding import PartitionSpec as P

GROUPS_TOK = 4
ROUTE_ROWS = 16
VMEM_LIMIT = 32 * 1024 * 1024


def dot(a, b, contract):
    return lax.dot_general(a, b, ((contract[:1], contract[1:]), ((), ())), preferred_element_type=jnp.float32)


def in_hbm(v):
    return pltpu.with_memory_space_constraint(v, pltpu.HBM)


def gated_parts(pre_gate):
    logistic = jax.nn.sigmoid(pre_gate)
    return (pre_gate * logistic, logistic * (1.0 + pre_gate * (1.0 - logistic)))


def ring_order(size):
    return [0] + list(range(1, size, 2)) + list(range(2, size, 2))[::-1]


def pack_kernel(tokens, upstream, expert_ids, slots, gate_fixed, out, route, sem):
    top_count, tok_rows = expert_ids.shape
    copies = [
        pltpu.make_async_copy(src, out.at[pl.ds(i * tok_rows, tok_rows), :], sem.at[i])
        for i, src in enumerate((tokens, upstream))
    ]
    for copy in copies:
        copy.start()
    gate = gate_fixed[...]
    route[...] = jnp.zeros_like(route)
    for i, field in enumerate((expert_ids[...], slots[...], gate >> 8, gate & 255)):
        empty = jnp.zeros((ROUTE_ROWS - top_count, tok_rows), jnp.float32)
        field = jnp.concatenate([field.astype(jnp.float32), empty], axis=0)
        route[:, i * tok_rows : (i + 1) * tok_rows] = field.astype(jnp.bfloat16)
    copies.append(pltpu.make_async_copy(route, out.at[pl.ds(2 * tok_rows, ROUTE_ROWS), :], sem.at[2]))
    copies[2].start()
    for copy in copies:
        copy.wait()


def pack_call(tokens, upstream, expert_ids, slots, gate_fixed):
    tok_rows, width = tokens.shape
    vmem, hbm = (pl.BlockSpec(memory_space=m) for m in (pltpu.VMEM, pltpu.HBM))
    operands = [in_hbm(v) for v in (tokens, upstream, expert_ids.T, slots.T, gate_fixed.T)]
    return pl.pallas_call(
        pack_kernel,
        in_specs=[hbm] * 2 + [vmem] * 3,
        out_specs=pl.BlockSpec(memory_space=pl.ANY),
        out_shape=jax.ShapeDtypeStruct((2 * tok_rows + ROUTE_ROWS, width), jnp.bfloat16),
        scratch_shapes=[pltpu.VMEM((ROUTE_ROWS, width), jnp.bfloat16), pltpu.SemaphoreType.DMA((3,))],
        name="pack",
    )(*operands)


def route_keys(route, first_expert, local_experts, capacity, rows, offset, tok_rows, top_count, per_group):
    field = lambda i: route[:top_count, i * tok_rows : (i + 1) * tok_rows]
    expert = field(0).astype(jnp.int32) - first_expert
    slot = field(1).astype(jnp.int32)
    gate = (field(2) * 256.0 + field(3)) / 65536.0
    valid = (expert >= 0) & (expert < local_experts) & (slot < capacity)
    key = jnp.where(valid, expert * rows + offset + slot, -1)
    gate = jnp.where(valid, gate, 0.0)
    pairs = []
    for i in range(per_group):
        key_out, gate_out = key[i : i + 1, :], gate[i : i + 1, :]
        for j in range(i + per_group, top_count, per_group):
            key_out = jnp.maximum(key_out, key[j : j + 1, :])
            gate_out = jnp.maximum(gate_out, gate[j : j + 1, :])
        pairs.append((key_out, gate_out))
    return pairs


def chunk_kernel(n_blocks, tok_rows, capacity, rows, top_count, per_group, first_ref, *refs):
    payloads, weights = refs[:n_blocks], refs[n_blocks : n_blocks + 3]
    parts, kept = refs[n_blocks + 3 : -16], refs[-16:-13]
    x_all, u_all, routes, w_gate, w_up, w_down, back_all, x_rows, s_rows, hids = refs[-13:-3]
    sem_in, sem_weight, sem_out = refs[-3:]
    experts, width, ff = w_gate.shape

    def fetch(b, start, size, to, i):
        copy = pltpu.make_async_copy(payloads[b].at[pl.ds(start, size), :], to, sem_in.at[b, i])
        copy.start()
        return copy

    here = [pl.ds(b * tok_rows, tok_rows) for b in range(n_blocks)]
    get_route = [fetch(b, 2 * tok_rows, ROUTE_ROWS, routes.at[b], 0) for b in range(n_blocks)]
    get_x = [fetch(b, 0, tok_rows, x_all.at[here[b], :], 1) for b in range(n_blocks)]
    get_u = [fetch(b, tok_rows, tok_rows, u_all.at[here[b], :], 2) for b in range(n_blocks)]
    get_weight = [
        [
            pltpu.make_async_copy(src.at[e], to.at[e], sem_weight.at[e, i])
            for i, (src, to) in enumerate(zip(weights, (w_gate, w_up, w_down)))
        ]
        for e in range(experts)
    ]
    for copies in get_weight:
        for copy in copies:
            copy.start()
    keep = []

    def keep_out(i, e, src):
        copy = pltpu.make_async_copy(src.at[e], kept[i].at[e], sem_out.at[e, i])
        copy.start()
        keep.append(copy)

    pairs = []
    for b in range(n_blocks):
        get_route[b].wait()
        route = routes[b].astype(jnp.float32)
        pairs.append(
            route_keys(route, first_ref[0], experts, capacity, rows, b * capacity, tok_rows, top_count, per_group)
        )
    place = lax.broadcasted_iota(jnp.int32, (experts * rows, n_blocks * tok_rows), 0)
    hot = jnp.zeros(place.shape, jnp.float32)
    gate_hot = jnp.zeros(place.shape, jnp.float32)
    for i in range(per_group):
        key = jnp.concatenate([pair[i][0] for pair in pairs], axis=1)
        gate = jnp.concatenate([pair[i][1] for pair in pairs], axis=1)
        match = place == key
        hot = jnp.where(match, 1.0, hot)
        gate_hot = jnp.where(match, gate, gate_hot)
    hot = hot.astype(jnp.bfloat16)
    row_gate = jnp.sum(gate_hot, axis=1, keepdims=True)

    for copy in get_x:
        copy.wait()
    gathered = dot(hot, x_all[...], (1, 0)).astype(jnp.bfloat16)
    for e in range(experts):
        x_rows[e] = gathered[e * rows : (e + 1) * rows, :]
        keep_out(0, e, x_rows)
    for copy in get_u:
        copy.wait()
    scaled = (dot(hot, u_all[...], (1, 0)) * row_gate).astype(jnp.bfloat16)
    for e in range(experts):
        s_rows[e] = scaled[e * rows : (e + 1) * rows, :]
        keep_out(1, e, s_rows)

    for e in range(experts):
        for copy in get_weight[e]:
            copy.wait()
        pre_gate = dot(x_rows[e], w_gate[e], (1, 0))
        pre_up = dot(x_rows[e], w_up[e], (1, 0))
        grad_hidden = dot(s_rows[e], w_down[e], (1, 1))
        active, slope = gated_parts(pre_gate)
        grad_gate_pre = (grad_hidden * pre_up * slope).astype(jnp.bfloat16)
        grad_up_pre = (grad_hidden * active).astype(jnp.bfloat16)
        hids[e, :, :ff] = grad_gate_pre
        hids[e, :, ff : 2 * ff] = grad_up_pre
        hids[e, :, 2 * ff :] = (active * pre_up).astype(jnp.bfloat16)
        keep_out(2, e, hids)
        back = dot(grad_gate_pre, w_gate[e], (1, 1)) + dot(grad_up_pre, w_up[e], (1, 1))
        back_all[e * rows : (e + 1) * rows, :] = back.astype(jnp.bfloat16)

    summed = dot(hot, back_all[...], (0, 0)).astype(jnp.bfloat16)
    start = 0
    for part in parts:
        part[...] = summed[start : start + part.shape[0], :]
        start += part.shape[0]
    for copy in keep:
        copy.wait()


def chunk_call(payloads, first_expert, weights, tok_rows, capacity, rows, top_count, per_group, joined):
    n_blocks = len(payloads)
    n_tok = n_blocks * tok_rows
    experts, width, ff = weights[0].shape
    part_shapes = [(n_tok, width)] if joined else [(tok_rows, width), (n_tok - tok_rows, width)]
    kept_shapes = [(experts, rows, width), (experts, rows, width), (experts, rows, 3 * ff)]
    smem, vmem, hbm = (pl.BlockSpec(memory_space=m) for m in (pltpu.SMEM, pltpu.VMEM, pltpu.HBM))
    buffer = lambda *shape: pltpu.VMEM(shape, jnp.bfloat16)
    semaphores = lambda *shape: pltpu.SemaphoreType.DMA(shape)
    return pl.pallas_call(
        functools.partial(chunk_kernel, n_blocks, tok_rows, capacity, rows, top_count, per_group),
        in_specs=[smem] + [pl.BlockSpec(memory_space=pl.ANY)] * n_blocks + [hbm] * 3,
        out_specs=[vmem] * len(part_shapes) + [hbm] * 3,
        out_shape=[jax.ShapeDtypeStruct(shape, jnp.bfloat16) for shape in part_shapes]
        + [pltpu.HBM(shape, jnp.bfloat16) for shape in kept_shapes],
        scratch_shapes=[
            buffer(n_tok, width),
            buffer(n_tok, width),
            buffer(n_blocks, ROUTE_ROWS, width),
            buffer(experts, width, ff),
            buffer(experts, width, ff),
            buffer(experts, ff, width),
            buffer(experts * rows, width),
            *[buffer(*shape) for shape in kept_shapes],
            semaphores(n_blocks, 3),
            semaphores(experts, 3),
            semaphores(experts, 3),
        ],
        compiler_params=pltpu.CompilerParams(vmem_limit_bytes=VMEM_LIMIT),
        cost_estimate=pl.CostEstimate(
            flops=2 * experts * rows * width * (5 * ff + 3 * n_tok),
            bytes_accessed=6 * experts * width * ff + 8 * n_tok * width,
            transcendentals=0,
        ),
        name="chunk",
    )(first_expert, *payloads, *[in_hbm(w) for w in weights])


def halves_of(n, ff, refs):
    cat = lambda part: jnp.concatenate([ref[0] for ref in part], axis=0)
    x_rows, s_rows, hid = cat(refs[:n]), cat(refs[n : 2 * n]), cat(refs[2 * n : 3 * n])
    return dot(x_rows, hid[:, : 2 * ff], (0, 0)), dot(hid[:, 2 * ff :], s_rows, (0, 0))


def send_kernel(n, ff, half_ref, *refs):
    gate_up, down = halves_of(n, ff, refs)
    out = refs[3 * n]
    depth = gate_up.shape[0]
    out[0, :depth, :] = gate_up.astype(jnp.bfloat16)
    out[0, depth:, :] = down.astype(jnp.bfloat16)


def keep_kernel(n, ff, half_ref, *refs):
    gate_up, down = halves_of(n, ff, refs)
    got = refs[3 * n]
    out_gate, out_up, out_down = refs[3 * n + 1 :]
    depth = gate_up.shape[0]
    gate_up = gate_up + got[0, :depth, :].astype(jnp.float32)
    out_gate[0] = gate_up[:, :ff].astype(jnp.bfloat16)
    out_up[0] = gate_up[:, ff:].astype(jnp.bfloat16)
    out_down[0] = (down + got[0, depth:, :].astype(jnp.float32)).astype(jnp.bfloat16)


def weight_call(half, x_rows, s_rows, hids, got=None):
    n = len(x_rows)
    experts, rows, width = x_rows[0].shape
    ff = hids[0].shape[2] // 3
    depth = width // 2
    piece = lambda shape: pl.BlockSpec((1,) + shape, lambda e, half: (e, 0, 0))
    split = pl.BlockSpec((1, rows, depth), lambda e, half: (e, 0, half[0]))
    in_specs = [split] * (2 * n) + [piece((rows, 3 * ff))] * n
    operands = [in_hbm(v) for v in (*x_rows, *s_rows, *hids)]
    packed = (depth + ff, depth)
    if got is None:
        kernel = send_kernel
        out_specs = piece(packed)
        out_shape = jax.ShapeDtypeStruct((experts,) + packed, jnp.bfloat16)
    else:
        kernel = keep_kernel
        in_specs = in_specs + [piece(packed)]
        operands = operands + [got]
        shapes = [(depth, ff), (depth, ff), (ff, depth)]
        out_specs = [piece(s) for s in shapes]
        out_shape = [jax.ShapeDtypeStruct((experts,) + s, jnp.bfloat16) for s in shapes]
    return pl.pallas_call(
        functools.partial(kernel, n, ff),
        grid_spec=pltpu.PrefetchScalarGridSpec(
            num_scalar_prefetch=1, grid=(experts,), in_specs=in_specs, out_specs=out_specs
        ),
        out_shape=out_shape,
        compiler_params=pltpu.CompilerParams(vmem_limit_bytes=VMEM_LIMIT),
        cost_estimate=pl.CostEstimate(
            flops=2 * experts * n * rows * 3 * ff * depth,
            bytes_accessed=2 * experts * (n * rows * (width + 3 * ff) + 3 * ff * depth),
            transcendentals=0,
        ),
        name="weight_grads",
    )(half, *operands)


def per_device(tokens, upstream, expert_ids, gate_fixed, slots, w_gate, w_up, w_down):
    local_experts = w_gate.shape[0]
    n_group = lax.axis_size("group")
    n_ingroup = lax.axis_size("ingroup")
    experts_all = local_experts * n_group * n_ingroup
    tok_rows, top_count = expert_ids.shape
    width = tokens.shape[1]
    per_group = top_count // GROUPS_TOK
    capacity = max(2, 3 * tok_rows * top_count // (2 * experts_all))
    rows = -(-n_ingroup * capacity // 16) * 16
    z, x, core = (lax.axis_index(a) for a in ("group", "ingroup", "dp"))
    first_expert = ((z * n_ingroup + x) * local_experts).astype(jnp.int32).reshape(1)
    half = core.astype(jnp.int32).reshape(1)
    weights = (w_gate, w_up, w_down)
    wide = lambda v: v.astype(jnp.float32)
    tie = lambda *trees: lax.optimization_barrier(trees)
    order = ring_order(n_group)
    along = lambda k: [(order[i], order[(i + k) % n_group]) for i in range(n_group)]
    shift = lambda s: [(i, (i + s) % n_ingroup) for i in range(n_ingroup)]

    def spread(column):
        return [column] + [lax.ppermute(column, "ingroup", shift(s)) for s in range(1, n_ingroup)]

    def chunk(blocks, joined=False):
        return chunk_call(blocks, first_expert, weights, tok_rows, capacity, rows, top_count, per_group, joined)

    def across(others):
        return [
            lax.ppermute(others[(s - 1) * tok_rows : s * tok_rows], "ingroup", shift(-s)) for s in range(1, n_ingroup)
        ]

    def homeward(part, backs, k):
        group_part = wide(part)
        for back in backs:
            group_part = group_part + wide(back)
        return lax.ppermute(group_part.astype(jnp.bfloat16), "group", along(-k))

    column = pack_call(tokens, upstream, expert_ids, slots, gate_fixed)
    blocks, chunks, near, backs, sent = {}, {}, None, {}, {}
    for k in range(n_group):
        ahead = lax.ppermute(column, "group", along(1)) if k < n_group - 1 else None
        pair = spread(column)
        if k > 0:
            chunks[k - 1] = chunk(blocks[k - 1], k - 1 == 1)
        if k > 2 and near is None:
            near = lax.ppermute(chunks[1][0], "group", along(-1))
        blocks[k], column, chunks, near = tie(pair, ahead, chunks, near)

    last = n_group - 1
    for k in range(2, last):
        backs[k] = across(chunks[k][1])
    backs[0] = across((wide(chunks[0][1]) + wide(near[tok_rows:])).astype(jnp.bfloat16))
    chunks[last] = chunk(blocks[last])
    kept = [[chunks[k][i] for k in range(n_group)] for i in (-3, -2, -1)]
    to_send = weight_call(1 - half, *kept)
    chunks, backs, to_send = tie(chunks, backs, to_send)
    backs[last] = across(chunks[last][1])
    got = lax.ppermute(to_send, "dp", [(0, 1), (1, 0)])
    for k in range(2, n_group):
        sent[k] = homeward(chunks[k][0], backs[k], k)
    total = wide(chunks[0][0]) + wide(near[:tok_rows])
    for back in backs[0]:
        total = total + wide(back)
    for k in range(2, n_group):
        total = total + wide(sent[k])
    grad_tokens = total.astype(jnp.bfloat16)

    x_rows, s_rows, hids = ([chunks[k][i] for k in range(n_group)] for i in (-3, -2, -1))
    grad_gate, grad_up, grad_down = weight_call(half, x_rows, s_rows, hids, got)
    return grad_tokens, grad_gate, grad_up, grad_down


def solution(mesh):
    rows_spec = P(("parts", "group", "ingroup", "dp"), None)
    weight_spec = P(("group", "ingroup"), None, None)
    out_specs = (
        rows_spec,
        P(("parts", "group", "ingroup"), "dp", None),
        P(("parts", "group", "ingroup"), "dp", None),
        P(("parts", "group", "ingroup"), None, "dp"),
    )
    return jax.shard_map(
        per_device,
        mesh=mesh,
        in_specs=(rows_spec,) * 5 + (weight_spec,) * 3,
        out_specs=out_specs,
        check_vma=False,
    )
```

time: 196 us -> 123 us (0.63); the launches traced: 192 us -> 122 us
  waiting for transfers between devices: 85.1 us -> 37.5 us
  blocking collectives: 34.4 us -> 0 us
  Pallas kernels: 41.1 us -> 57.8 us
  starting transfers between devices: 7.32 us -> 21.9 us
  between operations: 14.2 us -> 0.89 us
  local copies, waits for them, and re-layouts: 4.86 us -> 1.05 us
    all_gather x2 -> x0, waiting for transfers between devices: 68.5 us -> none  [per_device(): gather = lambda v: lax.all_gather(v, ('group', 'ingroup'))]
    all_gather x1 -> x0, blocking collectives: 34.4 us -> none  [per_device(): gather = lambda v: lax.all_gather(v, ('group', 'ingroup'))]
    ppermute x6 -> x13, waiting for transfers between devices: 15.2 us -> 37.5 us  [the longest x3 16.2 us: per_device(): ahead = lax.ppermute(column, 'group', along(1)) if k < n_group - 1 else None]
    pallas_call x0 -> x1, Pallas kernels: none -> 17.7 us  [pack_call(): pl.pallas_call(pack_kernel, in_specs=[hbm] * 2 + [vmem] * 3, out_specs=pl...]
    ppermute x6 -> x13, starting transfers between devices: 7.17 us -> 21.8 us  [the longest x3 7.17 us: per_device(): ahead = lax.ppermute(column, 'group', along(1)) if k < n_group - 1 else None]
    pallas_call x4, Pallas kernels: 34.4 us -> 29.4 us  [chunk_call(): pl.pallas_call(functools.partial(chunk_kernel, n_blocks, tok_rows, capaci...]
    pallas_call x2, Pallas kernels: 6.7 us -> 10.6 us  [weight_call(): pl.pallas_call(functools.partial(kernel, n, ff), grid_spec=pltpu.Prefetch...]
    unnamed x28 -> x2, local copies, waits for them, and re-layouts: 4.86 us -> 1.05 us
  transfers between devices with their start and end apart: 9 -> 14, of which waited for: 3 -> 11; matrix products, arithmetic and copies ran while one was open for 3% -> 2% of each run, Pallas kernels for 13% -> 28%
where the time goes in v4:
time: 123 us; the launch traced here: 122 us
  Pallas kernels  57.8 us (47%)
  waiting for transfers between devices  37.5 us (30%)
  starting transfers between devices  21.9 us (18%)
  other arithmetic  3.02 us (2%)
    pallas_call x4, Pallas kernels, chunk_call(): pl.pallas_call(functools.partial(chunk_kernel, n_blocks, tok_rows, capaci...  29.4 us
    pallas_call x1, Pallas kernels, pack_call(): pl.pallas_call(pack_kernel, in_specs=[hbm] * 2 + [vmem] * 3, out_specs=pl...  17.7 us
    ppermute x3, waiting for transfers between devices, per_device(): ahead = lax.ppermute(column, 'group', along(1)) if k < n_group - 1 else None  16.2 us
    ppermute x2, waiting for transfers between devices, homeward(): return lax.ppermute(group_part.astype(jnp.bfloat16), 'group', along(-k))  10.9 us
    pallas_call x2, Pallas kernels, weight_call(): pl.pallas_call(functools.partial(kernel, n, ff), grid_spec=pltpu.Prefetch...  10.6 us
    ppermute x3, starting transfers between devices, per_device(): ahead = lax.ppermute(column, 'group', along(1)) if k < n_group - 1 else None  7.17 us
    ppermute x4, starting transfers between devices, spread(): lax.ppermute(column, 'ingroup', shift(s))  5.96 us
    ppermute x3, waiting for transfers between devices, across(): lax.ppermute(others[(s - 1) * tok_rows:s * tok_rows], 'ingroup', shift(-s))  5.68 us
  transfers between devices with their start and end apart: 14, of which 11 were waited for; matrix products, arithmetic and copies ran while one was open for 2% of the time, Pallas kernels for 28%

profile of v4, /device:TPU:0, one launch (start us, length us, event | category | flops | bytes accessed | tf_op | source)
XLA Modules:
  0.0 122.1 jit_solution(2760084649532928657)
XLA Ops:
  0.6 17.7 %pack.1.refs_0_ = bf16[272,1024]{1,0:T(8,128)(2,1)} custom-call(bf16[128,1024]{1,0:T(8,128)(2,1)} %tokens.1, bf16[128,1024]{1,0:T(8,128)(2,1)} %upstream.1, s32[8,128]{1,0:T(8,128)} %bitcast.5, s32[8,128]{1,0:T(8,128)} %bitcast.6, s32[8,128]{1,0:T(8,128)} %bitcast.7), custom_call_target="tpu_custom_call" | custom-call | tf_op jit(solution)/shard_map/pack/pallas_call | solution.py:56
  18.4 3.1 %collective-permute-start.1 = (bf16[272,1024]{1,0:T(8,128)(2,1)}, bf16[272,1024]{1,0:T(8,128)(2,1)S(1)}, u32[]{:S(2)}, u32[]{:S(2)}) collective-permute-start(bf16[272,1024]{1,0:T(8,128)(2,1)} %pack.1.refs_0_), channel_id=1, source_target_pairs={{0,4},{4,12},{12,8},{8,0},{1,5},{5,13},{13,9},{9,1},{2,6},{6,14},{... | collective-permute-start | bytes 1671176 | tf_op jit(solution)/shard_map/ppermute | solution.py:314
  21.4 1.5 %collective-permute-start = (bf16[272,1024]{1,0:T(8,128)(2,1)}, bf16[272,1024]{1,0:T(8,128)(2,1)S(1)}, u32[]{:S(2)}, u32[]{:S(2)}) collective-permute-start(bf16[272,1024]{1,0:T(8,128)(2,1)} %pack.1.refs_0_), channel_id=1, source_target_pairs={{0,2},{2,0},{1,3},{3,1},{4,6},{6,4},{5,7},{7,5},{8,10},{10,8},{9,1... | collective-permute-start | bytes 1671176 | tf_op jit(solution)/shard_map/ppermute | solution.py:295
  22.9 12.4 %collective-permute-done.1.refs_0_ = bf16[272,1024]{1,0:T(8,128)(2,1)S(1)} collective-permute-done((bf16[272,1024]{1,0:T(8,128)(2,1)}, bf16[272,1024]{1,0:T(8,128)(2,1)S(1)}, u32[]{:S(2)}, u32[]{:S(2)}) %collective-permute-start.1) | collective-permute-done | bytes 557088 | tf_op jit(solution)/shard_map/ppermute | solution.py:314
  35.3 0.4 collective-permute-done.refs_1_
  35.7 2.6 %collective-permute-start.3 = (bf16[272,1024]{1,0:T(8,128)(2,1)S(1)}, bf16[272,1024]{1,0:T(8,128)(2,1)S(1)}, u32[]{:S(2)}, u32[]{:S(2)}) collective-permute-start(bf16[272,1024]{1,0:T(8,128)(2,1)S(1)} %collective-permute-done.1.refs_0_), channel_id=1, source_target_pairs={{0,4},{4,12},{12,8},{8,0},{1,5},{5,13},{13,9},{9,1},{2,6},{6,14},{... | collective-permute-start | bytes 1671176 | tf_op jit(solution)/shard_map/ppermute | solution.py:314
  38.3 1.5 %collective-permute-start.2 = (bf16[272,1024]{1,0:T(8,128)(2,1)S(1)}, bf16[272,1024]{1,0:T(8,128)(2,1)S(1)}, u32[]{:S(2)}, u32[]{:S(2)}) collective-permute-start(bf16[272,1024]{1,0:T(8,128)(2,1)S(1)} %collective-permute-done.1.refs_0_), channel_id=1, source_target_pairs={{0,2},{2,0},{1,3},{3,1},{4,6},{6,4},{5,7},{7,5},{8,10},{10,8},{9,1... | collective-permute-start | bytes 1671176 | tf_op jit(solution)/shard_map/ppermute | solution.py:295
  39.8 0.0 copy-start
  39.8 1.1 copy-done
  40.9 7.2 %chunk.4 = (bf16[128,1024]{1,0:T(8,128)(2,1)S(1)}, bf16[128,1024]{1,0:T(8,128)(2,1)S(1)}, bf16[4,96,1024]{2,1,0:T(8,128)(2,1)}, bf16[4,96,1024]{2,1,0:T(8,128)(2,1)}, bf16[4,96,768]{2,1,0:T(8,128)(2,1)}) custom-call(s32[1]{0:T(128)} %bitcast.3.first_ref, bf16[272,1024]{1,0:T(8,128)(2,1)S(1)} %copy-done, bf16[272,1024]{1,0:T(8,128)(2,1)S(1)} %collective-permute-done.refs_1_, ...), custom_call_target="tpu_custom_call" | custom-call | flops 1610612736 | bytes 8388608 | tf_op jit(solution)/shard_map/chunk/pallas_call | solution.py:183
  48.0 2.0 %collective-permute-done.3.refs_0_ = bf16[272,1024]{1,0:T(8,128)(2,1)S(1)} collective-permute-done((bf16[272,1024]{1,0:T(8,128)(2,1)S(1)}, bf16[272,1024]{1,0:T(8,128)(2,1)S(1)}, u32[]{:S(2)}, u32[]{:S(2)}) %collective-permute-start.3) | collective-permute-done | bytes 557088 | tf_op jit(solution)/shard_map/ppermute | solution.py:314
  50.0 1.2 collective-permute-done.2.refs_1_
  51.2 1.5 %collective-permute-start.5 = (bf16[272,1024]{1,0:T(8,128)(2,1)S(1)}, bf16[272,1024]{1,0:T(8,128)(2,1)S(1)}, u32[]{:S(2)}, u32[]{:S(2)}) collective-permute-start(bf16[272,1024]{1,0:T(8,128)(2,1)S(1)} %collective-permute-done.3.refs_0_), channel_id=1, source_target_pairs={{0,4},{4,12},{12,8},{8,0},{1,5},{5,13},{13,9},{9,1},{2,6},{6,14},{... | collective-permute-start | bytes 1671176 | tf_op jit(solution)/shard_map/ppermute | solution.py:314
  52.7 1.5 %collective-permute-start.4 = (bf16[272,1024]{1,0:T(8,128)(2,1)S(1)}, bf16[272,1024]{1,0:T(8,128)(2,1)S(1)}, u32[]{:S(2)}, u32[]{:S(2)}) collective-permute-start(bf16[272,1024]{1,0:T(8,128)(2,1)S(1)} %collective-permute-done.3.refs_0_), channel_id=1, source_target_pairs={{0,2},{2,0},{1,3},{3,1},{4,6},{6,4},{5,7},{7,5},{8,10},{10,8},{9,1... | collective-permute-start | bytes 1671176 | tf_op jit(solution)/shard_map/ppermute | solution.py:295
  54.2 8.0 %chunk.5 = (bf16[256,1024]{1,0:T(8,128)(2,1)}, bf16[4,96,1024]{2,1,0:T(8,128)(2,1)}, bf16[4,96,1024]{2,1,0:T(8,128)(2,1)}, bf16[4,96,768]{2,1,0:T(8,128)(2,1)}) custom-call(s32[1]{0:T(128)} %bitcast.3.first_ref, bf16[272,1024]{1,0:T(8,128)(2,1)S(1)} %collective-permute-done.1.refs_0_, bf16[272,1024]{1,0:T(8,128)(2,1)S(1)} %collective-permute-done.2.refs_1_, ...), custom_call_target="tpu_custom_call" | custom-call | flops 1610612736 | bytes 8388608 | tf_op jit(solution)/shard_map/chunk/pallas_call | solution.py:183
  62.2 1.9 %collective-permute-done.5.refs_0_ = bf16[272,1024]{1,0:T(8,128)(2,1)S(1)} collective-permute-done((bf16[272,1024]{1,0:T(8,128)(2,1)S(1)}, bf16[272,1024]{1,0:T(8,128)(2,1)S(1)}, u32[]{:S(2)}, u32[]{:S(2)}) %collective-permute-start.5) | collective-permute-done | bytes 557088 | tf_op jit(solution)/shard_map/ppermute | solution.py:314
  64.1 1.4 %collective-permute-done.4.refs_1_ = bf16[272,1024]{1,0:T(8,128)(2,1)S(1)} collective-permute-done((bf16[272,1024]{1,0:T(8,128)(2,1)S(1)}, bf16[272,1024]{1,0:T(8,128)(2,1)S(1)}, u32[]{:S(2)}, u32[]{:S(2)}) %collective-permute-start.4) | collective-permute-done | bytes 557088 | tf_op jit(solution)/shard_map/ppermute | solution.py:295
  65.5 1.5 %collective-permute-start.6 = (bf16[272,1024]{1,0:T(8,128)(2,1)S(1)}, bf16[272,1024]{1,0:T(8,128)(2,1)S(1)}, u32[]{:S(2)}, u32[]{:S(2)}) collective-permute-start(bf16[272,1024]{1,0:T(8,128)(2,1)S(1)} %collective-permute-done.5.refs_0_), channel_id=1, source_target_pairs={{0,2},{2,0},{1,3},{3,1},{4,6},{6,4},{5,7},{7,5},{8,10},{10,8},{9,1... | collective-permute-start | bytes 1671176 | tf_op jit(solution)/shard_map/ppermute | solution.py:295
  67.0 1.4 %collective-permute-start.7 = (bf16[256,1024]{1,0:T(8,128)(2,1)}, bf16[256,1024]{1,0:T(8,128)(2,1)}, u32[]{:S(2)}, u32[]{:S(2)}) collective-permute-start(bf16[256,1024]{1,0:T(8,128)(2,1)} %get-tuple-element.110), channel_id=1, source_target_pairs={{0,8},{4,0},{12,4},{8,12},{1,9},{5,1},{13,5},{9,13},{2,10},{6,2},{... | collective-permute-start | bytes 1572872 | tf_op jit(solution)/shard_map/ppermute | solution.py:319
  68.4 7.2 %chunk.6 = (bf16[128,1024]{1,0:T(8,128)(2,1)S(1)}, bf16[128,1024]{1,0:T(8,128)(2,1)S(1)}, bf16[4,96,1024]{2,1,0:T(8,128)(2,1)}, bf16[4,96,1024]{2,1,0:T(8,128)(2,1)}, bf16[4,96,768]{2,1,0:T(8,128)(2,1)}) custom-call(s32[1]{0:T(128)} %bitcast.3.first_ref, bf16[272,1024]{1,0:T(8,128)(2,1)S(1)} %collective-permute-done.3.refs_0_, ...), custom_call_target="tpu_custom_call" | custom-call | flops 1610612736 | bytes 8388608 | tf_op jit(solution)/shard_map/chunk/pallas_call | solution.py:183
  75.5 1.1 collective-permute-done.7
  76.7 0.5 collective-permute-done.6.refs_1_
  77.1 1.0 add_convert_fusion.3
  78.1 1.6 %collective-permute-start.8 = (bf16[128,1024]{1,0:T(8,128)(2,1)S(1)}, bf16[128,1024]{1,0:T(8,128)(2,1)S(1)}, u32[]{:S(2)}, u32[]{:S(2)}) collective-permute-start(bf16[128,1024]{1,0:T(8,128)(2,1)S(1)} %add_convert_fusion.3), channel_id=1, source_target_pairs={{0,2},{2,0},{1,3},{3,1},{4,6},{6,4},{5,7},{7,5},{8,10},{10,8},{9,1... | collective-permute-start | bytes 786440 | tf_op jit(solution)/shard_map/ppermute | solution.py:302
  79.7 0.5 collective-permute-start.9
  80.2 7.2 %chunk.7 = (bf16[128,1024]{1,0:T(8,128)(2,1)S(1)}, bf16[128,1024]{1,0:T(8,128)(2,1)S(1)}, bf16[4,96,1024]{2,1,0:T(8,128)(2,1)}, bf16[4,96,1024]{2,1,0:T(8,128)(2,1)}, bf16[4,96,768]{2,1,0:T(8,128)(2,1)}) custom-call(s32[1]{0:T(128)} %bitcast.3.first_ref, bf16[272,1024]{1,0:T(8,128)(2,1)S(1)} %collective-permute-done.5.refs_0_, ...), custom_call_target="tpu_custom_call" | custom-call | flops 1610612736 | bytes 8388608 | tf_op jit(solution)/shard_map/chunk/pallas_call | solution.py:183
  87.4 4.9 %weight_grads.2 = bf16[4,768,512]{2,1,0:T(8,128)(2,1)S(1)} custom-call(s32[1]{0:T(128)S(6)} %sub.3.half_ref, bf16[4,96,1024]{2,1,0:T(8,128)(2,1)} %get-tuple-element.148.refs_0_, bf16[4,96,1024]{2,1,0:T(8,128)(2,1)} %get-tuple-element.149.refs_1_, bf16[4,96,1024]{2,1,0:T(8,128)(2,1)} %get-tuple-element.150.refs_2_, ...), custom_call_target="tpu_custom_call" | custom-call | flops 1207959552 | bytes 8650752 | tf_op jit(solution)/shard_map/weight_grads/pallas_call | solution.py:258
  92.3 0.0 collective-permute-done.8
  92.3 0.0 collective-permute-done.9
  92.3 0.1 collective-permute-start.13
  92.4 1.6 %collective-permute-start.11 = (bf16[128,1024]{1,0:T(8,128)(2,1)S(1)}, bf16[128,1024]{1,0:T(8,128)(2,1)S(1)}, u32[]{:S(2)}, u32[]{:S(2)}) collective-permute-start(bf16[128,1024]{1,0:T(8,128)(2,1)S(1)} %get-tuple-element.147), channel_id=1, source_target_pairs={{0,2},{2,0},{1,3},{3,1},{4,6},{6,4},{5,7},{7,5},{8,10},{10,8},{9,1... | collective-permute-start | bytes 786440 | tf_op jit(solution)/shard_map/ppermute | solution.py:302
  94.0 0.1 add_convert_fusion.2
  94.0 1.4 %collective-permute-start.10 = (bf16[128,1024]{1,0:T(8,128)(2,1)S(1)}, bf16[128,1024]{1,0:T(8,128)(2,1)S(1)}, u32[]{:S(2)}, u32[]{:S(2)}) collective-permute-start(bf16[128,1024]{1,0:T(8,128)(2,1)S(1)} %add_convert_fusion.2), channel_id=1, source_target_pairs={{0,12},{4,8},{12,0},{8,4},{1,13},{5,9},{13,1},{9,5},{2,14},{6,10},... | collective-permute-start | bytes 786440 | tf_op jit(solution)/shard_map/ppermute | solution.py:309
  95.5 5.7 %collective-permute-done.11 = bf16[128,1024]{1,0:T(8,128)(2,1)S(1)} collective-permute-done((bf16[128,1024]{1,0:T(8,128)(2,1)S(1)}, bf16[128,1024]{1,0:T(8,128)(2,1)S(1)}, u32[]{:S(2)}, u32[]{:S(2)}) %collective-permute-start.11) | collective-permute-done | bytes 262176 | tf_op jit(solution)/shard_map/ppermute | solution.py:302
  101.1 0.1 add_convert_fusion.1
  101.2 2.2 %collective-permute-start.12 = (bf16[128,1024]{1,0:T(8,128)(2,1)S(1)}, bf16[128,1024]{1,0:T(8,128)(2,1)S(1)}, u32[]{:S(2)}, u32[]{:S(2)}) collective-permute-start(bf16[128,1024]{1,0:T(8,128)(2,1)S(1)} %add_convert_fusion.1), channel_id=1, source_target_pairs={{0,4},{4,12},{12,8},{8,0},{1,5},{5,13},{13,9},{9,1},{2,6},{6,14},{... | collective-permute-start | bytes 786440 | tf_op jit(solution)/shard_map/ppermute | solution.py:309
  103.5 0.9 collective-permute-done.10
  104.4 10.0 %collective-permute-done.12 = bf16[128,1024]{1,0:T(8,128)(2,1)S(1)} collective-permute-done((bf16[128,1024]{1,0:T(8,128)(2,1)S(1)}, bf16[128,1024]{1,0:T(8,128)(2,1)S(1)}, u32[]{:S(2)}, u32[]{:S(2)}) %collective-permute-start.12) | collective-permute-done | bytes 262176 | tf_op jit(solution)/shard_map/ppermute | solution.py:309
  114.4 1.9 %add_convert_fusion = bf16[128,1024]{1,0:T(8,128)(2,1)} fusion(bf16[128,1024]{1,0:T(8,128)(2,1)S(1)} %collective-permute-done.12, bf16[128,1024]{1,0:T(8,128)(2,1)S(1)} %collective-permute-done.10, bf16[128,1024]{1,0:T(8,128)(2,1)S(1)} %collective-permute-done.8, bf16[128,1024]{1,0:T(8,128)(2,1)S(1)} %get-tuple-element.142, ...), kind=kLoop, calls=%fused_computation | loop fusion | flops 1310720 | bytes 1572864 | tf_op jit(solution)/shard_map/convert_element_type | solution.py:339
  116.3 0.0 collective-permute-done.13.refs_12_
  116.3 5.7 %weight_grads.3 = (bf16[4,512,256]{2,1,0:T(8,128)(2,1)}, bf16[4,512,256]{2,1,0:T(8,128)(2,1)}, bf16[4,256,512]{2,1,0:T(8,128)(2,1)}) custom-call(s32[1]{0:T(128)} %bitcast.4.half_ref, bf16[4,96,1024]{2,1,0:T(8,128)(2,1)} %get-tuple-element.148.refs_0_, bf16[4,96,1024]{2,1,0:T(8,128)(2,1)} %get-tuple-element.149.refs_1_, ...), custom_call_target="tpu_custom_call" | custom-call | flops 1207959552 | bytes 8650752 | tf_op jit(solution)/shard_map/weight_grads/pallas_call | solution.py:258
Async XLA Ops:
  18.4 16.9 %collective-permute-start.1 = (bf16[272,1024]{1,0:T(8,128)(2,1)}, bf16[272,1024]{1,0:T(8,128)(2,1)S(1)}, u32[]{:S(2)}, u32[]{:S(2)}) collective-permute-start(bf16[272,1024]{1,0:T(8,128)(2,1)} %pack.1.refs_0_), channel_id=1, source_target_pairs={{0,4},{4,12},{12,8},{8,0},{1,5},{5,13},{13,9},{9,1},{2,6},{6,14},{... | collective-permute-start | bytes 1671176 | tf_op jit(solution)/shard_map/ppermute | solution.py:314
  21.4 14.3 %collective-permute-start = (bf16[272,1024]{1,0:T(8,128)(2,1)}, bf16[272,1024]{1,0:T(8,128)(2,1)S(1)}, u32[]{:S(2)}, u32[]{:S(2)}) collective-permute-start(bf16[272,1024]{1,0:T(8,128)(2,1)} %pack.1.refs_0_), channel_id=1, source_target_pairs={{0,2},{2,0},{1,3},{3,1},{4,6},{6,4},{5,7},{7,5},{8,10},{10,8},{9,1... | collective-permute-start | bytes 1671176 | tf_op jit(solution)/shard_map/ppermute | solution.py:295
  35.7 14.3 %collective-permute-start.3 = (bf16[272,1024]{1,0:T(8,128)(2,1)S(1)}, bf16[272,1024]{1,0:T(8,128)(2,1)S(1)}, u32[]{:S(2)}, u32[]{:S(2)}) collective-permute-start(bf16[272,1024]{1,0:T(8,128)(2,1)S(1)} %collective-permute-done.1.refs_0_), channel_id=1, source_target_pairs={{0,4},{4,12},{12,8},{8,0},{1,5},{5,13},{13,9},{9,1},{2,6},{6,14},{... | collective-permute-start | bytes 1671176 | tf_op jit(solution)/shard_map/ppermute | solution.py:314
  38.3 12.9 %collective-permute-start.2 = (bf16[272,1024]{1,0:T(8,128)(2,1)S(1)}, bf16[272,1024]{1,0:T(8,128)(2,1)S(1)}, u32[]{:S(2)}, u32[]{:S(2)}) collective-permute-start(bf16[272,1024]{1,0:T(8,128)(2,1)S(1)} %collective-permute-done.1.refs_0_), channel_id=1, source_target_pairs={{0,2},{2,0},{1,3},{3,1},{4,6},{6,4},{5,7},{7,5},{8,10},{10,8},{9,1... | collective-permute-start | bytes 1671176 | tf_op jit(solution)/shard_map/ppermute | solution.py:295
  39.8 1.1 copy-start
  51.2 12.9 %collective-permute-start.5 = (bf16[272,1024]{1,0:T(8,128)(2,1)S(1)}, bf16[272,1024]{1,0:T(8,128)(2,1)S(1)}, u32[]{:S(2)}, u32[]{:S(2)}) collective-permute-start(bf16[272,1024]{1,0:T(8,128)(2,1)S(1)} %collective-permute-done.3.refs_0_), channel_id=1, source_target_pairs={{0,4},{4,12},{12,8},{8,0},{1,5},{5,13},{13,9},{9,1},{2,6},{6,14},{... | collective-permute-start | bytes 1671176 | tf_op jit(solution)/shard_map/ppermute | solution.py:314
  52.7 12.8 %collective-permute-start.4 = (bf16[272,1024]{1,0:T(8,128)(2,1)S(1)}, bf16[272,1024]{1,0:T(8,128)(2,1)S(1)}, u32[]{:S(2)}, u32[]{:S(2)}) collective-permute-start(bf16[272,1024]{1,0:T(8,128)(2,1)S(1)} %collective-permute-done.3.refs_0_), channel_id=1, source_target_pairs={{0,2},{2,0},{1,3},{3,1},{4,6},{6,4},{5,7},{7,5},{8,10},{10,8},{9,1... | collective-permute-start | bytes 1671176 | tf_op jit(solution)/shard_map/ppermute | solution.py:295
  65.5 11.6 %collective-permute-start.6 = (bf16[272,1024]{1,0:T(8,128)(2,1)S(1)}, bf16[272,1024]{1,0:T(8,128)(2,1)S(1)}, u32[]{:S(2)}, u32[]{:S(2)}) collective-permute-start(bf16[272,1024]{1,0:T(8,128)(2,1)S(1)} %collective-permute-done.5.refs_0_), channel_id=1, source_target_pairs={{0,2},{2,0},{1,3},{3,1},{4,6},{6,4},{5,7},{7,5},{8,10},{10,8},{9,1... | collective-permute-start | bytes 1671176 | tf_op jit(solution)/shard_map/ppermute | solution.py:295
  67.0 9.6 %collective-permute-start.7 = (bf16[256,1024]{1,0:T(8,128)(2,1)}, bf16[256,1024]{1,0:T(8,128)(2,1)}, u32[]{:S(2)}, u32[]{:S(2)}) collective-permute-start(bf16[256,1024]{1,0:T(8,128)(2,1)} %get-tuple-element.110), channel_id=1, source_target_pairs={{0,8},{4,0},{12,4},{8,12},{1,9},{5,1},{13,5},{9,13},{2,10},{6,2},{... | collective-permute-start | bytes 1572872 | tf_op jit(solution)/shard_map/ppermute | solution.py:319
  78.1 14.2 %collective-permute-start.8 = (bf16[128,1024]{1,0:T(8,128)(2,1)S(1)}, bf16[128,1024]{1,0:T(8,128)(2,1)S(1)}, u32[]{:S(2)}, u32[]{:S(2)}) collective-permute-start(bf16[128,1024]{1,0:T(8,128)(2,1)S(1)} %add_convert_fusion.3), channel_id=1, source_target_pairs={{0,2},{2,0},{1,3},{3,1},{4,6},{6,4},{5,7},{7,5},{8,10},{10,8},{9,1... | collective-permute-start | bytes 786440 | tf_op jit(solution)/shard_map/ppermute | solution.py:302
  79.7 12.6 %collective-permute-start.9 = (bf16[128,1024]{1,0:T(8,128)(2,1)S(1)}, bf16[128,1024]{1,0:T(8,128)(2,1)S(1)}, u32[]{:S(2)}, u32[]{:S(2)}) collective-permute-start(bf16[128,1024]{1,0:T(8,128)(2,1)S(1)} %get-tuple-element.130), channel_id=1, source_target_pairs={{0,2},{2,0},{1,3},{3,1},{4,6},{6,4},{5,7},{7,5},{8,10},{10,8},{9,1... | collective-permute-start | bytes 786440 | tf_op jit(solution)/shard_map/ppermute | solution.py:302
  92.3 23.9 %collective-permute-start.13 = (bf16[4,768,512]{2,1,0:T(8,128)(2,1)S(1)}, bf16[4,768,512]{2,1,0:T(8,128)(2,1)S(1)}, u32[]{:S(2)}, u32[]{:S(2)}) collective-permute-start(bf16[4,768,512]{2,1,0:T(8,128)(2,1)S(1)} %weight_grads.2), channel_id=1, source_target_pairs={{0,1},{1,0},{2,3},{3,2},{4,5},{5,4},{6,7},{7,6},{8,9},{9,8},{10,11... | collective-permute-start | bytes 9437192 | tf_op jit(solution)/shard_map/ppermute | solution.py:331
  92.4 8.7 %collective-permute-start.11 = (bf16[128,1024]{1,0:T(8,128)(2,1)S(1)}, bf16[128,1024]{1,0:T(8,128)(2,1)S(1)}, u32[]{:S(2)}, u32[]{:S(2)}) collective-permute-start(bf16[128,1024]{1,0:T(8,128)(2,1)S(1)} %get-tuple-element.147), channel_id=1, source_target_pairs={{0,2},{2,0},{1,3},{3,1},{4,6},{6,4},{5,7},{7,5},{8,10},{10,8},{9,1... | collective-permute-start | bytes 786440 | tf_op jit(solution)/shard_map/ppermute | solution.py:302
  94.0 10.3 %collective-permute-start.10 = (bf16[128,1024]{1,0:T(8,128)(2,1)S(1)}, bf16[128,1024]{1,0:T(8,128)(2,1)S(1)}, u32[]{:S(2)}, u32[]{:S(2)}) collective-permute-start(bf16[128,1024]{1,0:T(8,128)(2,1)S(1)} %add_convert_fusion.2), channel_id=1, source_target_pairs={{0,12},{4,8},{12,0},{8,4},{1,13},{5,9},{13,1},{9,5},{2,14},{6,10},... | collective-permute-start | bytes 786440 | tf_op jit(solution)/shard_map/ppermute | solution.py:309
  101.2 13.2 %collective-permute-start.12 = (bf16[128,1024]{1,0:T(8,128)(2,1)S(1)}, bf16[128,1024]{1,0:T(8,128)(2,1)S(1)}, u32[]{:S(2)}, u32[]{:S(2)}) collective-permute-start(bf16[128,1024]{1,0:T(8,128)(2,1)S(1)} %add_convert_fusion.1), channel_id=1, source_target_pairs={{0,4},{4,12},{12,8},{8,0},{1,5},{5,13},{13,9},{9,1},{2,6},{6,14},{... | collective-permute-start | bytes 786440 | tf_op jit(solution)/shard_map/ppermute | solution.py:309

commit v5 on v4

--- a/solution.py
+++ b/solution.py
@@ -29,7 +29,7 @@
     return [0] + list(range(1, size, 2)) + list(range(2, size, 2))[::-1]
 
 
-def pack_kernel(tokens, upstream, expert_ids, slots, gate_fixed, out, route, sem):
+def pack_kernel(tokens, upstream, expert_ids, slots, gate_fixed, out, sem):
     top_count, tok_rows = expert_ids.shape
     copies = [
         pltpu.make_async_copy(src, out.at[pl.ds(i * tok_rows, tok_rows), :], sem.at[i])
@@ -38,13 +38,11 @@
     for copy in copies:
         copy.start()
     gate = gate_fixed[...]
-    route[...] = jnp.zeros_like(route)
+    out[2 * tok_rows :, :] = jnp.zeros((ROUTE_ROWS, out.shape[1]), jnp.bfloat16)
     for i, field in enumerate((expert_ids[...], slots[...], gate >> 8, gate & 255)):
         empty = jnp.zeros((ROUTE_ROWS - top_count, tok_rows), jnp.float32)
         field = jnp.concatenate([field.astype(jnp.float32), empty], axis=0)
-        route[:, i * tok_rows : (i + 1) * tok_rows] = field.astype(jnp.bfloat16)
-    copies.append(pltpu.make_async_copy(route, out.at[pl.ds(2 * tok_rows, ROUTE_ROWS), :], sem.at[2]))
-    copies[2].start()
+        out[2 * tok_rows :, i * tok_rows : (i + 1) * tok_rows] = field.astype(jnp.bfloat16)
     for copy in copies:
         copy.wait()
 
@@ -56,9 +54,9 @@
     return pl.pallas_call(
         pack_kernel,
         in_specs=[hbm] * 2 + [vmem] * 3,
-        out_specs=pl.BlockSpec(memory_space=pl.ANY),
+        out_specs=vmem,
         out_shape=jax.ShapeDtypeStruct((2 * tok_rows + ROUTE_ROWS, width), jnp.bfloat16),
-        scratch_shapes=[pltpu.VMEM((ROUTE_ROWS, width), jnp.bfloat16), pltpu.SemaphoreType.DMA((3,))],
+        scratch_shapes=[pltpu.SemaphoreType.DMA((2,))],
         name="pack",
     )(*operands)
 
@@ -302,11 +300,14 @@
             lax.ppermute(others[(s - 1) * tok_rows : s * tok_rows], "ingroup", shift(-s)) for s in range(1, n_ingroup)
         ]
 
-    def homeward(part, backs, k):
+    def group_sum(part, backs):
         group_part = wide(part)
         for back in backs:
             group_part = group_part + wide(back)
-        return lax.ppermute(group_part.astype(jnp.bfloat16), "group", along(-k))
+        return group_part.astype(jnp.bfloat16)
+
+    def homeward(group_part, k):
+        return lax.ppermute(group_part, "group", along(-k))
 
     column = pack_call(tokens, upstream, expert_ids, slots, gate_fixed)
     blocks, chunks, near, backs, sent = {}, {}, None, {}, {}
@@ -324,23 +325,26 @@
         backs[k] = across(chunks[k][1])
     backs[0] = across((wide(chunks[0][1]) + wide(near[tok_rows:])).astype(jnp.bfloat16))
     chunks[last] = chunk(blocks[last])
-    kept = [[chunks[k][i] for k in range(n_group)] for i in (-3, -2, -1)]
+    backs[last] = across(chunks[last][1])
+    x_rows, s_rows, hids = ([chunks[k][i] for k in range(n_group)] for i in (-3, -2, -1))
+    group_parts = {k: group_sum(chunks[k][0], backs[k]) for k in range(2, last)}
+    kept, group_parts, backs[0] = tie((x_rows, s_rows, hids), group_parts, backs[0])
+    for k in range(2, last):
+        sent[k] = homeward(group_parts[k], k)
     to_send = weight_call(1 - half, *kept)
-    chunks, backs, to_send = tie(chunks, backs, to_send)
-    backs[last] = across(chunks[last][1])
+    to_send, backs[last], sent = tie(to_send, backs[last], sent)
     got = lax.ppermute(to_send, "dp", [(0, 1), (1, 0)])
-    for k in range(2, n_group):
-        sent[k] = homeward(chunks[k][0], backs[k], k)
+    group_parts[last] = group_sum(chunks[last][0], backs[last])
+    sent[last] = homeward(group_parts[last], last)
+    got, _ = tie(got, group_parts[last])
+    grads = weight_call(half, *kept, got)
+    grads, sent = tie(grads, sent)
     total = wide(chunks[0][0]) + wide(near[:tok_rows])
     for back in backs[0]:
         total = total + wide(back)
     for k in range(2, n_group):
         total = total + wide(sent[k])
-    grad_tokens = total.astype(jnp.bfloat16)
-
-    x_rows, s_rows, hids = ([chunks[k][i] for k in range(n_group)] for i in (-3, -2, -1))
-    grad_gate, grad_up, grad_down = weight_call(half, x_rows, s_rows, hids, got)
-    return grad_tokens, grad_gate, grad_up, grad_down
+    return (total.astype(jnp.bfloat16), *grads)
 
 
 def solution(mesh):

time: 123 us -> 106 us (0.86)
  Pallas kernels: 57.8 us -> 41.8 us
  other arithmetic: 3.02 us -> 1.12 us
  starting transfers between devices: 21.9 us -> 23.6 us
    pallas_call x1, Pallas kernels: 17.7 us -> 2.57 us  [pack_call(): pl.pallas_call(pack_kernel, in_specs=[hbm] * 2 + [vmem] * 3, out_specs=vm...]
    ppermute x4, waiting for transfers between devices: 3.54 us -> 18 us  [spread(): lax.ppermute(column, 'ingroup', shift(s))]
    ppermute x2, waiting for transfers between devices: 10.9 us -> 0.01 us  [homeward(): return lax.ppermute(group_part, 'group', along(-k))]
    ppermute x3, waiting for transfers between devices: 16.2 us -> 5.34 us  [per_device(): ahead = lax.ppermute(column, 'group', along(1)) if k < n_group - 1 else None]
    ppermute x1, waiting for transfers between devices: 1.11 us -> 9.96 us  [per_device(): near = lax.ppermute(chunks[1][0], 'group', along(-1))]
    ppermute x2, starting transfers between devices: 3.66 us -> 9.46 us  [homeward(): return lax.ppermute(group_part, 'group', along(-k))]
    ppermute x3, waiting for transfers between devices: 5.68 us -> 0.01 us  [across(): lax.ppermute(others[(s - 1) * tok_rows:s * tok_rows], 'ingroup', shift(-s))]
    ppermute x3, starting transfers between devices: 7.17 us -> 3.24 us  [per_device(): ahead = lax.ppermute(column, 'group', along(1)) if k < n_group - 1 else None]
  transfers between devices with their start and end apart: 14 -> 14, of which waited for: 11 -> 8; matrix products, arithmetic and copies ran while one was open for 2% -> 0% of each run, Pallas kernels for 28% -> 37%
where the time goes in v5:
time: 106 us; the launch traced here: 105 us
  Pallas kernels  41.8 us (39%)
  waiting for transfers between devices  37.1 us (35%)
  starting transfers between devices  23.6 us (22%)
  other arithmetic  1.12 us (1%)
    pallas_call x4, Pallas kernels, chunk_call(): pl.pallas_call(functools.partial(chunk_kernel, n_blocks, tok_rows, capaci...  28.7 us
    ppermute x4, waiting for transfers between devices, spread(): lax.ppermute(column, 'ingroup', shift(s))  18 us
    pallas_call x2, Pallas kernels, weight_call(): pl.pallas_call(functools.partial(kernel, n, ff), grid_spec=pltpu.Prefetch...  10.6 us
    ppermute x1, waiting for transfers between devices, per_device(): near = lax.ppermute(chunks[1][0], 'group', along(-1))  9.96 us
    ppermute x2, starting transfers between devices, homeward(): return lax.ppermute(group_part, 'group', along(-k))  9.46 us
    ppermute x4, starting transfers between devices, spread(): lax.ppermute(column, 'ingroup', shift(s))  5.88 us
    ppermute x3, waiting for transfers between devices, per_device(): ahead = lax.ppermute(column, 'group', along(1)) if k < n_group - 1 else None  5.34 us
    ppermute x3, starting transfers between devices, across(): lax.ppermute(others[(s - 1) * tok_rows:s * tok_rows], 'ingroup', shift(-s))  4.13 us
  transfers between devices with their start and end apart: 14, of which 8 were waited for; matrix products, arithmetic and copies ran while one was open for 0% of the time, Pallas kernels for 37%

profile of v5, /device:TPU:0, one launch (start us, length us, event | category | flops | bytes accessed | tf_op | source)
XLA Modules:
  0.0 105.5 jit_solution(3504253814407065587)
XLA Ops:
  0.6 2.6 %pack.1.refs_0_ = bf16[272,1024]{1,0:T(8,128)(2,1)} custom-call(bf16[128,1024]{1,0:T(8,128)(2,1)} %tokens.1, bf16[128,1024]{1,0:T(8,128)(2,1)} %upstream.1, s32[8,128]{1,0:T(8,128)} %bitcast.5, s32[8,128]{1,0:T(8,128)} %bitcast.6, s32[8,128]{1,0:T(8,128)} %bitcast.7), custom_call_target="tpu_custom_call" | custom-call | tf_op jit(solution)/shard_map/pack/pallas_call | solution.py:54
  3.2 3.0 %collective-permute-start = (bf16[272,1024]{1,0:T(8,128)(2,1)}, bf16[272,1024]{1,0:T(8,128)(2,1)S(1)}, u32[]{:S(2)}, u32[]{:S(2)}) collective-permute-start(bf16[272,1024]{1,0:T(8,128)(2,1)} %pack.1.refs_0_), channel_id=1, source_target_pairs={{0,2},{2,0},{1,3},{3,1},{4,6},{6,4},{5,7},{7,5},{8,10},{10,8},{9,1... | collective-permute-start | bytes 1671176 | tf_op jit(solution)/shard_map/ppermute | solution.py:293
  6.2 1.6 %collective-permute-start.1 = (bf16[272,1024]{1,0:T(8,128)(2,1)}, bf16[272,1024]{1,0:T(8,128)(2,1)S(1)}, u32[]{:S(2)}, u32[]{:S(2)}) collective-permute-start(bf16[272,1024]{1,0:T(8,128)(2,1)} %pack.1.refs_0_), channel_id=1, source_target_pairs={{0,4},{4,12},{12,8},{8,0},{1,5},{5,13},{13,9},{9,1},{2,6},{6,14},{... | collective-permute-start | bytes 1671176 | tf_op jit(solution)/shard_map/ppermute | solution.py:315
  7.8 11.3 %collective-permute-done.refs_1_ = bf16[272,1024]{1,0:T(8,128)(2,1)S(1)} collective-permute-done((bf16[272,1024]{1,0:T(8,128)(2,1)}, bf16[272,1024]{1,0:T(8,128)(2,1)S(1)}, u32[]{:S(2)}, u32[]{:S(2)}) %collective-permute-start) | collective-permute-done | bytes 557088 | tf_op jit(solution)/shard_map/ppermute | solution.py:293
  19.0 2.4 %collective-permute-done.1.refs_0_ = bf16[272,1024]{1,0:T(8,128)(2,1)S(1)} collective-permute-done((bf16[272,1024]{1,0:T(8,128)(2,1)}, bf16[272,1024]{1,0:T(8,128)(2,1)S(1)}, u32[]{:S(2)}, u32[]{:S(2)}) %collective-permute-start.1) | collective-permute-done | bytes 557088 | tf_op jit(solution)/shard_map/ppermute | solution.py:315
  21.4 0.5 collective-permute-start.2
  21.9 0.9 collective-permute-start.3
  22.8 0.0 copy-start
  22.8 1.1 copy-done
  23.9 7.2 %chunk.4 = (bf16[128,1024]{1,0:T(8,128)(2,1)S(1)}, bf16[128,1024]{1,0:T(8,128)(2,1)S(1)}, bf16[4,96,1024]{2,1,0:T(8,128)(2,1)}, bf16[4,96,1024]{2,1,0:T(8,128)(2,1)}, bf16[4,96,768]{2,1,0:T(8,128)(2,1)}) custom-call(s32[1]{0:T(128)} %bitcast.3.first_ref, bf16[272,1024]{1,0:T(8,128)(2,1)S(1)} %copy-done, bf16[272,1024]{1,0:T(8,128)(2,1)S(1)} %collective-permute-done.refs_1_, ...), custom_call_target="tpu_custom_call" | custom-call | flops 1610612736 | bytes 8388608 | tf_op jit(solution)/shard_map/chunk/pallas_call | solution.py:181
  31.1 3.6 %collective-permute-done.2.refs_1_ = bf16[272,1024]{1,0:T(8,128)(2,1)S(1)} collective-permute-done((bf16[272,1024]{1,0:T(8,128)(2,1)S(1)}, bf16[272,1024]{1,0:T(8,128)(2,1)S(1)}, u32[]{:S(2)}, u32[]{:S(2)}) %collective-permute-start.2) | collective-permute-done | bytes 557088 | tf_op jit(solution)/shard_map/ppermute | solution.py:293
  34.6 1.4 %collective-permute-done.3.refs_0_ = bf16[272,1024]{1,0:T(8,128)(2,1)S(1)} collective-permute-done((bf16[272,1024]{1,0:T(8,128)(2,1)S(1)}, bf16[272,1024]{1,0:T(8,128)(2,1)S(1)}, u32[]{:S(2)}, u32[]{:S(2)}) %collective-permute-start.3) | collective-permute-done | bytes 557088 | tf_op jit(solution)/shard_map/ppermute | solution.py:315
  36.0 1.2 %collective-permute-start.4 = (bf16[272,1024]{1,0:T(8,128)(2,1)S(1)}, bf16[272,1024]{1,0:T(8,128)(2,1)S(1)}, u32[]{:S(2)}, u32[]{:S(2)}) collective-permute-start(bf16[272,1024]{1,0:T(8,128)(2,1)S(1)} %collective-permute-done.3.refs_0_), channel_id=1, source_target_pairs={{0,2},{2,0},{1,3},{3,1},{4,6},{6,4},{5,7},{7,5},{8,10},{10,8},{9,1... | collective-permute-start | bytes 1671176 | tf_op jit(solution)/shard_map/ppermute | solution.py:293
  37.3 0.8 collective-permute-start.5
  38.0 7.2 %chunk.5 = (bf16[256,1024]{1,0:T(8,128)(2,1)S(1)}, bf16[4,96,1024]{2,1,0:T(8,128)(2,1)}, bf16[4,96,1024]{2,1,0:T(8,128)(2,1)}, bf16[4,96,768]{2,1,0:T(8,128)(2,1)}) custom-call(s32[1]{0:T(128)} %bitcast.3.first_ref, bf16[272,1024]{1,0:T(8,128)(2,1)S(1)} %collective-permute-done.1.refs_0_, bf16[272,1024]{1,0:T(8,128)(2,1)S(1)} %collective-permute-done.2.refs_1_, ...), custom_call_target="tpu_custom_call" | custom-call | flops 1610612736 | bytes 8388608 | tf_op jit(solution)/shard_map/chunk/pallas_call | solution.py:181
  45.2 3.1 %collective-permute-done.4.refs_1_ = bf16[272,1024]{1,0:T(8,128)(2,1)S(1)} collective-permute-done((bf16[272,1024]{1,0:T(8,128)(2,1)S(1)}, bf16[272,1024]{1,0:T(8,128)(2,1)S(1)}, u32[]{:S(2)}, u32[]{:S(2)}) %collective-permute-start.4) | collective-permute-done | bytes 557088 | tf_op jit(solution)/shard_map/ppermute | solution.py:293
  48.3 1.5 %collective-permute-done.5.refs_0_ = bf16[272,1024]{1,0:T(8,128)(2,1)S(1)} collective-permute-done((bf16[272,1024]{1,0:T(8,128)(2,1)S(1)}, bf16[272,1024]{1,0:T(8,128)(2,1)S(1)}, u32[]{:S(2)}, u32[]{:S(2)}) %collective-permute-start.5) | collective-permute-done | bytes 557088 | tf_op jit(solution)/shard_map/ppermute | solution.py:315
  49.9 1.1 %collective-permute-start.6 = (bf16[272,1024]{1,0:T(8,128)(2,1)S(1)}, bf16[272,1024]{1,0:T(8,128)(2,1)S(1)}, u32[]{:S(2)}, u32[]{:S(2)}) collective-permute-start(bf16[272,1024]{1,0:T(8,128)(2,1)S(1)} %collective-permute-done.5.refs_0_), channel_id=1, source_target_pairs={{0,2},{2,0},{1,3},{3,1},{4,6},{6,4},{5,7},{7,5},{8,10},{10,8},{9,1... | collective-permute-start | bytes 1671176 | tf_op jit(solution)/shard_map/ppermute | solution.py:293
  51.0 0.9 collective-permute-start.7
  51.9 7.2 %chunk.6 = (bf16[128,1024]{1,0:T(8,128)(2,1)S(1)}, bf16[128,1024]{1,0:T(8,128)(2,1)S(1)}, bf16[4,96,1024]{2,1,0:T(8,128)(2,1)}, bf16[4,96,1024]{2,1,0:T(8,128)(2,1)}, bf16[4,96,768]{2,1,0:T(8,128)(2,1)}) custom-call(s32[1]{0:T(128)} %bitcast.3.first_ref, bf16[272,1024]{1,0:T(8,128)(2,1)S(1)} %collective-permute-done.3.refs_0_, ...), custom_call_target="tpu_custom_call" | custom-call | flops 1610612736 | bytes 8388608 | tf_op jit(solution)/shard_map/chunk/pallas_call | solution.py:181
  59.1 10.0 %collective-permute-done.7 = bf16[256,1024]{1,0:T(8,128)(2,1)S(1)} collective-permute-done((bf16[256,1024]{1,0:T(8,128)(2,1)S(1)}, bf16[256,1024]{1,0:T(8,128)(2,1)S(1)}, u32[]{:S(2)}, u32[]{:S(2)}) %collective-permute-start.7) | collective-permute-done | bytes 524320 | tf_op jit(solution)/shard_map/ppermute | solution.py:320
  69.0 0.0 collective-permute-done.6.refs_1_
  69.0 2.0 %collective-permute-start.8 = (bf16[128,1024]{1,0:T(8,128)(2,1)S(1)}, bf16[128,1024]{1,0:T(8,128)(2,1)S(1)}, u32[]{:S(2)}, u32[]{:S(2)}) collective-permute-start(bf16[128,1024]{1,0:T(8,128)(2,1)S(1)} %get-tuple-element.142), channel_id=1, source_target_pairs={{0,2},{2,0},{1,3},{3,1},{4,6},{6,4},{5,7},{7,5},{8,10},{10,8},{9,1... | collective-permute-start | bytes 786440 | tf_op jit(solution)/shard_map/ppermute | solution.py:300
  71.0 0.1 add_convert_fusion.2
  71.1 0.1 collective-permute-start.9
  71.2 7.2 %chunk.7 = (bf16[128,1024]{1,0:T(8,128)(2,1)S(1)}, bf16[128,1024]{1,0:T(8,128)(2,1)S(1)}, bf16[4,96,1024]{2,1,0:T(8,128)(2,1)}, bf16[4,96,1024]{2,1,0:T(8,128)(2,1)}, bf16[4,96,768]{2,1,0:T(8,128)(2,1)}) custom-call(s32[1]{0:T(128)} %bitcast.3.first_ref, bf16[272,1024]{1,0:T(8,128)(2,1)S(1)} %collective-permute-done.5.refs_0_, ...), custom_call_target="tpu_custom_call" | custom-call | flops 1610612736 | bytes 8388608 | tf_op jit(solution)/shard_map/chunk/pallas_call | solution.py:181
  78.4 2.0 %collective-permute-start.10 = (bf16[128,1024]{1,0:T(8,128)(2,1)S(1)}, bf16[128,1024]{1,0:T(8,128)(2,1)S(1)}, u32[]{:S(2)}, u32[]{:S(2)}) collective-permute-start(bf16[128,1024]{1,0:T(8,128)(2,1)S(1)} %get-tuple-element.157), channel_id=1, source_target_pairs={{0,2},{2,0},{1,3},{3,1},{4,6},{6,4},{5,7},{7,5},{8,10},{10,8},{9,1... | collective-permute-start | bytes 786440 | tf_op jit(solution)/shard_map/ppermute | solution.py:300
  80.4 0.0 collective-permute-done.8
  80.4 0.1 add_convert_fusion.3
  80.5 0.0 collective-permute-done.9
  80.5 7.7 %collective-permute-start.11 = (bf16[128,1024]{1,0:T(8,128)(2,1)S(1)}, bf16[128,1024]{1,0:T(8,128)(2,1)S(1)}, u32[]{:S(2)}, u32[]{:S(2)}) collective-permute-start(bf16[128,1024]{1,0:T(8,128)(2,1)S(1)} %add_convert_fusion.3), channel_id=1, source_target_pairs={{0,12},{4,8},{12,0},{8,4},{1,13},{5,9},{13,1},{9,5},{2,14},{6,10},... | collective-permute-start | bytes 786440 | tf_op jit(solution)/shard_map/ppermute | solution.py:310
  88.2 4.8 %weight_grads.2 = bf16[4,768,512]{2,1,0:T(8,128)(2,1)S(1)} custom-call(s32[1]{0:T(128)S(6)} %sub.3.half_ref, bf16[4,96,1024]{2,1,0:T(8,128)(2,1)} %get-tuple-element.145.refs_0_, bf16[4,96,1024]{2,1,0:T(8,128)(2,1)} %get-tuple-element.146.refs_1_, bf16[4,96,1024]{2,1,0:T(8,128)(2,1)} %get-tuple-element.147.refs_2_, ...), custom_call_target="tpu_custom_call" | custom-call | flops 1207959552 | bytes 8650752 | tf_op jit(solution)/shard_map/weight_grads/pallas_call | solution.py:256
  93.1 0.0 collective-permute-done.10
  93.1 0.0 collective-permute-done.11
  93.1 0.1 collective-permute-start.12
  93.2 0.1 add_convert_fusion.1
  93.3 1.7 %collective-permute-start.13 = (bf16[128,1024]{1,0:T(8,128)(2,1)S(1)}, bf16[128,1024]{1,0:T(8,128)(2,1)S(1)}, u32[]{:S(2)}, u32[]{:S(2)}) collective-permute-start(bf16[128,1024]{1,0:T(8,128)(2,1)S(1)} %add_convert_fusion.1), channel_id=1, source_target_pairs={{0,4},{4,12},{12,8},{8,0},{1,5},{5,13},{13,9},{9,1},{2,6},{6,14},{... | collective-permute-start | bytes 786440 | tf_op jit(solution)/shard_map/ppermute | solution.py:310
  95.0 3.8 %collective-permute-done.12.refs_12_ = bf16[4,768,512]{2,1,0:T(8,128)(2,1)S(1)} collective-permute-done((bf16[4,768,512]{2,1,0:T(8,128)(2,1)S(1)}, bf16[4,768,512]{2,1,0:T(8,128)(2,1)S(1)}, u32[]{:S(2)}, u32[]{:S(2)}) %collective-permute-start.12) | collective-permute-done | bytes 3145760 | tf_op jit(solution)/shard_map/ppermute | solution.py:336
  98.8 5.7 %weight_grads.3 = (bf16[4,512,256]{2,1,0:T(8,128)(2,1)}, bf16[4,512,256]{2,1,0:T(8,128)(2,1)}, bf16[4,256,512]{2,1,0:T(8,128)(2,1)}) custom-call(s32[1]{0:T(128)} %bitcast.4.half_ref, bf16[4,96,1024]{2,1,0:T(8,128)(2,1)} %get-tuple-element.145.refs_0_, bf16[4,96,1024]{2,1,0:T(8,128)(2,1)} %get-tuple-element.146.refs_1_, ...), custom_call_target="tpu_custom_call" | custom-call | flops 1207959552 | bytes 8650752 | tf_op jit(solution)/shard_map/weight_grads/pallas_call | solution.py:256
  104.6 0.0 collective-permute-done.13
  104.6 0.9 add_convert_fusion
Async XLA Ops:
  3.2 15.8 %collective-permute-start = (bf16[272,1024]{1,0:T(8,128)(2,1)}, bf16[272,1024]{1,0:T(8,128)(2,1)S(1)}, u32[]{:S(2)}, u32[]{:S(2)}) collective-permute-start(bf16[272,1024]{1,0:T(8,128)(2,1)} %pack.1.refs_0_), channel_id=1, source_target_pairs={{0,2},{2,0},{1,3},{3,1},{4,6},{6,4},{5,7},{7,5},{8,10},{10,8},{9,1... | collective-permute-start | bytes 1671176 | tf_op jit(solution)/shard_map/ppermute | solution.py:293
  6.2 15.2 %collective-permute-start.1 = (bf16[272,1024]{1,0:T(8,128)(2,1)}, bf16[272,1024]{1,0:T(8,128)(2,1)S(1)}, u32[]{:S(2)}, u32[]{:S(2)}) collective-permute-start(bf16[272,1024]{1,0:T(8,128)(2,1)} %pack.1.refs_0_), channel_id=1, source_target_pairs={{0,4},{4,12},{12,8},{8,0},{1,5},{5,13},{13,9},{9,1},{2,6},{6,14},{... | collective-permute-start | bytes 1671176 | tf_op jit(solution)/shard_map/ppermute | solution.py:315
  21.4 13.2 %collective-permute-start.2 = (bf16[272,1024]{1,0:T(8,128)(2,1)S(1)}, bf16[272,1024]{1,0:T(8,128)(2,1)S(1)}, u32[]{:S(2)}, u32[]{:S(2)}) collective-permute-start(bf16[272,1024]{1,0:T(8,128)(2,1)S(1)} %collective-permute-done.1.refs_0_), channel_id=1, source_target_pairs={{0,2},{2,0},{1,3},{3,1},{4,6},{6,4},{5,7},{7,5},{8,10},{10,8},{9,1... | collective-permute-start | bytes 1671176 | tf_op jit(solution)/shard_map/ppermute | solution.py:293
  21.9 14.1 %collective-permute-start.3 = (bf16[272,1024]{1,0:T(8,128)(2,1)S(1)}, bf16[272,1024]{1,0:T(8,128)(2,1)S(1)}, u32[]{:S(2)}, u32[]{:S(2)}) collective-permute-start(bf16[272,1024]{1,0:T(8,128)(2,1)S(1)} %collective-permute-done.1.refs_0_), channel_id=1, source_target_pairs={{0,4},{4,12},{12,8},{8,0},{1,5},{5,13},{13,9},{9,1},{2,6},{6,14},{... | collective-permute-start | bytes 1671176 | tf_op jit(solution)/shard_map/ppermute | solution.py:315
  22.8 1.1 copy-start
  36.0 12.3 %collective-permute-start.4 = (bf16[272,1024]{1,0:T(8,128)(2,1)S(1)}, bf16[272,1024]{1,0:T(8,128)(2,1)S(1)}, u32[]{:S(2)}, u32[]{:S(2)}) collective-permute-start(bf16[272,1024]{1,0:T(8,128)(2,1)S(1)} %collective-permute-done.3.refs_0_), channel_id=1, source_target_pairs={{0,2},{2,0},{1,3},{3,1},{4,6},{6,4},{5,7},{7,5},{8,10},{10,8},{9,1... | collective-permute-start | bytes 1671176 | tf_op jit(solution)/shard_map/ppermute | solution.py:293
  37.3 12.6 %collective-permute-start.5 = (bf16[272,1024]{1,0:T(8,128)(2,1)S(1)}, bf16[272,1024]{1,0:T(8,128)(2,1)S(1)}, u32[]{:S(2)}, u32[]{:S(2)}) collective-permute-start(bf16[272,1024]{1,0:T(8,128)(2,1)S(1)} %collective-permute-done.3.refs_0_), channel_id=1, source_target_pairs={{0,4},{4,12},{12,8},{8,0},{1,5},{5,13},{13,9},{9,1},{2,6},{6,14},{... | collective-permute-start | bytes 1671176 | tf_op jit(solution)/shard_map/ppermute | solution.py:315
  49.9 19.1 %collective-permute-start.6 = (bf16[272,1024]{1,0:T(8,128)(2,1)S(1)}, bf16[272,1024]{1,0:T(8,128)(2,1)S(1)}, u32[]{:S(2)}, u32[]{:S(2)}) collective-permute-start(bf16[272,1024]{1,0:T(8,128)(2,1)S(1)} %collective-permute-done.5.refs_0_), channel_id=1, source_target_pairs={{0,2},{2,0},{1,3},{3,1},{4,6},{6,4},{5,7},{7,5},{8,10},{10,8},{9,1... | collective-permute-start | bytes 1671176 | tf_op jit(solution)/shard_map/ppermute | solution.py:293
  51.0 18.0 %collective-permute-start.7 = (bf16[256,1024]{1,0:T(8,128)(2,1)S(1)}, bf16[256,1024]{1,0:T(8,128)(2,1)S(1)}, u32[]{:S(2)}, u32[]{:S(2)}) collective-permute-start(bf16[256,1024]{1,0:T(8,128)(2,1)S(1)} %get-tuple-element.114), channel_id=1, source_target_pairs={{0,8},{4,0},{12,4},{8,12},{1,9},{5,1},{13,5},{9,13},{2,10},{6,2},{... | collective-permute-start | bytes 1572872 | tf_op jit(solution)/shard_map/ppermute | solution.py:320
  69.0 11.4 %collective-permute-start.8 = (bf16[128,1024]{1,0:T(8,128)(2,1)S(1)}, bf16[128,1024]{1,0:T(8,128)(2,1)S(1)}, u32[]{:S(2)}, u32[]{:S(2)}) collective-permute-start(bf16[128,1024]{1,0:T(8,128)(2,1)S(1)} %get-tuple-element.142), channel_id=1, source_target_pairs={{0,2},{2,0},{1,3},{3,1},{4,6},{6,4},{5,7},{7,5},{8,10},{10,8},{9,1... | collective-permute-start | bytes 786440 | tf_op jit(solution)/shard_map/ppermute | solution.py:300
  71.1 9.4 %collective-permute-start.9 = (bf16[128,1024]{1,0:T(8,128)(2,1)S(1)}, bf16[128,1024]{1,0:T(8,128)(2,1)S(1)}, u32[]{:S(2)}, u32[]{:S(2)}) collective-permute-start(bf16[128,1024]{1,0:T(8,128)(2,1)S(1)} %add_convert_fusion.2), channel_id=1, source_target_pairs={{0,2},{2,0},{1,3},{3,1},{4,6},{6,4},{5,7},{7,5},{8,10},{10,8},{9,1... | collective-permute-start | bytes 786440 | tf_op jit(solution)/shard_map/ppermute | solution.py:300
  78.4 14.7 %collective-permute-start.10 = (bf16[128,1024]{1,0:T(8,128)(2,1)S(1)}, bf16[128,1024]{1,0:T(8,128)(2,1)S(1)}, u32[]{:S(2)}, u32[]{:S(2)}) collective-permute-start(bf16[128,1024]{1,0:T(8,128)(2,1)S(1)} %get-tuple-element.157), channel_id=1, source_target_pairs={{0,2},{2,0},{1,3},{3,1},{4,6},{6,4},{5,7},{7,5},{8,10},{10,8},{9,1... | collective-permute-start | bytes 786440 | tf_op jit(solution)/shard_map/ppermute | solution.py:300
  80.5 12.6 %collective-permute-start.11 = (bf16[128,1024]{1,0:T(8,128)(2,1)S(1)}, bf16[128,1024]{1,0:T(8,128)(2,1)S(1)}, u32[]{:S(2)}, u32[]{:S(2)}) collective-permute-start(bf16[128,1024]{1,0:T(8,128)(2,1)S(1)} %add_convert_fusion.3), channel_id=1, source_target_pairs={{0,12},{4,8},{12,0},{8,4},{1,13},{5,9},{13,1},{9,5},{2,14},{6,10},... | collective-permute-start | bytes 786440 | tf_op jit(solution)/shard_map/ppermute | solution.py:310
  93.1 5.7 %collective-permute-start.12 = (bf16[4,768,512]{2,1,0:T(8,128)(2,1)S(1)}, bf16[4,768,512]{2,1,0:T(8,128)(2,1)S(1)}, u32[]{:S(2)}, u32[]{:S(2)}) collective-permute-start(bf16[4,768,512]{2,1,0:T(8,128)(2,1)S(1)} %weight_grads.2), channel_id=1, source_target_pairs={{0,1},{1,0},{2,3},{3,2},{4,5},{5,4},{6,7},{7,6},{8,9},{9,8},{10,11... | collective-permute-start | bytes 9437192 | tf_op jit(solution)/shard_map/ppermute | solution.py:336
  93.3 11.3 %collective-permute-start.13 = (bf16[128,1024]{1,0:T(8,128)(2,1)S(1)}, bf16[128,1024]{1,0:T(8,128)(2,1)S(1)}, u32[]{:S(2)}, u32[]{:S(2)}) collective-permute-start(bf16[128,1024]{1,0:T(8,128)(2,1)S(1)} %add_convert_fusion.1), channel_id=1, source_target_pairs={{0,4},{4,12},{12,8},{8,0},{1,5},{5,13},{13,9},{9,1},{2,6},{6,14},{... | collective-permute-start | bytes 786440 | tf_op jit(solution)/shard_map/ppermute | solution.py:310

commit v6 on v5

--- a/solution.py
+++ b/solution.py
@@ -310,40 +310,38 @@
         return lax.ppermute(group_part, "group", along(-k))
 
     column = pack_call(tokens, upstream, expert_ids, slots, gate_fixed)
-    blocks, chunks, near, backs, sent = {}, {}, None, {}, {}
+    blocks, chunks, backs, sent = {}, {}, {}, {}
     for k in range(n_group):
         ahead = lax.ppermute(column, "group", along(1)) if k < n_group - 1 else None
         pair = spread(column)
         if k > 0:
             chunks[k - 1] = chunk(blocks[k - 1], k - 1 == 1)
-        if k > 2 and near is None:
-            near = lax.ppermute(chunks[1][0], "group", along(-1))
-        blocks[k], column, chunks, near = tie(pair, ahead, chunks, near)
+        blocks[k], column, chunks = tie(pair, ahead, chunks)
 
     last = n_group - 1
-    for k in range(2, last):
-        backs[k] = across(chunks[k][1])
+    for k in range(2, last - 1):
+        sent[k] = homeward(group_sum(chunks[k][0], across(chunks[k][1])), k)
+    near = lax.ppermute(chunks[1][0], "group", along(-1))
+    backs[last - 1] = across(chunks[last - 1][1])
+    chunks[last] = chunk(blocks[last])
+    chunks, near, backs = tie(chunks, near, backs)
+
+    backs[last] = across(chunks[last][1])
+    carried = homeward(group_sum(chunks[last - 1][0], backs[last - 1]), last)
+    kept = [[chunks[k][i] for k in range(n_group)] for i in (-3, -2, -1)]
+    to_send = weight_call(1 - half, *kept)
+    to_send, backs[last], carried = tie(to_send, backs[last], carried)
+
+    got = lax.ppermute(to_send, "dp", [(0, 1), (1, 0)])
+    sent[last] = homeward(group_sum(chunks[last][0], [*backs[last], carried]), last)
     backs[0] = across((wide(chunks[0][1]) + wide(near[tok_rows:])).astype(jnp.bfloat16))
-    chunks[last] = chunk(blocks[last])
-    backs[last] = across(chunks[last][1])
-    x_rows, s_rows, hids = ([chunks[k][i] for k in range(n_group)] for i in (-3, -2, -1))
-    group_parts = {k: group_sum(chunks[k][0], backs[k]) for k in range(2, last)}
-    kept, group_parts, backs[0] = tie((x_rows, s_rows, hids), group_parts, backs[0])
-    for k in range(2, last):
-        sent[k] = homeward(group_parts[k], k)
-    to_send = weight_call(1 - half, *kept)
-    to_send, backs[last], sent = tie(to_send, backs[last], sent)
-    got = lax.ppermute(to_send, "dp", [(0, 1), (1, 0)])
-    group_parts[last] = group_sum(chunks[last][0], backs[last])
-    sent[last] = homeward(group_parts[last], last)
-    got, _ = tie(got, group_parts[last])
     grads = weight_call(half, *kept, got)
-    grads, sent = tie(grads, sent)
+    grads, sent, backs[0] = tie(grads, sent, backs[0])
     total = wide(chunks[0][0]) + wide(near[:tok_rows])
     for back in backs[0]:
         total = total + wide(back)
-    for k in range(2, n_group):
-        total = total + wide(sent[k])
+    for back in sent.values():
+        total = total + wide(back)
     return (total.astype(jnp.bfloat16), *grads)
 
 

time: 106 us -> 96.4 us (0.909)
  waiting for transfers between devices: 37.1 us -> 29.1 us
  starting transfers between devices: 23.6 us -> 22.2 us
    ppermute x3, waiting for transfers between devices: 5.34 us -> 17 us  [per_device(): ahead = lax.ppermute(column, 'group', along(1)) if k < n_group - 1 else None]
    ppermute x4, waiting for transfers between devices: 18 us -> 6.66 us  [spread(): lax.ppermute(column, 'ingroup', shift(s))]
    ppermute x1, waiting for transfers between devices: 9.96 us -> 1.59 us  [per_device(): near = lax.ppermute(chunks[1][0], 'group', along(-1))]
    ppermute x2, starting transfers between devices: 9.46 us -> 4.36 us  [homeward(): return lax.ppermute(group_part, 'group', along(-k))]
    ppermute x3, starting transfers between devices: 3.24 us -> 7.17 us  [per_device(): ahead = lax.ppermute(column, 'group', along(1)) if k < n_group - 1 else None]
  transfers between devices with their start and end apart: 14 -> 14, of which waited for: 8 -> 9; matrix products, arithmetic and copies ran while one was open for 0% -> 0% of each run, Pallas kernels for 37% -> 41%
where the time goes in v6:
time: 96.4 us; the launch traced here: 96.1 us
  Pallas kernels  41.8 us (43%)
  waiting for transfers between devices  29.1 us (30%)
  starting transfers between devices  22.2 us (23%)
  other arithmetic  1.13 us (1%)
  local copies, waits for them, and re-layouts  1.05 us (1%)
    pallas_call x4, Pallas kernels, chunk_call(): pl.pallas_call(functools.partial(chunk_kernel, n_blocks, tok_rows, capaci...  28.6 us
    ppermute x3, waiting for transfers between devices, per_device(): ahead = lax.ppermute(column, 'group', along(1)) if k < n_group - 1 else None  17 us
    pallas_call x2, Pallas kernels, weight_call(): pl.pallas_call(functools.partial(kernel, n, ff), grid_spec=pltpu.Prefetch...  10.6 us
    ppermute x3, starting transfers between devices, per_device(): ahead = lax.ppermute(column, 'group', along(1)) if k < n_group - 1 else None  7.17 us
    ppermute x4, waiting for transfers between devices, spread(): lax.ppermute(column, 'ingroup', shift(s))  6.66 us
    ppermute x4, starting transfers between devices, spread(): lax.ppermute(column, 'ingroup', shift(s))  5.96 us
    ppermute x3, starting transfers between devices, across(): lax.ppermute(others[(s - 1) * tok_rows:s * tok_rows], 'ingroup', shift(-s))  4.47 us
    ppermute x2, starting transfers between devices, homeward(): return lax.ppermute(group_part, 'group', along(-k))  4.36 us
  transfers between devices with their start and end apart: 14, of which 9 were waited for; matrix products, arithmetic and copies ran while one was open for 0% of the time, Pallas kernels for 41%

profile of v6, /device:TPU:0, one launch (start us, length us, event | category | flops | bytes accessed | tf_op | source)
XLA Modules:
  0.0 96.1 jit_solution(11853257037631925117)
XLA Ops:
  0.6 2.6 %pack.1.refs_0_ = bf16[272,1024]{1,0:T(8,128)(2,1)} custom-call(bf16[128,1024]{1,0:T(8,128)(2,1)} %tokens.1, bf16[128,1024]{1,0:T(8,128)(2,1)} %upstream.1, s32[8,128]{1,0:T(8,128)} %bitcast.5, s32[8,128]{1,0:T(8,128)} %bitcast.6, s32[8,128]{1,0:T(8,128)} %bitcast.7), custom_call_target="tpu_custom_call" | custom-call | tf_op jit(solution)/shard_map/pack/pallas_call | solution.py:54
  3.2 3.1 %collective-permute-start.1 = (bf16[272,1024]{1,0:T(8,128)(2,1)}, bf16[272,1024]{1,0:T(8,128)(2,1)S(1)}, u32[]{:S(2)}, u32[]{:S(2)}) collective-permute-start(bf16[272,1024]{1,0:T(8,128)(2,1)} %pack.1.refs_0_), channel_id=1, source_target_pairs={{0,4},{4,12},{12,8},{8,0},{1,5},{5,13},{13,9},{9,1},{2,6},{6,14},{... | collective-permute-start | bytes 1671176 | tf_op jit(solution)/shard_map/ppermute | solution.py:315
  6.3 1.5 %collective-permute-start = (bf16[272,1024]{1,0:T(8,128)(2,1)}, bf16[272,1024]{1,0:T(8,128)(2,1)S(1)}, u32[]{:S(2)}, u32[]{:S(2)}) collective-permute-start(bf16[272,1024]{1,0:T(8,128)(2,1)} %pack.1.refs_0_), channel_id=1, source_target_pairs={{0,2},{2,0},{1,3},{3,1},{4,6},{6,4},{5,7},{7,5},{8,10},{10,8},{9,1... | collective-permute-start | bytes 1671176 | tf_op jit(solution)/shard_map/ppermute | solution.py:293
  7.8 12.4 %collective-permute-done.1.refs_0_ = bf16[272,1024]{1,0:T(8,128)(2,1)S(1)} collective-permute-done((bf16[272,1024]{1,0:T(8,128)(2,1)}, bf16[272,1024]{1,0:T(8,128)(2,1)S(1)}, u32[]{:S(2)}, u32[]{:S(2)}) %collective-permute-start.1) | collective-permute-done | bytes 557088 | tf_op jit(solution)/shard_map/ppermute | solution.py:315
  20.1 0.4 collective-permute-done.refs_1_
  20.6 2.6 %collective-permute-start.3 = (bf16[272,1024]{1,0:T(8,128)(2,1)S(1)}, bf16[272,1024]{1,0:T(8,128)(2,1)S(1)}, u32[]{:S(2)}, u32[]{:S(2)}) collective-permute-start(bf16[272,1024]{1,0:T(8,128)(2,1)S(1)} %collective-permute-done.1.refs_0_), channel_id=1, source_target_pairs={{0,4},{4,12},{12,8},{8,0},{1,5},{5,13},{13,9},{9,1},{2,6},{6,14},{... | collective-permute-start | bytes 1671176 | tf_op jit(solution)/shard_map/ppermute | solution.py:315
  23.2 1.5 %collective-permute-start.2 = (bf16[272,1024]{1,0:T(8,128)(2,1)S(1)}, bf16[272,1024]{1,0:T(8,128)(2,1)S(1)}, u32[]{:S(2)}, u32[]{:S(2)}) collective-permute-start(bf16[272,1024]{1,0:T(8,128)(2,1)S(1)} %collective-permute-done.1.refs_0_), channel_id=1, source_target_pairs={{0,2},{2,0},{1,3},{3,1},{4,6},{6,4},{5,7},{7,5},{8,10},{10,8},{9,1... | collective-permute-start | bytes 1671176 | tf_op jit(solution)/shard_map/ppermute | solution.py:293
  24.7 0.0 copy-start
  24.7 1.1 %copy-done = bf16[272,1024]{1,0:T(8,128)(2,1)S(1)} copy-done((bf16[272,1024]{1,0:T(8,128)(2,1)S(1)}, bf16[272,1024]{1,0:T(8,128)(2,1)}, u32[]{:S(2)}) %copy-start) | copy-done | bytes 557080
  25.7 7.2 %chunk.4 = (bf16[128,1024]{1,0:T(8,128)(2,1)S(1)}, bf16[128,1024]{1,0:T(8,128)(2,1)S(1)}, bf16[4,96,1024]{2,1,0:T(8,128)(2,1)}, bf16[4,96,1024]{2,1,0:T(8,128)(2,1)}, bf16[4,96,768]{2,1,0:T(8,128)(2,1)}) custom-call(s32[1]{0:T(128)} %bitcast.3.first_ref, bf16[272,1024]{1,0:T(8,128)(2,1)S(1)} %copy-done, bf16[272,1024]{1,0:T(8,128)(2,1)S(1)} %collective-permute-done.refs_1_, ...), custom_call_target="tpu_custom_call" | custom-call | flops 1610612736 | bytes 8388608 | tf_op jit(solution)/shard_map/chunk/pallas_call | solution.py:181
  32.9 2.0 %collective-permute-done.3.refs_0_ = bf16[272,1024]{1,0:T(8,128)(2,1)S(1)} collective-permute-done((bf16[272,1024]{1,0:T(8,128)(2,1)S(1)}, bf16[272,1024]{1,0:T(8,128)(2,1)S(1)}, u32[]{:S(2)}, u32[]{:S(2)}) %collective-permute-start.3) | collective-permute-done | bytes 557088 | tf_op jit(solution)/shard_map/ppermute | solution.py:315
  34.9 1.2 %collective-permute-done.2.refs_1_ = bf16[272,1024]{1,0:T(8,128)(2,1)S(1)} collective-permute-done((bf16[272,1024]{1,0:T(8,128)(2,1)S(1)}, bf16[272,1024]{1,0:T(8,128)(2,1)S(1)}, u32[]{:S(2)}, u32[]{:S(2)}) %collective-permute-start.2) | collective-permute-done | bytes 557088 | tf_op jit(solution)/shard_map/ppermute | solution.py:293
  36.1 1.5 %collective-permute-start.5 = (bf16[272,1024]{1,0:T(8,128)(2,1)S(1)}, bf16[272,1024]{1,0:T(8,128)(2,1)S(1)}, u32[]{:S(2)}, u32[]{:S(2)}) collective-permute-start(bf16[272,1024]{1,0:T(8,128)(2,1)S(1)} %collective-permute-done.3.refs_0_), channel_id=1, source_target_pairs={{0,4},{4,12},{12,8},{8,0},{1,5},{5,13},{13,9},{9,1},{2,6},{6,14},{... | collective-permute-start | bytes 1671176 | tf_op jit(solution)/shard_map/ppermute | solution.py:315
  37.6 1.5 %collective-permute-start.4 = (bf16[272,1024]{1,0:T(8,128)(2,1)S(1)}, bf16[272,1024]{1,0:T(8,128)(2,1)S(1)}, u32[]{:S(2)}, u32[]{:S(2)}) collective-permute-start(bf16[272,1024]{1,0:T(8,128)(2,1)S(1)} %collective-permute-done.3.refs_0_), channel_id=1, source_target_pairs={{0,2},{2,0},{1,3},{3,1},{4,6},{6,4},{5,7},{7,5},{8,10},{10,8},{9,1... | collective-permute-start | bytes 1671176 | tf_op jit(solution)/shard_map/ppermute | solution.py:293
  39.1 7.2 %chunk.5 = (bf16[256,1024]{1,0:T(8,128)(2,1)S(1)}, bf16[4,96,1024]{2,1,0:T(8,128)(2,1)}, bf16[4,96,1024]{2,1,0:T(8,128)(2,1)}, bf16[4,96,768]{2,1,0:T(8,128)(2,1)}) custom-call(s32[1]{0:T(128)} %bitcast.3.first_ref, bf16[272,1024]{1,0:T(8,128)(2,1)S(1)} %collective-permute-done.1.refs_0_, bf16[272,1024]{1,0:T(8,128)(2,1)S(1)} %collective-permute-done.2.refs_1_, ...), custom_call_target="tpu_custom_call" | custom-call | flops 1610612736 | bytes 8388608 | tf_op jit(solution)/shard_map/chunk/pallas_call | solution.py:181
  46.2 2.7 %collective-permute-done.5.refs_0_ = bf16[272,1024]{1,0:T(8,128)(2,1)S(1)} collective-permute-done((bf16[272,1024]{1,0:T(8,128)(2,1)S(1)}, bf16[272,1024]{1,0:T(8,128)(2,1)S(1)}, u32[]{:S(2)}, u32[]{:S(2)}) %collective-permute-start.5) | collective-permute-done | bytes 557088 | tf_op jit(solution)/shard_map/ppermute | solution.py:315
  48.9 1.4 %collective-permute-done.4.refs_1_ = bf16[272,1024]{1,0:T(8,128)(2,1)S(1)} collective-permute-done((bf16[272,1024]{1,0:T(8,128)(2,1)S(1)}, bf16[272,1024]{1,0:T(8,128)(2,1)S(1)}, u32[]{:S(2)}, u32[]{:S(2)}) %collective-permute-start.4) | collective-permute-done | bytes 557088 | tf_op jit(solution)/shard_map/ppermute | solution.py:293
  50.4 1.5 %collective-permute-start.6 = (bf16[272,1024]{1,0:T(8,128)(2,1)S(1)}, bf16[272,1024]{1,0:T(8,128)(2,1)S(1)}, u32[]{:S(2)}, u32[]{:S(2)}) collective-permute-start(bf16[272,1024]{1,0:T(8,128)(2,1)S(1)} %collective-permute-done.5.refs_0_), channel_id=1, source_target_pairs={{0,2},{2,0},{1,3},{3,1},{4,6},{6,4},{5,7},{7,5},{8,10},{10,8},{9,1... | collective-permute-start | bytes 1671176 | tf_op jit(solution)/shard_map/ppermute | solution.py:293
  51.9 7.2 %chunk.6 = (bf16[128,1024]{1,0:T(8,128)(2,1)S(1)}, bf16[128,1024]{1,0:T(8,128)(2,1)S(1)}, bf16[4,96,1024]{2,1,0:T(8,128)(2,1)}, bf16[4,96,1024]{2,1,0:T(8,128)(2,1)}, bf16[4,96,768]{2,1,0:T(8,128)(2,1)}) custom-call(s32[1]{0:T(128)} %bitcast.3.first_ref, bf16[272,1024]{1,0:T(8,128)(2,1)S(1)} %collective-permute-done.3.refs_0_, ...), custom_call_target="tpu_custom_call" | custom-call | flops 1610612736 | bytes 8388608 | tf_op jit(solution)/shard_map/chunk/pallas_call | solution.py:181
  59.0 3.6 %collective-permute-done.6.refs_1_ = bf16[272,1024]{1,0:T(8,128)(2,1)S(1)} collective-permute-done((bf16[272,1024]{1,0:T(8,128)(2,1)S(1)}, bf16[272,1024]{1,0:T(8,128)(2,1)S(1)}, u32[]{:S(2)}, u32[]{:S(2)}) %collective-permute-start.6) | collective-permute-done | bytes 557088 | tf_op jit(solution)/shard_map/ppermute | solution.py:293
  62.6 0.2 collective-permute-start.7
  62.8 1.5 %collective-permute-start.8 = (bf16[128,1024]{1,0:T(8,128)(2,1)S(1)}, bf16[128,1024]{1,0:T(8,128)(2,1)S(1)}, u32[]{:S(2)}, u32[]{:S(2)}) collective-permute-start(bf16[128,1024]{1,0:T(8,128)(2,1)S(1)} %get-tuple-element.139), channel_id=1, source_target_pairs={{0,2},{2,0},{1,3},{3,1},{4,6},{6,4},{5,7},{7,5},{8,10},{10,8},{9,1... | collective-permute-start | bytes 786440 | tf_op jit(solution)/shard_map/ppermute | solution.py:300
  64.3 7.2 %chunk.7 = (bf16[128,1024]{1,0:T(8,128)(2,1)S(1)}, bf16[128,1024]{1,0:T(8,128)(2,1)S(1)}, bf16[4,96,1024]{2,1,0:T(8,128)(2,1)}, bf16[4,96,1024]{2,1,0:T(8,128)(2,1)}, bf16[4,96,768]{2,1,0:T(8,128)(2,1)}) custom-call(s32[1]{0:T(128)} %bitcast.3.first_ref, bf16[272,1024]{1,0:T(8,128)(2,1)S(1)} %collective-permute-done.5.refs_0_, ...), custom_call_target="tpu_custom_call" | custom-call | flops 1610612736 | bytes 8388608 | tf_op jit(solution)/shard_map/chunk/pallas_call | solution.py:181
  71.4 0.0 collective-permute-done.8
  71.5 1.6 %collective-permute-done.7 = bf16[256,1024]{1,0:T(8,128)(2,1)S(1)} collective-permute-done((bf16[256,1024]{1,0:T(8,128)(2,1)S(1)}, bf16[256,1024]{1,0:T(8,128)(2,1)S(1)}, u32[]{:S(2)}, u32[]{:S(2)}) %collective-permute-start.7) | collective-permute-done | bytes 524320 | tf_op jit(solution)/shard_map/ppermute | solution.py:324
  73.0 0.1 add_convert_fusion.3
  73.1 4.2 %collective-permute-start.10 = (bf16[128,1024]{1,0:T(8,128)(2,1)S(1)}, bf16[128,1024]{1,0:T(8,128)(2,1)S(1)}, u32[]{:S(2)}, u32[]{:S(2)}) collective-permute-start(bf16[128,1024]{1,0:T(8,128)(2,1)S(1)} %add_convert_fusion.3), channel_id=1, source_target_pairs={{0,4},{4,12},{12,8},{8,0},{1,5},{5,13},{13,9},{9,1},{2,6},{6,14},{... | collective-permute-start | bytes 786440 | tf_op jit(solution)/shard_map/ppermute | solution.py:310
  77.3 1.5 %collective-permute-start.9 = (bf16[128,1024]{1,0:T(8,128)(2,1)S(1)}, bf16[128,1024]{1,0:T(8,128)(2,1)S(1)}, u32[]{:S(2)}, u32[]{:S(2)}) collective-permute-start(bf16[128,1024]{1,0:T(8,128)(2,1)S(1)} %get-tuple-element.164), channel_id=1, source_target_pairs={{0,2},{2,0},{1,3},{3,1},{4,6},{6,4},{5,7},{7,5},{8,10},{10,8},{9,1... | collective-permute-start | bytes 786440 | tf_op jit(solution)/shard_map/ppermute | solution.py:300
  78.8 4.8 %weight_grads.2 = bf16[4,768,512]{2,1,0:T(8,128)(2,1)S(1)} custom-call(s32[1]{0:T(128)S(6)} %sub.3.half_ref, bf16[4,96,1024]{2,1,0:T(8,128)(2,1)} %get-tuple-element.152.refs_0_, bf16[4,96,1024]{2,1,0:T(8,128)(2,1)} %get-tuple-element.153.refs_1_, bf16[4,96,1024]{2,1,0:T(8,128)(2,1)} %get-tuple-element.154.refs_2_, ...), custom_call_target="tpu_custom_call" | custom-call | flops 1207959552 | bytes 8650752 | tf_op jit(solution)/shard_map/weight_grads/pallas_call | solution.py:256
  83.7 0.0 collective-permute-done.10
  83.7 0.0 collective-permute-done.9
  83.7 0.1 collective-permute-start.11
  83.8 0.1 add_convert_fusion.1
  83.9 1.5 %collective-permute-start.13 = (bf16[128,1024]{1,0:T(8,128)(2,1)S(1)}, bf16[128,1024]{1,0:T(8,128)(2,1)S(1)}, u32[]{:S(2)}, u32[]{:S(2)}) collective-permute-start(bf16[128,1024]{1,0:T(8,128)(2,1)S(1)} %add_convert_fusion.1), channel_id=1, source_target_pairs={{0,2},{2,0},{1,3},{3,1},{4,6},{6,4},{5,7},{7,5},{8,10},{10,8},{9,1... | collective-permute-start | bytes 786440 | tf_op jit(solution)/shard_map/ppermute | solution.py:300
  85.3 0.1 add_convert_fusion.2
  85.5 0.1 collective-permute-start.12
  85.6 3.8 %collective-permute-done.11.refs_12_ = bf16[4,768,512]{2,1,0:T(8,128)(2,1)S(1)} collective-permute-done((bf16[4,768,512]{2,1,0:T(8,128)(2,1)S(1)}, bf16[4,768,512]{2,1,0:T(8,128)(2,1)S(1)}, u32[]{:S(2)}, u32[]{:S(2)}) %collective-permute-start.11) | collective-permute-done | bytes 3145760 | tf_op jit(solution)/shard_map/ppermute | solution.py:335
  89.4 5.7 %weight_grads.3 = (bf16[4,512,256]{2,1,0:T(8,128)(2,1)}, bf16[4,512,256]{2,1,0:T(8,128)(2,1)}, bf16[4,256,512]{2,1,0:T(8,128)(2,1)}) custom-call(s32[1]{0:T(128)} %bitcast.4.half_ref, bf16[4,96,1024]{2,1,0:T(8,128)(2,1)} %get-tuple-element.152.refs_0_, bf16[4,96,1024]{2,1,0:T(8,128)(2,1)} %get-tuple-element.153.refs_1_, ...), custom_call_target="tpu_custom_call" | custom-call | flops 1207959552 | bytes 8650752 | tf_op jit(solution)/shard_map/weight_grads/pallas_call | solution.py:256
  95.2 0.0 collective-permute-done.13
  95.2 0.0 collective-permute-done.12
  95.2 0.9 add_convert_fusion
Async XLA Ops:
  3.2 16.9 %collective-permute-start.1 = (bf16[272,1024]{1,0:T(8,128)(2,1)}, bf16[272,1024]{1,0:T(8,128)(2,1)S(1)}, u32[]{:S(2)}, u32[]{:S(2)}) collective-permute-start(bf16[272,1024]{1,0:T(8,128)(2,1)} %pack.1.refs_0_), channel_id=1, source_target_pairs={{0,4},{4,12},{12,8},{8,0},{1,5},{5,13},{13,9},{9,1},{2,6},{6,14},{... | collective-permute-start | bytes 1671176 | tf_op jit(solution)/shard_map/ppermute | solution.py:315
  6.3 14.3 %collective-permute-start = (bf16[272,1024]{1,0:T(8,128)(2,1)}, bf16[272,1024]{1,0:T(8,128)(2,1)S(1)}, u32[]{:S(2)}, u32[]{:S(2)}) collective-permute-start(bf16[272,1024]{1,0:T(8,128)(2,1)} %pack.1.refs_0_), channel_id=1, source_target_pairs={{0,2},{2,0},{1,3},{3,1},{4,6},{6,4},{5,7},{7,5},{8,10},{10,8},{9,1... | collective-permute-start | bytes 1671176 | tf_op jit(solution)/shard_map/ppermute | solution.py:293
  20.6 14.3 %collective-permute-start.3 = (bf16[272,1024]{1,0:T(8,128)(2,1)S(1)}, bf16[272,1024]{1,0:T(8,128)(2,1)S(1)}, u32[]{:S(2)}, u32[]{:S(2)}) collective-permute-start(bf16[272,1024]{1,0:T(8,128)(2,1)S(1)} %collective-permute-done.1.refs_0_), channel_id=1, source_target_pairs={{0,4},{4,12},{12,8},{8,0},{1,5},{5,13},{13,9},{9,1},{2,6},{6,14},{... | collective-permute-start | bytes 1671176 | tf_op jit(solution)/shard_map/ppermute | solution.py:315
  23.2 12.9 %collective-permute-start.2 = (bf16[272,1024]{1,0:T(8,128)(2,1)S(1)}, bf16[272,1024]{1,0:T(8,128)(2,1)S(1)}, u32[]{:S(2)}, u32[]{:S(2)}) collective-permute-start(bf16[272,1024]{1,0:T(8,128)(2,1)S(1)} %collective-permute-done.1.refs_0_), channel_id=1, source_target_pairs={{0,2},{2,0},{1,3},{3,1},{4,6},{6,4},{5,7},{7,5},{8,10},{10,8},{9,1... | collective-permute-start | bytes 1671176 | tf_op jit(solution)/shard_map/ppermute | solution.py:293
  24.7 1.1 %copy-start = (bf16[272,1024]{1,0:T(8,128)(2,1)S(1)}, bf16[272,1024]{1,0:T(8,128)(2,1)}, u32[]{:S(2)}) copy-start(bf16[272,1024]{1,0:T(8,128)(2,1)} %pack.1.refs_0_) | copy-start | bytes 1671172
  36.1 12.9 %collective-permute-start.5 = (bf16[272,1024]{1,0:T(8,128)(2,1)S(1)}, bf16[272,1024]{1,0:T(8,128)(2,1)S(1)}, u32[]{:S(2)}, u32[]{:S(2)}) collective-permute-start(bf16[272,1024]{1,0:T(8,128)(2,1)S(1)} %collective-permute-done.3.refs_0_), channel_id=1, source_target_pairs={{0,4},{4,12},{12,8},{8,0},{1,5},{5,13},{13,9},{9,1},{2,6},{6,14},{... | collective-permute-start | bytes 1671176 | tf_op jit(solution)/shard_map/ppermute | solution.py:315
  37.6 12.8 %collective-permute-start.4 = (bf16[272,1024]{1,0:T(8,128)(2,1)S(1)}, bf16[272,1024]{1,0:T(8,128)(2,1)S(1)}, u32[]{:S(2)}, u32[]{:S(2)}) collective-permute-start(bf16[272,1024]{1,0:T(8,128)(2,1)S(1)} %collective-permute-done.3.refs_0_), channel_id=1, source_target_pairs={{0,2},{2,0},{1,3},{3,1},{4,6},{6,4},{5,7},{7,5},{8,10},{10,8},{9,1... | collective-permute-start | bytes 1671176 | tf_op jit(solution)/shard_map/ppermute | solution.py:293
  50.4 12.2 %collective-permute-start.6 = (bf16[272,1024]{1,0:T(8,128)(2,1)S(1)}, bf16[272,1024]{1,0:T(8,128)(2,1)S(1)}, u32[]{:S(2)}, u32[]{:S(2)}) collective-permute-start(bf16[272,1024]{1,0:T(8,128)(2,1)S(1)} %collective-permute-done.5.refs_0_), channel_id=1, source_target_pairs={{0,2},{2,0},{1,3},{3,1},{4,6},{6,4},{5,7},{7,5},{8,10},{10,8},{9,1... | collective-permute-start | bytes 1671176 | tf_op jit(solution)/shard_map/ppermute | solution.py:293
  62.6 10.5 %collective-permute-start.7 = (bf16[256,1024]{1,0:T(8,128)(2,1)S(1)}, bf16[256,1024]{1,0:T(8,128)(2,1)S(1)}, u32[]{:S(2)}, u32[]{:S(2)}) collective-permute-start(bf16[256,1024]{1,0:T(8,128)(2,1)S(1)} %get-tuple-element.134), channel_id=1, source_target_pairs={{0,8},{4,0},{12,4},{8,12},{1,9},{5,1},{13,5},{9,13},{2,10},{6,2},{... | collective-permute-start | bytes 1572872 | tf_op jit(solution)/shard_map/ppermute | solution.py:324
  62.8 8.7 %collective-permute-start.8 = (bf16[128,1024]{1,0:T(8,128)(2,1)S(1)}, bf16[128,1024]{1,0:T(8,128)(2,1)S(1)}, u32[]{:S(2)}, u32[]{:S(2)}) collective-permute-start(bf16[128,1024]{1,0:T(8,128)(2,1)S(1)} %get-tuple-element.139), channel_id=1, source_target_pairs={{0,2},{2,0},{1,3},{3,1},{4,6},{6,4},{5,7},{7,5},{8,10},{10,8},{9,1... | collective-permute-start | bytes 786440 | tf_op jit(solution)/shard_map/ppermute | solution.py:300
  73.1 10.6 %collective-permute-start.10 = (bf16[128,1024]{1,0:T(8,128)(2,1)S(1)}, bf16[128,1024]{1,0:T(8,128)(2,1)S(1)}, u32[]{:S(2)}, u32[]{:S(2)}) collective-permute-start(bf16[128,1024]{1,0:T(8,128)(2,1)S(1)} %add_convert_fusion.3), channel_id=1, source_target_pairs={{0,4},{4,12},{12,8},{8,0},{1,5},{5,13},{13,9},{9,1},{2,6},{6,14},{... | collective-permute-start | bytes 786440 | tf_op jit(solution)/shard_map/ppermute | solution.py:310
  77.3 6.4 %collective-permute-start.9 = (bf16[128,1024]{1,0:T(8,128)(2,1)S(1)}, bf16[128,1024]{1,0:T(8,128)(2,1)S(1)}, u32[]{:S(2)}, u32[]{:S(2)}) collective-permute-start(bf16[128,1024]{1,0:T(8,128)(2,1)S(1)} %get-tuple-element.164), channel_id=1, source_target_pairs={{0,2},{2,0},{1,3},{3,1},{4,6},{6,4},{5,7},{7,5},{8,10},{10,8},{9,1... | collective-permute-start | bytes 786440 | tf_op jit(solution)/shard_map/ppermute | solution.py:300
  83.7 5.7 %collective-permute-start.11 = (bf16[4,768,512]{2,1,0:T(8,128)(2,1)S(1)}, bf16[4,768,512]{2,1,0:T(8,128)(2,1)S(1)}, u32[]{:S(2)}, u32[]{:S(2)}) collective-permute-start(bf16[4,768,512]{2,1,0:T(8,128)(2,1)S(1)} %weight_grads.2), channel_id=1, source_target_pairs={{0,1},{1,0},{2,3},{3,2},{4,5},{5,4},{6,7},{7,6},{8,9},{9,8},{10,11... | collective-permute-start | bytes 9437192 | tf_op jit(solution)/shard_map/ppermute | solution.py:335
  83.9 11.3 %collective-permute-start.13 = (bf16[128,1024]{1,0:T(8,128)(2,1)S(1)}, bf16[128,1024]{1,0:T(8,128)(2,1)S(1)}, u32[]{:S(2)}, u32[]{:S(2)}) collective-permute-start(bf16[128,1024]{1,0:T(8,128)(2,1)S(1)} %add_convert_fusion.1), channel_id=1, source_target_pairs={{0,2},{2,0},{1,3},{3,1},{4,6},{6,4},{5,7},{7,5},{8,10},{10,8},{9,1... | collective-permute-start | bytes 786440 | tf_op jit(solution)/shard_map/ppermute | solution.py:300
  85.5 9.7 %collective-permute-start.12 = (bf16[128,1024]{1,0:T(8,128)(2,1)S(1)}, bf16[128,1024]{1,0:T(8,128)(2,1)S(1)}, u32[]{:S(2)}, u32[]{:S(2)}) collective-permute-start(bf16[128,1024]{1,0:T(8,128)(2,1)S(1)} %add_convert_fusion.2), channel_id=1, source_target_pairs={{0,4},{4,12},{12,8},{8,0},{1,5},{5,13},{13,9},{9,1},{2,6},{6,14},{... | collective-permute-start | bytes 786440 | tf_op jit(solution)/shard_map/ppermute | solution.py:310

commit v7 on v6

--- a/solution.py
+++ b/solution.py
@@ -79,9 +79,9 @@
     return pairs
 
 
-def chunk_kernel(n_blocks, tok_rows, capacity, rows, top_count, per_group, first_ref, *refs):
+def chunk_kernel(n_blocks, tok_rows, capacity, rows, top_count, per_group, place_ref, *refs):
     payloads, weights = refs[:n_blocks], refs[n_blocks : n_blocks + 3]
-    parts, kept = refs[n_blocks + 3 : -16], refs[-16:-13]
+    parts, kept = refs[n_blocks + 3 : -15], refs[-15:-13]
     x_all, u_all, routes, w_gate, w_up, w_down, back_all, x_rows, s_rows, hids = refs[-13:-3]
     sem_in, sem_weight, sem_out = refs[-3:]
     experts, width, ff = w_gate.shape
@@ -106,18 +106,26 @@
         for copy in copies:
             copy.start()
     keep = []
-
-    def keep_out(i, e, src):
-        copy = pltpu.make_async_copy(src.at[e], kept[i].at[e], sem_out.at[e, i])
-        copy.start()
-        keep.append(copy)
+    depth = width // 2
+    core = place_ref[1]
+
+    def keep_out(e, src, start):
+        for i, out in enumerate(kept):
+            side = core if i == 0 else 1 - core
+            cols = pl.ds(pl.multiple_of(side * depth, depth), depth) if src.shape[2] == width else slice(None)
+            size = depth if src.shape[2] == width else src.shape[2]
+            copy = pltpu.make_async_copy(
+                src.at[e, :, cols], out.at[e, :, pl.ds(start, size)], sem_out.at[e, start // depth, i]
+            )
+            copy.start()
+            keep.append(copy)
 
     pairs = []
     for b in range(n_blocks):
         get_route[b].wait()
         route = routes[b].astype(jnp.float32)
         pairs.append(
-            route_keys(route, first_ref[0], experts, capacity, rows, b * capacity, tok_rows, top_count, per_group)
+            route_keys(route, place_ref[0], experts, capacity, rows, b * capacity, tok_rows, top_count, per_group)
         )
     place = lax.broadcasted_iota(jnp.int32, (experts * rows, n_blocks * tok_rows), 0)
     hot = jnp.zeros(place.shape, jnp.float32)
@@ -136,13 +144,13 @@
     gathered = dot(hot, x_all[...], (1, 0)).astype(jnp.bfloat16)
     for e in range(experts):
         x_rows[e] = gathered[e * rows : (e + 1) * rows, :]
-        keep_out(0, e, x_rows)
+        keep_out(e, x_rows, 0)
     for copy in get_u:
         copy.wait()
     scaled = (dot(hot, u_all[...], (1, 0)) * row_gate).astype(jnp.bfloat16)
     for e in range(experts):
         s_rows[e] = scaled[e * rows : (e + 1) * rows, :]
-        keep_out(1, e, s_rows)
+        keep_out(e, s_rows, depth)
 
     for e in range(experts):
         for copy in get_weight[e]:
@@ -156,7 +164,7 @@
         hids[e, :, :ff] = grad_gate_pre
         hids[e, :, ff : 2 * ff] = grad_up_pre
         hids[e, :, 2 * ff :] = (active * pre_up).astype(jnp.bfloat16)
-        keep_out(2, e, hids)
+        keep_out(e, hids, 2 * depth)
         back = dot(grad_gate_pre, w_gate[e], (1, 1)) + dot(grad_up_pre, w_up[e], (1, 1))
         back_all[e * rows : (e + 1) * rows, :] = back.astype(jnp.bfloat16)
 
@@ -169,21 +177,21 @@
         copy.wait()
 
 
-def chunk_call(payloads, first_expert, weights, tok_rows, capacity, rows, top_count, per_group, joined):
+def chunk_call(payloads, place, weights, tok_rows, capacity, rows, top_count, per_group, joined):
     n_blocks = len(payloads)
     n_tok = n_blocks * tok_rows
     experts, width, ff = weights[0].shape
     part_shapes = [(n_tok, width)] if joined else [(tok_rows, width), (n_tok - tok_rows, width)]
-    kept_shapes = [(experts, rows, width), (experts, rows, width), (experts, rows, 3 * ff)]
+    kept_shape = (experts, rows, width + 3 * ff)
     smem, vmem, hbm = (pl.BlockSpec(memory_space=m) for m in (pltpu.SMEM, pltpu.VMEM, pltpu.HBM))
     buffer = lambda *shape: pltpu.VMEM(shape, jnp.bfloat16)
     semaphores = lambda *shape: pltpu.SemaphoreType.DMA(shape)
     return pl.pallas_call(
         functools.partial(chunk_kernel, n_blocks, tok_rows, capacity, rows, top_count, per_group),
         in_specs=[smem] + [pl.BlockSpec(memory_space=pl.ANY)] * n_blocks + [hbm] * 3,
-        out_specs=[vmem] * len(part_shapes) + [hbm] * 3,
+        out_specs=[vmem] * len(part_shapes) + [hbm] * 2,
         out_shape=[jax.ShapeDtypeStruct(shape, jnp.bfloat16) for shape in part_shapes]
-        + [pltpu.HBM(shape, jnp.bfloat16) for shape in kept_shapes],
+        + [pltpu.HBM(kept_shape, jnp.bfloat16)] * 2,
         scratch_shapes=[
             buffer(n_tok, width),
             buffer(n_tok, width),
@@ -192,10 +200,12 @@
             buffer(experts, width, ff),
             buffer(experts, ff, width),
             buffer(experts * rows, width),
-            *[buffer(*shape) for shape in kept_shapes],
+            buffer(experts, rows, width),
+            buffer(experts, rows, width),
+            buffer(experts, rows, 3 * ff),
             semaphores(n_blocks, 3),
             semaphores(experts, 3),
-            semaphores(experts, 3),
+            semaphores(experts, 3, 2),
         ],
         compiler_params=pltpu.CompilerParams(vmem_limit_bytes=VMEM_LIMIT),
         cost_estimate=pl.CostEstimate(
@@ -204,69 +214,41 @@
             transcendentals=0,
         ),
         name="chunk",
-    )(first_expert, *payloads, *[in_hbm(w) for w in weights])
-
-
-def halves_of(n, ff, refs):
-    cat = lambda part: jnp.concatenate([ref[0] for ref in part], axis=0)
-    x_rows, s_rows, hid = cat(refs[:n]), cat(refs[n : 2 * n]), cat(refs[2 * n : 3 * n])
-    return dot(x_rows, hid[:, : 2 * ff], (0, 0)), dot(hid[:, 2 * ff :], s_rows, (0, 0))
-
-
-def send_kernel(n, ff, half_ref, *refs):
-    gate_up, down = halves_of(n, ff, refs)
-    out = refs[3 * n]
-    depth = gate_up.shape[0]
-    out[0, :depth, :] = gate_up.astype(jnp.bfloat16)
-    out[0, depth:, :] = down.astype(jnp.bfloat16)
-
-
-def keep_kernel(n, ff, half_ref, *refs):
-    gate_up, down = halves_of(n, ff, refs)
-    got = refs[3 * n]
-    out_gate, out_up, out_down = refs[3 * n + 1 :]
-    depth = gate_up.shape[0]
-    gate_up = gate_up + got[0, :depth, :].astype(jnp.float32)
+    )(place, *payloads, *[in_hbm(w) for w in weights])
+
+
+def weight_kernel(ff, n, *refs):
+    rows = jnp.concatenate([ref[0] for ref in refs[:n]], axis=0)
+    out_gate, out_up, out_down = refs[-3:]
+    depth = (rows.shape[1] - 3 * ff) // 2
+    x_rows, s_rows, hid = rows[:, :depth], rows[:, depth : 2 * depth], rows[:, 2 * depth :]
+    gate_up = dot(x_rows, hid[:, : 2 * ff], (0, 0))
     out_gate[0] = gate_up[:, :ff].astype(jnp.bfloat16)
     out_up[0] = gate_up[:, ff:].astype(jnp.bfloat16)
-    out_down[0] = (down + got[0, depth:, :].astype(jnp.float32)).astype(jnp.bfloat16)
-
-
-def weight_call(half, x_rows, s_rows, hids, got=None):
-    n = len(x_rows)
-    experts, rows, width = x_rows[0].shape
-    ff = hids[0].shape[2] // 3
-    depth = width // 2
-    piece = lambda shape: pl.BlockSpec((1,) + shape, lambda e, half: (e, 0, 0))
-    split = pl.BlockSpec((1, rows, depth), lambda e, half: (e, 0, half[0]))
-    in_specs = [split] * (2 * n) + [piece((rows, 3 * ff))] * n
-    operands = [in_hbm(v) for v in (*x_rows, *s_rows, *hids)]
-    packed = (depth + ff, depth)
-    if got is None:
-        kernel = send_kernel
-        out_specs = piece(packed)
-        out_shape = jax.ShapeDtypeStruct((experts,) + packed, jnp.bfloat16)
-    else:
-        kernel = keep_kernel
-        in_specs = in_specs + [piece(packed)]
-        operands = operands + [got]
-        shapes = [(depth, ff), (depth, ff), (ff, depth)]
-        out_specs = [piece(s) for s in shapes]
-        out_shape = [jax.ShapeDtypeStruct((experts,) + s, jnp.bfloat16) for s in shapes]
+    out_down[0] = dot(hid[:, 2 * ff :], s_rows, (0, 0)).astype(jnp.bfloat16)
+
+
+def weight_call(kept, ff, first, count, before):
+    n = len(kept)
+    experts, rows, width = kept[0].shape
+    depth = (width - 3 * ff) // 2
+    piece = lambda shape: pl.BlockSpec((1,) + shape, lambda e: (e + first, 0, 0))
+    shapes = [(depth, ff), (depth, ff), (ff, depth)]
     return pl.pallas_call(
-        functools.partial(kernel, n, ff),
-        grid_spec=pltpu.PrefetchScalarGridSpec(
-            num_scalar_prefetch=1, grid=(experts,), in_specs=in_specs, out_specs=out_specs
-        ),
-        out_shape=out_shape,
+        functools.partial(weight_kernel, ff, n),
+        grid=(count,),
+        in_specs=[piece((rows, width))] * n + [pl.BlockSpec(memory_space=pl.ANY)] * len(before),
+        out_specs=[piece(s) for s in shapes],
+        out_shape=[jax.ShapeDtypeStruct((experts,) + s, jnp.bfloat16) for s in shapes],
+        input_output_aliases={n + i: i for i in range(len(before))},
         compiler_params=pltpu.CompilerParams(vmem_limit_bytes=VMEM_LIMIT),
         cost_estimate=pl.CostEstimate(
-            flops=2 * experts * n * rows * 3 * ff * depth,
-            bytes_accessed=2 * experts * (n * rows * (width + 3 * ff) + 3 * ff * depth),
+            flops=2 * count * n * rows * 3 * ff * depth,
+            bytes_accessed=2 * count * (n * rows * width + 3 * ff * depth),
             transcendentals=0,
         ),
         name="weight_grads",
-    )(half, *operands)
+    )(*kept, *before)
 
 
 def per_device(tokens, upstream, expert_ids, gate_fixed, slots, w_gate, w_up, w_down):
@@ -280,8 +262,7 @@
     capacity = max(2, 3 * tok_rows * top_count // (2 * experts_all))
     rows = -(-n_ingroup * capacity // 16) * 16
     z, x, core = (lax.axis_index(a) for a in ("group", "ingroup", "dp"))
-    first_expert = ((z * n_ingroup + x) * local_experts).astype(jnp.int32).reshape(1)
-    half = core.astype(jnp.int32).reshape(1)
+    place = jnp.stack([(z * n_ingroup + x) * local_experts, core]).astype(jnp.int32)
     weights = (w_gate, w_up, w_down)
     wide = lambda v: v.astype(jnp.float32)
     tie = lambda *trees: lax.optimization_barrier(trees)
@@ -293,7 +274,7 @@
         return [column] + [lax.ppermute(column, "ingroup", shift(s)) for s in range(1, n_ingroup)]
 
     def chunk(blocks, joined=False):
-        return chunk_call(blocks, first_expert, weights, tok_rows, capacity, rows, top_count, per_group, joined)
+        return chunk_call(blocks, place, weights, tok_rows, capacity, rows, top_count, per_group, joined)
 
     def across(others):
         return [
@@ -310,32 +291,40 @@
         return lax.ppermute(group_part, "group", along(-k))
 
     column = pack_call(tokens, upstream, expert_ids, slots, gate_fixed)
-    blocks, chunks, backs, sent = {}, {}, {}, {}
+    def give(k):
+        return lax.ppermute(chunks[k][-1], "dp", [(0, 1), (1, 0)])
+
+    blocks, chunks, backs, sent, theirs = {}, {}, {}, {}, {}
     for k in range(n_group):
         ahead = lax.ppermute(column, "group", along(1)) if k < n_group - 1 else None
         pair = spread(column)
+        if k > 1:
+            theirs[k - 2] = give(k - 2)
         if k > 0:
             chunks[k - 1] = chunk(blocks[k - 1], k - 1 == 1)
-        blocks[k], column, chunks = tie(pair, ahead, chunks)
+        blocks[k], column, chunks, theirs = tie(pair, ahead, chunks, theirs)
 
     last = n_group - 1
     for k in range(2, last - 1):
         sent[k] = homeward(group_sum(chunks[k][0], across(chunks[k][1])), k)
     near = lax.ppermute(chunks[1][0], "group", along(-1))
     backs[last - 1] = across(chunks[last - 1][1])
+    theirs[last - 1] = give(last - 1)
     chunks[last] = chunk(blocks[last])
-    chunks, near, backs = tie(chunks, near, backs)
-
+    chunks, near, backs, theirs = tie(chunks, near, backs, theirs)
+
+    theirs[last] = give(last)
     backs[last] = across(chunks[last][1])
     carried = homeward(group_sum(chunks[last - 1][0], backs[last - 1]), last)
-    kept = [[chunks[k][i] for k in range(n_group)] for i in (-3, -2, -1)]
-    to_send = weight_call(1 - half, *kept)
-    to_send, backs[last], carried = tie(to_send, backs[last], carried)
-
-    got = lax.ppermute(to_send, "dp", [(0, 1), (1, 0)])
+    kept = [in_hbm(chunks[k][-2]) for k in range(n_group)] + [theirs[k] for k in range(n_group)]
+    ff = w_gate.shape[2]
+    grads = weight_call(kept, ff, 0, local_experts // 2, [])
+    other = (wide(chunks[0][1]) + wide(near[tok_rows:])).astype(jnp.bfloat16)
+    grads, backs[last], carried, other = tie(grads, backs[last], carried, other)
+
     sent[last] = homeward(group_sum(chunks[last][0], [*backs[last], carried]), last)
-    backs[0] = across((wide(chunks[0][1]) + wide(near[tok_rows:])).astype(jnp.bfloat16))
-    grads = weight_call(half, *kept, got)
+    backs[0] = across(other)
+    grads = weight_call(kept, ff, local_experts // 2, local_experts - local_experts // 2, grads)
     grads, sent, backs[0] = tie(grads, sent, backs[0])
     total = wide(chunks[0][0]) + wide(near[:tok_rows])
     for back in backs[0]:

time: 96.4 us -> 102 us (1.058)
  waiting for transfers between devices: 29.1 us -> 36.1 us
    ppermute x2, waiting for transfers between devices: 0.01 us -> 5.31 us  [homeward(): return lax.ppermute(group_part, 'group', along(-k))]
    ppermute x1 -> x4, waiting for transfers between devices: 3.82 us -> 0.01 us  [give(): return lax.ppermute(chunks[k][-1], 'dp', [(0, 1), (1, 0)])]
    pallas_call x2, Pallas kernels: 10.6 us -> 7.32 us  [weight_call(): pl.pallas_call(functools.partial(weight_kernel, ff, n), grid=(count,), in...]
    pallas_call x4, Pallas kernels: 28.6 us -> 31.4 us  [chunk_call(): pl.pallas_call(functools.partial(chunk_kernel, n_blocks, tok_rows, capaci...]
    ppermute x1, waiting for transfers between devices: 1.59 us -> 3.55 us  [per_device(): near = lax.ppermute(chunks[1][0], 'group', along(-1))]
    ppermute x2, starting transfers between devices: 4.36 us -> 2.55 us  [homeward(): return lax.ppermute(group_part, 'group', along(-k))]
    ppermute x3, waiting for transfers between devices: 17 us -> 18.6 us  [per_device(): ahead = lax.ppermute(column, 'group', along(1)) if k < n_group - 1 else None]
    ppermute x1, starting transfers between devices: 0.2 us -> 1.43 us  [per_device(): near = lax.ppermute(chunks[1][0], 'group', along(-1))]
  transfers between devices with their start and end apart: 14 -> 17, of which waited for: 9 -> 11; matrix products, arithmetic and copies ran while one was open for 0% -> 0% of each run, Pallas kernels for 41% -> 38%
where the time goes in v7:
time: 102 us
  Pallas kernels  41.3 us (40%)
  waiting for transfers between devices  36.1 us (35%)
  starting transfers between devices  21.6 us (21%)
  other arithmetic  1.2 us (1%)
  local copies, waits for them, and re-layouts  1.05 us (1%)
    pallas_call x4, Pallas kernels, chunk_call(): pl.pallas_call(functools.partial(chunk_kernel, n_blocks, tok_rows, capaci...  31.4 us
    ppermute x3, waiting for transfers between devices, per_device(): ahead = lax.ppermute(column, 'group', along(1)) if k < n_group - 1 else None  18.6 us
    ppermute x4, waiting for transfers between devices, spread(): lax.ppermute(column, 'ingroup', shift(s))  7.67 us
    pallas_call x2, Pallas kernels, weight_call(): pl.pallas_call(functools.partial(weight_kernel, ff, n), grid=(count,), in...  7.32 us
    ppermute x3, starting transfers between devices, per_device(): ahead = lax.ppermute(column, 'group', along(1)) if k < n_group - 1 else None  7.17 us
    ppermute x4, starting transfers between devices, spread(): lax.ppermute(column, 'ingroup', shift(s))  5.97 us
    ppermute x2, waiting for transfers between devices, homeward(): return lax.ppermute(group_part, 'group', along(-k))  5.31 us
    ppermute x3, starting transfers between devices, across(): lax.ppermute(others[(s - 1) * tok_rows:s * tok_rows], 'ingroup', shift(-s))  4.47 us
  transfers between devices with their start and end apart: 17, of which 11 were waited for; matrix products, arithmetic and copies ran while one was open for 0% of the time, Pallas kernels for 38%

profile of v7, /device:TPU:0, one launch (start us, length us, event | category | flops | bytes accessed | tf_op | source)
XLA Modules:
  0.0 102.0 jit_solution(6803396780612204729)
XLA Ops:
  0.6 2.6 %pack.1.refs_0_ = bf16[272,1024]{1,0:T(8,128)(2,1)} custom-call(bf16[128,1024]{1,0:T(8,128)(2,1)} %tokens.1, bf16[128,1024]{1,0:T(8,128)(2,1)} %upstream.1, s32[8,128]{1,0:T(8,128)} %bitcast.5, s32[8,128]{1,0:T(8,128)} %bitcast.6, s32[8,128]{1,0:T(8,128)} %bitcast.7), custom_call_target="tpu_custom_call" | custom-call | tf_op jit(solution)/shard_map/pack/pallas_call | solution.py:54
  3.2 3.1 %collective-permute-start.1 = (bf16[272,1024]{1,0:T(8,128)(2,1)}, bf16[272,1024]{1,0:T(8,128)(2,1)S(1)}, u32[]{:S(2)}, u32[]{:S(2)}) collective-permute-start(bf16[272,1024]{1,0:T(8,128)(2,1)} %pack.1.refs_0_), channel_id=1, source_target_pairs={{0,4},{4,12},{12,8},{8,0},{1,5},{5,13},{13,9},{9,1},{2,6},{6,14},{... | collective-permute-start | bytes 1671176 | tf_op jit(solution)/shard_map/ppermute | solution.py:299
  6.3 1.5 %collective-permute-start = (bf16[272,1024]{1,0:T(8,128)(2,1)}, bf16[272,1024]{1,0:T(8,128)(2,1)S(1)}, u32[]{:S(2)}, u32[]{:S(2)}) collective-permute-start(bf16[272,1024]{1,0:T(8,128)(2,1)} %pack.1.refs_0_), channel_id=1, source_target_pairs={{0,2},{2,0},{1,3},{3,1},{4,6},{6,4},{5,7},{7,5},{8,10},{10,8},{9,1... | collective-permute-start | bytes 1671176 | tf_op jit(solution)/shard_map/ppermute | solution.py:274
  7.8 12.4 %collective-permute-done.1.refs_0_ = bf16[272,1024]{1,0:T(8,128)(2,1)S(1)} collective-permute-done((bf16[272,1024]{1,0:T(8,128)(2,1)}, bf16[272,1024]{1,0:T(8,128)(2,1)S(1)}, u32[]{:S(2)}, u32[]{:S(2)}) %collective-permute-start.1) | collective-permute-done | bytes 557088 | tf_op jit(solution)/shard_map/ppermute | solution.py:299
  20.1 0.4 collective-permute-done.refs_1_
  20.6 2.6 %collective-permute-start.3 = (bf16[272,1024]{1,0:T(8,128)(2,1)S(1)}, bf16[272,1024]{1,0:T(8,128)(2,1)S(1)}, u32[]{:S(2)}, u32[]{:S(2)}) collective-permute-start(bf16[272,1024]{1,0:T(8,128)(2,1)S(1)} %collective-permute-done.1.refs_0_), channel_id=1, source_target_pairs={{0,4},{4,12},{12,8},{8,0},{1,5},{5,13},{13,9},{9,1},{2,6},{6,14},{... | collective-permute-start | bytes 1671176 | tf_op jit(solution)/shard_map/ppermute | solution.py:299
  23.2 1.5 %collective-permute-start.2 = (bf16[272,1024]{1,0:T(8,128)(2,1)S(1)}, bf16[272,1024]{1,0:T(8,128)(2,1)S(1)}, u32[]{:S(2)}, u32[]{:S(2)}) collective-permute-start(bf16[272,1024]{1,0:T(8,128)(2,1)S(1)} %collective-permute-done.1.refs_0_), channel_id=1, source_target_pairs={{0,2},{2,0},{1,3},{3,1},{4,6},{6,4},{5,7},{7,5},{8,10},{10,8},{9,1... | collective-permute-start | bytes 1671176 | tf_op jit(solution)/shard_map/ppermute | solution.py:274
  24.7 0.1 pad_add_fusion.place_ref
  24.7 0.0 copy-start
  24.7 1.1 %copy-done = bf16[272,1024]{1,0:T(8,128)(2,1)S(1)} copy-done((bf16[272,1024]{1,0:T(8,128)(2,1)S(1)}, bf16[272,1024]{1,0:T(8,128)(2,1)}, u32[]{:S(2)}) %copy-start) | copy-done | bytes 557080
  25.8 7.9 %chunk.4 = (bf16[128,1024]{1,0:T(8,128)(2,1)S(1)}, bf16[128,1024]{1,0:T(8,128)(2,1)S(1)}, bf16[4,96,1792]{2,1,0:T(8,128)(2,1)}, bf16[4,96,1792]{2,1,0:T(8,128)(2,1)}) custom-call(s32[2]{0:T(128)S(1)} %pad_add_fusion.place_ref, bf16[272,1024]{1,0:T(8,128)(2,1)S(1)} %copy-done, bf16[272,1024]{1,0:T(8,128)(2,1)S(1)} %collective-permute-done.refs_1_, ...), custom_call_target="tpu_custom_call" | custom-call | flops 1610612736 | bytes 8388608 | tf_op jit(solution)/shard_map/chunk/pallas_call | solution.py:189
  33.7 1.2 %collective-permute-done.3.refs_0_ = bf16[272,1024]{1,0:T(8,128)(2,1)S(1)} collective-permute-done((bf16[272,1024]{1,0:T(8,128)(2,1)S(1)}, bf16[272,1024]{1,0:T(8,128)(2,1)S(1)}, u32[]{:S(2)}, u32[]{:S(2)}) %collective-permute-start.3) | collective-permute-done | bytes 557088 | tf_op jit(solution)/shard_map/ppermute | solution.py:299
  34.9 1.2 %collective-permute-done.2.refs_1_ = bf16[272,1024]{1,0:T(8,128)(2,1)S(1)} collective-permute-done((bf16[272,1024]{1,0:T(8,128)(2,1)S(1)}, bf16[272,1024]{1,0:T(8,128)(2,1)S(1)}, u32[]{:S(2)}, u32[]{:S(2)}) %collective-permute-start.2) | collective-permute-done | bytes 557088 | tf_op jit(solution)/shard_map/ppermute | solution.py:274
  36.1 0.0 collective-permute-start.6
  36.1 1.5 %collective-permute-start.5 = (bf16[272,1024]{1,0:T(8,128)(2,1)S(1)}, bf16[272,1024]{1,0:T(8,128)(2,1)S(1)}, u32[]{:S(2)}, u32[]{:S(2)}) collective-permute-start(bf16[272,1024]{1,0:T(8,128)(2,1)S(1)} %collective-permute-done.3.refs_0_), channel_id=1, source_target_pairs={{0,4},{4,12},{12,8},{8,0},{1,5},{5,13},{13,9},{9,1},{2,6},{6,14},{... | collective-permute-start | bytes 1671176 | tf_op jit(solution)/shard_map/ppermute | solution.py:299
  37.6 1.5 %collective-permute-start.4 = (bf16[272,1024]{1,0:T(8,128)(2,1)S(1)}, bf16[272,1024]{1,0:T(8,128)(2,1)S(1)}, u32[]{:S(2)}, u32[]{:S(2)}) collective-permute-start(bf16[272,1024]{1,0:T(8,128)(2,1)S(1)} %collective-permute-done.3.refs_0_), channel_id=1, source_target_pairs={{0,2},{2,0},{1,3},{3,1},{4,6},{6,4},{5,7},{7,5},{8,10},{10,8},{9,1... | collective-permute-start | bytes 1671176 | tf_op jit(solution)/shard_map/ppermute | solution.py:274
  39.1 7.9 %chunk.5 = (bf16[256,1024]{1,0:T(8,128)(2,1)S(1)}, bf16[4,96,1792]{2,1,0:T(8,128)(2,1)}, bf16[4,96,1792]{2,1,0:T(8,128)(2,1)}) custom-call(s32[2]{0:T(128)S(1)} %pad_add_fusion.place_ref, bf16[272,1024]{1,0:T(8,128)(2,1)S(1)} %collective-permute-done.1.refs_0_, bf16[272,1024]{1,0:T(8,128)(2,1)S(1)} %collective-permute-done.2.refs_1_, ...), custom_call_target="tpu_custom_call" | custom-call | flops 1610612736 | bytes 8388608 | tf_op jit(solution)/shard_map/chunk/pallas_call | solution.py:189
  46.9 5.1 %collective-permute-done.5.refs_0_ = bf16[272,1024]{1,0:T(8,128)(2,1)S(1)} collective-permute-done((bf16[272,1024]{1,0:T(8,128)(2,1)S(1)}, bf16[272,1024]{1,0:T(8,128)(2,1)S(1)}, u32[]{:S(2)}, u32[]{:S(2)}) %collective-permute-start.5) | collective-permute-done | bytes 557088 | tf_op jit(solution)/shard_map/ppermute | solution.py:299
  52.0 0.3 collective-permute-done.4.refs_1_
  52.3 0.0 collective-permute-done.6.refs_4_
  52.3 0.0 collective-permute-start.8
  52.3 1.5 %collective-permute-start.7 = (bf16[272,1024]{1,0:T(8,128)(2,1)S(1)}, bf16[272,1024]{1,0:T(8,128)(2,1)S(1)}, u32[]{:S(2)}, u32[]{:S(2)}) collective-permute-start(bf16[272,1024]{1,0:T(8,128)(2,1)S(1)} %collective-permute-done.5.refs_0_), channel_id=1, source_target_pairs={{0,2},{2,0},{1,3},{3,1},{4,6},{6,4},{5,7},{7,5},{8,10},{10,8},{9,1... | collective-permute-start | bytes 1671176 | tf_op jit(solution)/shard_map/ppermute | solution.py:274
  53.8 7.9 %chunk.6 = (bf16[128,1024]{1,0:T(8,128)(2,1)S(1)}, bf16[128,1024]{1,0:T(8,128)(2,1)S(1)}, bf16[4,96,1792]{2,1,0:T(8,128)(2,1)}, bf16[4,96,1792]{2,1,0:T(8,128)(2,1)}) custom-call(s32[2]{0:T(128)S(1)} %pad_add_fusion.place_ref, bf16[272,1024]{1,0:T(8,128)(2,1)S(1)} %collective-permute-done.3.refs_0_, bf16[272,1024]{1,0:T(8,128)(2,1)S(1)} %collective-permute-done.4.refs_1_, ...), custom_call_target="tpu_custom_call" | custom-call | flops 1610612736 | bytes 8388608 | tf_op jit(solution)/shard_map/chunk/pallas_call | solution.py:189
  61.7 5.7 %collective-permute-done.7.refs_1_ = bf16[272,1024]{1,0:T(8,128)(2,1)S(1)} collective-permute-done((bf16[272,1024]{1,0:T(8,128)(2,1)S(1)}, bf16[272,1024]{1,0:T(8,128)(2,1)S(1)}, u32[]{:S(2)}, u32[]{:S(2)}) %collective-permute-start.7) | collective-permute-done | bytes 557088 | tf_op jit(solution)/shard_map/ppermute | solution.py:274
  67.4 0.0 collective-permute-done.8.refs_5_
  67.4 0.0 collective-permute-start.11
  67.4 1.4 %collective-permute-start.9 = (bf16[256,1024]{1,0:T(8,128)(2,1)S(1)}, bf16[256,1024]{1,0:T(8,128)(2,1)S(1)}, u32[]{:S(2)}, u32[]{:S(2)}) collective-permute-start(bf16[256,1024]{1,0:T(8,128)(2,1)S(1)} %get-tuple-element.118), channel_id=1, source_target_pairs={{0,8},{4,0},{12,4},{8,12},{1,9},{5,1},{13,5},{9,13},{2,10},{6,2},{... | collective-permute-start | bytes 1572872 | tf_op jit(solution)/shard_map/ppermute | solution.py:310
  68.8 1.5 %collective-permute-start.10 = (bf16[128,1024]{1,0:T(8,128)(2,1)S(1)}, bf16[128,1024]{1,0:T(8,128)(2,1)S(1)}, u32[]{:S(2)}, u32[]{:S(2)}) collective-permute-start(bf16[128,1024]{1,0:T(8,128)(2,1)S(1)} %get-tuple-element.121), channel_id=1, source_target_pairs={{0,2},{2,0},{1,3},{3,1},{4,6},{6,4},{5,7},{7,5},{8,10},{10,8},{9,1... | collective-permute-start | bytes 786440 | tf_op jit(solution)/shard_map/ppermute | solution.py:281
  70.3 7.9 %chunk.7 = (bf16[128,1024]{1,0:T(8,128)(2,1)S(1)}, bf16[128,1024]{1,0:T(8,128)(2,1)S(1)}, bf16[4,96,1792]{2,1,0:T(8,128)(2,1)}, bf16[4,96,1792]{2,1,0:T(8,128)(2,1)}) custom-call(s32[2]{0:T(128)S(1)} %pad_add_fusion.place_ref, bf16[272,1024]{1,0:T(8,128)(2,1)S(1)} %collective-permute-done.5.refs_0_, bf16[272,1024]{1,0:T(8,128)(2,1)S(1)} %collective-permute-done.7.refs_1_, ...), custom_call_target="tpu_custom_call" | custom-call | flops 1610612736 | bytes 8388608 | tf_op jit(solution)/shard_map/chunk/pallas_call | solution.py:189
  78.2 0.0 collective-permute-done.10
  78.2 3.5 %collective-permute-done.9 = bf16[256,1024]{1,0:T(8,128)(2,1)S(1)} collective-permute-done((bf16[256,1024]{1,0:T(8,128)(2,1)S(1)}, bf16[256,1024]{1,0:T(8,128)(2,1)S(1)}, u32[]{:S(2)}, u32[]{:S(2)}) %collective-permute-start.9) | collective-permute-done | bytes 524320 | tf_op jit(solution)/shard_map/ppermute | solution.py:310
  81.7 0.0 collective-permute-done.11.refs_6_
  81.7 0.0 collective-permute-start.12
  81.7 0.1 add_convert_fusion.3
  81.8 2.1 %collective-permute-start.14 = (bf16[128,1024]{1,0:T(8,128)(2,1)S(1)}, bf16[128,1024]{1,0:T(8,128)(2,1)S(1)}, u32[]{:S(2)}, u32[]{:S(2)}) collective-permute-start(bf16[128,1024]{1,0:T(8,128)(2,1)S(1)} %add_convert_fusion.3), channel_id=1, source_target_pairs={{0,4},{4,12},{12,8},{8,0},{1,5},{5,13},{13,9},{9,1},{2,6},{6,14},{... | collective-permute-start | bytes 786440 | tf_op jit(solution)/shard_map/ppermute | solution.py:291
  83.9 1.5 %collective-permute-start.13 = (bf16[128,1024]{1,0:T(8,128)(2,1)S(1)}, bf16[128,1024]{1,0:T(8,128)(2,1)S(1)}, u32[]{:S(2)}, u32[]{:S(2)}) collective-permute-start(bf16[128,1024]{1,0:T(8,128)(2,1)S(1)} %get-tuple-element.145), channel_id=1, source_target_pairs={{0,2},{2,0},{1,3},{3,1},{4,6},{6,4},{5,7},{7,5},{8,10},{10,8},{9,1... | collective-permute-start | bytes 786440 | tf_op jit(solution)/shard_map/ppermute | solution.py:281
  85.4 0.1 add_convert_fusion.2
  85.5 0.0 collective-permute-done.12.refs_7_
  85.5 3.7 %weight_grads.2 = (bf16[4,512,256]{2,1,0:T(8,128)(2,1)}, bf16[4,512,256]{2,1,0:T(8,128)(2,1)}, bf16[4,256,512]{2,1,0:T(8,128)(2,1)}) custom-call(bf16[4,96,1792]{2,1,0:T(8,128)(2,1)} %get-tuple-element.134.refs_0_, bf16[4,96,1792]{2,1,0:T(8,128)(2,1)} %get-tuple-element.135.refs_1_, bf16[4,96,1792]{2,1,0:T(8,128)(2,1)} %get-tuple-element.136.refs_2_, ...), custom_call_target="tpu_custom_call" | custom-call | flops 1207959552 | bytes 7077888 | tf_op jit(solution)/shard_map/weight_grads/pallas_call | solution.py:237
  89.2 2.3 %collective-permute-done.14 = bf16[128,1024]{1,0:T(8,128)(2,1)S(1)} collective-permute-done((bf16[128,1024]{1,0:T(8,128)(2,1)S(1)}, bf16[128,1024]{1,0:T(8,128)(2,1)S(1)}, u32[]{:S(2)}, u32[]{:S(2)}) %collective-permute-start.14) | collective-permute-done | bytes 262176 | tf_op jit(solution)/shard_map/ppermute | solution.py:291
  91.5 0.9 collective-permute-done.13
  92.4 0.1 add_convert_fusion.1
  92.5 0.4 collective-permute-start.15
  92.9 1.5 %collective-permute-start.16 = (bf16[128,1024]{1,0:T(8,128)(2,1)S(1)}, bf16[128,1024]{1,0:T(8,128)(2,1)S(1)}, u32[]{:S(2)}, u32[]{:S(2)}) collective-permute-start(bf16[128,1024]{1,0:T(8,128)(2,1)S(1)} %add_convert_fusion.2), channel_id=1, source_target_pairs={{0,2},{2,0},{1,3},{3,1},{4,6},{6,4},{5,7},{7,5},{8,10},{10,8},{9,1... | collective-permute-start | bytes 786440 | tf_op jit(solution)/shard_map/ppermute | solution.py:281
  94.4 3.6 %weight_grads.3 = (bf16[4,512,256]{2,1,0:T(8,128)(2,1)}, bf16[4,512,256]{2,1,0:T(8,128)(2,1)}, bf16[4,256,512]{2,1,0:T(8,128)(2,1)}) custom-call(bf16[4,96,1792]{2,1,0:T(8,128)(2,1)} %get-tuple-element.134.refs_0_, bf16[4,96,1792]{2,1,0:T(8,128)(2,1)} %get-tuple-element.135.refs_1_, ...), custom_call_target="tpu_custom_call", output_to_operand_aliasing={{0}: (8, {}), {1}: (9, {}), {2}: (10, {})} | custom-call | flops 1207959552 | bytes 7077888 | tf_op jit(solution)/shard_map/weight_grads/pallas_call | solution.py:237
  98.1 3.0 %collective-permute-done.15 = bf16[128,1024]{1,0:T(8,128)(2,1)S(1)} collective-permute-done((bf16[128,1024]{1,0:T(8,128)(2,1)S(1)}, bf16[128,1024]{1,0:T(8,128)(2,1)S(1)}, u32[]{:S(2)}, u32[]{:S(2)}) %collective-permute-start.15) | collective-permute-done | bytes 262176 | tf_op jit(solution)/shard_map/ppermute | solution.py:291
  101.1 0.0 collective-permute-done.16
  101.1 0.9 add_convert_fusion
Async XLA Ops:
  3.2 16.9 %collective-permute-start.1 = (bf16[272,1024]{1,0:T(8,128)(2,1)}, bf16[272,1024]{1,0:T(8,128)(2,1)S(1)}, u32[]{:S(2)}, u32[]{:S(2)}) collective-permute-start(bf16[272,1024]{1,0:T(8,128)(2,1)} %pack.1.refs_0_), channel_id=1, source_target_pairs={{0,4},{4,12},{12,8},{8,0},{1,5},{5,13},{13,9},{9,1},{2,6},{6,14},{... | collective-permute-start | bytes 1671176 | tf_op jit(solution)/shard_map/ppermute | solution.py:299
  6.3 14.3 %collective-permute-start = (bf16[272,1024]{1,0:T(8,128)(2,1)}, bf16[272,1024]{1,0:T(8,128)(2,1)S(1)}, u32[]{:S(2)}, u32[]{:S(2)}) collective-permute-start(bf16[272,1024]{1,0:T(8,128)(2,1)} %pack.1.refs_0_), channel_id=1, source_target_pairs={{0,2},{2,0},{1,3},{3,1},{4,6},{6,4},{5,7},{7,5},{8,10},{10,8},{9,1... | collective-permute-start | bytes 1671176 | tf_op jit(solution)/shard_map/ppermute | solution.py:274
  20.6 14.3 %collective-permute-start.3 = (bf16[272,1024]{1,0:T(8,128)(2,1)S(1)}, bf16[272,1024]{1,0:T(8,128)(2,1)S(1)}, u32[]{:S(2)}, u32[]{:S(2)}) collective-permute-start(bf16[272,1024]{1,0:T(8,128)(2,1)S(1)} %collective-permute-done.1.refs_0_), channel_id=1, source_target_pairs={{0,4},{4,12},{12,8},{8,0},{1,5},{5,13},{13,9},{9,1},{2,6},{6,14},{... | collective-permute-start | bytes 1671176 | tf_op jit(solution)/shard_map/ppermute | solution.py:299
  23.2 12.9 %collective-permute-start.2 = (bf16[272,1024]{1,0:T(8,128)(2,1)S(1)}, bf16[272,1024]{1,0:T(8,128)(2,1)S(1)}, u32[]{:S(2)}, u32[]{:S(2)}) collective-permute-start(bf16[272,1024]{1,0:T(8,128)(2,1)S(1)} %collective-permute-done.1.refs_0_), channel_id=1, source_target_pairs={{0,2},{2,0},{1,3},{3,1},{4,6},{6,4},{5,7},{7,5},{8,10},{10,8},{9,1... | collective-permute-start | bytes 1671176 | tf_op jit(solution)/shard_map/ppermute | solution.py:274
  24.7 1.1 %copy-start = (bf16[272,1024]{1,0:T(8,128)(2,1)S(1)}, bf16[272,1024]{1,0:T(8,128)(2,1)}, u32[]{:S(2)}) copy-start(bf16[272,1024]{1,0:T(8,128)(2,1)} %pack.1.refs_0_) | copy-start | bytes 1671172
  36.1 16.3 %collective-permute-start.6 = (bf16[4,96,1792]{2,1,0:T(8,128)(2,1)}, bf16[4,96,1792]{2,1,0:T(8,128)(2,1)S(1)}, u32[]{:S(2)}, u32[]{:S(2)}) collective-permute-start(bf16[4,96,1792]{2,1,0:T(8,128)(2,1)} %get-tuple-element.95), channel_id=1, source_target_pairs={{0,1},{1,0},{2,3},{3,2},{4,5},{5,4},{6,7},{7,6},{8,9},{9,8},{10,11... | collective-permute-start | bytes 4128776 | tf_op jit(solution)/shard_map/ppermute | solution.py:295
  36.1 15.9 %collective-permute-start.5 = (bf16[272,1024]{1,0:T(8,128)(2,1)S(1)}, bf16[272,1024]{1,0:T(8,128)(2,1)S(1)}, u32[]{:S(2)}, u32[]{:S(2)}) collective-permute-start(bf16[272,1024]{1,0:T(8,128)(2,1)S(1)} %collective-permute-done.3.refs_0_), channel_id=1, source_target_pairs={{0,4},{4,12},{12,8},{8,0},{1,5},{5,13},{13,9},{9,1},{2,6},{6,14},{... | collective-permute-start | bytes 1671176 | tf_op jit(solution)/shard_map/ppermute | solution.py:299
  37.6 14.8 %collective-permute-start.4 = (bf16[272,1024]{1,0:T(8,128)(2,1)S(1)}, bf16[272,1024]{1,0:T(8,128)(2,1)S(1)}, u32[]{:S(2)}, u32[]{:S(2)}) collective-permute-start(bf16[272,1024]{1,0:T(8,128)(2,1)S(1)} %collective-permute-done.3.refs_0_), channel_id=1, source_target_pairs={{0,2},{2,0},{1,3},{3,1},{4,6},{6,4},{5,7},{7,5},{8,10},{10,8},{9,1... | collective-permute-start | bytes 1671176 | tf_op jit(solution)/shard_map/ppermute | solution.py:274
  52.3 15.0 %collective-permute-start.8 = (bf16[4,96,1792]{2,1,0:T(8,128)(2,1)}, bf16[4,96,1792]{2,1,0:T(8,128)(2,1)S(1)}, u32[]{:S(2)}, u32[]{:S(2)}) collective-permute-start(bf16[4,96,1792]{2,1,0:T(8,128)(2,1)} %get-tuple-element.107), channel_id=1, source_target_pairs={{0,1},{1,0},{2,3},{3,2},{4,5},{5,4},{6,7},{7,6},{8,9},{9,8},{10,11... | collective-permute-start | bytes 4128776 | tf_op jit(solution)/shard_map/ppermute | solution.py:295
  52.3 15.0 %collective-permute-start.7 = (bf16[272,1024]{1,0:T(8,128)(2,1)S(1)}, bf16[272,1024]{1,0:T(8,128)(2,1)S(1)}, u32[]{:S(2)}, u32[]{:S(2)}) collective-permute-start(bf16[272,1024]{1,0:T(8,128)(2,1)S(1)} %collective-permute-done.5.refs_0_), channel_id=1, source_target_pairs={{0,2},{2,0},{1,3},{3,1},{4,6},{6,4},{5,7},{7,5},{8,10},{10,8},{9,1... | collective-permute-start | bytes 1671176 | tf_op jit(solution)/shard_map/ppermute | solution.py:274
  67.4 14.3 %collective-permute-start.11 = (bf16[4,96,1792]{2,1,0:T(8,128)(2,1)}, bf16[4,96,1792]{2,1,0:T(8,128)(2,1)S(1)}, u32[]{:S(2)}, u32[]{:S(2)}) collective-permute-start(bf16[4,96,1792]{2,1,0:T(8,128)(2,1)} %get-tuple-element.123), channel_id=1, source_target_pairs={{0,1},{1,0},{2,3},{3,2},{4,5},{5,4},{6,7},{7,6},{8,9},{9,8},{10,11... | collective-permute-start | bytes 4128776 | tf_op jit(solution)/shard_map/ppermute | solution.py:295
  67.4 14.3 %collective-permute-start.9 = (bf16[256,1024]{1,0:T(8,128)(2,1)S(1)}, bf16[256,1024]{1,0:T(8,128)(2,1)S(1)}, u32[]{:S(2)}, u32[]{:S(2)}) collective-permute-start(bf16[256,1024]{1,0:T(8,128)(2,1)S(1)} %get-tuple-element.118), channel_id=1, source_target_pairs={{0,8},{4,0},{12,4},{8,12},{1,9},{5,1},{13,5},{9,13},{2,10},{6,2},{... | collective-permute-start | bytes 1572872 | tf_op jit(solution)/shard_map/ppermute | solution.py:310
  68.8 9.4 %collective-permute-start.10 = (bf16[128,1024]{1,0:T(8,128)(2,1)S(1)}, bf16[128,1024]{1,0:T(8,128)(2,1)S(1)}, u32[]{:S(2)}, u32[]{:S(2)}) collective-permute-start(bf16[128,1024]{1,0:T(8,128)(2,1)S(1)} %get-tuple-element.121), channel_id=1, source_target_pairs={{0,2},{2,0},{1,3},{3,1},{4,6},{6,4},{5,7},{7,5},{8,10},{10,8},{9,1... | collective-permute-start | bytes 786440 | tf_op jit(solution)/shard_map/ppermute | solution.py:281
  81.7 3.8 %collective-permute-start.12 = (bf16[4,96,1792]{2,1,0:T(8,128)(2,1)}, bf16[4,96,1792]{2,1,0:T(8,128)(2,1)S(1)}, u32[]{:S(2)}, u32[]{:S(2)}) collective-permute-start(bf16[4,96,1792]{2,1,0:T(8,128)(2,1)} %get-tuple-element.141), channel_id=1, source_target_pairs={{0,1},{1,0},{2,3},{3,2},{4,5},{5,4},{6,7},{7,6},{8,9},{9,8},{10,11... | collective-permute-start | bytes 4128776 | tf_op jit(solution)/shard_map/ppermute | solution.py:295
  81.8 9.7 %collective-permute-start.14 = (bf16[128,1024]{1,0:T(8,128)(2,1)S(1)}, bf16[128,1024]{1,0:T(8,128)(2,1)S(1)}, u32[]{:S(2)}, u32[]{:S(2)}) collective-permute-start(bf16[128,1024]{1,0:T(8,128)(2,1)S(1)} %add_convert_fusion.3), channel_id=1, source_target_pairs={{0,4},{4,12},{12,8},{8,0},{1,5},{5,13},{13,9},{9,1},{2,6},{6,14},{... | collective-permute-start | bytes 786440 | tf_op jit(solution)/shard_map/ppermute | solution.py:291
  83.9 8.4 %collective-permute-start.13 = (bf16[128,1024]{1,0:T(8,128)(2,1)S(1)}, bf16[128,1024]{1,0:T(8,128)(2,1)S(1)}, u32[]{:S(2)}, u32[]{:S(2)}) collective-permute-start(bf16[128,1024]{1,0:T(8,128)(2,1)S(1)} %get-tuple-element.145), channel_id=1, source_target_pairs={{0,2},{2,0},{1,3},{3,1},{4,6},{6,4},{5,7},{7,5},{8,10},{10,8},{9,1... | collective-permute-start | bytes 786440 | tf_op jit(solution)/shard_map/ppermute | solution.py:281
  92.5 8.6 %collective-permute-start.15 = (bf16[128,1024]{1,0:T(8,128)(2,1)S(1)}, bf16[128,1024]{1,0:T(8,128)(2,1)S(1)}, u32[]{:S(2)}, u32[]{:S(2)}) collective-permute-start(bf16[128,1024]{1,0:T(8,128)(2,1)S(1)} %add_convert_fusion.1), channel_id=1, source_target_pairs={{0,4},{4,12},{12,8},{8,0},{1,5},{5,13},{13,9},{9,1},{2,6},{6,14},{... | collective-permute-start | bytes 786440 | tf_op jit(solution)/shard_map/ppermute | solution.py:291
  92.9 8.2 %collective-permute-start.16 = (bf16[128,1024]{1,0:T(8,128)(2,1)S(1)}, bf16[128,1024]{1,0:T(8,128)(2,1)S(1)}, u32[]{:S(2)}, u32[]{:S(2)}) collective-permute-start(bf16[128,1024]{1,0:T(8,128)(2,1)S(1)} %add_convert_fusion.2), channel_id=1, source_target_pairs={{0,2},{2,0},{1,3},{3,1},{4,6},{6,4},{5,7},{7,5},{8,10},{10,8},{9,1... | collective-permute-start | bytes 786440 | tf_op jit(solution)/shard_map/ppermute | solution.py:281

commit v8 on v6

--- a/solution.py
+++ b/solution.py
@@ -9,7 +9,7 @@
 
 GROUPS_TOK = 4
 ROUTE_ROWS = 16
-VMEM_LIMIT = 32 * 1024 * 1024
+VMEM_LIMIT = 24 * 1024 * 1024
 
 
 def dot(a, b, contract):
@@ -18,6 +18,10 @@
 
 def in_hbm(v):
     return pltpu.with_memory_space_constraint(v, pltpu.HBM)
+
+
+def in_vmem(v):
+    return pltpu.with_memory_space_constraint(v, pltpu.VMEM)
 
 
 def gated_parts(pre_gate):
@@ -55,8 +59,9 @@
         pack_kernel,
         in_specs=[hbm] * 2 + [vmem] * 3,
         out_specs=vmem,
-        out_shape=jax.ShapeDtypeStruct((2 * tok_rows + ROUTE_ROWS, width), jnp.bfloat16),
+        out_shape=pltpu.VMEM((2 * tok_rows + ROUTE_ROWS, width), jnp.bfloat16),
         scratch_shapes=[pltpu.SemaphoreType.DMA((2,))],
+        compiler_params=pltpu.CompilerParams(vmem_limit_bytes=VMEM_LIMIT),
         name="pack",
     )(*operands)
 
@@ -79,43 +84,38 @@
     return pairs
 
 
+def load_kernel(*refs):
+    n = len(refs) // 2
+    copies = [pltpu.make_async_copy(refs[i], refs[n + i], refs[-1].at[i]) for i in range(n)]
+    for copy in copies:
+        copy.start()
+    for copy in copies:
+        copy.wait()
+
+
+def load_call(arrays):
+    hbm, vmem = (pl.BlockSpec(memory_space=m) for m in (pltpu.HBM, pltpu.VMEM))
+    return pl.pallas_call(
+        load_kernel,
+        in_specs=[hbm] * len(arrays),
+        out_specs=[vmem] * len(arrays),
+        out_shape=[pltpu.VMEM(v.shape, v.dtype) for v in arrays],
+        scratch_shapes=[pltpu.SemaphoreType.DMA((len(arrays),))],
+        compiler_params=pltpu.CompilerParams(vmem_limit_bytes=VMEM_LIMIT),
+        name="load",
+    )(*[in_hbm(v) for v in arrays])
+
+
 def chunk_kernel(n_blocks, tok_rows, capacity, rows, top_count, per_group, first_ref, *refs):
-    payloads, weights = refs[:n_blocks], refs[n_blocks : n_blocks + 3]
-    parts, kept = refs[n_blocks + 3 : -16], refs[-16:-13]
-    x_all, u_all, routes, w_gate, w_up, w_down, back_all, x_rows, s_rows, hids = refs[-13:-3]
-    sem_in, sem_weight, sem_out = refs[-3:]
+    payloads = refs[:n_blocks]
+    w_gate, w_up, w_down = refs[n_blocks : n_blocks + 3]
+    parts = refs[n_blocks + 3 : -4]
+    x_rows, s_rows, hids, back_all = refs[-4:]
     experts, width, ff = w_gate.shape
-
-    def fetch(b, start, size, to, i):
-        copy = pltpu.make_async_copy(payloads[b].at[pl.ds(start, size), :], to, sem_in.at[b, i])
-        copy.start()
-        return copy
-
-    here = [pl.ds(b * tok_rows, tok_rows) for b in range(n_blocks)]
-    get_route = [fetch(b, 2 * tok_rows, ROUTE_ROWS, routes.at[b], 0) for b in range(n_blocks)]
-    get_x = [fetch(b, 0, tok_rows, x_all.at[here[b], :], 1) for b in range(n_blocks)]
-    get_u = [fetch(b, tok_rows, tok_rows, u_all.at[here[b], :], 2) for b in range(n_blocks)]
-    get_weight = [
-        [
-            pltpu.make_async_copy(src.at[e], to.at[e], sem_weight.at[e, i])
-            for i, (src, to) in enumerate(zip(weights, (w_gate, w_up, w_down)))
-        ]
-        for e in range(experts)
-    ]
-    for copies in get_weight:
-        for copy in copies:
-            copy.start()
-    keep = []
-
-    def keep_out(i, e, src):
-        copy = pltpu.make_async_copy(src.at[e], kept[i].at[e], sem_out.at[e, i])
-        copy.start()
-        keep.append(copy)
 
     pairs = []
     for b in range(n_blocks):
-        get_route[b].wait()
-        route = routes[b].astype(jnp.float32)
+        route = payloads[b][2 * tok_rows : 2 * tok_rows + ROUTE_ROWS, :].astype(jnp.float32)
         pairs.append(
             route_keys(route, first_ref[0], experts, capacity, rows, b * capacity, tok_rows, top_count, per_group)
         )
@@ -131,22 +131,16 @@
     hot = hot.astype(jnp.bfloat16)
     row_gate = jnp.sum(gate_hot, axis=1, keepdims=True)
 
-    for copy in get_x:
-        copy.wait()
-    gathered = dot(hot, x_all[...], (1, 0)).astype(jnp.bfloat16)
+    x_all = jnp.concatenate([payload[:tok_rows, :] for payload in payloads], axis=0)
+    gathered = dot(hot, x_all, (1, 0)).astype(jnp.bfloat16)
     for e in range(experts):
         x_rows[e] = gathered[e * rows : (e + 1) * rows, :]
-        keep_out(0, e, x_rows)
-    for copy in get_u:
-        copy.wait()
-    scaled = (dot(hot, u_all[...], (1, 0)) * row_gate).astype(jnp.bfloat16)
+    u_all = jnp.concatenate([payload[tok_rows : 2 * tok_rows, :] for payload in payloads], axis=0)
+    scaled = (dot(hot, u_all, (1, 0)) * row_gate).astype(jnp.bfloat16)
     for e in range(experts):
         s_rows[e] = scaled[e * rows : (e + 1) * rows, :]
-        keep_out(1, e, s_rows)
 
     for e in range(experts):
-        for copy in get_weight[e]:
-            copy.wait()
         pre_gate = dot(x_rows[e], w_gate[e], (1, 0))
         pre_up = dot(x_rows[e], w_up[e], (1, 0))
         grad_hidden = dot(s_rows[e], w_down[e], (1, 1))
@@ -156,7 +150,6 @@
         hids[e, :, :ff] = grad_gate_pre
         hids[e, :, ff : 2 * ff] = grad_up_pre
         hids[e, :, 2 * ff :] = (active * pre_up).astype(jnp.bfloat16)
-        keep_out(2, e, hids)
         back = dot(grad_gate_pre, w_gate[e], (1, 1)) + dot(grad_up_pre, w_up[e], (1, 1))
         back_all[e * rows : (e + 1) * rows, :] = back.astype(jnp.bfloat16)
 
@@ -165,8 +158,6 @@
     for part in parts:
         part[...] = summed[start : start + part.shape[0], :]
         start += part.shape[0]
-    for copy in keep:
-        copy.wait()
 
 
 def chunk_call(payloads, first_expert, weights, tok_rows, capacity, rows, top_count, per_group, joined):
@@ -175,28 +166,14 @@
     experts, width, ff = weights[0].shape
     part_shapes = [(n_tok, width)] if joined else [(tok_rows, width), (n_tok - tok_rows, width)]
     kept_shapes = [(experts, rows, width), (experts, rows, width), (experts, rows, 3 * ff)]
-    smem, vmem, hbm = (pl.BlockSpec(memory_space=m) for m in (pltpu.SMEM, pltpu.VMEM, pltpu.HBM))
-    buffer = lambda *shape: pltpu.VMEM(shape, jnp.bfloat16)
-    semaphores = lambda *shape: pltpu.SemaphoreType.DMA(shape)
+    smem, vmem = (pl.BlockSpec(memory_space=m) for m in (pltpu.SMEM, pltpu.VMEM))
+    out_shapes = part_shapes + kept_shapes
     return pl.pallas_call(
         functools.partial(chunk_kernel, n_blocks, tok_rows, capacity, rows, top_count, per_group),
-        in_specs=[smem] + [pl.BlockSpec(memory_space=pl.ANY)] * n_blocks + [hbm] * 3,
-        out_specs=[vmem] * len(part_shapes) + [hbm] * 3,
-        out_shape=[jax.ShapeDtypeStruct(shape, jnp.bfloat16) for shape in part_shapes]
-        + [pltpu.HBM(shape, jnp.bfloat16) for shape in kept_shapes],
-        scratch_shapes=[
-            buffer(n_tok, width),
-            buffer(n_tok, width),
-            buffer(n_blocks, ROUTE_ROWS, width),
-            buffer(experts, width, ff),
-            buffer(experts, width, ff),
-            buffer(experts, ff, width),
-            buffer(experts * rows, width),
-            *[buffer(*shape) for shape in kept_shapes],
-            semaphores(n_blocks, 3),
-            semaphores(experts, 3),
-            semaphores(experts, 3),
-        ],
+        in_specs=[smem] + [vmem] * (n_blocks + 3),
+        out_specs=[vmem] * len(out_shapes),
+        out_shape=[pltpu.VMEM(shape, jnp.bfloat16) for shape in out_shapes],
+        scratch_shapes=[pltpu.VMEM((experts * rows, width), jnp.bfloat16)],
         compiler_params=pltpu.CompilerParams(vmem_limit_bytes=VMEM_LIMIT),
         cost_estimate=pl.CostEstimate(
             flops=2 * experts * rows * width * (5 * ff + 3 * n_tok),
@@ -204,61 +181,72 @@
             transcendentals=0,
         ),
         name="chunk",
-    )(first_expert, *payloads, *[in_hbm(w) for w in weights])
-
-
-def halves_of(n, ff, refs):
-    cat = lambda part: jnp.concatenate([ref[0] for ref in part], axis=0)
-    x_rows, s_rows, hid = cat(refs[:n]), cat(refs[n : 2 * n]), cat(refs[2 * n : 3 * n])
+    )(first_expert, *[in_vmem(v) for v in payloads], *[in_vmem(w) for w in weights])
+
+
+def halves_of(n, e, side, refs):
+    depth = refs[0].shape[2] // 2
+    cols = pl.ds(pl.multiple_of(side * depth, depth), depth)
+    cat = lambda parts: jnp.concatenate(parts, axis=0)
+    x_rows, s_rows = (cat([ref[e, :, cols] for ref in refs[i * n : (i + 1) * n]]) for i in range(2))
+    hid = cat([ref[e] for ref in refs[2 * n : 3 * n]])
+    ff = hid.shape[1] // 3
     return dot(x_rows, hid[:, : 2 * ff], (0, 0)), dot(hid[:, 2 * ff :], s_rows, (0, 0))
 
 
-def send_kernel(n, ff, half_ref, *refs):
-    gate_up, down = halves_of(n, ff, refs)
+def send_kernel(n, side_ref, *refs):
     out = refs[3 * n]
-    depth = gate_up.shape[0]
-    out[0, :depth, :] = gate_up.astype(jnp.bfloat16)
-    out[0, depth:, :] = down.astype(jnp.bfloat16)
-
-
-def keep_kernel(n, ff, half_ref, *refs):
-    gate_up, down = halves_of(n, ff, refs)
-    got = refs[3 * n]
-    out_gate, out_up, out_down = refs[3 * n + 1 :]
-    depth = gate_up.shape[0]
-    gate_up = gate_up + got[0, :depth, :].astype(jnp.float32)
-    out_gate[0] = gate_up[:, :ff].astype(jnp.bfloat16)
-    out_up[0] = gate_up[:, ff:].astype(jnp.bfloat16)
-    out_down[0] = (down + got[0, depth:, :].astype(jnp.float32)).astype(jnp.bfloat16)
-
-
-def weight_call(half, x_rows, s_rows, hids, got=None):
+    for e in range(out.shape[0]):
+        gate_up, down = halves_of(n, e, side_ref[0], refs)
+        depth = gate_up.shape[0]
+        out[e, :depth, :] = gate_up.astype(jnp.bfloat16)
+        out[e, depth:, :] = down.astype(jnp.bfloat16)
+
+
+def keep_kernel(n, side_ref, *refs):
+    got, outs = refs[3 * n], refs[3 * n + 1 : 3 * n + 4]
+    buffers, sem = refs[3 * n + 4 : 3 * n + 7], refs[3 * n + 7]
+    copies = []
+    for e in range(got.shape[0]):
+        gate_up, down = halves_of(n, e, side_ref[0], refs)
+        depth = gate_up.shape[0]
+        ff = down.shape[0]
+        gate_up = gate_up + got[e, :depth, :].astype(jnp.float32)
+        buffers[0][e] = gate_up[:, :ff].astype(jnp.bfloat16)
+        buffers[1][e] = gate_up[:, ff:].astype(jnp.bfloat16)
+        buffers[2][e] = (down + got[e, depth:, :].astype(jnp.float32)).astype(jnp.bfloat16)
+        for i in range(3):
+            copy = pltpu.make_async_copy(buffers[i].at[e], outs[i].at[e], sem.at[e, i])
+            copy.start()
+            copies.append(copy)
+    for copy in copies:
+        copy.wait()
+
+
+def weight_call(side, x_rows, s_rows, hids, got=None):
     n = len(x_rows)
     experts, rows, width = x_rows[0].shape
     ff = hids[0].shape[2] // 3
     depth = width // 2
-    piece = lambda shape: pl.BlockSpec((1,) + shape, lambda e, half: (e, 0, 0))
-    split = pl.BlockSpec((1, rows, depth), lambda e, half: (e, 0, half[0]))
-    in_specs = [split] * (2 * n) + [piece((rows, 3 * ff))] * n
-    operands = [in_hbm(v) for v in (*x_rows, *s_rows, *hids)]
-    packed = (depth + ff, depth)
+    smem, vmem = (pl.BlockSpec(memory_space=m) for m in (pltpu.SMEM, pltpu.VMEM))
+    operands = [*x_rows, *s_rows, *hids]
+    scratch = []
     if got is None:
-        kernel = send_kernel
-        out_specs = piece(packed)
-        out_shape = jax.ShapeDtypeStruct((experts,) + packed, jnp.bfloat16)
+        kernel, out_specs = send_kernel, vmem
+        out_shape = pltpu.VMEM((experts, depth + ff, depth), jnp.bfloat16)
     else:
         kernel = keep_kernel
-        in_specs = in_specs + [piece(packed)]
         operands = operands + [got]
-        shapes = [(depth, ff), (depth, ff), (ff, depth)]
-        out_specs = [piece(s) for s in shapes]
-        out_shape = [jax.ShapeDtypeStruct((experts,) + s, jnp.bfloat16) for s in shapes]
+        shapes = [(experts, depth, ff), (experts, depth, ff), (experts, ff, depth)]
+        out_specs = [pl.BlockSpec(memory_space=pl.ANY)] * 3
+        out_shape = [jax.ShapeDtypeStruct(s, jnp.bfloat16) for s in shapes]
+        scratch = [pltpu.VMEM(s, jnp.bfloat16) for s in shapes] + [pltpu.SemaphoreType.DMA((experts, 3))]
     return pl.pallas_call(
-        functools.partial(kernel, n, ff),
-        grid_spec=pltpu.PrefetchScalarGridSpec(
-            num_scalar_prefetch=1, grid=(experts,), in_specs=in_specs, out_specs=out_specs
-        ),
+        functools.partial(kernel, n),
+        in_specs=[smem] + [vmem] * len(operands),
+        out_specs=out_specs,
         out_shape=out_shape,
+        scratch_shapes=scratch,
         compiler_params=pltpu.CompilerParams(vmem_limit_bytes=VMEM_LIMIT),
         cost_estimate=pl.CostEstimate(
             flops=2 * experts * n * rows * 3 * ff * depth,
@@ -266,7 +254,7 @@
             transcendentals=0,
         ),
         name="weight_grads",
-    )(half, *operands)
+    )(side, *[in_vmem(v) for v in operands])
 
 
 def per_device(tokens, upstream, expert_ids, gate_fixed, slots, w_gate, w_up, w_down):
@@ -282,7 +270,7 @@
     z, x, core = (lax.axis_index(a) for a in ("group", "ingroup", "dp"))
     first_expert = ((z * n_ingroup + x) * local_experts).astype(jnp.int32).reshape(1)
     half = core.astype(jnp.int32).reshape(1)
-    weights = (w_gate, w_up, w_down)
+    weights = load_call((w_gate, w_up, w_down))
     wide = lambda v: v.astype(jnp.float32)
     tie = lambda *trees: lax.optimization_barrier(trees)
     order = ring_order(n_group)
@@ -316,7 +304,7 @@
         pair = spread(column)
         if k > 0:
             chunks[k - 1] = chunk(blocks[k - 1], k - 1 == 1)
-        blocks[k], column, chunks = tie(pair, ahead, chunks)
+        blocks[k], column, chunks, weights = tie(pair, ahead, chunks, weights)
 
     last = n_group - 1
     for k in range(2, last - 1):

time: 96.4 us -> 103 us (1.068)
  local copies, waits for them, and re-layouts: 1.05 us -> 28.4 us
  Pallas kernels: 41.8 us -> 26.9 us
  waiting for transfers between devices: 29.1 us -> 23.3 us
    unnamed x2 -> x72, local copies, waits for them, and re-layouts: 1.05 us -> 28.4 us
    ppermute x3, waiting for transfers between devices: 17 us -> 4.61 us  [per_device(): ahead = lax.ppermute(column, 'group', along(1)) if k < n_group - 1 else None]
    pallas_call x4, Pallas kernels: 28.6 us -> 17.7 us  [chunk_call(): pl.pallas_call(functools.partial(chunk_kernel, n_blocks, tok_rows, capaci...]
    ppermute x4, waiting for transfers between devices: 6.66 us -> 12.6 us  [spread(): lax.ppermute(column, 'ingroup', shift(s))]
    pallas_call x2 -> x3, Pallas kernels: 10.6 us -> 7.45 us  [the longest x2 4.57 us: weight_call(): pl.pallas_call(functools.partial(kernel, n), in_specs=[smem] + [vmem] * l...]
    ppermute x3, starting transfers between devices: 7.17 us -> 4.1 us  [per_device(): ahead = lax.ppermute(column, 'group', along(1)) if k < n_group - 1 else None]
    ppermute x2, waiting for transfers between devices: 0.01 us -> 2.2 us  [homeward(): return lax.ppermute(group_part, 'group', along(-k))]
    ppermute x1, starting transfers between devices: 0.2 us -> 1.66 us  [per_device(): near = lax.ppermute(chunks[1][0], 'group', along(-1))]
  transfers between devices with their start and end apart: 14 -> 14, of which waited for: 9 -> 11; matrix products, arithmetic and copies ran while one was open for 0% -> 0% of each run, Pallas kernels for 41% -> 25%
where the time goes in v8:
time: 103 us; the launch traced here: 102 us
  local copies, waits for them, and re-layouts  28.4 us (28%)
  Pallas kernels  26.9 us (26%)
  waiting for transfers between devices  23.3 us (23%)
  starting transfers between devices  21.3 us (21%)
  other arithmetic  1.13 us (1%)
    unnamed x72, local copies, waits for them, and re-layouts  28.4 us
    pallas_call x4, Pallas kernels, chunk_call(): pl.pallas_call(functools.partial(chunk_kernel, n_blocks, tok_rows, capaci...  17.7 us
    ppermute x4, waiting for transfers between devices, spread(): lax.ppermute(column, 'ingroup', shift(s))  12.6 us
    ppermute x4, starting transfers between devices, spread(): lax.ppermute(column, 'ingroup', shift(s))  5.83 us
    ppermute x2, starting transfers between devices, homeward(): return lax.ppermute(group_part, 'group', along(-k))  5.64 us
    ppermute x3, waiting for transfers between devices, per_device(): ahead = lax.ppermute(column, 'group', along(1)) if k < n_group - 1 else None  4.61 us
    pallas_call x2, Pallas kernels, weight_call(): pl.pallas_call(functools.partial(kernel, n), in_specs=[smem] + [vmem] * l...  4.57 us
    ppermute x3, starting transfers between devices, per_device(): ahead = lax.ppermute(column, 'group', along(1)) if k < n_group - 1 else None  4.1 us
  transfers between devices with their start and end apart: 14, of which 11 were waited for; matrix products, arithmetic and copies ran while one was open for 0% of the time, Pallas kernels for 25%

profile of v8, /device:TPU:0, one launch (start us, length us, event | category | flops | bytes accessed | tf_op | source)
XLA Modules:
  0.0 101.9 jit_solution(15159466563872042159)
XLA Ops:
  0.6 1.8 %pack.1.refs_0_ = bf16[272,1024]{1,0:T(8,128)(2,1)S(1)} custom-call(bf16[128,1024]{1,0:T(8,128)(2,1)} %tokens.1, bf16[128,1024]{1,0:T(8,128)(2,1)} %upstream.1, s32[8,128]{1,0:T(8,128)} %bitcast.5, s32[8,128]{1,0:T(8,128)} %bitcast.6, s32[8,128]{1,0:T(8,128)} %bitcast.7), custom_call_target="tpu_custom_call" | custom-call | tf_op jit(solution)/shard_map/pack/pallas_call | solution.py:58
  2.4 3.0 %collective-permute-start = (bf16[272,1024]{1,0:T(8,128)(2,1)S(1)}, bf16[272,1024]{1,0:T(8,128)(2,1)S(1)}, u32[]{:S(2)}, u32[]{:S(2)}) collective-permute-start(bf16[272,1024]{1,0:T(8,128)(2,1)S(1)} %pack.1.refs_0_), channel_id=1, source_target_pairs={{0,2},{2,0},{1,3},{3,1},{4,6},{6,4},{5,7},{7,5},{8,10},{10,8},{9,1... | collective-permute-start | bytes 1671176 | tf_op jit(solution)/shard_map/ppermute | solution.py:281
  5.4 1.6 %collective-permute-start.1 = (bf16[272,1024]{1,0:T(8,128)(2,1)S(1)}, bf16[272,1024]{1,0:T(8,128)(2,1)}, u32[]{:S(2)}, u32[]{:S(2)}) collective-permute-start(bf16[272,1024]{1,0:T(8,128)(2,1)S(1)} %pack.1.refs_0_), channel_id=1, source_target_pairs={{0,4},{4,12},{12,8},{8,0},{1,5},{5,13},{13,9},{9,1},{2,6},{6,14},{... | collective-permute-start | bytes 1671176 | tf_op jit(solution)/shard_map/ppermute | solution.py:303
  7.0 2.9 %load.1 = (bf16[4,1024,256]{2,1,0:T(8,128)(2,1)S(1)}, bf16[4,1024,256]{2,1,0:T(8,128)(2,1)S(1)}, bf16[4,256,1024]{2,1,0:T(8,128)(2,1)S(1)}) custom-call(bf16[4,1024,256]{2,1,0:T(8,128)(2,1)} %refs_0_.1, bf16[4,1024,256]{2,1,0:T(8,128)(2,1)} %refs_1_.1, bf16[4,256,1024]{2,1,0:T(8,128)(2,1)} %refs_2_.1), custom_call_target="tpu_custom_call" | custom-call | tf_op jit(solution)/shard_map/load/pallas_call | solution.py:98
  9.9 1.3 %copy-done = bf16[4,1024,256]{2,1,0:T(8,128)(2,1)} copy-done((bf16[4,1024,256]{2,1,0:T(8,128)(2,1)}, bf16[4,1024,256]{2,1,0:T(8,128)(2,1)S(1)}, u32[]{:S(2)}) %copy-start) | copy-done | bytes 2097176
  11.2 1.4 %copy-done.2 = bf16[4,256,1024]{2,1,0:T(8,128)(2,1)} copy-done((bf16[4,256,1024]{2,1,0:T(8,128)(2,1)}, bf16[4,256,1024]{2,1,0:T(8,128)(2,1)S(1)}, u32[]{:S(2)}) %copy-start.2) | copy-done | bytes 2097176
  12.6 5.4 %collective-permute-done.refs_1_ = bf16[272,1024]{1,0:T(8,128)(2,1)S(1)} collective-permute-done((bf16[272,1024]{1,0:T(8,128)(2,1)S(1)}, bf16[272,1024]{1,0:T(8,128)(2,1)S(1)}, u32[]{:S(2)}, u32[]{:S(2)}) %collective-permute-start) | collective-permute-done | bytes 557088 | tf_op jit(solution)/shard_map/ppermute | solution.py:281
  18.1 0.8 copy-done.26
  18.9 1.7 %collective-permute-done.1.refs_0_ = bf16[272,1024]{1,0:T(8,128)(2,1)} collective-permute-done((bf16[272,1024]{1,0:T(8,128)(2,1)S(1)}, bf16[272,1024]{1,0:T(8,128)(2,1)}, u32[]{:S(2)}, u32[]{:S(2)}) %collective-permute-start.1) | collective-permute-done | bytes 557088 | tf_op jit(solution)/shard_map/ppermute | solution.py:303
  20.5 0.5 collective-permute-start.2
  21.0 1.2 %collective-permute-start.3 = (bf16[272,1024]{1,0:T(8,128)(2,1)}, bf16[272,1024]{1,0:T(8,128)(2,1)}, u32[]{:S(2)}, u32[]{:S(2)}) collective-permute-start(bf16[272,1024]{1,0:T(8,128)(2,1)} %collective-permute-done.1.refs_0_), channel_id=1, source_target_pairs={{0,4},{4,12},{12,8},{8,0},{1,5},{5,13},{13,9},{9,1},{2,6},{6,14},{... | collective-permute-start | bytes 1671176 | tf_op jit(solution)/shard_map/ppermute | solution.py:303
  22.2 1.6 %copy-done.1 = bf16[4,1024,256]{2,1,0:T(8,128)(2,1)S(1)} copy-done((bf16[4,1024,256]{2,1,0:T(8,128)(2,1)S(1)}, bf16[4,1024,256]{2,1,0:T(8,128)(2,1)}, u32[]{:S(2)}) %copy-start.1) | copy-done | bytes 2097176
  23.8 1.6 %copy-done.3 = bf16[4,256,1024]{2,1,0:T(8,128)(2,1)S(1)} copy-done((bf16[4,256,1024]{2,1,0:T(8,128)(2,1)S(1)}, bf16[4,256,1024]{2,1,0:T(8,128)(2,1)}, u32[]{:S(2)}) %copy-start.3) | copy-done | bytes 2097176
  25.4 1.1 %copy-done.25 = bf16[272,1024]{1,0:T(8,128)(2,1)S(1)} copy-done((bf16[272,1024]{1,0:T(8,128)(2,1)S(1)}, bf16[272,1024]{1,0:T(8,128)(2,1)}, u32[]{:S(2)}) %copy-start.25) | copy-done | bytes 557080
  26.4 1.1 %copy-done.27 = bf16[272,1024]{1,0:T(8,128)(2,1)S(1)} copy-done((bf16[272,1024]{1,0:T(8,128)(2,1)S(1)}, bf16[272,1024]{1,0:T(8,128)(2,1)}, u32[]{:S(2)}) %copy-start.27) | copy-done | bytes 557080
  27.5 3.7 %chunk.4 = (bf16[128,1024]{1,0:T(8,128)(2,1)S(1)}, bf16[128,1024]{1,0:T(8,128)(2,1)S(1)}, bf16[4,96,1024]{2,1,0:T(8,128)(2,1)S(1)}, bf16[4,96,1024]{2,1,0:T(8,128)(2,1)S(1)}, bf16[4,96,768]{2,1,0:T(8,128)(2,1)S(1)}) custom-call(s32[1]{0:T(128)} %bitcast.3.first_ref, bf16[272,1024]{1,0:T(8,128)(2,1)S(1)} %copy-done.25, bf16[272,1024]{1,0:T(8,128)(2,1)S(1)} %copy-done.27, ...), custom_call_target="tpu_custom_call" | custom-call | flops 1610612736 | bytes 8388608 | tf_op jit(solution)/shard_map/chunk/pallas_call | solution.py:171
  31.1 0.9 copy-done.4
  32.0 0.7 copy-done.28
  32.7 0.7 copy-done.30
  33.5 0.6 collective-permute-done.2.refs_1_
  34.0 1.4 %collective-permute-done.3.refs_0_ = bf16[272,1024]{1,0:T(8,128)(2,1)} collective-permute-done((bf16[272,1024]{1,0:T(8,128)(2,1)}, bf16[272,1024]{1,0:T(8,128)(2,1)}, u32[]{:S(2)}, u32[]{:S(2)}) %collective-permute-start.3) | collective-permute-done | bytes 557088 | tf_op jit(solution)/shard_map/ppermute | solution.py:303
  35.4 1.2 %collective-permute-start.4 = (bf16[272,1024]{1,0:T(8,128)(2,1)}, bf16[272,1024]{1,0:T(8,128)(2,1)S(1)}, u32[]{:S(2)}, u32[]{:S(2)}) collective-permute-start(bf16[272,1024]{1,0:T(8,128)(2,1)} %collective-permute-done.3.refs_0_), channel_id=1, source_target_pairs={{0,2},{2,0},{1,3},{3,1},{4,6},{6,4},{5,7},{7,5},{8,10},{10,8},{9,1... | collective-permute-start | bytes 1671176 | tf_op jit(solution)/shard_map/ppermute | solution.py:281
  36.7 1.3 %collective-permute-start.5 = (bf16[272,1024]{1,0:T(8,128)(2,1)}, bf16[272,1024]{1,0:T(8,128)(2,1)S(1)}, u32[]{:S(2)}, u32[]{:S(2)}) collective-permute-start(bf16[272,1024]{1,0:T(8,128)(2,1)} %collective-permute-done.3.refs_0_), channel_id=1, source_target_pairs={{0,4},{4,12},{12,8},{8,0},{1,5},{5,13},{13,9},{9,1},{2,6},{6,14},{... | collective-permute-start | bytes 1671176 | tf_op jit(solution)/shard_map/ppermute | solution.py:303
  38.0 4.9 %chunk.5 = (bf16[256,1024]{1,0:T(8,128)(2,1)S(1)}, bf16[4,96,1024]{2,1,0:T(8,128)(2,1)S(1)}, bf16[4,96,1024]{2,1,0:T(8,128)(2,1)S(1)}, bf16[4,96,768]{2,1,0:T(8,128)(2,1)S(1)}) custom-call(s32[1]{0:T(128)} %bitcast.3.first_ref, bf16[272,1024]{1,0:T(8,128)(2,1)} %collective-permute-done.1.refs_0_, bf16[272,1024]{1,0:T(8,128)(2,1)} %collective-permute-done.2.refs_1_, ...), custom_call_target="tpu_custom_call" | custom-call | flops 1610612736 | bytes 8388608 | tf_op jit(solution)/shard_map/chunk/pallas_call | solution.py:171
  42.9 0.9 copy-done.6
  43.8 0.9 copy-done.8
  44.7 3.3 %collective-permute-done.4.refs_1_ = bf16[272,1024]{1,0:T(8,128)(2,1)S(1)} collective-permute-done((bf16[272,1024]{1,0:T(8,128)(2,1)}, bf16[272,1024]{1,0:T(8,128)(2,1)S(1)}, u32[]{:S(2)}, u32[]{:S(2)}) %collective-permute-start.4) | collective-permute-done | bytes 557088 | tf_op jit(solution)/shard_map/ppermute | solution.py:281
  47.9 1.5 %collective-permute-done.5.refs_0_ = bf16[272,1024]{1,0:T(8,128)(2,1)S(1)} collective-permute-done((bf16[272,1024]{1,0:T(8,128)(2,1)}, bf16[272,1024]{1,0:T(8,128)(2,1)S(1)}, u32[]{:S(2)}, u32[]{:S(2)}) %collective-permute-start.5) | collective-permute-done | bytes 557088 | tf_op jit(solution)/shard_map/ppermute | solution.py:303
  49.5 1.1 %collective-permute-start.6 = (bf16[272,1024]{1,0:T(8,128)(2,1)S(1)}, bf16[272,1024]{1,0:T(8,128)(2,1)S(1)}, u32[]{:S(2)}, u32[]{:S(2)}) collective-permute-start(bf16[272,1024]{1,0:T(8,128)(2,1)S(1)} %collective-permute-done.5.refs_0_), channel_id=1, source_target_pairs={{0,2},{2,0},{1,3},{3,1},{4,6},{6,4},{5,7},{7,5},{8,10},{10,8},{9,1... | collective-permute-start | bytes 1671176 | tf_op jit(solution)/shard_map/ppermute | solution.py:281
  50.6 4.7 %chunk.6 = (bf16[128,1024]{1,0:T(8,128)(2,1)S(1)}, bf16[128,1024]{1,0:T(8,128)(2,1)S(1)}, bf16[4,96,1024]{2,1,0:T(8,128)(2,1)S(1)}, bf16[4,96,1024]{2,1,0:T(8,128)(2,1)S(1)}, bf16[4,96,768]{2,1,0:T(8,128)(2,1)S(1)}) custom-call(s32[1]{0:T(128)} %bitcast.3.first_ref, bf16[272,1024]{1,0:T(8,128)(2,1)} %collective-permute-done.3.refs_0_, ...), custom_call_target="tpu_custom_call" | custom-call | flops 1610612736 | bytes 8388608 | tf_op jit(solution)/shard_map/chunk/pallas_call | solution.py:171
  55.4 0.9 copy-done.10
  56.2 0.9 copy-done.12
  57.1 3.3 %collective-permute-done.6.refs_1_ = bf16[272,1024]{1,0:T(8,128)(2,1)S(1)} collective-permute-done((bf16[272,1024]{1,0:T(8,128)(2,1)S(1)}, bf16[272,1024]{1,0:T(8,128)(2,1)S(1)}, u32[]{:S(2)}, u32[]{:S(2)}) %collective-permute-start.6) | collective-permute-done | bytes 557088 | tf_op jit(solution)/shard_map/ppermute | solution.py:281
  60.4 1.7 %collective-permute-start.7 = (bf16[256,1024]{1,0:T(8,128)(2,1)S(1)}, bf16[256,1024]{1,0:T(8,128)(2,1)S(1)}, u32[]{:S(2)}, u32[]{:S(2)}) collective-permute-start(bf16[256,1024]{1,0:T(8,128)(2,1)S(1)} %get-tuple-element.161), channel_id=1, source_target_pairs={{0,8},{4,0},{12,4},{8,12},{1,9},{5,1},{13,5},{9,13},{2,10},{6,2},{... | collective-permute-start | bytes 1572872 | tf_op jit(solution)/shard_map/ppermute | solution.py:312
  62.1 0.7 collective-permute-start.8
  62.7 4.4 %chunk.7 = (bf16[128,1024]{1,0:T(8,128)(2,1)S(1)}, bf16[128,1024]{1,0:T(8,128)(2,1)}, bf16[4,96,1024]{2,1,0:T(8,128)(2,1)S(1)}, bf16[4,96,1024]{2,1,0:T(8,128)(2,1)S(1)}, bf16[4,96,768]{2,1,0:T(8,128)(2,1)S(1)}) custom-call(s32[1]{0:T(128)} %bitcast.3.first_ref, bf16[272,1024]{1,0:T(8,128)(2,1)S(1)} %collective-permute-done.5.refs_0_, ...), custom_call_target="tpu_custom_call" | custom-call | flops 1610612736 | bytes 8388608 | tf_op jit(solution)/shard_map/chunk/pallas_call | solution.py:171
  67.1 0.9 copy-done.14
  68.0 0.9 copy-done.16
  68.9 0.8 copy-done.22
  69.7 1.0 collective-permute-done.7
  70.8 1.9 %collective-permute-start.9 = (bf16[128,1024]{1,0:T(8,128)(2,1)}, bf16[128,1024]{1,0:T(8,128)(2,1)S(1)}, u32[]{:S(2)}, u32[]{:S(2)}) collective-permute-start(bf16[128,1024]{1,0:T(8,128)(2,1)} %get-tuple-element.194), channel_id=1, source_target_pairs={{0,2},{2,0},{1,3},{3,1},{4,6},{6,4},{5,7},{7,5},{8,10},{10,8},{9,1... | collective-permute-start | bytes 786440 | tf_op jit(solution)/shard_map/ppermute | solution.py:288
  72.7 0.1 add_convert_fusion.3
  72.8 4.1 %collective-permute-start.10 = (bf16[128,1024]{1,0:T(8,128)(2,1)S(1)}, bf16[128,1024]{1,0:T(8,128)(2,1)S(1)}, u32[]{:S(2)}, u32[]{:S(2)}) collective-permute-start(bf16[128,1024]{1,0:T(8,128)(2,1)S(1)} %add_convert_fusion.3), channel_id=1, source_target_pairs={{0,4},{4,12},{12,8},{8,0},{1,5},{5,13},{13,9},{9,1},{2,6},{6,14},{... | collective-permute-start | bytes 786440 | tf_op jit(solution)/shard_map/ppermute | solution.py:298
  76.8 1.1 %copy-done.5 = bf16[4,96,1024]{2,1,0:T(8,128)(2,1)S(1)} copy-done((bf16[4,96,1024]{2,1,0:T(8,128)(2,1)S(1)}, bf16[4,96,1024]{2,1,0:T(8,128)(2,1)}, u32[]{:S(2)}) %copy-start.5) | copy-done | bytes 786456
  78.0 1.1 %copy-done.7 = bf16[4,96,1024]{2,1,0:T(8,128)(2,1)S(1)} copy-done((bf16[4,96,1024]{2,1,0:T(8,128)(2,1)S(1)}, bf16[4,96,1024]{2,1,0:T(8,128)(2,1)}, u32[]{:S(2)}) %copy-start.7) | copy-done | bytes 786456
  79.1 1.1 %copy-done.9 = bf16[4,96,1024]{2,1,0:T(8,128)(2,1)S(1)} copy-done((bf16[4,96,1024]{2,1,0:T(8,128)(2,1)S(1)}, bf16[4,96,1024]{2,1,0:T(8,128)(2,1)}, u32[]{:S(2)}) %copy-start.9) | copy-done | bytes 786456
  80.2 1.1 %copy-done.11 = bf16[4,96,1024]{2,1,0:T(8,128)(2,1)S(1)} copy-done((bf16[4,96,1024]{2,1,0:T(8,128)(2,1)S(1)}, bf16[4,96,1024]{2,1,0:T(8,128)(2,1)}, u32[]{:S(2)}) %copy-start.11) | copy-done | bytes 786456
  81.4 1.1 %copy-done.13 = bf16[4,96,1024]{2,1,0:T(8,128)(2,1)S(1)} copy-done((bf16[4,96,1024]{2,1,0:T(8,128)(2,1)S(1)}, bf16[4,96,1024]{2,1,0:T(8,128)(2,1)}, u32[]{:S(2)}) %copy-start.13) | copy-done | bytes 786456
  82.5 1.1 %copy-done.15 = bf16[4,96,1024]{2,1,0:T(8,128)(2,1)S(1)} copy-done((bf16[4,96,1024]{2,1,0:T(8,128)(2,1)S(1)}, bf16[4,96,1024]{2,1,0:T(8,128)(2,1)}, u32[]{:S(2)}) %copy-start.15) | copy-done | bytes 786456
  83.6 1.1 %copy-done.17 = bf16[4,96,1024]{2,1,0:T(8,128)(2,1)S(1)} copy-done((bf16[4,96,1024]{2,1,0:T(8,128)(2,1)S(1)}, bf16[4,96,1024]{2,1,0:T(8,128)(2,1)}, u32[]{:S(2)}) %copy-start.17) | copy-done | bytes 786456
  84.8 1.1 %copy-done.19 = bf16[4,96,768]{2,1,0:T(8,128)(2,1)S(1)} copy-done((bf16[4,96,768]{2,1,0:T(8,128)(2,1)S(1)}, bf16[4,96,768]{2,1,0:T(8,128)(2,1)}, u32[]{:S(2)}) %copy-start.19) | copy-done | bytes 589848
  85.8 1.1 %copy-done.21 = bf16[4,96,768]{2,1,0:T(8,128)(2,1)S(1)} copy-done((bf16[4,96,768]{2,1,0:T(8,128)(2,1)S(1)}, bf16[4,96,768]{2,1,0:T(8,128)(2,1)}, u32[]{:S(2)}) %copy-start.21) | copy-done | bytes 589848
  86.9 1.1 %copy-done.23 = bf16[4,96,768]{2,1,0:T(8,128)(2,1)S(1)} copy-done((bf16[4,96,768]{2,1,0:T(8,128)(2,1)S(1)}, bf16[4,96,768]{2,1,0:T(8,128)(2,1)}, u32[]{:S(2)}) %copy-start.23) | copy-done | bytes 589848
  88.0 1.9 %weight_grads.2 = bf16[4,768,512]{2,1,0:T(8,128)(2,1)S(1)} custom-call(s32[1]{0:T(128)S(6)} %sub.3.side_ref, bf16[4,96,1024]{2,1,0:T(8,128)(2,1)S(1)} %get-tuple-element.182.refs_0_, bf16[4,96,1024]{2,1,0:T(8,128)(2,1)S(1)} %copy-done.7, bf16[4,96,1024]{2,1,0:T(8,128)(2,1)S(1)} %copy-done.11, bf16[4,96,1024]{2,1,0:T(8,128)(2,1)S(1)} %copy-done.15, ...), custom_call_target="tpu_custom_call" | custom-call | flops 1207959552 | bytes 8650752 | tf_op jit(solution)/shard_map/weight_grads/pallas_call | solution.py:244
  89.8 0.1 collective-permute-start.11
  89.9 0.1 add_convert_fusion.1
  90.0 1.5 %collective-permute-start.13 = (bf16[128,1024]{1,0:T(8,128)(2,1)S(1)}, bf16[128,1024]{1,0:T(8,128)(2,1)S(1)}, u32[]{:S(2)}, u32[]{:S(2)}) collective-permute-start(bf16[128,1024]{1,0:T(8,128)(2,1)S(1)} %add_convert_fusion.1), channel_id=1, source_target_pairs={{0,2},{2,0},{1,3},{3,1},{4,6},{6,4},{5,7},{7,5},{8,10},{10,8},{9,1... | collective-permute-start | bytes 786440 | tf_op jit(solution)/shard_map/ppermute | solution.py:288
  91.5 0.1 add_convert_fusion.2
  91.6 1.6 %collective-permute-start.12 = (bf16[128,1024]{1,0:T(8,128)(2,1)S(1)}, bf16[128,1024]{1,0:T(8,128)(2,1)S(1)}, u32[]{:S(2)}, u32[]{:S(2)}) collective-permute-start(bf16[128,1024]{1,0:T(8,128)(2,1)S(1)} %add_convert_fusion.2), channel_id=1, source_target_pairs={{0,4},{4,12},{12,8},{8,0},{1,5},{5,13},{13,9},{9,1},{2,6},{6,14},{... | collective-permute-start | bytes 786440 | tf_op jit(solution)/shard_map/ppermute | solution.py:298
  93.2 2.4 %collective-permute-done.11.refs_12_ = bf16[4,768,512]{2,1,0:T(8,128)(2,1)S(1)} collective-permute-done((bf16[4,768,512]{2,1,0:T(8,128)(2,1)S(1)}, bf16[4,768,512]{2,1,0:T(8,128)(2,1)S(1)}, u32[]{:S(2)}, u32[]{:S(2)}) %collective-permute-start.11) | collective-permute-done | bytes 3145760 | tf_op jit(solution)/shard_map/ppermute | solution.py:323
  95.6 2.7 %weight_grads.3 = (bf16[4,512,256]{2,1,0:T(8,128)(2,1)}, bf16[4,512,256]{2,1,0:T(8,128)(2,1)}, bf16[4,256,512]{2,1,0:T(8,128)(2,1)}) custom-call(s32[1]{0:T(128)} %bitcast.4.side_ref, bf16[4,96,1024]{2,1,0:T(8,128)(2,1)S(1)} %get-tuple-element.182.refs_0_, bf16[4,96,1024]{2,1,0:T(8,128)(2,1)S(1)} %copy-done.7, bf16[4,96,1024]{2,1,0:T(8,128)(2,1)S(1)} %copy-done.11, ...), custom_call_target="tpu_custom_call" | custom-call | flops 1207959552 | bytes 8650752 | tf_op jit(solution)/shard_map/weight_grads/pallas_call | solution.py:244
  98.3 0.5 collective-permute-done.13
  98.8 2.2 %collective-permute-done.12 = bf16[128,1024]{1,0:T(8,128)(2,1)S(1)} collective-permute-done((bf16[128,1024]{1,0:T(8,128)(2,1)S(1)}, bf16[128,1024]{1,0:T(8,128)(2,1)S(1)}, u32[]{:S(2)}, u32[]{:S(2)}) %collective-permute-start.12) | collective-permute-done | bytes 262176 | tf_op jit(solution)/shard_map/ppermute | solution.py:298
  101.0 0.9 add_convert_fusion
  (48 shorter events, 0.1 us)
Async XLA Ops:
  2.4 7.5 %copy-start.24 = (bf16[272,1024]{1,0:T(8,128)(2,1)}, bf16[272,1024]{1,0:T(8,128)(2,1)S(1)}, u32[]{:S(2)}) copy-start(bf16[272,1024]{1,0:T(8,128)(2,1)S(1)} %pack.1.refs_0_) | copy-start | bytes 1671172
  2.4 15.6 %collective-permute-start = (bf16[272,1024]{1,0:T(8,128)(2,1)S(1)}, bf16[272,1024]{1,0:T(8,128)(2,1)S(1)}, u32[]{:S(2)}, u32[]{:S(2)}) collective-permute-start(bf16[272,1024]{1,0:T(8,128)(2,1)S(1)} %pack.1.refs_0_), channel_id=1, source_target_pairs={{0,2},{2,0},{1,3},{3,1},{4,6},{6,4},{5,7},{7,5},{8,10},{10,8},{9,1... | collective-permute-start | bytes 1671176 | tf_op jit(solution)/shard_map/ppermute | solution.py:281
  5.4 15.1 %collective-permute-start.1 = (bf16[272,1024]{1,0:T(8,128)(2,1)S(1)}, bf16[272,1024]{1,0:T(8,128)(2,1)}, u32[]{:S(2)}, u32[]{:S(2)}) collective-permute-start(bf16[272,1024]{1,0:T(8,128)(2,1)S(1)} %pack.1.refs_0_), channel_id=1, source_target_pairs={{0,4},{4,12},{12,8},{8,0},{1,5},{5,13},{13,9},{9,1},{2,6},{6,14},{... | collective-permute-start | bytes 1671176 | tf_op jit(solution)/shard_map/ppermute | solution.py:303
  9.9 1.3 %copy-start = (bf16[4,1024,256]{2,1,0:T(8,128)(2,1)}, bf16[4,1024,256]{2,1,0:T(8,128)(2,1)S(1)}, u32[]{:S(2)}) copy-start(bf16[4,1024,256]{2,1,0:T(8,128)(2,1)S(1)} %get-tuple-element.173.refs_3_) | copy-start | bytes 6291460
  11.2 1.4 %copy-start.2 = (bf16[4,256,1024]{2,1,0:T(8,128)(2,1)}, bf16[4,256,1024]{2,1,0:T(8,128)(2,1)S(1)}, u32[]{:S(2)}) copy-start(bf16[4,256,1024]{2,1,0:T(8,128)(2,1)S(1)} %get-tuple-element.174.refs_4_) | copy-start | bytes 6291460
  18.0 0.8 copy-start.26
  20.5 13.5 %collective-permute-start.2 = (bf16[272,1024]{1,0:T(8,128)(2,1)}, bf16[272,1024]{1,0:T(8,128)(2,1)}, u32[]{:S(2)}, u32[]{:S(2)}) collective-permute-start(bf16[272,1024]{1,0:T(8,128)(2,1)} %collective-permute-done.1.refs_0_), channel_id=1, source_target_pairs={{0,2},{2,0},{1,3},{3,1},{4,6},{6,4},{5,7},{7,5},{8,10},{10,8},{9,1... | collective-permute-start | bytes 1671176 | tf_op jit(solution)/shard_map/ppermute | solution.py:281
  21.0 14.4 %collective-permute-start.3 = (bf16[272,1024]{1,0:T(8,128)(2,1)}, bf16[272,1024]{1,0:T(8,128)(2,1)}, u32[]{:S(2)}, u32[]{:S(2)}) collective-permute-start(bf16[272,1024]{1,0:T(8,128)(2,1)} %collective-permute-done.1.refs_0_), channel_id=1, source_target_pairs={{0,4},{4,12},{12,8},{8,0},{1,5},{5,13},{13,9},{9,1},{2,6},{6,14},{... | collective-permute-start | bytes 1671176 | tf_op jit(solution)/shard_map/ppermute | solution.py:303
  22.2 1.6 %copy-start.1 = (bf16[4,1024,256]{2,1,0:T(8,128)(2,1)S(1)}, bf16[4,1024,256]{2,1,0:T(8,128)(2,1)}, u32[]{:S(2)}) copy-start(bf16[4,1024,256]{2,1,0:T(8,128)(2,1)} %copy-done) | copy-start | bytes 6291460
  23.8 1.6 %copy-start.3 = (bf16[4,256,1024]{2,1,0:T(8,128)(2,1)S(1)}, bf16[4,256,1024]{2,1,0:T(8,128)(2,1)}, u32[]{:S(2)}) copy-start(bf16[4,256,1024]{2,1,0:T(8,128)(2,1)} %copy-done.2) | copy-start | bytes 6291460
  25.4 1.1 %copy-start.25 = (bf16[272,1024]{1,0:T(8,128)(2,1)S(1)}, bf16[272,1024]{1,0:T(8,128)(2,1)}, u32[]{:S(2)}) copy-start(bf16[272,1024]{1,0:T(8,128)(2,1)} %copy-done.24) | copy-start | bytes 1671172
  26.4 1.1 %copy-start.27 = (bf16[272,1024]{1,0:T(8,128)(2,1)S(1)}, bf16[272,1024]{1,0:T(8,128)(2,1)}, u32[]{:S(2)}) copy-start(bf16[272,1024]{1,0:T(8,128)(2,1)} %copy-done.26) | copy-start | bytes 1671172
  31.1 0.9 copy-start.4
  32.0 0.7 copy-start.28
  32.7 0.7 copy-start.30
  35.4 12.5 %collective-permute-start.4 = (bf16[272,1024]{1,0:T(8,128)(2,1)}, bf16[272,1024]{1,0:T(8,128)(2,1)S(1)}, u32[]{:S(2)}, u32[]{:S(2)}) collective-permute-start(bf16[272,1024]{1,0:T(8,128)(2,1)} %collective-permute-done.3.refs_0_), channel_id=1, source_target_pairs={{0,2},{2,0},{1,3},{3,1},{4,6},{6,4},{5,7},{7,5},{8,10},{10,8},{9,1... | collective-permute-start | bytes 1671176 | tf_op jit(solution)/shard_map/ppermute | solution.py:281
  36.7 12.8 %collective-permute-start.5 = (bf16[272,1024]{1,0:T(8,128)(2,1)}, bf16[272,1024]{1,0:T(8,128)(2,1)S(1)}, u32[]{:S(2)}, u32[]{:S(2)}) collective-permute-start(bf16[272,1024]{1,0:T(8,128)(2,1)} %collective-permute-done.3.refs_0_), channel_id=1, source_target_pairs={{0,4},{4,12},{12,8},{8,0},{1,5},{5,13},{13,9},{9,1},{2,6},{6,14},{... | collective-permute-start | bytes 1671176 | tf_op jit(solution)/shard_map/ppermute | solution.py:303
  42.9 0.9 copy-start.6
  43.8 0.9 copy-start.8
  44.7 10.7 %copy-start.18 = (bf16[4,96,768]{2,1,0:T(8,128)(2,1)}, bf16[4,96,768]{2,1,0:T(8,128)(2,1)S(1)}, u32[]{:S(2)}) copy-start(bf16[4,96,768]{2,1,0:T(8,128)(2,1)S(1)} %get-tuple-element.191.refs_9_) | copy-start | bytes 1769476
  49.5 11.0 %collective-permute-start.6 = (bf16[272,1024]{1,0:T(8,128)(2,1)S(1)}, bf16[272,1024]{1,0:T(8,128)(2,1)S(1)}, u32[]{:S(2)}, u32[]{:S(2)}) collective-permute-start(bf16[272,1024]{1,0:T(8,128)(2,1)S(1)} %collective-permute-done.5.refs_0_), channel_id=1, source_target_pairs={{0,2},{2,0},{1,3},{3,1},{4,6},{6,4},{5,7},{7,5},{8,10},{10,8},{9,1... | collective-permute-start | bytes 1671176 | tf_op jit(solution)/shard_map/ppermute | solution.py:281
  55.3 0.9 copy-start.10
  56.2 0.9 copy-start.12
  57.1 10.0 %copy-start.20 = (bf16[4,96,768]{2,1,0:T(8,128)(2,1)}, bf16[4,96,768]{2,1,0:T(8,128)(2,1)S(1)}, u32[]{:S(2)}) copy-start(bf16[4,96,768]{2,1,0:T(8,128)(2,1)S(1)} %get-tuple-element.192.refs_10_) | copy-start | bytes 1769476
  60.4 10.3 %collective-permute-start.7 = (bf16[256,1024]{1,0:T(8,128)(2,1)S(1)}, bf16[256,1024]{1,0:T(8,128)(2,1)S(1)}, u32[]{:S(2)}, u32[]{:S(2)}) collective-permute-start(bf16[256,1024]{1,0:T(8,128)(2,1)S(1)} %get-tuple-element.161), channel_id=1, source_target_pairs={{0,8},{4,0},{12,4},{8,12},{1,9},{5,1},{13,5},{9,13},{2,10},{6,2},{... | collective-permute-start | bytes 1572872 | tf_op jit(solution)/shard_map/ppermute | solution.py:312
  62.1 7.7 %collective-permute-start.8 = (bf16[128,1024]{1,0:T(8,128)(2,1)S(1)}, bf16[128,1024]{1,0:T(8,128)(2,1)S(1)}, u32[]{:S(2)}, u32[]{:S(2)}) collective-permute-start(bf16[128,1024]{1,0:T(8,128)(2,1)S(1)} %get-tuple-element.166), channel_id=1, source_target_pairs={{0,2},{2,0},{1,3},{3,1},{4,6},{6,4},{5,7},{7,5},{8,10},{10,8},{9,1... | collective-permute-start | bytes 786440 | tf_op jit(solution)/shard_map/ppermute | solution.py:288
  67.1 0.9 copy-start.14
  68.0 0.9 copy-start.16
  68.9 0.8 copy-start.22
  69.7 3.0 %copy-start.32 = (bf16[128,1024]{1,0:T(8,128)(2,1)}, bf16[128,1024]{1,0:T(8,128)(2,1)S(1)}, u32[]{:S(2)}) copy-start(bf16[128,1024]{1,0:T(8,128)(2,1)S(1)} %get-tuple-element.201) | copy-start | bytes 786436
  70.7 2.0 %copy-start.34 = (bf16[256,1024]{1,0:T(8,128)(2,1)}, bf16[256,1024]{1,0:T(8,128)(2,1)S(1)}, u32[]{:S(2)}) copy-start(bf16[256,1024]{1,0:T(8,128)(2,1)S(1)} %collective-permute-done.7) | copy-start | bytes 1572868
  70.8 19.1 %collective-permute-start.9 = (bf16[128,1024]{1,0:T(8,128)(2,1)}, bf16[128,1024]{1,0:T(8,128)(2,1)S(1)}, u32[]{:S(2)}, u32[]{:S(2)}) collective-permute-start(bf16[128,1024]{1,0:T(8,128)(2,1)} %get-tuple-element.194), channel_id=1, source_target_pairs={{0,2},{2,0},{1,3},{3,1},{4,6},{6,4},{5,7},{7,5},{8,10},{10,8},{9,1... | collective-permute-start | bytes 786440 | tf_op jit(solution)/shard_map/ppermute | solution.py:288
  72.8 17.1 %collective-permute-start.10 = (bf16[128,1024]{1,0:T(8,128)(2,1)S(1)}, bf16[128,1024]{1,0:T(8,128)(2,1)S(1)}, u32[]{:S(2)}, u32[]{:S(2)}) collective-permute-start(bf16[128,1024]{1,0:T(8,128)(2,1)S(1)} %add_convert_fusion.3), channel_id=1, source_target_pairs={{0,4},{4,12},{12,8},{8,0},{1,5},{5,13},{13,9},{9,1},{2,6},{6,14},{... | collective-permute-start | bytes 786440 | tf_op jit(solution)/shard_map/ppermute | solution.py:298
  76.8 1.1 %copy-start.5 = (bf16[4,96,1024]{2,1,0:T(8,128)(2,1)S(1)}, bf16[4,96,1024]{2,1,0:T(8,128)(2,1)}, u32[]{:S(2)}) copy-start(bf16[4,96,1024]{2,1,0:T(8,128)(2,1)} %copy-done.4) | copy-start | bytes 2359300
  78.0 1.1 %copy-start.7 = (bf16[4,96,1024]{2,1,0:T(8,128)(2,1)S(1)}, bf16[4,96,1024]{2,1,0:T(8,128)(2,1)}, u32[]{:S(2)}) copy-start(bf16[4,96,1024]{2,1,0:T(8,128)(2,1)} %copy-done.6) | copy-start | bytes 2359300
  79.1 1.1 %copy-start.9 = (bf16[4,96,1024]{2,1,0:T(8,128)(2,1)S(1)}, bf16[4,96,1024]{2,1,0:T(8,128)(2,1)}, u32[]{:S(2)}) copy-start(bf16[4,96,1024]{2,1,0:T(8,128)(2,1)} %copy-done.8) | copy-start | bytes 2359300
  80.2 1.1 %copy-start.11 = (bf16[4,96,1024]{2,1,0:T(8,128)(2,1)S(1)}, bf16[4,96,1024]{2,1,0:T(8,128)(2,1)}, u32[]{:S(2)}) copy-start(bf16[4,96,1024]{2,1,0:T(8,128)(2,1)} %copy-done.10) | copy-start | bytes 2359300
  81.4 1.1 %copy-start.13 = (bf16[4,96,1024]{2,1,0:T(8,128)(2,1)S(1)}, bf16[4,96,1024]{2,1,0:T(8,128)(2,1)}, u32[]{:S(2)}) copy-start(bf16[4,96,1024]{2,1,0:T(8,128)(2,1)} %copy-done.12) | copy-start | bytes 2359300
  82.5 1.1 %copy-start.15 = (bf16[4,96,1024]{2,1,0:T(8,128)(2,1)S(1)}, bf16[4,96,1024]{2,1,0:T(8,128)(2,1)}, u32[]{:S(2)}) copy-start(bf16[4,96,1024]{2,1,0:T(8,128)(2,1)} %copy-done.14) | copy-start | bytes 2359300
  83.6 1.1 %copy-start.17 = (bf16[4,96,1024]{2,1,0:T(8,128)(2,1)S(1)}, bf16[4,96,1024]{2,1,0:T(8,128)(2,1)}, u32[]{:S(2)}) copy-start(bf16[4,96,1024]{2,1,0:T(8,128)(2,1)} %copy-done.16) | copy-start | bytes 2359300
  84.8 1.1 %copy-start.19 = (bf16[4,96,768]{2,1,0:T(8,128)(2,1)S(1)}, bf16[4,96,768]{2,1,0:T(8,128)(2,1)}, u32[]{:S(2)}) copy-start(bf16[4,96,768]{2,1,0:T(8,128)(2,1)} %copy-done.18) | copy-start | bytes 1769476
  85.8 1.1 %copy-start.21 = (bf16[4,96,768]{2,1,0:T(8,128)(2,1)S(1)}, bf16[4,96,768]{2,1,0:T(8,128)(2,1)}, u32[]{:S(2)}) copy-start(bf16[4,96,768]{2,1,0:T(8,128)(2,1)} %copy-done.20) | copy-start | bytes 1769476
  86.9 1.1 %copy-start.23 = (bf16[4,96,768]{2,1,0:T(8,128)(2,1)S(1)}, bf16[4,96,768]{2,1,0:T(8,128)(2,1)}, u32[]{:S(2)}) copy-start(bf16[4,96,768]{2,1,0:T(8,128)(2,1)} %copy-done.22) | copy-start | bytes 1769476
  87.9 2.0 %copy-start.31 = (bf16[128,1024]{1,0:T(8,128)(2,1)S(1)}, bf16[128,1024]{1,0:T(8,128)(2,1)}, u32[]{:S(2)}) copy-start(bf16[128,1024]{1,0:T(8,128)(2,1)} %copy-done.30) | copy-start | bytes 786436
  87.9 2.0 %copy-start.35 = (bf16[256,1024]{1,0:T(8,128)(2,1)S(1)}, bf16[256,1024]{1,0:T(8,128)(2,1)}, u32[]{:S(2)}) copy-start(bf16[256,1024]{1,0:T(8,128)(2,1)} %copy-done.34) | copy-start | bytes 1572868
  88.0 3.5 %copy-start.33 = (bf16[128,1024]{1,0:T(8,128)(2,1)S(1)}, bf16[128,1024]{1,0:T(8,128)(2,1)}, u32[]{:S(2)}) copy-start(bf16[128,1024]{1,0:T(8,128)(2,1)} %copy-done.32) | copy-start | bytes 786436
  89.8 5.7 %collective-permute-start.11 = (bf16[4,768,512]{2,1,0:T(8,128)(2,1)S(1)}, bf16[4,768,512]{2,1,0:T(8,128)(2,1)S(1)}, u32[]{:S(2)}, u32[]{:S(2)}) collective-permute-start(bf16[4,768,512]{2,1,0:T(8,128)(2,1)S(1)} %weight_grads.2), channel_id=1, source_target_pairs={{0,1},{1,0},{2,3},{3,2},{4,5},{5,4},{6,7},{7,6},{8,9},{9,8},{10,11... | collective-permute-start | bytes 9437192 | tf_op jit(solution)/shard_map/ppermute | solution.py:323
  90.0 8.8 %collective-permute-start.13 = (bf16[128,1024]{1,0:T(8,128)(2,1)S(1)}, bf16[128,1024]{1,0:T(8,128)(2,1)S(1)}, u32[]{:S(2)}, u32[]{:S(2)}) collective-permute-start(bf16[128,1024]{1,0:T(8,128)(2,1)S(1)} %add_convert_fusion.1), channel_id=1, source_target_pairs={{0,2},{2,0},{1,3},{3,1},{4,6},{6,4},{5,7},{7,5},{8,10},{10,8},{9,1... | collective-permute-start | bytes 786440 | tf_op jit(solution)/shard_map/ppermute | solution.py:288
  91.6 9.4 %copy-start.29 = (bf16[128,1024]{1,0:T(8,128)(2,1)S(1)}, bf16[128,1024]{1,0:T(8,128)(2,1)}, u32[]{:S(2)}) copy-start(bf16[128,1024]{1,0:T(8,128)(2,1)} %copy-done.28) | copy-start | bytes 786436
  91.6 9.4 %collective-permute-start.12 = (bf16[128,1024]{1,0:T(8,128)(2,1)S(1)}, bf16[128,1024]{1,0:T(8,128)(2,1)S(1)}, u32[]{:S(2)}, u32[]{:S(2)}) collective-permute-start(bf16[128,1024]{1,0:T(8,128)(2,1)S(1)} %add_convert_fusion.2), channel_id=1, source_target_pairs={{0,4},{4,12},{12,8},{8,0},{1,5},{5,13},{13,9},{9,1},{2,6},{6,14},{... | collective-permute-start | bytes 786440 | tf_op jit(solution)/shard_map/ppermute | solution.py:298

commit v9 on v8

--- a/solution.py
+++ b/solution.py
@@ -297,6 +297,7 @@
     def homeward(group_part, k):
         return lax.ppermute(group_part, "group", along(-k))
 
+    tokens, first_expert, half, other_half = tie(tokens, first_expert, half, 1 - half)
     column = pack_call(tokens, upstream, expert_ids, slots, gate_fixed)
     blocks, chunks, backs, sent = {}, {}, {}, {}
     for k in range(n_group):
@@ -317,7 +318,7 @@
     backs[last] = across(chunks[last][1])
     carried = homeward(group_sum(chunks[last - 1][0], backs[last - 1]), last)
     kept = [[chunks[k][i] for k in range(n_group)] for i in (-3, -2, -1)]
-    to_send = weight_call(1 - half, *kept)
+    to_send = weight_call(other_half, *kept)
     to_send, backs[last], carried = tie(to_send, backs[last], carried)
 
     got = lax.ppermute(to_send, "dp", [(0, 1), (1, 0)])

time: 103 us -> 92.5 us (0.90)
  local copies, waits for them, and re-layouts: 28.4 us -> 0 us
  waiting for transfers between devices: 23.3 us -> 45.8 us
  Pallas kernels: 26.9 us -> 23.9 us
    unnamed x72 -> x0, local copies, waits for them, and re-layouts: 28.4 us -> none
    ppermute x4, waiting for transfers between devices: 12.6 us -> 29.1 us  [spread(): lax.ppermute(column, 'ingroup', shift(s))]
    ppermute x3, waiting for transfers between devices: 0.5 us -> 4.72 us  [across(): lax.ppermute(others[(s - 1) * tok_rows:s * tok_rows], 'ingroup', shift(-s))]
    pallas_call x4, Pallas kernels: 17.7 us -> 14.7 us  [chunk_call(): pl.pallas_call(functools.partial(chunk_kernel, n_blocks, tok_rows, capaci...]
    ppermute x2, waiting for transfers between devices: 2.2 us -> 4.57 us  [homeward(): return lax.ppermute(group_part, 'group', along(-k))]
  transfers between devices with their start and end apart: 14 -> 14, of which waited for: 11 -> 13; matrix products, arithmetic and copies ran while one was open for 0% -> 0% of each run, Pallas kernels for 25% -> 24%
where the time goes in v9:
time: 92.5 us; the launch traced here: 92.3 us
  waiting for transfers between devices  45.8 us (50%)
  Pallas kernels  23.9 us (26%)
  starting transfers between devices  20.8 us (22%)
  other arithmetic  1.13 us (1%)
    ppermute x4, waiting for transfers between devices, spread(): lax.ppermute(column, 'ingroup', shift(s))  29.1 us
    pallas_call x4, Pallas kernels, chunk_call(): pl.pallas_call(functools.partial(chunk_kernel, n_blocks, tok_rows, capaci...  14.7 us
    ppermute x2, starting transfers between devices, homeward(): return lax.ppermute(group_part, 'group', along(-k))  6.34 us
    ppermute x4, starting transfers between devices, spread(): lax.ppermute(column, 'ingroup', shift(s))  5.83 us
    ppermute x3, waiting for transfers between devices, per_device(): ahead = lax.ppermute(column, 'group', along(1)) if k < n_group - 1 else None  5.3 us
    ppermute x3, waiting for transfers between devices, across(): lax.ppermute(others[(s - 1) * tok_rows:s * tok_rows], 'ingroup', shift(-s))  4.72 us
    ppermute x2, waiting for transfers between devices, homeward(): return lax.ppermute(group_part, 'group', along(-k))  4.57 us
    pallas_call x2, Pallas kernels, weight_call(): pl.pallas_call(functools.partial(kernel, n), in_specs=[smem] + [vmem] * l...  4.57 us
  transfers between devices with their start and end apart: 14, of which 13 were waited for; matrix products, arithmetic and copies ran while one was open for 0% of the time, Pallas kernels for 24%

profile of v9, /device:TPU:0, one launch (start us, length us, event | category | flops | bytes accessed | tf_op | source)
XLA Modules:
  0.0 92.3 jit_solution(2383179769944051137)
XLA Ops:
  0.6 1.8 %pack.1.refs_0_ = bf16[272,1024]{1,0:T(8,128)(2,1)S(1)} custom-call(bf16[128,1024]{1,0:T(8,128)(2,1)} %tokens, bf16[128,1024]{1,0:T(8,128)(2,1)} %upstream.1, s32[8,128]{1,0:T(8,128)} %bitcast.5, s32[8,128]{1,0:T(8,128)} %bitcast.6, s32[8,128]{1,0:T(8,128)} %bitcast.7), custom_call_target="tpu_custom_call" | custom-call | tf_op jit(solution)/shard_map/pack/pallas_call | solution.py:58
  2.4 3.0 %collective-permute-start = (bf16[272,1024]{1,0:T(8,128)(2,1)S(1)}, bf16[272,1024]{1,0:T(8,128)(2,1)S(1)}, u32[]{:S(2)}, u32[]{:S(2)}) collective-permute-start(bf16[272,1024]{1,0:T(8,128)(2,1)S(1)} %pack.1.refs_0_), channel_id=1, source_target_pairs={{0,2},{2,0},{1,3},{3,1},{4,6},{6,4},{5,7},{7,5},{8,10},{10,8},{9,1... | collective-permute-start | bytes 1671176 | tf_op jit(solution)/shard_map/ppermute | solution.py:281
  5.4 1.6 %collective-permute-start.1 = (bf16[272,1024]{1,0:T(8,128)(2,1)S(1)}, bf16[272,1024]{1,0:T(8,128)(2,1)S(1)}, u32[]{:S(2)}, u32[]{:S(2)}) collective-permute-start(bf16[272,1024]{1,0:T(8,128)(2,1)S(1)} %pack.1.refs_0_), channel_id=1, source_target_pairs={{0,4},{4,12},{12,8},{8,0},{1,5},{5,13},{13,9},{9,1},{2,6},{6,14},{... | collective-permute-start | bytes 1671176 | tf_op jit(solution)/shard_map/ppermute | solution.py:304
  7.0 2.9 %load.1 = (bf16[4,1024,256]{2,1,0:T(8,128)(2,1)S(1)}, bf16[4,1024,256]{2,1,0:T(8,128)(2,1)S(1)}, bf16[4,256,1024]{2,1,0:T(8,128)(2,1)S(1)}) custom-call(bf16[4,1024,256]{2,1,0:T(8,128)(2,1)} %refs_0_.1, bf16[4,1024,256]{2,1,0:T(8,128)(2,1)} %refs_1_.1, bf16[4,256,1024]{2,1,0:T(8,128)(2,1)} %refs_2_.1), custom_call_target="tpu_custom_call" | custom-call | tf_op jit(solution)/shard_map/load/pallas_call | solution.py:98
  9.9 8.2 %collective-permute-done.refs_1_ = bf16[272,1024]{1,0:T(8,128)(2,1)S(1)} collective-permute-done((bf16[272,1024]{1,0:T(8,128)(2,1)S(1)}, bf16[272,1024]{1,0:T(8,128)(2,1)S(1)}, u32[]{:S(2)}, u32[]{:S(2)}) %collective-permute-start) | collective-permute-done | bytes 557088 | tf_op jit(solution)/shard_map/ppermute | solution.py:281
  18.0 2.4 %collective-permute-done.1.refs_0_ = bf16[272,1024]{1,0:T(8,128)(2,1)S(1)} collective-permute-done((bf16[272,1024]{1,0:T(8,128)(2,1)S(1)}, bf16[272,1024]{1,0:T(8,128)(2,1)S(1)}, u32[]{:S(2)}, u32[]{:S(2)}) %collective-permute-start.1) | collective-permute-done | bytes 557088 | tf_op jit(solution)/shard_map/ppermute | solution.py:304
  20.4 0.5 collective-permute-start.2
  20.9 0.8 collective-permute-start.3
  21.7 3.7 %chunk.4 = (bf16[128,1024]{1,0:T(8,128)(2,1)S(1)}, bf16[128,1024]{1,0:T(8,128)(2,1)S(1)}, bf16[4,96,1024]{2,1,0:T(8,128)(2,1)S(1)}, bf16[4,96,1024]{2,1,0:T(8,128)(2,1)S(1)}, bf16[4,96,768]{2,1,0:T(8,128)(2,1)S(1)}) custom-call(s32[1]{0:T(128)} %bitcast.first_ref, bf16[272,1024]{1,0:T(8,128)(2,1)S(1)} %pack.1.refs_0_, ...), custom_call_target="tpu_custom_call" | custom-call | flops 1610612736 | bytes 8388608 | tf_op jit(solution)/shard_map/chunk/pallas_call | solution.py:171
  25.4 8.2 %collective-permute-done.2.refs_1_ = bf16[272,1024]{1,0:T(8,128)(2,1)S(1)} collective-permute-done((bf16[272,1024]{1,0:T(8,128)(2,1)S(1)}, bf16[272,1024]{1,0:T(8,128)(2,1)S(1)}, u32[]{:S(2)}, u32[]{:S(2)}) %collective-permute-start.2) | collective-permute-done | bytes 557088 | tf_op jit(solution)/shard_map/ppermute | solution.py:281
  33.6 1.4 %collective-permute-done.3.refs_0_ = bf16[272,1024]{1,0:T(8,128)(2,1)S(1)} collective-permute-done((bf16[272,1024]{1,0:T(8,128)(2,1)S(1)}, bf16[272,1024]{1,0:T(8,128)(2,1)S(1)}, u32[]{:S(2)}, u32[]{:S(2)}) %collective-permute-start.3) | collective-permute-done | bytes 557088 | tf_op jit(solution)/shard_map/ppermute | solution.py:304
  35.0 1.2 %collective-permute-start.4 = (bf16[272,1024]{1,0:T(8,128)(2,1)S(1)}, bf16[272,1024]{1,0:T(8,128)(2,1)S(1)}, u32[]{:S(2)}, u32[]{:S(2)}) collective-permute-start(bf16[272,1024]{1,0:T(8,128)(2,1)S(1)} %collective-permute-done.3.refs_0_), channel_id=1, source_target_pairs={{0,2},{2,0},{1,3},{3,1},{4,6},{6,4},{5,7},{7,5},{8,10},{10,8},{9,1... | collective-permute-start | bytes 1671176 | tf_op jit(solution)/shard_map/ppermute | solution.py:281
  36.2 0.8 collective-permute-start.5
  37.0 3.7 %chunk.5 = (bf16[256,1024]{1,0:T(8,128)(2,1)S(1)}, bf16[4,96,1024]{2,1,0:T(8,128)(2,1)S(1)}, bf16[4,96,1024]{2,1,0:T(8,128)(2,1)S(1)}, bf16[4,96,768]{2,1,0:T(8,128)(2,1)S(1)}) custom-call(s32[1]{0:T(128)} %bitcast.first_ref, bf16[272,1024]{1,0:T(8,128)(2,1)S(1)} %collective-permute-done.1.refs_0_, bf16[272,1024]{1,0:T(8,128)(2,1)S(1)} %collective-permute-done.2.refs_1_, ...), custom_call_target="tpu_custom_call" | custom-call | flops 1610612736 | bytes 8388608 | tf_op jit(solution)/shard_map/chunk/pallas_call | solution.py:171
  40.7 6.6 %collective-permute-done.4.refs_1_ = bf16[272,1024]{1,0:T(8,128)(2,1)S(1)} collective-permute-done((bf16[272,1024]{1,0:T(8,128)(2,1)S(1)}, bf16[272,1024]{1,0:T(8,128)(2,1)S(1)}, u32[]{:S(2)}, u32[]{:S(2)}) %collective-permute-start.4) | collective-permute-done | bytes 557088 | tf_op jit(solution)/shard_map/ppermute | solution.py:281
  47.3 1.5 %collective-permute-done.5.refs_0_ = bf16[272,1024]{1,0:T(8,128)(2,1)S(1)} collective-permute-done((bf16[272,1024]{1,0:T(8,128)(2,1)S(1)}, bf16[272,1024]{1,0:T(8,128)(2,1)S(1)}, u32[]{:S(2)}, u32[]{:S(2)}) %collective-permute-start.5) | collective-permute-done | bytes 557088 | tf_op jit(solution)/shard_map/ppermute | solution.py:304
  48.8 1.1 %collective-permute-start.6 = (bf16[272,1024]{1,0:T(8,128)(2,1)S(1)}, bf16[272,1024]{1,0:T(8,128)(2,1)S(1)}, u32[]{:S(2)}, u32[]{:S(2)}) collective-permute-start(bf16[272,1024]{1,0:T(8,128)(2,1)S(1)} %collective-permute-done.5.refs_0_), channel_id=1, source_target_pairs={{0,2},{2,0},{1,3},{3,1},{4,6},{6,4},{5,7},{7,5},{8,10},{10,8},{9,1... | collective-permute-start | bytes 1671176 | tf_op jit(solution)/shard_map/ppermute | solution.py:281
  49.9 3.7 %chunk.6 = (bf16[128,1024]{1,0:T(8,128)(2,1)S(1)}, bf16[128,1024]{1,0:T(8,128)(2,1)S(1)}, bf16[4,96,1024]{2,1,0:T(8,128)(2,1)S(1)}, bf16[4,96,1024]{2,1,0:T(8,128)(2,1)S(1)}, bf16[4,96,768]{2,1,0:T(8,128)(2,1)S(1)}) custom-call(s32[1]{0:T(128)} %bitcast.first_ref, bf16[272,1024]{1,0:T(8,128)(2,1)S(1)} %collective-permute-done.3.refs_0_, ...), custom_call_target="tpu_custom_call" | custom-call | flops 1610612736 | bytes 8388608 | tf_op jit(solution)/shard_map/chunk/pallas_call | solution.py:171
  53.6 6.2 %collective-permute-done.6.refs_1_ = bf16[272,1024]{1,0:T(8,128)(2,1)S(1)} collective-permute-done((bf16[272,1024]{1,0:T(8,128)(2,1)S(1)}, bf16[272,1024]{1,0:T(8,128)(2,1)S(1)}, u32[]{:S(2)}, u32[]{:S(2)}) %collective-permute-start.6) | collective-permute-done | bytes 557088 | tf_op jit(solution)/shard_map/ppermute | solution.py:281
  59.8 1.6 %collective-permute-start.7 = (bf16[256,1024]{1,0:T(8,128)(2,1)S(1)}, bf16[256,1024]{1,0:T(8,128)(2,1)S(1)}, u32[]{:S(2)}, u32[]{:S(2)}) collective-permute-start(bf16[256,1024]{1,0:T(8,128)(2,1)S(1)} %get-tuple-element.167), channel_id=1, source_target_pairs={{0,8},{4,0},{12,4},{8,12},{1,9},{5,1},{13,5},{9,13},{2,10},{6,2},{... | collective-permute-start | bytes 1572872 | tf_op jit(solution)/shard_map/ppermute | solution.py:313
  61.4 0.7 collective-permute-start.8
  62.1 3.7 %chunk.7 = (bf16[128,1024]{1,0:T(8,128)(2,1)S(1)}, bf16[128,1024]{1,0:T(8,128)(2,1)S(1)}, bf16[4,96,1024]{2,1,0:T(8,128)(2,1)S(1)}, bf16[4,96,1024]{2,1,0:T(8,128)(2,1)S(1)}, bf16[4,96,768]{2,1,0:T(8,128)(2,1)S(1)}) custom-call(s32[1]{0:T(128)} %bitcast.first_ref, bf16[272,1024]{1,0:T(8,128)(2,1)S(1)} %collective-permute-done.5.refs_0_, ...), custom_call_target="tpu_custom_call" | custom-call | flops 1610612736 | bytes 8388608 | tf_op jit(solution)/shard_map/chunk/pallas_call | solution.py:171
  65.8 4.2 %collective-permute-done.8 = bf16[128,1024]{1,0:T(8,128)(2,1)S(1)} collective-permute-done((bf16[128,1024]{1,0:T(8,128)(2,1)S(1)}, bf16[128,1024]{1,0:T(8,128)(2,1)S(1)}, u32[]{:S(2)}, u32[]{:S(2)}) %collective-permute-start.8) | collective-permute-done | bytes 262176 | tf_op jit(solution)/shard_map/ppermute | solution.py:288
  70.0 0.7 collective-permute-done.7
  70.7 1.5 %collective-permute-start.9 = (bf16[128,1024]{1,0:T(8,128)(2,1)S(1)}, bf16[128,1024]{1,0:T(8,128)(2,1)S(1)}, u32[]{:S(2)}, u32[]{:S(2)}) collective-permute-start(bf16[128,1024]{1,0:T(8,128)(2,1)S(1)} %get-tuple-element.202), channel_id=1, source_target_pairs={{0,2},{2,0},{1,3},{3,1},{4,6},{6,4},{5,7},{7,5},{8,10},{10,8},{9,1... | collective-permute-start | bytes 786440 | tf_op jit(solution)/shard_map/ppermute | solution.py:288
  72.3 0.1 add_convert_fusion.3
  72.3 3.8 %collective-permute-start.10 = (bf16[128,1024]{1,0:T(8,128)(2,1)S(1)}, bf16[128,1024]{1,0:T(8,128)(2,1)S(1)}, u32[]{:S(2)}, u32[]{:S(2)}) collective-permute-start(bf16[128,1024]{1,0:T(8,128)(2,1)S(1)} %add_convert_fusion.3), channel_id=1, source_target_pairs={{0,4},{4,12},{12,8},{8,0},{1,5},{5,13},{13,9},{9,1},{2,6},{6,14},{... | collective-permute-start | bytes 786440 | tf_op jit(solution)/shard_map/ppermute | solution.py:298
  76.1 1.9 %weight_grads.2 = bf16[4,768,512]{2,1,0:T(8,128)(2,1)S(1)} custom-call(s32[1]{0:T(128)S(6)} %sub.3.side_ref, bf16[4,96,1024]{2,1,0:T(8,128)(2,1)S(1)} %get-tuple-element.189.refs_0_, bf16[4,96,1024]{2,1,0:T(8,128)(2,1)S(1)} %get-tuple-element.190.refs_1_, bf16[4,96,1024]{2,1,0:T(8,128)(2,1)S(1)} %get-tuple-element.191.refs_2_, ...), custom_call_target="tpu_custom_call" | custom-call | flops 1207959552 | bytes 8650752 | tf_op jit(solution)/shard_map/weight_grads/pallas_call | solution.py:244
  78.0 0.0 collective-permute-done.9
  78.0 2.3 %collective-permute-done.10 = bf16[128,1024]{1,0:T(8,128)(2,1)S(1)} collective-permute-done((bf16[128,1024]{1,0:T(8,128)(2,1)S(1)}, bf16[128,1024]{1,0:T(8,128)(2,1)S(1)}, u32[]{:S(2)}, u32[]{:S(2)}) %collective-permute-start.10) | collective-permute-done | bytes 262176 | tf_op jit(solution)/shard_map/ppermute | solution.py:298
  80.3 0.0 collective-permute-start.11
  80.3 0.1 add_convert_fusion.1
  80.4 1.6 %collective-permute-start.13 = (bf16[128,1024]{1,0:T(8,128)(2,1)S(1)}, bf16[128,1024]{1,0:T(8,128)(2,1)S(1)}, u32[]{:S(2)}, u32[]{:S(2)}) collective-permute-start(bf16[128,1024]{1,0:T(8,128)(2,1)S(1)} %add_convert_fusion.1), channel_id=1, source_target_pairs={{0,2},{2,0},{1,3},{3,1},{4,6},{6,4},{5,7},{7,5},{8,10},{10,8},{9,1... | collective-permute-start | bytes 786440 | tf_op jit(solution)/shard_map/ppermute | solution.py:288
  81.9 0.1 add_convert_fusion.2
  82.1 2.5 %collective-permute-start.12 = (bf16[128,1024]{1,0:T(8,128)(2,1)S(1)}, bf16[128,1024]{1,0:T(8,128)(2,1)S(1)}, u32[]{:S(2)}, u32[]{:S(2)}) collective-permute-start(bf16[128,1024]{1,0:T(8,128)(2,1)S(1)} %add_convert_fusion.2), channel_id=1, source_target_pairs={{0,4},{4,12},{12,8},{8,0},{1,5},{5,13},{13,9},{9,1},{2,6},{6,14},{... | collective-permute-start | bytes 786440 | tf_op jit(solution)/shard_map/ppermute | solution.py:298
  84.6 1.4 %collective-permute-done.11.refs_12_ = bf16[4,768,512]{2,1,0:T(8,128)(2,1)S(1)} collective-permute-done((bf16[4,768,512]{2,1,0:T(8,128)(2,1)S(1)}, bf16[4,768,512]{2,1,0:T(8,128)(2,1)S(1)}, u32[]{:S(2)}, u32[]{:S(2)}) %collective-permute-start.11) | collective-permute-done | bytes 3145760 | tf_op jit(solution)/shard_map/ppermute | solution.py:324
  86.0 2.7 %weight_grads.3 = (bf16[4,512,256]{2,1,0:T(8,128)(2,1)}, bf16[4,512,256]{2,1,0:T(8,128)(2,1)}, bf16[4,256,512]{2,1,0:T(8,128)(2,1)}) custom-call(s32[1]{0:T(128)} %bitcast.1.side_ref, bf16[4,96,1024]{2,1,0:T(8,128)(2,1)S(1)} %get-tuple-element.189.refs_0_, bf16[4,96,1024]{2,1,0:T(8,128)(2,1)S(1)} %get-tuple-element.190.refs_1_, ...), custom_call_target="tpu_custom_call" | custom-call | flops 1207959552 | bytes 8650752 | tf_op jit(solution)/shard_map/weight_grads/pallas_call | solution.py:244
  88.7 0.5 collective-permute-done.13
  89.2 2.3 %collective-permute-done.12 = bf16[128,1024]{1,0:T(8,128)(2,1)S(1)} collective-permute-done((bf16[128,1024]{1,0:T(8,128)(2,1)S(1)}, bf16[128,1024]{1,0:T(8,128)(2,1)S(1)}, u32[]{:S(2)}, u32[]{:S(2)}) %collective-permute-start.12) | collective-permute-done | bytes 262176 | tf_op jit(solution)/shard_map/ppermute | solution.py:298
  91.4 0.9 add_convert_fusion
Async XLA Ops:
  2.4 15.6 %collective-permute-start = (bf16[272,1024]{1,0:T(8,128)(2,1)S(1)}, bf16[272,1024]{1,0:T(8,128)(2,1)S(1)}, u32[]{:S(2)}, u32[]{:S(2)}) collective-permute-start(bf16[272,1024]{1,0:T(8,128)(2,1)S(1)} %pack.1.refs_0_), channel_id=1, source_target_pairs={{0,2},{2,0},{1,3},{3,1},{4,6},{6,4},{5,7},{7,5},{8,10},{10,8},{9,1... | collective-permute-start | bytes 1671176 | tf_op jit(solution)/shard_map/ppermute | solution.py:281
  5.4 15.0 %collective-permute-start.1 = (bf16[272,1024]{1,0:T(8,128)(2,1)S(1)}, bf16[272,1024]{1,0:T(8,128)(2,1)S(1)}, u32[]{:S(2)}, u32[]{:S(2)}) collective-permute-start(bf16[272,1024]{1,0:T(8,128)(2,1)S(1)} %pack.1.refs_0_), channel_id=1, source_target_pairs={{0,4},{4,12},{12,8},{8,0},{1,5},{5,13},{13,9},{9,1},{2,6},{6,14},{... | collective-permute-start | bytes 1671176 | tf_op jit(solution)/shard_map/ppermute | solution.py:304
  20.4 13.2 %collective-permute-start.2 = (bf16[272,1024]{1,0:T(8,128)(2,1)S(1)}, bf16[272,1024]{1,0:T(8,128)(2,1)S(1)}, u32[]{:S(2)}, u32[]{:S(2)}) collective-permute-start(bf16[272,1024]{1,0:T(8,128)(2,1)S(1)} %collective-permute-done.1.refs_0_), channel_id=1, source_target_pairs={{0,2},{2,0},{1,3},{3,1},{4,6},{6,4},{5,7},{7,5},{8,10},{10,8},{9,1... | collective-permute-start | bytes 1671176 | tf_op jit(solution)/shard_map/ppermute | solution.py:281
  20.9 14.1 %collective-permute-start.3 = (bf16[272,1024]{1,0:T(8,128)(2,1)S(1)}, bf16[272,1024]{1,0:T(8,128)(2,1)S(1)}, u32[]{:S(2)}, u32[]{:S(2)}) collective-permute-start(bf16[272,1024]{1,0:T(8,128)(2,1)S(1)} %collective-permute-done.1.refs_0_), channel_id=1, source_target_pairs={{0,4},{4,12},{12,8},{8,0},{1,5},{5,13},{13,9},{9,1},{2,6},{6,14},{... | collective-permute-start | bytes 1671176 | tf_op jit(solution)/shard_map/ppermute | solution.py:304
  35.0 12.3 %collective-permute-start.4 = (bf16[272,1024]{1,0:T(8,128)(2,1)S(1)}, bf16[272,1024]{1,0:T(8,128)(2,1)S(1)}, u32[]{:S(2)}, u32[]{:S(2)}) collective-permute-start(bf16[272,1024]{1,0:T(8,128)(2,1)S(1)} %collective-permute-done.3.refs_0_), channel_id=1, source_target_pairs={{0,2},{2,0},{1,3},{3,1},{4,6},{6,4},{5,7},{7,5},{8,10},{10,8},{9,1... | collective-permute-start | bytes 1671176 | tf_op jit(solution)/shard_map/ppermute | solution.py:281
  36.2 12.6 %collective-permute-start.5 = (bf16[272,1024]{1,0:T(8,128)(2,1)S(1)}, bf16[272,1024]{1,0:T(8,128)(2,1)S(1)}, u32[]{:S(2)}, u32[]{:S(2)}) collective-permute-start(bf16[272,1024]{1,0:T(8,128)(2,1)S(1)} %collective-permute-done.3.refs_0_), channel_id=1, source_target_pairs={{0,4},{4,12},{12,8},{8,0},{1,5},{5,13},{13,9},{9,1},{2,6},{6,14},{... | collective-permute-start | bytes 1671176 | tf_op jit(solution)/shard_map/ppermute | solution.py:304
  48.8 11.0 %collective-permute-start.6 = (bf16[272,1024]{1,0:T(8,128)(2,1)S(1)}, bf16[272,1024]{1,0:T(8,128)(2,1)S(1)}, u32[]{:S(2)}, u32[]{:S(2)}) collective-permute-start(bf16[272,1024]{1,0:T(8,128)(2,1)S(1)} %collective-permute-done.5.refs_0_), channel_id=1, source_target_pairs={{0,2},{2,0},{1,3},{3,1},{4,6},{6,4},{5,7},{7,5},{8,10},{10,8},{9,1... | collective-permute-start | bytes 1671176 | tf_op jit(solution)/shard_map/ppermute | solution.py:281
  59.8 10.9 %collective-permute-start.7 = (bf16[256,1024]{1,0:T(8,128)(2,1)S(1)}, bf16[256,1024]{1,0:T(8,128)(2,1)S(1)}, u32[]{:S(2)}, u32[]{:S(2)}) collective-permute-start(bf16[256,1024]{1,0:T(8,128)(2,1)S(1)} %get-tuple-element.167), channel_id=1, source_target_pairs={{0,8},{4,0},{12,4},{8,12},{1,9},{5,1},{13,5},{9,13},{2,10},{6,2},{... | collective-permute-start | bytes 1572872 | tf_op jit(solution)/shard_map/ppermute | solution.py:313
  61.4 8.6 %collective-permute-start.8 = (bf16[128,1024]{1,0:T(8,128)(2,1)S(1)}, bf16[128,1024]{1,0:T(8,128)(2,1)S(1)}, u32[]{:S(2)}, u32[]{:S(2)}) collective-permute-start(bf16[128,1024]{1,0:T(8,128)(2,1)S(1)} %get-tuple-element.172), channel_id=1, source_target_pairs={{0,2},{2,0},{1,3},{3,1},{4,6},{6,4},{5,7},{7,5},{8,10},{10,8},{9,1... | collective-permute-start | bytes 786440 | tf_op jit(solution)/shard_map/ppermute | solution.py:288
  70.7 7.3 %collective-permute-start.9 = (bf16[128,1024]{1,0:T(8,128)(2,1)S(1)}, bf16[128,1024]{1,0:T(8,128)(2,1)S(1)}, u32[]{:S(2)}, u32[]{:S(2)}) collective-permute-start(bf16[128,1024]{1,0:T(8,128)(2,1)S(1)} %get-tuple-element.202), channel_id=1, source_target_pairs={{0,2},{2,0},{1,3},{3,1},{4,6},{6,4},{5,7},{7,5},{8,10},{10,8},{9,1... | collective-permute-start | bytes 786440 | tf_op jit(solution)/shard_map/ppermute | solution.py:288
  72.3 8.0 %collective-permute-start.10 = (bf16[128,1024]{1,0:T(8,128)(2,1)S(1)}, bf16[128,1024]{1,0:T(8,128)(2,1)S(1)}, u32[]{:S(2)}, u32[]{:S(2)}) collective-permute-start(bf16[128,1024]{1,0:T(8,128)(2,1)S(1)} %add_convert_fusion.3), channel_id=1, source_target_pairs={{0,4},{4,12},{12,8},{8,0},{1,5},{5,13},{13,9},{9,1},{2,6},{6,14},{... | collective-permute-start | bytes 786440 | tf_op jit(solution)/shard_map/ppermute | solution.py:298
  80.3 5.7 %collective-permute-start.11 = (bf16[4,768,512]{2,1,0:T(8,128)(2,1)S(1)}, bf16[4,768,512]{2,1,0:T(8,128)(2,1)S(1)}, u32[]{:S(2)}, u32[]{:S(2)}) collective-permute-start(bf16[4,768,512]{2,1,0:T(8,128)(2,1)S(1)} %weight_grads.2), channel_id=1, source_target_pairs={{0,1},{1,0},{2,3},{3,2},{4,5},{5,4},{6,7},{7,6},{8,9},{9,8},{10,11... | collective-permute-start | bytes 9437192 | tf_op jit(solution)/shard_map/ppermute | solution.py:324
  80.4 8.8 %collective-permute-start.13 = (bf16[128,1024]{1,0:T(8,128)(2,1)S(1)}, bf16[128,1024]{1,0:T(8,128)(2,1)S(1)}, u32[]{:S(2)}, u32[]{:S(2)}) collective-permute-start(bf16[128,1024]{1,0:T(8,128)(2,1)S(1)} %add_convert_fusion.1), channel_id=1, source_target_pairs={{0,2},{2,0},{1,3},{3,1},{4,6},{6,4},{5,7},{7,5},{8,10},{10,8},{9,1... | collective-permute-start | bytes 786440 | tf_op jit(solution)/shard_map/ppermute | solution.py:288
  82.1 9.4 %collective-permute-start.12 = (bf16[128,1024]{1,0:T(8,128)(2,1)S(1)}, bf16[128,1024]{1,0:T(8,128)(2,1)S(1)}, u32[]{:S(2)}, u32[]{:S(2)}) collective-permute-start(bf16[128,1024]{1,0:T(8,128)(2,1)S(1)} %add_convert_fusion.2), channel_id=1, source_target_pairs={{0,4},{4,12},{12,8},{8,0},{1,5},{5,13},{13,9},{9,1},{2,6},{6,14},{... | collective-permute-start | bytes 786440 | tf_op jit(solution)/shard_map/ppermute | solution.py:298

commit v10 on v9

--- a/solution.py
+++ b/solution.py
@@ -33,20 +33,20 @@
     return [0] + list(range(1, size, 2)) + list(range(2, size, 2))[::-1]
 
 
-def pack_kernel(tokens, upstream, expert_ids, slots, gate_fixed, out, sem):
+def pack_kernel(tokens, upstream, expert_ids, slots, gate_fixed, tokens_out, out, sem):
     top_count, tok_rows = expert_ids.shape
     copies = [
-        pltpu.make_async_copy(src, out.at[pl.ds(i * tok_rows, tok_rows), :], sem.at[i])
-        for i, src in enumerate((tokens, upstream))
+        pltpu.make_async_copy(tokens, tokens_out, sem.at[0]),
+        pltpu.make_async_copy(upstream, out.at[pl.ds(0, tok_rows), :], sem.at[1]),
     ]
     for copy in copies:
         copy.start()
     gate = gate_fixed[...]
-    out[2 * tok_rows :, :] = jnp.zeros((ROUTE_ROWS, out.shape[1]), jnp.bfloat16)
+    out[tok_rows:, :] = jnp.zeros((ROUTE_ROWS, out.shape[1]), jnp.bfloat16)
     for i, field in enumerate((expert_ids[...], slots[...], gate >> 8, gate & 255)):
         empty = jnp.zeros((ROUTE_ROWS - top_count, tok_rows), jnp.float32)
         field = jnp.concatenate([field.astype(jnp.float32), empty], axis=0)
-        out[2 * tok_rows :, i * tok_rows : (i + 1) * tok_rows] = field.astype(jnp.bfloat16)
+        out[tok_rows:, i * tok_rows : (i + 1) * tok_rows] = field.astype(jnp.bfloat16)
     for copy in copies:
         copy.wait()
 
@@ -58,8 +58,8 @@
     return pl.pallas_call(
         pack_kernel,
         in_specs=[hbm] * 2 + [vmem] * 3,
-        out_specs=vmem,
-        out_shape=pltpu.VMEM((2 * tok_rows + ROUTE_ROWS, width), jnp.bfloat16),
+        out_specs=[vmem] * 2,
+        out_shape=[pltpu.VMEM((rows, width), jnp.bfloat16) for rows in (tok_rows, tok_rows + ROUTE_ROWS)],
         scratch_shapes=[pltpu.SemaphoreType.DMA((2,))],
         compiler_params=pltpu.CompilerParams(vmem_limit_bytes=VMEM_LIMIT),
         name="pack",
@@ -107,15 +107,15 @@
 
 
 def chunk_kernel(n_blocks, tok_rows, capacity, rows, top_count, per_group, first_ref, *refs):
-    payloads = refs[:n_blocks]
-    w_gate, w_up, w_down = refs[n_blocks : n_blocks + 3]
-    parts = refs[n_blocks + 3 : -4]
+    tokens, upstream = refs[:n_blocks], refs[n_blocks : 2 * n_blocks]
+    w_gate, w_up, w_down = refs[2 * n_blocks : 2 * n_blocks + 3]
+    parts = refs[2 * n_blocks + 3 : -4]
     x_rows, s_rows, hids, back_all = refs[-4:]
     experts, width, ff = w_gate.shape
 
     pairs = []
     for b in range(n_blocks):
-        route = payloads[b][2 * tok_rows : 2 * tok_rows + ROUTE_ROWS, :].astype(jnp.float32)
+        route = upstream[b][tok_rows : tok_rows + ROUTE_ROWS, :].astype(jnp.float32)
         pairs.append(
             route_keys(route, first_ref[0], experts, capacity, rows, b * capacity, tok_rows, top_count, per_group)
         )
@@ -131,11 +131,11 @@
     hot = hot.astype(jnp.bfloat16)
     row_gate = jnp.sum(gate_hot, axis=1, keepdims=True)
 
-    x_all = jnp.concatenate([payload[:tok_rows, :] for payload in payloads], axis=0)
+    x_all = jnp.concatenate([block[...] for block in tokens], axis=0)
     gathered = dot(hot, x_all, (1, 0)).astype(jnp.bfloat16)
     for e in range(experts):
         x_rows[e] = gathered[e * rows : (e + 1) * rows, :]
-    u_all = jnp.concatenate([payload[tok_rows : 2 * tok_rows, :] for payload in payloads], axis=0)
+    u_all = jnp.concatenate([block[:tok_rows, :] for block in upstream], axis=0)
     scaled = (dot(hot, u_all, (1, 0)) * row_gate).astype(jnp.bfloat16)
     for e in range(experts):
         s_rows[e] = scaled[e * rows : (e + 1) * rows, :]
@@ -160,8 +160,8 @@
         start += part.shape[0]
 
 
-def chunk_call(payloads, first_expert, weights, tok_rows, capacity, rows, top_count, per_group, joined):
-    n_blocks = len(payloads)
+def chunk_call(tokens, upstream, first_expert, weights, tok_rows, capacity, rows, top_count, per_group, joined):
+    n_blocks = len(tokens)
     n_tok = n_blocks * tok_rows
     experts, width, ff = weights[0].shape
     part_shapes = [(n_tok, width)] if joined else [(tok_rows, width), (n_tok - tok_rows, width)]
@@ -170,7 +170,7 @@
     out_shapes = part_shapes + kept_shapes
     return pl.pallas_call(
         functools.partial(chunk_kernel, n_blocks, tok_rows, capacity, rows, top_count, per_group),
-        in_specs=[smem] + [vmem] * (n_blocks + 3),
+        in_specs=[smem] + [vmem] * (2 * n_blocks + 3),
         out_specs=[vmem] * len(out_shapes),
         out_shape=[pltpu.VMEM(shape, jnp.bfloat16) for shape in out_shapes],
         scratch_shapes=[pltpu.VMEM((experts * rows, width), jnp.bfloat16)],
@@ -181,7 +181,7 @@
             transcendentals=0,
         ),
         name="chunk",
-    )(first_expert, *[in_vmem(v) for v in payloads], *[in_vmem(w) for w in weights])
+    )(first_expert, *[in_vmem(v) for v in (*tokens, *upstream, *weights)])
 
 
 def halves_of(n, e, side, refs):
@@ -281,7 +281,7 @@
         return [column] + [lax.ppermute(column, "ingroup", shift(s)) for s in range(1, n_ingroup)]
 
     def chunk(blocks, joined=False):
-        return chunk_call(blocks, first_expert, weights, tok_rows, capacity, rows, top_count, per_group, joined)
+        return chunk_call(*blocks, first_expert, weights, tok_rows, capacity, rows, top_count, per_group, joined)
 
     def across(others):
         return [
@@ -298,22 +298,29 @@
         return lax.ppermute(group_part, "group", along(-k))
 
     tokens, first_expert, half, other_half = tie(tokens, first_expert, half, 1 - half)
-    column = pack_call(tokens, upstream, expert_ids, slots, gate_fixed)
-    blocks, chunks, backs, sent = {}, {}, {}, {}
+    first_tokens, upstream = pack_call(tokens, upstream, expert_ids, slots, gate_fixed)
+    blocks, chunks, backs, sent, near = {}, {}, {}, {}, None
+    last = n_group - 1
     for k in range(n_group):
-        ahead = lax.ppermute(column, "group", along(1)) if k < n_group - 1 else None
-        pair = spread(column)
+        pair = [spread(tokens), spread(upstream)]
+        if k == 0:
+            pair[0][0] = first_tokens
+        if k < last:
+            tokens, upstream = (lax.ppermute(v, "group", along(1)) for v in (tokens, upstream))
         if k > 0:
             chunks[k - 1] = chunk(blocks[k - 1], k - 1 == 1)
-        blocks[k], column, chunks, weights = tie(pair, ahead, chunks, weights)
-
-    last = n_group - 1
+        if k == last:
+            near = lax.ppermute(chunks[1][0], "group", along(-1))
+        tokens, pair[0], chunks, weights = tie(tokens, pair[0], chunks, weights)
+        upstream, pair[1] = tie(upstream, pair[1])
+        blocks[k] = pair
+
     for k in range(2, last - 1):
         sent[k] = homeward(group_sum(chunks[k][0], across(chunks[k][1])), k)
-    near = lax.ppermute(chunks[1][0], "group", along(-1))
+    blocks[last], chunks, near = tie(blocks[last], chunks, near)
     backs[last - 1] = across(chunks[last - 1][1])
     chunks[last] = chunk(blocks[last])
-    chunks, near, backs = tie(chunks, near, backs)
+    chunks, backs = tie(chunks, backs)
 
     backs[last] = across(chunks[last][1])
     carried = homeward(group_sum(chunks[last - 1][0], backs[last - 1]), last)

time: 92.5 us -> 91.3 us (0.987)
  waiting for transfers between devices: 45.8 us -> 28.7 us
  starting transfers between devices: 20.8 us -> 36.6 us
    ppermute x4 -> x8, waiting for transfers between devices: 29.1 us -> 9.13 us  [spread(): lax.ppermute(column, 'ingroup', shift(s))]
    ppermute x2, starting transfers between devices: 6.34 us -> 14.9 us  [homeward(): return lax.ppermute(group_part, 'group', along(-k))]
    ppermute x3 -> x6, starting transfers between devices: 3.2 us -> 10.2 us  [per_device(): lax.ppermute(v, 'group', along(1))]
    ppermute x3 -> x6, waiting for transfers between devices: 5.3 us -> 9.68 us  [per_device(): lax.ppermute(v, 'group', along(1))]
    ppermute x3, starting transfers between devices: 3.8 us -> 0.92 us  [across(): lax.ppermute(others[(s - 1) * tok_rows:s * tok_rows], 'ingroup', shift(-s))]
    ppermute x4 -> x8, starting transfers between devices: 5.83 us -> 8.38 us  [spread(): lax.ppermute(column, 'ingroup', shift(s))]
    ppermute x2, waiting for transfers between devices: 4.57 us -> 2.91 us  [homeward(): return lax.ppermute(group_part, 'group', along(-k))]
  transfers between devices with their start and end apart: 14 -> 21, of which waited for: 13 -> 15; matrix products, arithmetic and copies ran while one was open for 0% -> 0% of each run, Pallas kernels for 24% -> 26%
where the time goes in v10:
time: 91.3 us; the launch traced here: 91.1 us
  starting transfers between devices  36.6 us (40%)
  waiting for transfers between devices  28.7 us (31%)
  Pallas kernels  23.9 us (26%)
  other arithmetic  1.13 us (1%)
    ppermute x2, starting transfers between devices, homeward(): return lax.ppermute(group_part, 'group', along(-k))  14.9 us
    pallas_call x4, Pallas kernels, chunk_call(): pl.pallas_call(functools.partial(chunk_kernel, n_blocks, tok_rows, capaci...  14.7 us
    ppermute x6, starting transfers between devices, per_device(): lax.ppermute(v, 'group', along(1))  10.2 us
    ppermute x6, waiting for transfers between devices, per_device(): lax.ppermute(v, 'group', along(1))  9.68 us
    ppermute x8, waiting for transfers between devices, spread(): lax.ppermute(column, 'ingroup', shift(s))  9.13 us
    ppermute x8, starting transfers between devices, spread(): lax.ppermute(column, 'ingroup', shift(s))  8.38 us
    ppermute x3, waiting for transfers between devices, across(): lax.ppermute(others[(s - 1) * tok_rows:s * tok_rows], 'ingroup', shift(-s))  5.38 us
    pallas_call x2, Pallas kernels, weight_call(): pl.pallas_call(functools.partial(kernel, n), in_specs=[smem] + [vmem] * l...  4.56 us
  transfers between devices with their start and end apart: 21, of which 15 were waited for; matrix products, arithmetic and copies ran while one was open for 0% of the time, Pallas kernels for 26%

profile of v10, /device:TPU:0, one launch (start us, length us, event | category | flops | bytes accessed | tf_op | source)
XLA Modules:
  0.0 91.1 jit_solution(18179798725573850034)
XLA Ops:
  0.6 3.0 %collective-permute-start.1 = (bf16[128,1024]{1,0:T(8,128)(2,1)}, bf16[128,1024]{1,0:T(8,128)(2,1)S(1)}, u32[]{:S(2)}, u32[]{:S(2)}) collective-permute-start(bf16[128,1024]{1,0:T(8,128)(2,1)} %tokens), channel_id=1, source_target_pairs={{0,2},{2,0},{1,3},{3,1},{4,6},{6,4},{5,7},{7,5},{8,10},{10,8},{9,1... | collective-permute-start | bytes 786440 | tf_op jit(solution)/shard_map/ppermute | solution.py:281
  3.6 1.6 %collective-permute-start = (bf16[128,1024]{1,0:T(8,128)(2,1)}, bf16[128,1024]{1,0:T(8,128)(2,1)S(1)}, u32[]{:S(2)}, u32[]{:S(2)}) collective-permute-start(bf16[128,1024]{1,0:T(8,128)(2,1)} %tokens), channel_id=1, source_target_pairs={{0,4},{4,12},{12,8},{8,0},{1,5},{5,13},{13,9},{9,1},{2,6},{6,14},{... | collective-permute-start | bytes 786440 | tf_op jit(solution)/shard_map/ppermute | solution.py:309
  5.2 1.8 %pack.1 = (bf16[128,1024]{1,0:T(8,128)(2,1)S(1)}, bf16[144,1024]{1,0:T(8,128)(2,1)S(1)}) custom-call(bf16[128,1024]{1,0:T(8,128)(2,1)} %tokens, bf16[128,1024]{1,0:T(8,128)(2,1)} %upstream.1, s32[8,128]{1,0:T(8,128)} %bitcast.5, s32[8,128]{1,0:T(8,128)} %bitcast.6, s32[8,128]{1,0:T(8,128)} %bitcast.7), custom_call_target="tpu_custom_call" | custom-call | tf_op jit(solution)/shard_map/pack/pallas_call | solution.py:58
  7.0 0.6 collective-permute-start.5
  7.6 2.6 %collective-permute-start.4 = (bf16[144,1024]{1,0:T(8,128)(2,1)S(1)}, bf16[144,1024]{1,0:T(8,128)(2,1)S(1)}, u32[]{:S(2)}, u32[]{:S(2)}) collective-permute-start(bf16[144,1024]{1,0:T(8,128)(2,1)S(1)} %get-tuple-element.150.refs_2_), channel_id=1, source_target_pairs={{0,4},{4,12},{12,8},{8,0},{1,5},{5,13},{13,9},{9,1},{2,6},{6,14},{... | collective-permute-start | bytes 884744 | tf_op jit(solution)/shard_map/ppermute | solution.py:309
  10.2 2.9 %load.1 = (bf16[4,1024,256]{2,1,0:T(8,128)(2,1)S(1)}, bf16[4,1024,256]{2,1,0:T(8,128)(2,1)S(1)}, bf16[4,256,1024]{2,1,0:T(8,128)(2,1)S(1)}) custom-call(bf16[4,1024,256]{2,1,0:T(8,128)(2,1)} %refs_0_.1, bf16[4,1024,256]{2,1,0:T(8,128)(2,1)} %refs_1_.1, bf16[4,256,1024]{2,1,0:T(8,128)(2,1)} %refs_2_.1), custom_call_target="tpu_custom_call" | custom-call | tf_op jit(solution)/shard_map/load/pallas_call | solution.py:98
  13.1 0.0 collective-permute-done.1.refs_1_
  13.1 0.9 collective-permute-done.refs_0_
  14.0 0.7 collective-permute-start.3
  14.7 0.8 collective-permute-start.2
  15.4 1.9 %collective-permute-done.5.refs_3_ = bf16[144,1024]{1,0:T(8,128)(2,1)S(1)} collective-permute-done((bf16[144,1024]{1,0:T(8,128)(2,1)S(1)}, bf16[144,1024]{1,0:T(8,128)(2,1)S(1)}, u32[]{:S(2)}, u32[]{:S(2)}) %collective-permute-start.5) | collective-permute-done | bytes 294944 | tf_op jit(solution)/shard_map/ppermute | solution.py:281
  17.3 3.0 %collective-permute-done.4.refs_2_ = bf16[144,1024]{1,0:T(8,128)(2,1)S(1)} collective-permute-done((bf16[144,1024]{1,0:T(8,128)(2,1)S(1)}, bf16[144,1024]{1,0:T(8,128)(2,1)S(1)}, u32[]{:S(2)}, u32[]{:S(2)}) %collective-permute-start.4) | collective-permute-done | bytes 294944 | tf_op jit(solution)/shard_map/ppermute | solution.py:309
  20.3 0.2 collective-permute-start.9
  20.5 1.1 %collective-permute-start.8 = (bf16[144,1024]{1,0:T(8,128)(2,1)S(1)}, bf16[144,1024]{1,0:T(8,128)(2,1)S(1)}, u32[]{:S(2)}, u32[]{:S(2)}) collective-permute-start(bf16[144,1024]{1,0:T(8,128)(2,1)S(1)} %collective-permute-done.4.refs_2_), channel_id=1, source_target_pairs={{0,4},{4,12},{12,8},{8,0},{1,5},{5,13},{13,9},{9,1},{2,6},{6,14},{... | collective-permute-start | bytes 884744 | tf_op jit(solution)/shard_map/ppermute | solution.py:309
  21.6 3.7 %chunk.4 = (bf16[128,1024]{1,0:T(8,128)(2,1)S(1)}, bf16[128,1024]{1,0:T(8,128)(2,1)S(1)}, bf16[4,96,1024]{2,1,0:T(8,128)(2,1)S(1)}, bf16[4,96,1024]{2,1,0:T(8,128)(2,1)S(1)}, bf16[4,96,768]{2,1,0:T(8,128)(2,1)S(1)}) custom-call(s32[1]{0:T(128)} %bitcast.first_ref, bf16[128,1024]{1,0:T(8,128)(2,1)S(1)} %get-tuple-element.147.refs_0_, ...), custom_call_target="tpu_custom_call" | custom-call | flops 1610612736 | bytes 8388608 | tf_op jit(solution)/shard_map/chunk/pallas_call | solution.py:171
  25.3 0.0 collective-permute-done.3.refs_1_
  25.3 0.6 collective-permute-done.2.refs_0_
  25.9 1.0 %collective-permute-start.7 = (bf16[128,1024]{1,0:T(8,128)(2,1)S(1)}, bf16[128,1024]{1,0:T(8,128)(2,1)S(1)}, u32[]{:S(2)}, u32[]{:S(2)}) collective-permute-start(bf16[128,1024]{1,0:T(8,128)(2,1)S(1)} %collective-permute-done.2.refs_0_), channel_id=1, source_target_pairs={{0,2},{2,0},{1,3},{3,1},{4,6},{6,4},{5,7},{7,5},{8,10},{10,8},{9,1... | collective-permute-start | bytes 786440 | tf_op jit(solution)/shard_map/ppermute | solution.py:281
  26.9 3.4 %collective-permute-start.6 = (bf16[128,1024]{1,0:T(8,128)(2,1)S(1)}, bf16[128,1024]{1,0:T(8,128)(2,1)S(1)}, u32[]{:S(2)}, u32[]{:S(2)}) collective-permute-start(bf16[128,1024]{1,0:T(8,128)(2,1)S(1)} %collective-permute-done.2.refs_0_), channel_id=1, source_target_pairs={{0,4},{4,12},{12,8},{8,0},{1,5},{5,13},{13,9},{9,1},{2,6},{6,14},{... | collective-permute-start | bytes 786440 | tf_op jit(solution)/shard_map/ppermute | solution.py:309
  30.3 0.0 collective-permute-done.9.refs_3_
  30.3 2.0 %collective-permute-done.8.refs_2_ = bf16[144,1024]{1,0:T(8,128)(2,1)S(1)} collective-permute-done((bf16[144,1024]{1,0:T(8,128)(2,1)S(1)}, bf16[144,1024]{1,0:T(8,128)(2,1)S(1)}, u32[]{:S(2)}, u32[]{:S(2)}) %collective-permute-start.8) | collective-permute-done | bytes 294944 | tf_op jit(solution)/shard_map/ppermute | solution.py:309
  32.2 0.9 %collective-permute-start.12 = (bf16[144,1024]{1,0:T(8,128)(2,1)S(1)}, bf16[144,1024]{1,0:T(8,128)(2,1)S(1)}, u32[]{:S(2)}, u32[]{:S(2)}) collective-permute-start(bf16[144,1024]{1,0:T(8,128)(2,1)S(1)} %collective-permute-done.8.refs_2_), channel_id=1, source_target_pairs={{0,2},{2,0},{1,3},{3,1},{4,6},{6,4},{5,7},{7,5},{8,10},{10,8},{9,1... | collective-permute-start | bytes 884744 | tf_op jit(solution)/shard_map/ppermute | solution.py:281
  33.2 0.8 collective-permute-start.11
  34.0 3.7 %chunk.5 = (bf16[256,1024]{1,0:T(8,128)(2,1)S(1)}, bf16[4,96,1024]{2,1,0:T(8,128)(2,1)S(1)}, bf16[4,96,1024]{2,1,0:T(8,128)(2,1)S(1)}, bf16[4,96,768]{2,1,0:T(8,128)(2,1)S(1)}) custom-call(s32[1]{0:T(128)} %bitcast.first_ref, bf16[128,1024]{1,0:T(8,128)(2,1)S(1)} %collective-permute-done.refs_0_, bf16[128,1024]{1,0:T(8,128)(2,1)S(1)} %collective-permute-done.3.refs_1_, ...), custom_call_target="tpu_custom_call" | custom-call | flops 1610612736 | bytes 8388608 | tf_op jit(solution)/shard_map/chunk/pallas_call | solution.py:171
  37.7 0.0 collective-permute-done.7.refs_1_
  37.7 0.2 collective-permute-done.6.refs_0_
  37.9 2.2 %collective-permute-start.14 = (bf16[256,1024]{1,0:T(8,128)(2,1)S(1)}, bf16[256,1024]{1,0:T(8,128)(2,1)S(1)}, u32[]{:S(2)}, u32[]{:S(2)}) collective-permute-start(bf16[256,1024]{1,0:T(8,128)(2,1)S(1)} %get-tuple-element.184), channel_id=1, source_target_pairs={{0,8},{4,0},{12,4},{8,12},{1,9},{5,1},{13,5},{9,13},{2,10},{6,2},{... | collective-permute-start | bytes 1572872 | tf_op jit(solution)/shard_map/ppermute | solution.py:313
  40.1 0.3 collective-permute-done.12.refs_3_
  40.4 3.0 %collective-permute-done.11.refs_2_ = bf16[144,1024]{1,0:T(8,128)(2,1)S(1)} collective-permute-done((bf16[144,1024]{1,0:T(8,128)(2,1)S(1)}, bf16[144,1024]{1,0:T(8,128)(2,1)S(1)}, u32[]{:S(2)}, u32[]{:S(2)}) %collective-permute-start.11) | collective-permute-done | bytes 294944 | tf_op jit(solution)/shard_map/ppermute | solution.py:309
  43.3 0.5 collective-permute-start.13
  43.9 1.5 %collective-permute-start.10 = (bf16[128,1024]{1,0:T(8,128)(2,1)S(1)}, bf16[128,1024]{1,0:T(8,128)(2,1)S(1)}, u32[]{:S(2)}, u32[]{:S(2)}) collective-permute-start(bf16[128,1024]{1,0:T(8,128)(2,1)S(1)} %collective-permute-done.6.refs_0_), channel_id=1, source_target_pairs={{0,2},{2,0},{1,3},{3,1},{4,6},{6,4},{5,7},{7,5},{8,10},{10,8},{9,1... | collective-permute-start | bytes 786440 | tf_op jit(solution)/shard_map/ppermute | solution.py:281
  45.4 3.7 %chunk.6 = (bf16[128,1024]{1,0:T(8,128)(2,1)S(1)}, bf16[128,1024]{1,0:T(8,128)(2,1)S(1)}, bf16[4,96,1024]{2,1,0:T(8,128)(2,1)S(1)}, bf16[4,96,1024]{2,1,0:T(8,128)(2,1)S(1)}, bf16[4,96,768]{2,1,0:T(8,128)(2,1)S(1)}) custom-call(s32[1]{0:T(128)} %bitcast.first_ref, bf16[128,1024]{1,0:T(8,128)(2,1)S(1)} %collective-permute-done.2.refs_0_, ...), custom_call_target="tpu_custom_call" | custom-call | flops 1610612736 | bytes 8388608 | tf_op jit(solution)/shard_map/chunk/pallas_call | solution.py:171
  49.0 6.9 %collective-permute-done.10.refs_1_ = bf16[128,1024]{1,0:T(8,128)(2,1)S(1)} collective-permute-done((bf16[128,1024]{1,0:T(8,128)(2,1)S(1)}, bf16[128,1024]{1,0:T(8,128)(2,1)S(1)}, u32[]{:S(2)}, u32[]{:S(2)}) %collective-permute-start.10) | collective-permute-done | bytes 262176 | tf_op jit(solution)/shard_map/ppermute | solution.py:281
  56.0 0.0 collective-permute-done.13.refs_3_
  56.0 0.0 collective-permute-done.14
  56.0 0.3 collective-permute-start.15
  56.3 3.7 %chunk.7 = (bf16[128,1024]{1,0:T(8,128)(2,1)S(1)}, bf16[128,1024]{1,0:T(8,128)(2,1)S(1)}, bf16[4,96,1024]{2,1,0:T(8,128)(2,1)S(1)}, bf16[4,96,1024]{2,1,0:T(8,128)(2,1)S(1)}, bf16[4,96,768]{2,1,0:T(8,128)(2,1)S(1)}) custom-call(s32[1]{0:T(128)} %bitcast.first_ref, bf16[128,1024]{1,0:T(8,128)(2,1)S(1)} %collective-permute-done.6.refs_0_, ...), custom_call_target="tpu_custom_call" | custom-call | flops 1610612736 | bytes 8388608 | tf_op jit(solution)/shard_map/chunk/pallas_call | solution.py:171
  59.9 2.4 %collective-permute-done.15 = bf16[128,1024]{1,0:T(8,128)(2,1)S(1)} collective-permute-done((bf16[128,1024]{1,0:T(8,128)(2,1)S(1)}, bf16[128,1024]{1,0:T(8,128)(2,1)S(1)}, u32[]{:S(2)}, u32[]{:S(2)}) %collective-permute-start.15) | collective-permute-done | bytes 262176 | tf_op jit(solution)/shard_map/ppermute | solution.py:288
  62.4 0.1 add_convert_fusion.3
  62.4 11.4 %collective-permute-start.17 = (bf16[128,1024]{1,0:T(8,128)(2,1)S(1)}, bf16[128,1024]{1,0:T(8,128)(2,1)S(1)}, u32[]{:S(2)}, u32[]{:S(2)}) collective-permute-start(bf16[128,1024]{1,0:T(8,128)(2,1)S(1)} %add_convert_fusion.3), channel_id=1, source_target_pairs={{0,4},{4,12},{12,8},{8,0},{1,5},{5,13},{13,9},{9,1},{2,6},{6,14},{... | collective-permute-start | bytes 786440 | tf_op jit(solution)/shard_map/ppermute | solution.py:298
  73.8 0.3 collective-permute-start.16
  74.1 1.9 %weight_grads.2 = bf16[4,768,512]{2,1,0:T(8,128)(2,1)S(1)} custom-call(s32[1]{0:T(128)S(6)} %sub.3.side_ref, bf16[4,96,1024]{2,1,0:T(8,128)(2,1)S(1)} %get-tuple-element.247.refs_0_, bf16[4,96,1024]{2,1,0:T(8,128)(2,1)S(1)} %get-tuple-element.248.refs_1_, bf16[4,96,1024]{2,1,0:T(8,128)(2,1)S(1)} %get-tuple-element.249.refs_2_, ...), custom_call_target="tpu_custom_call" | custom-call | flops 1207959552 | bytes 8650752 | tf_op jit(solution)/shard_map/weight_grads/pallas_call | solution.py:244
  75.9 1.7 %collective-permute-done.17 = bf16[128,1024]{1,0:T(8,128)(2,1)S(1)} collective-permute-done((bf16[128,1024]{1,0:T(8,128)(2,1)S(1)}, bf16[128,1024]{1,0:T(8,128)(2,1)S(1)}, u32[]{:S(2)}, u32[]{:S(2)}) %collective-permute-start.17) | collective-permute-done | bytes 262176 | tf_op jit(solution)/shard_map/ppermute | solution.py:298
  77.7 2.5 %collective-permute-done.16 = bf16[128,1024]{1,0:T(8,128)(2,1)S(1)} collective-permute-done((bf16[128,1024]{1,0:T(8,128)(2,1)S(1)}, bf16[128,1024]{1,0:T(8,128)(2,1)S(1)}, u32[]{:S(2)}, u32[]{:S(2)}) %collective-permute-start.16) | collective-permute-done | bytes 262176 | tf_op jit(solution)/shard_map/ppermute | solution.py:288
  80.2 0.0 collective-permute-start.18
  80.2 0.1 add_convert_fusion.1
  80.2 0.3 collective-permute-start.20
  80.6 0.1 add_convert_fusion.2
  80.7 3.5 %collective-permute-start.19 = (bf16[128,1024]{1,0:T(8,128)(2,1)S(1)}, bf16[128,1024]{1,0:T(8,128)(2,1)S(1)}, u32[]{:S(2)}, u32[]{:S(2)}) collective-permute-start(bf16[128,1024]{1,0:T(8,128)(2,1)S(1)} %add_convert_fusion.2), channel_id=1, source_target_pairs={{0,4},{4,12},{12,8},{8,0},{1,5},{5,13},{13,9},{9,1},{2,6},{6,14},{... | collective-permute-start | bytes 786440 | tf_op jit(solution)/shard_map/ppermute | solution.py:298
  84.2 1.6 %collective-permute-done.18.refs_12_ = bf16[4,768,512]{2,1,0:T(8,128)(2,1)S(1)} collective-permute-done((bf16[4,768,512]{2,1,0:T(8,128)(2,1)S(1)}, bf16[4,768,512]{2,1,0:T(8,128)(2,1)S(1)}, u32[]{:S(2)}, u32[]{:S(2)}) %collective-permute-start.18) | collective-permute-done | bytes 3145760 | tf_op jit(solution)/shard_map/ppermute | solution.py:331
  85.8 2.7 %weight_grads.3 = (bf16[4,512,256]{2,1,0:T(8,128)(2,1)}, bf16[4,512,256]{2,1,0:T(8,128)(2,1)}, bf16[4,256,512]{2,1,0:T(8,128)(2,1)}) custom-call(s32[1]{0:T(128)} %bitcast.1.side_ref, bf16[4,96,1024]{2,1,0:T(8,128)(2,1)S(1)} %get-tuple-element.247.refs_0_, bf16[4,96,1024]{2,1,0:T(8,128)(2,1)S(1)} %get-tuple-element.248.refs_1_, ...), custom_call_target="tpu_custom_call" | custom-call | flops 1207959552 | bytes 8650752 | tf_op jit(solution)/shard_map/weight_grads/pallas_call | solution.py:244
  88.5 0.5 collective-permute-done.20
  89.0 1.2 %collective-permute-done.19 = bf16[128,1024]{1,0:T(8,128)(2,1)S(1)} collective-permute-done((bf16[128,1024]{1,0:T(8,128)(2,1)S(1)}, bf16[128,1024]{1,0:T(8,128)(2,1)S(1)}, u32[]{:S(2)}, u32[]{:S(2)}) %collective-permute-start.19) | collective-permute-done | bytes 262176 | tf_op jit(solution)/shard_map/ppermute | solution.py:298
  90.2 0.9 add_convert_fusion
Async XLA Ops:
  0.6 12.4 %collective-permute-start.1 = (bf16[128,1024]{1,0:T(8,128)(2,1)}, bf16[128,1024]{1,0:T(8,128)(2,1)S(1)}, u32[]{:S(2)}, u32[]{:S(2)}) collective-permute-start(bf16[128,1024]{1,0:T(8,128)(2,1)} %tokens), channel_id=1, source_target_pairs={{0,2},{2,0},{1,3},{3,1},{4,6},{6,4},{5,7},{7,5},{8,10},{10,8},{9,1... | collective-permute-start | bytes 786440 | tf_op jit(solution)/shard_map/ppermute | solution.py:281
  3.6 10.3 %collective-permute-start = (bf16[128,1024]{1,0:T(8,128)(2,1)}, bf16[128,1024]{1,0:T(8,128)(2,1)S(1)}, u32[]{:S(2)}, u32[]{:S(2)}) collective-permute-start(bf16[128,1024]{1,0:T(8,128)(2,1)} %tokens), channel_id=1, source_target_pairs={{0,4},{4,12},{12,8},{8,0},{1,5},{5,13},{13,9},{9,1},{2,6},{6,14},{... | collective-permute-start | bytes 786440 | tf_op jit(solution)/shard_map/ppermute | solution.py:309
  7.0 10.3 %collective-permute-start.5 = (bf16[144,1024]{1,0:T(8,128)(2,1)S(1)}, bf16[144,1024]{1,0:T(8,128)(2,1)S(1)}, u32[]{:S(2)}, u32[]{:S(2)}) collective-permute-start(bf16[144,1024]{1,0:T(8,128)(2,1)S(1)} %get-tuple-element.150.refs_2_), channel_id=1, source_target_pairs={{0,2},{2,0},{1,3},{3,1},{4,6},{6,4},{5,7},{7,5},{8,10},{10,8},{9,1... | collective-permute-start | bytes 884744 | tf_op jit(solution)/shard_map/ppermute | solution.py:281
  7.6 12.7 %collective-permute-start.4 = (bf16[144,1024]{1,0:T(8,128)(2,1)S(1)}, bf16[144,1024]{1,0:T(8,128)(2,1)S(1)}, u32[]{:S(2)}, u32[]{:S(2)}) collective-permute-start(bf16[144,1024]{1,0:T(8,128)(2,1)S(1)} %get-tuple-element.150.refs_2_), channel_id=1, source_target_pairs={{0,4},{4,12},{12,8},{8,0},{1,5},{5,13},{13,9},{9,1},{2,6},{6,14},{... | collective-permute-start | bytes 884744 | tf_op jit(solution)/shard_map/ppermute | solution.py:309
  14.0 11.3 %collective-permute-start.3 = (bf16[128,1024]{1,0:T(8,128)(2,1)S(1)}, bf16[128,1024]{1,0:T(8,128)(2,1)S(1)}, u32[]{:S(2)}, u32[]{:S(2)}) collective-permute-start(bf16[128,1024]{1,0:T(8,128)(2,1)S(1)} %collective-permute-done.refs_0_), channel_id=1, source_target_pairs={{0,2},{2,0},{1,3},{3,1},{4,6},{6,4},{5,7},{7,5},{8,10},{10,8},{9,1... | collective-permute-start | bytes 786440 | tf_op jit(solution)/shard_map/ppermute | solution.py:281
  14.7 11.3 %collective-permute-start.2 = (bf16[128,1024]{1,0:T(8,128)(2,1)S(1)}, bf16[128,1024]{1,0:T(8,128)(2,1)S(1)}, u32[]{:S(2)}, u32[]{:S(2)}) collective-permute-start(bf16[128,1024]{1,0:T(8,128)(2,1)S(1)} %collective-permute-done.refs_0_), channel_id=1, source_target_pairs={{0,4},{4,12},{12,8},{8,0},{1,5},{5,13},{13,9},{9,1},{2,6},{6,14},{... | collective-permute-start | bytes 786440 | tf_op jit(solution)/shard_map/ppermute | solution.py:309
  20.3 10.0 %collective-permute-start.9 = (bf16[144,1024]{1,0:T(8,128)(2,1)S(1)}, bf16[144,1024]{1,0:T(8,128)(2,1)S(1)}, u32[]{:S(2)}, u32[]{:S(2)}) collective-permute-start(bf16[144,1024]{1,0:T(8,128)(2,1)S(1)} %collective-permute-done.4.refs_2_), channel_id=1, source_target_pairs={{0,2},{2,0},{1,3},{3,1},{4,6},{6,4},{5,7},{7,5},{8,10},{10,8},{9,1... | collective-permute-start | bytes 884744 | tf_op jit(solution)/shard_map/ppermute | solution.py:281
  20.5 11.7 %collective-permute-start.8 = (bf16[144,1024]{1,0:T(8,128)(2,1)S(1)}, bf16[144,1024]{1,0:T(8,128)(2,1)S(1)}, u32[]{:S(2)}, u32[]{:S(2)}) collective-permute-start(bf16[144,1024]{1,0:T(8,128)(2,1)S(1)} %collective-permute-done.4.refs_2_), channel_id=1, source_target_pairs={{0,4},{4,12},{12,8},{8,0},{1,5},{5,13},{13,9},{9,1},{2,6},{6,14},{... | collective-permute-start | bytes 884744 | tf_op jit(solution)/shard_map/ppermute | solution.py:309
  25.9 11.7 %collective-permute-start.7 = (bf16[128,1024]{1,0:T(8,128)(2,1)S(1)}, bf16[128,1024]{1,0:T(8,128)(2,1)S(1)}, u32[]{:S(2)}, u32[]{:S(2)}) collective-permute-start(bf16[128,1024]{1,0:T(8,128)(2,1)S(1)} %collective-permute-done.2.refs_0_), channel_id=1, source_target_pairs={{0,2},{2,0},{1,3},{3,1},{4,6},{6,4},{5,7},{7,5},{8,10},{10,8},{9,1... | collective-permute-start | bytes 786440 | tf_op jit(solution)/shard_map/ppermute | solution.py:281
  26.9 11.0 %collective-permute-start.6 = (bf16[128,1024]{1,0:T(8,128)(2,1)S(1)}, bf16[128,1024]{1,0:T(8,128)(2,1)S(1)}, u32[]{:S(2)}, u32[]{:S(2)}) collective-permute-start(bf16[128,1024]{1,0:T(8,128)(2,1)S(1)} %collective-permute-done.2.refs_0_), channel_id=1, source_target_pairs={{0,4},{4,12},{12,8},{8,0},{1,5},{5,13},{13,9},{9,1},{2,6},{6,14},{... | collective-permute-start | bytes 786440 | tf_op jit(solution)/shard_map/ppermute | solution.py:309
  32.2 8.1 %collective-permute-start.12 = (bf16[144,1024]{1,0:T(8,128)(2,1)S(1)}, bf16[144,1024]{1,0:T(8,128)(2,1)S(1)}, u32[]{:S(2)}, u32[]{:S(2)}) collective-permute-start(bf16[144,1024]{1,0:T(8,128)(2,1)S(1)} %collective-permute-done.8.refs_2_), channel_id=1, source_target_pairs={{0,2},{2,0},{1,3},{3,1},{4,6},{6,4},{5,7},{7,5},{8,10},{10,8},{9,1... | collective-permute-start | bytes 884744 | tf_op jit(solution)/shard_map/ppermute | solution.py:281
  33.2 10.2 %collective-permute-start.11 = (bf16[144,1024]{1,0:T(8,128)(2,1)S(1)}, bf16[144,1024]{1,0:T(8,128)(2,1)S(1)}, u32[]{:S(2)}, u32[]{:S(2)}) collective-permute-start(bf16[144,1024]{1,0:T(8,128)(2,1)S(1)} %collective-permute-done.8.refs_2_), channel_id=1, source_target_pairs={{0,4},{4,12},{12,8},{8,0},{1,5},{5,13},{13,9},{9,1},{2,6},{6,14},{... | collective-permute-start | bytes 884744 | tf_op jit(solution)/shard_map/ppermute | solution.py:309
  37.9 18.1 %collective-permute-start.14 = (bf16[256,1024]{1,0:T(8,128)(2,1)S(1)}, bf16[256,1024]{1,0:T(8,128)(2,1)S(1)}, u32[]{:S(2)}, u32[]{:S(2)}) collective-permute-start(bf16[256,1024]{1,0:T(8,128)(2,1)S(1)} %get-tuple-element.184), channel_id=1, source_target_pairs={{0,8},{4,0},{12,4},{8,12},{1,9},{5,1},{13,5},{9,13},{2,10},{6,2},{... | collective-permute-start | bytes 1572872 | tf_op jit(solution)/shard_map/ppermute | solution.py:313
  43.3 12.6 %collective-permute-start.13 = (bf16[144,1024]{1,0:T(8,128)(2,1)S(1)}, bf16[144,1024]{1,0:T(8,128)(2,1)S(1)}, u32[]{:S(2)}, u32[]{:S(2)}) collective-permute-start(bf16[144,1024]{1,0:T(8,128)(2,1)S(1)} %collective-permute-done.11.refs_2_), channel_id=1, source_target_pairs={{0,2},{2,0},{1,3},{3,1},{4,6},{6,4},{5,7},{7,5},{8,10},{10,8},{9,1... | collective-permute-start | bytes 884744 | tf_op jit(solution)/shard_map/ppermute | solution.py:281
  43.9 12.1 %collective-permute-start.10 = (bf16[128,1024]{1,0:T(8,128)(2,1)S(1)}, bf16[128,1024]{1,0:T(8,128)(2,1)S(1)}, u32[]{:S(2)}, u32[]{:S(2)}) collective-permute-start(bf16[128,1024]{1,0:T(8,128)(2,1)S(1)} %collective-permute-done.6.refs_0_), channel_id=1, source_target_pairs={{0,2},{2,0},{1,3},{3,1},{4,6},{6,4},{5,7},{7,5},{8,10},{10,8},{9,1... | collective-permute-start | bytes 786440 | tf_op jit(solution)/shard_map/ppermute | solution.py:281
  56.0 6.4 %collective-permute-start.15 = (bf16[128,1024]{1,0:T(8,128)(2,1)S(1)}, bf16[128,1024]{1,0:T(8,128)(2,1)S(1)}, u32[]{:S(2)}, u32[]{:S(2)}) collective-permute-start(bf16[128,1024]{1,0:T(8,128)(2,1)S(1)} %get-tuple-element.228), channel_id=1, source_target_pairs={{0,2},{2,0},{1,3},{3,1},{4,6},{6,4},{5,7},{7,5},{8,10},{10,8},{9,1... | collective-permute-start | bytes 786440 | tf_op jit(solution)/shard_map/ppermute | solution.py:288
  62.4 15.3 %collective-permute-start.17 = (bf16[128,1024]{1,0:T(8,128)(2,1)S(1)}, bf16[128,1024]{1,0:T(8,128)(2,1)S(1)}, u32[]{:S(2)}, u32[]{:S(2)}) collective-permute-start(bf16[128,1024]{1,0:T(8,128)(2,1)S(1)} %add_convert_fusion.3), channel_id=1, source_target_pairs={{0,4},{4,12},{12,8},{8,0},{1,5},{5,13},{13,9},{9,1},{2,6},{6,14},{... | collective-permute-start | bytes 786440 | tf_op jit(solution)/shard_map/ppermute | solution.py:298
  73.8 6.4 %collective-permute-start.16 = (bf16[128,1024]{1,0:T(8,128)(2,1)S(1)}, bf16[128,1024]{1,0:T(8,128)(2,1)S(1)}, u32[]{:S(2)}, u32[]{:S(2)}) collective-permute-start(bf16[128,1024]{1,0:T(8,128)(2,1)S(1)} %get-tuple-element.260), channel_id=1, source_target_pairs={{0,2},{2,0},{1,3},{3,1},{4,6},{6,4},{5,7},{7,5},{8,10},{10,8},{9,1... | collective-permute-start | bytes 786440 | tf_op jit(solution)/shard_map/ppermute | solution.py:288
  80.2 5.7 %collective-permute-start.18 = (bf16[4,768,512]{2,1,0:T(8,128)(2,1)S(1)}, bf16[4,768,512]{2,1,0:T(8,128)(2,1)S(1)}, u32[]{:S(2)}, u32[]{:S(2)}) collective-permute-start(bf16[4,768,512]{2,1,0:T(8,128)(2,1)S(1)} %weight_grads.2), channel_id=1, source_target_pairs={{0,1},{1,0},{2,3},{3,2},{4,5},{5,4},{6,7},{7,6},{8,9},{9,8},{10,11... | collective-permute-start | bytes 9437192 | tf_op jit(solution)/shard_map/ppermute | solution.py:331
  80.2 8.8 %collective-permute-start.20 = (bf16[128,1024]{1,0:T(8,128)(2,1)S(1)}, bf16[128,1024]{1,0:T(8,128)(2,1)S(1)}, u32[]{:S(2)}, u32[]{:S(2)}) collective-permute-start(bf16[128,1024]{1,0:T(8,128)(2,1)S(1)} %add_convert_fusion.1), channel_id=1, source_target_pairs={{0,2},{2,0},{1,3},{3,1},{4,6},{6,4},{5,7},{7,5},{8,10},{10,8},{9,1... | collective-permute-start | bytes 786440 | tf_op jit(solution)/shard_map/ppermute | solution.py:288
  80.7 9.5 %collective-permute-start.19 = (bf16[128,1024]{1,0:T(8,128)(2,1)S(1)}, bf16[128,1024]{1,0:T(8,128)(2,1)S(1)}, u32[]{:S(2)}, u32[]{:S(2)}) collective-permute-start(bf16[128,1024]{1,0:T(8,128)(2,1)S(1)} %add_convert_fusion.2), channel_id=1, source_target_pairs={{0,4},{4,12},{12,8},{8,0},{1,5},{5,13},{13,9},{9,1},{2,6},{6,14},{... | collective-permute-start | bytes 786440 | tf_op jit(solution)/shard_map/ppermute | solution.py:298

commit v11 on v10

--- a/solution.py
+++ b/solution.py
@@ -299,7 +299,7 @@
 
     tokens, first_expert, half, other_half = tie(tokens, first_expert, half, 1 - half)
     first_tokens, upstream = pack_call(tokens, upstream, expert_ids, slots, gate_fixed)
-    blocks, chunks, backs, sent, near = {}, {}, {}, {}, None
+    blocks, chunks, backs, sent = {}, {}, {}, {}
     last = n_group - 1
     for k in range(n_group):
         pair = [spread(tokens), spread(upstream)]
@@ -309,18 +309,17 @@
             tokens, upstream = (lax.ppermute(v, "group", along(1)) for v in (tokens, upstream))
         if k > 0:
             chunks[k - 1] = chunk(blocks[k - 1], k - 1 == 1)
-        if k == last:
-            near = lax.ppermute(chunks[1][0], "group", along(-1))
         tokens, pair[0], chunks, weights = tie(tokens, pair[0], chunks, weights)
         upstream, pair[1] = tie(upstream, pair[1])
         blocks[k] = pair
 
     for k in range(2, last - 1):
         sent[k] = homeward(group_sum(chunks[k][0], across(chunks[k][1])), k)
-    blocks[last], chunks, near = tie(blocks[last], chunks, near)
+    near = lax.ppermute(chunks[1][0], "group", along(-1))
+    blocks[last], chunks = tie(blocks[last], chunks)
     backs[last - 1] = across(chunks[last - 1][1])
     chunks[last] = chunk(blocks[last])
-    chunks, backs = tie(chunks, backs)
+    chunks, backs, near = tie(chunks, backs, near)
 
     backs[last] = across(chunks[last][1])
     carried = homeward(group_sum(chunks[last - 1][0], backs[last - 1]), last)

time: 91.3 us -> 81 us (0.89)
  waiting for transfers between devices: 28.7 us -> 20.7 us
  starting transfers between devices: 36.6 us -> 34.2 us
    ppermute x2, starting transfers between devices: 14.9 us -> 5.41 us  [homeward(): return lax.ppermute(group_part, 'group', along(-k))]
    ppermute x6, waiting for transfers between devices: 9.68 us -> 4.04 us  [per_device(): lax.ppermute(v, 'group', along(1))]
    ppermute x6, starting transfers between devices: 10.2 us -> 13.8 us  [per_device(): lax.ppermute(v, 'group', along(1))]
    ppermute x3, waiting for transfers between devices: 5.38 us -> 1.84 us  [across(): lax.ppermute(others[(s - 1) * tok_rows:s * tok_rows], 'ingroup', shift(-s))]
    ppermute x3, starting transfers between devices: 0.92 us -> 3.58 us  [across(): lax.ppermute(others[(s - 1) * tok_rows:s * tok_rows], 'ingroup', shift(-s))]
    ppermute x1, waiting for transfers between devices: 1.58 us -> 2.86 us  [per_device(): got = lax.ppermute(to_send, 'dp', [(0, 1), (1, 0)])]
    ppermute x8, starting transfers between devices: 8.38 us -> 9.6 us  [spread(): lax.ppermute(column, 'ingroup', shift(s))]
    ppermute x8, waiting for transfers between devices: 9.13 us -> 8.15 us  [spread(): lax.ppermute(column, 'ingroup', shift(s))]
  transfers between devices with their start and end apart: 21 -> 21, of which waited for: 15 -> 14; matrix products, arithmetic and copies ran while one was open for 0% -> 0% of each run, Pallas kernels for 26% -> 30%
where the time goes in v11:
time: 81 us; the launch traced here: 80.8 us
  starting transfers between devices  34.2 us (42%)
  Pallas kernels  23.9 us (30%)
  waiting for transfers between devices  20.7 us (26%)
  other arithmetic  1.13 us (1%)
    pallas_call x4, Pallas kernels, chunk_call(): pl.pallas_call(functools.partial(chunk_kernel, n_blocks, tok_rows, capaci...  14.7 us
    ppermute x6, starting transfers between devices, per_device(): lax.ppermute(v, 'group', along(1))  13.8 us
    ppermute x8, starting transfers between devices, spread(): lax.ppermute(column, 'ingroup', shift(s))  9.6 us
    ppermute x8, waiting for transfers between devices, spread(): lax.ppermute(column, 'ingroup', shift(s))  8.15 us
    ppermute x2, starting transfers between devices, homeward(): return lax.ppermute(group_part, 'group', along(-k))  5.41 us
    pallas_call x2, Pallas kernels, weight_call(): pl.pallas_call(functools.partial(kernel, n), in_specs=[smem] + [vmem] * l...  4.57 us
    ppermute x6, waiting for transfers between devices, per_device(): lax.ppermute(v, 'group', along(1))  4.04 us
    ppermute x3, starting transfers between devices, across(): lax.ppermute(others[(s - 1) * tok_rows:s * tok_rows], 'ingroup', shift(-s))  3.58 us
  transfers between devices with their start and end apart: 21, of which 14 were waited for; matrix products, arithmetic and copies ran while one was open for 0% of the time, Pallas kernels for 30%

profile of v11, /device:TPU:0, one launch (start us, length us, event | category | flops | bytes accessed | tf_op | source)
XLA Modules:
  0.0 80.8 jit_solution(5567983539590993040)
XLA Ops:
  0.6 3.1 %collective-permute-start = (bf16[128,1024]{1,0:T(8,128)(2,1)}, bf16[128,1024]{1,0:T(8,128)(2,1)S(1)}, u32[]{:S(2)}, u32[]{:S(2)}) collective-permute-start(bf16[128,1024]{1,0:T(8,128)(2,1)} %tokens), channel_id=1, source_target_pairs={{0,4},{4,12},{12,8},{8,0},{1,5},{5,13},{13,9},{9,1},{2,6},{6,14},{... | collective-permute-start | bytes 786440 | tf_op jit(solution)/shard_map/ppermute | solution.py:309
  3.7 1.5 %collective-permute-start.1 = (bf16[128,1024]{1,0:T(8,128)(2,1)}, bf16[128,1024]{1,0:T(8,128)(2,1)S(1)}, u32[]{:S(2)}, u32[]{:S(2)}) collective-permute-start(bf16[128,1024]{1,0:T(8,128)(2,1)} %tokens), channel_id=1, source_target_pairs={{0,2},{2,0},{1,3},{3,1},{4,6},{6,4},{5,7},{7,5},{8,10},{10,8},{9,1... | collective-permute-start | bytes 786440 | tf_op jit(solution)/shard_map/ppermute | solution.py:281
  5.2 1.8 %pack.1 = (bf16[128,1024]{1,0:T(8,128)(2,1)S(1)}, bf16[144,1024]{1,0:T(8,128)(2,1)S(1)}) custom-call(bf16[128,1024]{1,0:T(8,128)(2,1)} %tokens, bf16[128,1024]{1,0:T(8,128)(2,1)} %upstream.1, s32[8,128]{1,0:T(8,128)} %bitcast.5, s32[8,128]{1,0:T(8,128)} %bitcast.6, s32[8,128]{1,0:T(8,128)} %bitcast.7), custom_call_target="tpu_custom_call" | custom-call | tf_op jit(solution)/shard_map/pack/pallas_call | solution.py:58
  7.0 2.6 %collective-permute-start.4 = (bf16[144,1024]{1,0:T(8,128)(2,1)S(1)}, bf16[144,1024]{1,0:T(8,128)(2,1)S(1)}, u32[]{:S(2)}, u32[]{:S(2)}) collective-permute-start(bf16[144,1024]{1,0:T(8,128)(2,1)S(1)} %get-tuple-element.151.refs_2_), channel_id=1, source_target_pairs={{0,4},{4,12},{12,8},{8,0},{1,5},{5,13},{13,9},{9,1},{2,6},{6,14},{... | collective-permute-start | bytes 884744 | tf_op jit(solution)/shard_map/ppermute | solution.py:309
  9.6 0.5 collective-permute-start.5
  10.2 2.9 %load.1 = (bf16[4,1024,256]{2,1,0:T(8,128)(2,1)S(1)}, bf16[4,1024,256]{2,1,0:T(8,128)(2,1)S(1)}, bf16[4,256,1024]{2,1,0:T(8,128)(2,1)S(1)}) custom-call(bf16[4,1024,256]{2,1,0:T(8,128)(2,1)} %refs_0_.1, bf16[4,1024,256]{2,1,0:T(8,128)(2,1)} %refs_1_.1, bf16[4,256,1024]{2,1,0:T(8,128)(2,1)} %refs_2_.1), custom_call_target="tpu_custom_call" | custom-call | tf_op jit(solution)/shard_map/load/pallas_call | solution.py:98
  13.0 0.0 collective-permute-done.refs_0_
  13.1 0.0 collective-permute-done.1.refs_1_
  13.1 2.7 %collective-permute-start.2 = (bf16[128,1024]{1,0:T(8,128)(2,1)S(1)}, bf16[128,1024]{1,0:T(8,128)(2,1)S(1)}, u32[]{:S(2)}, u32[]{:S(2)}) collective-permute-start(bf16[128,1024]{1,0:T(8,128)(2,1)S(1)} %collective-permute-done.refs_0_), channel_id=1, source_target_pairs={{0,4},{4,12},{12,8},{8,0},{1,5},{5,13},{13,9},{9,1},{2,6},{6,14},{... | collective-permute-start | bytes 786440 | tf_op jit(solution)/shard_map/ppermute | solution.py:309
  15.7 1.5 %collective-permute-start.3 = (bf16[128,1024]{1,0:T(8,128)(2,1)S(1)}, bf16[128,1024]{1,0:T(8,128)(2,1)S(1)}, u32[]{:S(2)}, u32[]{:S(2)}) collective-permute-start(bf16[128,1024]{1,0:T(8,128)(2,1)S(1)} %collective-permute-done.refs_0_), channel_id=1, source_target_pairs={{0,2},{2,0},{1,3},{3,1},{4,6},{6,4},{5,7},{7,5},{8,10},{10,8},{9,1... | collective-permute-start | bytes 786440 | tf_op jit(solution)/shard_map/ppermute | solution.py:281
  17.2 1.2 %collective-permute-done.4.refs_2_ = bf16[144,1024]{1,0:T(8,128)(2,1)S(1)} collective-permute-done((bf16[144,1024]{1,0:T(8,128)(2,1)S(1)}, bf16[144,1024]{1,0:T(8,128)(2,1)S(1)}, u32[]{:S(2)}, u32[]{:S(2)}) %collective-permute-start.4) | collective-permute-done | bytes 294944 | tf_op jit(solution)/shard_map/ppermute | solution.py:309
  18.4 1.2 %collective-permute-done.5.refs_3_ = bf16[144,1024]{1,0:T(8,128)(2,1)S(1)} collective-permute-done((bf16[144,1024]{1,0:T(8,128)(2,1)S(1)}, bf16[144,1024]{1,0:T(8,128)(2,1)S(1)}, u32[]{:S(2)}, u32[]{:S(2)}) %collective-permute-start.5) | collective-permute-done | bytes 294944 | tf_op jit(solution)/shard_map/ppermute | solution.py:281
  19.6 2.5 %collective-permute-start.8 = (bf16[144,1024]{1,0:T(8,128)(2,1)S(1)}, bf16[144,1024]{1,0:T(8,128)(2,1)S(1)}, u32[]{:S(2)}, u32[]{:S(2)}) collective-permute-start(bf16[144,1024]{1,0:T(8,128)(2,1)S(1)} %collective-permute-done.4.refs_2_), channel_id=1, source_target_pairs={{0,4},{4,12},{12,8},{8,0},{1,5},{5,13},{13,9},{9,1},{2,6},{6,14},{... | collective-permute-start | bytes 884744 | tf_op jit(solution)/shard_map/ppermute | solution.py:309
  22.1 1.5 %collective-permute-start.9 = (bf16[144,1024]{1,0:T(8,128)(2,1)S(1)}, bf16[144,1024]{1,0:T(8,128)(2,1)S(1)}, u32[]{:S(2)}, u32[]{:S(2)}) collective-permute-start(bf16[144,1024]{1,0:T(8,128)(2,1)S(1)} %collective-permute-done.4.refs_2_), channel_id=1, source_target_pairs={{0,2},{2,0},{1,3},{3,1},{4,6},{6,4},{5,7},{7,5},{8,10},{10,8},{9,1... | collective-permute-start | bytes 884744 | tf_op jit(solution)/shard_map/ppermute | solution.py:281
  23.6 3.7 %chunk.4 = (bf16[128,1024]{1,0:T(8,128)(2,1)S(1)}, bf16[128,1024]{1,0:T(8,128)(2,1)S(1)}, bf16[4,96,1024]{2,1,0:T(8,128)(2,1)S(1)}, bf16[4,96,1024]{2,1,0:T(8,128)(2,1)S(1)}, bf16[4,96,768]{2,1,0:T(8,128)(2,1)S(1)}) custom-call(s32[1]{0:T(128)} %bitcast.first_ref, bf16[128,1024]{1,0:T(8,128)(2,1)S(1)} %get-tuple-element.148.refs_0_, ...), custom_call_target="tpu_custom_call" | custom-call | flops 1610612736 | bytes 8388608 | tf_op jit(solution)/shard_map/chunk/pallas_call | solution.py:171
  27.2 0.0 collective-permute-done.2.refs_0_
  27.2 0.0 collective-permute-done.3.refs_1_
  27.2 0.9 %collective-permute-start.6 = (bf16[128,1024]{1,0:T(8,128)(2,1)S(1)}, bf16[128,1024]{1,0:T(8,128)(2,1)S(1)}, u32[]{:S(2)}, u32[]{:S(2)}) collective-permute-start(bf16[128,1024]{1,0:T(8,128)(2,1)S(1)} %collective-permute-done.2.refs_0_), channel_id=1, source_target_pairs={{0,4},{4,12},{12,8},{8,0},{1,5},{5,13},{13,9},{9,1},{2,6},{6,14},{... | collective-permute-start | bytes 786440 | tf_op jit(solution)/shard_map/ppermute | solution.py:309
  28.2 1.0 %collective-permute-start.7 = (bf16[128,1024]{1,0:T(8,128)(2,1)S(1)}, bf16[128,1024]{1,0:T(8,128)(2,1)S(1)}, u32[]{:S(2)}, u32[]{:S(2)}) collective-permute-start(bf16[128,1024]{1,0:T(8,128)(2,1)S(1)} %collective-permute-done.2.refs_0_), channel_id=1, source_target_pairs={{0,2},{2,0},{1,3},{3,1},{4,6},{6,4},{5,7},{7,5},{8,10},{10,8},{9,1... | collective-permute-start | bytes 786440 | tf_op jit(solution)/shard_map/ppermute | solution.py:281
  29.2 1.2 %collective-permute-done.8.refs_2_ = bf16[144,1024]{1,0:T(8,128)(2,1)S(1)} collective-permute-done((bf16[144,1024]{1,0:T(8,128)(2,1)S(1)}, bf16[144,1024]{1,0:T(8,128)(2,1)S(1)}, u32[]{:S(2)}, u32[]{:S(2)}) %collective-permute-start.8) | collective-permute-done | bytes 294944 | tf_op jit(solution)/shard_map/ppermute | solution.py:309
  30.4 1.6 %collective-permute-done.9.refs_3_ = bf16[144,1024]{1,0:T(8,128)(2,1)S(1)} collective-permute-done((bf16[144,1024]{1,0:T(8,128)(2,1)S(1)}, bf16[144,1024]{1,0:T(8,128)(2,1)S(1)}, u32[]{:S(2)}, u32[]{:S(2)}) %collective-permute-start.9) | collective-permute-done | bytes 294944 | tf_op jit(solution)/shard_map/ppermute | solution.py:281
  32.0 2.0 %collective-permute-start.11 = (bf16[144,1024]{1,0:T(8,128)(2,1)S(1)}, bf16[144,1024]{1,0:T(8,128)(2,1)S(1)}, u32[]{:S(2)}, u32[]{:S(2)}) collective-permute-start(bf16[144,1024]{1,0:T(8,128)(2,1)S(1)} %collective-permute-done.8.refs_2_), channel_id=1, source_target_pairs={{0,4},{4,12},{12,8},{8,0},{1,5},{5,13},{13,9},{9,1},{2,6},{6,14},{... | collective-permute-start | bytes 884744 | tf_op jit(solution)/shard_map/ppermute | solution.py:309
  34.0 1.5 %collective-permute-start.12 = (bf16[144,1024]{1,0:T(8,128)(2,1)S(1)}, bf16[144,1024]{1,0:T(8,128)(2,1)S(1)}, u32[]{:S(2)}, u32[]{:S(2)}) collective-permute-start(bf16[144,1024]{1,0:T(8,128)(2,1)S(1)} %collective-permute-done.8.refs_2_), channel_id=1, source_target_pairs={{0,2},{2,0},{1,3},{3,1},{4,6},{6,4},{5,7},{7,5},{8,10},{10,8},{9,1... | collective-permute-start | bytes 884744 | tf_op jit(solution)/shard_map/ppermute | solution.py:281
  35.5 3.7 %chunk.5 = (bf16[256,1024]{1,0:T(8,128)(2,1)S(1)}, bf16[4,96,1024]{2,1,0:T(8,128)(2,1)S(1)}, bf16[4,96,1024]{2,1,0:T(8,128)(2,1)S(1)}, bf16[4,96,768]{2,1,0:T(8,128)(2,1)S(1)}) custom-call(s32[1]{0:T(128)} %bitcast.first_ref, bf16[128,1024]{1,0:T(8,128)(2,1)S(1)} %collective-permute-done.refs_0_, bf16[128,1024]{1,0:T(8,128)(2,1)S(1)} %collective-permute-done.3.refs_1_, ...), custom_call_target="tpu_custom_call" | custom-call | flops 1610612736 | bytes 8388608 | tf_op jit(solution)/shard_map/chunk/pallas_call | solution.py:171
  39.2 0.0 collective-permute-done.6.refs_0_
  39.2 0.0 collective-permute-done.7.refs_1_
  39.2 0.6 collective-permute-start.10
  39.8 1.6 %collective-permute-done.11.refs_2_ = bf16[144,1024]{1,0:T(8,128)(2,1)S(1)} collective-permute-done((bf16[144,1024]{1,0:T(8,128)(2,1)S(1)}, bf16[144,1024]{1,0:T(8,128)(2,1)S(1)}, u32[]{:S(2)}, u32[]{:S(2)}) %collective-permute-start.11) | collective-permute-done | bytes 294944 | tf_op jit(solution)/shard_map/ppermute | solution.py:309
  41.4 2.5 %collective-permute-done.12.refs_3_ = bf16[144,1024]{1,0:T(8,128)(2,1)S(1)} collective-permute-done((bf16[144,1024]{1,0:T(8,128)(2,1)S(1)}, bf16[144,1024]{1,0:T(8,128)(2,1)S(1)}, u32[]{:S(2)}, u32[]{:S(2)}) %collective-permute-start.12) | collective-permute-done | bytes 294944 | tf_op jit(solution)/shard_map/ppermute | solution.py:281
  44.0 1.5 %collective-permute-start.13 = (bf16[144,1024]{1,0:T(8,128)(2,1)S(1)}, bf16[144,1024]{1,0:T(8,128)(2,1)S(1)}, u32[]{:S(2)}, u32[]{:S(2)}) collective-permute-start(bf16[144,1024]{1,0:T(8,128)(2,1)S(1)} %collective-permute-done.11.refs_2_), channel_id=1, source_target_pairs={{0,2},{2,0},{1,3},{3,1},{4,6},{6,4},{5,7},{7,5},{8,10},{10,8},{9,1... | collective-permute-start | bytes 884744 | tf_op jit(solution)/shard_map/ppermute | solution.py:281
  45.4 3.7 %chunk.6 = (bf16[128,1024]{1,0:T(8,128)(2,1)S(1)}, bf16[128,1024]{1,0:T(8,128)(2,1)S(1)}, bf16[4,96,1024]{2,1,0:T(8,128)(2,1)S(1)}, bf16[4,96,1024]{2,1,0:T(8,128)(2,1)S(1)}, bf16[4,96,768]{2,1,0:T(8,128)(2,1)S(1)}) custom-call(s32[1]{0:T(128)} %bitcast.first_ref, bf16[128,1024]{1,0:T(8,128)(2,1)S(1)} %collective-permute-done.2.refs_0_, ...), custom_call_target="tpu_custom_call" | custom-call | flops 1610612736 | bytes 8388608 | tf_op jit(solution)/shard_map/chunk/pallas_call | solution.py:171
  49.1 0.4 collective-permute-done.10.refs_1_
  49.6 1.8 %collective-permute-start.15 = (bf16[256,1024]{1,0:T(8,128)(2,1)S(1)}, bf16[256,1024]{1,0:T(8,128)(2,1)S(1)}, u32[]{:S(2)}, u32[]{:S(2)}) collective-permute-start(bf16[256,1024]{1,0:T(8,128)(2,1)S(1)} %get-tuple-element.212), channel_id=1, source_target_pairs={{0,8},{4,0},{12,4},{8,12},{1,9},{5,1},{13,5},{9,13},{2,10},{6,2},{... | collective-permute-start | bytes 1572872 | tf_op jit(solution)/shard_map/ppermute | solution.py:318
  51.4 2.4 %collective-permute-done.13.refs_3_ = bf16[144,1024]{1,0:T(8,128)(2,1)S(1)} collective-permute-done((bf16[144,1024]{1,0:T(8,128)(2,1)S(1)}, bf16[144,1024]{1,0:T(8,128)(2,1)S(1)}, u32[]{:S(2)}, u32[]{:S(2)}) %collective-permute-start.13) | collective-permute-done | bytes 294944 | tf_op jit(solution)/shard_map/ppermute | solution.py:281
  53.8 1.5 %collective-permute-start.14 = (bf16[128,1024]{1,0:T(8,128)(2,1)S(1)}, bf16[128,1024]{1,0:T(8,128)(2,1)S(1)}, u32[]{:S(2)}, u32[]{:S(2)}) collective-permute-start(bf16[128,1024]{1,0:T(8,128)(2,1)S(1)} %get-tuple-element.230), channel_id=1, source_target_pairs={{0,2},{2,0},{1,3},{3,1},{4,6},{6,4},{5,7},{7,5},{8,10},{10,8},{9,1... | collective-permute-start | bytes 786440 | tf_op jit(solution)/shard_map/ppermute | solution.py:288
  55.3 3.7 %chunk.7 = (bf16[128,1024]{1,0:T(8,128)(2,1)S(1)}, bf16[128,1024]{1,0:T(8,128)(2,1)S(1)}, bf16[4,96,1024]{2,1,0:T(8,128)(2,1)S(1)}, bf16[4,96,1024]{2,1,0:T(8,128)(2,1)S(1)}, bf16[4,96,768]{2,1,0:T(8,128)(2,1)S(1)}) custom-call(s32[1]{0:T(128)} %bitcast.first_ref, bf16[128,1024]{1,0:T(8,128)(2,1)S(1)} %collective-permute-done.6.refs_0_, ...), custom_call_target="tpu_custom_call" | custom-call | flops 1610612736 | bytes 8388608 | tf_op jit(solution)/shard_map/chunk/pallas_call | solution.py:171
  59.0 1.3 %collective-permute-done.14 = bf16[128,1024]{1,0:T(8,128)(2,1)S(1)} collective-permute-done((bf16[128,1024]{1,0:T(8,128)(2,1)S(1)}, bf16[128,1024]{1,0:T(8,128)(2,1)S(1)}, u32[]{:S(2)}, u32[]{:S(2)}) %collective-permute-start.14) | collective-permute-done | bytes 262176 | tf_op jit(solution)/shard_map/ppermute | solution.py:288
  60.3 0.5 collective-permute-done.15
  60.8 1.5 %collective-permute-start.16 = (bf16[128,1024]{1,0:T(8,128)(2,1)S(1)}, bf16[128,1024]{1,0:T(8,128)(2,1)S(1)}, u32[]{:S(2)}, u32[]{:S(2)}) collective-permute-start(bf16[128,1024]{1,0:T(8,128)(2,1)S(1)} %get-tuple-element.262), channel_id=1, source_target_pairs={{0,2},{2,0},{1,3},{3,1},{4,6},{6,4},{5,7},{7,5},{8,10},{10,8},{9,1... | collective-permute-start | bytes 786440 | tf_op jit(solution)/shard_map/ppermute | solution.py:288
  62.3 0.1 add_convert_fusion.3
  62.4 3.4 %collective-permute-start.17 = (bf16[128,1024]{1,0:T(8,128)(2,1)S(1)}, bf16[128,1024]{1,0:T(8,128)(2,1)S(1)}, u32[]{:S(2)}, u32[]{:S(2)}) collective-permute-start(bf16[128,1024]{1,0:T(8,128)(2,1)S(1)} %add_convert_fusion.3), channel_id=1, source_target_pairs={{0,4},{4,12},{12,8},{8,0},{1,5},{5,13},{13,9},{9,1},{2,6},{6,14},{... | collective-permute-start | bytes 786440 | tf_op jit(solution)/shard_map/ppermute | solution.py:298
  65.8 1.9 %weight_grads.2 = bf16[4,768,512]{2,1,0:T(8,128)(2,1)S(1)} custom-call(s32[1]{0:T(128)S(6)} %sub.3.side_ref, bf16[4,96,1024]{2,1,0:T(8,128)(2,1)S(1)} %get-tuple-element.249.refs_0_, bf16[4,96,1024]{2,1,0:T(8,128)(2,1)S(1)} %get-tuple-element.250.refs_1_, bf16[4,96,1024]{2,1,0:T(8,128)(2,1)S(1)} %get-tuple-element.251.refs_2_, ...), custom_call_target="tpu_custom_call" | custom-call | flops 1207959552 | bytes 8650752 | tf_op jit(solution)/shard_map/weight_grads/pallas_call | solution.py:244
  67.7 0.0 collective-permute-done.16
  67.7 2.0 %collective-permute-done.17 = bf16[128,1024]{1,0:T(8,128)(2,1)S(1)} collective-permute-done((bf16[128,1024]{1,0:T(8,128)(2,1)S(1)}, bf16[128,1024]{1,0:T(8,128)(2,1)S(1)}, u32[]{:S(2)}, u32[]{:S(2)}) %collective-permute-start.17) | collective-permute-done | bytes 262176 | tf_op jit(solution)/shard_map/ppermute | solution.py:298
  69.7 0.0 collective-permute-start.18
  69.7 0.1 add_convert_fusion.1
  69.8 0.6 collective-permute-start.20
  70.4 0.1 add_convert_fusion.2
  70.5 2.0 %collective-permute-start.19 = (bf16[128,1024]{1,0:T(8,128)(2,1)S(1)}, bf16[128,1024]{1,0:T(8,128)(2,1)S(1)}, u32[]{:S(2)}, u32[]{:S(2)}) collective-permute-start(bf16[128,1024]{1,0:T(8,128)(2,1)S(1)} %add_convert_fusion.2), channel_id=1, source_target_pairs={{0,4},{4,12},{12,8},{8,0},{1,5},{5,13},{13,9},{9,1},{2,6},{6,14},{... | collective-permute-start | bytes 786440 | tf_op jit(solution)/shard_map/ppermute | solution.py:298
  72.5 2.9 %collective-permute-done.18.refs_12_ = bf16[4,768,512]{2,1,0:T(8,128)(2,1)S(1)} collective-permute-done((bf16[4,768,512]{2,1,0:T(8,128)(2,1)S(1)}, bf16[4,768,512]{2,1,0:T(8,128)(2,1)S(1)}, u32[]{:S(2)}, u32[]{:S(2)}) %collective-permute-start.18) | collective-permute-done | bytes 3145760 | tf_op jit(solution)/shard_map/ppermute | solution.py:330
  75.4 2.7 %weight_grads.3 = (bf16[4,512,256]{2,1,0:T(8,128)(2,1)}, bf16[4,512,256]{2,1,0:T(8,128)(2,1)}, bf16[4,256,512]{2,1,0:T(8,128)(2,1)}) custom-call(s32[1]{0:T(128)} %bitcast.1.side_ref, bf16[4,96,1024]{2,1,0:T(8,128)(2,1)S(1)} %get-tuple-element.249.refs_0_, bf16[4,96,1024]{2,1,0:T(8,128)(2,1)S(1)} %get-tuple-element.250.refs_1_, ...), custom_call_target="tpu_custom_call" | custom-call | flops 1207959552 | bytes 8650752 | tf_op jit(solution)/shard_map/weight_grads/pallas_call | solution.py:244
  78.1 0.5 collective-permute-done.20
  78.6 1.3 %collective-permute-done.19 = bf16[128,1024]{1,0:T(8,128)(2,1)S(1)} collective-permute-done((bf16[128,1024]{1,0:T(8,128)(2,1)S(1)}, bf16[128,1024]{1,0:T(8,128)(2,1)S(1)}, u32[]{:S(2)}, u32[]{:S(2)}) %collective-permute-start.19) | collective-permute-done | bytes 262176 | tf_op jit(solution)/shard_map/ppermute | solution.py:298
  79.9 0.9 %add_convert_fusion = bf16[128,1024]{1,0:T(8,128)(2,1)} fusion(bf16[128,1024]{1,0:T(8,128)(2,1)S(1)} %collective-permute-done.19, bf16[128,1024]{1,0:T(8,128)(2,1)S(1)} %collective-permute-done.20, bf16[128,1024]{1,0:T(8,128)(2,1)S(1)} %get-tuple-element.246, bf16[256,1024]{1,0:T(8,128)(2,1)S(1)} %collective-permute-done.15), kind=kLoop, calls=%fused_computation | loop fusion | flops 1048576 | bytes 1310720 | tf_op jit(solution)/shard_map/convert_element_type | solution.py:340
Async XLA Ops:
  0.6 12.4 %collective-permute-start = (bf16[128,1024]{1,0:T(8,128)(2,1)}, bf16[128,1024]{1,0:T(8,128)(2,1)S(1)}, u32[]{:S(2)}, u32[]{:S(2)}) collective-permute-start(bf16[128,1024]{1,0:T(8,128)(2,1)} %tokens), channel_id=1, source_target_pairs={{0,4},{4,12},{12,8},{8,0},{1,5},{5,13},{13,9},{9,1},{2,6},{6,14},{... | collective-permute-start | bytes 786440 | tf_op jit(solution)/shard_map/ppermute | solution.py:309
  3.7 9.3 %collective-permute-start.1 = (bf16[128,1024]{1,0:T(8,128)(2,1)}, bf16[128,1024]{1,0:T(8,128)(2,1)S(1)}, u32[]{:S(2)}, u32[]{:S(2)}) collective-permute-start(bf16[128,1024]{1,0:T(8,128)(2,1)} %tokens), channel_id=1, source_target_pairs={{0,2},{2,0},{1,3},{3,1},{4,6},{6,4},{5,7},{7,5},{8,10},{10,8},{9,1... | collective-permute-start | bytes 786440 | tf_op jit(solution)/shard_map/ppermute | solution.py:281
  7.0 11.4 %collective-permute-start.4 = (bf16[144,1024]{1,0:T(8,128)(2,1)S(1)}, bf16[144,1024]{1,0:T(8,128)(2,1)S(1)}, u32[]{:S(2)}, u32[]{:S(2)}) collective-permute-start(bf16[144,1024]{1,0:T(8,128)(2,1)S(1)} %get-tuple-element.151.refs_2_), channel_id=1, source_target_pairs={{0,4},{4,12},{12,8},{8,0},{1,5},{5,13},{13,9},{9,1},{2,6},{6,14},{... | collective-permute-start | bytes 884744 | tf_op jit(solution)/shard_map/ppermute | solution.py:309
  9.6 9.9 %collective-permute-start.5 = (bf16[144,1024]{1,0:T(8,128)(2,1)S(1)}, bf16[144,1024]{1,0:T(8,128)(2,1)S(1)}, u32[]{:S(2)}, u32[]{:S(2)}) collective-permute-start(bf16[144,1024]{1,0:T(8,128)(2,1)S(1)} %get-tuple-element.151.refs_2_), channel_id=1, source_target_pairs={{0,2},{2,0},{1,3},{3,1},{4,6},{6,4},{5,7},{7,5},{8,10},{10,8},{9,1... | collective-permute-start | bytes 884744 | tf_op jit(solution)/shard_map/ppermute | solution.py:281
  13.1 14.2 %collective-permute-start.2 = (bf16[128,1024]{1,0:T(8,128)(2,1)S(1)}, bf16[128,1024]{1,0:T(8,128)(2,1)S(1)}, u32[]{:S(2)}, u32[]{:S(2)}) collective-permute-start(bf16[128,1024]{1,0:T(8,128)(2,1)S(1)} %collective-permute-done.refs_0_), channel_id=1, source_target_pairs={{0,4},{4,12},{12,8},{8,0},{1,5},{5,13},{13,9},{9,1},{2,6},{6,14},{... | collective-permute-start | bytes 786440 | tf_op jit(solution)/shard_map/ppermute | solution.py:309
  15.7 11.5 %collective-permute-start.3 = (bf16[128,1024]{1,0:T(8,128)(2,1)S(1)}, bf16[128,1024]{1,0:T(8,128)(2,1)S(1)}, u32[]{:S(2)}, u32[]{:S(2)}) collective-permute-start(bf16[128,1024]{1,0:T(8,128)(2,1)S(1)} %collective-permute-done.refs_0_), channel_id=1, source_target_pairs={{0,2},{2,0},{1,3},{3,1},{4,6},{6,4},{5,7},{7,5},{8,10},{10,8},{9,1... | collective-permute-start | bytes 786440 | tf_op jit(solution)/shard_map/ppermute | solution.py:281
  19.6 10.8 %collective-permute-start.8 = (bf16[144,1024]{1,0:T(8,128)(2,1)S(1)}, bf16[144,1024]{1,0:T(8,128)(2,1)S(1)}, u32[]{:S(2)}, u32[]{:S(2)}) collective-permute-start(bf16[144,1024]{1,0:T(8,128)(2,1)S(1)} %collective-permute-done.4.refs_2_), channel_id=1, source_target_pairs={{0,4},{4,12},{12,8},{8,0},{1,5},{5,13},{13,9},{9,1},{2,6},{6,14},{... | collective-permute-start | bytes 884744 | tf_op jit(solution)/shard_map/ppermute | solution.py:309
  22.1 9.9 %collective-permute-start.9 = (bf16[144,1024]{1,0:T(8,128)(2,1)S(1)}, bf16[144,1024]{1,0:T(8,128)(2,1)S(1)}, u32[]{:S(2)}, u32[]{:S(2)}) collective-permute-start(bf16[144,1024]{1,0:T(8,128)(2,1)S(1)} %collective-permute-done.4.refs_2_), channel_id=1, source_target_pairs={{0,2},{2,0},{1,3},{3,1},{4,6},{6,4},{5,7},{7,5},{8,10},{10,8},{9,1... | collective-permute-start | bytes 884744 | tf_op jit(solution)/shard_map/ppermute | solution.py:281
  27.2 11.9 %collective-permute-start.6 = (bf16[128,1024]{1,0:T(8,128)(2,1)S(1)}, bf16[128,1024]{1,0:T(8,128)(2,1)S(1)}, u32[]{:S(2)}, u32[]{:S(2)}) collective-permute-start(bf16[128,1024]{1,0:T(8,128)(2,1)S(1)} %collective-permute-done.2.refs_0_), channel_id=1, source_target_pairs={{0,4},{4,12},{12,8},{8,0},{1,5},{5,13},{13,9},{9,1},{2,6},{6,14},{... | collective-permute-start | bytes 786440 | tf_op jit(solution)/shard_map/ppermute | solution.py:309
  28.2 11.0 %collective-permute-start.7 = (bf16[128,1024]{1,0:T(8,128)(2,1)S(1)}, bf16[128,1024]{1,0:T(8,128)(2,1)S(1)}, u32[]{:S(2)}, u32[]{:S(2)}) collective-permute-start(bf16[128,1024]{1,0:T(8,128)(2,1)S(1)} %collective-permute-done.2.refs_0_), channel_id=1, source_target_pairs={{0,2},{2,0},{1,3},{3,1},{4,6},{6,4},{5,7},{7,5},{8,10},{10,8},{9,1... | collective-permute-start | bytes 786440 | tf_op jit(solution)/shard_map/ppermute | solution.py:281
  32.0 9.4 %collective-permute-start.11 = (bf16[144,1024]{1,0:T(8,128)(2,1)S(1)}, bf16[144,1024]{1,0:T(8,128)(2,1)S(1)}, u32[]{:S(2)}, u32[]{:S(2)}) collective-permute-start(bf16[144,1024]{1,0:T(8,128)(2,1)S(1)} %collective-permute-done.8.refs_2_), channel_id=1, source_target_pairs={{0,4},{4,12},{12,8},{8,0},{1,5},{5,13},{13,9},{9,1},{2,6},{6,14},{... | collective-permute-start | bytes 884744 | tf_op jit(solution)/shard_map/ppermute | solution.py:309
  34.0 9.9 %collective-permute-start.12 = (bf16[144,1024]{1,0:T(8,128)(2,1)S(1)}, bf16[144,1024]{1,0:T(8,128)(2,1)S(1)}, u32[]{:S(2)}, u32[]{:S(2)}) collective-permute-start(bf16[144,1024]{1,0:T(8,128)(2,1)S(1)} %collective-permute-done.8.refs_2_), channel_id=1, source_target_pairs={{0,2},{2,0},{1,3},{3,1},{4,6},{6,4},{5,7},{7,5},{8,10},{10,8},{9,1... | collective-permute-start | bytes 884744 | tf_op jit(solution)/shard_map/ppermute | solution.py:281
  39.2 10.4 %collective-permute-start.10 = (bf16[128,1024]{1,0:T(8,128)(2,1)S(1)}, bf16[128,1024]{1,0:T(8,128)(2,1)S(1)}, u32[]{:S(2)}, u32[]{:S(2)}) collective-permute-start(bf16[128,1024]{1,0:T(8,128)(2,1)S(1)} %collective-permute-done.6.refs_0_), channel_id=1, source_target_pairs={{0,2},{2,0},{1,3},{3,1},{4,6},{6,4},{5,7},{7,5},{8,10},{10,8},{9,1... | collective-permute-start | bytes 786440 | tf_op jit(solution)/shard_map/ppermute | solution.py:281
  44.0 9.9 %collective-permute-start.13 = (bf16[144,1024]{1,0:T(8,128)(2,1)S(1)}, bf16[144,1024]{1,0:T(8,128)(2,1)S(1)}, u32[]{:S(2)}, u32[]{:S(2)}) collective-permute-start(bf16[144,1024]{1,0:T(8,128)(2,1)S(1)} %collective-permute-done.11.refs_2_), channel_id=1, source_target_pairs={{0,2},{2,0},{1,3},{3,1},{4,6},{6,4},{5,7},{7,5},{8,10},{10,8},{9,1... | collective-permute-start | bytes 884744 | tf_op jit(solution)/shard_map/ppermute | solution.py:281
  49.6 11.3 %collective-permute-start.15 = (bf16[256,1024]{1,0:T(8,128)(2,1)S(1)}, bf16[256,1024]{1,0:T(8,128)(2,1)S(1)}, u32[]{:S(2)}, u32[]{:S(2)}) collective-permute-start(bf16[256,1024]{1,0:T(8,128)(2,1)S(1)} %get-tuple-element.212), channel_id=1, source_target_pairs={{0,8},{4,0},{12,4},{8,12},{1,9},{5,1},{13,5},{9,13},{2,10},{6,2},{... | collective-permute-start | bytes 1572872 | tf_op jit(solution)/shard_map/ppermute | solution.py:318
  53.8 6.5 %collective-permute-start.14 = (bf16[128,1024]{1,0:T(8,128)(2,1)S(1)}, bf16[128,1024]{1,0:T(8,128)(2,1)S(1)}, u32[]{:S(2)}, u32[]{:S(2)}) collective-permute-start(bf16[128,1024]{1,0:T(8,128)(2,1)S(1)} %get-tuple-element.230), channel_id=1, source_target_pairs={{0,2},{2,0},{1,3},{3,1},{4,6},{6,4},{5,7},{7,5},{8,10},{10,8},{9,1... | collective-permute-start | bytes 786440 | tf_op jit(solution)/shard_map/ppermute | solution.py:288
  60.8 6.9 %collective-permute-start.16 = (bf16[128,1024]{1,0:T(8,128)(2,1)S(1)}, bf16[128,1024]{1,0:T(8,128)(2,1)S(1)}, u32[]{:S(2)}, u32[]{:S(2)}) collective-permute-start(bf16[128,1024]{1,0:T(8,128)(2,1)S(1)} %get-tuple-element.262), channel_id=1, source_target_pairs={{0,2},{2,0},{1,3},{3,1},{4,6},{6,4},{5,7},{7,5},{8,10},{10,8},{9,1... | collective-permute-start | bytes 786440 | tf_op jit(solution)/shard_map/ppermute | solution.py:288
  62.4 7.3 %collective-permute-start.17 = (bf16[128,1024]{1,0:T(8,128)(2,1)S(1)}, bf16[128,1024]{1,0:T(8,128)(2,1)S(1)}, u32[]{:S(2)}, u32[]{:S(2)}) collective-permute-start(bf16[128,1024]{1,0:T(8,128)(2,1)S(1)} %add_convert_fusion.3), channel_id=1, source_target_pairs={{0,4},{4,12},{12,8},{8,0},{1,5},{5,13},{13,9},{9,1},{2,6},{6,14},{... | collective-permute-start | bytes 786440 | tf_op jit(solution)/shard_map/ppermute | solution.py:298
  69.7 5.7 %collective-permute-start.18 = (bf16[4,768,512]{2,1,0:T(8,128)(2,1)S(1)}, bf16[4,768,512]{2,1,0:T(8,128)(2,1)S(1)}, u32[]{:S(2)}, u32[]{:S(2)}) collective-permute-start(bf16[4,768,512]{2,1,0:T(8,128)(2,1)S(1)} %weight_grads.2), channel_id=1, source_target_pairs={{0,1},{1,0},{2,3},{3,2},{4,5},{5,4},{6,7},{7,6},{8,9},{9,8},{10,11... | collective-permute-start | bytes 9437192 | tf_op jit(solution)/shard_map/ppermute | solution.py:330
  69.8 8.8 %collective-permute-start.20 = (bf16[128,1024]{1,0:T(8,128)(2,1)S(1)}, bf16[128,1024]{1,0:T(8,128)(2,1)S(1)}, u32[]{:S(2)}, u32[]{:S(2)}) collective-permute-start(bf16[128,1024]{1,0:T(8,128)(2,1)S(1)} %add_convert_fusion.1), channel_id=1, source_target_pairs={{0,2},{2,0},{1,3},{3,1},{4,6},{6,4},{5,7},{7,5},{8,10},{10,8},{9,1... | collective-permute-start | bytes 786440 | tf_op jit(solution)/shard_map/ppermute | solution.py:288
  70.5 9.4 %collective-permute-start.19 = (bf16[128,1024]{1,0:T(8,128)(2,1)S(1)}, bf16[128,1024]{1,0:T(8,128)(2,1)S(1)}, u32[]{:S(2)}, u32[]{:S(2)}) collective-permute-start(bf16[128,1024]{1,0:T(8,128)(2,1)S(1)} %add_convert_fusion.2), channel_id=1, source_target_pairs={{0,4},{4,12},{12,8},{8,0},{1,5},{5,13},{13,9},{9,1},{2,6},{6,14},{... | collective-permute-start | bytes 786440 | tf_op jit(solution)/shard_map/ppermute | solution.py:298

commit v12 on v11

--- a/solution.py
+++ b/solution.py
@@ -160,11 +160,11 @@
         start += part.shape[0]
 
 
-def chunk_call(tokens, upstream, first_expert, weights, tok_rows, capacity, rows, top_count, per_group, joined):
+def chunk_call(tokens, upstream, first_expert, weights, tok_rows, capacity, rows, top_count, per_group):
     n_blocks = len(tokens)
     n_tok = n_blocks * tok_rows
     experts, width, ff = weights[0].shape
-    part_shapes = [(n_tok, width)] if joined else [(tok_rows, width), (n_tok - tok_rows, width)]
+    part_shapes = [(tok_rows, width), (n_tok - tok_rows, width)]
     kept_shapes = [(experts, rows, width), (experts, rows, width), (experts, rows, 3 * ff)]
     smem, vmem = (pl.BlockSpec(memory_space=m) for m in (pltpu.SMEM, pltpu.VMEM))
     out_shapes = part_shapes + kept_shapes
@@ -280,8 +280,8 @@
     def spread(column):
         return [column] + [lax.ppermute(column, "ingroup", shift(s)) for s in range(1, n_ingroup)]
 
-    def chunk(blocks, joined=False):
-        return chunk_call(*blocks, first_expert, weights, tok_rows, capacity, rows, top_count, per_group, joined)
+    def chunk(blocks):
+        return chunk_call(*blocks, first_expert, weights, tok_rows, capacity, rows, top_count, per_group)
 
     def across(others):
         return [
@@ -302,37 +302,42 @@
     blocks, chunks, backs, sent = {}, {}, {}, {}
     last = n_group - 1
     for k in range(n_group):
-        pair = [spread(tokens), spread(upstream)]
+        pair = [spread(tokens), spread(upstream) if k < last else [upstream]]
+        if k == last:
+            pair[1] += [lax.ppermute(block, "group", along(1)) for block in blocks[k - 1][1][1:]]
         if k == 0:
             pair[0][0] = first_tokens
         if k < last:
             tokens, upstream = (lax.ppermute(v, "group", along(1)) for v in (tokens, upstream))
         if k > 0:
-            chunks[k - 1] = chunk(blocks[k - 1], k - 1 == 1)
+            chunks[k - 1] = chunk(blocks[k - 1])
         tokens, pair[0], chunks, weights = tie(tokens, pair[0], chunks, weights)
         upstream, pair[1] = tie(upstream, pair[1])
         blocks[k] = pair
 
     for k in range(2, last - 1):
         sent[k] = homeward(group_sum(chunks[k][0], across(chunks[k][1])), k)
-    near = lax.ppermute(chunks[1][0], "group", along(-1))
-    blocks[last], chunks = tie(blocks[last], chunks)
     backs[last - 1] = across(chunks[last - 1][1])
+    near_other, blocks[last] = tie(chunks[1][1], blocks[last])
+    near_other = homeward(near_other, 1)
     chunks[last] = chunk(blocks[last])
-    chunks, backs, near = tie(chunks, backs, near)
+    chunks, backs = tie(chunks, backs)
 
     backs[last] = across(chunks[last][1])
     carried = homeward(group_sum(chunks[last - 1][0], backs[last - 1]), last)
+    sent[1] = homeward(chunks[1][0], 1)
     kept = [[chunks[k][i] for k in range(n_group)] for i in (-3, -2, -1)]
     to_send = weight_call(other_half, *kept)
-    to_send, backs[last], carried = tie(to_send, backs[last], carried)
+    other = (wide(chunks[0][1]) + wide(near_other)).astype(jnp.bfloat16)
+    to_send, backs[last], carried, other = tie(to_send, backs[last], carried, other)
 
     got = lax.ppermute(to_send, "dp", [(0, 1), (1, 0)])
     sent[last] = homeward(group_sum(chunks[last][0], [*backs[last], carried]), last)
-    backs[0] = across((wide(chunks[0][1]) + wide(near[tok_rows:])).astype(jnp.bfloat16))
+    backs[0] = across(other)
+    got, sent[1] = tie(got, sent[1])
     grads = weight_call(half, *kept, got)
     grads, sent, backs[0] = tie(grads, sent, backs[0])
-    total = wide(chunks[0][0]) + wide(near[:tok_rows])
+    total = wide(chunks[0][0])
     for back in backs[0]:
         total = total + wide(back)
     for back in sent.values():

time: 81 us -> 88.5 us (1.093)
  waiting for transfers between devices: 20.7 us -> 33 us
  starting transfers between devices: 34.2 us -> 29.4 us
    ppermute x2 -> x4, waiting for transfers between devices: 3.36 us -> 15.3 us  [homeward(): return lax.ppermute(group_part, 'group', along(-k))]
    ppermute x6, starting transfers between devices: 13.8 us -> 9.92 us  [per_device(): lax.ppermute(v, 'group', along(1))]
    ppermute x8 -> x7, waiting for transfers between devices: 8.15 us -> 11 us  [spread(): lax.ppermute(column, 'ingroup', shift(s))]
    ppermute x1, waiting for transfers between devices: 2.86 us -> 0.01 us  [per_device(): got = lax.ppermute(to_send, 'dp', [(0, 1), (1, 0)])]
    ppermute x3, waiting for transfers between devices: 1.84 us -> 0.01 us  [across(): lax.ppermute(others[(s - 1) * tok_rows:s * tok_rows], 'ingroup', shift(-s))]
    ppermute x1, waiting for transfers between devices: 0.49 us -> 2.24 us  [per_device(): lax.ppermute(block, 'group', along(1))]
    ppermute x1, starting transfers between devices: 1.84 us -> 0.88 us  [per_device(): lax.ppermute(block, 'group', along(1))]
    ppermute x2 -> x4, starting transfers between devices: 5.41 us -> 5.7 us  [homeward(): return lax.ppermute(group_part, 'group', along(-k))]
  transfers between devices with their start and end apart: 21 -> 22, of which waited for: 14 -> 10; matrix products, arithmetic and copies ran while one was open for 0% -> 0% of each run, Pallas kernels for 30% -> 25%
where the time goes in v12:
time: 88.5 us; the launch traced here: 88.3 us
  waiting for transfers between devices  33 us (37%)
  starting transfers between devices  29.4 us (33%)
  Pallas kernels  23.9 us (27%)
  other arithmetic  1.13 us (1%)
    ppermute x4, waiting for transfers between devices, homeward(): return lax.ppermute(group_part, 'group', along(-k))  15.3 us
    pallas_call x4, Pallas kernels, chunk_call(): pl.pallas_call(functools.partial(chunk_kernel, n_blocks, tok_rows, capaci...  14.7 us
    ppermute x7, waiting for transfers between devices, spread(): lax.ppermute(column, 'ingroup', shift(s))  11 us
    ppermute x6, starting transfers between devices, per_device(): lax.ppermute(v, 'group', along(1))  9.92 us
    ppermute x7, starting transfers between devices, spread(): lax.ppermute(column, 'ingroup', shift(s))  9.77 us
    ppermute x4, starting transfers between devices, homeward(): return lax.ppermute(group_part, 'group', along(-k))  5.7 us
    pallas_call x2, Pallas kernels, weight_call(): pl.pallas_call(functools.partial(kernel, n), in_specs=[smem] + [vmem] * l...  4.57 us
    ppermute x6, waiting for transfers between devices, per_device(): lax.ppermute(v, 'group', along(1))  4.48 us
  transfers between devices with their start and end apart: 22, of which 10 were waited for; matrix products, arithmetic and copies ran while one was open for 0% of the time, Pallas kernels for 25%

profile of v12, /device:TPU:0, one launch (start us, length us, event | category | flops | bytes accessed | tf_op | source)
XLA Modules:
  0.0 88.3 jit_solution(14220817786426258258)
XLA Ops:
  0.6 1.8 %pack.1 = (bf16[128,1024]{1,0:T(8,128)(2,1)S(1)}, bf16[144,1024]{1,0:T(8,128)(2,1)S(1)}) custom-call(bf16[128,1024]{1,0:T(8,128)(2,1)} %tokens, bf16[128,1024]{1,0:T(8,128)(2,1)} %upstream.1, s32[8,128]{1,0:T(8,128)} %bitcast.5, s32[8,128]{1,0:T(8,128)} %bitcast.6, s32[8,128]{1,0:T(8,128)} %bitcast.7), custom_call_target="tpu_custom_call" | custom-call | tf_op jit(solution)/shard_map/pack/pallas_call | solution.py:58
  2.4 3.0 %collective-permute-start.5 = (bf16[144,1024]{1,0:T(8,128)(2,1)S(1)}, bf16[144,1024]{1,0:T(8,128)(2,1)S(1)}, u32[]{:S(2)}, u32[]{:S(2)}) collective-permute-start(bf16[144,1024]{1,0:T(8,128)(2,1)S(1)} %get-tuple-element.146.refs_2_), channel_id=1, source_target_pairs={{0,2},{2,0},{1,3},{3,1},{4,6},{6,4},{5,7},{7,5},{8,10},{10,8},{9,1... | collective-permute-start | bytes 884744 | tf_op jit(solution)/shard_map/ppermute | solution.py:281
  5.4 1.6 %collective-permute-start.4 = (bf16[144,1024]{1,0:T(8,128)(2,1)S(1)}, bf16[144,1024]{1,0:T(8,128)(2,1)S(1)}, u32[]{:S(2)}, u32[]{:S(2)}) collective-permute-start(bf16[144,1024]{1,0:T(8,128)(2,1)S(1)} %get-tuple-element.146.refs_2_), channel_id=1, source_target_pairs={{0,4},{4,12},{12,8},{8,0},{1,5},{5,13},{13,9},{9,1},{2,6},{6,14},{... | collective-permute-start | bytes 884744 | tf_op jit(solution)/shard_map/ppermute | solution.py:311
  7.0 0.5 collective-permute-start.1
  7.5 2.6 %collective-permute-start = (bf16[128,1024]{1,0:T(8,128)(2,1)}, bf16[128,1024]{1,0:T(8,128)(2,1)S(1)}, u32[]{:S(2)}, u32[]{:S(2)}) collective-permute-start(bf16[128,1024]{1,0:T(8,128)(2,1)} %tokens), channel_id=1, source_target_pairs={{0,4},{4,12},{12,8},{8,0},{1,5},{5,13},{13,9},{9,1},{2,6},{6,14},{... | collective-permute-start | bytes 786440 | tf_op jit(solution)/shard_map/ppermute | solution.py:311
  10.1 2.9 %load.1 = (bf16[4,1024,256]{2,1,0:T(8,128)(2,1)S(1)}, bf16[4,1024,256]{2,1,0:T(8,128)(2,1)S(1)}, bf16[4,256,1024]{2,1,0:T(8,128)(2,1)S(1)}) custom-call(bf16[4,1024,256]{2,1,0:T(8,128)(2,1)} %refs_0_.1, bf16[4,1024,256]{2,1,0:T(8,128)(2,1)} %refs_1_.1, bf16[4,256,1024]{2,1,0:T(8,128)(2,1)} %refs_2_.1), custom_call_target="tpu_custom_call" | custom-call | tf_op jit(solution)/shard_map/load/pallas_call | solution.py:98
  13.0 5.0 %collective-permute-done.1.refs_1_ = bf16[128,1024]{1,0:T(8,128)(2,1)S(1)} collective-permute-done((bf16[128,1024]{1,0:T(8,128)(2,1)}, bf16[128,1024]{1,0:T(8,128)(2,1)S(1)}, u32[]{:S(2)}, u32[]{:S(2)}) %collective-permute-start.1) | collective-permute-done | bytes 262176 | tf_op jit(solution)/shard_map/ppermute | solution.py:281
  18.0 2.4 %collective-permute-done.refs_0_ = bf16[128,1024]{1,0:T(8,128)(2,1)S(1)} collective-permute-done((bf16[128,1024]{1,0:T(8,128)(2,1)}, bf16[128,1024]{1,0:T(8,128)(2,1)S(1)}, u32[]{:S(2)}, u32[]{:S(2)}) %collective-permute-start) | collective-permute-done | bytes 262176 | tf_op jit(solution)/shard_map/ppermute | solution.py:311
  20.4 0.5 collective-permute-start.3
  20.9 0.9 %collective-permute-start.2 = (bf16[128,1024]{1,0:T(8,128)(2,1)S(1)}, bf16[128,1024]{1,0:T(8,128)(2,1)S(1)}, u32[]{:S(2)}, u32[]{:S(2)}) collective-permute-start(bf16[128,1024]{1,0:T(8,128)(2,1)S(1)} %collective-permute-done.refs_0_), channel_id=1, source_target_pairs={{0,4},{4,12},{12,8},{8,0},{1,5},{5,13},{13,9},{9,1},{2,6},{6,14},{... | collective-permute-start | bytes 786440 | tf_op jit(solution)/shard_map/ppermute | solution.py:311
  21.8 0.0 collective-permute-done.5.refs_3_
  21.8 0.0 collective-permute-done.4.refs_2_
  21.8 1.5 %collective-permute-start.9 = (bf16[144,1024]{1,0:T(8,128)(2,1)S(1)}, bf16[144,1024]{1,0:T(8,128)(2,1)S(1)}, u32[]{:S(2)}, u32[]{:S(2)}) collective-permute-start(bf16[144,1024]{1,0:T(8,128)(2,1)S(1)} %collective-permute-done.4.refs_2_), channel_id=1, source_target_pairs={{0,2},{2,0},{1,3},{3,1},{4,6},{6,4},{5,7},{7,5},{8,10},{10,8},{9,1... | collective-permute-start | bytes 884744 | tf_op jit(solution)/shard_map/ppermute | solution.py:281
  23.3 3.3 %collective-permute-start.8 = (bf16[144,1024]{1,0:T(8,128)(2,1)S(1)}, bf16[144,1024]{1,0:T(8,128)(2,1)S(1)}, u32[]{:S(2)}, u32[]{:S(2)}) collective-permute-start(bf16[144,1024]{1,0:T(8,128)(2,1)S(1)} %collective-permute-done.4.refs_2_), channel_id=1, source_target_pairs={{0,4},{4,12},{12,8},{8,0},{1,5},{5,13},{13,9},{9,1},{2,6},{6,14},{... | collective-permute-start | bytes 884744 | tf_op jit(solution)/shard_map/ppermute | solution.py:311
  26.6 3.7 %chunk.4 = (bf16[128,1024]{1,0:T(8,128)(2,1)S(1)}, bf16[128,1024]{1,0:T(8,128)(2,1)S(1)}, bf16[4,96,1024]{2,1,0:T(8,128)(2,1)S(1)}, bf16[4,96,1024]{2,1,0:T(8,128)(2,1)S(1)}, bf16[4,96,768]{2,1,0:T(8,128)(2,1)S(1)}) custom-call(s32[1]{0:T(128)} %bitcast.first_ref, bf16[128,1024]{1,0:T(8,128)(2,1)S(1)} %get-tuple-element.143.refs_0_, ...), custom_call_target="tpu_custom_call" | custom-call | flops 1610612736 | bytes 8388608 | tf_op jit(solution)/shard_map/chunk/pallas_call | solution.py:171
  30.3 0.0 collective-permute-done.3.refs_1_
  30.3 0.7 collective-permute-done.2.refs_0_
  31.0 1.5 %collective-permute-start.7 = (bf16[128,1024]{1,0:T(8,128)(2,1)S(1)}, bf16[128,1024]{1,0:T(8,128)(2,1)S(1)}, u32[]{:S(2)}, u32[]{:S(2)}) collective-permute-start(bf16[128,1024]{1,0:T(8,128)(2,1)S(1)} %collective-permute-done.2.refs_0_), channel_id=1, source_target_pairs={{0,2},{2,0},{1,3},{3,1},{4,6},{6,4},{5,7},{7,5},{8,10},{10,8},{9,1... | collective-permute-start | bytes 786440 | tf_op jit(solution)/shard_map/ppermute | solution.py:281
  32.6 0.8 collective-permute-start.6
  33.4 2.6 %collective-permute-done.9.refs_3_ = bf16[144,1024]{1,0:T(8,128)(2,1)S(1)} collective-permute-done((bf16[144,1024]{1,0:T(8,128)(2,1)S(1)}, bf16[144,1024]{1,0:T(8,128)(2,1)S(1)}, u32[]{:S(2)}, u32[]{:S(2)}) %collective-permute-start.9) | collective-permute-done | bytes 294944 | tf_op jit(solution)/shard_map/ppermute | solution.py:281
  36.0 1.4 %collective-permute-done.8.refs_2_ = bf16[144,1024]{1,0:T(8,128)(2,1)S(1)} collective-permute-done((bf16[144,1024]{1,0:T(8,128)(2,1)S(1)}, bf16[144,1024]{1,0:T(8,128)(2,1)S(1)}, u32[]{:S(2)}, u32[]{:S(2)}) %collective-permute-start.8) | collective-permute-done | bytes 294944 | tf_op jit(solution)/shard_map/ppermute | solution.py:311
  37.3 1.6 %collective-permute-start.12 = (bf16[144,1024]{1,0:T(8,128)(2,1)S(1)}, bf16[144,1024]{1,0:T(8,128)(2,1)S(1)}, u32[]{:S(2)}, u32[]{:S(2)}) collective-permute-start(bf16[144,1024]{1,0:T(8,128)(2,1)S(1)} %collective-permute-done.8.refs_2_), channel_id=1, source_target_pairs={{0,2},{2,0},{1,3},{3,1},{4,6},{6,4},{5,7},{7,5},{8,10},{10,8},{9,1... | collective-permute-start | bytes 884744 | tf_op jit(solution)/shard_map/ppermute | solution.py:281
  38.9 0.8 collective-permute-start.11
  39.7 3.7 %chunk.5 = (bf16[128,1024]{1,0:T(8,128)(2,1)S(1)}, bf16[128,1024]{1,0:T(8,128)(2,1)S(1)}, bf16[4,96,1024]{2,1,0:T(8,128)(2,1)S(1)}, bf16[4,96,1024]{2,1,0:T(8,128)(2,1)S(1)}, bf16[4,96,768]{2,1,0:T(8,128)(2,1)S(1)}) custom-call(s32[1]{0:T(128)} %bitcast.first_ref, bf16[128,1024]{1,0:T(8,128)(2,1)S(1)} %collective-permute-done.refs_0_, ...), custom_call_target="tpu_custom_call" | custom-call | flops 1610612736 | bytes 8388608 | tf_op jit(solution)/shard_map/chunk/pallas_call | solution.py:171
  43.3 0.0 collective-permute-done.7.refs_1_
  43.4 0.0 collective-permute-done.6.refs_0_
  43.4 1.1 %collective-permute-start.10 = (bf16[128,1024]{1,0:T(8,128)(2,1)S(1)}, bf16[128,1024]{1,0:T(8,128)(2,1)S(1)}, u32[]{:S(2)}, u32[]{:S(2)}) collective-permute-start(bf16[128,1024]{1,0:T(8,128)(2,1)S(1)} %collective-permute-done.6.refs_0_), channel_id=1, source_target_pairs={{0,2},{2,0},{1,3},{3,1},{4,6},{6,4},{5,7},{7,5},{8,10},{10,8},{9,1... | collective-permute-start | bytes 786440 | tf_op jit(solution)/shard_map/ppermute | solution.py:281
  44.5 3.4 %collective-permute-done.12.refs_3_ = bf16[144,1024]{1,0:T(8,128)(2,1)S(1)} collective-permute-done((bf16[144,1024]{1,0:T(8,128)(2,1)S(1)}, bf16[144,1024]{1,0:T(8,128)(2,1)S(1)}, u32[]{:S(2)}, u32[]{:S(2)}) %collective-permute-start.12) | collective-permute-done | bytes 294944 | tf_op jit(solution)/shard_map/ppermute | solution.py:281
  47.9 0.0 collective-permute-done.11.refs_2_
  47.9 0.9 collective-permute-start.13
  48.8 3.7 %chunk.6 = (bf16[128,1024]{1,0:T(8,128)(2,1)S(1)}, bf16[128,1024]{1,0:T(8,128)(2,1)S(1)}, bf16[4,96,1024]{2,1,0:T(8,128)(2,1)S(1)}, bf16[4,96,1024]{2,1,0:T(8,128)(2,1)S(1)}, bf16[4,96,768]{2,1,0:T(8,128)(2,1)S(1)}) custom-call(s32[1]{0:T(128)} %bitcast.first_ref, bf16[128,1024]{1,0:T(8,128)(2,1)S(1)} %collective-permute-done.2.refs_0_, ...), custom_call_target="tpu_custom_call" | custom-call | flops 1610612736 | bytes 8388608 | tf_op jit(solution)/shard_map/chunk/pallas_call | solution.py:171
  52.5 0.0 collective-permute-done.10.refs_1_
  52.5 0.9 %collective-permute-start.14 = (bf16[128,1024]{1,0:T(8,128)(2,1)S(1)}, bf16[128,1024]{1,0:T(8,128)(2,1)S(1)}, u32[]{:S(2)}, u32[]{:S(2)}) collective-permute-start(bf16[128,1024]{1,0:T(8,128)(2,1)S(1)} %get-tuple-element.210), channel_id=1, source_target_pairs={{0,2},{2,0},{1,3},{3,1},{4,6},{6,4},{5,7},{7,5},{8,10},{10,8},{9,1... | collective-permute-start | bytes 786440 | tf_op jit(solution)/shard_map/ppermute | solution.py:288
  53.4 2.2 %collective-permute-done.13.refs_3_ = bf16[144,1024]{1,0:T(8,128)(2,1)S(1)} collective-permute-done((bf16[144,1024]{1,0:T(8,128)(2,1)S(1)}, bf16[144,1024]{1,0:T(8,128)(2,1)S(1)}, u32[]{:S(2)}, u32[]{:S(2)}) %collective-permute-start.13) | collective-permute-done | bytes 294944 | tf_op jit(solution)/shard_map/ppermute | solution.py:307
  55.6 1.4 %collective-permute-start.17 = (bf16[128,1024]{1,0:T(8,128)(2,1)S(1)}, bf16[128,1024]{1,0:T(8,128)(2,1)S(1)}, u32[]{:S(2)}, u32[]{:S(2)}) collective-permute-start(bf16[128,1024]{1,0:T(8,128)(2,1)S(1)} %get-tuple-element.250), channel_id=1, source_target_pairs={{0,8},{4,0},{12,4},{8,12},{1,9},{5,1},{13,5},{9,13},{2,10},{6,2},{... | collective-permute-start | bytes 786440 | tf_op jit(solution)/shard_map/ppermute | solution.py:298
  57.0 3.7 %chunk.7 = (bf16[128,1024]{1,0:T(8,128)(2,1)S(1)}, bf16[128,1024]{1,0:T(8,128)(2,1)S(1)}, bf16[4,96,1024]{2,1,0:T(8,128)(2,1)S(1)}, bf16[4,96,1024]{2,1,0:T(8,128)(2,1)S(1)}, bf16[4,96,768]{2,1,0:T(8,128)(2,1)S(1)}) custom-call(s32[1]{0:T(128)} %bitcast.first_ref, bf16[128,1024]{1,0:T(8,128)(2,1)S(1)} %collective-permute-done.6.refs_0_, ...), custom_call_target="tpu_custom_call" | custom-call | flops 1610612736 | bytes 8388608 | tf_op jit(solution)/shard_map/chunk/pallas_call | solution.py:171
  60.7 0.0 collective-permute-done.14
  60.7 0.1 add_convert_fusion.3
  60.8 2.2 %collective-permute-start.16 = (bf16[128,1024]{1,0:T(8,128)(2,1)S(1)}, bf16[128,1024]{1,0:T(8,128)(2,1)S(1)}, u32[]{:S(2)}, u32[]{:S(2)}) collective-permute-start(bf16[128,1024]{1,0:T(8,128)(2,1)S(1)} %add_convert_fusion.3), channel_id=1, source_target_pairs={{0,4},{4,12},{12,8},{8,0},{1,5},{5,13},{13,9},{9,1},{2,6},{6,14},{... | collective-permute-start | bytes 786440 | tf_op jit(solution)/shard_map/ppermute | solution.py:298
  62.9 1.1 %collective-permute-start.15 = (bf16[128,1024]{1,0:T(8,128)(2,1)S(1)}, bf16[128,1024]{1,0:T(8,128)(2,1)S(1)}, u32[]{:S(2)}, u32[]{:S(2)}) collective-permute-start(bf16[128,1024]{1,0:T(8,128)(2,1)S(1)} %get-tuple-element.246), channel_id=1, source_target_pairs={{0,2},{2,0},{1,3},{3,1},{4,6},{6,4},{5,7},{7,5},{8,10},{10,8},{9,1... | collective-permute-start | bytes 786440 | tf_op jit(solution)/shard_map/ppermute | solution.py:288
  64.0 1.9 %weight_grads.2 = bf16[4,768,512]{2,1,0:T(8,128)(2,1)S(1)} custom-call(s32[1]{0:T(128)S(6)} %sub.3.side_ref, bf16[4,96,1024]{2,1,0:T(8,128)(2,1)S(1)} %get-tuple-element.233.refs_0_, bf16[4,96,1024]{2,1,0:T(8,128)(2,1)S(1)} %get-tuple-element.234.refs_1_, bf16[4,96,1024]{2,1,0:T(8,128)(2,1)S(1)} %get-tuple-element.235.refs_2_, ...), custom_call_target="tpu_custom_call" | custom-call | flops 1207959552 | bytes 8650752 | tf_op jit(solution)/shard_map/weight_grads/pallas_call | solution.py:244
  65.9 0.0 collective-permute-done.17
  65.9 0.1 add_convert_fusion.2
  66.0 4.7 %collective-permute-done.16 = bf16[128,1024]{1,0:T(8,128)(2,1)S(1)} collective-permute-done((bf16[128,1024]{1,0:T(8,128)(2,1)S(1)}, bf16[128,1024]{1,0:T(8,128)(2,1)S(1)}, u32[]{:S(2)}, u32[]{:S(2)}) %collective-permute-start.16) | collective-permute-done | bytes 262176 | tf_op jit(solution)/shard_map/ppermute | solution.py:298
  70.7 0.0 collective-permute-done.15
  70.7 0.0 collective-permute-start.18
  70.7 2.1 %collective-permute-start.19 = (bf16[128,1024]{1,0:T(8,128)(2,1)S(1)}, bf16[128,1024]{1,0:T(8,128)(2,1)S(1)}, u32[]{:S(2)}, u32[]{:S(2)}) collective-permute-start(bf16[128,1024]{1,0:T(8,128)(2,1)S(1)} %get-tuple-element.252), channel_id=1, source_target_pairs={{0,8},{4,0},{12,4},{8,12},{1,9},{5,1},{13,5},{9,13},{2,10},{6,2},{... | collective-permute-start | bytes 786440 | tf_op jit(solution)/shard_map/ppermute | solution.py:298
  72.8 0.1 add_convert_fusion.1
  72.9 0.1 collective-permute-start.20
  73.0 1.1 %collective-permute-start.21 = (bf16[128,1024]{1,0:T(8,128)(2,1)S(1)}, bf16[128,1024]{1,0:T(8,128)(2,1)S(1)}, u32[]{:S(2)}, u32[]{:S(2)}) collective-permute-start(bf16[128,1024]{1,0:T(8,128)(2,1)S(1)} %add_convert_fusion.2), channel_id=1, source_target_pairs={{0,2},{2,0},{1,3},{3,1},{4,6},{6,4},{5,7},{7,5},{8,10},{10,8},{9,1... | collective-permute-start | bytes 786440 | tf_op jit(solution)/shard_map/ppermute | solution.py:288
  74.1 5.7 %collective-permute-done.19 = bf16[128,1024]{1,0:T(8,128)(2,1)S(1)} collective-permute-done((bf16[128,1024]{1,0:T(8,128)(2,1)S(1)}, bf16[128,1024]{1,0:T(8,128)(2,1)S(1)}, u32[]{:S(2)}, u32[]{:S(2)}) %collective-permute-start.19) | collective-permute-done | bytes 262176 | tf_op jit(solution)/shard_map/ppermute | solution.py:298
  79.8 0.0 collective-permute-done.18.refs_12_
  79.8 2.7 %weight_grads.3 = (bf16[4,512,256]{2,1,0:T(8,128)(2,1)}, bf16[4,512,256]{2,1,0:T(8,128)(2,1)}, bf16[4,256,512]{2,1,0:T(8,128)(2,1)}) custom-call(s32[1]{0:T(128)} %bitcast.1.side_ref, bf16[4,96,1024]{2,1,0:T(8,128)(2,1)S(1)} %get-tuple-element.233.refs_0_, bf16[4,96,1024]{2,1,0:T(8,128)(2,1)S(1)} %get-tuple-element.234.refs_1_, ...), custom_call_target="tpu_custom_call" | custom-call | flops 1207959552 | bytes 8650752 | tf_op jit(solution)/shard_map/weight_grads/pallas_call | solution.py:244
  82.5 4.9 %collective-permute-done.20 = bf16[128,1024]{1,0:T(8,128)(2,1)S(1)} collective-permute-done((bf16[128,1024]{1,0:T(8,128)(2,1)S(1)}, bf16[128,1024]{1,0:T(8,128)(2,1)S(1)}, u32[]{:S(2)}, u32[]{:S(2)}) %collective-permute-start.20) | collective-permute-done | bytes 262176 | tf_op jit(solution)/shard_map/ppermute | solution.py:298
  87.4 0.0 collective-permute-done.21
  87.4 0.9 add_convert_fusion
Async XLA Ops:
  2.4 19.4 %collective-permute-start.5 = (bf16[144,1024]{1,0:T(8,128)(2,1)S(1)}, bf16[144,1024]{1,0:T(8,128)(2,1)S(1)}, u32[]{:S(2)}, u32[]{:S(2)}) collective-permute-start(bf16[144,1024]{1,0:T(8,128)(2,1)S(1)} %get-tuple-element.146.refs_2_), channel_id=1, source_target_pairs={{0,2},{2,0},{1,3},{3,1},{4,6},{6,4},{5,7},{7,5},{8,10},{10,8},{9,1... | collective-permute-start | bytes 884744 | tf_op jit(solution)/shard_map/ppermute | solution.py:281
  5.4 16.4 %collective-permute-start.4 = (bf16[144,1024]{1,0:T(8,128)(2,1)S(1)}, bf16[144,1024]{1,0:T(8,128)(2,1)S(1)}, u32[]{:S(2)}, u32[]{:S(2)}) collective-permute-start(bf16[144,1024]{1,0:T(8,128)(2,1)S(1)} %get-tuple-element.146.refs_2_), channel_id=1, source_target_pairs={{0,4},{4,12},{12,8},{8,0},{1,5},{5,13},{13,9},{9,1},{2,6},{6,14},{... | collective-permute-start | bytes 884744 | tf_op jit(solution)/shard_map/ppermute | solution.py:311
  7.0 11.0 %collective-permute-start.1 = (bf16[128,1024]{1,0:T(8,128)(2,1)}, bf16[128,1024]{1,0:T(8,128)(2,1)S(1)}, u32[]{:S(2)}, u32[]{:S(2)}) collective-permute-start(bf16[128,1024]{1,0:T(8,128)(2,1)} %tokens), channel_id=1, source_target_pairs={{0,2},{2,0},{1,3},{3,1},{4,6},{6,4},{5,7},{7,5},{8,10},{10,8},{9,1... | collective-permute-start | bytes 786440 | tf_op jit(solution)/shard_map/ppermute | solution.py:281
  7.5 12.9 %collective-permute-start = (bf16[128,1024]{1,0:T(8,128)(2,1)}, bf16[128,1024]{1,0:T(8,128)(2,1)S(1)}, u32[]{:S(2)}, u32[]{:S(2)}) collective-permute-start(bf16[128,1024]{1,0:T(8,128)(2,1)} %tokens), channel_id=1, source_target_pairs={{0,4},{4,12},{12,8},{8,0},{1,5},{5,13},{13,9},{9,1},{2,6},{6,14},{... | collective-permute-start | bytes 786440 | tf_op jit(solution)/shard_map/ppermute | solution.py:311
  20.4 9.9 %collective-permute-start.3 = (bf16[128,1024]{1,0:T(8,128)(2,1)S(1)}, bf16[128,1024]{1,0:T(8,128)(2,1)S(1)}, u32[]{:S(2)}, u32[]{:S(2)}) collective-permute-start(bf16[128,1024]{1,0:T(8,128)(2,1)S(1)} %collective-permute-done.refs_0_), channel_id=1, source_target_pairs={{0,2},{2,0},{1,3},{3,1},{4,6},{6,4},{5,7},{7,5},{8,10},{10,8},{9,1... | collective-permute-start | bytes 786440 | tf_op jit(solution)/shard_map/ppermute | solution.py:281
  20.9 10.1 %collective-permute-start.2 = (bf16[128,1024]{1,0:T(8,128)(2,1)S(1)}, bf16[128,1024]{1,0:T(8,128)(2,1)S(1)}, u32[]{:S(2)}, u32[]{:S(2)}) collective-permute-start(bf16[128,1024]{1,0:T(8,128)(2,1)S(1)} %collective-permute-done.refs_0_), channel_id=1, source_target_pairs={{0,4},{4,12},{12,8},{8,0},{1,5},{5,13},{13,9},{9,1},{2,6},{6,14},{... | collective-permute-start | bytes 786440 | tf_op jit(solution)/shard_map/ppermute | solution.py:311
  21.8 14.1 %collective-permute-start.9 = (bf16[144,1024]{1,0:T(8,128)(2,1)S(1)}, bf16[144,1024]{1,0:T(8,128)(2,1)S(1)}, u32[]{:S(2)}, u32[]{:S(2)}) collective-permute-start(bf16[144,1024]{1,0:T(8,128)(2,1)S(1)} %collective-permute-done.4.refs_2_), channel_id=1, source_target_pairs={{0,2},{2,0},{1,3},{3,1},{4,6},{6,4},{5,7},{7,5},{8,10},{10,8},{9,1... | collective-permute-start | bytes 884744 | tf_op jit(solution)/shard_map/ppermute | solution.py:281
  23.3 14.0 %collective-permute-start.8 = (bf16[144,1024]{1,0:T(8,128)(2,1)S(1)}, bf16[144,1024]{1,0:T(8,128)(2,1)S(1)}, u32[]{:S(2)}, u32[]{:S(2)}) collective-permute-start(bf16[144,1024]{1,0:T(8,128)(2,1)S(1)} %collective-permute-done.4.refs_2_), channel_id=1, source_target_pairs={{0,4},{4,12},{12,8},{8,0},{1,5},{5,13},{13,9},{9,1},{2,6},{6,14},{... | collective-permute-start | bytes 884744 | tf_op jit(solution)/shard_map/ppermute | solution.py:311
  31.0 12.3 %collective-permute-start.7 = (bf16[128,1024]{1,0:T(8,128)(2,1)S(1)}, bf16[128,1024]{1,0:T(8,128)(2,1)S(1)}, u32[]{:S(2)}, u32[]{:S(2)}) collective-permute-start(bf16[128,1024]{1,0:T(8,128)(2,1)S(1)} %collective-permute-done.2.refs_0_), channel_id=1, source_target_pairs={{0,2},{2,0},{1,3},{3,1},{4,6},{6,4},{5,7},{7,5},{8,10},{10,8},{9,1... | collective-permute-start | bytes 786440 | tf_op jit(solution)/shard_map/ppermute | solution.py:281
  32.6 10.8 %collective-permute-start.6 = (bf16[128,1024]{1,0:T(8,128)(2,1)S(1)}, bf16[128,1024]{1,0:T(8,128)(2,1)S(1)}, u32[]{:S(2)}, u32[]{:S(2)}) collective-permute-start(bf16[128,1024]{1,0:T(8,128)(2,1)S(1)} %collective-permute-done.2.refs_0_), channel_id=1, source_target_pairs={{0,4},{4,12},{12,8},{8,0},{1,5},{5,13},{13,9},{9,1},{2,6},{6,14},{... | collective-permute-start | bytes 786440 | tf_op jit(solution)/shard_map/ppermute | solution.py:311
  37.3 10.6 %collective-permute-start.12 = (bf16[144,1024]{1,0:T(8,128)(2,1)S(1)}, bf16[144,1024]{1,0:T(8,128)(2,1)S(1)}, u32[]{:S(2)}, u32[]{:S(2)}) collective-permute-start(bf16[144,1024]{1,0:T(8,128)(2,1)S(1)} %collective-permute-done.8.refs_2_), channel_id=1, source_target_pairs={{0,2},{2,0},{1,3},{3,1},{4,6},{6,4},{5,7},{7,5},{8,10},{10,8},{9,1... | collective-permute-start | bytes 884744 | tf_op jit(solution)/shard_map/ppermute | solution.py:281
  38.9 9.0 %collective-permute-start.11 = (bf16[144,1024]{1,0:T(8,128)(2,1)S(1)}, bf16[144,1024]{1,0:T(8,128)(2,1)S(1)}, u32[]{:S(2)}, u32[]{:S(2)}) collective-permute-start(bf16[144,1024]{1,0:T(8,128)(2,1)S(1)} %collective-permute-done.8.refs_2_), channel_id=1, source_target_pairs={{0,4},{4,12},{12,8},{8,0},{1,5},{5,13},{13,9},{9,1},{2,6},{6,14},{... | collective-permute-start | bytes 884744 | tf_op jit(solution)/shard_map/ppermute | solution.py:311
  43.4 9.1 %collective-permute-start.10 = (bf16[128,1024]{1,0:T(8,128)(2,1)S(1)}, bf16[128,1024]{1,0:T(8,128)(2,1)S(1)}, u32[]{:S(2)}, u32[]{:S(2)}) collective-permute-start(bf16[128,1024]{1,0:T(8,128)(2,1)S(1)} %collective-permute-done.6.refs_0_), channel_id=1, source_target_pairs={{0,2},{2,0},{1,3},{3,1},{4,6},{6,4},{5,7},{7,5},{8,10},{10,8},{9,1... | collective-permute-start | bytes 786440 | tf_op jit(solution)/shard_map/ppermute | solution.py:281
  47.9 7.7 %collective-permute-start.13 = (bf16[144,1024]{1,0:T(8,128)(2,1)S(1)}, bf16[144,1024]{1,0:T(8,128)(2,1)S(1)}, u32[]{:S(2)}, u32[]{:S(2)}) collective-permute-start(bf16[144,1024]{1,0:T(8,128)(2,1)S(1)} %collective-permute-done.12.refs_3_), channel_id=1, source_target_pairs={{0,4},{4,12},{12,8},{8,0},{1,5},{5,13},{13,9},{9,1},{2,6},{6,14},{... | collective-permute-start | bytes 884744 | tf_op jit(solution)/shard_map/ppermute | solution.py:307
  52.5 8.2 %collective-permute-start.14 = (bf16[128,1024]{1,0:T(8,128)(2,1)S(1)}, bf16[128,1024]{1,0:T(8,128)(2,1)S(1)}, u32[]{:S(2)}, u32[]{:S(2)}) collective-permute-start(bf16[128,1024]{1,0:T(8,128)(2,1)S(1)} %get-tuple-element.210), channel_id=1, source_target_pairs={{0,2},{2,0},{1,3},{3,1},{4,6},{6,4},{5,7},{7,5},{8,10},{10,8},{9,1... | collective-permute-start | bytes 786440 | tf_op jit(solution)/shard_map/ppermute | solution.py:288
  55.6 10.3 %collective-permute-start.17 = (bf16[128,1024]{1,0:T(8,128)(2,1)S(1)}, bf16[128,1024]{1,0:T(8,128)(2,1)S(1)}, u32[]{:S(2)}, u32[]{:S(2)}) collective-permute-start(bf16[128,1024]{1,0:T(8,128)(2,1)S(1)} %get-tuple-element.250), channel_id=1, source_target_pairs={{0,8},{4,0},{12,4},{8,12},{1,9},{5,1},{13,5},{9,13},{2,10},{6,2},{... | collective-permute-start | bytes 786440 | tf_op jit(solution)/shard_map/ppermute | solution.py:298
  60.8 9.9 %collective-permute-start.16 = (bf16[128,1024]{1,0:T(8,128)(2,1)S(1)}, bf16[128,1024]{1,0:T(8,128)(2,1)S(1)}, u32[]{:S(2)}, u32[]{:S(2)}) collective-permute-start(bf16[128,1024]{1,0:T(8,128)(2,1)S(1)} %add_convert_fusion.3), channel_id=1, source_target_pairs={{0,4},{4,12},{12,8},{8,0},{1,5},{5,13},{13,9},{9,1},{2,6},{6,14},{... | collective-permute-start | bytes 786440 | tf_op jit(solution)/shard_map/ppermute | solution.py:298
  62.9 7.7 %collective-permute-start.15 = (bf16[128,1024]{1,0:T(8,128)(2,1)S(1)}, bf16[128,1024]{1,0:T(8,128)(2,1)S(1)}, u32[]{:S(2)}, u32[]{:S(2)}) collective-permute-start(bf16[128,1024]{1,0:T(8,128)(2,1)S(1)} %get-tuple-element.246), channel_id=1, source_target_pairs={{0,2},{2,0},{1,3},{3,1},{4,6},{6,4},{5,7},{7,5},{8,10},{10,8},{9,1... | collective-permute-start | bytes 786440 | tf_op jit(solution)/shard_map/ppermute | solution.py:288
  70.7 9.1 %collective-permute-start.18 = (bf16[4,768,512]{2,1,0:T(8,128)(2,1)S(1)}, bf16[4,768,512]{2,1,0:T(8,128)(2,1)S(1)}, u32[]{:S(2)}, u32[]{:S(2)}) collective-permute-start(bf16[4,768,512]{2,1,0:T(8,128)(2,1)S(1)} %weight_grads.2), channel_id=1, source_target_pairs={{0,1},{1,0},{2,3},{3,2},{4,5},{5,4},{6,7},{7,6},{8,9},{9,8},{10,11... | collective-permute-start | bytes 9437192 | tf_op jit(solution)/shard_map/ppermute | solution.py:334
  70.7 9.1 %collective-permute-start.19 = (bf16[128,1024]{1,0:T(8,128)(2,1)S(1)}, bf16[128,1024]{1,0:T(8,128)(2,1)S(1)}, u32[]{:S(2)}, u32[]{:S(2)}) collective-permute-start(bf16[128,1024]{1,0:T(8,128)(2,1)S(1)} %get-tuple-element.252), channel_id=1, source_target_pairs={{0,8},{4,0},{12,4},{8,12},{1,9},{5,1},{13,5},{9,13},{2,10},{6,2},{... | collective-permute-start | bytes 786440 | tf_op jit(solution)/shard_map/ppermute | solution.py:298
  72.9 14.5 %collective-permute-start.20 = (bf16[128,1024]{1,0:T(8,128)(2,1)S(1)}, bf16[128,1024]{1,0:T(8,128)(2,1)S(1)}, u32[]{:S(2)}, u32[]{:S(2)}) collective-permute-start(bf16[128,1024]{1,0:T(8,128)(2,1)S(1)} %add_convert_fusion.1), channel_id=1, source_target_pairs={{0,4},{4,12},{12,8},{8,0},{1,5},{5,13},{13,9},{9,1},{2,6},{6,14},{... | collective-permute-start | bytes 786440 | tf_op jit(solution)/shard_map/ppermute | solution.py:298
  73.0 14.4 %collective-permute-start.21 = (bf16[128,1024]{1,0:T(8,128)(2,1)S(1)}, bf16[128,1024]{1,0:T(8,128)(2,1)S(1)}, u32[]{:S(2)}, u32[]{:S(2)}) collective-permute-start(bf16[128,1024]{1,0:T(8,128)(2,1)S(1)} %add_convert_fusion.2), channel_id=1, source_target_pairs={{0,2},{2,0},{1,3},{3,1},{4,6},{6,4},{5,7},{7,5},{8,10},{10,8},{9,1... | collective-permute-start | bytes 786440 | tf_op jit(solution)/shard_map/ppermute | solution.py:288

commit v13 on v12

--- a/solution.py
+++ b/solution.py
@@ -62,6 +62,7 @@
         out_shape=[pltpu.VMEM((rows, width), jnp.bfloat16) for rows in (tok_rows, tok_rows + ROUTE_ROWS)],
         scratch_shapes=[pltpu.SemaphoreType.DMA((2,))],
         compiler_params=pltpu.CompilerParams(vmem_limit_bytes=VMEM_LIMIT),
+        cost_estimate=pl.CostEstimate(flops=0, bytes_accessed=8 * tokens.size, transcendentals=0),
         name="pack",
     )(*operands)
 
@@ -102,6 +103,9 @@
         out_shape=[pltpu.VMEM(v.shape, v.dtype) for v in arrays],
         scratch_shapes=[pltpu.SemaphoreType.DMA((len(arrays),))],
         compiler_params=pltpu.CompilerParams(vmem_limit_bytes=VMEM_LIMIT),
+        cost_estimate=pl.CostEstimate(
+            flops=0, bytes_accessed=sum(4 * v.size for v in arrays), transcendentals=0
+        ),
         name="load",
     )(*[in_hbm(v) for v in arrays])
 
@@ -270,7 +274,6 @@
     z, x, core = (lax.axis_index(a) for a in ("group", "ingroup", "dp"))
     first_expert = ((z * n_ingroup + x) * local_experts).astype(jnp.int32).reshape(1)
     half = core.astype(jnp.int32).reshape(1)
-    weights = load_call((w_gate, w_up, w_down))
     wide = lambda v: v.astype(jnp.float32)
     tie = lambda *trees: lax.optimization_barrier(trees)
     order = ring_order(n_group)
@@ -298,6 +301,7 @@
         return lax.ppermute(group_part, "group", along(-k))
 
     tokens, first_expert, half, other_half = tie(tokens, first_expert, half, 1 - half)
+    weights = load_call((w_gate, w_up, w_down))
     first_tokens, upstream = pack_call(tokens, upstream, expert_ids, slots, gate_fixed)
     blocks, chunks, backs, sent = {}, {}, {}, {}
     last = n_group - 1
@@ -311,30 +315,28 @@
             tokens, upstream = (lax.ppermute(v, "group", along(1)) for v in (tokens, upstream))
         if k > 0:
             chunks[k - 1] = chunk(blocks[k - 1])
-        tokens, pair[0], chunks, weights = tie(tokens, pair[0], chunks, weights)
-        upstream, pair[1] = tie(upstream, pair[1])
+        upstream, pair[1], chunks, weights = tie(upstream, pair[1], chunks, weights)
+        tokens, pair[0] = tie(tokens, pair[0])
         blocks[k] = pair
 
     for k in range(2, last - 1):
         sent[k] = homeward(group_sum(chunks[k][0], across(chunks[k][1])), k)
+    backs[1] = across(chunks[1][1])
     backs[last - 1] = across(chunks[last - 1][1])
-    near_other, blocks[last] = tie(chunks[1][1], blocks[last])
-    near_other = homeward(near_other, 1)
     chunks[last] = chunk(blocks[last])
-    chunks, backs = tie(chunks, backs)
+    chunks, backs[1] = tie(chunks, backs[1])
 
     backs[last] = across(chunks[last][1])
+    sent[1] = homeward(group_sum(chunks[1][0], backs[1]), 1)
     carried = homeward(group_sum(chunks[last - 1][0], backs[last - 1]), last)
-    sent[1] = homeward(chunks[1][0], 1)
     kept = [[chunks[k][i] for k in range(n_group)] for i in (-3, -2, -1)]
+    kept, backs[last - 1] = tie(kept, backs[last - 1])
     to_send = weight_call(other_half, *kept)
-    other = (wide(chunks[0][1]) + wide(near_other)).astype(jnp.bfloat16)
-    to_send, backs[last], carried, other = tie(to_send, backs[last], carried, other)
-
     got = lax.ppermute(to_send, "dp", [(0, 1), (1, 0)])
+    other, to_send = tie(chunks[0][1], to_send)
+    backs[0] = across(other)
     sent[last] = homeward(group_sum(chunks[last][0], [*backs[last], carried]), last)
-    backs[0] = across(other)
-    got, sent[1] = tie(got, sent[1])
+    got, carried, backs[last] = tie(got, carried, backs[last])
     grads = weight_call(half, *kept, got)
     grads, sent, backs[0] = tie(grads, sent, backs[0])
     total = wide(chunks[0][0])

time: 88.5 us -> 88.1 us (level); the launches traced: 88.3 us -> 86.9 us
  waiting for transfers between devices: 33 us -> 24.7 us
  starting transfers between devices: 29.4 us -> 36.4 us
    ppermute x4 -> x3, waiting for transfers between devices: 15.3 us -> 7.43 us  [homeward(): return lax.ppermute(group_part, 'group', along(-k))]
    ppermute x3 -> x4, waiting for transfers between devices: 0.01 us -> 7.83 us  [across(): lax.ppermute(others[(s - 1) * tok_rows:s * tok_rows], 'ingroup', shift(-s))]
    ppermute x7, waiting for transfers between devices: 11 us -> 4.18 us  [spread(): lax.ppermute(column, 'ingroup', shift(s))]
    ppermute x6, starting transfers between devices: 9.92 us -> 14 us  [per_device(): lax.ppermute(v, 'group', along(1))]
    ppermute x4 -> x3, starting transfers between devices: 5.7 us -> 8.07 us  [homeward(): return lax.ppermute(group_part, 'group', along(-k))]
    ppermute x1, waiting for transfers between devices: 2.24 us -> 0.01 us  [per_device(): lax.ppermute(block, 'group', along(1))]
    ppermute x3 -> x4, starting transfers between devices: 3.09 us -> 4.12 us  [across(): lax.ppermute(others[(s - 1) * tok_rows:s * tok_rows], 'ingroup', shift(-s))]
  transfers between devices with their start and end apart: 22 -> 22, of which waited for: 10 -> 13; matrix products, arithmetic and copies ran while one was open for 0% -> 0% of each run, Pallas kernels for 25% -> 23%
where the time goes in v13:
time: 88.1 us; the launch traced here: 86.9 us
  starting transfers between devices  36.4 us (41%)
  waiting for transfers between devices  24.7 us (28%)
  Pallas kernels  23.9 us (27%)
  other arithmetic  1.13 us (1%)
    pallas_call x4, Pallas kernels, chunk_call(): pl.pallas_call(functools.partial(chunk_kernel, n_blocks, tok_rows, capaci...  14.7 us
    ppermute x6, starting transfers between devices, per_device(): lax.ppermute(v, 'group', along(1))  14 us
    ppermute x7, starting transfers between devices, spread(): lax.ppermute(column, 'ingroup', shift(s))  9.07 us
    ppermute x3, starting transfers between devices, homeward(): return lax.ppermute(group_part, 'group', along(-k))  8.07 us
    ppermute x4, waiting for transfers between devices, across(): lax.ppermute(others[(s - 1) * tok_rows:s * tok_rows], 'ingroup', shift(-s))  7.83 us
    ppermute x3, waiting for transfers between devices, homeward(): return lax.ppermute(group_part, 'group', along(-k))  7.43 us
    ppermute x6, waiting for transfers between devices, per_device(): lax.ppermute(v, 'group', along(1))  5.2 us
    pallas_call x2, Pallas kernels, weight_call(): pl.pallas_call(functools.partial(kernel, n), in_specs=[smem] + [vmem] * l...  4.57 us
  transfers between devices with their start and end apart: 22, of which 13 were waited for; matrix products, arithmetic and copies ran while one was open for 0% of the time, Pallas kernels for 23%

profile of v13, /device:TPU:0, one launch (start us, length us, event | category | flops | bytes accessed | tf_op | source)
XLA Modules:
  0.0 86.9 jit_solution(16368847499722778361)
XLA Ops:
  0.6 1.8 %pack.1 = (bf16[128,1024]{1,0:T(8,128)(2,1)S(1)}, bf16[144,1024]{1,0:T(8,128)(2,1)S(1)}) custom-call(bf16[128,1024]{1,0:T(8,128)(2,1)} %tokens, bf16[128,1024]{1,0:T(8,128)(2,1)} %upstream.1, s32[8,128]{1,0:T(8,128)} %bitcast.5, s32[8,128]{1,0:T(8,128)} %bitcast.6, s32[8,128]{1,0:T(8,128)} %bitcast.7), custom_call_target="tpu_custom_call" | custom-call | bytes 1048576 | tf_op jit(solution)/shard_map/pack/pallas_call | solution.py:58
  2.4 3.1 %collective-permute-start = (bf16[144,1024]{1,0:T(8,128)(2,1)S(1)}, bf16[144,1024]{1,0:T(8,128)(2,1)S(1)}, u32[]{:S(2)}, u32[]{:S(2)}) collective-permute-start(bf16[144,1024]{1,0:T(8,128)(2,1)S(1)} %get-tuple-element.149.refs_2_), channel_id=1, source_target_pairs={{0,4},{4,12},{12,8},{8,0},{1,5},{5,13},{13,9},{9,1},{2,6},{6,14},{... | collective-permute-start | bytes 884744 | tf_op jit(solution)/shard_map/ppermute | solution.py:315
  5.5 1.5 %collective-permute-start.1 = (bf16[144,1024]{1,0:T(8,128)(2,1)S(1)}, bf16[144,1024]{1,0:T(8,128)(2,1)S(1)}, u32[]{:S(2)}, u32[]{:S(2)}) collective-permute-start(bf16[144,1024]{1,0:T(8,128)(2,1)S(1)} %get-tuple-element.149.refs_2_), channel_id=1, source_target_pairs={{0,2},{2,0},{1,3},{3,1},{4,6},{6,4},{5,7},{7,5},{8,10},{10,8},{9,1... | collective-permute-start | bytes 884744 | tf_op jit(solution)/shard_map/ppermute | solution.py:284
  7.0 2.6 %collective-permute-start.4 = (bf16[128,1024]{1,0:T(8,128)(2,1)}, bf16[128,1024]{1,0:T(8,128)(2,1)S(1)}, u32[]{:S(2)}, u32[]{:S(2)}) collective-permute-start(bf16[128,1024]{1,0:T(8,128)(2,1)} %tokens), channel_id=1, source_target_pairs={{0,4},{4,12},{12,8},{8,0},{1,5},{5,13},{13,9},{9,1},{2,6},{6,14},{... | collective-permute-start | bytes 786440 | tf_op jit(solution)/shard_map/ppermute | solution.py:315
  9.6 0.5 collective-permute-start.5
  10.1 2.9 %load.1 = (bf16[4,1024,256]{2,1,0:T(8,128)(2,1)S(1)}, bf16[4,1024,256]{2,1,0:T(8,128)(2,1)S(1)}, bf16[4,256,1024]{2,1,0:T(8,128)(2,1)S(1)}) custom-call(bf16[4,1024,256]{2,1,0:T(8,128)(2,1)} %refs_0_.1, bf16[4,1024,256]{2,1,0:T(8,128)(2,1)} %refs_1_.1, bf16[4,256,1024]{2,1,0:T(8,128)(2,1)} %refs_2_.1), custom_call_target="tpu_custom_call" | custom-call | bytes 12582912 | tf_op jit(solution)/shard_map/load/pallas_call | solution.py:99
  13.0 1.3 %collective-permute-done.refs_2_ = bf16[144,1024]{1,0:T(8,128)(2,1)S(1)} collective-permute-done((bf16[144,1024]{1,0:T(8,128)(2,1)S(1)}, bf16[144,1024]{1,0:T(8,128)(2,1)S(1)}, u32[]{:S(2)}, u32[]{:S(2)}) %collective-permute-start) | collective-permute-done | bytes 294944 | tf_op jit(solution)/shard_map/ppermute | solution.py:315
  14.3 1.1 %collective-permute-done.1.refs_3_ = bf16[144,1024]{1,0:T(8,128)(2,1)S(1)} collective-permute-done((bf16[144,1024]{1,0:T(8,128)(2,1)S(1)}, bf16[144,1024]{1,0:T(8,128)(2,1)S(1)}, u32[]{:S(2)}, u32[]{:S(2)}) %collective-permute-start.1) | collective-permute-done | bytes 294944 | tf_op jit(solution)/shard_map/ppermute | solution.py:284
  15.4 2.6 %collective-permute-start.2 = (bf16[144,1024]{1,0:T(8,128)(2,1)S(1)}, bf16[144,1024]{1,0:T(8,128)(2,1)S(1)}, u32[]{:S(2)}, u32[]{:S(2)}) collective-permute-start(bf16[144,1024]{1,0:T(8,128)(2,1)S(1)} %collective-permute-done.refs_2_), channel_id=1, source_target_pairs={{0,4},{4,12},{12,8},{8,0},{1,5},{5,13},{13,9},{9,1},{2,6},{6,14},{... | collective-permute-start | bytes 884744 | tf_op jit(solution)/shard_map/ppermute | solution.py:315
  18.0 1.5 %collective-permute-start.3 = (bf16[144,1024]{1,0:T(8,128)(2,1)S(1)}, bf16[144,1024]{1,0:T(8,128)(2,1)S(1)}, u32[]{:S(2)}, u32[]{:S(2)}) collective-permute-start(bf16[144,1024]{1,0:T(8,128)(2,1)S(1)} %collective-permute-done.refs_2_), channel_id=1, source_target_pairs={{0,2},{2,0},{1,3},{3,1},{4,6},{6,4},{5,7},{7,5},{8,10},{10,8},{9,1... | collective-permute-start | bytes 884744 | tf_op jit(solution)/shard_map/ppermute | solution.py:284
  19.5 0.5 collective-permute-done.4.refs_0_
  20.0 1.1 %collective-permute-done.5.refs_1_ = bf16[128,1024]{1,0:T(8,128)(2,1)S(1)} collective-permute-done((bf16[128,1024]{1,0:T(8,128)(2,1)}, bf16[128,1024]{1,0:T(8,128)(2,1)S(1)}, u32[]{:S(2)}, u32[]{:S(2)}) %collective-permute-start.5) | collective-permute-done | bytes 262176 | tf_op jit(solution)/shard_map/ppermute | solution.py:284
  21.0 2.6 %collective-permute-start.8 = (bf16[128,1024]{1,0:T(8,128)(2,1)S(1)}, bf16[128,1024]{1,0:T(8,128)(2,1)S(1)}, u32[]{:S(2)}, u32[]{:S(2)}) collective-permute-start(bf16[128,1024]{1,0:T(8,128)(2,1)S(1)} %collective-permute-done.4.refs_0_), channel_id=1, source_target_pairs={{0,4},{4,12},{12,8},{8,0},{1,5},{5,13},{13,9},{9,1},{2,6},{6,14},{... | collective-permute-start | bytes 786440 | tf_op jit(solution)/shard_map/ppermute | solution.py:315
  23.6 1.5 %collective-permute-start.9 = (bf16[128,1024]{1,0:T(8,128)(2,1)S(1)}, bf16[128,1024]{1,0:T(8,128)(2,1)S(1)}, u32[]{:S(2)}, u32[]{:S(2)}) collective-permute-start(bf16[128,1024]{1,0:T(8,128)(2,1)S(1)} %collective-permute-done.4.refs_0_), channel_id=1, source_target_pairs={{0,2},{2,0},{1,3},{3,1},{4,6},{6,4},{5,7},{7,5},{8,10},{10,8},{9,1... | collective-permute-start | bytes 786440 | tf_op jit(solution)/shard_map/ppermute | solution.py:284
  25.1 3.7 %chunk.4 = (bf16[128,1024]{1,0:T(8,128)(2,1)S(1)}, bf16[128,1024]{1,0:T(8,128)(2,1)S(1)}, bf16[4,96,1024]{2,1,0:T(8,128)(2,1)S(1)}, bf16[4,96,1024]{2,1,0:T(8,128)(2,1)S(1)}, bf16[4,96,768]{2,1,0:T(8,128)(2,1)S(1)}) custom-call(s32[1]{0:T(128)} %bitcast.first_ref, bf16[128,1024]{1,0:T(8,128)(2,1)S(1)} %get-tuple-element.147.refs_0_, ...), custom_call_target="tpu_custom_call" | custom-call | flops 1610612736 | bytes 8388608 | tf_op jit(solution)/shard_map/chunk/pallas_call | solution.py:175
  28.8 0.0 collective-permute-done.2.refs_2_
  28.8 0.0 collective-permute-done.3.refs_3_
  28.8 1.1 %collective-permute-start.6 = (bf16[144,1024]{1,0:T(8,128)(2,1)S(1)}, bf16[144,1024]{1,0:T(8,128)(2,1)S(1)}, u32[]{:S(2)}, u32[]{:S(2)}) collective-permute-start(bf16[144,1024]{1,0:T(8,128)(2,1)S(1)} %collective-permute-done.2.refs_2_), channel_id=1, source_target_pairs={{0,4},{4,12},{12,8},{8,0},{1,5},{5,13},{13,9},{9,1},{2,6},{6,14},{... | collective-permute-start | bytes 884744 | tf_op jit(solution)/shard_map/ppermute | solution.py:315
  30.0 1.5 %collective-permute-start.7 = (bf16[144,1024]{1,0:T(8,128)(2,1)S(1)}, bf16[144,1024]{1,0:T(8,128)(2,1)S(1)}, u32[]{:S(2)}, u32[]{:S(2)}) collective-permute-start(bf16[144,1024]{1,0:T(8,128)(2,1)S(1)} %collective-permute-done.2.refs_2_), channel_id=1, source_target_pairs={{0,2},{2,0},{1,3},{3,1},{4,6},{6,4},{5,7},{7,5},{8,10},{10,8},{9,1... | collective-permute-start | bytes 884744 | tf_op jit(solution)/shard_map/ppermute | solution.py:284
  31.4 0.5 collective-permute-done.8.refs_0_
  31.9 1.7 %collective-permute-done.9.refs_1_ = bf16[128,1024]{1,0:T(8,128)(2,1)S(1)} collective-permute-done((bf16[128,1024]{1,0:T(8,128)(2,1)S(1)}, bf16[128,1024]{1,0:T(8,128)(2,1)S(1)}, u32[]{:S(2)}, u32[]{:S(2)}) %collective-permute-start.9) | collective-permute-done | bytes 262176 | tf_op jit(solution)/shard_map/ppermute | solution.py:284
  33.6 2.0 %collective-permute-start.11 = (bf16[128,1024]{1,0:T(8,128)(2,1)S(1)}, bf16[128,1024]{1,0:T(8,128)(2,1)S(1)}, u32[]{:S(2)}, u32[]{:S(2)}) collective-permute-start(bf16[128,1024]{1,0:T(8,128)(2,1)S(1)} %collective-permute-done.8.refs_0_), channel_id=1, source_target_pairs={{0,4},{4,12},{12,8},{8,0},{1,5},{5,13},{13,9},{9,1},{2,6},{6,14},{... | collective-permute-start | bytes 786440 | tf_op jit(solution)/shard_map/ppermute | solution.py:315
  35.6 1.5 %collective-permute-start.12 = (bf16[128,1024]{1,0:T(8,128)(2,1)S(1)}, bf16[128,1024]{1,0:T(8,128)(2,1)S(1)}, u32[]{:S(2)}, u32[]{:S(2)}) collective-permute-start(bf16[128,1024]{1,0:T(8,128)(2,1)S(1)} %collective-permute-done.8.refs_0_), channel_id=1, source_target_pairs={{0,2},{2,0},{1,3},{3,1},{4,6},{6,4},{5,7},{7,5},{8,10},{10,8},{9,1... | collective-permute-start | bytes 786440 | tf_op jit(solution)/shard_map/ppermute | solution.py:284
  37.1 3.7 %chunk.5 = (bf16[128,1024]{1,0:T(8,128)(2,1)S(1)}, bf16[128,1024]{1,0:T(8,128)(2,1)S(1)}, bf16[4,96,1024]{2,1,0:T(8,128)(2,1)S(1)}, bf16[4,96,1024]{2,1,0:T(8,128)(2,1)S(1)}, bf16[4,96,768]{2,1,0:T(8,128)(2,1)S(1)}) custom-call(s32[1]{0:T(128)} %bitcast.first_ref, bf16[128,1024]{1,0:T(8,128)(2,1)S(1)} %collective-permute-done.4.refs_0_, ...), custom_call_target="tpu_custom_call" | custom-call | flops 1610612736 | bytes 8388608 | tf_op jit(solution)/shard_map/chunk/pallas_call | solution.py:175
  40.7 0.0 collective-permute-done.6.refs_2_
  40.7 0.0 collective-permute-done.7.refs_3_
  40.8 1.1 %collective-permute-start.10 = (bf16[144,1024]{1,0:T(8,128)(2,1)S(1)}, bf16[144,1024]{1,0:T(8,128)(2,1)S(1)}, u32[]{:S(2)}, u32[]{:S(2)}) collective-permute-start(bf16[144,1024]{1,0:T(8,128)(2,1)S(1)} %collective-permute-done.7.refs_3_), channel_id=1, source_target_pairs={{0,4},{4,12},{12,8},{8,0},{1,5},{5,13},{13,9},{9,1},{2,6},{6,14},{... | collective-permute-start | bytes 884744 | tf_op jit(solution)/shard_map/ppermute | solution.py:311
  41.9 3.0 %collective-permute-done.11.refs_0_ = bf16[128,1024]{1,0:T(8,128)(2,1)S(1)} collective-permute-done((bf16[128,1024]{1,0:T(8,128)(2,1)S(1)}, bf16[128,1024]{1,0:T(8,128)(2,1)S(1)}, u32[]{:S(2)}, u32[]{:S(2)}) %collective-permute-start.11) | collective-permute-done | bytes 262176 | tf_op jit(solution)/shard_map/ppermute | solution.py:315
  44.8 0.0 collective-permute-done.12.refs_1_
  44.8 1.1 %collective-permute-start.13 = (bf16[128,1024]{1,0:T(8,128)(2,1)S(1)}, bf16[128,1024]{1,0:T(8,128)(2,1)S(1)}, u32[]{:S(2)}, u32[]{:S(2)}) collective-permute-start(bf16[128,1024]{1,0:T(8,128)(2,1)S(1)} %collective-permute-done.11.refs_0_), channel_id=1, source_target_pairs={{0,2},{2,0},{1,3},{3,1},{4,6},{6,4},{5,7},{7,5},{8,10},{10,8},{9,1... | collective-permute-start | bytes 786440 | tf_op jit(solution)/shard_map/ppermute | solution.py:284
  45.9 3.7 %chunk.6 = (bf16[128,1024]{1,0:T(8,128)(2,1)S(1)}, bf16[128,1024]{1,0:T(8,128)(2,1)S(1)}, bf16[4,96,1024]{2,1,0:T(8,128)(2,1)S(1)}, bf16[4,96,1024]{2,1,0:T(8,128)(2,1)S(1)}, bf16[4,96,768]{2,1,0:T(8,128)(2,1)S(1)}) custom-call(s32[1]{0:T(128)} %bitcast.first_ref, bf16[128,1024]{1,0:T(8,128)(2,1)S(1)} %collective-permute-done.8.refs_0_, ...), custom_call_target="tpu_custom_call" | custom-call | flops 1610612736 | bytes 8388608 | tf_op jit(solution)/shard_map/chunk/pallas_call | solution.py:175
  49.6 0.0 collective-permute-done.10.refs_3_
  49.6 1.2 %collective-permute-start.14 = (bf16[128,1024]{1,0:T(8,128)(2,1)S(1)}, bf16[128,1024]{1,0:T(8,128)(2,1)S(1)}, u32[]{:S(2)}, u32[]{:S(2)}) collective-permute-start(bf16[128,1024]{1,0:T(8,128)(2,1)S(1)} %get-tuple-element.208), channel_id=1, source_target_pairs={{0,2},{2,0},{1,3},{3,1},{4,6},{6,4},{5,7},{7,5},{8,10},{10,8},{9,1... | collective-permute-start | bytes 786440 | tf_op jit(solution)/shard_map/ppermute | solution.py:291
  50.9 0.9 collective-permute-start.15
  51.7 0.3 collective-permute-done.13.refs_1_
  52.0 3.7 %chunk.7 = (bf16[128,1024]{1,0:T(8,128)(2,1)S(1)}, bf16[128,1024]{1,0:T(8,128)(2,1)S(1)}, bf16[4,96,1024]{2,1,0:T(8,128)(2,1)S(1)}, bf16[4,96,1024]{2,1,0:T(8,128)(2,1)S(1)}, bf16[4,96,768]{2,1,0:T(8,128)(2,1)S(1)}) custom-call(s32[1]{0:T(128)} %bitcast.first_ref, bf16[128,1024]{1,0:T(8,128)(2,1)S(1)} %collective-permute-done.11.refs_0_, ...), custom_call_target="tpu_custom_call" | custom-call | flops 1610612736 | bytes 8388608 | tf_op jit(solution)/shard_map/chunk/pallas_call | solution.py:175
  55.7 3.2 %collective-permute-done.14 = bf16[128,1024]{1,0:T(8,128)(2,1)S(1)} collective-permute-done((bf16[128,1024]{1,0:T(8,128)(2,1)S(1)}, bf16[128,1024]{1,0:T(8,128)(2,1)S(1)}, u32[]{:S(2)}, u32[]{:S(2)}) %collective-permute-start.14) | collective-permute-done | bytes 262176 | tf_op jit(solution)/shard_map/ppermute | solution.py:291
  58.9 3.5 %collective-permute-done.15 = bf16[128,1024]{1,0:T(8,128)(2,1)S(1)} collective-permute-done((bf16[128,1024]{1,0:T(8,128)(2,1)S(1)}, bf16[128,1024]{1,0:T(8,128)(2,1)S(1)}, u32[]{:S(2)}, u32[]{:S(2)}) %collective-permute-start.15) | collective-permute-done | bytes 262176 | tf_op jit(solution)/shard_map/ppermute | solution.py:291
  62.5 1.9 %weight_grads.2 = bf16[4,768,512]{2,1,0:T(8,128)(2,1)S(1)} custom-call(s32[1]{0:T(128)S(6)} %sub.3.side_ref, bf16[4,96,1024]{2,1,0:T(8,128)(2,1)S(1)} %get-tuple-element.244.refs_0_, bf16[4,96,1024]{2,1,0:T(8,128)(2,1)S(1)} %get-tuple-element.245.refs_1_, bf16[4,96,1024]{2,1,0:T(8,128)(2,1)S(1)} %get-tuple-element.246.refs_2_, ...), custom_call_target="tpu_custom_call" | custom-call | flops 1207959552 | bytes 8650752 | tf_op jit(solution)/shard_map/weight_grads/pallas_call | solution.py:248
  64.3 0.1 collective-permute-start.16
  64.4 0.1 add_convert_fusion.3
  64.5 1.7 %collective-permute-start.17 = (bf16[128,1024]{1,0:T(8,128)(2,1)S(1)}, bf16[128,1024]{1,0:T(8,128)(2,1)S(1)}, u32[]{:S(2)}, u32[]{:S(2)}) collective-permute-start(bf16[128,1024]{1,0:T(8,128)(2,1)S(1)} %add_convert_fusion.3), channel_id=1, source_target_pairs={{0,4},{4,12},{12,8},{8,0},{1,5},{5,13},{13,9},{9,1},{2,6},{6,14},{... | collective-permute-start | bytes 786440 | tf_op jit(solution)/shard_map/ppermute | solution.py:301
  66.2 1.5 %collective-permute-start.18 = (bf16[128,1024]{1,0:T(8,128)(2,1)S(1)}, bf16[128,1024]{1,0:T(8,128)(2,1)S(1)}, u32[]{:S(2)}, u32[]{:S(2)}) collective-permute-start(bf16[128,1024]{1,0:T(8,128)(2,1)S(1)} %get-tuple-element.258), channel_id=1, source_target_pairs={{0,2},{2,0},{1,3},{3,1},{4,6},{6,4},{5,7},{7,5},{8,10},{10,8},{9,1... | collective-permute-start | bytes 786440 | tf_op jit(solution)/shard_map/ppermute | solution.py:291
  67.7 0.5 collective-permute-start.21
  68.2 0.1 add_convert_fusion.2
  68.3 1.3 %collective-permute-start.19 = (bf16[128,1024]{1,0:T(8,128)(2,1)S(1)}, bf16[128,1024]{1,0:T(8,128)(2,1)S(1)}, u32[]{:S(2)}, u32[]{:S(2)}) collective-permute-start(bf16[128,1024]{1,0:T(8,128)(2,1)S(1)} %add_convert_fusion.2), channel_id=1, source_target_pairs={{0,8},{4,0},{12,4},{8,12},{1,9},{5,1},{13,5},{9,13},{2,10},{6,2},{... | collective-permute-start | bytes 786440 | tf_op jit(solution)/shard_map/ppermute | solution.py:301
  69.6 4.6 %collective-permute-done.17 = bf16[128,1024]{1,0:T(8,128)(2,1)S(1)} collective-permute-done((bf16[128,1024]{1,0:T(8,128)(2,1)S(1)}, bf16[128,1024]{1,0:T(8,128)(2,1)S(1)}, u32[]{:S(2)}, u32[]{:S(2)}) %collective-permute-start.17) | collective-permute-done | bytes 262176 | tf_op jit(solution)/shard_map/ppermute | solution.py:301
  74.2 1.1 %collective-permute-done.18 = bf16[128,1024]{1,0:T(8,128)(2,1)S(1)} collective-permute-done((bf16[128,1024]{1,0:T(8,128)(2,1)S(1)}, bf16[128,1024]{1,0:T(8,128)(2,1)S(1)}, u32[]{:S(2)}, u32[]{:S(2)}) %collective-permute-start.18) | collective-permute-done | bytes 262176 | tf_op jit(solution)/shard_map/ppermute | solution.py:291
  75.4 0.1 add_convert_fusion.1
  75.5 5.0 %collective-permute-start.20 = (bf16[128,1024]{1,0:T(8,128)(2,1)S(1)}, bf16[128,1024]{1,0:T(8,128)(2,1)S(1)}, u32[]{:S(2)}, u32[]{:S(2)}) collective-permute-start(bf16[128,1024]{1,0:T(8,128)(2,1)S(1)} %add_convert_fusion.1), channel_id=1, source_target_pairs={{0,4},{4,12},{12,8},{8,0},{1,5},{5,13},{13,9},{9,1},{2,6},{6,14},{... | collective-permute-start | bytes 786440 | tf_op jit(solution)/shard_map/ppermute | solution.py:301
  80.5 0.0 collective-permute-done.16.refs_12_
  80.5 2.7 %weight_grads.3 = (bf16[4,512,256]{2,1,0:T(8,128)(2,1)}, bf16[4,512,256]{2,1,0:T(8,128)(2,1)}, bf16[4,256,512]{2,1,0:T(8,128)(2,1)}) custom-call(s32[1]{0:T(128)} %bitcast.1.side_ref, bf16[4,96,1024]{2,1,0:T(8,128)(2,1)S(1)} %get-tuple-element.244.refs_0_, bf16[4,96,1024]{2,1,0:T(8,128)(2,1)S(1)} %get-tuple-element.245.refs_1_, ...), custom_call_target="tpu_custom_call" | custom-call | flops 1207959552 | bytes 8650752 | tf_op jit(solution)/shard_map/weight_grads/pallas_call | solution.py:248
  83.2 0.0 collective-permute-done.21
  83.2 0.0 collective-permute-done.19
  83.3 2.8 %collective-permute-done.20 = bf16[128,1024]{1,0:T(8,128)(2,1)S(1)} collective-permute-done((bf16[128,1024]{1,0:T(8,128)(2,1)S(1)}, bf16[128,1024]{1,0:T(8,128)(2,1)S(1)}, u32[]{:S(2)}, u32[]{:S(2)}) %collective-permute-start.20) | collective-permute-done | bytes 262176 | tf_op jit(solution)/shard_map/ppermute | solution.py:301
  86.1 0.9 %add_convert_fusion = bf16[128,1024]{1,0:T(8,128)(2,1)} fusion(bf16[128,1024]{1,0:T(8,128)(2,1)S(1)} %collective-permute-done.20, bf16[128,1024]{1,0:T(8,128)(2,1)S(1)} %collective-permute-done.19, bf16[128,1024]{1,0:T(8,128)(2,1)S(1)} %collective-permute-done.21, bf16[128,1024]{1,0:T(8,128)(2,1)S(1)} %get-tuple-element.230), kind=kLoop, calls=%fused_computation | loop fusion | flops 1048576 | bytes 1310720 | tf_op jit(solution)/shard_map/convert_element_type | solution.py:347
Async XLA Ops:
  2.4 11.9 %collective-permute-start = (bf16[144,1024]{1,0:T(8,128)(2,1)S(1)}, bf16[144,1024]{1,0:T(8,128)(2,1)S(1)}, u32[]{:S(2)}, u32[]{:S(2)}) collective-permute-start(bf16[144,1024]{1,0:T(8,128)(2,1)S(1)} %get-tuple-element.149.refs_2_), channel_id=1, source_target_pairs={{0,4},{4,12},{12,8},{8,0},{1,5},{5,13},{13,9},{9,1},{2,6},{6,14},{... | collective-permute-start | bytes 884744 | tf_op jit(solution)/shard_map/ppermute | solution.py:315
  5.5 9.9 %collective-permute-start.1 = (bf16[144,1024]{1,0:T(8,128)(2,1)S(1)}, bf16[144,1024]{1,0:T(8,128)(2,1)S(1)}, u32[]{:S(2)}, u32[]{:S(2)}) collective-permute-start(bf16[144,1024]{1,0:T(8,128)(2,1)S(1)} %get-tuple-element.149.refs_2_), channel_id=1, source_target_pairs={{0,2},{2,0},{1,3},{3,1},{4,6},{6,4},{5,7},{7,5},{8,10},{10,8},{9,1... | collective-permute-start | bytes 884744 | tf_op jit(solution)/shard_map/ppermute | solution.py:284
  7.0 13.0 %collective-permute-start.4 = (bf16[128,1024]{1,0:T(8,128)(2,1)}, bf16[128,1024]{1,0:T(8,128)(2,1)S(1)}, u32[]{:S(2)}, u32[]{:S(2)}) collective-permute-start(bf16[128,1024]{1,0:T(8,128)(2,1)} %tokens), channel_id=1, source_target_pairs={{0,4},{4,12},{12,8},{8,0},{1,5},{5,13},{13,9},{9,1},{2,6},{6,14},{... | collective-permute-start | bytes 786440 | tf_op jit(solution)/shard_map/ppermute | solution.py:315
  9.6 11.5 %collective-permute-start.5 = (bf16[128,1024]{1,0:T(8,128)(2,1)}, bf16[128,1024]{1,0:T(8,128)(2,1)S(1)}, u32[]{:S(2)}, u32[]{:S(2)}) collective-permute-start(bf16[128,1024]{1,0:T(8,128)(2,1)} %tokens), channel_id=1, source_target_pairs={{0,2},{2,0},{1,3},{3,1},{4,6},{6,4},{5,7},{7,5},{8,10},{10,8},{9,1... | collective-permute-start | bytes 786440 | tf_op jit(solution)/shard_map/ppermute | solution.py:284
  15.4 13.4 %collective-permute-start.2 = (bf16[144,1024]{1,0:T(8,128)(2,1)S(1)}, bf16[144,1024]{1,0:T(8,128)(2,1)S(1)}, u32[]{:S(2)}, u32[]{:S(2)}) collective-permute-start(bf16[144,1024]{1,0:T(8,128)(2,1)S(1)} %collective-permute-done.refs_2_), channel_id=1, source_target_pairs={{0,4},{4,12},{12,8},{8,0},{1,5},{5,13},{13,9},{9,1},{2,6},{6,14},{... | collective-permute-start | bytes 884744 | tf_op jit(solution)/shard_map/ppermute | solution.py:315
  18.0 10.8 %collective-permute-start.3 = (bf16[144,1024]{1,0:T(8,128)(2,1)S(1)}, bf16[144,1024]{1,0:T(8,128)(2,1)S(1)}, u32[]{:S(2)}, u32[]{:S(2)}) collective-permute-start(bf16[144,1024]{1,0:T(8,128)(2,1)S(1)} %collective-permute-done.refs_2_), channel_id=1, source_target_pairs={{0,2},{2,0},{1,3},{3,1},{4,6},{6,4},{5,7},{7,5},{8,10},{10,8},{9,1... | collective-permute-start | bytes 884744 | tf_op jit(solution)/shard_map/ppermute | solution.py:284
  21.0 10.9 %collective-permute-start.8 = (bf16[128,1024]{1,0:T(8,128)(2,1)S(1)}, bf16[128,1024]{1,0:T(8,128)(2,1)S(1)}, u32[]{:S(2)}, u32[]{:S(2)}) collective-permute-start(bf16[128,1024]{1,0:T(8,128)(2,1)S(1)} %collective-permute-done.4.refs_0_), channel_id=1, source_target_pairs={{0,4},{4,12},{12,8},{8,0},{1,5},{5,13},{13,9},{9,1},{2,6},{6,14},{... | collective-permute-start | bytes 786440 | tf_op jit(solution)/shard_map/ppermute | solution.py:315
  23.6 9.9 %collective-permute-start.9 = (bf16[128,1024]{1,0:T(8,128)(2,1)S(1)}, bf16[128,1024]{1,0:T(8,128)(2,1)S(1)}, u32[]{:S(2)}, u32[]{:S(2)}) collective-permute-start(bf16[128,1024]{1,0:T(8,128)(2,1)S(1)} %collective-permute-done.4.refs_0_), channel_id=1, source_target_pairs={{0,2},{2,0},{1,3},{3,1},{4,6},{6,4},{5,7},{7,5},{8,10},{10,8},{9,1... | collective-permute-start | bytes 786440 | tf_op jit(solution)/shard_map/ppermute | solution.py:284
  28.8 11.9 %collective-permute-start.6 = (bf16[144,1024]{1,0:T(8,128)(2,1)S(1)}, bf16[144,1024]{1,0:T(8,128)(2,1)S(1)}, u32[]{:S(2)}, u32[]{:S(2)}) collective-permute-start(bf16[144,1024]{1,0:T(8,128)(2,1)S(1)} %collective-permute-done.2.refs_2_), channel_id=1, source_target_pairs={{0,4},{4,12},{12,8},{8,0},{1,5},{5,13},{13,9},{9,1},{2,6},{6,14},{... | collective-permute-start | bytes 884744 | tf_op jit(solution)/shard_map/ppermute | solution.py:315
  30.0 10.8 %collective-permute-start.7 = (bf16[144,1024]{1,0:T(8,128)(2,1)S(1)}, bf16[144,1024]{1,0:T(8,128)(2,1)S(1)}, u32[]{:S(2)}, u32[]{:S(2)}) collective-permute-start(bf16[144,1024]{1,0:T(8,128)(2,1)S(1)} %collective-permute-done.2.refs_2_), channel_id=1, source_target_pairs={{0,2},{2,0},{1,3},{3,1},{4,6},{6,4},{5,7},{7,5},{8,10},{10,8},{9,1... | collective-permute-start | bytes 884744 | tf_op jit(solution)/shard_map/ppermute | solution.py:284
  33.6 11.3 %collective-permute-start.11 = (bf16[128,1024]{1,0:T(8,128)(2,1)S(1)}, bf16[128,1024]{1,0:T(8,128)(2,1)S(1)}, u32[]{:S(2)}, u32[]{:S(2)}) collective-permute-start(bf16[128,1024]{1,0:T(8,128)(2,1)S(1)} %collective-permute-done.8.refs_0_), channel_id=1, source_target_pairs={{0,4},{4,12},{12,8},{8,0},{1,5},{5,13},{13,9},{9,1},{2,6},{6,14},{... | collective-permute-start | bytes 786440 | tf_op jit(solution)/shard_map/ppermute | solution.py:315
  35.6 9.3 %collective-permute-start.12 = (bf16[128,1024]{1,0:T(8,128)(2,1)S(1)}, bf16[128,1024]{1,0:T(8,128)(2,1)S(1)}, u32[]{:S(2)}, u32[]{:S(2)}) collective-permute-start(bf16[128,1024]{1,0:T(8,128)(2,1)S(1)} %collective-permute-done.8.refs_0_), channel_id=1, source_target_pairs={{0,2},{2,0},{1,3},{3,1},{4,6},{6,4},{5,7},{7,5},{8,10},{10,8},{9,1... | collective-permute-start | bytes 786440 | tf_op jit(solution)/shard_map/ppermute | solution.py:284
  40.8 8.9 %collective-permute-start.10 = (bf16[144,1024]{1,0:T(8,128)(2,1)S(1)}, bf16[144,1024]{1,0:T(8,128)(2,1)S(1)}, u32[]{:S(2)}, u32[]{:S(2)}) collective-permute-start(bf16[144,1024]{1,0:T(8,128)(2,1)S(1)} %collective-permute-done.7.refs_3_), channel_id=1, source_target_pairs={{0,4},{4,12},{12,8},{8,0},{1,5},{5,13},{13,9},{9,1},{2,6},{6,14},{... | collective-permute-start | bytes 884744 | tf_op jit(solution)/shard_map/ppermute | solution.py:311
  44.8 7.2 %collective-permute-start.13 = (bf16[128,1024]{1,0:T(8,128)(2,1)S(1)}, bf16[128,1024]{1,0:T(8,128)(2,1)S(1)}, u32[]{:S(2)}, u32[]{:S(2)}) collective-permute-start(bf16[128,1024]{1,0:T(8,128)(2,1)S(1)} %collective-permute-done.11.refs_0_), channel_id=1, source_target_pairs={{0,2},{2,0},{1,3},{3,1},{4,6},{6,4},{5,7},{7,5},{8,10},{10,8},{9,1... | collective-permute-start | bytes 786440 | tf_op jit(solution)/shard_map/ppermute | solution.py:284
  49.6 9.3 %collective-permute-start.14 = (bf16[128,1024]{1,0:T(8,128)(2,1)S(1)}, bf16[128,1024]{1,0:T(8,128)(2,1)S(1)}, u32[]{:S(2)}, u32[]{:S(2)}) collective-permute-start(bf16[128,1024]{1,0:T(8,128)(2,1)S(1)} %get-tuple-element.208), channel_id=1, source_target_pairs={{0,2},{2,0},{1,3},{3,1},{4,6},{6,4},{5,7},{7,5},{8,10},{10,8},{9,1... | collective-permute-start | bytes 786440 | tf_op jit(solution)/shard_map/ppermute | solution.py:291
  50.9 11.6 %collective-permute-start.15 = (bf16[128,1024]{1,0:T(8,128)(2,1)S(1)}, bf16[128,1024]{1,0:T(8,128)(2,1)S(1)}, u32[]{:S(2)}, u32[]{:S(2)}) collective-permute-start(bf16[128,1024]{1,0:T(8,128)(2,1)S(1)} %get-tuple-element.213), channel_id=1, source_target_pairs={{0,2},{2,0},{1,3},{3,1},{4,6},{6,4},{5,7},{7,5},{8,10},{10,8},{9,1... | collective-permute-start | bytes 786440 | tf_op jit(solution)/shard_map/ppermute | solution.py:291
  64.3 16.2 %collective-permute-start.16 = (bf16[4,768,512]{2,1,0:T(8,128)(2,1)S(1)}, bf16[4,768,512]{2,1,0:T(8,128)(2,1)S(1)}, u32[]{:S(2)}, u32[]{:S(2)}) collective-permute-start(bf16[4,768,512]{2,1,0:T(8,128)(2,1)S(1)} %weight_grads.2), channel_id=1, source_target_pairs={{0,1},{1,0},{2,3},{3,2},{4,5},{5,4},{6,7},{7,6},{8,9},{9,8},{10,11... | collective-permute-start | bytes 9437192 | tf_op jit(solution)/shard_map/ppermute | solution.py:335
  64.5 9.8 %collective-permute-start.17 = (bf16[128,1024]{1,0:T(8,128)(2,1)S(1)}, bf16[128,1024]{1,0:T(8,128)(2,1)S(1)}, u32[]{:S(2)}, u32[]{:S(2)}) collective-permute-start(bf16[128,1024]{1,0:T(8,128)(2,1)S(1)} %add_convert_fusion.3), channel_id=1, source_target_pairs={{0,4},{4,12},{12,8},{8,0},{1,5},{5,13},{13,9},{9,1},{2,6},{6,14},{... | collective-permute-start | bytes 786440 | tf_op jit(solution)/shard_map/ppermute | solution.py:301
  66.2 9.1 %collective-permute-start.18 = (bf16[128,1024]{1,0:T(8,128)(2,1)S(1)}, bf16[128,1024]{1,0:T(8,128)(2,1)S(1)}, u32[]{:S(2)}, u32[]{:S(2)}) collective-permute-start(bf16[128,1024]{1,0:T(8,128)(2,1)S(1)} %get-tuple-element.258), channel_id=1, source_target_pairs={{0,2},{2,0},{1,3},{3,1},{4,6},{6,4},{5,7},{7,5},{8,10},{10,8},{9,1... | collective-permute-start | bytes 786440 | tf_op jit(solution)/shard_map/ppermute | solution.py:291
  67.7 15.5 %collective-permute-start.21 = (bf16[128,1024]{1,0:T(8,128)(2,1)S(1)}, bf16[128,1024]{1,0:T(8,128)(2,1)S(1)}, u32[]{:S(2)}, u32[]{:S(2)}) collective-permute-start(bf16[128,1024]{1,0:T(8,128)(2,1)S(1)} %get-tuple-element.267), channel_id=1, source_target_pairs={{0,2},{2,0},{1,3},{3,1},{4,6},{6,4},{5,7},{7,5},{8,10},{10,8},{9,1... | collective-permute-start | bytes 786440 | tf_op jit(solution)/shard_map/ppermute | solution.py:291
  68.3 14.9 %collective-permute-start.19 = (bf16[128,1024]{1,0:T(8,128)(2,1)S(1)}, bf16[128,1024]{1,0:T(8,128)(2,1)S(1)}, u32[]{:S(2)}, u32[]{:S(2)}) collective-permute-start(bf16[128,1024]{1,0:T(8,128)(2,1)S(1)} %add_convert_fusion.2), channel_id=1, source_target_pairs={{0,8},{4,0},{12,4},{8,12},{1,9},{5,1},{13,5},{9,13},{2,10},{6,2},{... | collective-permute-start | bytes 786440 | tf_op jit(solution)/shard_map/ppermute | solution.py:301
  75.5 10.6 %collective-permute-start.20 = (bf16[128,1024]{1,0:T(8,128)(2,1)S(1)}, bf16[128,1024]{1,0:T(8,128)(2,1)S(1)}, u32[]{:S(2)}, u32[]{:S(2)}) collective-permute-start(bf16[128,1024]{1,0:T(8,128)(2,1)S(1)} %add_convert_fusion.1), channel_id=1, source_target_pairs={{0,4},{4,12},{12,8},{8,0},{1,5},{5,13},{13,9},{9,1},{2,6},{6,14},{... | collective-permute-start | bytes 786440 | tf_op jit(solution)/shard_map/ppermute | solution.py:301

commit v14 on v11

--- a/solution.py
+++ b/solution.py
@@ -62,6 +62,7 @@
         out_shape=[pltpu.VMEM((rows, width), jnp.bfloat16) for rows in (tok_rows, tok_rows + ROUTE_ROWS)],
         scratch_shapes=[pltpu.SemaphoreType.DMA((2,))],
         compiler_params=pltpu.CompilerParams(vmem_limit_bytes=VMEM_LIMIT),
+        cost_estimate=pl.CostEstimate(flops=0, bytes_accessed=8 * tokens.size, transcendentals=0),
         name="pack",
     )(*operands)
 
@@ -102,6 +103,9 @@
         out_shape=[pltpu.VMEM(v.shape, v.dtype) for v in arrays],
         scratch_shapes=[pltpu.SemaphoreType.DMA((len(arrays),))],
         compiler_params=pltpu.CompilerParams(vmem_limit_bytes=VMEM_LIMIT),
+        cost_estimate=pl.CostEstimate(
+            flops=0, bytes_accessed=sum(4 * v.size for v in arrays), transcendentals=0
+        ),
         name="load",
     )(*[in_hbm(v) for v in arrays])
 
@@ -270,7 +274,6 @@
     z, x, core = (lax.axis_index(a) for a in ("group", "ingroup", "dp"))
     first_expert = ((z * n_ingroup + x) * local_experts).astype(jnp.int32).reshape(1)
     half = core.astype(jnp.int32).reshape(1)
-    weights = load_call((w_gate, w_up, w_down))
     wide = lambda v: v.astype(jnp.float32)
     tie = lambda *trees: lax.optimization_barrier(trees)
     order = ring_order(n_group)
@@ -298,38 +301,42 @@
         return lax.ppermute(group_part, "group", along(-k))
 
     tokens, first_expert, half, other_half = tie(tokens, first_expert, half, 1 - half)
+    weights = load_call((w_gate, w_up, w_down))
     first_tokens, upstream = pack_call(tokens, upstream, expert_ids, slots, gate_fixed)
     blocks, chunks, backs, sent = {}, {}, {}, {}
     last = n_group - 1
     for k in range(n_group):
-        pair = [spread(tokens), spread(upstream)]
+        pair = [spread(tokens) if k < last else [tokens], spread(upstream)]
+        if k == last:
+            pair[0] += [lax.ppermute(block, "group", along(1)) for block in blocks[k - 1][0][1:]]
         if k == 0:
             pair[0][0] = first_tokens
         if k < last:
             tokens, upstream = (lax.ppermute(v, "group", along(1)) for v in (tokens, upstream))
         if k > 0:
             chunks[k - 1] = chunk(blocks[k - 1], k - 1 == 1)
-        tokens, pair[0], chunks, weights = tie(tokens, pair[0], chunks, weights)
-        upstream, pair[1] = tie(upstream, pair[1])
+        upstream, pair[1], chunks, weights = tie(upstream, pair[1], chunks, weights)
+        tokens, pair[0] = tie(tokens, pair[0])
         blocks[k] = pair
 
     for k in range(2, last - 1):
         sent[k] = homeward(group_sum(chunks[k][0], across(chunks[k][1])), k)
-    near = lax.ppermute(chunks[1][0], "group", along(-1))
-    blocks[last], chunks = tie(blocks[last], chunks)
     backs[last - 1] = across(chunks[last - 1][1])
+    near, blocks[last] = tie(chunks[1][0], blocks[last])
+    near = homeward(near, 1)
     chunks[last] = chunk(blocks[last])
-    chunks, backs, near = tie(chunks, backs, near)
-
     backs[last] = across(chunks[last][1])
+    chunks, backs[last - 1], near = tie(chunks, backs[last - 1], near)
+
     carried = homeward(group_sum(chunks[last - 1][0], backs[last - 1]), last)
     kept = [[chunks[k][i] for k in range(n_group)] for i in (-3, -2, -1)]
     to_send = weight_call(other_half, *kept)
-    to_send, backs[last], carried = tie(to_send, backs[last], carried)
+    other = (wide(chunks[0][1]) + wide(near[tok_rows:])).astype(jnp.bfloat16)
+    to_send, backs[last], carried, other = tie(to_send, backs[last], carried, other)
 
     got = lax.ppermute(to_send, "dp", [(0, 1), (1, 0)])
     sent[last] = homeward(group_sum(chunks[last][0], [*backs[last], carried]), last)
-    backs[0] = across((wide(chunks[0][1]) + wide(near[tok_rows:])).astype(jnp.bfloat16))
+    backs[0] = across(other)
     grads = weight_call(half, *kept, got)
     grads, sent, backs[0] = tie(grads, sent, backs[0])
     total = wide(chunks[0][0]) + wide(near[:tok_rows])

time: 81 us -> 82.3 us (1.016)
  waiting for transfers between devices: 20.7 us -> 30.2 us
  starting transfers between devices: 34.2 us -> 26.1 us
    ppermute x6, waiting for transfers between devices: 4.04 us -> 10.6 us  [per_device(): lax.ppermute(v, 'group', along(1))]
    ppermute x8 -> x7, waiting for transfers between devices: 8.15 us -> 4.24 us  [spread(): lax.ppermute(column, 'ingroup', shift(s))]
    ppermute x6, starting transfers between devices: 13.8 us -> 10.1 us  [per_device(): lax.ppermute(v, 'group', along(1))]
    ppermute x8 -> x7, starting transfers between devices: 9.6 us -> 6.68 us  [spread(): lax.ppermute(column, 'ingroup', shift(s))]
    ppermute x2 -> x3, waiting for transfers between devices: 3.36 us -> 5.59 us  [homeward(): return lax.ppermute(group_part, 'group', along(-k))]
    ppermute x1, waiting for transfers between devices: 0.49 us -> 2.46 us  [per_device(): lax.ppermute(block, 'group', along(1))]
    ppermute x3, waiting for transfers between devices: 1.84 us -> 3.33 us  [across(): lax.ppermute(others[(s - 1) * tok_rows:s * tok_rows], 'ingroup', shift(-s))]
    ppermute x3, starting transfers between devices: 3.58 us -> 2.09 us  [across(): lax.ppermute(others[(s - 1) * tok_rows:s * tok_rows], 'ingroup', shift(-s))]
  transfers between devices with their start and end apart: 21 -> 21, of which waited for: 14 -> 16; matrix products, arithmetic and copies ran while one was open for 0% -> 0% of each run, Pallas kernels for 30% -> 27%
where the time goes in v14:
time: 82.3 us; the launch traced here: 82.1 us
  waiting for transfers between devices  30.2 us (37%)
  starting transfers between devices  26.1 us (32%)
  Pallas kernels  23.9 us (29%)
  other arithmetic  1.13 us (1%)
    pallas_call x4, Pallas kernels, chunk_call(): pl.pallas_call(functools.partial(chunk_kernel, n_blocks, tok_rows, capaci...  14.7 us
    ppermute x6, waiting for transfers between devices, per_device(): lax.ppermute(v, 'group', along(1))  10.6 us
    ppermute x6, starting transfers between devices, per_device(): lax.ppermute(v, 'group', along(1))  10.1 us
    ppermute x7, starting transfers between devices, spread(): lax.ppermute(column, 'ingroup', shift(s))  6.68 us
    ppermute x3, starting transfers between devices, homeward(): return lax.ppermute(group_part, 'group', along(-k))  5.69 us
    ppermute x3, waiting for transfers between devices, homeward(): return lax.ppermute(group_part, 'group', along(-k))  5.59 us
    pallas_call x2, Pallas kernels, weight_call(): pl.pallas_call(functools.partial(kernel, n), in_specs=[smem] + [vmem] * l...  4.56 us
    ppermute x7, waiting for transfers between devices, spread(): lax.ppermute(column, 'ingroup', shift(s))  4.24 us
  transfers between devices with their start and end apart: 21, of which 16 were waited for; matrix products, arithmetic and copies ran while one was open for 0% of the time, Pallas kernels for 27%

profile of v14, /device:TPU:0, one launch (start us, length us, event | category | flops | bytes accessed | tf_op | source)
XLA Modules:
  0.0 82.1 jit_solution(14954284803817877779)
XLA Ops:
  0.6 1.8 %pack.1 = (bf16[128,1024]{1,0:T(8,128)(2,1)S(1)}, bf16[144,1024]{1,0:T(8,128)(2,1)S(1)}) custom-call(bf16[128,1024]{1,0:T(8,128)(2,1)} %tokens, bf16[128,1024]{1,0:T(8,128)(2,1)} %upstream.1, s32[8,128]{1,0:T(8,128)} %bitcast.5, s32[8,128]{1,0:T(8,128)} %bitcast.6, s32[8,128]{1,0:T(8,128)} %bitcast.7), custom_call_target="tpu_custom_call" | custom-call | bytes 1048576 | tf_op jit(solution)/shard_map/pack/pallas_call | solution.py:58
  2.4 3.0 %collective-permute-start.1 = (bf16[144,1024]{1,0:T(8,128)(2,1)S(1)}, bf16[144,1024]{1,0:T(8,128)(2,1)S(1)}, u32[]{:S(2)}, u32[]{:S(2)}) collective-permute-start(bf16[144,1024]{1,0:T(8,128)(2,1)S(1)} %get-tuple-element.139.refs_2_), channel_id=1, source_target_pairs={{0,2},{2,0},{1,3},{3,1},{4,6},{6,4},{5,7},{7,5},{8,10},{10,8},{9,1... | collective-permute-start | bytes 884744 | tf_op jit(solution)/shard_map/ppermute | solution.py:284
  5.4 1.6 %collective-permute-start = (bf16[144,1024]{1,0:T(8,128)(2,1)S(1)}, bf16[144,1024]{1,0:T(8,128)(2,1)S(1)}, u32[]{:S(2)}, u32[]{:S(2)}) collective-permute-start(bf16[144,1024]{1,0:T(8,128)(2,1)S(1)} %get-tuple-element.139.refs_2_), channel_id=1, source_target_pairs={{0,4},{4,12},{12,8},{8,0},{1,5},{5,13},{13,9},{9,1},{2,6},{6,14},{... | collective-permute-start | bytes 884744 | tf_op jit(solution)/shard_map/ppermute | solution.py:315
  7.0 0.5 collective-permute-start.5
  7.5 2.6 %collective-permute-start.4 = (bf16[128,1024]{1,0:T(8,128)(2,1)}, bf16[128,1024]{1,0:T(8,128)(2,1)S(1)}, u32[]{:S(2)}, u32[]{:S(2)}) collective-permute-start(bf16[128,1024]{1,0:T(8,128)(2,1)} %tokens), channel_id=1, source_target_pairs={{0,4},{4,12},{12,8},{8,0},{1,5},{5,13},{13,9},{9,1},{2,6},{6,14},{... | collective-permute-start | bytes 786440 | tf_op jit(solution)/shard_map/ppermute | solution.py:315
  10.1 2.9 %load.1 = (bf16[4,1024,256]{2,1,0:T(8,128)(2,1)S(1)}, bf16[4,1024,256]{2,1,0:T(8,128)(2,1)S(1)}, bf16[4,256,1024]{2,1,0:T(8,128)(2,1)S(1)}) custom-call(bf16[4,1024,256]{2,1,0:T(8,128)(2,1)} %refs_0_.1, bf16[4,1024,256]{2,1,0:T(8,128)(2,1)} %refs_1_.1, bf16[4,256,1024]{2,1,0:T(8,128)(2,1)} %refs_2_.1), custom_call_target="tpu_custom_call" | custom-call | bytes 12582912 | tf_op jit(solution)/shard_map/load/pallas_call | solution.py:99
  13.0 0.2 collective-permute-done.1.refs_3_
  13.3 3.0 %collective-permute-done.refs_2_ = bf16[144,1024]{1,0:T(8,128)(2,1)S(1)} collective-permute-done((bf16[144,1024]{1,0:T(8,128)(2,1)S(1)}, bf16[144,1024]{1,0:T(8,128)(2,1)S(1)}, u32[]{:S(2)}, u32[]{:S(2)}) %collective-permute-start) | collective-permute-done | bytes 294944 | tf_op jit(solution)/shard_map/ppermute | solution.py:315
  16.3 0.2 collective-permute-start.3
  16.4 1.2 %collective-permute-start.2 = (bf16[144,1024]{1,0:T(8,128)(2,1)S(1)}, bf16[144,1024]{1,0:T(8,128)(2,1)S(1)}, u32[]{:S(2)}, u32[]{:S(2)}) collective-permute-start(bf16[144,1024]{1,0:T(8,128)(2,1)S(1)} %collective-permute-done.refs_2_), channel_id=1, source_target_pairs={{0,4},{4,12},{12,8},{8,0},{1,5},{5,13},{13,9},{9,1},{2,6},{6,14},{... | collective-permute-start | bytes 884744 | tf_op jit(solution)/shard_map/ppermute | solution.py:315
  17.6 1.3 %collective-permute-done.5.refs_1_ = bf16[128,1024]{1,0:T(8,128)(2,1)S(1)} collective-permute-done((bf16[128,1024]{1,0:T(8,128)(2,1)}, bf16[128,1024]{1,0:T(8,128)(2,1)S(1)}, u32[]{:S(2)}, u32[]{:S(2)}) %collective-permute-start.5) | collective-permute-done | bytes 262176 | tf_op jit(solution)/shard_map/ppermute | solution.py:284
  18.9 3.0 %collective-permute-done.4.refs_0_ = bf16[128,1024]{1,0:T(8,128)(2,1)S(1)} collective-permute-done((bf16[128,1024]{1,0:T(8,128)(2,1)}, bf16[128,1024]{1,0:T(8,128)(2,1)S(1)}, u32[]{:S(2)}, u32[]{:S(2)}) %collective-permute-start.4) | collective-permute-done | bytes 262176 | tf_op jit(solution)/shard_map/ppermute | solution.py:315
  21.9 0.2 collective-permute-start.9
  22.0 1.3 %collective-permute-start.8 = (bf16[128,1024]{1,0:T(8,128)(2,1)S(1)}, bf16[128,1024]{1,0:T(8,128)(2,1)S(1)}, u32[]{:S(2)}, u32[]{:S(2)}) collective-permute-start(bf16[128,1024]{1,0:T(8,128)(2,1)S(1)} %collective-permute-done.4.refs_0_), channel_id=1, source_target_pairs={{0,4},{4,12},{12,8},{8,0},{1,5},{5,13},{13,9},{9,1},{2,6},{6,14},{... | collective-permute-start | bytes 786440 | tf_op jit(solution)/shard_map/ppermute | solution.py:315
  23.3 3.7 %chunk.4 = (bf16[128,1024]{1,0:T(8,128)(2,1)S(1)}, bf16[128,1024]{1,0:T(8,128)(2,1)S(1)}, bf16[4,96,1024]{2,1,0:T(8,128)(2,1)S(1)}, bf16[4,96,1024]{2,1,0:T(8,128)(2,1)S(1)}, bf16[4,96,768]{2,1,0:T(8,128)(2,1)S(1)}) custom-call(s32[1]{0:T(128)} %bitcast.first_ref, bf16[128,1024]{1,0:T(8,128)(2,1)S(1)} %get-tuple-element.137.refs_0_, ...), custom_call_target="tpu_custom_call" | custom-call | flops 1610612736 | bytes 8388608 | tf_op jit(solution)/shard_map/chunk/pallas_call | solution.py:175
  27.0 0.0 collective-permute-done.3.refs_3_
  27.0 1.2 %collective-permute-done.2.refs_2_ = bf16[144,1024]{1,0:T(8,128)(2,1)S(1)} collective-permute-done((bf16[144,1024]{1,0:T(8,128)(2,1)S(1)}, bf16[144,1024]{1,0:T(8,128)(2,1)S(1)}, u32[]{:S(2)}, u32[]{:S(2)}) %collective-permute-start.2) | collective-permute-done | bytes 294944 | tf_op jit(solution)/shard_map/ppermute | solution.py:315
  28.2 0.9 %collective-permute-start.7 = (bf16[144,1024]{1,0:T(8,128)(2,1)S(1)}, bf16[144,1024]{1,0:T(8,128)(2,1)S(1)}, u32[]{:S(2)}, u32[]{:S(2)}) collective-permute-start(bf16[144,1024]{1,0:T(8,128)(2,1)S(1)} %collective-permute-done.2.refs_2_), channel_id=1, source_target_pairs={{0,2},{2,0},{1,3},{3,1},{4,6},{6,4},{5,7},{7,5},{8,10},{10,8},{9,1... | collective-permute-start | bytes 884744 | tf_op jit(solution)/shard_map/ppermute | solution.py:284
  29.1 2.7 %collective-permute-start.6 = (bf16[144,1024]{1,0:T(8,128)(2,1)S(1)}, bf16[144,1024]{1,0:T(8,128)(2,1)S(1)}, u32[]{:S(2)}, u32[]{:S(2)}) collective-permute-start(bf16[144,1024]{1,0:T(8,128)(2,1)S(1)} %collective-permute-done.2.refs_2_), channel_id=1, source_target_pairs={{0,4},{4,12},{12,8},{8,0},{1,5},{5,13},{13,9},{9,1},{2,6},{6,14},{... | collective-permute-start | bytes 884744 | tf_op jit(solution)/shard_map/ppermute | solution.py:315
  31.8 0.0 collective-permute-done.9.refs_1_
  31.8 2.0 %collective-permute-done.8.refs_0_ = bf16[128,1024]{1,0:T(8,128)(2,1)S(1)} collective-permute-done((bf16[128,1024]{1,0:T(8,128)(2,1)S(1)}, bf16[128,1024]{1,0:T(8,128)(2,1)S(1)}, u32[]{:S(2)}, u32[]{:S(2)}) %collective-permute-start.8) | collective-permute-done | bytes 262176 | tf_op jit(solution)/shard_map/ppermute | solution.py:315
  33.8 0.9 %collective-permute-start.12 = (bf16[128,1024]{1,0:T(8,128)(2,1)S(1)}, bf16[128,1024]{1,0:T(8,128)(2,1)S(1)}, u32[]{:S(2)}, u32[]{:S(2)}) collective-permute-start(bf16[128,1024]{1,0:T(8,128)(2,1)S(1)} %collective-permute-done.8.refs_0_), channel_id=1, source_target_pairs={{0,2},{2,0},{1,3},{3,1},{4,6},{6,4},{5,7},{7,5},{8,10},{10,8},{9,1... | collective-permute-start | bytes 786440 | tf_op jit(solution)/shard_map/ppermute | solution.py:284
  34.7 0.8 collective-permute-start.11
  35.5 3.7 %chunk.5 = (bf16[256,1024]{1,0:T(8,128)(2,1)S(1)}, bf16[4,96,1024]{2,1,0:T(8,128)(2,1)S(1)}, bf16[4,96,1024]{2,1,0:T(8,128)(2,1)S(1)}, bf16[4,96,768]{2,1,0:T(8,128)(2,1)S(1)}) custom-call(s32[1]{0:T(128)} %bitcast.first_ref, bf16[128,1024]{1,0:T(8,128)(2,1)S(1)} %collective-permute-done.4.refs_0_, bf16[128,1024]{1,0:T(8,128)(2,1)S(1)} %collective-permute-done.9.refs_1_, ...), custom_call_target="tpu_custom_call" | custom-call | flops 1610612736 | bytes 8388608 | tf_op jit(solution)/shard_map/chunk/pallas_call | solution.py:175
  39.2 0.0 collective-permute-done.7.refs_3_
  39.2 0.9 %collective-permute-done.6.refs_2_ = bf16[144,1024]{1,0:T(8,128)(2,1)S(1)} collective-permute-done((bf16[144,1024]{1,0:T(8,128)(2,1)S(1)}, bf16[144,1024]{1,0:T(8,128)(2,1)S(1)}, u32[]{:S(2)}, u32[]{:S(2)}) %collective-permute-start.6) | collective-permute-done | bytes 294944 | tf_op jit(solution)/shard_map/ppermute | solution.py:315
  40.1 0.9 %collective-permute-start.10 = (bf16[144,1024]{1,0:T(8,128)(2,1)S(1)}, bf16[144,1024]{1,0:T(8,128)(2,1)S(1)}, u32[]{:S(2)}, u32[]{:S(2)}) collective-permute-start(bf16[144,1024]{1,0:T(8,128)(2,1)S(1)} %collective-permute-done.6.refs_2_), channel_id=1, source_target_pairs={{0,2},{2,0},{1,3},{3,1},{4,6},{6,4},{5,7},{7,5},{8,10},{10,8},{9,1... | collective-permute-start | bytes 884744 | tf_op jit(solution)/shard_map/ppermute | solution.py:284
  41.1 2.7 %collective-permute-done.12.refs_1_ = bf16[128,1024]{1,0:T(8,128)(2,1)S(1)} collective-permute-done((bf16[128,1024]{1,0:T(8,128)(2,1)S(1)}, bf16[128,1024]{1,0:T(8,128)(2,1)S(1)}, u32[]{:S(2)}, u32[]{:S(2)}) %collective-permute-start.12) | collective-permute-done | bytes 262176 | tf_op jit(solution)/shard_map/ppermute | solution.py:284
  43.8 0.5 collective-permute-done.11.refs_0_
  44.3 1.6 %collective-permute-start.13 = (bf16[128,1024]{1,0:T(8,128)(2,1)S(1)}, bf16[128,1024]{1,0:T(8,128)(2,1)S(1)}, u32[]{:S(2)}, u32[]{:S(2)}) collective-permute-start(bf16[128,1024]{1,0:T(8,128)(2,1)S(1)} %collective-permute-done.12.refs_1_), channel_id=1, source_target_pairs={{0,4},{4,12},{12,8},{8,0},{1,5},{5,13},{13,9},{9,1},{2,6},{6,14},{... | collective-permute-start | bytes 786440 | tf_op jit(solution)/shard_map/ppermute | solution.py:311
  45.9 3.7 %chunk.6 = (bf16[128,1024]{1,0:T(8,128)(2,1)S(1)}, bf16[128,1024]{1,0:T(8,128)(2,1)S(1)}, bf16[4,96,1024]{2,1,0:T(8,128)(2,1)S(1)}, bf16[4,96,1024]{2,1,0:T(8,128)(2,1)S(1)}, bf16[4,96,768]{2,1,0:T(8,128)(2,1)S(1)}) custom-call(s32[1]{0:T(128)} %bitcast.first_ref, bf16[128,1024]{1,0:T(8,128)(2,1)S(1)} %collective-permute-done.8.refs_0_, ...), custom_call_target="tpu_custom_call" | custom-call | flops 1610612736 | bytes 8388608 | tf_op jit(solution)/shard_map/chunk/pallas_call | solution.py:175
  49.6 2.5 %collective-permute-done.13.refs_1_ = bf16[128,1024]{1,0:T(8,128)(2,1)S(1)} collective-permute-done((bf16[128,1024]{1,0:T(8,128)(2,1)S(1)}, bf16[128,1024]{1,0:T(8,128)(2,1)S(1)}, u32[]{:S(2)}, u32[]{:S(2)}) %collective-permute-start.13) | collective-permute-done | bytes 262176 | tf_op jit(solution)/shard_map/ppermute | solution.py:311
  52.0 0.0 collective-permute-done.10.refs_3_
  52.0 1.5 %collective-permute-start.15 = (bf16[256,1024]{1,0:T(8,128)(2,1)S(1)}, bf16[256,1024]{1,0:T(8,128)(2,1)S(1)}, u32[]{:S(2)}, u32[]{:S(2)}) collective-permute-start(bf16[256,1024]{1,0:T(8,128)(2,1)S(1)} %get-tuple-element.221), channel_id=1, source_target_pairs={{0,8},{4,0},{12,4},{8,12},{1,9},{5,1},{13,5},{9,13},{2,10},{6,2},{... | collective-permute-start | bytes 1572872 | tf_op jit(solution)/shard_map/ppermute | solution.py:301
  53.6 0.2 collective-permute-start.14
  53.8 3.7 %chunk.7 = (bf16[128,1024]{1,0:T(8,128)(2,1)S(1)}, bf16[128,1024]{1,0:T(8,128)(2,1)S(1)}, bf16[4,96,1024]{2,1,0:T(8,128)(2,1)S(1)}, bf16[4,96,1024]{2,1,0:T(8,128)(2,1)S(1)}, bf16[4,96,768]{2,1,0:T(8,128)(2,1)S(1)}) custom-call(s32[1]{0:T(128)} %bitcast.first_ref, bf16[128,1024]{1,0:T(8,128)(2,1)S(1)} %collective-permute-done.11.refs_0_, ...), custom_call_target="tpu_custom_call" | custom-call | flops 1610612736 | bytes 8388608 | tf_op jit(solution)/shard_map/chunk/pallas_call | solution.py:175
  57.5 1.9 %collective-permute-start.16 = (bf16[128,1024]{1,0:T(8,128)(2,1)S(1)}, bf16[128,1024]{1,0:T(8,128)(2,1)S(1)}, u32[]{:S(2)}, u32[]{:S(2)}) collective-permute-start(bf16[128,1024]{1,0:T(8,128)(2,1)S(1)} %get-tuple-element.217), channel_id=1, source_target_pairs={{0,2},{2,0},{1,3},{3,1},{4,6},{6,4},{5,7},{7,5},{8,10},{10,8},{9,1... | collective-permute-start | bytes 786440 | tf_op jit(solution)/shard_map/ppermute | solution.py:291
  59.3 3.0 %collective-permute-done.14 = bf16[128,1024]{1,0:T(8,128)(2,1)S(1)} collective-permute-done((bf16[128,1024]{1,0:T(8,128)(2,1)S(1)}, bf16[128,1024]{1,0:T(8,128)(2,1)S(1)}, u32[]{:S(2)}, u32[]{:S(2)}) %collective-permute-start.14) | collective-permute-done | bytes 262176 | tf_op jit(solution)/shard_map/ppermute | solution.py:291
  62.3 1.3 %collective-permute-done.15 = bf16[256,1024]{1,0:T(8,128)(2,1)S(1)} collective-permute-done((bf16[256,1024]{1,0:T(8,128)(2,1)S(1)}, bf16[256,1024]{1,0:T(8,128)(2,1)S(1)}, u32[]{:S(2)}, u32[]{:S(2)}) %collective-permute-start.15) | collective-permute-done | bytes 524320 | tf_op jit(solution)/shard_map/ppermute | solution.py:301
  63.6 0.1 add_convert_fusion.3
  63.7 2.6 %collective-permute-start.17 = (bf16[128,1024]{1,0:T(8,128)(2,1)S(1)}, bf16[128,1024]{1,0:T(8,128)(2,1)S(1)}, u32[]{:S(2)}, u32[]{:S(2)}) collective-permute-start(bf16[128,1024]{1,0:T(8,128)(2,1)S(1)} %add_convert_fusion.3), channel_id=1, source_target_pairs={{0,4},{4,12},{12,8},{8,0},{1,5},{5,13},{13,9},{9,1},{2,6},{6,14},{... | collective-permute-start | bytes 786440 | tf_op jit(solution)/shard_map/ppermute | solution.py:301
  66.2 1.9 %weight_grads.2 = bf16[4,768,512]{2,1,0:T(8,128)(2,1)S(1)} custom-call(s32[1]{0:T(128)S(6)} %sub.3.side_ref, bf16[4,96,1024]{2,1,0:T(8,128)(2,1)S(1)} %get-tuple-element.225.refs_0_, bf16[4,96,1024]{2,1,0:T(8,128)(2,1)S(1)} %get-tuple-element.226.refs_1_, bf16[4,96,1024]{2,1,0:T(8,128)(2,1)S(1)} %get-tuple-element.227.refs_2_, ...), custom_call_target="tpu_custom_call" | custom-call | flops 1207959552 | bytes 8650752 | tf_op jit(solution)/shard_map/weight_grads/pallas_call | solution.py:248
  68.1 0.1 add_convert_fusion.2
  68.2 0.0 collective-permute-done.16
  68.2 2.9 %collective-permute-done.17 = bf16[128,1024]{1,0:T(8,128)(2,1)S(1)} collective-permute-done((bf16[128,1024]{1,0:T(8,128)(2,1)S(1)}, bf16[128,1024]{1,0:T(8,128)(2,1)S(1)}, u32[]{:S(2)}, u32[]{:S(2)}) %collective-permute-start.17) | collective-permute-done | bytes 262176 | tf_op jit(solution)/shard_map/ppermute | solution.py:301
  71.1 0.0 collective-permute-start.18
  71.1 0.1 add_convert_fusion.1
  71.2 1.6 %collective-permute-start.19 = (bf16[128,1024]{1,0:T(8,128)(2,1)S(1)}, bf16[128,1024]{1,0:T(8,128)(2,1)S(1)}, u32[]{:S(2)}, u32[]{:S(2)}) collective-permute-start(bf16[128,1024]{1,0:T(8,128)(2,1)S(1)} %add_convert_fusion.1), channel_id=1, source_target_pairs={{0,4},{4,12},{12,8},{8,0},{1,5},{5,13},{13,9},{9,1},{2,6},{6,14},{... | collective-permute-start | bytes 786440 | tf_op jit(solution)/shard_map/ppermute | solution.py:301
  72.8 0.0 collective-permute-start.20
  72.8 3.9 %collective-permute-done.18.refs_12_ = bf16[4,768,512]{2,1,0:T(8,128)(2,1)S(1)} collective-permute-done((bf16[4,768,512]{2,1,0:T(8,128)(2,1)S(1)}, bf16[4,768,512]{2,1,0:T(8,128)(2,1)S(1)}, u32[]{:S(2)}, u32[]{:S(2)}) %collective-permute-start.18) | collective-permute-done | bytes 3145760 | tf_op jit(solution)/shard_map/ppermute | solution.py:337
  76.7 2.7 %weight_grads.3 = (bf16[4,512,256]{2,1,0:T(8,128)(2,1)}, bf16[4,512,256]{2,1,0:T(8,128)(2,1)}, bf16[4,256,512]{2,1,0:T(8,128)(2,1)}) custom-call(s32[1]{0:T(128)} %bitcast.1.side_ref, bf16[4,96,1024]{2,1,0:T(8,128)(2,1)S(1)} %get-tuple-element.225.refs_0_, bf16[4,96,1024]{2,1,0:T(8,128)(2,1)S(1)} %get-tuple-element.226.refs_1_, ...), custom_call_target="tpu_custom_call" | custom-call | flops 1207959552 | bytes 8650752 | tf_op jit(solution)/shard_map/weight_grads/pallas_call | solution.py:248
  79.4 1.4 %collective-permute-done.19 = bf16[128,1024]{1,0:T(8,128)(2,1)S(1)} collective-permute-done((bf16[128,1024]{1,0:T(8,128)(2,1)S(1)}, bf16[128,1024]{1,0:T(8,128)(2,1)S(1)}, u32[]{:S(2)}, u32[]{:S(2)}) %collective-permute-start.19) | collective-permute-done | bytes 262176 | tf_op jit(solution)/shard_map/ppermute | solution.py:301
  80.9 0.4 collective-permute-done.20
  81.2 0.9 %add_convert_fusion = bf16[128,1024]{1,0:T(8,128)(2,1)} fusion(bf16[128,1024]{1,0:T(8,128)(2,1)S(1)} %collective-permute-done.19, bf16[128,1024]{1,0:T(8,128)(2,1)S(1)} %collective-permute-done.20, bf16[128,1024]{1,0:T(8,128)(2,1)S(1)} %get-tuple-element.222, bf16[256,1024]{1,0:T(8,128)(2,1)S(1)} %collective-permute-done.15), kind=kLoop, calls=%fused_computation | loop fusion | flops 1048576 | bytes 1310720 | tf_op jit(solution)/shard_map/convert_element_type | solution.py:347
Async XLA Ops:
  2.4 10.8 %collective-permute-start.1 = (bf16[144,1024]{1,0:T(8,128)(2,1)S(1)}, bf16[144,1024]{1,0:T(8,128)(2,1)S(1)}, u32[]{:S(2)}, u32[]{:S(2)}) collective-permute-start(bf16[144,1024]{1,0:T(8,128)(2,1)S(1)} %get-tuple-element.139.refs_2_), channel_id=1, source_target_pairs={{0,2},{2,0},{1,3},{3,1},{4,6},{6,4},{5,7},{7,5},{8,10},{10,8},{9,1... | collective-permute-start | bytes 884744 | tf_op jit(solution)/shard_map/ppermute | solution.py:284
  5.4 10.8 %collective-permute-start = (bf16[144,1024]{1,0:T(8,128)(2,1)S(1)}, bf16[144,1024]{1,0:T(8,128)(2,1)S(1)}, u32[]{:S(2)}, u32[]{:S(2)}) collective-permute-start(bf16[144,1024]{1,0:T(8,128)(2,1)S(1)} %get-tuple-element.139.refs_2_), channel_id=1, source_target_pairs={{0,4},{4,12},{12,8},{8,0},{1,5},{5,13},{13,9},{9,1},{2,6},{6,14},{... | collective-permute-start | bytes 884744 | tf_op jit(solution)/shard_map/ppermute | solution.py:315
  7.0 11.9 %collective-permute-start.5 = (bf16[128,1024]{1,0:T(8,128)(2,1)}, bf16[128,1024]{1,0:T(8,128)(2,1)S(1)}, u32[]{:S(2)}, u32[]{:S(2)}) collective-permute-start(bf16[128,1024]{1,0:T(8,128)(2,1)} %tokens), channel_id=1, source_target_pairs={{0,2},{2,0},{1,3},{3,1},{4,6},{6,4},{5,7},{7,5},{8,10},{10,8},{9,1... | collective-permute-start | bytes 786440 | tf_op jit(solution)/shard_map/ppermute | solution.py:284
  7.5 14.3 %collective-permute-start.4 = (bf16[128,1024]{1,0:T(8,128)(2,1)}, bf16[128,1024]{1,0:T(8,128)(2,1)S(1)}, u32[]{:S(2)}, u32[]{:S(2)}) collective-permute-start(bf16[128,1024]{1,0:T(8,128)(2,1)} %tokens), channel_id=1, source_target_pairs={{0,4},{4,12},{12,8},{8,0},{1,5},{5,13},{13,9},{9,1},{2,6},{6,14},{... | collective-permute-start | bytes 786440 | tf_op jit(solution)/shard_map/ppermute | solution.py:315
  16.3 10.7 %collective-permute-start.3 = (bf16[144,1024]{1,0:T(8,128)(2,1)S(1)}, bf16[144,1024]{1,0:T(8,128)(2,1)S(1)}, u32[]{:S(2)}, u32[]{:S(2)}) collective-permute-start(bf16[144,1024]{1,0:T(8,128)(2,1)S(1)} %collective-permute-done.refs_2_), channel_id=1, source_target_pairs={{0,2},{2,0},{1,3},{3,1},{4,6},{6,4},{5,7},{7,5},{8,10},{10,8},{9,1... | collective-permute-start | bytes 884744 | tf_op jit(solution)/shard_map/ppermute | solution.py:284
  16.4 11.8 %collective-permute-start.2 = (bf16[144,1024]{1,0:T(8,128)(2,1)S(1)}, bf16[144,1024]{1,0:T(8,128)(2,1)S(1)}, u32[]{:S(2)}, u32[]{:S(2)}) collective-permute-start(bf16[144,1024]{1,0:T(8,128)(2,1)S(1)} %collective-permute-done.refs_2_), channel_id=1, source_target_pairs={{0,4},{4,12},{12,8},{8,0},{1,5},{5,13},{13,9},{9,1},{2,6},{6,14},{... | collective-permute-start | bytes 884744 | tf_op jit(solution)/shard_map/ppermute | solution.py:315
  21.9 10.0 %collective-permute-start.9 = (bf16[128,1024]{1,0:T(8,128)(2,1)S(1)}, bf16[128,1024]{1,0:T(8,128)(2,1)S(1)}, u32[]{:S(2)}, u32[]{:S(2)}) collective-permute-start(bf16[128,1024]{1,0:T(8,128)(2,1)S(1)} %collective-permute-done.4.refs_0_), channel_id=1, source_target_pairs={{0,2},{2,0},{1,3},{3,1},{4,6},{6,4},{5,7},{7,5},{8,10},{10,8},{9,1... | collective-permute-start | bytes 786440 | tf_op jit(solution)/shard_map/ppermute | solution.py:284
  22.0 11.8 %collective-permute-start.8 = (bf16[128,1024]{1,0:T(8,128)(2,1)S(1)}, bf16[128,1024]{1,0:T(8,128)(2,1)S(1)}, u32[]{:S(2)}, u32[]{:S(2)}) collective-permute-start(bf16[128,1024]{1,0:T(8,128)(2,1)S(1)} %collective-permute-done.4.refs_0_), channel_id=1, source_target_pairs={{0,4},{4,12},{12,8},{8,0},{1,5},{5,13},{13,9},{9,1},{2,6},{6,14},{... | collective-permute-start | bytes 786440 | tf_op jit(solution)/shard_map/ppermute | solution.py:315
  28.2 11.0 %collective-permute-start.7 = (bf16[144,1024]{1,0:T(8,128)(2,1)S(1)}, bf16[144,1024]{1,0:T(8,128)(2,1)S(1)}, u32[]{:S(2)}, u32[]{:S(2)}) collective-permute-start(bf16[144,1024]{1,0:T(8,128)(2,1)S(1)} %collective-permute-done.2.refs_2_), channel_id=1, source_target_pairs={{0,2},{2,0},{1,3},{3,1},{4,6},{6,4},{5,7},{7,5},{8,10},{10,8},{9,1... | collective-permute-start | bytes 884744 | tf_op jit(solution)/shard_map/ppermute | solution.py:284
  29.1 11.0 %collective-permute-start.6 = (bf16[144,1024]{1,0:T(8,128)(2,1)S(1)}, bf16[144,1024]{1,0:T(8,128)(2,1)S(1)}, u32[]{:S(2)}, u32[]{:S(2)}) collective-permute-start(bf16[144,1024]{1,0:T(8,128)(2,1)S(1)} %collective-permute-done.2.refs_2_), channel_id=1, source_target_pairs={{0,4},{4,12},{12,8},{8,0},{1,5},{5,13},{13,9},{9,1},{2,6},{6,14},{... | collective-permute-start | bytes 884744 | tf_op jit(solution)/shard_map/ppermute | solution.py:315
  33.8 9.9 %collective-permute-start.12 = (bf16[128,1024]{1,0:T(8,128)(2,1)S(1)}, bf16[128,1024]{1,0:T(8,128)(2,1)S(1)}, u32[]{:S(2)}, u32[]{:S(2)}) collective-permute-start(bf16[128,1024]{1,0:T(8,128)(2,1)S(1)} %collective-permute-done.8.refs_0_), channel_id=1, source_target_pairs={{0,2},{2,0},{1,3},{3,1},{4,6},{6,4},{5,7},{7,5},{8,10},{10,8},{9,1... | collective-permute-start | bytes 786440 | tf_op jit(solution)/shard_map/ppermute | solution.py:284
  34.7 9.5 %collective-permute-start.11 = (bf16[128,1024]{1,0:T(8,128)(2,1)S(1)}, bf16[128,1024]{1,0:T(8,128)(2,1)S(1)}, u32[]{:S(2)}, u32[]{:S(2)}) collective-permute-start(bf16[128,1024]{1,0:T(8,128)(2,1)S(1)} %collective-permute-done.8.refs_0_), channel_id=1, source_target_pairs={{0,4},{4,12},{12,8},{8,0},{1,5},{5,13},{13,9},{9,1},{2,6},{6,14},{... | collective-permute-start | bytes 786440 | tf_op jit(solution)/shard_map/ppermute | solution.py:315
  40.1 11.9 %collective-permute-start.10 = (bf16[144,1024]{1,0:T(8,128)(2,1)S(1)}, bf16[144,1024]{1,0:T(8,128)(2,1)S(1)}, u32[]{:S(2)}, u32[]{:S(2)}) collective-permute-start(bf16[144,1024]{1,0:T(8,128)(2,1)S(1)} %collective-permute-done.6.refs_2_), channel_id=1, source_target_pairs={{0,2},{2,0},{1,3},{3,1},{4,6},{6,4},{5,7},{7,5},{8,10},{10,8},{9,1... | collective-permute-start | bytes 884744 | tf_op jit(solution)/shard_map/ppermute | solution.py:284
  44.3 7.8 %collective-permute-start.13 = (bf16[128,1024]{1,0:T(8,128)(2,1)S(1)}, bf16[128,1024]{1,0:T(8,128)(2,1)S(1)}, u32[]{:S(2)}, u32[]{:S(2)}) collective-permute-start(bf16[128,1024]{1,0:T(8,128)(2,1)S(1)} %collective-permute-done.12.refs_1_), channel_id=1, source_target_pairs={{0,4},{4,12},{12,8},{8,0},{1,5},{5,13},{13,9},{9,1},{2,6},{6,14},{... | collective-permute-start | bytes 786440 | tf_op jit(solution)/shard_map/ppermute | solution.py:311
  52.0 11.6 %collective-permute-start.15 = (bf16[256,1024]{1,0:T(8,128)(2,1)S(1)}, bf16[256,1024]{1,0:T(8,128)(2,1)S(1)}, u32[]{:S(2)}, u32[]{:S(2)}) collective-permute-start(bf16[256,1024]{1,0:T(8,128)(2,1)S(1)} %get-tuple-element.221), channel_id=1, source_target_pairs={{0,8},{4,0},{12,4},{8,12},{1,9},{5,1},{13,5},{9,13},{2,10},{6,2},{... | collective-permute-start | bytes 1572872 | tf_op jit(solution)/shard_map/ppermute | solution.py:301
  53.6 8.7 %collective-permute-start.14 = (bf16[128,1024]{1,0:T(8,128)(2,1)S(1)}, bf16[128,1024]{1,0:T(8,128)(2,1)S(1)}, u32[]{:S(2)}, u32[]{:S(2)}) collective-permute-start(bf16[128,1024]{1,0:T(8,128)(2,1)S(1)} %get-tuple-element.200), channel_id=1, source_target_pairs={{0,2},{2,0},{1,3},{3,1},{4,6},{6,4},{5,7},{7,5},{8,10},{10,8},{9,1... | collective-permute-start | bytes 786440 | tf_op jit(solution)/shard_map/ppermute | solution.py:291
  57.5 10.7 %collective-permute-start.16 = (bf16[128,1024]{1,0:T(8,128)(2,1)S(1)}, bf16[128,1024]{1,0:T(8,128)(2,1)S(1)}, u32[]{:S(2)}, u32[]{:S(2)}) collective-permute-start(bf16[128,1024]{1,0:T(8,128)(2,1)S(1)} %get-tuple-element.217), channel_id=1, source_target_pairs={{0,2},{2,0},{1,3},{3,1},{4,6},{6,4},{5,7},{7,5},{8,10},{10,8},{9,1... | collective-permute-start | bytes 786440 | tf_op jit(solution)/shard_map/ppermute | solution.py:291
  63.7 7.4 %collective-permute-start.17 = (bf16[128,1024]{1,0:T(8,128)(2,1)S(1)}, bf16[128,1024]{1,0:T(8,128)(2,1)S(1)}, u32[]{:S(2)}, u32[]{:S(2)}) collective-permute-start(bf16[128,1024]{1,0:T(8,128)(2,1)S(1)} %add_convert_fusion.3), channel_id=1, source_target_pairs={{0,4},{4,12},{12,8},{8,0},{1,5},{5,13},{13,9},{9,1},{2,6},{6,14},{... | collective-permute-start | bytes 786440 | tf_op jit(solution)/shard_map/ppermute | solution.py:301
  71.1 5.7 %collective-permute-start.18 = (bf16[4,768,512]{2,1,0:T(8,128)(2,1)S(1)}, bf16[4,768,512]{2,1,0:T(8,128)(2,1)S(1)}, u32[]{:S(2)}, u32[]{:S(2)}) collective-permute-start(bf16[4,768,512]{2,1,0:T(8,128)(2,1)S(1)} %weight_grads.2), channel_id=1, source_target_pairs={{0,1},{1,0},{2,3},{3,2},{4,5},{5,4},{6,7},{7,6},{8,9},{9,8},{10,11... | collective-permute-start | bytes 9437192 | tf_op jit(solution)/shard_map/ppermute | solution.py:337
  71.2 9.7 %collective-permute-start.19 = (bf16[128,1024]{1,0:T(8,128)(2,1)S(1)}, bf16[128,1024]{1,0:T(8,128)(2,1)S(1)}, u32[]{:S(2)}, u32[]{:S(2)}) collective-permute-start(bf16[128,1024]{1,0:T(8,128)(2,1)S(1)} %add_convert_fusion.1), channel_id=1, source_target_pairs={{0,4},{4,12},{12,8},{8,0},{1,5},{5,13},{13,9},{9,1},{2,6},{6,14},{... | collective-permute-start | bytes 786440 | tf_op jit(solution)/shard_map/ppermute | solution.py:301
  72.8 8.4 %collective-permute-start.20 = (bf16[128,1024]{1,0:T(8,128)(2,1)S(1)}, bf16[128,1024]{1,0:T(8,128)(2,1)S(1)}, u32[]{:S(2)}, u32[]{:S(2)}) collective-permute-start(bf16[128,1024]{1,0:T(8,128)(2,1)S(1)} %add_convert_fusion.2), channel_id=1, source_target_pairs={{0,2},{2,0},{1,3},{3,1},{4,6},{6,4},{5,7},{7,5},{8,10},{10,8},{9,1... | collective-permute-start | bytes 786440 | tf_op jit(solution)/shard_map/ppermute | solution.py:291

commit v15 on v13

--- a/solution.py
+++ b/solution.py
@@ -306,37 +306,40 @@
     blocks, chunks, backs, sent = {}, {}, {}, {}
     last = n_group - 1
     for k in range(n_group):
-        pair = [spread(tokens), spread(upstream) if k < last else [upstream]]
+        pair = [spread(tokens) if k < last else [tokens], spread(upstream)]
         if k == last:
-            pair[1] += [lax.ppermute(block, "group", along(1)) for block in blocks[k - 1][1][1:]]
+            other, *held = tie(chunks[1][1], *blocks[k - 1][0])
+            backs[1] = across(other)
+            blocks[k - 1][0] = held
+            pair[0] += [lax.ppermute(block, "group", along(1)) for block in held[1:]]
         if k == 0:
             pair[0][0] = first_tokens
         if k < last:
             tokens, upstream = (lax.ppermute(v, "group", along(1)) for v in (tokens, upstream))
         if k > 0:
             chunks[k - 1] = chunk(blocks[k - 1])
+        if k == last:
+            backs[k - 1] = across(chunks[k - 1][1])
+            backs[1], chunks = tie(backs[1], chunks)
         upstream, pair[1], chunks, weights = tie(upstream, pair[1], chunks, weights)
         tokens, pair[0] = tie(tokens, pair[0])
         blocks[k] = pair
 
     for k in range(2, last - 1):
         sent[k] = homeward(group_sum(chunks[k][0], across(chunks[k][1])), k)
-    backs[1] = across(chunks[1][1])
-    backs[last - 1] = across(chunks[last - 1][1])
     chunks[last] = chunk(blocks[last])
-    chunks, backs[1] = tie(chunks, backs[1])
-
     backs[last] = across(chunks[last][1])
     sent[1] = homeward(group_sum(chunks[1][0], backs[1]), 1)
+    chunks, backs[last - 1] = tie(chunks, backs[last - 1])
+
     carried = homeward(group_sum(chunks[last - 1][0], backs[last - 1]), last)
     kept = [[chunks[k][i] for k in range(n_group)] for i in (-3, -2, -1)]
-    kept, backs[last - 1] = tie(kept, backs[last - 1])
     to_send = weight_call(other_half, *kept)
+    to_send, backs[last], carried, other, sent = tie(to_send, backs[last], carried, chunks[0][1], sent)
+
     got = lax.ppermute(to_send, "dp", [(0, 1), (1, 0)])
-    other, to_send = tie(chunks[0][1], to_send)
+    sent[last] = homeward(group_sum(chunks[last][0], [*backs[last], carried]), last)
     backs[0] = across(other)
-    sent[last] = homeward(group_sum(chunks[last][0], [*backs[last], carried]), last)
-    got, carried, backs[last] = tie(got, carried, backs[last])
     grads = weight_call(half, *kept, got)
     grads, sent, backs[0] = tie(grads, sent, backs[0])
     total = wide(chunks[0][0])

time: 88.1 us -> 81.2 us (0.922); the launches traced: 86.9 us -> 81 us
  starting transfers between devices: 36.4 us -> 26.6 us
  waiting for transfers between devices: 24.7 us -> 28.6 us
    ppermute x6, waiting for transfers between devices: 5.2 us -> 10.6 us  [per_device(): lax.ppermute(v, 'group', along(1))]
    ppermute x3, starting transfers between devices: 8.07 us -> 3.28 us  [homeward(): return lax.ppermute(group_part, 'group', along(-k))]
    ppermute x4, waiting for transfers between devices: 7.83 us -> 3.66 us  [across(): lax.ppermute(others[(s - 1) * tok_rows:s * tok_rows], 'ingroup', shift(-s))]
    ppermute x6, starting transfers between devices: 14 us -> 10.1 us  [per_device(): lax.ppermute(v, 'group', along(1))]
    ppermute x1, waiting for transfers between devices: 0.01 us -> 3.4 us  [per_device(): got = lax.ppermute(to_send, 'dp', [(0, 1), (1, 0)])]
    ppermute x7, starting transfers between devices: 9.07 us -> 6.68 us  [spread(): lax.ppermute(column, 'ingroup', shift(s))]
    ppermute x3, waiting for transfers between devices: 7.43 us -> 6.34 us  [homeward(): return lax.ppermute(group_part, 'group', along(-k))]
  transfers between devices with their start and end apart: 22 -> 22, of which waited for: 13 -> 14; matrix products, arithmetic and copies ran while one was open for 0% -> 0% of each run, Pallas kernels for 23% -> 27%
where the time goes in v15:
time: 81.2 us; the launch traced here: 81 us
  waiting for transfers between devices  28.6 us (35%)
  starting transfers between devices  26.6 us (33%)
  Pallas kernels  23.9 us (29%)
  other arithmetic  1.13 us (1%)
    pallas_call x4, Pallas kernels, chunk_call(): pl.pallas_call(functools.partial(chunk_kernel, n_blocks, tok_rows, capaci...  14.7 us
    ppermute x6, waiting for transfers between devices, per_device(): lax.ppermute(v, 'group', along(1))  10.6 us
    ppermute x6, starting transfers between devices, per_device(): lax.ppermute(v, 'group', along(1))  10.1 us
    ppermute x7, starting transfers between devices, spread(): lax.ppermute(column, 'ingroup', shift(s))  6.68 us
    ppermute x3, waiting for transfers between devices, homeward(): return lax.ppermute(group_part, 'group', along(-k))  6.34 us
    ppermute x4, starting transfers between devices, across(): lax.ppermute(others[(s - 1) * tok_rows:s * tok_rows], 'ingroup', shift(-s))  4.94 us
    pallas_call x2, Pallas kernels, weight_call(): pl.pallas_call(functools.partial(kernel, n), in_specs=[smem] + [vmem] * l...  4.57 us
    ppermute x7, waiting for transfers between devices, spread(): lax.ppermute(column, 'ingroup', shift(s))  4.24 us
  transfers between devices with their start and end apart: 22, of which 14 were waited for; matrix products, arithmetic and copies ran while one was open for 0% of the time, Pallas kernels for 27%

profile of v15, /device:TPU:0, one launch (start us, length us, event | category | flops | bytes accessed | tf_op | source)
XLA Modules:
  0.0 81.0 jit_solution(557780258799294326)
XLA Ops:
  0.6 1.8 %pack.1 = (bf16[128,1024]{1,0:T(8,128)(2,1)S(1)}, bf16[144,1024]{1,0:T(8,128)(2,1)S(1)}) custom-call(bf16[128,1024]{1,0:T(8,128)(2,1)} %tokens, bf16[128,1024]{1,0:T(8,128)(2,1)} %upstream.1, s32[8,128]{1,0:T(8,128)} %bitcast.5, s32[8,128]{1,0:T(8,128)} %bitcast.6, s32[8,128]{1,0:T(8,128)} %bitcast.7), custom_call_target="tpu_custom_call" | custom-call | bytes 1048576 | tf_op jit(solution)/shard_map/pack/pallas_call | solution.py:58
  2.4 3.0 %collective-permute-start.1 = (bf16[144,1024]{1,0:T(8,128)(2,1)S(1)}, bf16[144,1024]{1,0:T(8,128)(2,1)S(1)}, u32[]{:S(2)}, u32[]{:S(2)}) collective-permute-start(bf16[144,1024]{1,0:T(8,128)(2,1)S(1)} %get-tuple-element.153.refs_2_), channel_id=1, source_target_pairs={{0,2},{2,0},{1,3},{3,1},{4,6},{6,4},{5,7},{7,5},{8,10},{10,8},{9,1... | collective-permute-start | bytes 884744 | tf_op jit(solution)/shard_map/ppermute | solution.py:284
  5.4 1.6 %collective-permute-start = (bf16[144,1024]{1,0:T(8,128)(2,1)S(1)}, bf16[144,1024]{1,0:T(8,128)(2,1)S(1)}, u32[]{:S(2)}, u32[]{:S(2)}) collective-permute-start(bf16[144,1024]{1,0:T(8,128)(2,1)S(1)} %get-tuple-element.153.refs_2_), channel_id=1, source_target_pairs={{0,4},{4,12},{12,8},{8,0},{1,5},{5,13},{13,9},{9,1},{2,6},{6,14},{... | collective-permute-start | bytes 884744 | tf_op jit(solution)/shard_map/ppermute | solution.py:318
  7.0 0.5 collective-permute-start.5
  7.5 2.6 %collective-permute-start.4 = (bf16[128,1024]{1,0:T(8,128)(2,1)}, bf16[128,1024]{1,0:T(8,128)(2,1)S(1)}, u32[]{:S(2)}, u32[]{:S(2)}) collective-permute-start(bf16[128,1024]{1,0:T(8,128)(2,1)} %tokens), channel_id=1, source_target_pairs={{0,4},{4,12},{12,8},{8,0},{1,5},{5,13},{13,9},{9,1},{2,6},{6,14},{... | collective-permute-start | bytes 786440 | tf_op jit(solution)/shard_map/ppermute | solution.py:318
  10.1 2.9 %load.1 = (bf16[4,1024,256]{2,1,0:T(8,128)(2,1)S(1)}, bf16[4,1024,256]{2,1,0:T(8,128)(2,1)S(1)}, bf16[4,256,1024]{2,1,0:T(8,128)(2,1)S(1)}) custom-call(bf16[4,1024,256]{2,1,0:T(8,128)(2,1)} %refs_0_.1, bf16[4,1024,256]{2,1,0:T(8,128)(2,1)} %refs_1_.1, bf16[4,256,1024]{2,1,0:T(8,128)(2,1)} %refs_2_.1), custom_call_target="tpu_custom_call" | custom-call | bytes 12582912 | tf_op jit(solution)/shard_map/load/pallas_call | solution.py:99
  13.0 0.2 collective-permute-done.1.refs_3_
  13.3 3.0 %collective-permute-done.refs_2_ = bf16[144,1024]{1,0:T(8,128)(2,1)S(1)} collective-permute-done((bf16[144,1024]{1,0:T(8,128)(2,1)S(1)}, bf16[144,1024]{1,0:T(8,128)(2,1)S(1)}, u32[]{:S(2)}, u32[]{:S(2)}) %collective-permute-start) | collective-permute-done | bytes 294944 | tf_op jit(solution)/shard_map/ppermute | solution.py:318
  16.3 0.2 collective-permute-start.3
  16.4 1.2 %collective-permute-start.2 = (bf16[144,1024]{1,0:T(8,128)(2,1)S(1)}, bf16[144,1024]{1,0:T(8,128)(2,1)S(1)}, u32[]{:S(2)}, u32[]{:S(2)}) collective-permute-start(bf16[144,1024]{1,0:T(8,128)(2,1)S(1)} %collective-permute-done.refs_2_), channel_id=1, source_target_pairs={{0,4},{4,12},{12,8},{8,0},{1,5},{5,13},{13,9},{9,1},{2,6},{6,14},{... | collective-permute-start | bytes 884744 | tf_op jit(solution)/shard_map/ppermute | solution.py:318
  17.6 1.3 %collective-permute-done.5.refs_1_ = bf16[128,1024]{1,0:T(8,128)(2,1)S(1)} collective-permute-done((bf16[128,1024]{1,0:T(8,128)(2,1)}, bf16[128,1024]{1,0:T(8,128)(2,1)S(1)}, u32[]{:S(2)}, u32[]{:S(2)}) %collective-permute-start.5) | collective-permute-done | bytes 262176 | tf_op jit(solution)/shard_map/ppermute | solution.py:284
  18.9 3.0 %collective-permute-done.4.refs_0_ = bf16[128,1024]{1,0:T(8,128)(2,1)S(1)} collective-permute-done((bf16[128,1024]{1,0:T(8,128)(2,1)}, bf16[128,1024]{1,0:T(8,128)(2,1)S(1)}, u32[]{:S(2)}, u32[]{:S(2)}) %collective-permute-start.4) | collective-permute-done | bytes 262176 | tf_op jit(solution)/shard_map/ppermute | solution.py:318
  21.9 0.2 collective-permute-start.9
  22.0 1.3 %collective-permute-start.8 = (bf16[128,1024]{1,0:T(8,128)(2,1)S(1)}, bf16[128,1024]{1,0:T(8,128)(2,1)S(1)}, u32[]{:S(2)}, u32[]{:S(2)}) collective-permute-start(bf16[128,1024]{1,0:T(8,128)(2,1)S(1)} %collective-permute-done.4.refs_0_), channel_id=1, source_target_pairs={{0,4},{4,12},{12,8},{8,0},{1,5},{5,13},{13,9},{9,1},{2,6},{6,14},{... | collective-permute-start | bytes 786440 | tf_op jit(solution)/shard_map/ppermute | solution.py:318
  23.3 3.7 %chunk.4 = (bf16[128,1024]{1,0:T(8,128)(2,1)S(1)}, bf16[128,1024]{1,0:T(8,128)(2,1)S(1)}, bf16[4,96,1024]{2,1,0:T(8,128)(2,1)S(1)}, bf16[4,96,1024]{2,1,0:T(8,128)(2,1)S(1)}, bf16[4,96,768]{2,1,0:T(8,128)(2,1)S(1)}) custom-call(s32[1]{0:T(128)} %bitcast.first_ref, bf16[128,1024]{1,0:T(8,128)(2,1)S(1)} %get-tuple-element.151.refs_0_, ...), custom_call_target="tpu_custom_call" | custom-call | flops 1610612736 | bytes 8388608 | tf_op jit(solution)/shard_map/chunk/pallas_call | solution.py:175
  27.0 0.0 collective-permute-done.3.refs_3_
  27.0 1.2 %collective-permute-done.2.refs_2_ = bf16[144,1024]{1,0:T(8,128)(2,1)S(1)} collective-permute-done((bf16[144,1024]{1,0:T(8,128)(2,1)S(1)}, bf16[144,1024]{1,0:T(8,128)(2,1)S(1)}, u32[]{:S(2)}, u32[]{:S(2)}) %collective-permute-start.2) | collective-permute-done | bytes 294944 | tf_op jit(solution)/shard_map/ppermute | solution.py:318
  28.2 0.9 %collective-permute-start.7 = (bf16[144,1024]{1,0:T(8,128)(2,1)S(1)}, bf16[144,1024]{1,0:T(8,128)(2,1)S(1)}, u32[]{:S(2)}, u32[]{:S(2)}) collective-permute-start(bf16[144,1024]{1,0:T(8,128)(2,1)S(1)} %collective-permute-done.2.refs_2_), channel_id=1, source_target_pairs={{0,2},{2,0},{1,3},{3,1},{4,6},{6,4},{5,7},{7,5},{8,10},{10,8},{9,1... | collective-permute-start | bytes 884744 | tf_op jit(solution)/shard_map/ppermute | solution.py:284
  29.1 2.7 %collective-permute-start.6 = (bf16[144,1024]{1,0:T(8,128)(2,1)S(1)}, bf16[144,1024]{1,0:T(8,128)(2,1)S(1)}, u32[]{:S(2)}, u32[]{:S(2)}) collective-permute-start(bf16[144,1024]{1,0:T(8,128)(2,1)S(1)} %collective-permute-done.2.refs_2_), channel_id=1, source_target_pairs={{0,4},{4,12},{12,8},{8,0},{1,5},{5,13},{13,9},{9,1},{2,6},{6,14},{... | collective-permute-start | bytes 884744 | tf_op jit(solution)/shard_map/ppermute | solution.py:318
  31.8 0.0 collective-permute-done.9.refs_1_
  31.8 2.0 %collective-permute-done.8.refs_0_ = bf16[128,1024]{1,0:T(8,128)(2,1)S(1)} collective-permute-done((bf16[128,1024]{1,0:T(8,128)(2,1)S(1)}, bf16[128,1024]{1,0:T(8,128)(2,1)S(1)}, u32[]{:S(2)}, u32[]{:S(2)}) %collective-permute-start.8) | collective-permute-done | bytes 262176 | tf_op jit(solution)/shard_map/ppermute | solution.py:318
  33.8 0.9 %collective-permute-start.12 = (bf16[128,1024]{1,0:T(8,128)(2,1)S(1)}, bf16[128,1024]{1,0:T(8,128)(2,1)S(1)}, u32[]{:S(2)}, u32[]{:S(2)}) collective-permute-start(bf16[128,1024]{1,0:T(8,128)(2,1)S(1)} %collective-permute-done.8.refs_0_), channel_id=1, source_target_pairs={{0,2},{2,0},{1,3},{3,1},{4,6},{6,4},{5,7},{7,5},{8,10},{10,8},{9,1... | collective-permute-start | bytes 786440 | tf_op jit(solution)/shard_map/ppermute | solution.py:284
  34.7 0.8 collective-permute-start.11
  35.5 3.7 %chunk.5 = (bf16[128,1024]{1,0:T(8,128)(2,1)S(1)}, bf16[128,1024]{1,0:T(8,128)(2,1)S(1)}, bf16[4,96,1024]{2,1,0:T(8,128)(2,1)S(1)}, bf16[4,96,1024]{2,1,0:T(8,128)(2,1)S(1)}, bf16[4,96,768]{2,1,0:T(8,128)(2,1)S(1)}) custom-call(s32[1]{0:T(128)} %bitcast.first_ref, bf16[128,1024]{1,0:T(8,128)(2,1)S(1)} %collective-permute-done.4.refs_0_, ...), custom_call_target="tpu_custom_call" | custom-call | flops 1610612736 | bytes 8388608 | tf_op jit(solution)/shard_map/chunk/pallas_call | solution.py:175
  39.2 0.0 collective-permute-done.7.refs_3_
  39.2 0.9 %collective-permute-done.6.refs_2_ = bf16[144,1024]{1,0:T(8,128)(2,1)S(1)} collective-permute-done((bf16[144,1024]{1,0:T(8,128)(2,1)S(1)}, bf16[144,1024]{1,0:T(8,128)(2,1)S(1)}, u32[]{:S(2)}, u32[]{:S(2)}) %collective-permute-start.6) | collective-permute-done | bytes 294944 | tf_op jit(solution)/shard_map/ppermute | solution.py:318
  40.1 0.9 %collective-permute-start.10 = (bf16[144,1024]{1,0:T(8,128)(2,1)S(1)}, bf16[144,1024]{1,0:T(8,128)(2,1)S(1)}, u32[]{:S(2)}, u32[]{:S(2)}) collective-permute-start(bf16[144,1024]{1,0:T(8,128)(2,1)S(1)} %collective-permute-done.6.refs_2_), channel_id=1, source_target_pairs={{0,2},{2,0},{1,3},{3,1},{4,6},{6,4},{5,7},{7,5},{8,10},{10,8},{9,1... | collective-permute-start | bytes 884744 | tf_op jit(solution)/shard_map/ppermute | solution.py:284
  41.1 2.7 %collective-permute-done.12.refs_1_ = bf16[128,1024]{1,0:T(8,128)(2,1)S(1)} collective-permute-done((bf16[128,1024]{1,0:T(8,128)(2,1)S(1)}, bf16[128,1024]{1,0:T(8,128)(2,1)S(1)}, u32[]{:S(2)}, u32[]{:S(2)}) %collective-permute-start.12) | collective-permute-done | bytes 262176 | tf_op jit(solution)/shard_map/ppermute | solution.py:284
  43.8 0.5 collective-permute-done.11.refs_0_
  44.3 1.6 %collective-permute-start.14 = (bf16[128,1024]{1,0:T(8,128)(2,1)S(1)}, bf16[128,1024]{1,0:T(8,128)(2,1)S(1)}, u32[]{:S(2)}, u32[]{:S(2)}) collective-permute-start(bf16[128,1024]{1,0:T(8,128)(2,1)S(1)} %collective-permute-done.12.refs_1_), channel_id=1, source_target_pairs={{0,4},{4,12},{12,8},{8,0},{1,5},{5,13},{13,9},{9,1},{2,6},{6,14},{... | collective-permute-start | bytes 786440 | tf_op jit(solution)/shard_map/ppermute | solution.py:314
  45.9 1.5 %collective-permute-start.13 = (bf16[128,1024]{1,0:T(8,128)(2,1)S(1)}, bf16[128,1024]{1,0:T(8,128)(2,1)S(1)}, u32[]{:S(2)}, u32[]{:S(2)}) collective-permute-start(bf16[128,1024]{1,0:T(8,128)(2,1)S(1)} %get-tuple-element.187), channel_id=1, source_target_pairs={{0,2},{2,0},{1,3},{3,1},{4,6},{6,4},{5,7},{7,5},{8,10},{10,8},{9,1... | collective-permute-start | bytes 786440 | tf_op jit(solution)/shard_map/ppermute | solution.py:291
  47.4 3.7 %chunk.6 = (bf16[128,1024]{1,0:T(8,128)(2,1)S(1)}, bf16[128,1024]{1,0:T(8,128)(2,1)S(1)}, bf16[4,96,1024]{2,1,0:T(8,128)(2,1)S(1)}, bf16[4,96,1024]{2,1,0:T(8,128)(2,1)S(1)}, bf16[4,96,768]{2,1,0:T(8,128)(2,1)S(1)}) custom-call(s32[1]{0:T(128)} %bitcast.first_ref, bf16[128,1024]{1,0:T(8,128)(2,1)S(1)} %collective-permute-done.8.refs_0_, ...), custom_call_target="tpu_custom_call" | custom-call | flops 1610612736 | bytes 8388608 | tf_op jit(solution)/shard_map/chunk/pallas_call | solution.py:175
  51.1 0.6 collective-permute-start.15
  51.7 0.3 collective-permute-done.14.refs_1_
  52.0 3.7 %collective-permute-done.13 = bf16[128,1024]{1,0:T(8,128)(2,1)S(1)} collective-permute-done((bf16[128,1024]{1,0:T(8,128)(2,1)S(1)}, bf16[128,1024]{1,0:T(8,128)(2,1)S(1)}, u32[]{:S(2)}, u32[]{:S(2)}) %collective-permute-start.13) | collective-permute-done | bytes 262176 | tf_op jit(solution)/shard_map/ppermute | solution.py:291
  55.7 0.0 collective-permute-done.10.refs_3_
  55.7 0.1 add_convert_fusion.2
  55.8 2.4 %collective-permute-start.18 = (bf16[128,1024]{1,0:T(8,128)(2,1)S(1)}, bf16[128,1024]{1,0:T(8,128)(2,1)S(1)}, u32[]{:S(2)}, u32[]{:S(2)}) collective-permute-start(bf16[128,1024]{1,0:T(8,128)(2,1)S(1)} %add_convert_fusion.2), channel_id=1, source_target_pairs={{0,8},{4,0},{12,4},{8,12},{1,9},{5,1},{13,5},{9,13},{2,10},{6,2},{... | collective-permute-start | bytes 786440 | tf_op jit(solution)/shard_map/ppermute | solution.py:301
  58.2 3.7 %chunk.7 = (bf16[128,1024]{1,0:T(8,128)(2,1)S(1)}, bf16[128,1024]{1,0:T(8,128)(2,1)S(1)}, bf16[4,96,1024]{2,1,0:T(8,128)(2,1)S(1)}, bf16[4,96,1024]{2,1,0:T(8,128)(2,1)S(1)}, bf16[4,96,768]{2,1,0:T(8,128)(2,1)S(1)}) custom-call(s32[1]{0:T(128)} %bitcast.first_ref, bf16[128,1024]{1,0:T(8,128)(2,1)S(1)} %collective-permute-done.11.refs_0_, ...), custom_call_target="tpu_custom_call" | custom-call | flops 1610612736 | bytes 8388608 | tf_op jit(solution)/shard_map/chunk/pallas_call | solution.py:175
  61.8 0.0 collective-permute-done.15
  61.8 0.1 add_convert_fusion.3
  61.9 0.1 collective-permute-start.17
  62.0 1.6 %collective-permute-start.16 = (bf16[128,1024]{1,0:T(8,128)(2,1)S(1)}, bf16[128,1024]{1,0:T(8,128)(2,1)S(1)}, u32[]{:S(2)}, u32[]{:S(2)}) collective-permute-start(bf16[128,1024]{1,0:T(8,128)(2,1)S(1)} %get-tuple-element.244), channel_id=1, source_target_pairs={{0,2},{2,0},{1,3},{3,1},{4,6},{6,4},{5,7},{7,5},{8,10},{10,8},{9,1... | collective-permute-start | bytes 786440 | tf_op jit(solution)/shard_map/ppermute | solution.py:291
  63.5 1.9 %weight_grads.2 = bf16[4,768,512]{2,1,0:T(8,128)(2,1)S(1)} custom-call(s32[1]{0:T(128)S(6)} %sub.3.side_ref, bf16[4,96,1024]{2,1,0:T(8,128)(2,1)S(1)} %get-tuple-element.250.refs_0_, bf16[4,96,1024]{2,1,0:T(8,128)(2,1)S(1)} %get-tuple-element.251.refs_1_, bf16[4,96,1024]{2,1,0:T(8,128)(2,1)S(1)} %get-tuple-element.252.refs_2_, ...), custom_call_target="tpu_custom_call" | custom-call | flops 1207959552 | bytes 8650752 | tf_op jit(solution)/shard_map/weight_grads/pallas_call | solution.py:248
  65.4 0.0 collective-permute-done.18
  65.4 4.9 %collective-permute-done.17 = bf16[128,1024]{1,0:T(8,128)(2,1)S(1)} collective-permute-done((bf16[128,1024]{1,0:T(8,128)(2,1)S(1)}, bf16[128,1024]{1,0:T(8,128)(2,1)S(1)}, u32[]{:S(2)}, u32[]{:S(2)}) %collective-permute-start.17) | collective-permute-done | bytes 262176 | tf_op jit(solution)/shard_map/ppermute | solution.py:301
  70.3 0.0 collective-permute-done.16
  70.3 0.0 collective-permute-start.19
  70.3 0.1 add_convert_fusion.1
  70.5 0.8 %collective-permute-start.20 = (bf16[128,1024]{1,0:T(8,128)(2,1)S(1)}, bf16[128,1024]{1,0:T(8,128)(2,1)S(1)}, u32[]{:S(2)}, u32[]{:S(2)}) collective-permute-start(bf16[128,1024]{1,0:T(8,128)(2,1)S(1)} %add_convert_fusion.1), channel_id=1, source_target_pairs={{0,4},{4,12},{12,8},{8,0},{1,5},{5,13},{13,9},{9,1},{2,6},{6,14},{... | collective-permute-start | bytes 786440 | tf_op jit(solution)/shard_map/ppermute | solution.py:301
  71.3 1.3 %collective-permute-start.21 = (bf16[128,1024]{1,0:T(8,128)(2,1)S(1)}, bf16[128,1024]{1,0:T(8,128)(2,1)S(1)}, u32[]{:S(2)}, u32[]{:S(2)}) collective-permute-start(bf16[128,1024]{1,0:T(8,128)(2,1)S(1)} %get-tuple-element.275), channel_id=1, source_target_pairs={{0,2},{2,0},{1,3},{3,1},{4,6},{6,4},{5,7},{7,5},{8,10},{10,8},{9,1... | collective-permute-start | bytes 786440 | tf_op jit(solution)/shard_map/ppermute | solution.py:291
  72.6 3.4 %collective-permute-done.19.refs_12_ = bf16[4,768,512]{2,1,0:T(8,128)(2,1)S(1)} collective-permute-done((bf16[4,768,512]{2,1,0:T(8,128)(2,1)S(1)}, bf16[4,768,512]{2,1,0:T(8,128)(2,1)S(1)}, u32[]{:S(2)}, u32[]{:S(2)}) %collective-permute-start.19) | collective-permute-done | bytes 3145760 | tf_op jit(solution)/shard_map/ppermute | solution.py:340
  76.0 2.7 %weight_grads.3 = (bf16[4,512,256]{2,1,0:T(8,128)(2,1)}, bf16[4,512,256]{2,1,0:T(8,128)(2,1)}, bf16[4,256,512]{2,1,0:T(8,128)(2,1)}) custom-call(s32[1]{0:T(128)} %bitcast.1.side_ref, bf16[4,96,1024]{2,1,0:T(8,128)(2,1)S(1)} %get-tuple-element.250.refs_0_, bf16[4,96,1024]{2,1,0:T(8,128)(2,1)S(1)} %get-tuple-element.251.refs_1_, ...), custom_call_target="tpu_custom_call" | custom-call | flops 1207959552 | bytes 8650752 | tf_op jit(solution)/shard_map/weight_grads/pallas_call | solution.py:248
  78.7 1.4 %collective-permute-done.20 = bf16[128,1024]{1,0:T(8,128)(2,1)S(1)} collective-permute-done((bf16[128,1024]{1,0:T(8,128)(2,1)S(1)}, bf16[128,1024]{1,0:T(8,128)(2,1)S(1)}, u32[]{:S(2)}, u32[]{:S(2)}) %collective-permute-start.20) | collective-permute-done | bytes 262176 | tf_op jit(solution)/shard_map/ppermute | solution.py:301
  80.1 0.0 collective-permute-done.21
  80.1 0.9 %add_convert_fusion = bf16[128,1024]{1,0:T(8,128)(2,1)} fusion(bf16[128,1024]{1,0:T(8,128)(2,1)S(1)} %collective-permute-done.20, bf16[128,1024]{1,0:T(8,128)(2,1)S(1)} %collective-permute-done.18, bf16[128,1024]{1,0:T(8,128)(2,1)S(1)} %collective-permute-done.21, bf16[128,1024]{1,0:T(8,128)(2,1)S(1)} %get-tuple-element.248), kind=kLoop, calls=%fused_computation | loop fusion | flops 1048576 | bytes 1310720 | tf_op jit(solution)/shard_map/convert_element_type | solution.py:350
Async XLA Ops:
  2.4 10.8 %collective-permute-start.1 = (bf16[144,1024]{1,0:T(8,128)(2,1)S(1)}, bf16[144,1024]{1,0:T(8,128)(2,1)S(1)}, u32[]{:S(2)}, u32[]{:S(2)}) collective-permute-start(bf16[144,1024]{1,0:T(8,128)(2,1)S(1)} %get-tuple-element.153.refs_2_), channel_id=1, source_target_pairs={{0,2},{2,0},{1,3},{3,1},{4,6},{6,4},{5,7},{7,5},{8,10},{10,8},{9,1... | collective-permute-start | bytes 884744 | tf_op jit(solution)/shard_map/ppermute | solution.py:284
  5.4 10.8 %collective-permute-start = (bf16[144,1024]{1,0:T(8,128)(2,1)S(1)}, bf16[144,1024]{1,0:T(8,128)(2,1)S(1)}, u32[]{:S(2)}, u32[]{:S(2)}) collective-permute-start(bf16[144,1024]{1,0:T(8,128)(2,1)S(1)} %get-tuple-element.153.refs_2_), channel_id=1, source_target_pairs={{0,4},{4,12},{12,8},{8,0},{1,5},{5,13},{13,9},{9,1},{2,6},{6,14},{... | collective-permute-start | bytes 884744 | tf_op jit(solution)/shard_map/ppermute | solution.py:318
  7.0 11.9 %collective-permute-start.5 = (bf16[128,1024]{1,0:T(8,128)(2,1)}, bf16[128,1024]{1,0:T(8,128)(2,1)S(1)}, u32[]{:S(2)}, u32[]{:S(2)}) collective-permute-start(bf16[128,1024]{1,0:T(8,128)(2,1)} %tokens), channel_id=1, source_target_pairs={{0,2},{2,0},{1,3},{3,1},{4,6},{6,4},{5,7},{7,5},{8,10},{10,8},{9,1... | collective-permute-start | bytes 786440 | tf_op jit(solution)/shard_map/ppermute | solution.py:284
  7.5 14.3 %collective-permute-start.4 = (bf16[128,1024]{1,0:T(8,128)(2,1)}, bf16[128,1024]{1,0:T(8,128)(2,1)S(1)}, u32[]{:S(2)}, u32[]{:S(2)}) collective-permute-start(bf16[128,1024]{1,0:T(8,128)(2,1)} %tokens), channel_id=1, source_target_pairs={{0,4},{4,12},{12,8},{8,0},{1,5},{5,13},{13,9},{9,1},{2,6},{6,14},{... | collective-permute-start | bytes 786440 | tf_op jit(solution)/shard_map/ppermute | solution.py:318
  16.3 10.7 %collective-permute-start.3 = (bf16[144,1024]{1,0:T(8,128)(2,1)S(1)}, bf16[144,1024]{1,0:T(8,128)(2,1)S(1)}, u32[]{:S(2)}, u32[]{:S(2)}) collective-permute-start(bf16[144,1024]{1,0:T(8,128)(2,1)S(1)} %collective-permute-done.refs_2_), channel_id=1, source_target_pairs={{0,2},{2,0},{1,3},{3,1},{4,6},{6,4},{5,7},{7,5},{8,10},{10,8},{9,1... | collective-permute-start | bytes 884744 | tf_op jit(solution)/shard_map/ppermute | solution.py:284
  16.4 11.8 %collective-permute-start.2 = (bf16[144,1024]{1,0:T(8,128)(2,1)S(1)}, bf16[144,1024]{1,0:T(8,128)(2,1)S(1)}, u32[]{:S(2)}, u32[]{:S(2)}) collective-permute-start(bf16[144,1024]{1,0:T(8,128)(2,1)S(1)} %collective-permute-done.refs_2_), channel_id=1, source_target_pairs={{0,4},{4,12},{12,8},{8,0},{1,5},{5,13},{13,9},{9,1},{2,6},{6,14},{... | collective-permute-start | bytes 884744 | tf_op jit(solution)/shard_map/ppermute | solution.py:318
  21.9 10.0 %collective-permute-start.9 = (bf16[128,1024]{1,0:T(8,128)(2,1)S(1)}, bf16[128,1024]{1,0:T(8,128)(2,1)S(1)}, u32[]{:S(2)}, u32[]{:S(2)}) collective-permute-start(bf16[128,1024]{1,0:T(8,128)(2,1)S(1)} %collective-permute-done.4.refs_0_), channel_id=1, source_target_pairs={{0,2},{2,0},{1,3},{3,1},{4,6},{6,4},{5,7},{7,5},{8,10},{10,8},{9,1... | collective-permute-start | bytes 786440 | tf_op jit(solution)/shard_map/ppermute | solution.py:284
  22.0 11.8 %collective-permute-start.8 = (bf16[128,1024]{1,0:T(8,128)(2,1)S(1)}, bf16[128,1024]{1,0:T(8,128)(2,1)S(1)}, u32[]{:S(2)}, u32[]{:S(2)}) collective-permute-start(bf16[128,1024]{1,0:T(8,128)(2,1)S(1)} %collective-permute-done.4.refs_0_), channel_id=1, source_target_pairs={{0,4},{4,12},{12,8},{8,0},{1,5},{5,13},{13,9},{9,1},{2,6},{6,14},{... | collective-permute-start | bytes 786440 | tf_op jit(solution)/shard_map/ppermute | solution.py:318
  28.2 11.0 %collective-permute-start.7 = (bf16[144,1024]{1,0:T(8,128)(2,1)S(1)}, bf16[144,1024]{1,0:T(8,128)(2,1)S(1)}, u32[]{:S(2)}, u32[]{:S(2)}) collective-permute-start(bf16[144,1024]{1,0:T(8,128)(2,1)S(1)} %collective-permute-done.2.refs_2_), channel_id=1, source_target_pairs={{0,2},{2,0},{1,3},{3,1},{4,6},{6,4},{5,7},{7,5},{8,10},{10,8},{9,1... | collective-permute-start | bytes 884744 | tf_op jit(solution)/shard_map/ppermute | solution.py:284
  29.1 11.0 %collective-permute-start.6 = (bf16[144,1024]{1,0:T(8,128)(2,1)S(1)}, bf16[144,1024]{1,0:T(8,128)(2,1)S(1)}, u32[]{:S(2)}, u32[]{:S(2)}) collective-permute-start(bf16[144,1024]{1,0:T(8,128)(2,1)S(1)} %collective-permute-done.2.refs_2_), channel_id=1, source_target_pairs={{0,4},{4,12},{12,8},{8,0},{1,5},{5,13},{13,9},{9,1},{2,6},{6,14},{... | collective-permute-start | bytes 884744 | tf_op jit(solution)/shard_map/ppermute | solution.py:318
  33.8 9.9 %collective-permute-start.12 = (bf16[128,1024]{1,0:T(8,128)(2,1)S(1)}, bf16[128,1024]{1,0:T(8,128)(2,1)S(1)}, u32[]{:S(2)}, u32[]{:S(2)}) collective-permute-start(bf16[128,1024]{1,0:T(8,128)(2,1)S(1)} %collective-permute-done.8.refs_0_), channel_id=1, source_target_pairs={{0,2},{2,0},{1,3},{3,1},{4,6},{6,4},{5,7},{7,5},{8,10},{10,8},{9,1... | collective-permute-start | bytes 786440 | tf_op jit(solution)/shard_map/ppermute | solution.py:284
  34.7 9.5 %collective-permute-start.11 = (bf16[128,1024]{1,0:T(8,128)(2,1)S(1)}, bf16[128,1024]{1,0:T(8,128)(2,1)S(1)}, u32[]{:S(2)}, u32[]{:S(2)}) collective-permute-start(bf16[128,1024]{1,0:T(8,128)(2,1)S(1)} %collective-permute-done.8.refs_0_), channel_id=1, source_target_pairs={{0,4},{4,12},{12,8},{8,0},{1,5},{5,13},{13,9},{9,1},{2,6},{6,14},{... | collective-permute-start | bytes 786440 | tf_op jit(solution)/shard_map/ppermute | solution.py:318
  40.1 15.6 %collective-permute-start.10 = (bf16[144,1024]{1,0:T(8,128)(2,1)S(1)}, bf16[144,1024]{1,0:T(8,128)(2,1)S(1)}, u32[]{:S(2)}, u32[]{:S(2)}) collective-permute-start(bf16[144,1024]{1,0:T(8,128)(2,1)S(1)} %collective-permute-done.6.refs_2_), channel_id=1, source_target_pairs={{0,2},{2,0},{1,3},{3,1},{4,6},{6,4},{5,7},{7,5},{8,10},{10,8},{9,1... | collective-permute-start | bytes 884744 | tf_op jit(solution)/shard_map/ppermute | solution.py:284
  44.3 7.8 %collective-permute-start.14 = (bf16[128,1024]{1,0:T(8,128)(2,1)S(1)}, bf16[128,1024]{1,0:T(8,128)(2,1)S(1)}, u32[]{:S(2)}, u32[]{:S(2)}) collective-permute-start(bf16[128,1024]{1,0:T(8,128)(2,1)S(1)} %collective-permute-done.12.refs_1_), channel_id=1, source_target_pairs={{0,4},{4,12},{12,8},{8,0},{1,5},{5,13},{13,9},{9,1},{2,6},{6,14},{... | collective-permute-start | bytes 786440 | tf_op jit(solution)/shard_map/ppermute | solution.py:314
  45.9 9.8 %collective-permute-start.13 = (bf16[128,1024]{1,0:T(8,128)(2,1)S(1)}, bf16[128,1024]{1,0:T(8,128)(2,1)S(1)}, u32[]{:S(2)}, u32[]{:S(2)}) collective-permute-start(bf16[128,1024]{1,0:T(8,128)(2,1)S(1)} %get-tuple-element.187), channel_id=1, source_target_pairs={{0,2},{2,0},{1,3},{3,1},{4,6},{6,4},{5,7},{7,5},{8,10},{10,8},{9,1... | collective-permute-start | bytes 786440 | tf_op jit(solution)/shard_map/ppermute | solution.py:291
  51.1 10.7 %collective-permute-start.15 = (bf16[128,1024]{1,0:T(8,128)(2,1)S(1)}, bf16[128,1024]{1,0:T(8,128)(2,1)S(1)}, u32[]{:S(2)}, u32[]{:S(2)}) collective-permute-start(bf16[128,1024]{1,0:T(8,128)(2,1)S(1)} %get-tuple-element.205), channel_id=1, source_target_pairs={{0,2},{2,0},{1,3},{3,1},{4,6},{6,4},{5,7},{7,5},{8,10},{10,8},{9,1... | collective-permute-start | bytes 786440 | tf_op jit(solution)/shard_map/ppermute | solution.py:291
  55.8 9.7 %collective-permute-start.18 = (bf16[128,1024]{1,0:T(8,128)(2,1)S(1)}, bf16[128,1024]{1,0:T(8,128)(2,1)S(1)}, u32[]{:S(2)}, u32[]{:S(2)}) collective-permute-start(bf16[128,1024]{1,0:T(8,128)(2,1)S(1)} %add_convert_fusion.2), channel_id=1, source_target_pairs={{0,8},{4,0},{12,4},{8,12},{1,9},{5,1},{13,5},{9,13},{2,10},{6,2},{... | collective-permute-start | bytes 786440 | tf_op jit(solution)/shard_map/ppermute | solution.py:301
  61.9 8.4 %collective-permute-start.17 = (bf16[128,1024]{1,0:T(8,128)(2,1)S(1)}, bf16[128,1024]{1,0:T(8,128)(2,1)S(1)}, u32[]{:S(2)}, u32[]{:S(2)}) collective-permute-start(bf16[128,1024]{1,0:T(8,128)(2,1)S(1)} %add_convert_fusion.3), channel_id=1, source_target_pairs={{0,4},{4,12},{12,8},{8,0},{1,5},{5,13},{13,9},{9,1},{2,6},{6,14},{... | collective-permute-start | bytes 786440 | tf_op jit(solution)/shard_map/ppermute | solution.py:301
  62.0 8.3 %collective-permute-start.16 = (bf16[128,1024]{1,0:T(8,128)(2,1)S(1)}, bf16[128,1024]{1,0:T(8,128)(2,1)S(1)}, u32[]{:S(2)}, u32[]{:S(2)}) collective-permute-start(bf16[128,1024]{1,0:T(8,128)(2,1)S(1)} %get-tuple-element.244), channel_id=1, source_target_pairs={{0,2},{2,0},{1,3},{3,1},{4,6},{6,4},{5,7},{7,5},{8,10},{10,8},{9,1... | collective-permute-start | bytes 786440 | tf_op jit(solution)/shard_map/ppermute | solution.py:291
  70.3 5.7 %collective-permute-start.19 = (bf16[4,768,512]{2,1,0:T(8,128)(2,1)S(1)}, bf16[4,768,512]{2,1,0:T(8,128)(2,1)S(1)}, u32[]{:S(2)}, u32[]{:S(2)}) collective-permute-start(bf16[4,768,512]{2,1,0:T(8,128)(2,1)S(1)} %weight_grads.2), channel_id=1, source_target_pairs={{0,1},{1,0},{2,3},{3,2},{4,5},{5,4},{6,7},{7,6},{8,9},{9,8},{10,11... | collective-permute-start | bytes 9437192 | tf_op jit(solution)/shard_map/ppermute | solution.py:340
  70.5 9.7 %collective-permute-start.20 = (bf16[128,1024]{1,0:T(8,128)(2,1)S(1)}, bf16[128,1024]{1,0:T(8,128)(2,1)S(1)}, u32[]{:S(2)}, u32[]{:S(2)}) collective-permute-start(bf16[128,1024]{1,0:T(8,128)(2,1)S(1)} %add_convert_fusion.1), channel_id=1, source_target_pairs={{0,4},{4,12},{12,8},{8,0},{1,5},{5,13},{13,9},{9,1},{2,6},{6,14},{... | collective-permute-start | bytes 786440 | tf_op jit(solution)/shard_map/ppermute | solution.py:301
  71.3 8.8 %collective-permute-start.21 = (bf16[128,1024]{1,0:T(8,128)(2,1)S(1)}, bf16[128,1024]{1,0:T(8,128)(2,1)S(1)}, u32[]{:S(2)}, u32[]{:S(2)}) collective-permute-start(bf16[128,1024]{1,0:T(8,128)(2,1)S(1)} %get-tuple-element.275), channel_id=1, source_target_pairs={{0,2},{2,0},{1,3},{3,1},{4,6},{6,4},{5,7},{7,5},{8,10},{10,8},{9,1... | collective-permute-start | bytes 786440 | tf_op jit(solution)/shard_map/ppermute | solution.py:291

commit v16 on v15

--- a/solution.py
+++ b/solution.py
@@ -320,7 +320,6 @@
             chunks[k - 1] = chunk(blocks[k - 1])
         if k == last:
             backs[k - 1] = across(chunks[k - 1][1])
-            backs[1], chunks = tie(backs[1], chunks)
         upstream, pair[1], chunks, weights = tie(upstream, pair[1], chunks, weights)
         tokens, pair[0] = tie(tokens, pair[0])
         blocks[k] = pair
@@ -329,13 +328,14 @@
         sent[k] = homeward(group_sum(chunks[k][0], across(chunks[k][1])), k)
     chunks[last] = chunk(blocks[last])
     backs[last] = across(chunks[last][1])
+    chunks, backs[last - 1], backs[1] = tie(chunks, backs[last - 1], backs[1])
+
     sent[1] = homeward(group_sum(chunks[1][0], backs[1]), 1)
-    chunks, backs[last - 1] = tie(chunks, backs[last - 1])
-
     carried = homeward(group_sum(chunks[last - 1][0], backs[last - 1]), last)
     kept = [[chunks[k][i] for k in range(n_group)] for i in (-3, -2, -1)]
     to_send = weight_call(other_half, *kept)
-    to_send, backs[last], carried, other, sent = tie(to_send, backs[last], carried, chunks[0][1], sent)
+    to_send, backs[last], other = tie(to_send, backs[last], chunks[0][1])
+    to_send, carried, sent = tie(to_send, carried, sent)
 
     got = lax.ppermute(to_send, "dp", [(0, 1), (1, 0)])
     sent[last] = homeward(group_sum(chunks[last][0], [*backs[last], carried]), last)

time: 81.2 us -> 85 us (1.047)
  waiting for transfers between devices: 28.6 us -> 32.3 us
    ppermute x3, waiting for transfers between devices: 6.34 us -> 9.92 us  [homeward(): return lax.ppermute(group_part, 'group', along(-k))]
  transfers between devices with their start and end apart: 22 -> 22, of which waited for: 14 -> 15; matrix products, arithmetic and copies ran while one was open for 0% -> 0% of each run, Pallas kernels for 27% -> 26%
where the time goes in v16:
time: 85 us; the launch traced here: 84.8 us
  waiting for transfers between devices  32.3 us (38%)
  starting transfers between devices  26.7 us (31%)
  Pallas kernels  23.9 us (28%)
  other arithmetic  1.13 us (1%)
    pallas_call x4, Pallas kernels, chunk_call(): pl.pallas_call(functools.partial(chunk_kernel, n_blocks, tok_rows, capaci...  14.7 us
    ppermute x6, waiting for transfers between devices, per_device(): lax.ppermute(v, 'group', along(1))  10.6 us
    ppermute x6, starting transfers between devices, per_device(): lax.ppermute(v, 'group', along(1))  10.1 us
    ppermute x3, waiting for transfers between devices, homeward(): return lax.ppermute(group_part, 'group', along(-k))  9.92 us
    ppermute x7, starting transfers between devices, spread(): lax.ppermute(column, 'ingroup', shift(s))  6.68 us
    ppermute x4, starting transfers between devices, across(): lax.ppermute(others[(s - 1) * tok_rows:s * tok_rows], 'ingroup', shift(-s))  4.8 us
    pallas_call x2, Pallas kernels, weight_call(): pl.pallas_call(functools.partial(kernel, n), in_specs=[smem] + [vmem] * l...  4.58 us
    ppermute x4, waiting for transfers between devices, across(): lax.ppermute(others[(s - 1) * tok_rows:s * tok_rows], 'ingroup', shift(-s))  4.38 us
  transfers between devices with their start and end apart: 22, of which 15 were waited for; matrix products, arithmetic and copies ran while one was open for 0% of the time, Pallas kernels for 26%

profile of v16, /device:TPU:0, one launch (start us, length us, event | category | flops | bytes accessed | tf_op | source)
XLA Modules:
  0.0 84.8 jit_solution(17512450045320229971)
XLA Ops:
  0.6 1.8 %pack.1 = (bf16[128,1024]{1,0:T(8,128)(2,1)S(1)}, bf16[144,1024]{1,0:T(8,128)(2,1)S(1)}) custom-call(bf16[128,1024]{1,0:T(8,128)(2,1)} %tokens, bf16[128,1024]{1,0:T(8,128)(2,1)} %upstream.1, s32[8,128]{1,0:T(8,128)} %bitcast.5, s32[8,128]{1,0:T(8,128)} %bitcast.6, s32[8,128]{1,0:T(8,128)} %bitcast.7), custom_call_target="tpu_custom_call" | custom-call | bytes 1048576 | tf_op jit(solution)/shard_map/pack/pallas_call | solution.py:58
  2.4 3.0 %collective-permute-start.1 = (bf16[144,1024]{1,0:T(8,128)(2,1)S(1)}, bf16[144,1024]{1,0:T(8,128)(2,1)S(1)}, u32[]{:S(2)}, u32[]{:S(2)}) collective-permute-start(bf16[144,1024]{1,0:T(8,128)(2,1)S(1)} %get-tuple-element.142.refs_2_), channel_id=1, source_target_pairs={{0,2},{2,0},{1,3},{3,1},{4,6},{6,4},{5,7},{7,5},{8,10},{10,8},{9,1... | collective-permute-start | bytes 884744 | tf_op jit(solution)/shard_map/ppermute | solution.py:284
  5.4 1.6 %collective-permute-start = (bf16[144,1024]{1,0:T(8,128)(2,1)S(1)}, bf16[144,1024]{1,0:T(8,128)(2,1)S(1)}, u32[]{:S(2)}, u32[]{:S(2)}) collective-permute-start(bf16[144,1024]{1,0:T(8,128)(2,1)S(1)} %get-tuple-element.142.refs_2_), channel_id=1, source_target_pairs={{0,4},{4,12},{12,8},{8,0},{1,5},{5,13},{13,9},{9,1},{2,6},{6,14},{... | collective-permute-start | bytes 884744 | tf_op jit(solution)/shard_map/ppermute | solution.py:318
  7.0 0.5 collective-permute-start.5
  7.5 2.6 %collective-permute-start.4 = (bf16[128,1024]{1,0:T(8,128)(2,1)}, bf16[128,1024]{1,0:T(8,128)(2,1)S(1)}, u32[]{:S(2)}, u32[]{:S(2)}) collective-permute-start(bf16[128,1024]{1,0:T(8,128)(2,1)} %tokens), channel_id=1, source_target_pairs={{0,4},{4,12},{12,8},{8,0},{1,5},{5,13},{13,9},{9,1},{2,6},{6,14},{... | collective-permute-start | bytes 786440 | tf_op jit(solution)/shard_map/ppermute | solution.py:318
  10.1 2.9 %load.1 = (bf16[4,1024,256]{2,1,0:T(8,128)(2,1)S(1)}, bf16[4,1024,256]{2,1,0:T(8,128)(2,1)S(1)}, bf16[4,256,1024]{2,1,0:T(8,128)(2,1)S(1)}) custom-call(bf16[4,1024,256]{2,1,0:T(8,128)(2,1)} %refs_0_.1, bf16[4,1024,256]{2,1,0:T(8,128)(2,1)} %refs_1_.1, bf16[4,256,1024]{2,1,0:T(8,128)(2,1)} %refs_2_.1), custom_call_target="tpu_custom_call" | custom-call | bytes 12582912 | tf_op jit(solution)/shard_map/load/pallas_call | solution.py:99
  13.0 0.2 collective-permute-done.1.refs_3_
  13.3 3.0 %collective-permute-done.refs_2_ = bf16[144,1024]{1,0:T(8,128)(2,1)S(1)} collective-permute-done((bf16[144,1024]{1,0:T(8,128)(2,1)S(1)}, bf16[144,1024]{1,0:T(8,128)(2,1)S(1)}, u32[]{:S(2)}, u32[]{:S(2)}) %collective-permute-start) | collective-permute-done | bytes 294944 | tf_op jit(solution)/shard_map/ppermute | solution.py:318
  16.3 0.2 collective-permute-start.3
  16.4 1.2 %collective-permute-start.2 = (bf16[144,1024]{1,0:T(8,128)(2,1)S(1)}, bf16[144,1024]{1,0:T(8,128)(2,1)S(1)}, u32[]{:S(2)}, u32[]{:S(2)}) collective-permute-start(bf16[144,1024]{1,0:T(8,128)(2,1)S(1)} %collective-permute-done.refs_2_), channel_id=1, source_target_pairs={{0,4},{4,12},{12,8},{8,0},{1,5},{5,13},{13,9},{9,1},{2,6},{6,14},{... | collective-permute-start | bytes 884744 | tf_op jit(solution)/shard_map/ppermute | solution.py:318
  17.6 1.3 %collective-permute-done.5.refs_1_ = bf16[128,1024]{1,0:T(8,128)(2,1)S(1)} collective-permute-done((bf16[128,1024]{1,0:T(8,128)(2,1)}, bf16[128,1024]{1,0:T(8,128)(2,1)S(1)}, u32[]{:S(2)}, u32[]{:S(2)}) %collective-permute-start.5) | collective-permute-done | bytes 262176 | tf_op jit(solution)/shard_map/ppermute | solution.py:284
  18.9 3.0 %collective-permute-done.4.refs_0_ = bf16[128,1024]{1,0:T(8,128)(2,1)S(1)} collective-permute-done((bf16[128,1024]{1,0:T(8,128)(2,1)}, bf16[128,1024]{1,0:T(8,128)(2,1)S(1)}, u32[]{:S(2)}, u32[]{:S(2)}) %collective-permute-start.4) | collective-permute-done | bytes 262176 | tf_op jit(solution)/shard_map/ppermute | solution.py:318
  21.9 0.2 collective-permute-start.9
  22.0 1.3 %collective-permute-start.8 = (bf16[128,1024]{1,0:T(8,128)(2,1)S(1)}, bf16[128,1024]{1,0:T(8,128)(2,1)S(1)}, u32[]{:S(2)}, u32[]{:S(2)}) collective-permute-start(bf16[128,1024]{1,0:T(8,128)(2,1)S(1)} %collective-permute-done.4.refs_0_), channel_id=1, source_target_pairs={{0,4},{4,12},{12,8},{8,0},{1,5},{5,13},{13,9},{9,1},{2,6},{6,14},{... | collective-permute-start | bytes 786440 | tf_op jit(solution)/shard_map/ppermute | solution.py:318
  23.3 3.7 %chunk.4 = (bf16[128,1024]{1,0:T(8,128)(2,1)S(1)}, bf16[128,1024]{1,0:T(8,128)(2,1)S(1)}, bf16[4,96,1024]{2,1,0:T(8,128)(2,1)S(1)}, bf16[4,96,1024]{2,1,0:T(8,128)(2,1)S(1)}, bf16[4,96,768]{2,1,0:T(8,128)(2,1)S(1)}) custom-call(s32[1]{0:T(128)} %bitcast.first_ref, bf16[128,1024]{1,0:T(8,128)(2,1)S(1)} %get-tuple-element.140.refs_0_, ...), custom_call_target="tpu_custom_call" | custom-call | flops 1610612736 | bytes 8388608 | tf_op jit(solution)/shard_map/chunk/pallas_call | solution.py:175
  27.0 0.0 collective-permute-done.3.refs_3_
  27.0 1.2 %collective-permute-done.2.refs_2_ = bf16[144,1024]{1,0:T(8,128)(2,1)S(1)} collective-permute-done((bf16[144,1024]{1,0:T(8,128)(2,1)S(1)}, bf16[144,1024]{1,0:T(8,128)(2,1)S(1)}, u32[]{:S(2)}, u32[]{:S(2)}) %collective-permute-start.2) | collective-permute-done | bytes 294944 | tf_op jit(solution)/shard_map/ppermute | solution.py:318
  28.2 0.9 %collective-permute-start.7 = (bf16[144,1024]{1,0:T(8,128)(2,1)S(1)}, bf16[144,1024]{1,0:T(8,128)(2,1)S(1)}, u32[]{:S(2)}, u32[]{:S(2)}) collective-permute-start(bf16[144,1024]{1,0:T(8,128)(2,1)S(1)} %collective-permute-done.2.refs_2_), channel_id=1, source_target_pairs={{0,2},{2,0},{1,3},{3,1},{4,6},{6,4},{5,7},{7,5},{8,10},{10,8},{9,1... | collective-permute-start | bytes 884744 | tf_op jit(solution)/shard_map/ppermute | solution.py:284
  29.1 2.7 %collective-permute-start.6 = (bf16[144,1024]{1,0:T(8,128)(2,1)S(1)}, bf16[144,1024]{1,0:T(8,128)(2,1)S(1)}, u32[]{:S(2)}, u32[]{:S(2)}) collective-permute-start(bf16[144,1024]{1,0:T(8,128)(2,1)S(1)} %collective-permute-done.2.refs_2_), channel_id=1, source_target_pairs={{0,4},{4,12},{12,8},{8,0},{1,5},{5,13},{13,9},{9,1},{2,6},{6,14},{... | collective-permute-start | bytes 884744 | tf_op jit(solution)/shard_map/ppermute | solution.py:318
  31.8 0.0 collective-permute-done.9.refs_1_
  31.8 2.0 %collective-permute-done.8.refs_0_ = bf16[128,1024]{1,0:T(8,128)(2,1)S(1)} collective-permute-done((bf16[128,1024]{1,0:T(8,128)(2,1)S(1)}, bf16[128,1024]{1,0:T(8,128)(2,1)S(1)}, u32[]{:S(2)}, u32[]{:S(2)}) %collective-permute-start.8) | collective-permute-done | bytes 262176 | tf_op jit(solution)/shard_map/ppermute | solution.py:318
  33.8 0.9 %collective-permute-start.12 = (bf16[128,1024]{1,0:T(8,128)(2,1)S(1)}, bf16[128,1024]{1,0:T(8,128)(2,1)S(1)}, u32[]{:S(2)}, u32[]{:S(2)}) collective-permute-start(bf16[128,1024]{1,0:T(8,128)(2,1)S(1)} %collective-permute-done.8.refs_0_), channel_id=1, source_target_pairs={{0,2},{2,0},{1,3},{3,1},{4,6},{6,4},{5,7},{7,5},{8,10},{10,8},{9,1... | collective-permute-start | bytes 786440 | tf_op jit(solution)/shard_map/ppermute | solution.py:284
  34.7 0.8 collective-permute-start.11
  35.5 3.7 %chunk.5 = (bf16[128,1024]{1,0:T(8,128)(2,1)S(1)}, bf16[128,1024]{1,0:T(8,128)(2,1)S(1)}, bf16[4,96,1024]{2,1,0:T(8,128)(2,1)S(1)}, bf16[4,96,1024]{2,1,0:T(8,128)(2,1)S(1)}, bf16[4,96,768]{2,1,0:T(8,128)(2,1)S(1)}) custom-call(s32[1]{0:T(128)} %bitcast.first_ref, bf16[128,1024]{1,0:T(8,128)(2,1)S(1)} %collective-permute-done.4.refs_0_, ...), custom_call_target="tpu_custom_call" | custom-call | flops 1610612736 | bytes 8388608 | tf_op jit(solution)/shard_map/chunk/pallas_call | solution.py:175
  39.2 0.0 collective-permute-done.7.refs_3_
  39.2 0.9 %collective-permute-done.6.refs_2_ = bf16[144,1024]{1,0:T(8,128)(2,1)S(1)} collective-permute-done((bf16[144,1024]{1,0:T(8,128)(2,1)S(1)}, bf16[144,1024]{1,0:T(8,128)(2,1)S(1)}, u32[]{:S(2)}, u32[]{:S(2)}) %collective-permute-start.6) | collective-permute-done | bytes 294944 | tf_op jit(solution)/shard_map/ppermute | solution.py:318
  40.1 0.9 %collective-permute-start.10 = (bf16[144,1024]{1,0:T(8,128)(2,1)S(1)}, bf16[144,1024]{1,0:T(8,128)(2,1)S(1)}, u32[]{:S(2)}, u32[]{:S(2)}) collective-permute-start(bf16[144,1024]{1,0:T(8,128)(2,1)S(1)} %collective-permute-done.6.refs_2_), channel_id=1, source_target_pairs={{0,2},{2,0},{1,3},{3,1},{4,6},{6,4},{5,7},{7,5},{8,10},{10,8},{9,1... | collective-permute-start | bytes 884744 | tf_op jit(solution)/shard_map/ppermute | solution.py:284
  41.1 2.7 %collective-permute-done.12.refs_1_ = bf16[128,1024]{1,0:T(8,128)(2,1)S(1)} collective-permute-done((bf16[128,1024]{1,0:T(8,128)(2,1)S(1)}, bf16[128,1024]{1,0:T(8,128)(2,1)S(1)}, u32[]{:S(2)}, u32[]{:S(2)}) %collective-permute-start.12) | collective-permute-done | bytes 262176 | tf_op jit(solution)/shard_map/ppermute | solution.py:284
  43.8 0.5 collective-permute-done.11.refs_0_
  44.3 1.6 %collective-permute-start.13 = (bf16[128,1024]{1,0:T(8,128)(2,1)S(1)}, bf16[128,1024]{1,0:T(8,128)(2,1)S(1)}, u32[]{:S(2)}, u32[]{:S(2)}) collective-permute-start(bf16[128,1024]{1,0:T(8,128)(2,1)S(1)} %collective-permute-done.12.refs_1_), channel_id=1, source_target_pairs={{0,4},{4,12},{12,8},{8,0},{1,5},{5,13},{13,9},{9,1},{2,6},{6,14},{... | collective-permute-start | bytes 786440 | tf_op jit(solution)/shard_map/ppermute | solution.py:314
  45.9 1.5 %collective-permute-start.15 = (bf16[128,1024]{1,0:T(8,128)(2,1)S(1)}, bf16[128,1024]{1,0:T(8,128)(2,1)S(1)}, u32[]{:S(2)}, u32[]{:S(2)}) collective-permute-start(bf16[128,1024]{1,0:T(8,128)(2,1)S(1)} %get-tuple-element.223), channel_id=1, source_target_pairs={{0,2},{2,0},{1,3},{3,1},{4,6},{6,4},{5,7},{7,5},{8,10},{10,8},{9,1... | collective-permute-start | bytes 786440 | tf_op jit(solution)/shard_map/ppermute | solution.py:291
  47.4 3.7 %chunk.6 = (bf16[128,1024]{1,0:T(8,128)(2,1)S(1)}, bf16[128,1024]{1,0:T(8,128)(2,1)S(1)}, bf16[4,96,1024]{2,1,0:T(8,128)(2,1)S(1)}, bf16[4,96,1024]{2,1,0:T(8,128)(2,1)S(1)}, bf16[4,96,768]{2,1,0:T(8,128)(2,1)S(1)}) custom-call(s32[1]{0:T(128)} %bitcast.first_ref, bf16[128,1024]{1,0:T(8,128)(2,1)S(1)} %collective-permute-done.8.refs_0_, ...), custom_call_target="tpu_custom_call" | custom-call | flops 1610612736 | bytes 8388608 | tf_op jit(solution)/shard_map/chunk/pallas_call | solution.py:175
  51.1 0.6 collective-permute-start.14
  51.7 0.3 collective-permute-done.13.refs_1_
  52.0 0.0 collective-permute-done.10.refs_3_
  52.0 3.7 %chunk.7 = (bf16[128,1024]{1,0:T(8,128)(2,1)S(1)}, bf16[128,1024]{1,0:T(8,128)(2,1)S(1)}, bf16[4,96,1024]{2,1,0:T(8,128)(2,1)S(1)}, bf16[4,96,1024]{2,1,0:T(8,128)(2,1)S(1)}, bf16[4,96,768]{2,1,0:T(8,128)(2,1)S(1)}) custom-call(s32[1]{0:T(128)} %bitcast.first_ref, bf16[128,1024]{1,0:T(8,128)(2,1)S(1)} %collective-permute-done.11.refs_0_, ...), custom_call_target="tpu_custom_call" | custom-call | flops 1610612736 | bytes 8388608 | tf_op jit(solution)/shard_map/chunk/pallas_call | solution.py:175
  55.7 1.2 %collective-permute-start.16 = (bf16[128,1024]{1,0:T(8,128)(2,1)S(1)}, bf16[128,1024]{1,0:T(8,128)(2,1)S(1)}, u32[]{:S(2)}, u32[]{:S(2)}) collective-permute-start(bf16[128,1024]{1,0:T(8,128)(2,1)S(1)} %get-tuple-element.219), channel_id=1, source_target_pairs={{0,2},{2,0},{1,3},{3,1},{4,6},{6,4},{5,7},{7,5},{8,10},{10,8},{9,1... | collective-permute-start | bytes 786440 | tf_op jit(solution)/shard_map/ppermute | solution.py:291
  56.9 0.0 collective-permute-done.15
  56.9 4.4 %collective-permute-done.14 = bf16[128,1024]{1,0:T(8,128)(2,1)S(1)} collective-permute-done((bf16[128,1024]{1,0:T(8,128)(2,1)S(1)}, bf16[128,1024]{1,0:T(8,128)(2,1)S(1)}, u32[]{:S(2)}, u32[]{:S(2)}) %collective-permute-start.14) | collective-permute-done | bytes 262176 | tf_op jit(solution)/shard_map/ppermute | solution.py:291
  61.3 0.1 add_convert_fusion.2
  61.4 2.2 %collective-permute-start.18 = (bf16[128,1024]{1,0:T(8,128)(2,1)S(1)}, bf16[128,1024]{1,0:T(8,128)(2,1)S(1)}, u32[]{:S(2)}, u32[]{:S(2)}) collective-permute-start(bf16[128,1024]{1,0:T(8,128)(2,1)S(1)} %add_convert_fusion.2), channel_id=1, source_target_pairs={{0,8},{4,0},{12,4},{8,12},{1,9},{5,1},{13,5},{9,13},{2,10},{6,2},{... | collective-permute-start | bytes 786440 | tf_op jit(solution)/shard_map/ppermute | solution.py:301
  63.6 0.1 add_convert_fusion.3
  63.7 0.1 collective-permute-start.17
  63.7 1.9 %weight_grads.2 = bf16[4,768,512]{2,1,0:T(8,128)(2,1)S(1)} custom-call(s32[1]{0:T(128)S(6)} %sub.3.side_ref, bf16[4,96,1024]{2,1,0:T(8,128)(2,1)S(1)} %get-tuple-element.226.refs_0_, bf16[4,96,1024]{2,1,0:T(8,128)(2,1)S(1)} %get-tuple-element.227.refs_1_, bf16[4,96,1024]{2,1,0:T(8,128)(2,1)S(1)} %get-tuple-element.228.refs_2_, ...), custom_call_target="tpu_custom_call" | custom-call | flops 1207959552 | bytes 8650752 | tf_op jit(solution)/shard_map/weight_grads/pallas_call | solution.py:248
  65.6 0.0 collective-permute-done.16
  65.6 5.0 %collective-permute-done.18 = bf16[128,1024]{1,0:T(8,128)(2,1)S(1)} collective-permute-done((bf16[128,1024]{1,0:T(8,128)(2,1)S(1)}, bf16[128,1024]{1,0:T(8,128)(2,1)S(1)}, u32[]{:S(2)}, u32[]{:S(2)}) %collective-permute-start.18) | collective-permute-done | bytes 262176 | tf_op jit(solution)/shard_map/ppermute | solution.py:301
  70.7 3.5 %collective-permute-done.17 = bf16[128,1024]{1,0:T(8,128)(2,1)S(1)} collective-permute-done((bf16[128,1024]{1,0:T(8,128)(2,1)S(1)}, bf16[128,1024]{1,0:T(8,128)(2,1)S(1)}, u32[]{:S(2)}, u32[]{:S(2)}) %collective-permute-start.17) | collective-permute-done | bytes 262176 | tf_op jit(solution)/shard_map/ppermute | solution.py:301
  74.1 0.0 collective-permute-start.19
  74.1 0.1 add_convert_fusion.1
  74.2 1.2 %collective-permute-start.20 = (bf16[128,1024]{1,0:T(8,128)(2,1)S(1)}, bf16[128,1024]{1,0:T(8,128)(2,1)S(1)}, u32[]{:S(2)}, u32[]{:S(2)}) collective-permute-start(bf16[128,1024]{1,0:T(8,128)(2,1)S(1)} %add_convert_fusion.1), channel_id=1, source_target_pairs={{0,4},{4,12},{12,8},{8,0},{1,5},{5,13},{13,9},{9,1},{2,6},{6,14},{... | collective-permute-start | bytes 786440 | tf_op jit(solution)/shard_map/ppermute | solution.py:301
  75.5 1.5 %collective-permute-start.21 = (bf16[128,1024]{1,0:T(8,128)(2,1)S(1)}, bf16[128,1024]{1,0:T(8,128)(2,1)S(1)}, u32[]{:S(2)}, u32[]{:S(2)}) collective-permute-start(bf16[128,1024]{1,0:T(8,128)(2,1)S(1)} %get-tuple-element.253), channel_id=1, source_target_pairs={{0,2},{2,0},{1,3},{3,1},{4,6},{6,4},{5,7},{7,5},{8,10},{10,8},{9,1... | collective-permute-start | bytes 786440 | tf_op jit(solution)/shard_map/ppermute | solution.py:291
  77.0 2.8 %collective-permute-done.19.refs_12_ = bf16[4,768,512]{2,1,0:T(8,128)(2,1)S(1)} collective-permute-done((bf16[4,768,512]{2,1,0:T(8,128)(2,1)S(1)}, bf16[4,768,512]{2,1,0:T(8,128)(2,1)S(1)}, u32[]{:S(2)}, u32[]{:S(2)}) %collective-permute-start.19) | collective-permute-done | bytes 3145760 | tf_op jit(solution)/shard_map/ppermute | solution.py:340
  79.8 2.7 %weight_grads.3 = (bf16[4,512,256]{2,1,0:T(8,128)(2,1)}, bf16[4,512,256]{2,1,0:T(8,128)(2,1)}, bf16[4,256,512]{2,1,0:T(8,128)(2,1)}) custom-call(s32[1]{0:T(128)} %bitcast.1.side_ref, bf16[4,96,1024]{2,1,0:T(8,128)(2,1)S(1)} %get-tuple-element.226.refs_0_, bf16[4,96,1024]{2,1,0:T(8,128)(2,1)S(1)} %get-tuple-element.227.refs_1_, ...), custom_call_target="tpu_custom_call" | custom-call | flops 1207959552 | bytes 8650752 | tf_op jit(solution)/shard_map/weight_grads/pallas_call | solution.py:248
  82.5 1.4 %collective-permute-done.20 = bf16[128,1024]{1,0:T(8,128)(2,1)S(1)} collective-permute-done((bf16[128,1024]{1,0:T(8,128)(2,1)S(1)}, bf16[128,1024]{1,0:T(8,128)(2,1)S(1)}, u32[]{:S(2)}, u32[]{:S(2)}) %collective-permute-start.20) | collective-permute-done | bytes 262176 | tf_op jit(solution)/shard_map/ppermute | solution.py:301
  83.9 0.0 collective-permute-done.21
  83.9 0.9 %add_convert_fusion = bf16[128,1024]{1,0:T(8,128)(2,1)} fusion(bf16[128,1024]{1,0:T(8,128)(2,1)S(1)} %collective-permute-done.20, bf16[128,1024]{1,0:T(8,128)(2,1)S(1)} %collective-permute-done.18, bf16[128,1024]{1,0:T(8,128)(2,1)S(1)} %collective-permute-done.21, bf16[128,1024]{1,0:T(8,128)(2,1)S(1)} %get-tuple-element.224), kind=kLoop, calls=%fused_computation | loop fusion | flops 1048576 | bytes 1310720 | tf_op jit(solution)/shard_map/convert_element_type | solution.py:350
Async XLA Ops:
  2.4 10.8 %collective-permute-start.1 = (bf16[144,1024]{1,0:T(8,128)(2,1)S(1)}, bf16[144,1024]{1,0:T(8,128)(2,1)S(1)}, u32[]{:S(2)}, u32[]{:S(2)}) collective-permute-start(bf16[144,1024]{1,0:T(8,128)(2,1)S(1)} %get-tuple-element.142.refs_2_), channel_id=1, source_target_pairs={{0,2},{2,0},{1,3},{3,1},{4,6},{6,4},{5,7},{7,5},{8,10},{10,8},{9,1... | collective-permute-start | bytes 884744 | tf_op jit(solution)/shard_map/ppermute | solution.py:284
  5.4 10.8 %collective-permute-start = (bf16[144,1024]{1,0:T(8,128)(2,1)S(1)}, bf16[144,1024]{1,0:T(8,128)(2,1)S(1)}, u32[]{:S(2)}, u32[]{:S(2)}) collective-permute-start(bf16[144,1024]{1,0:T(8,128)(2,1)S(1)} %get-tuple-element.142.refs_2_), channel_id=1, source_target_pairs={{0,4},{4,12},{12,8},{8,0},{1,5},{5,13},{13,9},{9,1},{2,6},{6,14},{... | collective-permute-start | bytes 884744 | tf_op jit(solution)/shard_map/ppermute | solution.py:318
  7.0 11.9 %collective-permute-start.5 = (bf16[128,1024]{1,0:T(8,128)(2,1)}, bf16[128,1024]{1,0:T(8,128)(2,1)S(1)}, u32[]{:S(2)}, u32[]{:S(2)}) collective-permute-start(bf16[128,1024]{1,0:T(8,128)(2,1)} %tokens), channel_id=1, source_target_pairs={{0,2},{2,0},{1,3},{3,1},{4,6},{6,4},{5,7},{7,5},{8,10},{10,8},{9,1... | collective-permute-start | bytes 786440 | tf_op jit(solution)/shard_map/ppermute | solution.py:284
  7.5 14.3 %collective-permute-start.4 = (bf16[128,1024]{1,0:T(8,128)(2,1)}, bf16[128,1024]{1,0:T(8,128)(2,1)S(1)}, u32[]{:S(2)}, u32[]{:S(2)}) collective-permute-start(bf16[128,1024]{1,0:T(8,128)(2,1)} %tokens), channel_id=1, source_target_pairs={{0,4},{4,12},{12,8},{8,0},{1,5},{5,13},{13,9},{9,1},{2,6},{6,14},{... | collective-permute-start | bytes 786440 | tf_op jit(solution)/shard_map/ppermute | solution.py:318
  16.3 10.7 %collective-permute-start.3 = (bf16[144,1024]{1,0:T(8,128)(2,1)S(1)}, bf16[144,1024]{1,0:T(8,128)(2,1)S(1)}, u32[]{:S(2)}, u32[]{:S(2)}) collective-permute-start(bf16[144,1024]{1,0:T(8,128)(2,1)S(1)} %collective-permute-done.refs_2_), channel_id=1, source_target_pairs={{0,2},{2,0},{1,3},{3,1},{4,6},{6,4},{5,7},{7,5},{8,10},{10,8},{9,1... | collective-permute-start | bytes 884744 | tf_op jit(solution)/shard_map/ppermute | solution.py:284
  16.4 11.8 %collective-permute-start.2 = (bf16[144,1024]{1,0:T(8,128)(2,1)S(1)}, bf16[144,1024]{1,0:T(8,128)(2,1)S(1)}, u32[]{:S(2)}, u32[]{:S(2)}) collective-permute-start(bf16[144,1024]{1,0:T(8,128)(2,1)S(1)} %collective-permute-done.refs_2_), channel_id=1, source_target_pairs={{0,4},{4,12},{12,8},{8,0},{1,5},{5,13},{13,9},{9,1},{2,6},{6,14},{... | collective-permute-start | bytes 884744 | tf_op jit(solution)/shard_map/ppermute | solution.py:318
  21.9 10.0 %collective-permute-start.9 = (bf16[128,1024]{1,0:T(8,128)(2,1)S(1)}, bf16[128,1024]{1,0:T(8,128)(2,1)S(1)}, u32[]{:S(2)}, u32[]{:S(2)}) collective-permute-start(bf16[128,1024]{1,0:T(8,128)(2,1)S(1)} %collective-permute-done.4.refs_0_), channel_id=1, source_target_pairs={{0,2},{2,0},{1,3},{3,1},{4,6},{6,4},{5,7},{7,5},{8,10},{10,8},{9,1... | collective-permute-start | bytes 786440 | tf_op jit(solution)/shard_map/ppermute | solution.py:284
  22.0 11.8 %collective-permute-start.8 = (bf16[128,1024]{1,0:T(8,128)(2,1)S(1)}, bf16[128,1024]{1,0:T(8,128)(2,1)S(1)}, u32[]{:S(2)}, u32[]{:S(2)}) collective-permute-start(bf16[128,1024]{1,0:T(8,128)(2,1)S(1)} %collective-permute-done.4.refs_0_), channel_id=1, source_target_pairs={{0,4},{4,12},{12,8},{8,0},{1,5},{5,13},{13,9},{9,1},{2,6},{6,14},{... | collective-permute-start | bytes 786440 | tf_op jit(solution)/shard_map/ppermute | solution.py:318
  28.2 11.0 %collective-permute-start.7 = (bf16[144,1024]{1,0:T(8,128)(2,1)S(1)}, bf16[144,1024]{1,0:T(8,128)(2,1)S(1)}, u32[]{:S(2)}, u32[]{:S(2)}) collective-permute-start(bf16[144,1024]{1,0:T(8,128)(2,1)S(1)} %collective-permute-done.2.refs_2_), channel_id=1, source_target_pairs={{0,2},{2,0},{1,3},{3,1},{4,6},{6,4},{5,7},{7,5},{8,10},{10,8},{9,1... | collective-permute-start | bytes 884744 | tf_op jit(solution)/shard_map/ppermute | solution.py:284
  29.1 11.0 %collective-permute-start.6 = (bf16[144,1024]{1,0:T(8,128)(2,1)S(1)}, bf16[144,1024]{1,0:T(8,128)(2,1)S(1)}, u32[]{:S(2)}, u32[]{:S(2)}) collective-permute-start(bf16[144,1024]{1,0:T(8,128)(2,1)S(1)} %collective-permute-done.2.refs_2_), channel_id=1, source_target_pairs={{0,4},{4,12},{12,8},{8,0},{1,5},{5,13},{13,9},{9,1},{2,6},{6,14},{... | collective-permute-start | bytes 884744 | tf_op jit(solution)/shard_map/ppermute | solution.py:318
  33.8 9.9 %collective-permute-start.12 = (bf16[128,1024]{1,0:T(8,128)(2,1)S(1)}, bf16[128,1024]{1,0:T(8,128)(2,1)S(1)}, u32[]{:S(2)}, u32[]{:S(2)}) collective-permute-start(bf16[128,1024]{1,0:T(8,128)(2,1)S(1)} %collective-permute-done.8.refs_0_), channel_id=1, source_target_pairs={{0,2},{2,0},{1,3},{3,1},{4,6},{6,4},{5,7},{7,5},{8,10},{10,8},{9,1... | collective-permute-start | bytes 786440 | tf_op jit(solution)/shard_map/ppermute | solution.py:284
  34.7 9.5 %collective-permute-start.11 = (bf16[128,1024]{1,0:T(8,128)(2,1)S(1)}, bf16[128,1024]{1,0:T(8,128)(2,1)S(1)}, u32[]{:S(2)}, u32[]{:S(2)}) collective-permute-start(bf16[128,1024]{1,0:T(8,128)(2,1)S(1)} %collective-permute-done.8.refs_0_), channel_id=1, source_target_pairs={{0,4},{4,12},{12,8},{8,0},{1,5},{5,13},{13,9},{9,1},{2,6},{6,14},{... | collective-permute-start | bytes 786440 | tf_op jit(solution)/shard_map/ppermute | solution.py:318
  40.1 11.9 %collective-permute-start.10 = (bf16[144,1024]{1,0:T(8,128)(2,1)S(1)}, bf16[144,1024]{1,0:T(8,128)(2,1)S(1)}, u32[]{:S(2)}, u32[]{:S(2)}) collective-permute-start(bf16[144,1024]{1,0:T(8,128)(2,1)S(1)} %collective-permute-done.6.refs_2_), channel_id=1, source_target_pairs={{0,2},{2,0},{1,3},{3,1},{4,6},{6,4},{5,7},{7,5},{8,10},{10,8},{9,1... | collective-permute-start | bytes 884744 | tf_op jit(solution)/shard_map/ppermute | solution.py:284
  44.3 7.8 %collective-permute-start.13 = (bf16[128,1024]{1,0:T(8,128)(2,1)S(1)}, bf16[128,1024]{1,0:T(8,128)(2,1)S(1)}, u32[]{:S(2)}, u32[]{:S(2)}) collective-permute-start(bf16[128,1024]{1,0:T(8,128)(2,1)S(1)} %collective-permute-done.12.refs_1_), channel_id=1, source_target_pairs={{0,4},{4,12},{12,8},{8,0},{1,5},{5,13},{13,9},{9,1},{2,6},{6,14},{... | collective-permute-start | bytes 786440 | tf_op jit(solution)/shard_map/ppermute | solution.py:314
  45.9 11.0 %collective-permute-start.15 = (bf16[128,1024]{1,0:T(8,128)(2,1)S(1)}, bf16[128,1024]{1,0:T(8,128)(2,1)S(1)}, u32[]{:S(2)}, u32[]{:S(2)}) collective-permute-start(bf16[128,1024]{1,0:T(8,128)(2,1)S(1)} %get-tuple-element.223), channel_id=1, source_target_pairs={{0,2},{2,0},{1,3},{3,1},{4,6},{6,4},{5,7},{7,5},{8,10},{10,8},{9,1... | collective-permute-start | bytes 786440 | tf_op jit(solution)/shard_map/ppermute | solution.py:291
  51.1 10.2 %collective-permute-start.14 = (bf16[128,1024]{1,0:T(8,128)(2,1)S(1)}, bf16[128,1024]{1,0:T(8,128)(2,1)S(1)}, u32[]{:S(2)}, u32[]{:S(2)}) collective-permute-start(bf16[128,1024]{1,0:T(8,128)(2,1)S(1)} %get-tuple-element.193), channel_id=1, source_target_pairs={{0,2},{2,0},{1,3},{3,1},{4,6},{6,4},{5,7},{7,5},{8,10},{10,8},{9,1... | collective-permute-start | bytes 786440 | tf_op jit(solution)/shard_map/ppermute | solution.py:291
  55.7 9.9 %collective-permute-start.16 = (bf16[128,1024]{1,0:T(8,128)(2,1)S(1)}, bf16[128,1024]{1,0:T(8,128)(2,1)S(1)}, u32[]{:S(2)}, u32[]{:S(2)}) collective-permute-start(bf16[128,1024]{1,0:T(8,128)(2,1)S(1)} %get-tuple-element.219), channel_id=1, source_target_pairs={{0,2},{2,0},{1,3},{3,1},{4,6},{6,4},{5,7},{7,5},{8,10},{10,8},{9,1... | collective-permute-start | bytes 786440 | tf_op jit(solution)/shard_map/ppermute | solution.py:291
  61.4 9.3 %collective-permute-start.18 = (bf16[128,1024]{1,0:T(8,128)(2,1)S(1)}, bf16[128,1024]{1,0:T(8,128)(2,1)S(1)}, u32[]{:S(2)}, u32[]{:S(2)}) collective-permute-start(bf16[128,1024]{1,0:T(8,128)(2,1)S(1)} %add_convert_fusion.2), channel_id=1, source_target_pairs={{0,8},{4,0},{12,4},{8,12},{1,9},{5,1},{13,5},{9,13},{2,10},{6,2},{... | collective-permute-start | bytes 786440 | tf_op jit(solution)/shard_map/ppermute | solution.py:301
  63.7 10.5 %collective-permute-start.17 = (bf16[128,1024]{1,0:T(8,128)(2,1)S(1)}, bf16[128,1024]{1,0:T(8,128)(2,1)S(1)}, u32[]{:S(2)}, u32[]{:S(2)}) collective-permute-start(bf16[128,1024]{1,0:T(8,128)(2,1)S(1)} %add_convert_fusion.3), channel_id=1, source_target_pairs={{0,4},{4,12},{12,8},{8,0},{1,5},{5,13},{13,9},{9,1},{2,6},{6,14},{... | collective-permute-start | bytes 786440 | tf_op jit(solution)/shard_map/ppermute | solution.py:301
  74.1 5.7 %collective-permute-start.19 = (bf16[4,768,512]{2,1,0:T(8,128)(2,1)S(1)}, bf16[4,768,512]{2,1,0:T(8,128)(2,1)S(1)}, u32[]{:S(2)}, u32[]{:S(2)}) collective-permute-start(bf16[4,768,512]{2,1,0:T(8,128)(2,1)S(1)} %weight_grads.2), channel_id=1, source_target_pairs={{0,1},{1,0},{2,3},{3,2},{4,5},{5,4},{6,7},{7,6},{8,9},{9,8},{10,11... | collective-permute-start | bytes 9437192 | tf_op jit(solution)/shard_map/ppermute | solution.py:340
  74.2 9.7 %collective-permute-start.20 = (bf16[128,1024]{1,0:T(8,128)(2,1)S(1)}, bf16[128,1024]{1,0:T(8,128)(2,1)S(1)}, u32[]{:S(2)}, u32[]{:S(2)}) collective-permute-start(bf16[128,1024]{1,0:T(8,128)(2,1)S(1)} %add_convert_fusion.1), channel_id=1, source_target_pairs={{0,4},{4,12},{12,8},{8,0},{1,5},{5,13},{13,9},{9,1},{2,6},{6,14},{... | collective-permute-start | bytes 786440 | tf_op jit(solution)/shard_map/ppermute | solution.py:301
  75.5 8.4 %collective-permute-start.21 = (bf16[128,1024]{1,0:T(8,128)(2,1)S(1)}, bf16[128,1024]{1,0:T(8,128)(2,1)S(1)}, u32[]{:S(2)}, u32[]{:S(2)}) collective-permute-start(bf16[128,1024]{1,0:T(8,128)(2,1)S(1)} %get-tuple-element.253), channel_id=1, source_target_pairs={{0,2},{2,0},{1,3},{3,1},{4,6},{6,4},{5,7},{7,5},{8,10},{10,8},{9,1... | collective-permute-start | bytes 786440 | tf_op jit(solution)/shard_map/ppermute | solution.py:291

commit v17 on v16

--- a/solution.py
+++ b/solution.py
@@ -328,14 +328,15 @@
         sent[k] = homeward(group_sum(chunks[k][0], across(chunks[k][1])), k)
     chunks[last] = chunk(blocks[last])
     backs[last] = across(chunks[last][1])
-    chunks, backs[last - 1], backs[1] = tie(chunks, backs[last - 1], backs[1])
+    chunks, backs[1] = tie(chunks, backs[1])
 
     sent[1] = homeward(group_sum(chunks[1][0], backs[1]), 1)
     carried = homeward(group_sum(chunks[last - 1][0], backs[last - 1]), last)
     kept = [[chunks[k][i] for k in range(n_group)] for i in (-3, -2, -1)]
+    kept, backs[last - 1], sent = tie(kept, backs[last - 1], sent)
     to_send = weight_call(other_half, *kept)
     to_send, backs[last], other = tie(to_send, backs[last], chunks[0][1])
-    to_send, carried, sent = tie(to_send, carried, sent)
+    to_send, carried = tie(to_send, carried)
 
     got = lax.ppermute(to_send, "dp", [(0, 1), (1, 0)])
     sent[last] = homeward(group_sum(chunks[last][0], [*backs[last], carried]), last)

time: 85 us -> 81.6 us (0.960)
  waiting for transfers between devices: 32.3 us -> 29.2 us
    ppermute x3, waiting for transfers between devices: 9.92 us -> 6.79 us  [homeward(): return lax.ppermute(group_part, 'group', along(-k))]
    ppermute x1, waiting for transfers between devices: 2.82 us -> 3.85 us  [per_device(): got = lax.ppermute(to_send, 'dp', [(0, 1), (1, 0)])]
    ppermute x4, waiting for transfers between devices: 4.38 us -> 3.35 us  [across(): lax.ppermute(others[(s - 1) * tok_rows:s * tok_rows], 'ingroup', shift(-s))]
  transfers between devices with their start and end apart: 22 -> 22, of which waited for: 15 -> 15; matrix products, arithmetic and copies ran while one was open for 0% -> 0% of each run, Pallas kernels for 26% -> 27%
where the time goes in v17:
time: 81.6 us; the launch traced here: 81.4 us
  waiting for transfers between devices  29.2 us (36%)
  starting transfers between devices  26.4 us (32%)
  Pallas kernels  23.9 us (29%)
  other arithmetic  1.13 us (1%)
    pallas_call x4, Pallas kernels, chunk_call(): pl.pallas_call(functools.partial(chunk_kernel, n_blocks, tok_rows, capaci...  14.7 us
    ppermute x6, waiting for transfers between devices, per_device(): lax.ppermute(v, 'group', along(1))  10.6 us
    ppermute x6, starting transfers between devices, per_device(): lax.ppermute(v, 'group', along(1))  10.1 us
    ppermute x3, waiting for transfers between devices, homeward(): return lax.ppermute(group_part, 'group', along(-k))  6.79 us
    ppermute x7, starting transfers between devices, spread(): lax.ppermute(column, 'ingroup', shift(s))  6.68 us
    ppermute x4, starting transfers between devices, across(): lax.ppermute(others[(s - 1) * tok_rows:s * tok_rows], 'ingroup', shift(-s))  4.91 us
    pallas_call x2, Pallas kernels, weight_call(): pl.pallas_call(functools.partial(kernel, n), in_specs=[smem] + [vmem] * l...  4.57 us
    ppermute x7, waiting for transfers between devices, spread(): lax.ppermute(column, 'ingroup', shift(s))  4.24 us
  transfers between devices with their start and end apart: 22, of which 15 were waited for; matrix products, arithmetic and copies ran while one was open for 0% of the time, Pallas kernels for 27%

profile of v17, /device:TPU:0, one launch (start us, length us, event | category | flops | bytes accessed | tf_op | source)
XLA Modules:
  0.0 81.4 jit_solution(1048377708843500202)
XLA Ops:
  0.6 1.8 %pack.1 = (bf16[128,1024]{1,0:T(8,128)(2,1)S(1)}, bf16[144,1024]{1,0:T(8,128)(2,1)S(1)}) custom-call(bf16[128,1024]{1,0:T(8,128)(2,1)} %tokens, bf16[128,1024]{1,0:T(8,128)(2,1)} %upstream.1, s32[8,128]{1,0:T(8,128)} %bitcast.5, s32[8,128]{1,0:T(8,128)} %bitcast.6, s32[8,128]{1,0:T(8,128)} %bitcast.7), custom_call_target="tpu_custom_call" | custom-call | bytes 1048576 | tf_op jit(solution)/shard_map/pack/pallas_call | solution.py:58
  2.4 3.0 %collective-permute-start.1 = (bf16[144,1024]{1,0:T(8,128)(2,1)S(1)}, bf16[144,1024]{1,0:T(8,128)(2,1)S(1)}, u32[]{:S(2)}, u32[]{:S(2)}) collective-permute-start(bf16[144,1024]{1,0:T(8,128)(2,1)S(1)} %get-tuple-element.153.refs_2_), channel_id=1, source_target_pairs={{0,2},{2,0},{1,3},{3,1},{4,6},{6,4},{5,7},{7,5},{8,10},{10,8},{9,1... | collective-permute-start | bytes 884744 | tf_op jit(solution)/shard_map/ppermute | solution.py:284
  5.4 1.6 %collective-permute-start = (bf16[144,1024]{1,0:T(8,128)(2,1)S(1)}, bf16[144,1024]{1,0:T(8,128)(2,1)S(1)}, u32[]{:S(2)}, u32[]{:S(2)}) collective-permute-start(bf16[144,1024]{1,0:T(8,128)(2,1)S(1)} %get-tuple-element.153.refs_2_), channel_id=1, source_target_pairs={{0,4},{4,12},{12,8},{8,0},{1,5},{5,13},{13,9},{9,1},{2,6},{6,14},{... | collective-permute-start | bytes 884744 | tf_op jit(solution)/shard_map/ppermute | solution.py:318
  7.0 0.5 collective-permute-start.5
  7.5 2.6 %collective-permute-start.4 = (bf16[128,1024]{1,0:T(8,128)(2,1)}, bf16[128,1024]{1,0:T(8,128)(2,1)S(1)}, u32[]{:S(2)}, u32[]{:S(2)}) collective-permute-start(bf16[128,1024]{1,0:T(8,128)(2,1)} %tokens), channel_id=1, source_target_pairs={{0,4},{4,12},{12,8},{8,0},{1,5},{5,13},{13,9},{9,1},{2,6},{6,14},{... | collective-permute-start | bytes 786440 | tf_op jit(solution)/shard_map/ppermute | solution.py:318
  10.1 2.9 %load.1 = (bf16[4,1024,256]{2,1,0:T(8,128)(2,1)S(1)}, bf16[4,1024,256]{2,1,0:T(8,128)(2,1)S(1)}, bf16[4,256,1024]{2,1,0:T(8,128)(2,1)S(1)}) custom-call(bf16[4,1024,256]{2,1,0:T(8,128)(2,1)} %refs_0_.1, bf16[4,1024,256]{2,1,0:T(8,128)(2,1)} %refs_1_.1, bf16[4,256,1024]{2,1,0:T(8,128)(2,1)} %refs_2_.1), custom_call_target="tpu_custom_call" | custom-call | bytes 12582912 | tf_op jit(solution)/shard_map/load/pallas_call | solution.py:99
  13.0 0.2 collective-permute-done.1.refs_3_
  13.3 3.0 %collective-permute-done.refs_2_ = bf16[144,1024]{1,0:T(8,128)(2,1)S(1)} collective-permute-done((bf16[144,1024]{1,0:T(8,128)(2,1)S(1)}, bf16[144,1024]{1,0:T(8,128)(2,1)S(1)}, u32[]{:S(2)}, u32[]{:S(2)}) %collective-permute-start) | collective-permute-done | bytes 294944 | tf_op jit(solution)/shard_map/ppermute | solution.py:318
  16.3 0.2 collective-permute-start.3
  16.4 1.2 %collective-permute-start.2 = (bf16[144,1024]{1,0:T(8,128)(2,1)S(1)}, bf16[144,1024]{1,0:T(8,128)(2,1)S(1)}, u32[]{:S(2)}, u32[]{:S(2)}) collective-permute-start(bf16[144,1024]{1,0:T(8,128)(2,1)S(1)} %collective-permute-done.refs_2_), channel_id=1, source_target_pairs={{0,4},{4,12},{12,8},{8,0},{1,5},{5,13},{13,9},{9,1},{2,6},{6,14},{... | collective-permute-start | bytes 884744 | tf_op jit(solution)/shard_map/ppermute | solution.py:318
  17.6 1.3 %collective-permute-done.5.refs_1_ = bf16[128,1024]{1,0:T(8,128)(2,1)S(1)} collective-permute-done((bf16[128,1024]{1,0:T(8,128)(2,1)}, bf16[128,1024]{1,0:T(8,128)(2,1)S(1)}, u32[]{:S(2)}, u32[]{:S(2)}) %collective-permute-start.5) | collective-permute-done | bytes 262176 | tf_op jit(solution)/shard_map/ppermute | solution.py:284
  18.9 3.0 %collective-permute-done.4.refs_0_ = bf16[128,1024]{1,0:T(8,128)(2,1)S(1)} collective-permute-done((bf16[128,1024]{1,0:T(8,128)(2,1)}, bf16[128,1024]{1,0:T(8,128)(2,1)S(1)}, u32[]{:S(2)}, u32[]{:S(2)}) %collective-permute-start.4) | collective-permute-done | bytes 262176 | tf_op jit(solution)/shard_map/ppermute | solution.py:318
  21.9 0.2 collective-permute-start.9
  22.0 1.3 %collective-permute-start.8 = (bf16[128,1024]{1,0:T(8,128)(2,1)S(1)}, bf16[128,1024]{1,0:T(8,128)(2,1)S(1)}, u32[]{:S(2)}, u32[]{:S(2)}) collective-permute-start(bf16[128,1024]{1,0:T(8,128)(2,1)S(1)} %collective-permute-done.4.refs_0_), channel_id=1, source_target_pairs={{0,4},{4,12},{12,8},{8,0},{1,5},{5,13},{13,9},{9,1},{2,6},{6,14},{... | collective-permute-start | bytes 786440 | tf_op jit(solution)/shard_map/ppermute | solution.py:318
  23.3 3.7 %chunk.4 = (bf16[128,1024]{1,0:T(8,128)(2,1)S(1)}, bf16[128,1024]{1,0:T(8,128)(2,1)S(1)}, bf16[4,96,1024]{2,1,0:T(8,128)(2,1)S(1)}, bf16[4,96,1024]{2,1,0:T(8,128)(2,1)S(1)}, bf16[4,96,768]{2,1,0:T(8,128)(2,1)S(1)}) custom-call(s32[1]{0:T(128)} %bitcast.first_ref, bf16[128,1024]{1,0:T(8,128)(2,1)S(1)} %get-tuple-element.151.refs_0_, ...), custom_call_target="tpu_custom_call" | custom-call | flops 1610612736 | bytes 8388608 | tf_op jit(solution)/shard_map/chunk/pallas_call | solution.py:175
  27.0 0.0 collective-permute-done.3.refs_3_
  27.0 1.2 %collective-permute-done.2.refs_2_ = bf16[144,1024]{1,0:T(8,128)(2,1)S(1)} collective-permute-done((bf16[144,1024]{1,0:T(8,128)(2,1)S(1)}, bf16[144,1024]{1,0:T(8,128)(2,1)S(1)}, u32[]{:S(2)}, u32[]{:S(2)}) %collective-permute-start.2) | collective-permute-done | bytes 294944 | tf_op jit(solution)/shard_map/ppermute | solution.py:318
  28.2 0.9 %collective-permute-start.7 = (bf16[144,1024]{1,0:T(8,128)(2,1)S(1)}, bf16[144,1024]{1,0:T(8,128)(2,1)S(1)}, u32[]{:S(2)}, u32[]{:S(2)}) collective-permute-start(bf16[144,1024]{1,0:T(8,128)(2,1)S(1)} %collective-permute-done.2.refs_2_), channel_id=1, source_target_pairs={{0,2},{2,0},{1,3},{3,1},{4,6},{6,4},{5,7},{7,5},{8,10},{10,8},{9,1... | collective-permute-start | bytes 884744 | tf_op jit(solution)/shard_map/ppermute | solution.py:284
  29.1 2.7 %collective-permute-start.6 = (bf16[144,1024]{1,0:T(8,128)(2,1)S(1)}, bf16[144,1024]{1,0:T(8,128)(2,1)S(1)}, u32[]{:S(2)}, u32[]{:S(2)}) collective-permute-start(bf16[144,1024]{1,0:T(8,128)(2,1)S(1)} %collective-permute-done.2.refs_2_), channel_id=1, source_target_pairs={{0,4},{4,12},{12,8},{8,0},{1,5},{5,13},{13,9},{9,1},{2,6},{6,14},{... | collective-permute-start | bytes 884744 | tf_op jit(solution)/shard_map/ppermute | solution.py:318
  31.8 0.0 collective-permute-done.9.refs_1_
  31.8 2.0 %collective-permute-done.8.refs_0_ = bf16[128,1024]{1,0:T(8,128)(2,1)S(1)} collective-permute-done((bf16[128,1024]{1,0:T(8,128)(2,1)S(1)}, bf16[128,1024]{1,0:T(8,128)(2,1)S(1)}, u32[]{:S(2)}, u32[]{:S(2)}) %collective-permute-start.8) | collective-permute-done | bytes 262176 | tf_op jit(solution)/shard_map/ppermute | solution.py:318
  33.8 0.9 %collective-permute-start.12 = (bf16[128,1024]{1,0:T(8,128)(2,1)S(1)}, bf16[128,1024]{1,0:T(8,128)(2,1)S(1)}, u32[]{:S(2)}, u32[]{:S(2)}) collective-permute-start(bf16[128,1024]{1,0:T(8,128)(2,1)S(1)} %collective-permute-done.8.refs_0_), channel_id=1, source_target_pairs={{0,2},{2,0},{1,3},{3,1},{4,6},{6,4},{5,7},{7,5},{8,10},{10,8},{9,1... | collective-permute-start | bytes 786440 | tf_op jit(solution)/shard_map/ppermute | solution.py:284
  34.7 0.8 collective-permute-start.11
  35.5 3.7 %chunk.5 = (bf16[128,1024]{1,0:T(8,128)(2,1)S(1)}, bf16[128,1024]{1,0:T(8,128)(2,1)S(1)}, bf16[4,96,1024]{2,1,0:T(8,128)(2,1)S(1)}, bf16[4,96,1024]{2,1,0:T(8,128)(2,1)S(1)}, bf16[4,96,768]{2,1,0:T(8,128)(2,1)S(1)}) custom-call(s32[1]{0:T(128)} %bitcast.first_ref, bf16[128,1024]{1,0:T(8,128)(2,1)S(1)} %collective-permute-done.4.refs_0_, ...), custom_call_target="tpu_custom_call" | custom-call | flops 1610612736 | bytes 8388608 | tf_op jit(solution)/shard_map/chunk/pallas_call | solution.py:175
  39.2 0.0 collective-permute-done.7.refs_3_
  39.2 0.9 %collective-permute-done.6.refs_2_ = bf16[144,1024]{1,0:T(8,128)(2,1)S(1)} collective-permute-done((bf16[144,1024]{1,0:T(8,128)(2,1)S(1)}, bf16[144,1024]{1,0:T(8,128)(2,1)S(1)}, u32[]{:S(2)}, u32[]{:S(2)}) %collective-permute-start.6) | collective-permute-done | bytes 294944 | tf_op jit(solution)/shard_map/ppermute | solution.py:318
  40.1 0.9 %collective-permute-start.10 = (bf16[144,1024]{1,0:T(8,128)(2,1)S(1)}, bf16[144,1024]{1,0:T(8,128)(2,1)S(1)}, u32[]{:S(2)}, u32[]{:S(2)}) collective-permute-start(bf16[144,1024]{1,0:T(8,128)(2,1)S(1)} %collective-permute-done.6.refs_2_), channel_id=1, source_target_pairs={{0,2},{2,0},{1,3},{3,1},{4,6},{6,4},{5,7},{7,5},{8,10},{10,8},{9,1... | collective-permute-start | bytes 884744 | tf_op jit(solution)/shard_map/ppermute | solution.py:284
  41.1 2.7 %collective-permute-done.12.refs_1_ = bf16[128,1024]{1,0:T(8,128)(2,1)S(1)} collective-permute-done((bf16[128,1024]{1,0:T(8,128)(2,1)S(1)}, bf16[128,1024]{1,0:T(8,128)(2,1)S(1)}, u32[]{:S(2)}, u32[]{:S(2)}) %collective-permute-start.12) | collective-permute-done | bytes 262176 | tf_op jit(solution)/shard_map/ppermute | solution.py:284
  43.8 0.5 collective-permute-done.11.refs_0_
  44.3 1.6 %collective-permute-start.13 = (bf16[128,1024]{1,0:T(8,128)(2,1)S(1)}, bf16[128,1024]{1,0:T(8,128)(2,1)S(1)}, u32[]{:S(2)}, u32[]{:S(2)}) collective-permute-start(bf16[128,1024]{1,0:T(8,128)(2,1)S(1)} %collective-permute-done.12.refs_1_), channel_id=1, source_target_pairs={{0,4},{4,12},{12,8},{8,0},{1,5},{5,13},{13,9},{9,1},{2,6},{6,14},{... | collective-permute-start | bytes 786440 | tf_op jit(solution)/shard_map/ppermute | solution.py:314
  45.9 1.5 %collective-permute-start.14 = (bf16[128,1024]{1,0:T(8,128)(2,1)S(1)}, bf16[128,1024]{1,0:T(8,128)(2,1)S(1)}, u32[]{:S(2)}, u32[]{:S(2)}) collective-permute-start(bf16[128,1024]{1,0:T(8,128)(2,1)S(1)} %get-tuple-element.234), channel_id=1, source_target_pairs={{0,2},{2,0},{1,3},{3,1},{4,6},{6,4},{5,7},{7,5},{8,10},{10,8},{9,1... | collective-permute-start | bytes 786440 | tf_op jit(solution)/shard_map/ppermute | solution.py:291
  47.4 3.7 %chunk.6 = (bf16[128,1024]{1,0:T(8,128)(2,1)S(1)}, bf16[128,1024]{1,0:T(8,128)(2,1)S(1)}, bf16[4,96,1024]{2,1,0:T(8,128)(2,1)S(1)}, bf16[4,96,1024]{2,1,0:T(8,128)(2,1)S(1)}, bf16[4,96,768]{2,1,0:T(8,128)(2,1)S(1)}) custom-call(s32[1]{0:T(128)} %bitcast.first_ref, bf16[128,1024]{1,0:T(8,128)(2,1)S(1)} %collective-permute-done.8.refs_0_, ...), custom_call_target="tpu_custom_call" | custom-call | flops 1610612736 | bytes 8388608 | tf_op jit(solution)/shard_map/chunk/pallas_call | solution.py:175
  51.1 0.6 collective-permute-start.15
  51.7 0.3 collective-permute-done.13.refs_1_
  52.0 0.0 collective-permute-done.10.refs_3_
  52.0 3.7 %chunk.7 = (bf16[128,1024]{1,0:T(8,128)(2,1)S(1)}, bf16[128,1024]{1,0:T(8,128)(2,1)S(1)}, bf16[4,96,1024]{2,1,0:T(8,128)(2,1)S(1)}, bf16[4,96,1024]{2,1,0:T(8,128)(2,1)S(1)}, bf16[4,96,768]{2,1,0:T(8,128)(2,1)S(1)}) custom-call(s32[1]{0:T(128)} %bitcast.first_ref, bf16[128,1024]{1,0:T(8,128)(2,1)S(1)} %collective-permute-done.11.refs_0_, ...), custom_call_target="tpu_custom_call" | custom-call | flops 1610612736 | bytes 8388608 | tf_op jit(solution)/shard_map/chunk/pallas_call | solution.py:175
  55.7 1.2 %collective-permute-start.17 = (bf16[128,1024]{1,0:T(8,128)(2,1)S(1)}, bf16[128,1024]{1,0:T(8,128)(2,1)S(1)}, u32[]{:S(2)}, u32[]{:S(2)}) collective-permute-start(bf16[128,1024]{1,0:T(8,128)(2,1)S(1)} %get-tuple-element.230), channel_id=1, source_target_pairs={{0,2},{2,0},{1,3},{3,1},{4,6},{6,4},{5,7},{7,5},{8,10},{10,8},{9,1... | collective-permute-start | bytes 786440 | tf_op jit(solution)/shard_map/ppermute | solution.py:291
  56.9 0.0 collective-permute-done.14
  56.9 0.1 add_convert_fusion.3
  57.0 1.0 %collective-permute-start.16 = (bf16[128,1024]{1,0:T(8,128)(2,1)S(1)}, bf16[128,1024]{1,0:T(8,128)(2,1)S(1)}, u32[]{:S(2)}, u32[]{:S(2)}) collective-permute-start(bf16[128,1024]{1,0:T(8,128)(2,1)S(1)} %add_convert_fusion.3), channel_id=1, source_target_pairs={{0,8},{4,0},{12,4},{8,12},{1,9},{5,1},{13,5},{9,13},{2,10},{6,2},{... | collective-permute-start | bytes 786440 | tf_op jit(solution)/shard_map/ppermute | solution.py:301
  58.0 3.3 %collective-permute-done.15 = bf16[128,1024]{1,0:T(8,128)(2,1)S(1)} collective-permute-done((bf16[128,1024]{1,0:T(8,128)(2,1)S(1)}, bf16[128,1024]{1,0:T(8,128)(2,1)S(1)}, u32[]{:S(2)}, u32[]{:S(2)}) %collective-permute-start.15) | collective-permute-done | bytes 262176 | tf_op jit(solution)/shard_map/ppermute | solution.py:291
  61.3 0.1 add_convert_fusion.2
  61.4 2.1 %collective-permute-start.18 = (bf16[128,1024]{1,0:T(8,128)(2,1)S(1)}, bf16[128,1024]{1,0:T(8,128)(2,1)S(1)}, u32[]{:S(2)}, u32[]{:S(2)}) collective-permute-start(bf16[128,1024]{1,0:T(8,128)(2,1)S(1)} %add_convert_fusion.2), channel_id=1, source_target_pairs={{0,4},{4,12},{12,8},{8,0},{1,5},{5,13},{13,9},{9,1},{2,6},{6,14},{... | collective-permute-start | bytes 786440 | tf_op jit(solution)/shard_map/ppermute | solution.py:301
  63.4 0.7 collective-permute-done.16
  64.1 1.9 %weight_grads.2 = bf16[4,768,512]{2,1,0:T(8,128)(2,1)S(1)} custom-call(s32[1]{0:T(128)S(6)} %sub.3.side_ref, bf16[4,96,1024]{2,1,0:T(8,128)(2,1)S(1)} %get-tuple-element.251.refs_0_, bf16[4,96,1024]{2,1,0:T(8,128)(2,1)S(1)} %get-tuple-element.252.refs_1_, bf16[4,96,1024]{2,1,0:T(8,128)(2,1)S(1)} %get-tuple-element.253.refs_2_, ...), custom_call_target="tpu_custom_call" | custom-call | flops 1207959552 | bytes 8650752 | tf_op jit(solution)/shard_map/weight_grads/pallas_call | solution.py:248
  66.0 0.0 collective-permute-done.17
  66.0 4.7 %collective-permute-done.18 = bf16[128,1024]{1,0:T(8,128)(2,1)S(1)} collective-permute-done((bf16[128,1024]{1,0:T(8,128)(2,1)S(1)}, bf16[128,1024]{1,0:T(8,128)(2,1)S(1)}, u32[]{:S(2)}, u32[]{:S(2)}) %collective-permute-start.18) | collective-permute-done | bytes 262176 | tf_op jit(solution)/shard_map/ppermute | solution.py:301
  70.7 0.0 collective-permute-start.19
  70.7 0.1 add_convert_fusion.1
  70.8 0.1 collective-permute-start.20
  70.9 1.6 %collective-permute-start.21 = (bf16[128,1024]{1,0:T(8,128)(2,1)S(1)}, bf16[128,1024]{1,0:T(8,128)(2,1)S(1)}, u32[]{:S(2)}, u32[]{:S(2)}) collective-permute-start(bf16[128,1024]{1,0:T(8,128)(2,1)S(1)} %get-tuple-element.275), channel_id=1, source_target_pairs={{0,2},{2,0},{1,3},{3,1},{4,6},{6,4},{5,7},{7,5},{8,10},{10,8},{9,1... | collective-permute-start | bytes 786440 | tf_op jit(solution)/shard_map/ppermute | solution.py:291
  72.5 3.9 %collective-permute-done.19.refs_12_ = bf16[4,768,512]{2,1,0:T(8,128)(2,1)S(1)} collective-permute-done((bf16[4,768,512]{2,1,0:T(8,128)(2,1)S(1)}, bf16[4,768,512]{2,1,0:T(8,128)(2,1)S(1)}, u32[]{:S(2)}, u32[]{:S(2)}) %collective-permute-start.19) | collective-permute-done | bytes 3145760 | tf_op jit(solution)/shard_map/ppermute | solution.py:341
  76.3 2.7 %weight_grads.3 = (bf16[4,512,256]{2,1,0:T(8,128)(2,1)}, bf16[4,512,256]{2,1,0:T(8,128)(2,1)}, bf16[4,256,512]{2,1,0:T(8,128)(2,1)}) custom-call(s32[1]{0:T(128)} %bitcast.1.side_ref, bf16[4,96,1024]{2,1,0:T(8,128)(2,1)S(1)} %get-tuple-element.251.refs_0_, bf16[4,96,1024]{2,1,0:T(8,128)(2,1)S(1)} %get-tuple-element.252.refs_1_, ...), custom_call_target="tpu_custom_call" | custom-call | flops 1207959552 | bytes 8650752 | tf_op jit(solution)/shard_map/weight_grads/pallas_call | solution.py:248
  79.0 1.4 %collective-permute-done.20 = bf16[128,1024]{1,0:T(8,128)(2,1)S(1)} collective-permute-done((bf16[128,1024]{1,0:T(8,128)(2,1)S(1)}, bf16[128,1024]{1,0:T(8,128)(2,1)S(1)}, u32[]{:S(2)}, u32[]{:S(2)}) %collective-permute-start.20) | collective-permute-done | bytes 262176 | tf_op jit(solution)/shard_map/ppermute | solution.py:301
  80.5 0.0 collective-permute-done.21
  80.5 0.9 %add_convert_fusion = bf16[128,1024]{1,0:T(8,128)(2,1)} fusion(bf16[128,1024]{1,0:T(8,128)(2,1)S(1)} %collective-permute-done.20, bf16[128,1024]{1,0:T(8,128)(2,1)S(1)} %collective-permute-done.16, bf16[128,1024]{1,0:T(8,128)(2,1)S(1)} %collective-permute-done.21, bf16[128,1024]{1,0:T(8,128)(2,1)S(1)} %get-tuple-element.235), kind=kLoop, calls=%fused_computation | loop fusion | flops 1048576 | bytes 1310720 | tf_op jit(solution)/shard_map/convert_element_type | solution.py:351
Async XLA Ops:
  2.4 10.8 %collective-permute-start.1 = (bf16[144,1024]{1,0:T(8,128)(2,1)S(1)}, bf16[144,1024]{1,0:T(8,128)(2,1)S(1)}, u32[]{:S(2)}, u32[]{:S(2)}) collective-permute-start(bf16[144,1024]{1,0:T(8,128)(2,1)S(1)} %get-tuple-element.153.refs_2_), channel_id=1, source_target_pairs={{0,2},{2,0},{1,3},{3,1},{4,6},{6,4},{5,7},{7,5},{8,10},{10,8},{9,1... | collective-permute-start | bytes 884744 | tf_op jit(solution)/shard_map/ppermute | solution.py:284
  5.4 10.8 %collective-permute-start = (bf16[144,1024]{1,0:T(8,128)(2,1)S(1)}, bf16[144,1024]{1,0:T(8,128)(2,1)S(1)}, u32[]{:S(2)}, u32[]{:S(2)}) collective-permute-start(bf16[144,1024]{1,0:T(8,128)(2,1)S(1)} %get-tuple-element.153.refs_2_), channel_id=1, source_target_pairs={{0,4},{4,12},{12,8},{8,0},{1,5},{5,13},{13,9},{9,1},{2,6},{6,14},{... | collective-permute-start | bytes 884744 | tf_op jit(solution)/shard_map/ppermute | solution.py:318
  7.0 11.9 %collective-permute-start.5 = (bf16[128,1024]{1,0:T(8,128)(2,1)}, bf16[128,1024]{1,0:T(8,128)(2,1)S(1)}, u32[]{:S(2)}, u32[]{:S(2)}) collective-permute-start(bf16[128,1024]{1,0:T(8,128)(2,1)} %tokens), channel_id=1, source_target_pairs={{0,2},{2,0},{1,3},{3,1},{4,6},{6,4},{5,7},{7,5},{8,10},{10,8},{9,1... | collective-permute-start | bytes 786440 | tf_op jit(solution)/shard_map/ppermute | solution.py:284
  7.5 14.3 %collective-permute-start.4 = (bf16[128,1024]{1,0:T(8,128)(2,1)}, bf16[128,1024]{1,0:T(8,128)(2,1)S(1)}, u32[]{:S(2)}, u32[]{:S(2)}) collective-permute-start(bf16[128,1024]{1,0:T(8,128)(2,1)} %tokens), channel_id=1, source_target_pairs={{0,4},{4,12},{12,8},{8,0},{1,5},{5,13},{13,9},{9,1},{2,6},{6,14},{... | collective-permute-start | bytes 786440 | tf_op jit(solution)/shard_map/ppermute | solution.py:318
  16.3 10.7 %collective-permute-start.3 = (bf16[144,1024]{1,0:T(8,128)(2,1)S(1)}, bf16[144,1024]{1,0:T(8,128)(2,1)S(1)}, u32[]{:S(2)}, u32[]{:S(2)}) collective-permute-start(bf16[144,1024]{1,0:T(8,128)(2,1)S(1)} %collective-permute-done.refs_2_), channel_id=1, source_target_pairs={{0,2},{2,0},{1,3},{3,1},{4,6},{6,4},{5,7},{7,5},{8,10},{10,8},{9,1... | collective-permute-start | bytes 884744 | tf_op jit(solution)/shard_map/ppermute | solution.py:284
  16.4 11.8 %collective-permute-start.2 = (bf16[144,1024]{1,0:T(8,128)(2,1)S(1)}, bf16[144,1024]{1,0:T(8,128)(2,1)S(1)}, u32[]{:S(2)}, u32[]{:S(2)}) collective-permute-start(bf16[144,1024]{1,0:T(8,128)(2,1)S(1)} %collective-permute-done.refs_2_), channel_id=1, source_target_pairs={{0,4},{4,12},{12,8},{8,0},{1,5},{5,13},{13,9},{9,1},{2,6},{6,14},{... | collective-permute-start | bytes 884744 | tf_op jit(solution)/shard_map/ppermute | solution.py:318
  21.9 10.0 %collective-permute-start.9 = (bf16[128,1024]{1,0:T(8,128)(2,1)S(1)}, bf16[128,1024]{1,0:T(8,128)(2,1)S(1)}, u32[]{:S(2)}, u32[]{:S(2)}) collective-permute-start(bf16[128,1024]{1,0:T(8,128)(2,1)S(1)} %collective-permute-done.4.refs_0_), channel_id=1, source_target_pairs={{0,2},{2,0},{1,3},{3,1},{4,6},{6,4},{5,7},{7,5},{8,10},{10,8},{9,1... | collective-permute-start | bytes 786440 | tf_op jit(solution)/shard_map/ppermute | solution.py:284
  22.0 11.8 %collective-permute-start.8 = (bf16[128,1024]{1,0:T(8,128)(2,1)S(1)}, bf16[128,1024]{1,0:T(8,128)(2,1)S(1)}, u32[]{:S(2)}, u32[]{:S(2)}) collective-permute-start(bf16[128,1024]{1,0:T(8,128)(2,1)S(1)} %collective-permute-done.4.refs_0_), channel_id=1, source_target_pairs={{0,4},{4,12},{12,8},{8,0},{1,5},{5,13},{13,9},{9,1},{2,6},{6,14},{... | collective-permute-start | bytes 786440 | tf_op jit(solution)/shard_map/ppermute | solution.py:318
  28.2 11.0 %collective-permute-start.7 = (bf16[144,1024]{1,0:T(8,128)(2,1)S(1)}, bf16[144,1024]{1,0:T(8,128)(2,1)S(1)}, u32[]{:S(2)}, u32[]{:S(2)}) collective-permute-start(bf16[144,1024]{1,0:T(8,128)(2,1)S(1)} %collective-permute-done.2.refs_2_), channel_id=1, source_target_pairs={{0,2},{2,0},{1,3},{3,1},{4,6},{6,4},{5,7},{7,5},{8,10},{10,8},{9,1... | collective-permute-start | bytes 884744 | tf_op jit(solution)/shard_map/ppermute | solution.py:284
  29.1 11.0 %collective-permute-start.6 = (bf16[144,1024]{1,0:T(8,128)(2,1)S(1)}, bf16[144,1024]{1,0:T(8,128)(2,1)S(1)}, u32[]{:S(2)}, u32[]{:S(2)}) collective-permute-start(bf16[144,1024]{1,0:T(8,128)(2,1)S(1)} %collective-permute-done.2.refs_2_), channel_id=1, source_target_pairs={{0,4},{4,12},{12,8},{8,0},{1,5},{5,13},{13,9},{9,1},{2,6},{6,14},{... | collective-permute-start | bytes 884744 | tf_op jit(solution)/shard_map/ppermute | solution.py:318
  33.8 9.9 %collective-permute-start.12 = (bf16[128,1024]{1,0:T(8,128)(2,1)S(1)}, bf16[128,1024]{1,0:T(8,128)(2,1)S(1)}, u32[]{:S(2)}, u32[]{:S(2)}) collective-permute-start(bf16[128,1024]{1,0:T(8,128)(2,1)S(1)} %collective-permute-done.8.refs_0_), channel_id=1, source_target_pairs={{0,2},{2,0},{1,3},{3,1},{4,6},{6,4},{5,7},{7,5},{8,10},{10,8},{9,1... | collective-permute-start | bytes 786440 | tf_op jit(solution)/shard_map/ppermute | solution.py:284
  34.7 9.5 %collective-permute-start.11 = (bf16[128,1024]{1,0:T(8,128)(2,1)S(1)}, bf16[128,1024]{1,0:T(8,128)(2,1)S(1)}, u32[]{:S(2)}, u32[]{:S(2)}) collective-permute-start(bf16[128,1024]{1,0:T(8,128)(2,1)S(1)} %collective-permute-done.8.refs_0_), channel_id=1, source_target_pairs={{0,4},{4,12},{12,8},{8,0},{1,5},{5,13},{13,9},{9,1},{2,6},{6,14},{... | collective-permute-start | bytes 786440 | tf_op jit(solution)/shard_map/ppermute | solution.py:318
  40.1 11.9 %collective-permute-start.10 = (bf16[144,1024]{1,0:T(8,128)(2,1)S(1)}, bf16[144,1024]{1,0:T(8,128)(2,1)S(1)}, u32[]{:S(2)}, u32[]{:S(2)}) collective-permute-start(bf16[144,1024]{1,0:T(8,128)(2,1)S(1)} %collective-permute-done.6.refs_2_), channel_id=1, source_target_pairs={{0,2},{2,0},{1,3},{3,1},{4,6},{6,4},{5,7},{7,5},{8,10},{10,8},{9,1... | collective-permute-start | bytes 884744 | tf_op jit(solution)/shard_map/ppermute | solution.py:284
  44.3 7.8 %collective-permute-start.13 = (bf16[128,1024]{1,0:T(8,128)(2,1)S(1)}, bf16[128,1024]{1,0:T(8,128)(2,1)S(1)}, u32[]{:S(2)}, u32[]{:S(2)}) collective-permute-start(bf16[128,1024]{1,0:T(8,128)(2,1)S(1)} %collective-permute-done.12.refs_1_), channel_id=1, source_target_pairs={{0,4},{4,12},{12,8},{8,0},{1,5},{5,13},{13,9},{9,1},{2,6},{6,14},{... | collective-permute-start | bytes 786440 | tf_op jit(solution)/shard_map/ppermute | solution.py:314
  45.9 11.0 %collective-permute-start.14 = (bf16[128,1024]{1,0:T(8,128)(2,1)S(1)}, bf16[128,1024]{1,0:T(8,128)(2,1)S(1)}, u32[]{:S(2)}, u32[]{:S(2)}) collective-permute-start(bf16[128,1024]{1,0:T(8,128)(2,1)S(1)} %get-tuple-element.234), channel_id=1, source_target_pairs={{0,2},{2,0},{1,3},{3,1},{4,6},{6,4},{5,7},{7,5},{8,10},{10,8},{9,1... | collective-permute-start | bytes 786440 | tf_op jit(solution)/shard_map/ppermute | solution.py:291
  51.1 10.2 %collective-permute-start.15 = (bf16[128,1024]{1,0:T(8,128)(2,1)S(1)}, bf16[128,1024]{1,0:T(8,128)(2,1)S(1)}, u32[]{:S(2)}, u32[]{:S(2)}) collective-permute-start(bf16[128,1024]{1,0:T(8,128)(2,1)S(1)} %get-tuple-element.204), channel_id=1, source_target_pairs={{0,2},{2,0},{1,3},{3,1},{4,6},{6,4},{5,7},{7,5},{8,10},{10,8},{9,1... | collective-permute-start | bytes 786440 | tf_op jit(solution)/shard_map/ppermute | solution.py:291
  55.7 10.3 %collective-permute-start.17 = (bf16[128,1024]{1,0:T(8,128)(2,1)S(1)}, bf16[128,1024]{1,0:T(8,128)(2,1)S(1)}, u32[]{:S(2)}, u32[]{:S(2)}) collective-permute-start(bf16[128,1024]{1,0:T(8,128)(2,1)S(1)} %get-tuple-element.230), channel_id=1, source_target_pairs={{0,2},{2,0},{1,3},{3,1},{4,6},{6,4},{5,7},{7,5},{8,10},{10,8},{9,1... | collective-permute-start | bytes 786440 | tf_op jit(solution)/shard_map/ppermute | solution.py:291
  57.0 7.1 %collective-permute-start.16 = (bf16[128,1024]{1,0:T(8,128)(2,1)S(1)}, bf16[128,1024]{1,0:T(8,128)(2,1)S(1)}, u32[]{:S(2)}, u32[]{:S(2)}) collective-permute-start(bf16[128,1024]{1,0:T(8,128)(2,1)S(1)} %add_convert_fusion.3), channel_id=1, source_target_pairs={{0,8},{4,0},{12,4},{8,12},{1,9},{5,1},{13,5},{9,13},{2,10},{6,2},{... | collective-permute-start | bytes 786440 | tf_op jit(solution)/shard_map/ppermute | solution.py:301
  61.4 9.3 %collective-permute-start.18 = (bf16[128,1024]{1,0:T(8,128)(2,1)S(1)}, bf16[128,1024]{1,0:T(8,128)(2,1)S(1)}, u32[]{:S(2)}, u32[]{:S(2)}) collective-permute-start(bf16[128,1024]{1,0:T(8,128)(2,1)S(1)} %add_convert_fusion.2), channel_id=1, source_target_pairs={{0,4},{4,12},{12,8},{8,0},{1,5},{5,13},{13,9},{9,1},{2,6},{6,14},{... | collective-permute-start | bytes 786440 | tf_op jit(solution)/shard_map/ppermute | solution.py:301
  70.7 5.7 %collective-permute-start.19 = (bf16[4,768,512]{2,1,0:T(8,128)(2,1)S(1)}, bf16[4,768,512]{2,1,0:T(8,128)(2,1)S(1)}, u32[]{:S(2)}, u32[]{:S(2)}) collective-permute-start(bf16[4,768,512]{2,1,0:T(8,128)(2,1)S(1)} %weight_grads.2), channel_id=1, source_target_pairs={{0,1},{1,0},{2,3},{3,2},{4,5},{5,4},{6,7},{7,6},{8,9},{9,8},{10,11... | collective-permute-start | bytes 9437192 | tf_op jit(solution)/shard_map/ppermute | solution.py:341
  70.8 9.7 %collective-permute-start.20 = (bf16[128,1024]{1,0:T(8,128)(2,1)S(1)}, bf16[128,1024]{1,0:T(8,128)(2,1)S(1)}, u32[]{:S(2)}, u32[]{:S(2)}) collective-permute-start(bf16[128,1024]{1,0:T(8,128)(2,1)S(1)} %add_convert_fusion.1), channel_id=1, source_target_pairs={{0,4},{4,12},{12,8},{8,0},{1,5},{5,13},{13,9},{9,1},{2,6},{6,14},{... | collective-permute-start | bytes 786440 | tf_op jit(solution)/shard_map/ppermute | solution.py:301
  70.9 9.6 %collective-permute-start.21 = (bf16[128,1024]{1,0:T(8,128)(2,1)S(1)}, bf16[128,1024]{1,0:T(8,128)(2,1)S(1)}, u32[]{:S(2)}, u32[]{:S(2)}) collective-permute-start(bf16[128,1024]{1,0:T(8,128)(2,1)S(1)} %get-tuple-element.275), channel_id=1, source_target_pairs={{0,2},{2,0},{1,3},{3,1},{4,6},{6,4},{5,7},{7,5},{8,10},{10,8},{9,1... | collective-permute-start | bytes 786440 | tf_op jit(solution)/shard_map/ppermute | solution.py:291

commit v18 on v17

--- a/solution.py
+++ b/solution.py
@@ -208,8 +208,8 @@
 
 
 def keep_kernel(n, side_ref, *refs):
-    got, outs = refs[3 * n], refs[3 * n + 1 : 3 * n + 4]
-    buffers, sem = refs[3 * n + 4 : 3 * n + 7], refs[3 * n + 7]
+    got, outs = refs[3 * n], refs[3 * n + 2 : 3 * n + 5]
+    buffers, sem = refs[3 * n + 5 : 3 * n + 8], refs[3 * n + 8]
     copies = []
     for e in range(got.shape[0]):
         gate_up, down = halves_of(n, e, side_ref[0], refs)
@@ -227,7 +227,7 @@
         copy.wait()
 
 
-def weight_call(side, x_rows, s_rows, hids, got=None):
+def weight_call(side, x_rows, s_rows, hids, got=None, pace=None):
     n = len(x_rows)
     experts, rows, width = x_rows[0].shape
     ff = hids[0].shape[2] // 3
@@ -240,7 +240,7 @@
         out_shape = pltpu.VMEM((experts, depth + ff, depth), jnp.bfloat16)
     else:
         kernel = keep_kernel
-        operands = operands + [got]
+        operands = operands + [got, pace]
         shapes = [(experts, depth, ff), (experts, depth, ff), (experts, ff, depth)]
         out_specs = [pl.BlockSpec(memory_space=pl.ANY)] * 3
         out_shape = [jax.ShapeDtypeStruct(s, jnp.bfloat16) for s in shapes]
@@ -303,6 +303,7 @@
     tokens, first_expert, half, other_half = tie(tokens, first_expert, half, 1 - half)
     weights = load_call((w_gate, w_up, w_down))
     first_tokens, upstream = pack_call(tokens, upstream, expert_ids, slots, gate_fixed)
+    pace = lax.slice(upstream, (tok_rows, 0), (tok_rows + 8, 128))
     blocks, chunks, backs, sent = {}, {}, {}, {}
     last = n_group - 1
     for k in range(n_group):
@@ -320,7 +321,9 @@
             chunks[k - 1] = chunk(blocks[k - 1])
         if k == last:
             backs[k - 1] = across(chunks[k - 1][1])
-        upstream, pair[1], chunks, weights = tie(upstream, pair[1], chunks, weights)
+        if k > 0:
+            pace = lax.ppermute(pace, "dp", [(0, 1), (1, 0)])
+        upstream, pair[1], chunks, weights, pace = tie(upstream, pair[1], chunks, weights, pace)
         tokens, pair[0] = tie(tokens, pair[0])
         blocks[k] = pair
 
@@ -341,7 +344,7 @@
     got = lax.ppermute(to_send, "dp", [(0, 1), (1, 0)])
     sent[last] = homeward(group_sum(chunks[last][0], [*backs[last], carried]), last)
     backs[0] = across(other)
-    grads = weight_call(half, *kept, got)
+    grads = weight_call(half, *kept, got, pace)
     grads, sent, backs[0] = tie(grads, sent, backs[0])
     total = wide(chunks[0][0])
     for back in backs[0]:

time: 81.6 us -> 83.4 us (1.022)
  waiting for transfers between devices: 29.2 us -> 30.5 us
    ppermute x3, waiting for transfers between devices: 6.79 us -> 8.66 us  [homeward(): return lax.ppermute(group_part, 'group', along(-k))]
  transfers between devices with their start and end apart: 22 -> 25, of which waited for: 15 -> 16; matrix products, arithmetic and copies ran while one was open for 0% -> 0% of each run, Pallas kernels for 27% -> 27%
where the time goes in v18:
time: 83.4 us; the launch traced here: 83.2 us
  waiting for transfers between devices  30.5 us (37%)
  starting transfers between devices  26.8 us (32%)
  Pallas kernels  23.9 us (29%)
  other arithmetic  1.13 us (1%)
    pallas_call x4, Pallas kernels, chunk_call(): pl.pallas_call(functools.partial(chunk_kernel, n_blocks, tok_rows, capaci...  14.7 us
    ppermute x6, starting transfers between devices, per_device(): lax.ppermute(v, 'group', along(1))  10.9 us
    ppermute x6, waiting for transfers between devices, per_device(): lax.ppermute(v, 'group', along(1))  10.8 us
    ppermute x3, waiting for transfers between devices, homeward(): return lax.ppermute(group_part, 'group', along(-k))  8.66 us
    ppermute x7, starting transfers between devices, spread(): lax.ppermute(column, 'ingroup', shift(s))  6.4 us
    pallas_call x2, Pallas kernels, weight_call(): pl.pallas_call(functools.partial(kernel, n), in_specs=[smem] + [vmem] * l...  4.57 us
    ppermute x4, starting transfers between devices, across(): lax.ppermute(others[(s - 1) * tok_rows:s * tok_rows], 'ingroup', shift(-s))  4.24 us
    ppermute x1, waiting for transfers between devices, per_device(): got = lax.ppermute(to_send, 'dp', [(0, 1), (1, 0)])  3.89 us
  transfers between devices with their start and end apart: 25, of which 16 were waited for; matrix products, arithmetic and copies ran while one was open for 0% of the time, Pallas kernels for 27%

profile of v18, /device:TPU:0, one launch (start us, length us, event | category | flops | bytes accessed | tf_op | source)
XLA Modules:
  0.0 83.2 jit_solution(16901687352534275238)
XLA Ops:
  0.6 1.8 %pack.1 = (bf16[128,1024]{1,0:T(8,128)(2,1)S(1)}, bf16[144,1024]{1,0:T(8,128)(2,1)S(1)}) custom-call(bf16[128,1024]{1,0:T(8,128)(2,1)} %tokens, bf16[128,1024]{1,0:T(8,128)(2,1)} %upstream.1, s32[8,128]{1,0:T(8,128)} %bitcast.5, s32[8,128]{1,0:T(8,128)} %bitcast.6, s32[8,128]{1,0:T(8,128)} %bitcast.7), custom_call_target="tpu_custom_call" | custom-call | bytes 1048576 | tf_op jit(solution)/shard_map/pack/pallas_call | solution.py:58
  2.4 3.0 %collective-permute-start.1 = (bf16[144,1024]{1,0:T(8,128)(2,1)S(1)}, bf16[144,1024]{1,0:T(8,128)(2,1)S(1)}, u32[]{:S(2)}, u32[]{:S(2)}) collective-permute-start(bf16[144,1024]{1,0:T(8,128)(2,1)S(1)} %get-tuple-element.157.refs_2_), channel_id=1, source_target_pairs={{0,2},{2,0},{1,3},{3,1},{4,6},{6,4},{5,7},{7,5},{8,10},{10,8},{9,1... | collective-permute-start | bytes 884744 | tf_op jit(solution)/shard_map/ppermute | solution.py:284
  5.4 1.6 %collective-permute-start = (bf16[144,1024]{1,0:T(8,128)(2,1)S(1)}, bf16[144,1024]{1,0:T(8,128)(2,1)S(1)}, u32[]{:S(2)}, u32[]{:S(2)}) collective-permute-start(bf16[144,1024]{1,0:T(8,128)(2,1)S(1)} %get-tuple-element.157.refs_2_), channel_id=1, source_target_pairs={{0,4},{4,12},{12,8},{8,0},{1,5},{5,13},{13,9},{9,1},{2,6},{6,14},{... | collective-permute-start | bytes 884744 | tf_op jit(solution)/shard_map/ppermute | solution.py:319
  7.0 0.5 collective-permute-start.5
  7.5 2.6 %collective-permute-start.4 = (bf16[128,1024]{1,0:T(8,128)(2,1)}, bf16[128,1024]{1,0:T(8,128)(2,1)S(1)}, u32[]{:S(2)}, u32[]{:S(2)}) collective-permute-start(bf16[128,1024]{1,0:T(8,128)(2,1)} %tokens), channel_id=1, source_target_pairs={{0,4},{4,12},{12,8},{8,0},{1,5},{5,13},{13,9},{9,1},{2,6},{6,14},{... | collective-permute-start | bytes 786440 | tf_op jit(solution)/shard_map/ppermute | solution.py:319
  10.1 2.9 %load.1 = (bf16[4,1024,256]{2,1,0:T(8,128)(2,1)S(1)}, bf16[4,1024,256]{2,1,0:T(8,128)(2,1)S(1)}, bf16[4,256,1024]{2,1,0:T(8,128)(2,1)S(1)}) custom-call(bf16[4,1024,256]{2,1,0:T(8,128)(2,1)} %refs_0_.1, bf16[4,1024,256]{2,1,0:T(8,128)(2,1)} %refs_1_.1, bf16[4,256,1024]{2,1,0:T(8,128)(2,1)} %refs_2_.1), custom_call_target="tpu_custom_call" | custom-call | bytes 12582912 | tf_op jit(solution)/shard_map/load/pallas_call | solution.py:99
  13.0 0.2 collective-permute-done.1.refs_3_
  13.3 3.0 %collective-permute-done.refs_2_ = bf16[144,1024]{1,0:T(8,128)(2,1)S(1)} collective-permute-done((bf16[144,1024]{1,0:T(8,128)(2,1)S(1)}, bf16[144,1024]{1,0:T(8,128)(2,1)S(1)}, u32[]{:S(2)}, u32[]{:S(2)}) %collective-permute-start) | collective-permute-done | bytes 294944 | tf_op jit(solution)/shard_map/ppermute | solution.py:319
  16.3 0.2 collective-permute-start.3
  16.4 1.2 %collective-permute-start.2 = (bf16[144,1024]{1,0:T(8,128)(2,1)S(1)}, bf16[144,1024]{1,0:T(8,128)(2,1)S(1)}, u32[]{:S(2)}, u32[]{:S(2)}) collective-permute-start(bf16[144,1024]{1,0:T(8,128)(2,1)S(1)} %collective-permute-done.refs_2_), channel_id=1, source_target_pairs={{0,4},{4,12},{12,8},{8,0},{1,5},{5,13},{13,9},{9,1},{2,6},{6,14},{... | collective-permute-start | bytes 884744 | tf_op jit(solution)/shard_map/ppermute | solution.py:319
  17.6 1.3 %collective-permute-done.5.refs_1_ = bf16[128,1024]{1,0:T(8,128)(2,1)S(1)} collective-permute-done((bf16[128,1024]{1,0:T(8,128)(2,1)}, bf16[128,1024]{1,0:T(8,128)(2,1)S(1)}, u32[]{:S(2)}, u32[]{:S(2)}) %collective-permute-start.5) | collective-permute-done | bytes 262176 | tf_op jit(solution)/shard_map/ppermute | solution.py:284
  18.9 3.0 %collective-permute-done.4.refs_0_ = bf16[128,1024]{1,0:T(8,128)(2,1)S(1)} collective-permute-done((bf16[128,1024]{1,0:T(8,128)(2,1)}, bf16[128,1024]{1,0:T(8,128)(2,1)S(1)}, u32[]{:S(2)}, u32[]{:S(2)}) %collective-permute-start.4) | collective-permute-done | bytes 262176 | tf_op jit(solution)/shard_map/ppermute | solution.py:319
  21.9 0.2 collective-permute-start.10
  22.0 1.3 %collective-permute-start.9 = (bf16[128,1024]{1,0:T(8,128)(2,1)S(1)}, bf16[128,1024]{1,0:T(8,128)(2,1)S(1)}, u32[]{:S(2)}, u32[]{:S(2)}) collective-permute-start(bf16[128,1024]{1,0:T(8,128)(2,1)S(1)} %collective-permute-done.4.refs_0_), channel_id=1, source_target_pairs={{0,4},{4,12},{12,8},{8,0},{1,5},{5,13},{13,9},{9,1},{2,6},{6,14},{... | collective-permute-start | bytes 786440 | tf_op jit(solution)/shard_map/ppermute | solution.py:319
  23.3 0.0 collective-permute-start.6
  23.3 3.7 %chunk.4 = (bf16[128,1024]{1,0:T(8,128)(2,1)S(1)}, bf16[128,1024]{1,0:T(8,128)(2,1)S(1)}, bf16[4,96,1024]{2,1,0:T(8,128)(2,1)S(1)}, bf16[4,96,1024]{2,1,0:T(8,128)(2,1)S(1)}, bf16[4,96,768]{2,1,0:T(8,128)(2,1)S(1)}) custom-call(s32[1]{0:T(128)} %bitcast.first_ref, bf16[128,1024]{1,0:T(8,128)(2,1)S(1)} %get-tuple-element.155.refs_0_, ...), custom_call_target="tpu_custom_call" | custom-call | flops 1610612736 | bytes 8388608 | tf_op jit(solution)/shard_map/chunk/pallas_call | solution.py:175
  27.0 0.0 collective-permute-done.6
  27.0 0.0 collective-permute-done.3.refs_3_
  27.0 1.2 %collective-permute-done.2.refs_2_ = bf16[144,1024]{1,0:T(8,128)(2,1)S(1)} collective-permute-done((bf16[144,1024]{1,0:T(8,128)(2,1)S(1)}, bf16[144,1024]{1,0:T(8,128)(2,1)S(1)}, u32[]{:S(2)}, u32[]{:S(2)}) %collective-permute-start.2) | collective-permute-done | bytes 294944 | tf_op jit(solution)/shard_map/ppermute | solution.py:319
  28.2 0.9 %collective-permute-start.8 = (bf16[144,1024]{1,0:T(8,128)(2,1)S(1)}, bf16[144,1024]{1,0:T(8,128)(2,1)S(1)}, u32[]{:S(2)}, u32[]{:S(2)}) collective-permute-start(bf16[144,1024]{1,0:T(8,128)(2,1)S(1)} %collective-permute-done.2.refs_2_), channel_id=1, source_target_pairs={{0,2},{2,0},{1,3},{3,1},{4,6},{6,4},{5,7},{7,5},{8,10},{10,8},{9,1... | collective-permute-start | bytes 884744 | tf_op jit(solution)/shard_map/ppermute | solution.py:284
  29.1 2.7 %collective-permute-start.7 = (bf16[144,1024]{1,0:T(8,128)(2,1)S(1)}, bf16[144,1024]{1,0:T(8,128)(2,1)S(1)}, u32[]{:S(2)}, u32[]{:S(2)}) collective-permute-start(bf16[144,1024]{1,0:T(8,128)(2,1)S(1)} %collective-permute-done.2.refs_2_), channel_id=1, source_target_pairs={{0,4},{4,12},{12,8},{8,0},{1,5},{5,13},{13,9},{9,1},{2,6},{6,14},{... | collective-permute-start | bytes 884744 | tf_op jit(solution)/shard_map/ppermute | solution.py:319
  31.8 0.0 collective-permute-done.10.refs_1_
  31.9 0.5 collective-permute-done.9.refs_0_
  32.3 0.5 collective-permute-start.14
  32.8 1.6 %collective-permute-start.13 = (bf16[128,1024]{1,0:T(8,128)(2,1)S(1)}, bf16[128,1024]{1,0:T(8,128)(2,1)S(1)}, u32[]{:S(2)}, u32[]{:S(2)}) collective-permute-start(bf16[128,1024]{1,0:T(8,128)(2,1)S(1)} %collective-permute-done.9.refs_0_), channel_id=1, source_target_pairs={{0,4},{4,12},{12,8},{8,0},{1,5},{5,13},{13,9},{9,1},{2,6},{6,14},{... | collective-permute-start | bytes 786440 | tf_op jit(solution)/shard_map/ppermute | solution.py:319
  34.4 0.0 collective-permute-start.11
  34.4 3.7 %chunk.5 = (bf16[128,1024]{1,0:T(8,128)(2,1)S(1)}, bf16[128,1024]{1,0:T(8,128)(2,1)S(1)}, bf16[4,96,1024]{2,1,0:T(8,128)(2,1)S(1)}, bf16[4,96,1024]{2,1,0:T(8,128)(2,1)S(1)}, bf16[4,96,768]{2,1,0:T(8,128)(2,1)S(1)}) custom-call(s32[1]{0:T(128)} %bitcast.first_ref, bf16[128,1024]{1,0:T(8,128)(2,1)S(1)} %collective-permute-done.4.refs_0_, ...), custom_call_target="tpu_custom_call" | custom-call | flops 1610612736 | bytes 8388608 | tf_op jit(solution)/shard_map/chunk/pallas_call | solution.py:175
  38.1 0.0 collective-permute-done.11
  38.1 0.1 collective-permute-done.8.refs_3_
  38.1 1.8 %collective-permute-done.7.refs_2_ = bf16[144,1024]{1,0:T(8,128)(2,1)S(1)} collective-permute-done((bf16[144,1024]{1,0:T(8,128)(2,1)S(1)}, bf16[144,1024]{1,0:T(8,128)(2,1)S(1)}, u32[]{:S(2)}, u32[]{:S(2)}) %collective-permute-start.7) | collective-permute-done | bytes 294944 | tf_op jit(solution)/shard_map/ppermute | solution.py:319
  39.9 1.1 %collective-permute-start.12 = (bf16[144,1024]{1,0:T(8,128)(2,1)S(1)}, bf16[144,1024]{1,0:T(8,128)(2,1)S(1)}, u32[]{:S(2)}, u32[]{:S(2)}) collective-permute-start(bf16[144,1024]{1,0:T(8,128)(2,1)S(1)} %collective-permute-done.7.refs_2_), channel_id=1, source_target_pairs={{0,2},{2,0},{1,3},{3,1},{4,6},{6,4},{5,7},{7,5},{8,10},{10,8},{9,1... | collective-permute-start | bytes 884744 | tf_op jit(solution)/shard_map/ppermute | solution.py:284
  41.1 1.9 %collective-permute-done.14.refs_1_ = bf16[128,1024]{1,0:T(8,128)(2,1)S(1)} collective-permute-done((bf16[128,1024]{1,0:T(8,128)(2,1)S(1)}, bf16[128,1024]{1,0:T(8,128)(2,1)S(1)}, u32[]{:S(2)}, u32[]{:S(2)}) %collective-permute-start.14) | collective-permute-done | bytes 262176 | tf_op jit(solution)/shard_map/ppermute | solution.py:284
  42.9 1.4 %collective-permute-done.13.refs_0_ = bf16[128,1024]{1,0:T(8,128)(2,1)S(1)} collective-permute-done((bf16[128,1024]{1,0:T(8,128)(2,1)S(1)}, bf16[128,1024]{1,0:T(8,128)(2,1)S(1)}, u32[]{:S(2)}, u32[]{:S(2)}) %collective-permute-start.13) | collective-permute-done | bytes 262176 | tf_op jit(solution)/shard_map/ppermute | solution.py:319
  44.3 2.3 %collective-permute-start.16 = (bf16[128,1024]{1,0:T(8,128)(2,1)S(1)}, bf16[128,1024]{1,0:T(8,128)(2,1)S(1)}, u32[]{:S(2)}, u32[]{:S(2)}) collective-permute-start(bf16[128,1024]{1,0:T(8,128)(2,1)S(1)} %collective-permute-done.14.refs_1_), channel_id=1, source_target_pairs={{0,4},{4,12},{12,8},{8,0},{1,5},{5,13},{13,9},{9,1},{2,6},{6,14},{... | collective-permute-start | bytes 786440 | tf_op jit(solution)/shard_map/ppermute | solution.py:315
  46.6 0.0 collective-permute-start.15
  46.6 0.7 collective-permute-start.17
  47.3 3.7 %chunk.6 = (bf16[128,1024]{1,0:T(8,128)(2,1)S(1)}, bf16[128,1024]{1,0:T(8,128)(2,1)S(1)}, bf16[4,96,1024]{2,1,0:T(8,128)(2,1)S(1)}, bf16[4,96,1024]{2,1,0:T(8,128)(2,1)S(1)}, bf16[4,96,768]{2,1,0:T(8,128)(2,1)S(1)}) custom-call(s32[1]{0:T(128)} %bitcast.first_ref, bf16[128,1024]{1,0:T(8,128)(2,1)S(1)} %collective-permute-done.9.refs_0_, ...), custom_call_target="tpu_custom_call" | custom-call | flops 1610612736 | bytes 8388608 | tf_op jit(solution)/shard_map/chunk/pallas_call | solution.py:175
  51.0 1.4 %collective-permute-start.18 = (bf16[128,1024]{1,0:T(8,128)(2,1)S(1)}, bf16[128,1024]{1,0:T(8,128)(2,1)S(1)}, u32[]{:S(2)}, u32[]{:S(2)}) collective-permute-start(bf16[128,1024]{1,0:T(8,128)(2,1)S(1)} %get-tuple-element.210), channel_id=1, source_target_pairs={{0,2},{2,0},{1,3},{3,1},{4,6},{6,4},{5,7},{7,5},{8,10},{10,8},{9,1... | collective-permute-start | bytes 786440 | tf_op jit(solution)/shard_map/ppermute | solution.py:291
  52.4 0.3 collective-permute-done.16.refs_1_
  52.7 0.0 collective-permute-done.15.refs_13_
  52.7 0.0 collective-permute-done.12.refs_3_
  52.7 3.7 %chunk.7 = (bf16[128,1024]{1,0:T(8,128)(2,1)S(1)}, bf16[128,1024]{1,0:T(8,128)(2,1)S(1)}, bf16[4,96,1024]{2,1,0:T(8,128)(2,1)S(1)}, bf16[4,96,1024]{2,1,0:T(8,128)(2,1)S(1)}, bf16[4,96,768]{2,1,0:T(8,128)(2,1)S(1)}) custom-call(s32[1]{0:T(128)} %bitcast.first_ref, bf16[128,1024]{1,0:T(8,128)(2,1)S(1)} %collective-permute-done.13.refs_0_, ...), custom_call_target="tpu_custom_call" | custom-call | flops 1610612736 | bytes 8388608 | tf_op jit(solution)/shard_map/chunk/pallas_call | solution.py:175
  56.3 0.6 collective-permute-start.20
  56.9 0.0 collective-permute-done.17
  56.9 0.1 add_convert_fusion.3
  57.0 0.9 %collective-permute-start.19 = (bf16[128,1024]{1,0:T(8,128)(2,1)S(1)}, bf16[128,1024]{1,0:T(8,128)(2,1)S(1)}, u32[]{:S(2)}, u32[]{:S(2)}) collective-permute-start(bf16[128,1024]{1,0:T(8,128)(2,1)S(1)} %add_convert_fusion.3), channel_id=1, source_target_pairs={{0,8},{4,0},{12,4},{8,12},{1,9},{5,1},{13,5},{9,13},{2,10},{6,2},{... | collective-permute-start | bytes 786440 | tf_op jit(solution)/shard_map/ppermute | solution.py:301
  57.9 3.4 %collective-permute-done.18 = bf16[128,1024]{1,0:T(8,128)(2,1)S(1)} collective-permute-done((bf16[128,1024]{1,0:T(8,128)(2,1)S(1)}, bf16[128,1024]{1,0:T(8,128)(2,1)S(1)}, u32[]{:S(2)}, u32[]{:S(2)}) %collective-permute-start.18) | collective-permute-done | bytes 262176 | tf_op jit(solution)/shard_map/ppermute | solution.py:291
  61.3 0.1 add_convert_fusion.2
  61.4 2.0 %collective-permute-start.21 = (bf16[128,1024]{1,0:T(8,128)(2,1)S(1)}, bf16[128,1024]{1,0:T(8,128)(2,1)S(1)}, u32[]{:S(2)}, u32[]{:S(2)}) collective-permute-start(bf16[128,1024]{1,0:T(8,128)(2,1)S(1)} %add_convert_fusion.2), channel_id=1, source_target_pairs={{0,4},{4,12},{12,8},{8,0},{1,5},{5,13},{13,9},{9,1},{2,6},{6,14},{... | collective-permute-start | bytes 786440 | tf_op jit(solution)/shard_map/ppermute | solution.py:301
  63.4 1.5 %collective-permute-done.19 = bf16[128,1024]{1,0:T(8,128)(2,1)S(1)} collective-permute-done((bf16[128,1024]{1,0:T(8,128)(2,1)S(1)}, bf16[128,1024]{1,0:T(8,128)(2,1)S(1)}, u32[]{:S(2)}, u32[]{:S(2)}) %collective-permute-start.19) | collective-permute-done | bytes 262176 | tf_op jit(solution)/shard_map/ppermute | solution.py:301
  64.9 1.9 %weight_grads.2 = bf16[4,768,512]{2,1,0:T(8,128)(2,1)S(1)} custom-call(s32[1]{0:T(128)S(6)} %sub.3.side_ref, bf16[4,96,1024]{2,1,0:T(8,128)(2,1)S(1)} %get-tuple-element.258.refs_0_, bf16[4,96,1024]{2,1,0:T(8,128)(2,1)S(1)} %get-tuple-element.259.refs_1_, bf16[4,96,1024]{2,1,0:T(8,128)(2,1)S(1)} %get-tuple-element.260.refs_2_, ...), custom_call_target="tpu_custom_call" | custom-call | flops 1207959552 | bytes 8650752 | tf_op jit(solution)/shard_map/weight_grads/pallas_call | solution.py:248
  66.8 0.0 collective-permute-done.20
  66.8 5.7 %collective-permute-done.21 = bf16[128,1024]{1,0:T(8,128)(2,1)S(1)} collective-permute-done((bf16[128,1024]{1,0:T(8,128)(2,1)S(1)}, bf16[128,1024]{1,0:T(8,128)(2,1)S(1)}, u32[]{:S(2)}, u32[]{:S(2)}) %collective-permute-start.21) | collective-permute-done | bytes 262176 | tf_op jit(solution)/shard_map/ppermute | solution.py:301
  72.5 0.0 collective-permute-start.22
  72.5 0.1 add_convert_fusion.1
  72.6 0.1 collective-permute-start.23
  72.7 1.6 %collective-permute-start.24 = (bf16[128,1024]{1,0:T(8,128)(2,1)S(1)}, bf16[128,1024]{1,0:T(8,128)(2,1)S(1)}, u32[]{:S(2)}, u32[]{:S(2)}) collective-permute-start(bf16[128,1024]{1,0:T(8,128)(2,1)S(1)} %get-tuple-element.283), channel_id=1, source_target_pairs={{0,2},{2,0},{1,3},{3,1},{4,6},{6,4},{5,7},{7,5},{8,10},{10,8},{9,1... | collective-permute-start | bytes 786440 | tf_op jit(solution)/shard_map/ppermute | solution.py:291
  74.3 3.9 %collective-permute-done.22.refs_12_ = bf16[4,768,512]{2,1,0:T(8,128)(2,1)S(1)} collective-permute-done((bf16[4,768,512]{2,1,0:T(8,128)(2,1)S(1)}, bf16[4,768,512]{2,1,0:T(8,128)(2,1)S(1)}, u32[]{:S(2)}, u32[]{:S(2)}) %collective-permute-start.22) | collective-permute-done | bytes 3145760 | tf_op jit(solution)/shard_map/ppermute | solution.py:344
  78.2 2.7 %weight_grads.3 = (bf16[4,512,256]{2,1,0:T(8,128)(2,1)}, bf16[4,512,256]{2,1,0:T(8,128)(2,1)}, bf16[4,256,512]{2,1,0:T(8,128)(2,1)}) custom-call(s32[1]{0:T(128)} %bitcast.1.side_ref, bf16[4,96,1024]{2,1,0:T(8,128)(2,1)S(1)} %get-tuple-element.258.refs_0_, bf16[4,96,1024]{2,1,0:T(8,128)(2,1)S(1)} %get-tuple-element.259.refs_1_, ...), custom_call_target="tpu_custom_call" | custom-call | flops 1207959552 | bytes 8650752 | tf_op jit(solution)/shard_map/weight_grads/pallas_call | solution.py:248
  80.9 1.4 %collective-permute-done.23 = bf16[128,1024]{1,0:T(8,128)(2,1)S(1)} collective-permute-done((bf16[128,1024]{1,0:T(8,128)(2,1)S(1)}, bf16[128,1024]{1,0:T(8,128)(2,1)S(1)}, u32[]{:S(2)}, u32[]{:S(2)}) %collective-permute-start.23) | collective-permute-done | bytes 262176 | tf_op jit(solution)/shard_map/ppermute | solution.py:301
  82.3 0.0 collective-permute-done.24
  82.3 0.9 %add_convert_fusion = bf16[128,1024]{1,0:T(8,128)(2,1)} fusion(bf16[128,1024]{1,0:T(8,128)(2,1)S(1)} %collective-permute-done.23, bf16[128,1024]{1,0:T(8,128)(2,1)S(1)} %collective-permute-done.19, bf16[128,1024]{1,0:T(8,128)(2,1)S(1)} %collective-permute-done.24, bf16[128,1024]{1,0:T(8,128)(2,1)S(1)} %get-tuple-element.242), kind=kLoop, calls=%fused_computation | loop fusion | flops 1048576 | bytes 1310720 | tf_op jit(solution)/shard_map/convert_element_type | solution.py:354
  (1 shorter events, 0.0 us)
Async XLA Ops:
  2.4 10.8 %collective-permute-start.1 = (bf16[144,1024]{1,0:T(8,128)(2,1)S(1)}, bf16[144,1024]{1,0:T(8,128)(2,1)S(1)}, u32[]{:S(2)}, u32[]{:S(2)}) collective-permute-start(bf16[144,1024]{1,0:T(8,128)(2,1)S(1)} %get-tuple-element.157.refs_2_), channel_id=1, source_target_pairs={{0,2},{2,0},{1,3},{3,1},{4,6},{6,4},{5,7},{7,5},{8,10},{10,8},{9,1... | collective-permute-start | bytes 884744 | tf_op jit(solution)/shard_map/ppermute | solution.py:284
  5.4 10.8 %collective-permute-start = (bf16[144,1024]{1,0:T(8,128)(2,1)S(1)}, bf16[144,1024]{1,0:T(8,128)(2,1)S(1)}, u32[]{:S(2)}, u32[]{:S(2)}) collective-permute-start(bf16[144,1024]{1,0:T(8,128)(2,1)S(1)} %get-tuple-element.157.refs_2_), channel_id=1, source_target_pairs={{0,4},{4,12},{12,8},{8,0},{1,5},{5,13},{13,9},{9,1},{2,6},{6,14},{... | collective-permute-start | bytes 884744 | tf_op jit(solution)/shard_map/ppermute | solution.py:319
  7.0 11.9 %collective-permute-start.5 = (bf16[128,1024]{1,0:T(8,128)(2,1)}, bf16[128,1024]{1,0:T(8,128)(2,1)S(1)}, u32[]{:S(2)}, u32[]{:S(2)}) collective-permute-start(bf16[128,1024]{1,0:T(8,128)(2,1)} %tokens), channel_id=1, source_target_pairs={{0,2},{2,0},{1,3},{3,1},{4,6},{6,4},{5,7},{7,5},{8,10},{10,8},{9,1... | collective-permute-start | bytes 786440 | tf_op jit(solution)/shard_map/ppermute | solution.py:284
  7.5 14.3 %collective-permute-start.4 = (bf16[128,1024]{1,0:T(8,128)(2,1)}, bf16[128,1024]{1,0:T(8,128)(2,1)S(1)}, u32[]{:S(2)}, u32[]{:S(2)}) collective-permute-start(bf16[128,1024]{1,0:T(8,128)(2,1)} %tokens), channel_id=1, source_target_pairs={{0,4},{4,12},{12,8},{8,0},{1,5},{5,13},{13,9},{9,1},{2,6},{6,14},{... | collective-permute-start | bytes 786440 | tf_op jit(solution)/shard_map/ppermute | solution.py:319
  16.3 10.7 %collective-permute-start.3 = (bf16[144,1024]{1,0:T(8,128)(2,1)S(1)}, bf16[144,1024]{1,0:T(8,128)(2,1)S(1)}, u32[]{:S(2)}, u32[]{:S(2)}) collective-permute-start(bf16[144,1024]{1,0:T(8,128)(2,1)S(1)} %collective-permute-done.refs_2_), channel_id=1, source_target_pairs={{0,2},{2,0},{1,3},{3,1},{4,6},{6,4},{5,7},{7,5},{8,10},{10,8},{9,1... | collective-permute-start | bytes 884744 | tf_op jit(solution)/shard_map/ppermute | solution.py:284
  16.4 11.8 %collective-permute-start.2 = (bf16[144,1024]{1,0:T(8,128)(2,1)S(1)}, bf16[144,1024]{1,0:T(8,128)(2,1)S(1)}, u32[]{:S(2)}, u32[]{:S(2)}) collective-permute-start(bf16[144,1024]{1,0:T(8,128)(2,1)S(1)} %collective-permute-done.refs_2_), channel_id=1, source_target_pairs={{0,4},{4,12},{12,8},{8,0},{1,5},{5,13},{13,9},{9,1},{2,6},{6,14},{... | collective-permute-start | bytes 884744 | tf_op jit(solution)/shard_map/ppermute | solution.py:319
  21.9 10.0 %collective-permute-start.10 = (bf16[128,1024]{1,0:T(8,128)(2,1)S(1)}, bf16[128,1024]{1,0:T(8,128)(2,1)S(1)}, u32[]{:S(2)}, u32[]{:S(2)}) collective-permute-start(bf16[128,1024]{1,0:T(8,128)(2,1)S(1)} %collective-permute-done.4.refs_0_), channel_id=1, source_target_pairs={{0,2},{2,0},{1,3},{3,1},{4,6},{6,4},{5,7},{7,5},{8,10},{10,8},{9,1... | collective-permute-start | bytes 786440 | tf_op jit(solution)/shard_map/ppermute | solution.py:284
  22.0 10.3 %collective-permute-start.9 = (bf16[128,1024]{1,0:T(8,128)(2,1)S(1)}, bf16[128,1024]{1,0:T(8,128)(2,1)S(1)}, u32[]{:S(2)}, u32[]{:S(2)}) collective-permute-start(bf16[128,1024]{1,0:T(8,128)(2,1)S(1)} %collective-permute-done.4.refs_0_), channel_id=1, source_target_pairs={{0,4},{4,12},{12,8},{8,0},{1,5},{5,13},{13,9},{9,1},{2,6},{6,14},{... | collective-permute-start | bytes 786440 | tf_op jit(solution)/shard_map/ppermute | solution.py:319
  23.3 3.7 %collective-permute-start.6 = (bf16[8,128]{1,0:T(8,128)(2,1)S(1)}, bf16[8,128]{1,0:T(8,128)(2,1)S(1)}, u32[]{:S(2)}, u32[]{:S(2)}) collective-permute-start(bf16[8,128]{1,0:T(8,128)(2,1)S(1)} %slice.3), channel_id=1, source_target_pairs={{0,1},{1,0},{2,3},{3,2},{4,5},{5,4},{6,7},{7,6},{8,9},{9,8},{10,11... | collective-permute-start | bytes 6152 | tf_op jit(solution)/shard_map/ppermute | solution.py:325
  28.2 9.9 %collective-permute-start.8 = (bf16[144,1024]{1,0:T(8,128)(2,1)S(1)}, bf16[144,1024]{1,0:T(8,128)(2,1)S(1)}, u32[]{:S(2)}, u32[]{:S(2)}) collective-permute-start(bf16[144,1024]{1,0:T(8,128)(2,1)S(1)} %collective-permute-done.2.refs_2_), channel_id=1, source_target_pairs={{0,2},{2,0},{1,3},{3,1},{4,6},{6,4},{5,7},{7,5},{8,10},{10,8},{9,1... | collective-permute-start | bytes 884744 | tf_op jit(solution)/shard_map/ppermute | solution.py:284
  29.1 10.8 %collective-permute-start.7 = (bf16[144,1024]{1,0:T(8,128)(2,1)S(1)}, bf16[144,1024]{1,0:T(8,128)(2,1)S(1)}, u32[]{:S(2)}, u32[]{:S(2)}) collective-permute-start(bf16[144,1024]{1,0:T(8,128)(2,1)S(1)} %collective-permute-done.2.refs_2_), channel_id=1, source_target_pairs={{0,4},{4,12},{12,8},{8,0},{1,5},{5,13},{13,9},{9,1},{2,6},{6,14},{... | collective-permute-start | bytes 884744 | tf_op jit(solution)/shard_map/ppermute | solution.py:319
  32.3 10.6 %collective-permute-start.14 = (bf16[128,1024]{1,0:T(8,128)(2,1)S(1)}, bf16[128,1024]{1,0:T(8,128)(2,1)S(1)}, u32[]{:S(2)}, u32[]{:S(2)}) collective-permute-start(bf16[128,1024]{1,0:T(8,128)(2,1)S(1)} %collective-permute-done.9.refs_0_), channel_id=1, source_target_pairs={{0,2},{2,0},{1,3},{3,1},{4,6},{6,4},{5,7},{7,5},{8,10},{10,8},{9,1... | collective-permute-start | bytes 786440 | tf_op jit(solution)/shard_map/ppermute | solution.py:284
  32.8 11.5 %collective-permute-start.13 = (bf16[128,1024]{1,0:T(8,128)(2,1)S(1)}, bf16[128,1024]{1,0:T(8,128)(2,1)S(1)}, u32[]{:S(2)}, u32[]{:S(2)}) collective-permute-start(bf16[128,1024]{1,0:T(8,128)(2,1)S(1)} %collective-permute-done.9.refs_0_), channel_id=1, source_target_pairs={{0,4},{4,12},{12,8},{8,0},{1,5},{5,13},{13,9},{9,1},{2,6},{6,14},{... | collective-permute-start | bytes 786440 | tf_op jit(solution)/shard_map/ppermute | solution.py:319
  34.4 3.7 %collective-permute-start.11 = (bf16[8,128]{1,0:T(8,128)(2,1)S(1)}, bf16[8,128]{1,0:T(8,128)(2,1)S(1)}, u32[]{:S(2)}, u32[]{:S(2)}) collective-permute-start(bf16[8,128]{1,0:T(8,128)(2,1)S(1)} %collective-permute-done.6), channel_id=1, source_target_pairs={{0,1},{1,0},{2,3},{3,2},{4,5},{5,4},{6,7},{7,6},{8,9},{9,8},{10,11... | collective-permute-start | bytes 6152 | tf_op jit(solution)/shard_map/ppermute | solution.py:325
  39.9 12.7 %collective-permute-start.12 = (bf16[144,1024]{1,0:T(8,128)(2,1)S(1)}, bf16[144,1024]{1,0:T(8,128)(2,1)S(1)}, u32[]{:S(2)}, u32[]{:S(2)}) collective-permute-start(bf16[144,1024]{1,0:T(8,128)(2,1)S(1)} %collective-permute-done.7.refs_2_), channel_id=1, source_target_pairs={{0,2},{2,0},{1,3},{3,1},{4,6},{6,4},{5,7},{7,5},{8,10},{10,8},{9,1... | collective-permute-start | bytes 884744 | tf_op jit(solution)/shard_map/ppermute | solution.py:284
  44.3 8.4 %collective-permute-start.16 = (bf16[128,1024]{1,0:T(8,128)(2,1)S(1)}, bf16[128,1024]{1,0:T(8,128)(2,1)S(1)}, u32[]{:S(2)}, u32[]{:S(2)}) collective-permute-start(bf16[128,1024]{1,0:T(8,128)(2,1)S(1)} %collective-permute-done.14.refs_1_), channel_id=1, source_target_pairs={{0,4},{4,12},{12,8},{8,0},{1,5},{5,13},{13,9},{9,1},{2,6},{6,14},{... | collective-permute-start | bytes 786440 | tf_op jit(solution)/shard_map/ppermute | solution.py:315
  46.6 6.0 %collective-permute-start.15 = (bf16[8,128]{1,0:T(8,128)(2,1)S(1)}, bf16[8,128]{1,0:T(8,128)(2,1)S(1)}, u32[]{:S(2)}, u32[]{:S(2)}) collective-permute-start(bf16[8,128]{1,0:T(8,128)(2,1)S(1)} %collective-permute-done.11), channel_id=1, source_target_pairs={{0,1},{1,0},{2,3},{3,2},{4,5},{5,4},{6,7},{7,6},{8,9},{9,8},{10,11... | collective-permute-start | bytes 6152 | tf_op jit(solution)/shard_map/ppermute | solution.py:325
  46.6 10.3 %collective-permute-start.17 = (bf16[128,1024]{1,0:T(8,128)(2,1)S(1)}, bf16[128,1024]{1,0:T(8,128)(2,1)S(1)}, u32[]{:S(2)}, u32[]{:S(2)}) collective-permute-start(bf16[128,1024]{1,0:T(8,128)(2,1)S(1)} %get-tuple-element.241), channel_id=1, source_target_pairs={{0,2},{2,0},{1,3},{3,1},{4,6},{6,4},{5,7},{7,5},{8,10},{10,8},{9,1... | collective-permute-start | bytes 786440 | tf_op jit(solution)/shard_map/ppermute | solution.py:291
  51.0 10.4 %collective-permute-start.18 = (bf16[128,1024]{1,0:T(8,128)(2,1)S(1)}, bf16[128,1024]{1,0:T(8,128)(2,1)S(1)}, u32[]{:S(2)}, u32[]{:S(2)}) collective-permute-start(bf16[128,1024]{1,0:T(8,128)(2,1)S(1)} %get-tuple-element.210), channel_id=1, source_target_pairs={{0,2},{2,0},{1,3},{3,1},{4,6},{6,4},{5,7},{7,5},{8,10},{10,8},{9,1... | collective-permute-start | bytes 786440 | tf_op jit(solution)/shard_map/ppermute | solution.py:291
  56.3 10.4 %collective-permute-start.20 = (bf16[128,1024]{1,0:T(8,128)(2,1)S(1)}, bf16[128,1024]{1,0:T(8,128)(2,1)S(1)}, u32[]{:S(2)}, u32[]{:S(2)}) collective-permute-start(bf16[128,1024]{1,0:T(8,128)(2,1)S(1)} %get-tuple-element.237), channel_id=1, source_target_pairs={{0,2},{2,0},{1,3},{3,1},{4,6},{6,4},{5,7},{7,5},{8,10},{10,8},{9,1... | collective-permute-start | bytes 786440 | tf_op jit(solution)/shard_map/ppermute | solution.py:291
  57.0 7.9 %collective-permute-start.19 = (bf16[128,1024]{1,0:T(8,128)(2,1)S(1)}, bf16[128,1024]{1,0:T(8,128)(2,1)S(1)}, u32[]{:S(2)}, u32[]{:S(2)}) collective-permute-start(bf16[128,1024]{1,0:T(8,128)(2,1)S(1)} %add_convert_fusion.3), channel_id=1, source_target_pairs={{0,8},{4,0},{12,4},{8,12},{1,9},{5,1},{13,5},{9,13},{2,10},{6,2},{... | collective-permute-start | bytes 786440 | tf_op jit(solution)/shard_map/ppermute | solution.py:301
  61.4 11.1 %collective-permute-start.21 = (bf16[128,1024]{1,0:T(8,128)(2,1)S(1)}, bf16[128,1024]{1,0:T(8,128)(2,1)S(1)}, u32[]{:S(2)}, u32[]{:S(2)}) collective-permute-start(bf16[128,1024]{1,0:T(8,128)(2,1)S(1)} %add_convert_fusion.2), channel_id=1, source_target_pairs={{0,4},{4,12},{12,8},{8,0},{1,5},{5,13},{13,9},{9,1},{2,6},{6,14},{... | collective-permute-start | bytes 786440 | tf_op jit(solution)/shard_map/ppermute | solution.py:301
  72.5 5.7 %collective-permute-start.22 = (bf16[4,768,512]{2,1,0:T(8,128)(2,1)S(1)}, bf16[4,768,512]{2,1,0:T(8,128)(2,1)S(1)}, u32[]{:S(2)}, u32[]{:S(2)}) collective-permute-start(bf16[4,768,512]{2,1,0:T(8,128)(2,1)S(1)} %weight_grads.2), channel_id=1, source_target_pairs={{0,1},{1,0},{2,3},{3,2},{4,5},{5,4},{6,7},{7,6},{8,9},{9,8},{10,11... | collective-permute-start | bytes 9437192 | tf_op jit(solution)/shard_map/ppermute | solution.py:344
  72.6 9.7 %collective-permute-start.23 = (bf16[128,1024]{1,0:T(8,128)(2,1)S(1)}, bf16[128,1024]{1,0:T(8,128)(2,1)S(1)}, u32[]{:S(2)}, u32[]{:S(2)}) collective-permute-start(bf16[128,1024]{1,0:T(8,128)(2,1)S(1)} %add_convert_fusion.1), channel_id=1, source_target_pairs={{0,4},{4,12},{12,8},{8,0},{1,5},{5,13},{13,9},{9,1},{2,6},{6,14},{... | collective-permute-start | bytes 786440 | tf_op jit(solution)/shard_map/ppermute | solution.py:301
  72.7 9.6 %collective-permute-start.24 = (bf16[128,1024]{1,0:T(8,128)(2,1)S(1)}, bf16[128,1024]{1,0:T(8,128)(2,1)S(1)}, u32[]{:S(2)}, u32[]{:S(2)}) collective-permute-start(bf16[128,1024]{1,0:T(8,128)(2,1)S(1)} %get-tuple-element.283), channel_id=1, source_target_pairs={{0,2},{2,0},{1,3},{3,1},{4,6},{6,4},{5,7},{7,5},{8,10},{10,8},{9,1... | collective-permute-start | bytes 786440 | tf_op jit(solution)/shard_map/ppermute | solution.py:291

commit v19 on v11

--- a/solution.py
+++ b/solution.py
@@ -309,27 +309,30 @@
             tokens, upstream = (lax.ppermute(v, "group", along(1)) for v in (tokens, upstream))
         if k > 0:
             chunks[k - 1] = chunk(blocks[k - 1], k - 1 == 1)
-        tokens, pair[0], chunks, weights = tie(tokens, pair[0], chunks, weights)
-        upstream, pair[1] = tie(upstream, pair[1])
+        upstream, pair[1], chunks, weights = tie(upstream, pair[1], chunks, weights)
+        tokens, pair[0] = tie(tokens, pair[0])
         blocks[k] = pair
 
     for k in range(2, last - 1):
         sent[k] = homeward(group_sum(chunks[k][0], across(chunks[k][1])), k)
-    near = lax.ppermute(chunks[1][0], "group", along(-1))
+    near = homeward(chunks[1][0], 1)
     blocks[last], chunks = tie(blocks[last], chunks)
     backs[last - 1] = across(chunks[last - 1][1])
     chunks[last] = chunk(blocks[last])
-    chunks, backs, near = tie(chunks, backs, near)
-
     backs[last] = across(chunks[last][1])
+    chunks, backs[last - 1] = tie(chunks, backs[last - 1])
+
     carried = homeward(group_sum(chunks[last - 1][0], backs[last - 1]), last)
     kept = [[chunks[k][i] for k in range(n_group)] for i in (-3, -2, -1)]
+    kept, near = tie(kept, near)
     to_send = weight_call(other_half, *kept)
-    to_send, backs[last], carried = tie(to_send, backs[last], carried)
+    other = (wide(chunks[0][1]) + wide(near[tok_rows:])).astype(jnp.bfloat16)
+    to_send, backs[last], other = tie(to_send, backs[last], other)
+    to_send, carried = tie(to_send, carried)
 
     got = lax.ppermute(to_send, "dp", [(0, 1), (1, 0)])
     sent[last] = homeward(group_sum(chunks[last][0], [*backs[last], carried]), last)
-    backs[0] = across((wide(chunks[0][1]) + wide(near[tok_rows:])).astype(jnp.bfloat16))
+    backs[0] = across(other)
     grads = weight_call(half, *kept, got)
     grads, sent, backs[0] = tie(grads, sent, backs[0])
     total = wide(chunks[0][0]) + wide(near[:tok_rows])

time: 81 us -> 82.3 us (1.016)
  waiting for transfers between devices: 20.7 us -> 21.7 us
    ppermute x1 -> x0, starting transfers between devices: 1.84 us -> none  [per_device(): near = lax.ppermute(chunks[1][0], 'group', along(-1))]
    ppermute x2 -> x3, waiting for transfers between devices: 3.36 us -> 4.71 us  [homeward(): return lax.ppermute(group_part, 'group', along(-k))]
    ppermute x8, waiting for transfers between devices: 8.15 us -> 9.22 us  [spread(): lax.ppermute(column, 'ingroup', shift(s))]
    ppermute x1, waiting for transfers between devices: 2.86 us -> 1.9 us  [per_device(): got = lax.ppermute(to_send, 'dp', [(0, 1), (1, 0)])]
    ppermute x3, starting transfers between devices: 3.58 us -> 4.53 us  [across(): lax.ppermute(others[(s - 1) * tok_rows:s * tok_rows], 'ingroup', shift(-s))]
    ppermute x2 -> x3, starting transfers between devices: 5.41 us -> 6.03 us  [homeward(): return lax.ppermute(group_part, 'group', along(-k))]
  transfers between devices with their start and end apart: 21 -> 21, of which waited for: 14 -> 15; matrix products, arithmetic and copies ran while one was open for 0% -> 0% of each run, Pallas kernels for 30% -> 27%
where the time goes in v19:
time: 82.3 us; the launch traced here: 82.1 us
  starting transfers between devices  34.6 us (42%)
  Pallas kernels  23.9 us (29%)
  waiting for transfers between devices  21.7 us (26%)
  other arithmetic  1.13 us (1%)
    pallas_call x4, Pallas kernels, chunk_call(): pl.pallas_call(functools.partial(chunk_kernel, n_blocks, tok_rows, capaci...  14.7 us
    ppermute x6, starting transfers between devices, per_device(): lax.ppermute(v, 'group', along(1))  14 us
    ppermute x8, starting transfers between devices, spread(): lax.ppermute(column, 'ingroup', shift(s))  10.1 us
    ppermute x8, waiting for transfers between devices, spread(): lax.ppermute(column, 'ingroup', shift(s))  9.22 us
    ppermute x3, starting transfers between devices, homeward(): return lax.ppermute(group_part, 'group', along(-k))  6.03 us
    ppermute x3, waiting for transfers between devices, homeward(): return lax.ppermute(group_part, 'group', along(-k))  4.71 us
    pallas_call x2, Pallas kernels, weight_call(): pl.pallas_call(functools.partial(kernel, n), in_specs=[smem] + [vmem] * l...  4.57 us
    ppermute x3, starting transfers between devices, across(): lax.ppermute(others[(s - 1) * tok_rows:s * tok_rows], 'ingroup', shift(-s))  4.53 us
  transfers between devices with their start and end apart: 21, of which 15 were waited for; matrix products, arithmetic and copies ran while one was open for 0% of the time, Pallas kernels for 27%

profile of v19, /device:TPU:0, one launch (start us, length us, event | category | flops | bytes accessed | tf_op | source)
XLA Modules:
  0.0 82.1 jit_solution(16289782627617861713)
XLA Ops:
  0.6 1.8 %pack.1 = (bf16[128,1024]{1,0:T(8,128)(2,1)S(1)}, bf16[144,1024]{1,0:T(8,128)(2,1)S(1)}) custom-call(bf16[128,1024]{1,0:T(8,128)(2,1)} %tokens, bf16[128,1024]{1,0:T(8,128)(2,1)} %upstream.1, s32[8,128]{1,0:T(8,128)} %bitcast.5, s32[8,128]{1,0:T(8,128)} %bitcast.6, s32[8,128]{1,0:T(8,128)} %bitcast.7), custom_call_target="tpu_custom_call" | custom-call | tf_op jit(solution)/shard_map/pack/pallas_call | solution.py:58
  2.4 3.1 %collective-permute-start.7 = (bf16[144,1024]{1,0:T(8,128)(2,1)S(1)}, bf16[144,1024]{1,0:T(8,128)(2,1)S(1)}, u32[]{:S(2)}, u32[]{:S(2)}) collective-permute-start(bf16[144,1024]{1,0:T(8,128)(2,1)S(1)} %get-tuple-element.169.refs_2_), channel_id=1, source_target_pairs={{0,4},{4,12},{12,8},{8,0},{1,5},{5,13},{13,9},{9,1},{2,6},{6,14},{... | collective-permute-start | bytes 884744 | tf_op jit(solution)/shard_map/ppermute | solution.py:309
  5.5 1.5 %collective-permute-start.8 = (bf16[144,1024]{1,0:T(8,128)(2,1)S(1)}, bf16[144,1024]{1,0:T(8,128)(2,1)S(1)}, u32[]{:S(2)}, u32[]{:S(2)}) collective-permute-start(bf16[144,1024]{1,0:T(8,128)(2,1)S(1)} %get-tuple-element.169.refs_2_), channel_id=1, source_target_pairs={{0,2},{2,0},{1,3},{3,1},{4,6},{6,4},{5,7},{7,5},{8,10},{10,8},{9,1... | collective-permute-start | bytes 884744 | tf_op jit(solution)/shard_map/ppermute | solution.py:281
  7.0 2.6 %collective-permute-start = (bf16[128,1024]{1,0:T(8,128)(2,1)}, bf16[128,1024]{1,0:T(8,128)(2,1)S(1)}, u32[]{:S(2)}, u32[]{:S(2)}) collective-permute-start(bf16[128,1024]{1,0:T(8,128)(2,1)} %tokens), channel_id=1, source_target_pairs={{0,4},{4,12},{12,8},{8,0},{1,5},{5,13},{13,9},{9,1},{2,6},{6,14},{... | collective-permute-start | bytes 786440 | tf_op jit(solution)/shard_map/ppermute | solution.py:309
  9.6 0.5 collective-permute-start.1
  10.1 2.9 %load.1 = (bf16[4,1024,256]{2,1,0:T(8,128)(2,1)S(1)}, bf16[4,1024,256]{2,1,0:T(8,128)(2,1)S(1)}, bf16[4,256,1024]{2,1,0:T(8,128)(2,1)S(1)}) custom-call(bf16[4,1024,256]{2,1,0:T(8,128)(2,1)} %refs_0_.1, bf16[4,1024,256]{2,1,0:T(8,128)(2,1)} %refs_1_.1, bf16[4,256,1024]{2,1,0:T(8,128)(2,1)} %refs_2_.1), custom_call_target="tpu_custom_call" | custom-call | tf_op jit(solution)/shard_map/load/pallas_call | solution.py:98
  13.0 1.3 %collective-permute-done.7.refs_2_ = bf16[144,1024]{1,0:T(8,128)(2,1)S(1)} collective-permute-done((bf16[144,1024]{1,0:T(8,128)(2,1)S(1)}, bf16[144,1024]{1,0:T(8,128)(2,1)S(1)}, u32[]{:S(2)}, u32[]{:S(2)}) %collective-permute-start.7) | collective-permute-done | bytes 294944 | tf_op jit(solution)/shard_map/ppermute | solution.py:309
  14.3 1.1 %collective-permute-done.8.refs_3_ = bf16[144,1024]{1,0:T(8,128)(2,1)S(1)} collective-permute-done((bf16[144,1024]{1,0:T(8,128)(2,1)S(1)}, bf16[144,1024]{1,0:T(8,128)(2,1)S(1)}, u32[]{:S(2)}, u32[]{:S(2)}) %collective-permute-start.8) | collective-permute-done | bytes 294944 | tf_op jit(solution)/shard_map/ppermute | solution.py:281
  15.4 2.6 %collective-permute-start.9 = (bf16[144,1024]{1,0:T(8,128)(2,1)S(1)}, bf16[144,1024]{1,0:T(8,128)(2,1)S(1)}, u32[]{:S(2)}, u32[]{:S(2)}) collective-permute-start(bf16[144,1024]{1,0:T(8,128)(2,1)S(1)} %collective-permute-done.7.refs_2_), channel_id=1, source_target_pairs={{0,4},{4,12},{12,8},{8,0},{1,5},{5,13},{13,9},{9,1},{2,6},{6,14},{... | collective-permute-start | bytes 884744 | tf_op jit(solution)/shard_map/ppermute | solution.py:309
  18.0 1.5 %collective-permute-start.10 = (bf16[144,1024]{1,0:T(8,128)(2,1)S(1)}, bf16[144,1024]{1,0:T(8,128)(2,1)S(1)}, u32[]{:S(2)}, u32[]{:S(2)}) collective-permute-start(bf16[144,1024]{1,0:T(8,128)(2,1)S(1)} %collective-permute-done.7.refs_2_), channel_id=1, source_target_pairs={{0,2},{2,0},{1,3},{3,1},{4,6},{6,4},{5,7},{7,5},{8,10},{10,8},{9,1... | collective-permute-start | bytes 884744 | tf_op jit(solution)/shard_map/ppermute | solution.py:281
  19.5 0.5 collective-permute-done.refs_0_
  20.0 1.1 %collective-permute-done.1.refs_1_ = bf16[128,1024]{1,0:T(8,128)(2,1)S(1)} collective-permute-done((bf16[128,1024]{1,0:T(8,128)(2,1)}, bf16[128,1024]{1,0:T(8,128)(2,1)S(1)}, u32[]{:S(2)}, u32[]{:S(2)}) %collective-permute-start.1) | collective-permute-done | bytes 262176 | tf_op jit(solution)/shard_map/ppermute | solution.py:281
  21.0 2.6 %collective-permute-start.2 = (bf16[128,1024]{1,0:T(8,128)(2,1)S(1)}, bf16[128,1024]{1,0:T(8,128)(2,1)S(1)}, u32[]{:S(2)}, u32[]{:S(2)}) collective-permute-start(bf16[128,1024]{1,0:T(8,128)(2,1)S(1)} %collective-permute-done.refs_0_), channel_id=1, source_target_pairs={{0,4},{4,12},{12,8},{8,0},{1,5},{5,13},{13,9},{9,1},{2,6},{6,14},{... | collective-permute-start | bytes 786440 | tf_op jit(solution)/shard_map/ppermute | solution.py:309
  23.6 1.5 %collective-permute-start.3 = (bf16[128,1024]{1,0:T(8,128)(2,1)S(1)}, bf16[128,1024]{1,0:T(8,128)(2,1)S(1)}, u32[]{:S(2)}, u32[]{:S(2)}) collective-permute-start(bf16[128,1024]{1,0:T(8,128)(2,1)S(1)} %collective-permute-done.refs_0_), channel_id=1, source_target_pairs={{0,2},{2,0},{1,3},{3,1},{4,6},{6,4},{5,7},{7,5},{8,10},{10,8},{9,1... | collective-permute-start | bytes 786440 | tf_op jit(solution)/shard_map/ppermute | solution.py:281
  25.1 3.7 %chunk.4 = (bf16[128,1024]{1,0:T(8,128)(2,1)S(1)}, bf16[128,1024]{1,0:T(8,128)(2,1)S(1)}, bf16[4,96,1024]{2,1,0:T(8,128)(2,1)S(1)}, bf16[4,96,1024]{2,1,0:T(8,128)(2,1)S(1)}, bf16[4,96,768]{2,1,0:T(8,128)(2,1)S(1)}) custom-call(s32[1]{0:T(128)} %bitcast.first_ref, bf16[128,1024]{1,0:T(8,128)(2,1)S(1)} %get-tuple-element.167.refs_0_, ...), custom_call_target="tpu_custom_call" | custom-call | flops 1610612736 | bytes 8388608 | tf_op jit(solution)/shard_map/chunk/pallas_call | solution.py:171
  28.8 0.0 collective-permute-done.9.refs_2_
  28.8 0.0 collective-permute-done.10.refs_3_
  28.8 1.1 %collective-permute-start.11 = (bf16[144,1024]{1,0:T(8,128)(2,1)S(1)}, bf16[144,1024]{1,0:T(8,128)(2,1)S(1)}, u32[]{:S(2)}, u32[]{:S(2)}) collective-permute-start(bf16[144,1024]{1,0:T(8,128)(2,1)S(1)} %collective-permute-done.9.refs_2_), channel_id=1, source_target_pairs={{0,4},{4,12},{12,8},{8,0},{1,5},{5,13},{13,9},{9,1},{2,6},{6,14},{... | collective-permute-start | bytes 884744 | tf_op jit(solution)/shard_map/ppermute | solution.py:309
  30.0 1.5 %collective-permute-start.12 = (bf16[144,1024]{1,0:T(8,128)(2,1)S(1)}, bf16[144,1024]{1,0:T(8,128)(2,1)S(1)}, u32[]{:S(2)}, u32[]{:S(2)}) collective-permute-start(bf16[144,1024]{1,0:T(8,128)(2,1)S(1)} %collective-permute-done.9.refs_2_), channel_id=1, source_target_pairs={{0,2},{2,0},{1,3},{3,1},{4,6},{6,4},{5,7},{7,5},{8,10},{10,8},{9,1... | collective-permute-start | bytes 884744 | tf_op jit(solution)/shard_map/ppermute | solution.py:281
  31.4 0.5 collective-permute-done.2.refs_0_
  31.9 1.7 %collective-permute-done.3.refs_1_ = bf16[128,1024]{1,0:T(8,128)(2,1)S(1)} collective-permute-done((bf16[128,1024]{1,0:T(8,128)(2,1)S(1)}, bf16[128,1024]{1,0:T(8,128)(2,1)S(1)}, u32[]{:S(2)}, u32[]{:S(2)}) %collective-permute-start.3) | collective-permute-done | bytes 262176 | tf_op jit(solution)/shard_map/ppermute | solution.py:281
  33.6 2.0 %collective-permute-start.4 = (bf16[128,1024]{1,0:T(8,128)(2,1)S(1)}, bf16[128,1024]{1,0:T(8,128)(2,1)S(1)}, u32[]{:S(2)}, u32[]{:S(2)}) collective-permute-start(bf16[128,1024]{1,0:T(8,128)(2,1)S(1)} %collective-permute-done.2.refs_0_), channel_id=1, source_target_pairs={{0,4},{4,12},{12,8},{8,0},{1,5},{5,13},{13,9},{9,1},{2,6},{6,14},{... | collective-permute-start | bytes 786440 | tf_op jit(solution)/shard_map/ppermute | solution.py:309
  35.6 1.5 %collective-permute-start.5 = (bf16[128,1024]{1,0:T(8,128)(2,1)S(1)}, bf16[128,1024]{1,0:T(8,128)(2,1)S(1)}, u32[]{:S(2)}, u32[]{:S(2)}) collective-permute-start(bf16[128,1024]{1,0:T(8,128)(2,1)S(1)} %collective-permute-done.2.refs_0_), channel_id=1, source_target_pairs={{0,2},{2,0},{1,3},{3,1},{4,6},{6,4},{5,7},{7,5},{8,10},{10,8},{9,1... | collective-permute-start | bytes 786440 | tf_op jit(solution)/shard_map/ppermute | solution.py:281
  37.1 3.7 %chunk.5 = (bf16[256,1024]{1,0:T(8,128)(2,1)S(1)}, bf16[4,96,1024]{2,1,0:T(8,128)(2,1)S(1)}, bf16[4,96,1024]{2,1,0:T(8,128)(2,1)S(1)}, bf16[4,96,768]{2,1,0:T(8,128)(2,1)S(1)}) custom-call(s32[1]{0:T(128)} %bitcast.first_ref, bf16[128,1024]{1,0:T(8,128)(2,1)S(1)} %collective-permute-done.refs_0_, bf16[128,1024]{1,0:T(8,128)(2,1)S(1)} %collective-permute-done.3.refs_1_, ...), custom_call_target="tpu_custom_call" | custom-call | flops 1610612736 | bytes 8388608 | tf_op jit(solution)/shard_map/chunk/pallas_call | solution.py:171
  40.7 0.0 collective-permute-done.11.refs_2_
  40.8 0.0 collective-permute-done.12.refs_3_
  40.8 0.6 collective-permute-start.13
  41.4 1.6 %collective-permute-done.4.refs_0_ = bf16[128,1024]{1,0:T(8,128)(2,1)S(1)} collective-permute-done((bf16[128,1024]{1,0:T(8,128)(2,1)S(1)}, bf16[128,1024]{1,0:T(8,128)(2,1)S(1)}, u32[]{:S(2)}, u32[]{:S(2)}) %collective-permute-start.4) | collective-permute-done | bytes 262176 | tf_op jit(solution)/shard_map/ppermute | solution.py:309
  43.0 2.5 %collective-permute-done.5.refs_1_ = bf16[128,1024]{1,0:T(8,128)(2,1)S(1)} collective-permute-done((bf16[128,1024]{1,0:T(8,128)(2,1)S(1)}, bf16[128,1024]{1,0:T(8,128)(2,1)S(1)}, u32[]{:S(2)}, u32[]{:S(2)}) %collective-permute-start.5) | collective-permute-done | bytes 262176 | tf_op jit(solution)/shard_map/ppermute | solution.py:281
  45.5 1.5 %collective-permute-start.6 = (bf16[128,1024]{1,0:T(8,128)(2,1)S(1)}, bf16[128,1024]{1,0:T(8,128)(2,1)S(1)}, u32[]{:S(2)}, u32[]{:S(2)}) collective-permute-start(bf16[128,1024]{1,0:T(8,128)(2,1)S(1)} %collective-permute-done.4.refs_0_), channel_id=1, source_target_pairs={{0,2},{2,0},{1,3},{3,1},{4,6},{6,4},{5,7},{7,5},{8,10},{10,8},{9,1... | collective-permute-start | bytes 786440 | tf_op jit(solution)/shard_map/ppermute | solution.py:281
  47.0 3.7 %chunk.6 = (bf16[128,1024]{1,0:T(8,128)(2,1)S(1)}, bf16[128,1024]{1,0:T(8,128)(2,1)S(1)}, bf16[4,96,1024]{2,1,0:T(8,128)(2,1)S(1)}, bf16[4,96,1024]{2,1,0:T(8,128)(2,1)S(1)}, bf16[4,96,768]{2,1,0:T(8,128)(2,1)S(1)}) custom-call(s32[1]{0:T(128)} %bitcast.first_ref, bf16[128,1024]{1,0:T(8,128)(2,1)S(1)} %collective-permute-done.2.refs_0_, ...), custom_call_target="tpu_custom_call" | custom-call | flops 1610612736 | bytes 8388608 | tf_op jit(solution)/shard_map/chunk/pallas_call | solution.py:171
  50.7 1.1 %collective-permute-done.13.refs_3_ = bf16[144,1024]{1,0:T(8,128)(2,1)S(1)} collective-permute-done((bf16[144,1024]{1,0:T(8,128)(2,1)S(1)}, bf16[144,1024]{1,0:T(8,128)(2,1)S(1)}, u32[]{:S(2)}, u32[]{:S(2)}) %collective-permute-start.13) | collective-permute-done | bytes 294944 | tf_op jit(solution)/shard_map/ppermute | solution.py:281
  51.8 1.8 %collective-permute-start.15 = (bf16[256,1024]{1,0:T(8,128)(2,1)S(1)}, bf16[256,1024]{1,0:T(8,128)(2,1)S(1)}, u32[]{:S(2)}, u32[]{:S(2)}) collective-permute-start(bf16[256,1024]{1,0:T(8,128)(2,1)S(1)} %get-tuple-element.225), channel_id=1, source_target_pairs={{0,8},{4,0},{12,4},{8,12},{1,9},{5,1},{13,5},{9,13},{2,10},{6,2},{... | collective-permute-start | bytes 1572872 | tf_op jit(solution)/shard_map/ppermute | solution.py:298
  53.7 1.7 %collective-permute-done.6.refs_1_ = bf16[128,1024]{1,0:T(8,128)(2,1)S(1)} collective-permute-done((bf16[128,1024]{1,0:T(8,128)(2,1)S(1)}, bf16[128,1024]{1,0:T(8,128)(2,1)S(1)}, u32[]{:S(2)}, u32[]{:S(2)}) %collective-permute-start.6) | collective-permute-done | bytes 262176 | tf_op jit(solution)/shard_map/ppermute | solution.py:281
  55.4 1.5 %collective-permute-start.14 = (bf16[128,1024]{1,0:T(8,128)(2,1)S(1)}, bf16[128,1024]{1,0:T(8,128)(2,1)S(1)}, u32[]{:S(2)}, u32[]{:S(2)}) collective-permute-start(bf16[128,1024]{1,0:T(8,128)(2,1)S(1)} %get-tuple-element.243), channel_id=1, source_target_pairs={{0,2},{2,0},{1,3},{3,1},{4,6},{6,4},{5,7},{7,5},{8,10},{10,8},{9,1... | collective-permute-start | bytes 786440 | tf_op jit(solution)/shard_map/ppermute | solution.py:288
  56.9 3.7 %chunk.7 = (bf16[128,1024]{1,0:T(8,128)(2,1)S(1)}, bf16[128,1024]{1,0:T(8,128)(2,1)S(1)}, bf16[4,96,1024]{2,1,0:T(8,128)(2,1)S(1)}, bf16[4,96,1024]{2,1,0:T(8,128)(2,1)S(1)}, bf16[4,96,768]{2,1,0:T(8,128)(2,1)S(1)}) custom-call(s32[1]{0:T(128)} %bitcast.first_ref, bf16[128,1024]{1,0:T(8,128)(2,1)S(1)} %collective-permute-done.4.refs_0_, ...), custom_call_target="tpu_custom_call" | custom-call | flops 1610612736 | bytes 8388608 | tf_op jit(solution)/shard_map/chunk/pallas_call | solution.py:171
  60.6 0.6 collective-permute-start.16
  61.2 1.3 %collective-permute-done.14 = bf16[128,1024]{1,0:T(8,128)(2,1)S(1)} collective-permute-done((bf16[128,1024]{1,0:T(8,128)(2,1)S(1)}, bf16[128,1024]{1,0:T(8,128)(2,1)S(1)}, u32[]{:S(2)}, u32[]{:S(2)}) %collective-permute-start.14) | collective-permute-done | bytes 262176 | tf_op jit(solution)/shard_map/ppermute | solution.py:288
  62.5 0.1 add_convert_fusion.2
  62.6 3.0 %collective-permute-start.17 = (bf16[128,1024]{1,0:T(8,128)(2,1)S(1)}, bf16[128,1024]{1,0:T(8,128)(2,1)S(1)}, u32[]{:S(2)}, u32[]{:S(2)}) collective-permute-start(bf16[128,1024]{1,0:T(8,128)(2,1)S(1)} %add_convert_fusion.2), channel_id=1, source_target_pairs={{0,4},{4,12},{12,8},{8,0},{1,5},{5,13},{13,9},{9,1},{2,6},{6,14},{... | collective-permute-start | bytes 786440 | tf_op jit(solution)/shard_map/ppermute | solution.py:298
  65.6 0.0 collective-permute-done.15
  65.6 1.9 %weight_grads.2 = bf16[4,768,512]{2,1,0:T(8,128)(2,1)S(1)} custom-call(s32[1]{0:T(128)S(6)} %sub.3.side_ref, bf16[4,96,1024]{2,1,0:T(8,128)(2,1)S(1)} %get-tuple-element.274.refs_0_, bf16[4,96,1024]{2,1,0:T(8,128)(2,1)S(1)} %get-tuple-element.275.refs_1_, bf16[4,96,1024]{2,1,0:T(8,128)(2,1)S(1)} %get-tuple-element.276.refs_2_, ...), custom_call_target="tpu_custom_call" | custom-call | flops 1207959552 | bytes 8650752 | tf_op jit(solution)/shard_map/weight_grads/pallas_call | solution.py:244
  67.4 0.1 add_convert_fusion.3
  67.5 0.0 collective-permute-done.16
  67.5 3.3 %collective-permute-done.17 = bf16[128,1024]{1,0:T(8,128)(2,1)S(1)} collective-permute-done((bf16[128,1024]{1,0:T(8,128)(2,1)S(1)}, bf16[128,1024]{1,0:T(8,128)(2,1)S(1)}, u32[]{:S(2)}, u32[]{:S(2)}) %collective-permute-start.17) | collective-permute-done | bytes 262176 | tf_op jit(solution)/shard_map/ppermute | solution.py:298
  70.8 0.0 collective-permute-start.18
  70.8 0.1 add_convert_fusion.1
  70.9 1.2 %collective-permute-start.19 = (bf16[128,1024]{1,0:T(8,128)(2,1)S(1)}, bf16[128,1024]{1,0:T(8,128)(2,1)S(1)}, u32[]{:S(2)}, u32[]{:S(2)}) collective-permute-start(bf16[128,1024]{1,0:T(8,128)(2,1)S(1)} %add_convert_fusion.1), channel_id=1, source_target_pairs={{0,4},{4,12},{12,8},{8,0},{1,5},{5,13},{13,9},{9,1},{2,6},{6,14},{... | collective-permute-start | bytes 786440 | tf_op jit(solution)/shard_map/ppermute | solution.py:298
  72.1 2.4 %collective-permute-start.20 = (bf16[128,1024]{1,0:T(8,128)(2,1)S(1)}, bf16[128,1024]{1,0:T(8,128)(2,1)S(1)}, u32[]{:S(2)}, u32[]{:S(2)}) collective-permute-start(bf16[128,1024]{1,0:T(8,128)(2,1)S(1)} %add_convert_fusion.3), channel_id=1, source_target_pairs={{0,2},{2,0},{1,3},{3,1},{4,6},{6,4},{5,7},{7,5},{8,10},{10,8},{9,1... | collective-permute-start | bytes 786440 | tf_op jit(solution)/shard_map/ppermute | solution.py:288
  74.6 1.9 %collective-permute-done.18.refs_12_ = bf16[4,768,512]{2,1,0:T(8,128)(2,1)S(1)} collective-permute-done((bf16[4,768,512]{2,1,0:T(8,128)(2,1)S(1)}, bf16[4,768,512]{2,1,0:T(8,128)(2,1)S(1)}, u32[]{:S(2)}, u32[]{:S(2)}) %collective-permute-start.18) | collective-permute-done | bytes 3145760 | tf_op jit(solution)/shard_map/ppermute | solution.py:333
  76.4 2.7 %weight_grads.3 = (bf16[4,512,256]{2,1,0:T(8,128)(2,1)}, bf16[4,512,256]{2,1,0:T(8,128)(2,1)}, bf16[4,256,512]{2,1,0:T(8,128)(2,1)}) custom-call(s32[1]{0:T(128)} %bitcast.1.side_ref, bf16[4,96,1024]{2,1,0:T(8,128)(2,1)S(1)} %get-tuple-element.274.refs_0_, bf16[4,96,1024]{2,1,0:T(8,128)(2,1)S(1)} %get-tuple-element.275.refs_1_, ...), custom_call_target="tpu_custom_call" | custom-call | flops 1207959552 | bytes 8650752 | tf_op jit(solution)/shard_map/weight_grads/pallas_call | solution.py:244
  79.2 1.4 %collective-permute-done.19 = bf16[128,1024]{1,0:T(8,128)(2,1)S(1)} collective-permute-done((bf16[128,1024]{1,0:T(8,128)(2,1)S(1)}, bf16[128,1024]{1,0:T(8,128)(2,1)S(1)}, u32[]{:S(2)}, u32[]{:S(2)}) %collective-permute-start.19) | collective-permute-done | bytes 262176 | tf_op jit(solution)/shard_map/ppermute | solution.py:298
  80.6 0.7 collective-permute-done.20
  81.2 0.9 %add_convert_fusion = bf16[128,1024]{1,0:T(8,128)(2,1)} fusion(bf16[128,1024]{1,0:T(8,128)(2,1)S(1)} %collective-permute-done.19, bf16[128,1024]{1,0:T(8,128)(2,1)S(1)} %collective-permute-done.20, bf16[128,1024]{1,0:T(8,128)(2,1)S(1)} %get-tuple-element.259, bf16[256,1024]{1,0:T(8,128)(2,1)S(1)} %collective-permute-done.15), kind=kLoop, calls=%fused_computation | loop fusion | flops 1048576 | bytes 1310720 | tf_op jit(solution)/shard_map/convert_element_type | solution.py:343
Async XLA Ops:
  2.4 11.9 %collective-permute-start.7 = (bf16[144,1024]{1,0:T(8,128)(2,1)S(1)}, bf16[144,1024]{1,0:T(8,128)(2,1)S(1)}, u32[]{:S(2)}, u32[]{:S(2)}) collective-permute-start(bf16[144,1024]{1,0:T(8,128)(2,1)S(1)} %get-tuple-element.169.refs_2_), channel_id=1, source_target_pairs={{0,4},{4,12},{12,8},{8,0},{1,5},{5,13},{13,9},{9,1},{2,6},{6,14},{... | collective-permute-start | bytes 884744 | tf_op jit(solution)/shard_map/ppermute | solution.py:309
  5.5 9.9 %collective-permute-start.8 = (bf16[144,1024]{1,0:T(8,128)(2,1)S(1)}, bf16[144,1024]{1,0:T(8,128)(2,1)S(1)}, u32[]{:S(2)}, u32[]{:S(2)}) collective-permute-start(bf16[144,1024]{1,0:T(8,128)(2,1)S(1)} %get-tuple-element.169.refs_2_), channel_id=1, source_target_pairs={{0,2},{2,0},{1,3},{3,1},{4,6},{6,4},{5,7},{7,5},{8,10},{10,8},{9,1... | collective-permute-start | bytes 884744 | tf_op jit(solution)/shard_map/ppermute | solution.py:281
  7.0 13.0 %collective-permute-start = (bf16[128,1024]{1,0:T(8,128)(2,1)}, bf16[128,1024]{1,0:T(8,128)(2,1)S(1)}, u32[]{:S(2)}, u32[]{:S(2)}) collective-permute-start(bf16[128,1024]{1,0:T(8,128)(2,1)} %tokens), channel_id=1, source_target_pairs={{0,4},{4,12},{12,8},{8,0},{1,5},{5,13},{13,9},{9,1},{2,6},{6,14},{... | collective-permute-start | bytes 786440 | tf_op jit(solution)/shard_map/ppermute | solution.py:309
  9.6 11.5 %collective-permute-start.1 = (bf16[128,1024]{1,0:T(8,128)(2,1)}, bf16[128,1024]{1,0:T(8,128)(2,1)S(1)}, u32[]{:S(2)}, u32[]{:S(2)}) collective-permute-start(bf16[128,1024]{1,0:T(8,128)(2,1)} %tokens), channel_id=1, source_target_pairs={{0,2},{2,0},{1,3},{3,1},{4,6},{6,4},{5,7},{7,5},{8,10},{10,8},{9,1... | collective-permute-start | bytes 786440 | tf_op jit(solution)/shard_map/ppermute | solution.py:281
  15.4 13.4 %collective-permute-start.9 = (bf16[144,1024]{1,0:T(8,128)(2,1)S(1)}, bf16[144,1024]{1,0:T(8,128)(2,1)S(1)}, u32[]{:S(2)}, u32[]{:S(2)}) collective-permute-start(bf16[144,1024]{1,0:T(8,128)(2,1)S(1)} %collective-permute-done.7.refs_2_), channel_id=1, source_target_pairs={{0,4},{4,12},{12,8},{8,0},{1,5},{5,13},{13,9},{9,1},{2,6},{6,14},{... | collective-permute-start | bytes 884744 | tf_op jit(solution)/shard_map/ppermute | solution.py:309
  18.0 10.8 %collective-permute-start.10 = (bf16[144,1024]{1,0:T(8,128)(2,1)S(1)}, bf16[144,1024]{1,0:T(8,128)(2,1)S(1)}, u32[]{:S(2)}, u32[]{:S(2)}) collective-permute-start(bf16[144,1024]{1,0:T(8,128)(2,1)S(1)} %collective-permute-done.7.refs_2_), channel_id=1, source_target_pairs={{0,2},{2,0},{1,3},{3,1},{4,6},{6,4},{5,7},{7,5},{8,10},{10,8},{9,1... | collective-permute-start | bytes 884744 | tf_op jit(solution)/shard_map/ppermute | solution.py:281
  21.0 10.9 %collective-permute-start.2 = (bf16[128,1024]{1,0:T(8,128)(2,1)S(1)}, bf16[128,1024]{1,0:T(8,128)(2,1)S(1)}, u32[]{:S(2)}, u32[]{:S(2)}) collective-permute-start(bf16[128,1024]{1,0:T(8,128)(2,1)S(1)} %collective-permute-done.refs_0_), channel_id=1, source_target_pairs={{0,4},{4,12},{12,8},{8,0},{1,5},{5,13},{13,9},{9,1},{2,6},{6,14},{... | collective-permute-start | bytes 786440 | tf_op jit(solution)/shard_map/ppermute | solution.py:309
  23.6 9.9 %collective-permute-start.3 = (bf16[128,1024]{1,0:T(8,128)(2,1)S(1)}, bf16[128,1024]{1,0:T(8,128)(2,1)S(1)}, u32[]{:S(2)}, u32[]{:S(2)}) collective-permute-start(bf16[128,1024]{1,0:T(8,128)(2,1)S(1)} %collective-permute-done.refs_0_), channel_id=1, source_target_pairs={{0,2},{2,0},{1,3},{3,1},{4,6},{6,4},{5,7},{7,5},{8,10},{10,8},{9,1... | collective-permute-start | bytes 786440 | tf_op jit(solution)/shard_map/ppermute | solution.py:281
  28.8 11.9 %collective-permute-start.11 = (bf16[144,1024]{1,0:T(8,128)(2,1)S(1)}, bf16[144,1024]{1,0:T(8,128)(2,1)S(1)}, u32[]{:S(2)}, u32[]{:S(2)}) collective-permute-start(bf16[144,1024]{1,0:T(8,128)(2,1)S(1)} %collective-permute-done.9.refs_2_), channel_id=1, source_target_pairs={{0,4},{4,12},{12,8},{8,0},{1,5},{5,13},{13,9},{9,1},{2,6},{6,14},{... | collective-permute-start | bytes 884744 | tf_op jit(solution)/shard_map/ppermute | solution.py:309
  30.0 10.8 %collective-permute-start.12 = (bf16[144,1024]{1,0:T(8,128)(2,1)S(1)}, bf16[144,1024]{1,0:T(8,128)(2,1)S(1)}, u32[]{:S(2)}, u32[]{:S(2)}) collective-permute-start(bf16[144,1024]{1,0:T(8,128)(2,1)S(1)} %collective-permute-done.9.refs_2_), channel_id=1, source_target_pairs={{0,2},{2,0},{1,3},{3,1},{4,6},{6,4},{5,7},{7,5},{8,10},{10,8},{9,1... | collective-permute-start | bytes 884744 | tf_op jit(solution)/shard_map/ppermute | solution.py:281
  33.6 9.4 %collective-permute-start.4 = (bf16[128,1024]{1,0:T(8,128)(2,1)S(1)}, bf16[128,1024]{1,0:T(8,128)(2,1)S(1)}, u32[]{:S(2)}, u32[]{:S(2)}) collective-permute-start(bf16[128,1024]{1,0:T(8,128)(2,1)S(1)} %collective-permute-done.2.refs_0_), channel_id=1, source_target_pairs={{0,4},{4,12},{12,8},{8,0},{1,5},{5,13},{13,9},{9,1},{2,6},{6,14},{... | collective-permute-start | bytes 786440 | tf_op jit(solution)/shard_map/ppermute | solution.py:309
  35.6 9.9 %collective-permute-start.5 = (bf16[128,1024]{1,0:T(8,128)(2,1)S(1)}, bf16[128,1024]{1,0:T(8,128)(2,1)S(1)}, u32[]{:S(2)}, u32[]{:S(2)}) collective-permute-start(bf16[128,1024]{1,0:T(8,128)(2,1)S(1)} %collective-permute-done.2.refs_0_), channel_id=1, source_target_pairs={{0,2},{2,0},{1,3},{3,1},{4,6},{6,4},{5,7},{7,5},{8,10},{10,8},{9,1... | collective-permute-start | bytes 786440 | tf_op jit(solution)/shard_map/ppermute | solution.py:281
  40.8 11.1 %collective-permute-start.13 = (bf16[144,1024]{1,0:T(8,128)(2,1)S(1)}, bf16[144,1024]{1,0:T(8,128)(2,1)S(1)}, u32[]{:S(2)}, u32[]{:S(2)}) collective-permute-start(bf16[144,1024]{1,0:T(8,128)(2,1)S(1)} %collective-permute-done.11.refs_2_), channel_id=1, source_target_pairs={{0,2},{2,0},{1,3},{3,1},{4,6},{6,4},{5,7},{7,5},{8,10},{10,8},{9,1... | collective-permute-start | bytes 884744 | tf_op jit(solution)/shard_map/ppermute | solution.py:281
  45.5 9.9 %collective-permute-start.6 = (bf16[128,1024]{1,0:T(8,128)(2,1)S(1)}, bf16[128,1024]{1,0:T(8,128)(2,1)S(1)}, u32[]{:S(2)}, u32[]{:S(2)}) collective-permute-start(bf16[128,1024]{1,0:T(8,128)(2,1)S(1)} %collective-permute-done.4.refs_0_), channel_id=1, source_target_pairs={{0,2},{2,0},{1,3},{3,1},{4,6},{6,4},{5,7},{7,5},{8,10},{10,8},{9,1... | collective-permute-start | bytes 786440 | tf_op jit(solution)/shard_map/ppermute | solution.py:281
  51.8 13.7 %collective-permute-start.15 = (bf16[256,1024]{1,0:T(8,128)(2,1)S(1)}, bf16[256,1024]{1,0:T(8,128)(2,1)S(1)}, u32[]{:S(2)}, u32[]{:S(2)}) collective-permute-start(bf16[256,1024]{1,0:T(8,128)(2,1)S(1)} %get-tuple-element.225), channel_id=1, source_target_pairs={{0,8},{4,0},{12,4},{8,12},{1,9},{5,1},{13,5},{9,13},{2,10},{6,2},{... | collective-permute-start | bytes 1572872 | tf_op jit(solution)/shard_map/ppermute | solution.py:298
  55.4 7.1 %collective-permute-start.14 = (bf16[128,1024]{1,0:T(8,128)(2,1)S(1)}, bf16[128,1024]{1,0:T(8,128)(2,1)S(1)}, u32[]{:S(2)}, u32[]{:S(2)}) collective-permute-start(bf16[128,1024]{1,0:T(8,128)(2,1)S(1)} %get-tuple-element.243), channel_id=1, source_target_pairs={{0,2},{2,0},{1,3},{3,1},{4,6},{6,4},{5,7},{7,5},{8,10},{10,8},{9,1... | collective-permute-start | bytes 786440 | tf_op jit(solution)/shard_map/ppermute | solution.py:288
  60.6 6.9 %collective-permute-start.16 = (bf16[128,1024]{1,0:T(8,128)(2,1)S(1)}, bf16[128,1024]{1,0:T(8,128)(2,1)S(1)}, u32[]{:S(2)}, u32[]{:S(2)}) collective-permute-start(bf16[128,1024]{1,0:T(8,128)(2,1)S(1)} %get-tuple-element.255), channel_id=1, source_target_pairs={{0,2},{2,0},{1,3},{3,1},{4,6},{6,4},{5,7},{7,5},{8,10},{10,8},{9,1... | collective-permute-start | bytes 786440 | tf_op jit(solution)/shard_map/ppermute | solution.py:288
  62.6 8.2 %collective-permute-start.17 = (bf16[128,1024]{1,0:T(8,128)(2,1)S(1)}, bf16[128,1024]{1,0:T(8,128)(2,1)S(1)}, u32[]{:S(2)}, u32[]{:S(2)}) collective-permute-start(bf16[128,1024]{1,0:T(8,128)(2,1)S(1)} %add_convert_fusion.2), channel_id=1, source_target_pairs={{0,4},{4,12},{12,8},{8,0},{1,5},{5,13},{13,9},{9,1},{2,6},{6,14},{... | collective-permute-start | bytes 786440 | tf_op jit(solution)/shard_map/ppermute | solution.py:298
  70.8 5.7 %collective-permute-start.18 = (bf16[4,768,512]{2,1,0:T(8,128)(2,1)S(1)}, bf16[4,768,512]{2,1,0:T(8,128)(2,1)S(1)}, u32[]{:S(2)}, u32[]{:S(2)}) collective-permute-start(bf16[4,768,512]{2,1,0:T(8,128)(2,1)S(1)} %weight_grads.2), channel_id=1, source_target_pairs={{0,1},{1,0},{2,3},{3,2},{4,5},{5,4},{6,7},{7,6},{8,9},{9,8},{10,11... | collective-permute-start | bytes 9437192 | tf_op jit(solution)/shard_map/ppermute | solution.py:333
  70.9 9.7 %collective-permute-start.19 = (bf16[128,1024]{1,0:T(8,128)(2,1)S(1)}, bf16[128,1024]{1,0:T(8,128)(2,1)S(1)}, u32[]{:S(2)}, u32[]{:S(2)}) collective-permute-start(bf16[128,1024]{1,0:T(8,128)(2,1)S(1)} %add_convert_fusion.1), channel_id=1, source_target_pairs={{0,4},{4,12},{12,8},{8,0},{1,5},{5,13},{13,9},{9,1},{2,6},{6,14},{... | collective-permute-start | bytes 786440 | tf_op jit(solution)/shard_map/ppermute | solution.py:298
  72.1 9.1 %collective-permute-start.20 = (bf16[128,1024]{1,0:T(8,128)(2,1)S(1)}, bf16[128,1024]{1,0:T(8,128)(2,1)S(1)}, u32[]{:S(2)}, u32[]{:S(2)}) collective-permute-start(bf16[128,1024]{1,0:T(8,128)(2,1)S(1)} %add_convert_fusion.3), channel_id=1, source_target_pairs={{0,2},{2,0},{1,3},{3,1},{4,6},{6,4},{5,7},{7,5},{8,10},{10,8},{9,1... | collective-permute-start | bytes 786440 | tf_op jit(solution)/shard_map/ppermute | solution.py:288

commit v20 on v11

--- a/solution.py
+++ b/solution.py
@@ -8,7 +8,7 @@
 from jax.sharding import PartitionSpec as P
 
 GROUPS_TOK = 4
-ROUTE_ROWS = 16
+ROUTE_ROWS = 8
 VMEM_LIMIT = 24 * 1024 * 1024
 
 
@@ -44,9 +44,9 @@
     gate = gate_fixed[...]
     out[tok_rows:, :] = jnp.zeros((ROUTE_ROWS, out.shape[1]), jnp.bfloat16)
     for i, field in enumerate((expert_ids[...], slots[...], gate >> 8, gate & 255)):
-        empty = jnp.zeros((ROUTE_ROWS - top_count, tok_rows), jnp.float32)
-        field = jnp.concatenate([field.astype(jnp.float32), empty], axis=0)
-        out[tok_rows:, i * tok_rows : (i + 1) * tok_rows] = field.astype(jnp.bfloat16)
+        out[tok_rows : tok_rows + top_count, i * tok_rows : (i + 1) * tok_rows] = field.astype(jnp.float32).astype(
+            jnp.bfloat16
+        )
     for copy in copies:
         copy.wait()
 
@@ -319,9 +319,10 @@
     blocks[last], chunks = tie(blocks[last], chunks)
     backs[last - 1] = across(chunks[last - 1][1])
     chunks[last] = chunk(blocks[last])
+    last_back = across(chunks[last][1])
     chunks, backs, near = tie(chunks, backs, near)
 
-    backs[last] = across(chunks[last][1])
+    backs[last] = last_back
     carried = homeward(group_sum(chunks[last - 1][0], backs[last - 1]), last)
     kept = [[chunks[k][i] for k in range(n_group)] for i in (-3, -2, -1)]
     to_send = weight_call(other_half, *kept)

time: 81 us -> 80.1 us (0.989)
  waiting for transfers between devices: 20.7 us -> 17.9 us
  starting transfers between devices: 34.2 us -> 36.2 us
    ppermute x1, waiting for transfers between devices: 2.86 us -> 1.36 us  [per_device(): got = lax.ppermute(to_send, 'dp', [(0, 1), (1, 0)])]
    ppermute x8, waiting for transfers between devices: 8.15 us -> 7.07 us  [spread(): lax.ppermute(column, 'ingroup', shift(s))]
    ppermute x6, waiting for transfers between devices: 4.04 us -> 2.98 us  [per_device(): lax.ppermute(v, 'group', along(1))]
    ppermute x2, waiting for transfers between devices: 3.36 us -> 4.4 us  [homeward(): return lax.ppermute(group_part, 'group', along(-k))]
    ppermute x2, starting transfers between devices: 5.41 us -> 6.45 us  [homeward(): return lax.ppermute(group_part, 'group', along(-k))]
where the time goes in v20:
time: 80.1 us; the launch traced here: 79.9 us
  starting transfers between devices  36.2 us (45%)
  Pallas kernels  23.9 us (30%)
  waiting for transfers between devices  17.9 us (22%)
  other arithmetic  1.13 us (1%)
    pallas_call x4, Pallas kernels, chunk_call(): pl.pallas_call(functools.partial(chunk_kernel, n_blocks, tok_rows, capaci...  14.7 us
    ppermute x6, starting transfers between devices, per_device(): lax.ppermute(v, 'group', along(1))  14.1 us
    ppermute x8, starting transfers between devices, spread(): lax.ppermute(column, 'ingroup', shift(s))  9.65 us
    ppermute x8, waiting for transfers between devices, spread(): lax.ppermute(column, 'ingroup', shift(s))  7.07 us
    ppermute x2, starting transfers between devices, homeward(): return lax.ppermute(group_part, 'group', along(-k))  6.45 us
    pallas_call x2, Pallas kernels, weight_call(): pl.pallas_call(functools.partial(kernel, n), in_specs=[smem] + [vmem] * l...  4.57 us
    ppermute x2, waiting for transfers between devices, homeward(): return lax.ppermute(group_part, 'group', along(-k))  4.4 us
    ppermute x3, starting transfers between devices, across(): lax.ppermute(others[(s - 1) * tok_rows:s * tok_rows], 'ingroup', shift(-s))  3.75 us
  transfers between devices with their start and end apart: 21, of which 14 were waited for; matrix products, arithmetic and copies ran while one was open for 0% of the time, Pallas kernels for 30%

profile of v20, /device:TPU:0, one launch (start us, length us, event | category | flops | bytes accessed | tf_op | source)
XLA Modules:
  0.0 79.9 jit_solution(9205091583930849116)
XLA Ops:
  0.6 3.1 %collective-permute-start = (bf16[128,1024]{1,0:T(8,128)(2,1)}, bf16[128,1024]{1,0:T(8,128)(2,1)S(1)}, u32[]{:S(2)}, u32[]{:S(2)}) collective-permute-start(bf16[128,1024]{1,0:T(8,128)(2,1)} %tokens), channel_id=1, source_target_pairs={{0,4},{4,12},{12,8},{8,0},{1,5},{5,13},{13,9},{9,1},{2,6},{6,14},{... | collective-permute-start | bytes 786440 | tf_op jit(solution)/shard_map/ppermute | solution.py:309
  3.7 1.5 %collective-permute-start.1 = (bf16[128,1024]{1,0:T(8,128)(2,1)}, bf16[128,1024]{1,0:T(8,128)(2,1)S(1)}, u32[]{:S(2)}, u32[]{:S(2)}) collective-permute-start(bf16[128,1024]{1,0:T(8,128)(2,1)} %tokens), channel_id=1, source_target_pairs={{0,2},{2,0},{1,3},{3,1},{4,6},{6,4},{5,7},{7,5},{8,10},{10,8},{9,1... | collective-permute-start | bytes 786440 | tf_op jit(solution)/shard_map/ppermute | solution.py:281
  5.2 1.8 %pack.1 = (bf16[128,1024]{1,0:T(8,128)(2,1)S(1)}, bf16[136,1024]{1,0:T(8,128)(2,1)S(1)}) custom-call(bf16[128,1024]{1,0:T(8,128)(2,1)} %tokens, bf16[128,1024]{1,0:T(8,128)(2,1)} %upstream.1, s32[8,128]{1,0:T(8,128)} %bitcast.5, s32[8,128]{1,0:T(8,128)} %bitcast.6, s32[8,128]{1,0:T(8,128)} %bitcast.7), custom_call_target="tpu_custom_call" | custom-call | tf_op jit(solution)/shard_map/pack/pallas_call | solution.py:58
  7.0 2.6 %collective-permute-start.4 = (bf16[136,1024]{1,0:T(8,128)(2,1)S(1)}, bf16[136,1024]{1,0:T(8,128)(2,1)S(1)}, u32[]{:S(2)}, u32[]{:S(2)}) collective-permute-start(bf16[136,1024]{1,0:T(8,128)(2,1)S(1)} %get-tuple-element.150.refs_2_), channel_id=1, source_target_pairs={{0,4},{4,12},{12,8},{8,0},{1,5},{5,13},{13,9},{9,1},{2,6},{6,14},{... | collective-permute-start | bytes 835592 | tf_op jit(solution)/shard_map/ppermute | solution.py:309
  9.6 0.5 collective-permute-start.5
  10.2 2.9 %load.1 = (bf16[4,1024,256]{2,1,0:T(8,128)(2,1)S(1)}, bf16[4,1024,256]{2,1,0:T(8,128)(2,1)S(1)}, bf16[4,256,1024]{2,1,0:T(8,128)(2,1)S(1)}) custom-call(bf16[4,1024,256]{2,1,0:T(8,128)(2,1)} %refs_0_.1, bf16[4,1024,256]{2,1,0:T(8,128)(2,1)} %refs_1_.1, bf16[4,256,1024]{2,1,0:T(8,128)(2,1)} %refs_2_.1), custom_call_target="tpu_custom_call" | custom-call | tf_op jit(solution)/shard_map/load/pallas_call | solution.py:98
  13.0 0.0 collective-permute-done.refs_0_
  13.1 0.0 collective-permute-done.1.refs_1_
  13.1 2.7 %collective-permute-start.2 = (bf16[128,1024]{1,0:T(8,128)(2,1)S(1)}, bf16[128,1024]{1,0:T(8,128)(2,1)S(1)}, u32[]{:S(2)}, u32[]{:S(2)}) collective-permute-start(bf16[128,1024]{1,0:T(8,128)(2,1)S(1)} %collective-permute-done.refs_0_), channel_id=1, source_target_pairs={{0,4},{4,12},{12,8},{8,0},{1,5},{5,13},{13,9},{9,1},{2,6},{6,14},{... | collective-permute-start | bytes 786440 | tf_op jit(solution)/shard_map/ppermute | solution.py:309
  15.7 1.5 %collective-permute-start.3 = (bf16[128,1024]{1,0:T(8,128)(2,1)S(1)}, bf16[128,1024]{1,0:T(8,128)(2,1)S(1)}, u32[]{:S(2)}, u32[]{:S(2)}) collective-permute-start(bf16[128,1024]{1,0:T(8,128)(2,1)S(1)} %collective-permute-done.refs_0_), channel_id=1, source_target_pairs={{0,2},{2,0},{1,3},{3,1},{4,6},{6,4},{5,7},{7,5},{8,10},{10,8},{9,1... | collective-permute-start | bytes 786440 | tf_op jit(solution)/shard_map/ppermute | solution.py:281
  17.2 0.8 %collective-permute-done.4.refs_2_ = bf16[136,1024]{1,0:T(8,128)(2,1)S(1)} collective-permute-done((bf16[136,1024]{1,0:T(8,128)(2,1)S(1)}, bf16[136,1024]{1,0:T(8,128)(2,1)S(1)}, u32[]{:S(2)}, u32[]{:S(2)}) %collective-permute-start.4) | collective-permute-done | bytes 278560 | tf_op jit(solution)/shard_map/ppermute | solution.py:309
  18.0 1.2 %collective-permute-done.5.refs_3_ = bf16[136,1024]{1,0:T(8,128)(2,1)S(1)} collective-permute-done((bf16[136,1024]{1,0:T(8,128)(2,1)S(1)}, bf16[136,1024]{1,0:T(8,128)(2,1)S(1)}, u32[]{:S(2)}, u32[]{:S(2)}) %collective-permute-start.5) | collective-permute-done | bytes 278560 | tf_op jit(solution)/shard_map/ppermute | solution.py:281
  19.2 2.5 %collective-permute-start.8 = (bf16[136,1024]{1,0:T(8,128)(2,1)S(1)}, bf16[136,1024]{1,0:T(8,128)(2,1)S(1)}, u32[]{:S(2)}, u32[]{:S(2)}) collective-permute-start(bf16[136,1024]{1,0:T(8,128)(2,1)S(1)} %collective-permute-done.4.refs_2_), channel_id=1, source_target_pairs={{0,4},{4,12},{12,8},{8,0},{1,5},{5,13},{13,9},{9,1},{2,6},{6,14},{... | collective-permute-start | bytes 835592 | tf_op jit(solution)/shard_map/ppermute | solution.py:309
  21.7 1.5 %collective-permute-start.9 = (bf16[136,1024]{1,0:T(8,128)(2,1)S(1)}, bf16[136,1024]{1,0:T(8,128)(2,1)S(1)}, u32[]{:S(2)}, u32[]{:S(2)}) collective-permute-start(bf16[136,1024]{1,0:T(8,128)(2,1)S(1)} %collective-permute-done.4.refs_2_), channel_id=1, source_target_pairs={{0,2},{2,0},{1,3},{3,1},{4,6},{6,4},{5,7},{7,5},{8,10},{10,8},{9,1... | collective-permute-start | bytes 835592 | tf_op jit(solution)/shard_map/ppermute | solution.py:281
  23.2 3.7 %chunk.4 = (bf16[128,1024]{1,0:T(8,128)(2,1)S(1)}, bf16[128,1024]{1,0:T(8,128)(2,1)S(1)}, bf16[4,96,1024]{2,1,0:T(8,128)(2,1)S(1)}, bf16[4,96,1024]{2,1,0:T(8,128)(2,1)S(1)}, bf16[4,96,768]{2,1,0:T(8,128)(2,1)S(1)}) custom-call(s32[1]{0:T(128)} %bitcast.first_ref, bf16[128,1024]{1,0:T(8,128)(2,1)S(1)} %get-tuple-element.147.refs_0_, ...), custom_call_target="tpu_custom_call" | custom-call | flops 1610612736 | bytes 8388608 | tf_op jit(solution)/shard_map/chunk/pallas_call | solution.py:171
  26.9 0.0 collective-permute-done.2.refs_0_
  26.9 0.0 collective-permute-done.3.refs_1_
  26.9 0.9 %collective-permute-start.6 = (bf16[128,1024]{1,0:T(8,128)(2,1)S(1)}, bf16[128,1024]{1,0:T(8,128)(2,1)S(1)}, u32[]{:S(2)}, u32[]{:S(2)}) collective-permute-start(bf16[128,1024]{1,0:T(8,128)(2,1)S(1)} %collective-permute-done.2.refs_0_), channel_id=1, source_target_pairs={{0,4},{4,12},{12,8},{8,0},{1,5},{5,13},{13,9},{9,1},{2,6},{6,14},{... | collective-permute-start | bytes 786440 | tf_op jit(solution)/shard_map/ppermute | solution.py:309
  27.8 1.0 %collective-permute-start.7 = (bf16[128,1024]{1,0:T(8,128)(2,1)S(1)}, bf16[128,1024]{1,0:T(8,128)(2,1)S(1)}, u32[]{:S(2)}, u32[]{:S(2)}) collective-permute-start(bf16[128,1024]{1,0:T(8,128)(2,1)S(1)} %collective-permute-done.2.refs_0_), channel_id=1, source_target_pairs={{0,2},{2,0},{1,3},{3,1},{4,6},{6,4},{5,7},{7,5},{8,10},{10,8},{9,1... | collective-permute-start | bytes 786440 | tf_op jit(solution)/shard_map/ppermute | solution.py:281
  28.8 0.9 %collective-permute-done.8.refs_2_ = bf16[136,1024]{1,0:T(8,128)(2,1)S(1)} collective-permute-done((bf16[136,1024]{1,0:T(8,128)(2,1)S(1)}, bf16[136,1024]{1,0:T(8,128)(2,1)S(1)}, u32[]{:S(2)}, u32[]{:S(2)}) %collective-permute-start.8) | collective-permute-done | bytes 278560 | tf_op jit(solution)/shard_map/ppermute | solution.py:309
  29.7 1.3 %collective-permute-done.9.refs_3_ = bf16[136,1024]{1,0:T(8,128)(2,1)S(1)} collective-permute-done((bf16[136,1024]{1,0:T(8,128)(2,1)S(1)}, bf16[136,1024]{1,0:T(8,128)(2,1)S(1)}, u32[]{:S(2)}, u32[]{:S(2)}) %collective-permute-start.9) | collective-permute-done | bytes 278560 | tf_op jit(solution)/shard_map/ppermute | solution.py:281
  31.0 2.3 %collective-permute-start.11 = (bf16[136,1024]{1,0:T(8,128)(2,1)S(1)}, bf16[136,1024]{1,0:T(8,128)(2,1)S(1)}, u32[]{:S(2)}, u32[]{:S(2)}) collective-permute-start(bf16[136,1024]{1,0:T(8,128)(2,1)S(1)} %collective-permute-done.8.refs_2_), channel_id=1, source_target_pairs={{0,4},{4,12},{12,8},{8,0},{1,5},{5,13},{13,9},{9,1},{2,6},{6,14},{... | collective-permute-start | bytes 835592 | tf_op jit(solution)/shard_map/ppermute | solution.py:309
  33.3 1.5 %collective-permute-start.12 = (bf16[136,1024]{1,0:T(8,128)(2,1)S(1)}, bf16[136,1024]{1,0:T(8,128)(2,1)S(1)}, u32[]{:S(2)}, u32[]{:S(2)}) collective-permute-start(bf16[136,1024]{1,0:T(8,128)(2,1)S(1)} %collective-permute-done.8.refs_2_), channel_id=1, source_target_pairs={{0,2},{2,0},{1,3},{3,1},{4,6},{6,4},{5,7},{7,5},{8,10},{10,8},{9,1... | collective-permute-start | bytes 835592 | tf_op jit(solution)/shard_map/ppermute | solution.py:281
  34.8 3.7 %chunk.5 = (bf16[256,1024]{1,0:T(8,128)(2,1)S(1)}, bf16[4,96,1024]{2,1,0:T(8,128)(2,1)S(1)}, bf16[4,96,1024]{2,1,0:T(8,128)(2,1)S(1)}, bf16[4,96,768]{2,1,0:T(8,128)(2,1)S(1)}) custom-call(s32[1]{0:T(128)} %bitcast.first_ref, bf16[128,1024]{1,0:T(8,128)(2,1)S(1)} %collective-permute-done.refs_0_, bf16[128,1024]{1,0:T(8,128)(2,1)S(1)} %collective-permute-done.3.refs_1_, ...), custom_call_target="tpu_custom_call" | custom-call | flops 1610612736 | bytes 8388608 | tf_op jit(solution)/shard_map/chunk/pallas_call | solution.py:171
  38.5 0.0 collective-permute-done.6.refs_0_
  38.5 0.0 collective-permute-done.7.refs_1_
  38.5 0.6 collective-permute-start.10
  39.1 1.3 %collective-permute-done.11.refs_2_ = bf16[136,1024]{1,0:T(8,128)(2,1)S(1)} collective-permute-done((bf16[136,1024]{1,0:T(8,128)(2,1)S(1)}, bf16[136,1024]{1,0:T(8,128)(2,1)S(1)}, u32[]{:S(2)}, u32[]{:S(2)}) %collective-permute-start.11) | collective-permute-done | bytes 278560 | tf_op jit(solution)/shard_map/ppermute | solution.py:309
  40.4 2.5 %collective-permute-done.12.refs_3_ = bf16[136,1024]{1,0:T(8,128)(2,1)S(1)} collective-permute-done((bf16[136,1024]{1,0:T(8,128)(2,1)S(1)}, bf16[136,1024]{1,0:T(8,128)(2,1)S(1)}, u32[]{:S(2)}, u32[]{:S(2)}) %collective-permute-start.12) | collective-permute-done | bytes 278560 | tf_op jit(solution)/shard_map/ppermute | solution.py:281
  42.8 1.5 %collective-permute-start.13 = (bf16[136,1024]{1,0:T(8,128)(2,1)S(1)}, bf16[136,1024]{1,0:T(8,128)(2,1)S(1)}, u32[]{:S(2)}, u32[]{:S(2)}) collective-permute-start(bf16[136,1024]{1,0:T(8,128)(2,1)S(1)} %collective-permute-done.11.refs_2_), channel_id=1, source_target_pairs={{0,2},{2,0},{1,3},{3,1},{4,6},{6,4},{5,7},{7,5},{8,10},{10,8},{9,1... | collective-permute-start | bytes 835592 | tf_op jit(solution)/shard_map/ppermute | solution.py:281
  44.4 3.7 %chunk.6 = (bf16[128,1024]{1,0:T(8,128)(2,1)S(1)}, bf16[128,1024]{1,0:T(8,128)(2,1)S(1)}, bf16[4,96,1024]{2,1,0:T(8,128)(2,1)S(1)}, bf16[4,96,1024]{2,1,0:T(8,128)(2,1)S(1)}, bf16[4,96,768]{2,1,0:T(8,128)(2,1)S(1)}) custom-call(s32[1]{0:T(128)} %bitcast.first_ref, bf16[128,1024]{1,0:T(8,128)(2,1)S(1)} %collective-permute-done.2.refs_0_, ...), custom_call_target="tpu_custom_call" | custom-call | flops 1610612736 | bytes 8388608 | tf_op jit(solution)/shard_map/chunk/pallas_call | solution.py:171
  48.1 0.4 collective-permute-done.10.refs_1_
  48.5 2.2 %collective-permute-start.15 = (bf16[256,1024]{1,0:T(8,128)(2,1)S(1)}, bf16[256,1024]{1,0:T(8,128)(2,1)S(1)}, u32[]{:S(2)}, u32[]{:S(2)}) collective-permute-start(bf16[256,1024]{1,0:T(8,128)(2,1)S(1)} %get-tuple-element.211), channel_id=1, source_target_pairs={{0,8},{4,0},{12,4},{8,12},{1,9},{5,1},{13,5},{9,13},{2,10},{6,2},{... | collective-permute-start | bytes 1572872 | tf_op jit(solution)/shard_map/ppermute | solution.py:318
  50.7 1.7 %collective-permute-done.13.refs_3_ = bf16[136,1024]{1,0:T(8,128)(2,1)S(1)} collective-permute-done((bf16[136,1024]{1,0:T(8,128)(2,1)S(1)}, bf16[136,1024]{1,0:T(8,128)(2,1)S(1)}, u32[]{:S(2)}, u32[]{:S(2)}) %collective-permute-start.13) | collective-permute-done | bytes 278560 | tf_op jit(solution)/shard_map/ppermute | solution.py:281
  52.4 1.5 %collective-permute-start.14 = (bf16[128,1024]{1,0:T(8,128)(2,1)S(1)}, bf16[128,1024]{1,0:T(8,128)(2,1)S(1)}, u32[]{:S(2)}, u32[]{:S(2)}) collective-permute-start(bf16[128,1024]{1,0:T(8,128)(2,1)S(1)} %get-tuple-element.229), channel_id=1, source_target_pairs={{0,2},{2,0},{1,3},{3,1},{4,6},{6,4},{5,7},{7,5},{8,10},{10,8},{9,1... | collective-permute-start | bytes 786440 | tf_op jit(solution)/shard_map/ppermute | solution.py:288
  53.9 3.7 %chunk.7 = (bf16[128,1024]{1,0:T(8,128)(2,1)S(1)}, bf16[128,1024]{1,0:T(8,128)(2,1)S(1)}, bf16[4,96,1024]{2,1,0:T(8,128)(2,1)S(1)}, bf16[4,96,1024]{2,1,0:T(8,128)(2,1)S(1)}, bf16[4,96,768]{2,1,0:T(8,128)(2,1)S(1)}) custom-call(s32[1]{0:T(128)} %bitcast.first_ref, bf16[128,1024]{1,0:T(8,128)(2,1)S(1)} %collective-permute-done.6.refs_0_, ...), custom_call_target="tpu_custom_call" | custom-call | flops 1610612736 | bytes 8388608 | tf_op jit(solution)/shard_map/chunk/pallas_call | solution.py:171
  57.6 0.6 collective-permute-start.16
  58.2 1.3 %collective-permute-done.14 = bf16[128,1024]{1,0:T(8,128)(2,1)S(1)} collective-permute-done((bf16[128,1024]{1,0:T(8,128)(2,1)S(1)}, bf16[128,1024]{1,0:T(8,128)(2,1)S(1)}, u32[]{:S(2)}, u32[]{:S(2)}) %collective-permute-start.14) | collective-permute-done | bytes 262176 | tf_op jit(solution)/shard_map/ppermute | solution.py:288
  59.5 0.3 collective-permute-done.15
  59.8 0.1 add_convert_fusion.3
  59.8 4.0 %collective-permute-start.17 = (bf16[128,1024]{1,0:T(8,128)(2,1)S(1)}, bf16[128,1024]{1,0:T(8,128)(2,1)S(1)}, u32[]{:S(2)}, u32[]{:S(2)}) collective-permute-start(bf16[128,1024]{1,0:T(8,128)(2,1)S(1)} %add_convert_fusion.3), channel_id=1, source_target_pairs={{0,4},{4,12},{12,8},{8,0},{1,5},{5,13},{13,9},{9,1},{2,6},{6,14},{... | collective-permute-start | bytes 786440 | tf_op jit(solution)/shard_map/ppermute | solution.py:298
  63.9 1.9 %weight_grads.2 = bf16[4,768,512]{2,1,0:T(8,128)(2,1)S(1)} custom-call(s32[1]{0:T(128)S(6)} %sub.3.side_ref, bf16[4,96,1024]{2,1,0:T(8,128)(2,1)S(1)} %get-tuple-element.248.refs_0_, bf16[4,96,1024]{2,1,0:T(8,128)(2,1)S(1)} %get-tuple-element.249.refs_1_, bf16[4,96,1024]{2,1,0:T(8,128)(2,1)S(1)} %get-tuple-element.250.refs_2_, ...), custom_call_target="tpu_custom_call" | custom-call | flops 1207959552 | bytes 8650752 | tf_op jit(solution)/shard_map/weight_grads/pallas_call | solution.py:244
  65.7 0.0 collective-permute-done.16
  65.8 2.0 %collective-permute-done.17 = bf16[128,1024]{1,0:T(8,128)(2,1)S(1)} collective-permute-done((bf16[128,1024]{1,0:T(8,128)(2,1)S(1)}, bf16[128,1024]{1,0:T(8,128)(2,1)S(1)}, u32[]{:S(2)}, u32[]{:S(2)}) %collective-permute-start.17) | collective-permute-done | bytes 262176 | tf_op jit(solution)/shard_map/ppermute | solution.py:298
  67.8 0.0 collective-permute-start.18
  67.8 0.1 add_convert_fusion.1
  67.8 1.7 %collective-permute-start.20 = (bf16[128,1024]{1,0:T(8,128)(2,1)S(1)}, bf16[128,1024]{1,0:T(8,128)(2,1)S(1)}, u32[]{:S(2)}, u32[]{:S(2)}) collective-permute-start(bf16[128,1024]{1,0:T(8,128)(2,1)S(1)} %add_convert_fusion.1), channel_id=1, source_target_pairs={{0,2},{2,0},{1,3},{3,1},{4,6},{6,4},{5,7},{7,5},{8,10},{10,8},{9,1... | collective-permute-start | bytes 786440 | tf_op jit(solution)/shard_map/ppermute | solution.py:288
  69.5 0.1 add_convert_fusion.2
  69.6 2.4 %collective-permute-start.19 = (bf16[128,1024]{1,0:T(8,128)(2,1)S(1)}, bf16[128,1024]{1,0:T(8,128)(2,1)S(1)}, u32[]{:S(2)}, u32[]{:S(2)}) collective-permute-start(bf16[128,1024]{1,0:T(8,128)(2,1)S(1)} %add_convert_fusion.2), channel_id=1, source_target_pairs={{0,4},{4,12},{12,8},{8,0},{1,5},{5,13},{13,9},{9,1},{2,6},{6,14},{... | collective-permute-start | bytes 786440 | tf_op jit(solution)/shard_map/ppermute | solution.py:298
  72.0 1.4 %collective-permute-done.18.refs_12_ = bf16[4,768,512]{2,1,0:T(8,128)(2,1)S(1)} collective-permute-done((bf16[4,768,512]{2,1,0:T(8,128)(2,1)S(1)}, bf16[4,768,512]{2,1,0:T(8,128)(2,1)S(1)}, u32[]{:S(2)}, u32[]{:S(2)}) %collective-permute-start.18) | collective-permute-done | bytes 3145760 | tf_op jit(solution)/shard_map/ppermute | solution.py:331
  73.4 2.7 %weight_grads.3 = (bf16[4,512,256]{2,1,0:T(8,128)(2,1)}, bf16[4,512,256]{2,1,0:T(8,128)(2,1)}, bf16[4,256,512]{2,1,0:T(8,128)(2,1)}) custom-call(s32[1]{0:T(128)} %bitcast.1.side_ref, bf16[4,96,1024]{2,1,0:T(8,128)(2,1)S(1)} %get-tuple-element.248.refs_0_, bf16[4,96,1024]{2,1,0:T(8,128)(2,1)S(1)} %get-tuple-element.249.refs_1_, ...), custom_call_target="tpu_custom_call" | custom-call | flops 1207959552 | bytes 8650752 | tf_op jit(solution)/shard_map/weight_grads/pallas_call | solution.py:244
  76.1 0.5 collective-permute-done.20
  76.6 2.4 %collective-permute-done.19 = bf16[128,1024]{1,0:T(8,128)(2,1)S(1)} collective-permute-done((bf16[128,1024]{1,0:T(8,128)(2,1)S(1)}, bf16[128,1024]{1,0:T(8,128)(2,1)S(1)}, u32[]{:S(2)}, u32[]{:S(2)}) %collective-permute-start.19) | collective-permute-done | bytes 262176 | tf_op jit(solution)/shard_map/ppermute | solution.py:298
  79.0 0.9 %add_convert_fusion = bf16[128,1024]{1,0:T(8,128)(2,1)} fusion(bf16[128,1024]{1,0:T(8,128)(2,1)S(1)} %collective-permute-done.19, bf16[128,1024]{1,0:T(8,128)(2,1)S(1)} %collective-permute-done.20, bf16[128,1024]{1,0:T(8,128)(2,1)S(1)} %get-tuple-element.245, bf16[256,1024]{1,0:T(8,128)(2,1)S(1)} %collective-permute-done.15), kind=kLoop, calls=%fused_computation | loop fusion | flops 1048576 | bytes 1310720 | tf_op jit(solution)/shard_map/convert_element_type | solution.py:341
Async XLA Ops:
  0.6 12.4 %collective-permute-start = (bf16[128,1024]{1,0:T(8,128)(2,1)}, bf16[128,1024]{1,0:T(8,128)(2,1)S(1)}, u32[]{:S(2)}, u32[]{:S(2)}) collective-permute-start(bf16[128,1024]{1,0:T(8,128)(2,1)} %tokens), channel_id=1, source_target_pairs={{0,4},{4,12},{12,8},{8,0},{1,5},{5,13},{13,9},{9,1},{2,6},{6,14},{... | collective-permute-start | bytes 786440 | tf_op jit(solution)/shard_map/ppermute | solution.py:309
  3.7 9.3 %collective-permute-start.1 = (bf16[128,1024]{1,0:T(8,128)(2,1)}, bf16[128,1024]{1,0:T(8,128)(2,1)S(1)}, u32[]{:S(2)}, u32[]{:S(2)}) collective-permute-start(bf16[128,1024]{1,0:T(8,128)(2,1)} %tokens), channel_id=1, source_target_pairs={{0,2},{2,0},{1,3},{3,1},{4,6},{6,4},{5,7},{7,5},{8,10},{10,8},{9,1... | collective-permute-start | bytes 786440 | tf_op jit(solution)/shard_map/ppermute | solution.py:281
  7.0 11.1 %collective-permute-start.4 = (bf16[136,1024]{1,0:T(8,128)(2,1)S(1)}, bf16[136,1024]{1,0:T(8,128)(2,1)S(1)}, u32[]{:S(2)}, u32[]{:S(2)}) collective-permute-start(bf16[136,1024]{1,0:T(8,128)(2,1)S(1)} %get-tuple-element.150.refs_2_), channel_id=1, source_target_pairs={{0,4},{4,12},{12,8},{8,0},{1,5},{5,13},{13,9},{9,1},{2,6},{6,14},{... | collective-permute-start | bytes 835592 | tf_op jit(solution)/shard_map/ppermute | solution.py:309
  9.6 9.6 %collective-permute-start.5 = (bf16[136,1024]{1,0:T(8,128)(2,1)S(1)}, bf16[136,1024]{1,0:T(8,128)(2,1)S(1)}, u32[]{:S(2)}, u32[]{:S(2)}) collective-permute-start(bf16[136,1024]{1,0:T(8,128)(2,1)S(1)} %get-tuple-element.150.refs_2_), channel_id=1, source_target_pairs={{0,2},{2,0},{1,3},{3,1},{4,6},{6,4},{5,7},{7,5},{8,10},{10,8},{9,1... | collective-permute-start | bytes 835592 | tf_op jit(solution)/shard_map/ppermute | solution.py:281
  13.1 13.8 %collective-permute-start.2 = (bf16[128,1024]{1,0:T(8,128)(2,1)S(1)}, bf16[128,1024]{1,0:T(8,128)(2,1)S(1)}, u32[]{:S(2)}, u32[]{:S(2)}) collective-permute-start(bf16[128,1024]{1,0:T(8,128)(2,1)S(1)} %collective-permute-done.refs_0_), channel_id=1, source_target_pairs={{0,4},{4,12},{12,8},{8,0},{1,5},{5,13},{13,9},{9,1},{2,6},{6,14},{... | collective-permute-start | bytes 786440 | tf_op jit(solution)/shard_map/ppermute | solution.py:309
  15.7 11.1 %collective-permute-start.3 = (bf16[128,1024]{1,0:T(8,128)(2,1)S(1)}, bf16[128,1024]{1,0:T(8,128)(2,1)S(1)}, u32[]{:S(2)}, u32[]{:S(2)}) collective-permute-start(bf16[128,1024]{1,0:T(8,128)(2,1)S(1)} %collective-permute-done.refs_0_), channel_id=1, source_target_pairs={{0,2},{2,0},{1,3},{3,1},{4,6},{6,4},{5,7},{7,5},{8,10},{10,8},{9,1... | collective-permute-start | bytes 786440 | tf_op jit(solution)/shard_map/ppermute | solution.py:281
  19.2 10.5 %collective-permute-start.8 = (bf16[136,1024]{1,0:T(8,128)(2,1)S(1)}, bf16[136,1024]{1,0:T(8,128)(2,1)S(1)}, u32[]{:S(2)}, u32[]{:S(2)}) collective-permute-start(bf16[136,1024]{1,0:T(8,128)(2,1)S(1)} %collective-permute-done.4.refs_2_), channel_id=1, source_target_pairs={{0,4},{4,12},{12,8},{8,0},{1,5},{5,13},{13,9},{9,1},{2,6},{6,14},{... | collective-permute-start | bytes 835592 | tf_op jit(solution)/shard_map/ppermute | solution.py:309
  21.7 9.3 %collective-permute-start.9 = (bf16[136,1024]{1,0:T(8,128)(2,1)S(1)}, bf16[136,1024]{1,0:T(8,128)(2,1)S(1)}, u32[]{:S(2)}, u32[]{:S(2)}) collective-permute-start(bf16[136,1024]{1,0:T(8,128)(2,1)S(1)} %collective-permute-done.4.refs_2_), channel_id=1, source_target_pairs={{0,2},{2,0},{1,3},{3,1},{4,6},{6,4},{5,7},{7,5},{8,10},{10,8},{9,1... | collective-permute-start | bytes 835592 | tf_op jit(solution)/shard_map/ppermute | solution.py:281
  26.9 11.6 %collective-permute-start.6 = (bf16[128,1024]{1,0:T(8,128)(2,1)S(1)}, bf16[128,1024]{1,0:T(8,128)(2,1)S(1)}, u32[]{:S(2)}, u32[]{:S(2)}) collective-permute-start(bf16[128,1024]{1,0:T(8,128)(2,1)S(1)} %collective-permute-done.2.refs_0_), channel_id=1, source_target_pairs={{0,4},{4,12},{12,8},{8,0},{1,5},{5,13},{13,9},{9,1},{2,6},{6,14},{... | collective-permute-start | bytes 786440 | tf_op jit(solution)/shard_map/ppermute | solution.py:309
  27.8 10.7 %collective-permute-start.7 = (bf16[128,1024]{1,0:T(8,128)(2,1)S(1)}, bf16[128,1024]{1,0:T(8,128)(2,1)S(1)}, u32[]{:S(2)}, u32[]{:S(2)}) collective-permute-start(bf16[128,1024]{1,0:T(8,128)(2,1)S(1)} %collective-permute-done.2.refs_0_), channel_id=1, source_target_pairs={{0,2},{2,0},{1,3},{3,1},{4,6},{6,4},{5,7},{7,5},{8,10},{10,8},{9,1... | collective-permute-start | bytes 786440 | tf_op jit(solution)/shard_map/ppermute | solution.py:281
  31.0 9.3 %collective-permute-start.11 = (bf16[136,1024]{1,0:T(8,128)(2,1)S(1)}, bf16[136,1024]{1,0:T(8,128)(2,1)S(1)}, u32[]{:S(2)}, u32[]{:S(2)}) collective-permute-start(bf16[136,1024]{1,0:T(8,128)(2,1)S(1)} %collective-permute-done.8.refs_2_), channel_id=1, source_target_pairs={{0,4},{4,12},{12,8},{8,0},{1,5},{5,13},{13,9},{9,1},{2,6},{6,14},{... | collective-permute-start | bytes 835592 | tf_op jit(solution)/shard_map/ppermute | solution.py:309
  33.3 9.5 %collective-permute-start.12 = (bf16[136,1024]{1,0:T(8,128)(2,1)S(1)}, bf16[136,1024]{1,0:T(8,128)(2,1)S(1)}, u32[]{:S(2)}, u32[]{:S(2)}) collective-permute-start(bf16[136,1024]{1,0:T(8,128)(2,1)S(1)} %collective-permute-done.8.refs_2_), channel_id=1, source_target_pairs={{0,2},{2,0},{1,3},{3,1},{4,6},{6,4},{5,7},{7,5},{8,10},{10,8},{9,1... | collective-permute-start | bytes 835592 | tf_op jit(solution)/shard_map/ppermute | solution.py:281
  38.5 10.0 %collective-permute-start.10 = (bf16[128,1024]{1,0:T(8,128)(2,1)S(1)}, bf16[128,1024]{1,0:T(8,128)(2,1)S(1)}, u32[]{:S(2)}, u32[]{:S(2)}) collective-permute-start(bf16[128,1024]{1,0:T(8,128)(2,1)S(1)} %collective-permute-done.6.refs_0_), channel_id=1, source_target_pairs={{0,2},{2,0},{1,3},{3,1},{4,6},{6,4},{5,7},{7,5},{8,10},{10,8},{9,1... | collective-permute-start | bytes 786440 | tf_op jit(solution)/shard_map/ppermute | solution.py:281
  42.8 9.6 %collective-permute-start.13 = (bf16[136,1024]{1,0:T(8,128)(2,1)S(1)}, bf16[136,1024]{1,0:T(8,128)(2,1)S(1)}, u32[]{:S(2)}, u32[]{:S(2)}) collective-permute-start(bf16[136,1024]{1,0:T(8,128)(2,1)S(1)} %collective-permute-done.11.refs_2_), channel_id=1, source_target_pairs={{0,2},{2,0},{1,3},{3,1},{4,6},{6,4},{5,7},{7,5},{8,10},{10,8},{9,1... | collective-permute-start | bytes 835592 | tf_op jit(solution)/shard_map/ppermute | solution.py:281
  48.5 11.3 %collective-permute-start.15 = (bf16[256,1024]{1,0:T(8,128)(2,1)S(1)}, bf16[256,1024]{1,0:T(8,128)(2,1)S(1)}, u32[]{:S(2)}, u32[]{:S(2)}) collective-permute-start(bf16[256,1024]{1,0:T(8,128)(2,1)S(1)} %get-tuple-element.211), channel_id=1, source_target_pairs={{0,8},{4,0},{12,4},{8,12},{1,9},{5,1},{13,5},{9,13},{2,10},{6,2},{... | collective-permute-start | bytes 1572872 | tf_op jit(solution)/shard_map/ppermute | solution.py:318
  52.4 7.1 %collective-permute-start.14 = (bf16[128,1024]{1,0:T(8,128)(2,1)S(1)}, bf16[128,1024]{1,0:T(8,128)(2,1)S(1)}, u32[]{:S(2)}, u32[]{:S(2)}) collective-permute-start(bf16[128,1024]{1,0:T(8,128)(2,1)S(1)} %get-tuple-element.229), channel_id=1, source_target_pairs={{0,2},{2,0},{1,3},{3,1},{4,6},{6,4},{5,7},{7,5},{8,10},{10,8},{9,1... | collective-permute-start | bytes 786440 | tf_op jit(solution)/shard_map/ppermute | solution.py:288
  57.6 8.1 %collective-permute-start.16 = (bf16[128,1024]{1,0:T(8,128)(2,1)S(1)}, bf16[128,1024]{1,0:T(8,128)(2,1)S(1)}, u32[]{:S(2)}, u32[]{:S(2)}) collective-permute-start(bf16[128,1024]{1,0:T(8,128)(2,1)S(1)} %get-tuple-element.241), channel_id=1, source_target_pairs={{0,2},{2,0},{1,3},{3,1},{4,6},{6,4},{5,7},{7,5},{8,10},{10,8},{9,1... | collective-permute-start | bytes 786440 | tf_op jit(solution)/shard_map/ppermute | solution.py:288
  59.8 7.9 %collective-permute-start.17 = (bf16[128,1024]{1,0:T(8,128)(2,1)S(1)}, bf16[128,1024]{1,0:T(8,128)(2,1)S(1)}, u32[]{:S(2)}, u32[]{:S(2)}) collective-permute-start(bf16[128,1024]{1,0:T(8,128)(2,1)S(1)} %add_convert_fusion.3), channel_id=1, source_target_pairs={{0,4},{4,12},{12,8},{8,0},{1,5},{5,13},{13,9},{9,1},{2,6},{6,14},{... | collective-permute-start | bytes 786440 | tf_op jit(solution)/shard_map/ppermute | solution.py:298
  67.8 5.7 %collective-permute-start.18 = (bf16[4,768,512]{2,1,0:T(8,128)(2,1)S(1)}, bf16[4,768,512]{2,1,0:T(8,128)(2,1)S(1)}, u32[]{:S(2)}, u32[]{:S(2)}) collective-permute-start(bf16[4,768,512]{2,1,0:T(8,128)(2,1)S(1)} %weight_grads.2), channel_id=1, source_target_pairs={{0,1},{1,0},{2,3},{3,2},{4,5},{5,4},{6,7},{7,6},{8,9},{9,8},{10,11... | collective-permute-start | bytes 9437192 | tf_op jit(solution)/shard_map/ppermute | solution.py:331
  67.8 8.8 %collective-permute-start.20 = (bf16[128,1024]{1,0:T(8,128)(2,1)S(1)}, bf16[128,1024]{1,0:T(8,128)(2,1)S(1)}, u32[]{:S(2)}, u32[]{:S(2)}) collective-permute-start(bf16[128,1024]{1,0:T(8,128)(2,1)S(1)} %add_convert_fusion.1), channel_id=1, source_target_pairs={{0,2},{2,0},{1,3},{3,1},{4,6},{6,4},{5,7},{7,5},{8,10},{10,8},{9,1... | collective-permute-start | bytes 786440 | tf_op jit(solution)/shard_map/ppermute | solution.py:288
  69.6 9.4 %collective-permute-start.19 = (bf16[128,1024]{1,0:T(8,128)(2,1)S(1)}, bf16[128,1024]{1,0:T(8,128)(2,1)S(1)}, u32[]{:S(2)}, u32[]{:S(2)}) collective-permute-start(bf16[128,1024]{1,0:T(8,128)(2,1)S(1)} %add_convert_fusion.2), channel_id=1, source_target_pairs={{0,4},{4,12},{12,8},{8,0},{1,5},{5,13},{13,9},{9,1},{2,6},{6,14},{... | collective-permute-start | bytes 786440 | tf_op jit(solution)/shard_map/ppermute | solution.py:298

commit v21 on v20

--- a/solution.py
+++ b/solution.py
@@ -332,7 +332,8 @@
     sent[last] = homeward(group_sum(chunks[last][0], [*backs[last], carried]), last)
     backs[0] = across((wide(chunks[0][1]) + wide(near[tok_rows:])).astype(jnp.bfloat16))
     grads = weight_call(half, *kept, got)
-    grads, sent, backs[0] = tie(grads, sent, backs[0])
+    grads, sent = tie(grads, sent)
+    grads, backs[0] = tie(grads, backs[0])
     total = wide(chunks[0][0]) + wide(near[:tok_rows])
     for back in backs[0]:
         total = total + wide(back)

time: 80.1 us -> 80.1 us (level)
    ppermute x2, waiting for transfers between devices: 4.4 us -> 3.44 us  [homeward(): return lax.ppermute(group_part, 'group', along(-k))]
    ppermute x3, waiting for transfers between devices: 1.8 us -> 2.75 us  [across(): lax.ppermute(others[(s - 1) * tok_rows:s * tok_rows], 'ingroup', shift(-s))]
where the time goes in v21:
time: 80.1 us; the launch traced here: 79.9 us
  starting transfers between devices  36.2 us (45%)
  Pallas kernels  23.9 us (30%)
  waiting for transfers between devices  17.9 us (22%)
  other arithmetic  1.13 us (1%)
    pallas_call x4, Pallas kernels, chunk_call(): pl.pallas_call(functools.partial(chunk_kernel, n_blocks, tok_rows, capaci...  14.7 us
    ppermute x6, starting transfers between devices, per_device(): lax.ppermute(v, 'group', along(1))  14.1 us
    ppermute x8, starting transfers between devices, spread(): lax.ppermute(column, 'ingroup', shift(s))  9.65 us
    ppermute x8, waiting for transfers between devices, spread(): lax.ppermute(column, 'ingroup', shift(s))  7.07 us
    ppermute x2, starting transfers between devices, homeward(): return lax.ppermute(group_part, 'group', along(-k))  6.55 us
    pallas_call x2, Pallas kernels, weight_call(): pl.pallas_call(functools.partial(kernel, n), in_specs=[smem] + [vmem] * l...  4.57 us
    ppermute x3, starting transfers between devices, across(): lax.ppermute(others[(s - 1) * tok_rows:s * tok_rows], 'ingroup', shift(-s))  3.65 us
    ppermute x2, waiting for transfers between devices, homeward(): return lax.ppermute(group_part, 'group', along(-k))  3.44 us
  transfers between devices with their start and end apart: 21, of which 14 were waited for; matrix products, arithmetic and copies ran while one was open for 0% of the time, Pallas kernels for 30%

profile of v21, /device:TPU:0, one launch (start us, length us, event | category | flops | bytes accessed | tf_op | source)
XLA Modules:
  0.0 79.9 jit_solution(3881614528499268520)
XLA Ops:
  0.6 3.1 %collective-permute-start = (bf16[128,1024]{1,0:T(8,128)(2,1)}, bf16[128,1024]{1,0:T(8,128)(2,1)S(1)}, u32[]{:S(2)}, u32[]{:S(2)}) collective-permute-start(bf16[128,1024]{1,0:T(8,128)(2,1)} %tokens), channel_id=1, source_target_pairs={{0,4},{4,12},{12,8},{8,0},{1,5},{5,13},{13,9},{9,1},{2,6},{6,14},{... | collective-permute-start | bytes 786440 | tf_op jit(solution)/shard_map/ppermute | solution.py:309
  3.7 1.5 %collective-permute-start.1 = (bf16[128,1024]{1,0:T(8,128)(2,1)}, bf16[128,1024]{1,0:T(8,128)(2,1)S(1)}, u32[]{:S(2)}, u32[]{:S(2)}) collective-permute-start(bf16[128,1024]{1,0:T(8,128)(2,1)} %tokens), channel_id=1, source_target_pairs={{0,2},{2,0},{1,3},{3,1},{4,6},{6,4},{5,7},{7,5},{8,10},{10,8},{9,1... | collective-permute-start | bytes 786440 | tf_op jit(solution)/shard_map/ppermute | solution.py:281
  5.2 1.8 %pack.1 = (bf16[128,1024]{1,0:T(8,128)(2,1)S(1)}, bf16[136,1024]{1,0:T(8,128)(2,1)S(1)}) custom-call(bf16[128,1024]{1,0:T(8,128)(2,1)} %tokens, bf16[128,1024]{1,0:T(8,128)(2,1)} %upstream.1, s32[8,128]{1,0:T(8,128)} %bitcast.5, s32[8,128]{1,0:T(8,128)} %bitcast.6, s32[8,128]{1,0:T(8,128)} %bitcast.7), custom_call_target="tpu_custom_call" | custom-call | tf_op jit(solution)/shard_map/pack/pallas_call | solution.py:58
  7.0 2.6 %collective-permute-start.4 = (bf16[136,1024]{1,0:T(8,128)(2,1)S(1)}, bf16[136,1024]{1,0:T(8,128)(2,1)S(1)}, u32[]{:S(2)}, u32[]{:S(2)}) collective-permute-start(bf16[136,1024]{1,0:T(8,128)(2,1)S(1)} %get-tuple-element.153.refs_2_), channel_id=1, source_target_pairs={{0,4},{4,12},{12,8},{8,0},{1,5},{5,13},{13,9},{9,1},{2,6},{6,14},{... | collective-permute-start | bytes 835592 | tf_op jit(solution)/shard_map/ppermute | solution.py:309
  9.6 0.5 collective-permute-start.5
  10.2 2.9 %load.1 = (bf16[4,1024,256]{2,1,0:T(8,128)(2,1)S(1)}, bf16[4,1024,256]{2,1,0:T(8,128)(2,1)S(1)}, bf16[4,256,1024]{2,1,0:T(8,128)(2,1)S(1)}) custom-call(bf16[4,1024,256]{2,1,0:T(8,128)(2,1)} %refs_0_.1, bf16[4,1024,256]{2,1,0:T(8,128)(2,1)} %refs_1_.1, bf16[4,256,1024]{2,1,0:T(8,128)(2,1)} %refs_2_.1), custom_call_target="tpu_custom_call" | custom-call | tf_op jit(solution)/shard_map/load/pallas_call | solution.py:98
  13.0 0.0 collective-permute-done.refs_0_
  13.1 0.0 collective-permute-done.1.refs_1_
  13.1 2.7 %collective-permute-start.2 = (bf16[128,1024]{1,0:T(8,128)(2,1)S(1)}, bf16[128,1024]{1,0:T(8,128)(2,1)S(1)}, u32[]{:S(2)}, u32[]{:S(2)}) collective-permute-start(bf16[128,1024]{1,0:T(8,128)(2,1)S(1)} %collective-permute-done.refs_0_), channel_id=1, source_target_pairs={{0,4},{4,12},{12,8},{8,0},{1,5},{5,13},{13,9},{9,1},{2,6},{6,14},{... | collective-permute-start | bytes 786440 | tf_op jit(solution)/shard_map/ppermute | solution.py:309
  15.7 1.5 %collective-permute-start.3 = (bf16[128,1024]{1,0:T(8,128)(2,1)S(1)}, bf16[128,1024]{1,0:T(8,128)(2,1)S(1)}, u32[]{:S(2)}, u32[]{:S(2)}) collective-permute-start(bf16[128,1024]{1,0:T(8,128)(2,1)S(1)} %collective-permute-done.refs_0_), channel_id=1, source_target_pairs={{0,2},{2,0},{1,3},{3,1},{4,6},{6,4},{5,7},{7,5},{8,10},{10,8},{9,1... | collective-permute-start | bytes 786440 | tf_op jit(solution)/shard_map/ppermute | solution.py:281
  17.2 0.8 %collective-permute-done.4.refs_2_ = bf16[136,1024]{1,0:T(8,128)(2,1)S(1)} collective-permute-done((bf16[136,1024]{1,0:T(8,128)(2,1)S(1)}, bf16[136,1024]{1,0:T(8,128)(2,1)S(1)}, u32[]{:S(2)}, u32[]{:S(2)}) %collective-permute-start.4) | collective-permute-done | bytes 278560 | tf_op jit(solution)/shard_map/ppermute | solution.py:309
  18.0 1.2 %collective-permute-done.5.refs_3_ = bf16[136,1024]{1,0:T(8,128)(2,1)S(1)} collective-permute-done((bf16[136,1024]{1,0:T(8,128)(2,1)S(1)}, bf16[136,1024]{1,0:T(8,128)(2,1)S(1)}, u32[]{:S(2)}, u32[]{:S(2)}) %collective-permute-start.5) | collective-permute-done | bytes 278560 | tf_op jit(solution)/shard_map/ppermute | solution.py:281
  19.2 2.5 %collective-permute-start.8 = (bf16[136,1024]{1,0:T(8,128)(2,1)S(1)}, bf16[136,1024]{1,0:T(8,128)(2,1)S(1)}, u32[]{:S(2)}, u32[]{:S(2)}) collective-permute-start(bf16[136,1024]{1,0:T(8,128)(2,1)S(1)} %collective-permute-done.4.refs_2_), channel_id=1, source_target_pairs={{0,4},{4,12},{12,8},{8,0},{1,5},{5,13},{13,9},{9,1},{2,6},{6,14},{... | collective-permute-start | bytes 835592 | tf_op jit(solution)/shard_map/ppermute | solution.py:309
  21.7 1.5 %collective-permute-start.9 = (bf16[136,1024]{1,0:T(8,128)(2,1)S(1)}, bf16[136,1024]{1,0:T(8,128)(2,1)S(1)}, u32[]{:S(2)}, u32[]{:S(2)}) collective-permute-start(bf16[136,1024]{1,0:T(8,128)(2,1)S(1)} %collective-permute-done.4.refs_2_), channel_id=1, source_target_pairs={{0,2},{2,0},{1,3},{3,1},{4,6},{6,4},{5,7},{7,5},{8,10},{10,8},{9,1... | collective-permute-start | bytes 835592 | tf_op jit(solution)/shard_map/ppermute | solution.py:281
  23.2 3.7 %chunk.4 = (bf16[128,1024]{1,0:T(8,128)(2,1)S(1)}, bf16[128,1024]{1,0:T(8,128)(2,1)S(1)}, bf16[4,96,1024]{2,1,0:T(8,128)(2,1)S(1)}, bf16[4,96,1024]{2,1,0:T(8,128)(2,1)S(1)}, bf16[4,96,768]{2,1,0:T(8,128)(2,1)S(1)}) custom-call(s32[1]{0:T(128)} %bitcast.first_ref, bf16[128,1024]{1,0:T(8,128)(2,1)S(1)} %get-tuple-element.150.refs_0_, ...), custom_call_target="tpu_custom_call" | custom-call | flops 1610612736 | bytes 8388608 | tf_op jit(solution)/shard_map/chunk/pallas_call | solution.py:171
  26.9 0.0 collective-permute-done.2.refs_0_
  26.9 0.0 collective-permute-done.3.refs_1_
  26.9 0.9 %collective-permute-start.6 = (bf16[128,1024]{1,0:T(8,128)(2,1)S(1)}, bf16[128,1024]{1,0:T(8,128)(2,1)S(1)}, u32[]{:S(2)}, u32[]{:S(2)}) collective-permute-start(bf16[128,1024]{1,0:T(8,128)(2,1)S(1)} %collective-permute-done.2.refs_0_), channel_id=1, source_target_pairs={{0,4},{4,12},{12,8},{8,0},{1,5},{5,13},{13,9},{9,1},{2,6},{6,14},{... | collective-permute-start | bytes 786440 | tf_op jit(solution)/shard_map/ppermute | solution.py:309
  27.8 1.0 %collective-permute-start.7 = (bf16[128,1024]{1,0:T(8,128)(2,1)S(1)}, bf16[128,1024]{1,0:T(8,128)(2,1)S(1)}, u32[]{:S(2)}, u32[]{:S(2)}) collective-permute-start(bf16[128,1024]{1,0:T(8,128)(2,1)S(1)} %collective-permute-done.2.refs_0_), channel_id=1, source_target_pairs={{0,2},{2,0},{1,3},{3,1},{4,6},{6,4},{5,7},{7,5},{8,10},{10,8},{9,1... | collective-permute-start | bytes 786440 | tf_op jit(solution)/shard_map/ppermute | solution.py:281
  28.8 0.9 %collective-permute-done.8.refs_2_ = bf16[136,1024]{1,0:T(8,128)(2,1)S(1)} collective-permute-done((bf16[136,1024]{1,0:T(8,128)(2,1)S(1)}, bf16[136,1024]{1,0:T(8,128)(2,1)S(1)}, u32[]{:S(2)}, u32[]{:S(2)}) %collective-permute-start.8) | collective-permute-done | bytes 278560 | tf_op jit(solution)/shard_map/ppermute | solution.py:309
  29.7 1.3 %collective-permute-done.9.refs_3_ = bf16[136,1024]{1,0:T(8,128)(2,1)S(1)} collective-permute-done((bf16[136,1024]{1,0:T(8,128)(2,1)S(1)}, bf16[136,1024]{1,0:T(8,128)(2,1)S(1)}, u32[]{:S(2)}, u32[]{:S(2)}) %collective-permute-start.9) | collective-permute-done | bytes 278560 | tf_op jit(solution)/shard_map/ppermute | solution.py:281
  31.0 2.3 %collective-permute-start.11 = (bf16[136,1024]{1,0:T(8,128)(2,1)S(1)}, bf16[136,1024]{1,0:T(8,128)(2,1)S(1)}, u32[]{:S(2)}, u32[]{:S(2)}) collective-permute-start(bf16[136,1024]{1,0:T(8,128)(2,1)S(1)} %collective-permute-done.8.refs_2_), channel_id=1, source_target_pairs={{0,4},{4,12},{12,8},{8,0},{1,5},{5,13},{13,9},{9,1},{2,6},{6,14},{... | collective-permute-start | bytes 835592 | tf_op jit(solution)/shard_map/ppermute | solution.py:309
  33.3 1.5 %collective-permute-start.12 = (bf16[136,1024]{1,0:T(8,128)(2,1)S(1)}, bf16[136,1024]{1,0:T(8,128)(2,1)S(1)}, u32[]{:S(2)}, u32[]{:S(2)}) collective-permute-start(bf16[136,1024]{1,0:T(8,128)(2,1)S(1)} %collective-permute-done.8.refs_2_), channel_id=1, source_target_pairs={{0,2},{2,0},{1,3},{3,1},{4,6},{6,4},{5,7},{7,5},{8,10},{10,8},{9,1... | collective-permute-start | bytes 835592 | tf_op jit(solution)/shard_map/ppermute | solution.py:281
  34.8 3.7 %chunk.5 = (bf16[256,1024]{1,0:T(8,128)(2,1)S(1)}, bf16[4,96,1024]{2,1,0:T(8,128)(2,1)S(1)}, bf16[4,96,1024]{2,1,0:T(8,128)(2,1)S(1)}, bf16[4,96,768]{2,1,0:T(8,128)(2,1)S(1)}) custom-call(s32[1]{0:T(128)} %bitcast.first_ref, bf16[128,1024]{1,0:T(8,128)(2,1)S(1)} %collective-permute-done.refs_0_, bf16[128,1024]{1,0:T(8,128)(2,1)S(1)} %collective-permute-done.3.refs_1_, ...), custom_call_target="tpu_custom_call" | custom-call | flops 1610612736 | bytes 8388608 | tf_op jit(solution)/shard_map/chunk/pallas_call | solution.py:171
  38.5 0.0 collective-permute-done.6.refs_0_
  38.5 0.0 collective-permute-done.7.refs_1_
  38.5 0.6 collective-permute-start.10
  39.1 1.3 %collective-permute-done.11.refs_2_ = bf16[136,1024]{1,0:T(8,128)(2,1)S(1)} collective-permute-done((bf16[136,1024]{1,0:T(8,128)(2,1)S(1)}, bf16[136,1024]{1,0:T(8,128)(2,1)S(1)}, u32[]{:S(2)}, u32[]{:S(2)}) %collective-permute-start.11) | collective-permute-done | bytes 278560 | tf_op jit(solution)/shard_map/ppermute | solution.py:309
  40.4 2.5 %collective-permute-done.12.refs_3_ = bf16[136,1024]{1,0:T(8,128)(2,1)S(1)} collective-permute-done((bf16[136,1024]{1,0:T(8,128)(2,1)S(1)}, bf16[136,1024]{1,0:T(8,128)(2,1)S(1)}, u32[]{:S(2)}, u32[]{:S(2)}) %collective-permute-start.12) | collective-permute-done | bytes 278560 | tf_op jit(solution)/shard_map/ppermute | solution.py:281
  42.8 1.5 %collective-permute-start.13 = (bf16[136,1024]{1,0:T(8,128)(2,1)S(1)}, bf16[136,1024]{1,0:T(8,128)(2,1)S(1)}, u32[]{:S(2)}, u32[]{:S(2)}) collective-permute-start(bf16[136,1024]{1,0:T(8,128)(2,1)S(1)} %collective-permute-done.11.refs_2_), channel_id=1, source_target_pairs={{0,2},{2,0},{1,3},{3,1},{4,6},{6,4},{5,7},{7,5},{8,10},{10,8},{9,1... | collective-permute-start | bytes 835592 | tf_op jit(solution)/shard_map/ppermute | solution.py:281
  44.4 3.7 %chunk.6 = (bf16[128,1024]{1,0:T(8,128)(2,1)S(1)}, bf16[128,1024]{1,0:T(8,128)(2,1)S(1)}, bf16[4,96,1024]{2,1,0:T(8,128)(2,1)S(1)}, bf16[4,96,1024]{2,1,0:T(8,128)(2,1)S(1)}, bf16[4,96,768]{2,1,0:T(8,128)(2,1)S(1)}) custom-call(s32[1]{0:T(128)} %bitcast.first_ref, bf16[128,1024]{1,0:T(8,128)(2,1)S(1)} %collective-permute-done.2.refs_0_, ...), custom_call_target="tpu_custom_call" | custom-call | flops 1610612736 | bytes 8388608 | tf_op jit(solution)/shard_map/chunk/pallas_call | solution.py:171
  48.1 0.4 collective-permute-done.10.refs_1_
  48.5 2.2 %collective-permute-start.15 = (bf16[256,1024]{1,0:T(8,128)(2,1)S(1)}, bf16[256,1024]{1,0:T(8,128)(2,1)S(1)}, u32[]{:S(2)}, u32[]{:S(2)}) collective-permute-start(bf16[256,1024]{1,0:T(8,128)(2,1)S(1)} %get-tuple-element.214), channel_id=1, source_target_pairs={{0,8},{4,0},{12,4},{8,12},{1,9},{5,1},{13,5},{9,13},{2,10},{6,2},{... | collective-permute-start | bytes 1572872 | tf_op jit(solution)/shard_map/ppermute | solution.py:318
  50.7 1.7 %collective-permute-done.13.refs_3_ = bf16[136,1024]{1,0:T(8,128)(2,1)S(1)} collective-permute-done((bf16[136,1024]{1,0:T(8,128)(2,1)S(1)}, bf16[136,1024]{1,0:T(8,128)(2,1)S(1)}, u32[]{:S(2)}, u32[]{:S(2)}) %collective-permute-start.13) | collective-permute-done | bytes 278560 | tf_op jit(solution)/shard_map/ppermute | solution.py:281
  52.4 1.5 %collective-permute-start.14 = (bf16[128,1024]{1,0:T(8,128)(2,1)S(1)}, bf16[128,1024]{1,0:T(8,128)(2,1)S(1)}, u32[]{:S(2)}, u32[]{:S(2)}) collective-permute-start(bf16[128,1024]{1,0:T(8,128)(2,1)S(1)} %get-tuple-element.232), channel_id=1, source_target_pairs={{0,2},{2,0},{1,3},{3,1},{4,6},{6,4},{5,7},{7,5},{8,10},{10,8},{9,1... | collective-permute-start | bytes 786440 | tf_op jit(solution)/shard_map/ppermute | solution.py:288
  53.9 3.7 %chunk.7 = (bf16[128,1024]{1,0:T(8,128)(2,1)S(1)}, bf16[128,1024]{1,0:T(8,128)(2,1)S(1)}, bf16[4,96,1024]{2,1,0:T(8,128)(2,1)S(1)}, bf16[4,96,1024]{2,1,0:T(8,128)(2,1)S(1)}, bf16[4,96,768]{2,1,0:T(8,128)(2,1)S(1)}) custom-call(s32[1]{0:T(128)} %bitcast.first_ref, bf16[128,1024]{1,0:T(8,128)(2,1)S(1)} %collective-permute-done.6.refs_0_, ...), custom_call_target="tpu_custom_call" | custom-call | flops 1610612736 | bytes 8388608 | tf_op jit(solution)/shard_map/chunk/pallas_call | solution.py:171
  57.6 0.6 collective-permute-start.16
  58.2 1.3 %collective-permute-done.14 = bf16[128,1024]{1,0:T(8,128)(2,1)S(1)} collective-permute-done((bf16[128,1024]{1,0:T(8,128)(2,1)S(1)}, bf16[128,1024]{1,0:T(8,128)(2,1)S(1)}, u32[]{:S(2)}, u32[]{:S(2)}) %collective-permute-start.14) | collective-permute-done | bytes 262176 | tf_op jit(solution)/shard_map/ppermute | solution.py:288
  59.5 0.3 collective-permute-done.15
  59.8 0.1 add_convert_fusion.3
  59.8 4.0 %collective-permute-start.17 = (bf16[128,1024]{1,0:T(8,128)(2,1)S(1)}, bf16[128,1024]{1,0:T(8,128)(2,1)S(1)}, u32[]{:S(2)}, u32[]{:S(2)}) collective-permute-start(bf16[128,1024]{1,0:T(8,128)(2,1)S(1)} %add_convert_fusion.3), channel_id=1, source_target_pairs={{0,4},{4,12},{12,8},{8,0},{1,5},{5,13},{13,9},{9,1},{2,6},{6,14},{... | collective-permute-start | bytes 786440 | tf_op jit(solution)/shard_map/ppermute | solution.py:298
  63.9 1.9 %weight_grads.2 = bf16[4,768,512]{2,1,0:T(8,128)(2,1)S(1)} custom-call(s32[1]{0:T(128)S(6)} %sub.3.side_ref, bf16[4,96,1024]{2,1,0:T(8,128)(2,1)S(1)} %get-tuple-element.251.refs_0_, bf16[4,96,1024]{2,1,0:T(8,128)(2,1)S(1)} %get-tuple-element.252.refs_1_, bf16[4,96,1024]{2,1,0:T(8,128)(2,1)S(1)} %get-tuple-element.253.refs_2_, ...), custom_call_target="tpu_custom_call" | custom-call | flops 1207959552 | bytes 8650752 | tf_op jit(solution)/shard_map/weight_grads/pallas_call | solution.py:244
  65.7 0.0 collective-permute-done.16
  65.8 2.0 %collective-permute-done.17 = bf16[128,1024]{1,0:T(8,128)(2,1)S(1)} collective-permute-done((bf16[128,1024]{1,0:T(8,128)(2,1)S(1)}, bf16[128,1024]{1,0:T(8,128)(2,1)S(1)}, u32[]{:S(2)}, u32[]{:S(2)}) %collective-permute-start.17) | collective-permute-done | bytes 262176 | tf_op jit(solution)/shard_map/ppermute | solution.py:298
  67.8 0.0 collective-permute-start.18
  67.8 0.1 add_convert_fusion.2
  67.9 2.5 %collective-permute-start.19 = (bf16[128,1024]{1,0:T(8,128)(2,1)S(1)}, bf16[128,1024]{1,0:T(8,128)(2,1)S(1)}, u32[]{:S(2)}, u32[]{:S(2)}) collective-permute-start(bf16[128,1024]{1,0:T(8,128)(2,1)S(1)} %add_convert_fusion.2), channel_id=1, source_target_pairs={{0,4},{4,12},{12,8},{8,0},{1,5},{5,13},{13,9},{9,1},{2,6},{6,14},{... | collective-permute-start | bytes 786440 | tf_op jit(solution)/shard_map/ppermute | solution.py:298
  70.4 0.1 add_convert_fusion.1
  70.5 1.6 %collective-permute-start.20 = (bf16[128,1024]{1,0:T(8,128)(2,1)S(1)}, bf16[128,1024]{1,0:T(8,128)(2,1)S(1)}, u32[]{:S(2)}, u32[]{:S(2)}) collective-permute-start(bf16[128,1024]{1,0:T(8,128)(2,1)S(1)} %add_convert_fusion.1), channel_id=1, source_target_pairs={{0,2},{2,0},{1,3},{3,1},{4,6},{6,4},{5,7},{7,5},{8,10},{10,8},{9,1... | collective-permute-start | bytes 786440 | tf_op jit(solution)/shard_map/ppermute | solution.py:288
  72.0 1.4 %collective-permute-done.18.refs_12_ = bf16[4,768,512]{2,1,0:T(8,128)(2,1)S(1)} collective-permute-done((bf16[4,768,512]{2,1,0:T(8,128)(2,1)S(1)}, bf16[4,768,512]{2,1,0:T(8,128)(2,1)S(1)}, u32[]{:S(2)}, u32[]{:S(2)}) %collective-permute-start.18) | collective-permute-done | bytes 3145760 | tf_op jit(solution)/shard_map/ppermute | solution.py:331
  73.4 2.7 %weight_grads.3 = (bf16[4,512,256]{2,1,0:T(8,128)(2,1)}, bf16[4,512,256]{2,1,0:T(8,128)(2,1)}, bf16[4,256,512]{2,1,0:T(8,128)(2,1)}) custom-call(s32[1]{0:T(128)} %bitcast.1.side_ref, bf16[4,96,1024]{2,1,0:T(8,128)(2,1)S(1)} %get-tuple-element.251.refs_0_, bf16[4,96,1024]{2,1,0:T(8,128)(2,1)S(1)} %get-tuple-element.252.refs_1_, ...), custom_call_target="tpu_custom_call" | custom-call | flops 1207959552 | bytes 8650752 | tf_op jit(solution)/shard_map/weight_grads/pallas_call | solution.py:244
  76.1 1.4 %collective-permute-done.19 = bf16[128,1024]{1,0:T(8,128)(2,1)S(1)} collective-permute-done((bf16[128,1024]{1,0:T(8,128)(2,1)S(1)}, bf16[128,1024]{1,0:T(8,128)(2,1)S(1)}, u32[]{:S(2)}, u32[]{:S(2)}) %collective-permute-start.19) | collective-permute-done | bytes 262176 | tf_op jit(solution)/shard_map/ppermute | solution.py:298
  77.6 1.4 %collective-permute-done.20 = bf16[128,1024]{1,0:T(8,128)(2,1)S(1)} collective-permute-done((bf16[128,1024]{1,0:T(8,128)(2,1)S(1)}, bf16[128,1024]{1,0:T(8,128)(2,1)S(1)}, u32[]{:S(2)}, u32[]{:S(2)}) %collective-permute-start.20) | collective-permute-done | bytes 262176 | tf_op jit(solution)/shard_map/ppermute | solution.py:288
  79.0 0.9 %add_convert_fusion = bf16[128,1024]{1,0:T(8,128)(2,1)} fusion(bf16[128,1024]{1,0:T(8,128)(2,1)S(1)} %collective-permute-done.19, bf16[128,1024]{1,0:T(8,128)(2,1)S(1)} %collective-permute-done.20, bf16[128,1024]{1,0:T(8,128)(2,1)S(1)} %get-tuple-element.248, bf16[256,1024]{1,0:T(8,128)(2,1)S(1)} %collective-permute-done.15), kind=kLoop, calls=%fused_computation | loop fusion | flops 1048576 | bytes 1310720 | tf_op jit(solution)/shard_map/convert_element_type | solution.py:342
Async XLA Ops:
  0.6 12.4 %collective-permute-start = (bf16[128,1024]{1,0:T(8,128)(2,1)}, bf16[128,1024]{1,0:T(8,128)(2,1)S(1)}, u32[]{:S(2)}, u32[]{:S(2)}) collective-permute-start(bf16[128,1024]{1,0:T(8,128)(2,1)} %tokens), channel_id=1, source_target_pairs={{0,4},{4,12},{12,8},{8,0},{1,5},{5,13},{13,9},{9,1},{2,6},{6,14},{... | collective-permute-start | bytes 786440 | tf_op jit(solution)/shard_map/ppermute | solution.py:309
  3.7 9.3 %collective-permute-start.1 = (bf16[128,1024]{1,0:T(8,128)(2,1)}, bf16[128,1024]{1,0:T(8,128)(2,1)S(1)}, u32[]{:S(2)}, u32[]{:S(2)}) collective-permute-start(bf16[128,1024]{1,0:T(8,128)(2,1)} %tokens), channel_id=1, source_target_pairs={{0,2},{2,0},{1,3},{3,1},{4,6},{6,4},{5,7},{7,5},{8,10},{10,8},{9,1... | collective-permute-start | bytes 786440 | tf_op jit(solution)/shard_map/ppermute | solution.py:281
  7.0 11.1 %collective-permute-start.4 = (bf16[136,1024]{1,0:T(8,128)(2,1)S(1)}, bf16[136,1024]{1,0:T(8,128)(2,1)S(1)}, u32[]{:S(2)}, u32[]{:S(2)}) collective-permute-start(bf16[136,1024]{1,0:T(8,128)(2,1)S(1)} %get-tuple-element.153.refs_2_), channel_id=1, source_target_pairs={{0,4},{4,12},{12,8},{8,0},{1,5},{5,13},{13,9},{9,1},{2,6},{6,14},{... | collective-permute-start | bytes 835592 | tf_op jit(solution)/shard_map/ppermute | solution.py:309
  9.6 9.6 %collective-permute-start.5 = (bf16[136,1024]{1,0:T(8,128)(2,1)S(1)}, bf16[136,1024]{1,0:T(8,128)(2,1)S(1)}, u32[]{:S(2)}, u32[]{:S(2)}) collective-permute-start(bf16[136,1024]{1,0:T(8,128)(2,1)S(1)} %get-tuple-element.153.refs_2_), channel_id=1, source_target_pairs={{0,2},{2,0},{1,3},{3,1},{4,6},{6,4},{5,7},{7,5},{8,10},{10,8},{9,1... | collective-permute-start | bytes 835592 | tf_op jit(solution)/shard_map/ppermute | solution.py:281
  13.1 13.8 %collective-permute-start.2 = (bf16[128,1024]{1,0:T(8,128)(2,1)S(1)}, bf16[128,1024]{1,0:T(8,128)(2,1)S(1)}, u32[]{:S(2)}, u32[]{:S(2)}) collective-permute-start(bf16[128,1024]{1,0:T(8,128)(2,1)S(1)} %collective-permute-done.refs_0_), channel_id=1, source_target_pairs={{0,4},{4,12},{12,8},{8,0},{1,5},{5,13},{13,9},{9,1},{2,6},{6,14},{... | collective-permute-start | bytes 786440 | tf_op jit(solution)/shard_map/ppermute | solution.py:309
  15.7 11.1 %collective-permute-start.3 = (bf16[128,1024]{1,0:T(8,128)(2,1)S(1)}, bf16[128,1024]{1,0:T(8,128)(2,1)S(1)}, u32[]{:S(2)}, u32[]{:S(2)}) collective-permute-start(bf16[128,1024]{1,0:T(8,128)(2,1)S(1)} %collective-permute-done.refs_0_), channel_id=1, source_target_pairs={{0,2},{2,0},{1,3},{3,1},{4,6},{6,4},{5,7},{7,5},{8,10},{10,8},{9,1... | collective-permute-start | bytes 786440 | tf_op jit(solution)/shard_map/ppermute | solution.py:281
  19.2 10.5 %collective-permute-start.8 = (bf16[136,1024]{1,0:T(8,128)(2,1)S(1)}, bf16[136,1024]{1,0:T(8,128)(2,1)S(1)}, u32[]{:S(2)}, u32[]{:S(2)}) collective-permute-start(bf16[136,1024]{1,0:T(8,128)(2,1)S(1)} %collective-permute-done.4.refs_2_), channel_id=1, source_target_pairs={{0,4},{4,12},{12,8},{8,0},{1,5},{5,13},{13,9},{9,1},{2,6},{6,14},{... | collective-permute-start | bytes 835592 | tf_op jit(solution)/shard_map/ppermute | solution.py:309
  21.7 9.3 %collective-permute-start.9 = (bf16[136,1024]{1,0:T(8,128)(2,1)S(1)}, bf16[136,1024]{1,0:T(8,128)(2,1)S(1)}, u32[]{:S(2)}, u32[]{:S(2)}) collective-permute-start(bf16[136,1024]{1,0:T(8,128)(2,1)S(1)} %collective-permute-done.4.refs_2_), channel_id=1, source_target_pairs={{0,2},{2,0},{1,3},{3,1},{4,6},{6,4},{5,7},{7,5},{8,10},{10,8},{9,1... | collective-permute-start | bytes 835592 | tf_op jit(solution)/shard_map/ppermute | solution.py:281
  26.9 11.6 %collective-permute-start.6 = (bf16[128,1024]{1,0:T(8,128)(2,1)S(1)}, bf16[128,1024]{1,0:T(8,128)(2,1)S(1)}, u32[]{:S(2)}, u32[]{:S(2)}) collective-permute-start(bf16[128,1024]{1,0:T(8,128)(2,1)S(1)} %collective-permute-done.2.refs_0_), channel_id=1, source_target_pairs={{0,4},{4,12},{12,8},{8,0},{1,5},{5,13},{13,9},{9,1},{2,6},{6,14},{... | collective-permute-start | bytes 786440 | tf_op jit(solution)/shard_map/ppermute | solution.py:309
  27.8 10.7 %collective-permute-start.7 = (bf16[128,1024]{1,0:T(8,128)(2,1)S(1)}, bf16[128,1024]{1,0:T(8,128)(2,1)S(1)}, u32[]{:S(2)}, u32[]{:S(2)}) collective-permute-start(bf16[128,1024]{1,0:T(8,128)(2,1)S(1)} %collective-permute-done.2.refs_0_), channel_id=1, source_target_pairs={{0,2},{2,0},{1,3},{3,1},{4,6},{6,4},{5,7},{7,5},{8,10},{10,8},{9,1... | collective-permute-start | bytes 786440 | tf_op jit(solution)/shard_map/ppermute | solution.py:281
  31.0 9.3 %collective-permute-start.11 = (bf16[136,1024]{1,0:T(8,128)(2,1)S(1)}, bf16[136,1024]{1,0:T(8,128)(2,1)S(1)}, u32[]{:S(2)}, u32[]{:S(2)}) collective-permute-start(bf16[136,1024]{1,0:T(8,128)(2,1)S(1)} %collective-permute-done.8.refs_2_), channel_id=1, source_target_pairs={{0,4},{4,12},{12,8},{8,0},{1,5},{5,13},{13,9},{9,1},{2,6},{6,14},{... | collective-permute-start | bytes 835592 | tf_op jit(solution)/shard_map/ppermute | solution.py:309
  33.3 9.5 %collective-permute-start.12 = (bf16[136,1024]{1,0:T(8,128)(2,1)S(1)}, bf16[136,1024]{1,0:T(8,128)(2,1)S(1)}, u32[]{:S(2)}, u32[]{:S(2)}) collective-permute-start(bf16[136,1024]{1,0:T(8,128)(2,1)S(1)} %collective-permute-done.8.refs_2_), channel_id=1, source_target_pairs={{0,2},{2,0},{1,3},{3,1},{4,6},{6,4},{5,7},{7,5},{8,10},{10,8},{9,1... | collective-permute-start | bytes 835592 | tf_op jit(solution)/shard_map/ppermute | solution.py:281
  38.5 10.0 %collective-permute-start.10 = (bf16[128,1024]{1,0:T(8,128)(2,1)S(1)}, bf16[128,1024]{1,0:T(8,128)(2,1)S(1)}, u32[]{:S(2)}, u32[]{:S(2)}) collective-permute-start(bf16[128,1024]{1,0:T(8,128)(2,1)S(1)} %collective-permute-done.6.refs_0_), channel_id=1, source_target_pairs={{0,2},{2,0},{1,3},{3,1},{4,6},{6,4},{5,7},{7,5},{8,10},{10,8},{9,1... | collective-permute-start | bytes 786440 | tf_op jit(solution)/shard_map/ppermute | solution.py:281
  42.8 9.6 %collective-permute-start.13 = (bf16[136,1024]{1,0:T(8,128)(2,1)S(1)}, bf16[136,1024]{1,0:T(8,128)(2,1)S(1)}, u32[]{:S(2)}, u32[]{:S(2)}) collective-permute-start(bf16[136,1024]{1,0:T(8,128)(2,1)S(1)} %collective-permute-done.11.refs_2_), channel_id=1, source_target_pairs={{0,2},{2,0},{1,3},{3,1},{4,6},{6,4},{5,7},{7,5},{8,10},{10,8},{9,1... | collective-permute-start | bytes 835592 | tf_op jit(solution)/shard_map/ppermute | solution.py:281
  48.5 11.3 %collective-permute-start.15 = (bf16[256,1024]{1,0:T(8,128)(2,1)S(1)}, bf16[256,1024]{1,0:T(8,128)(2,1)S(1)}, u32[]{:S(2)}, u32[]{:S(2)}) collective-permute-start(bf16[256,1024]{1,0:T(8,128)(2,1)S(1)} %get-tuple-element.214), channel_id=1, source_target_pairs={{0,8},{4,0},{12,4},{8,12},{1,9},{5,1},{13,5},{9,13},{2,10},{6,2},{... | collective-permute-start | bytes 1572872 | tf_op jit(solution)/shard_map/ppermute | solution.py:318
  52.4 7.1 %collective-permute-start.14 = (bf16[128,1024]{1,0:T(8,128)(2,1)S(1)}, bf16[128,1024]{1,0:T(8,128)(2,1)S(1)}, u32[]{:S(2)}, u32[]{:S(2)}) collective-permute-start(bf16[128,1024]{1,0:T(8,128)(2,1)S(1)} %get-tuple-element.232), channel_id=1, source_target_pairs={{0,2},{2,0},{1,3},{3,1},{4,6},{6,4},{5,7},{7,5},{8,10},{10,8},{9,1... | collective-permute-start | bytes 786440 | tf_op jit(solution)/shard_map/ppermute | solution.py:288
  57.6 8.1 %collective-permute-start.16 = (bf16[128,1024]{1,0:T(8,128)(2,1)S(1)}, bf16[128,1024]{1,0:T(8,128)(2,1)S(1)}, u32[]{:S(2)}, u32[]{:S(2)}) collective-permute-start(bf16[128,1024]{1,0:T(8,128)(2,1)S(1)} %get-tuple-element.244), channel_id=1, source_target_pairs={{0,2},{2,0},{1,3},{3,1},{4,6},{6,4},{5,7},{7,5},{8,10},{10,8},{9,1... | collective-permute-start | bytes 786440 | tf_op jit(solution)/shard_map/ppermute | solution.py:288
  59.8 7.9 %collective-permute-start.17 = (bf16[128,1024]{1,0:T(8,128)(2,1)S(1)}, bf16[128,1024]{1,0:T(8,128)(2,1)S(1)}, u32[]{:S(2)}, u32[]{:S(2)}) collective-permute-start(bf16[128,1024]{1,0:T(8,128)(2,1)S(1)} %add_convert_fusion.3), channel_id=1, source_target_pairs={{0,4},{4,12},{12,8},{8,0},{1,5},{5,13},{13,9},{9,1},{2,6},{6,14},{... | collective-permute-start | bytes 786440 | tf_op jit(solution)/shard_map/ppermute | solution.py:298
  67.8 5.7 %collective-permute-start.18 = (bf16[4,768,512]{2,1,0:T(8,128)(2,1)S(1)}, bf16[4,768,512]{2,1,0:T(8,128)(2,1)S(1)}, u32[]{:S(2)}, u32[]{:S(2)}) collective-permute-start(bf16[4,768,512]{2,1,0:T(8,128)(2,1)S(1)} %weight_grads.2), channel_id=1, source_target_pairs={{0,1},{1,0},{2,3},{3,2},{4,5},{5,4},{6,7},{7,6},{8,9},{9,8},{10,11... | collective-permute-start | bytes 9437192 | tf_op jit(solution)/shard_map/ppermute | solution.py:331
  67.9 9.7 %collective-permute-start.19 = (bf16[128,1024]{1,0:T(8,128)(2,1)S(1)}, bf16[128,1024]{1,0:T(8,128)(2,1)S(1)}, u32[]{:S(2)}, u32[]{:S(2)}) collective-permute-start(bf16[128,1024]{1,0:T(8,128)(2,1)S(1)} %add_convert_fusion.2), channel_id=1, source_target_pairs={{0,4},{4,12},{12,8},{8,0},{1,5},{5,13},{13,9},{9,1},{2,6},{6,14},{... | collective-permute-start | bytes 786440 | tf_op jit(solution)/shard_map/ppermute | solution.py:298
  70.5 8.5 %collective-permute-start.20 = (bf16[128,1024]{1,0:T(8,128)(2,1)S(1)}, bf16[128,1024]{1,0:T(8,128)(2,1)S(1)}, u32[]{:S(2)}, u32[]{:S(2)}) collective-permute-start(bf16[128,1024]{1,0:T(8,128)(2,1)S(1)} %add_convert_fusion.1), channel_id=1, source_target_pairs={{0,2},{2,0},{1,3},{3,1},{4,6},{6,4},{5,7},{7,5},{8,10},{10,8},{9,1... | collective-permute-start | bytes 786440 | tf_op jit(solution)/shard_map/ppermute | solution.py:288

commit v22 on v21

--- a/solution.py
+++ b/solution.py
@@ -323,10 +323,11 @@
     chunks, backs, near = tie(chunks, backs, near)
 
     backs[last] = last_back
-    carried = homeward(group_sum(chunks[last - 1][0], backs[last - 1]), last)
     kept = [[chunks[k][i] for k in range(n_group)] for i in (-3, -2, -1)]
     to_send = weight_call(other_half, *kept)
-    to_send, backs[last], carried = tie(to_send, backs[last], carried)
+    passed, to_send = tie(group_sum(chunks[last - 1][0], backs[last - 1]), to_send)
+    carried = homeward(passed, last)
+    to_send, backs[last] = tie(to_send, backs[last])
 
     got = lax.ppermute(to_send, "dp", [(0, 1), (1, 0)])
     sent[last] = homeward(group_sum(chunks[last][0], [*backs[last], carried]), last)

time: 80.1 us -> 85.3 us (1.065)
  waiting for transfers between devices: 17.9 us -> 24.3 us
  starting transfers between devices: 36.2 us -> 34.9 us
    ppermute x2, waiting for transfers between devices: 3.44 us -> 8.87 us  [homeward(): return lax.ppermute(group_part, 'group', along(-k))]
    ppermute x3, waiting for transfers between devices: 2.75 us -> 5.12 us  [across(): lax.ppermute(others[(s - 1) * tok_rows:s * tok_rows], 'ingroup', shift(-s))]
    ppermute x1, waiting for transfers between devices: 1.36 us -> 0.01 us  [per_device(): got = lax.ppermute(to_send, 'dp', [(0, 1), (1, 0)])]
    ppermute x2, starting transfers between devices: 6.55 us -> 5.3 us  [homeward(): return lax.ppermute(group_part, 'group', along(-k))]
  transfers between devices with their start and end apart: 21 -> 21, of which waited for: 14 -> 14; matrix products, arithmetic and copies ran while one was open for 0% -> 0% of each run, Pallas kernels for 30% -> 28%
where the time goes in v22:
time: 85.3 us; the launch traced here: 85.1 us
  starting transfers between devices  34.9 us (41%)
  waiting for transfers between devices  24.3 us (28%)
  Pallas kernels  23.9 us (28%)
  other arithmetic  1.13 us (1%)
    pallas_call x4, Pallas kernels, chunk_call(): pl.pallas_call(functools.partial(chunk_kernel, n_blocks, tok_rows, capaci...  14.7 us
    ppermute x6, starting transfers between devices, per_device(): lax.ppermute(v, 'group', along(1))  14.1 us
    ppermute x8, starting transfers between devices, spread(): lax.ppermute(column, 'ingroup', shift(s))  9.65 us
    ppermute x2, waiting for transfers between devices, homeward(): return lax.ppermute(group_part, 'group', along(-k))  8.87 us
    ppermute x8, waiting for transfers between devices, spread(): lax.ppermute(column, 'ingroup', shift(s))  7.07 us
    ppermute x2, starting transfers between devices, homeward(): return lax.ppermute(group_part, 'group', along(-k))  5.3 us
    ppermute x3, waiting for transfers between devices, across(): lax.ppermute(others[(s - 1) * tok_rows:s * tok_rows], 'ingroup', shift(-s))  5.12 us
    pallas_call x2, Pallas kernels, weight_call(): pl.pallas_call(functools.partial(kernel, n), in_specs=[smem] + [vmem] * l...  4.57 us
  transfers between devices with their start and end apart: 21, of which 14 were waited for; matrix products, arithmetic and copies ran while one was open for 0% of the time, Pallas kernels for 28%

profile of v22, /device:TPU:0, one launch (start us, length us, event | category | flops | bytes accessed | tf_op | source)
XLA Modules:
  0.0 85.1 jit_solution(14523705096953300469)
XLA Ops:
  0.6 3.1 %collective-permute-start = (bf16[128,1024]{1,0:T(8,128)(2,1)}, bf16[128,1024]{1,0:T(8,128)(2,1)S(1)}, u32[]{:S(2)}, u32[]{:S(2)}) collective-permute-start(bf16[128,1024]{1,0:T(8,128)(2,1)} %tokens), channel_id=1, source_target_pairs={{0,4},{4,12},{12,8},{8,0},{1,5},{5,13},{13,9},{9,1},{2,6},{6,14},{... | collective-permute-start | bytes 786440 | tf_op jit(solution)/shard_map/ppermute | solution.py:309
  3.7 1.5 %collective-permute-start.1 = (bf16[128,1024]{1,0:T(8,128)(2,1)}, bf16[128,1024]{1,0:T(8,128)(2,1)S(1)}, u32[]{:S(2)}, u32[]{:S(2)}) collective-permute-start(bf16[128,1024]{1,0:T(8,128)(2,1)} %tokens), channel_id=1, source_target_pairs={{0,2},{2,0},{1,3},{3,1},{4,6},{6,4},{5,7},{7,5},{8,10},{10,8},{9,1... | collective-permute-start | bytes 786440 | tf_op jit(solution)/shard_map/ppermute | solution.py:281
  5.2 1.8 %pack.1 = (bf16[128,1024]{1,0:T(8,128)(2,1)S(1)}, bf16[136,1024]{1,0:T(8,128)(2,1)S(1)}) custom-call(bf16[128,1024]{1,0:T(8,128)(2,1)} %tokens, bf16[128,1024]{1,0:T(8,128)(2,1)} %upstream.1, s32[8,128]{1,0:T(8,128)} %bitcast.5, s32[8,128]{1,0:T(8,128)} %bitcast.6, s32[8,128]{1,0:T(8,128)} %bitcast.7), custom_call_target="tpu_custom_call" | custom-call | tf_op jit(solution)/shard_map/pack/pallas_call | solution.py:58
  7.0 2.6 %collective-permute-start.4 = (bf16[136,1024]{1,0:T(8,128)(2,1)S(1)}, bf16[136,1024]{1,0:T(8,128)(2,1)S(1)}, u32[]{:S(2)}, u32[]{:S(2)}) collective-permute-start(bf16[136,1024]{1,0:T(8,128)(2,1)S(1)} %get-tuple-element.154.refs_2_), channel_id=1, source_target_pairs={{0,4},{4,12},{12,8},{8,0},{1,5},{5,13},{13,9},{9,1},{2,6},{6,14},{... | collective-permute-start | bytes 835592 | tf_op jit(solution)/shard_map/ppermute | solution.py:309
  9.6 0.5 collective-permute-start.5
  10.2 2.9 %load.1 = (bf16[4,1024,256]{2,1,0:T(8,128)(2,1)S(1)}, bf16[4,1024,256]{2,1,0:T(8,128)(2,1)S(1)}, bf16[4,256,1024]{2,1,0:T(8,128)(2,1)S(1)}) custom-call(bf16[4,1024,256]{2,1,0:T(8,128)(2,1)} %refs_0_.1, bf16[4,1024,256]{2,1,0:T(8,128)(2,1)} %refs_1_.1, bf16[4,256,1024]{2,1,0:T(8,128)(2,1)} %refs_2_.1), custom_call_target="tpu_custom_call" | custom-call | tf_op jit(solution)/shard_map/load/pallas_call | solution.py:98
  13.0 0.0 collective-permute-done.refs_0_
  13.1 0.0 collective-permute-done.1.refs_1_
  13.1 2.7 %collective-permute-start.2 = (bf16[128,1024]{1,0:T(8,128)(2,1)S(1)}, bf16[128,1024]{1,0:T(8,128)(2,1)S(1)}, u32[]{:S(2)}, u32[]{:S(2)}) collective-permute-start(bf16[128,1024]{1,0:T(8,128)(2,1)S(1)} %collective-permute-done.refs_0_), channel_id=1, source_target_pairs={{0,4},{4,12},{12,8},{8,0},{1,5},{5,13},{13,9},{9,1},{2,6},{6,14},{... | collective-permute-start | bytes 786440 | tf_op jit(solution)/shard_map/ppermute | solution.py:309
  15.7 1.5 %collective-permute-start.3 = (bf16[128,1024]{1,0:T(8,128)(2,1)S(1)}, bf16[128,1024]{1,0:T(8,128)(2,1)S(1)}, u32[]{:S(2)}, u32[]{:S(2)}) collective-permute-start(bf16[128,1024]{1,0:T(8,128)(2,1)S(1)} %collective-permute-done.refs_0_), channel_id=1, source_target_pairs={{0,2},{2,0},{1,3},{3,1},{4,6},{6,4},{5,7},{7,5},{8,10},{10,8},{9,1... | collective-permute-start | bytes 786440 | tf_op jit(solution)/shard_map/ppermute | solution.py:281
  17.2 0.8 collective-permute-done.4.refs_2_
  18.0 1.2 %collective-permute-done.5.refs_3_ = bf16[136,1024]{1,0:T(8,128)(2,1)S(1)} collective-permute-done((bf16[136,1024]{1,0:T(8,128)(2,1)S(1)}, bf16[136,1024]{1,0:T(8,128)(2,1)S(1)}, u32[]{:S(2)}, u32[]{:S(2)}) %collective-permute-start.5) | collective-permute-done | bytes 278560 | tf_op jit(solution)/shard_map/ppermute | solution.py:281
  19.2 2.5 %collective-permute-start.8 = (bf16[136,1024]{1,0:T(8,128)(2,1)S(1)}, bf16[136,1024]{1,0:T(8,128)(2,1)S(1)}, u32[]{:S(2)}, u32[]{:S(2)}) collective-permute-start(bf16[136,1024]{1,0:T(8,128)(2,1)S(1)} %collective-permute-done.4.refs_2_), channel_id=1, source_target_pairs={{0,4},{4,12},{12,8},{8,0},{1,5},{5,13},{13,9},{9,1},{2,6},{6,14},{... | collective-permute-start | bytes 835592 | tf_op jit(solution)/shard_map/ppermute | solution.py:309
  21.7 1.5 %collective-permute-start.9 = (bf16[136,1024]{1,0:T(8,128)(2,1)S(1)}, bf16[136,1024]{1,0:T(8,128)(2,1)S(1)}, u32[]{:S(2)}, u32[]{:S(2)}) collective-permute-start(bf16[136,1024]{1,0:T(8,128)(2,1)S(1)} %collective-permute-done.4.refs_2_), channel_id=1, source_target_pairs={{0,2},{2,0},{1,3},{3,1},{4,6},{6,4},{5,7},{7,5},{8,10},{10,8},{9,1... | collective-permute-start | bytes 835592 | tf_op jit(solution)/shard_map/ppermute | solution.py:281
  23.2 3.7 %chunk.4 = (bf16[128,1024]{1,0:T(8,128)(2,1)S(1)}, bf16[128,1024]{1,0:T(8,128)(2,1)S(1)}, bf16[4,96,1024]{2,1,0:T(8,128)(2,1)S(1)}, bf16[4,96,1024]{2,1,0:T(8,128)(2,1)S(1)}, bf16[4,96,768]{2,1,0:T(8,128)(2,1)S(1)}) custom-call(s32[1]{0:T(128)} %bitcast.first_ref, bf16[128,1024]{1,0:T(8,128)(2,1)S(1)} %get-tuple-element.151.refs_0_, ...), custom_call_target="tpu_custom_call" | custom-call | flops 1610612736 | bytes 8388608 | tf_op jit(solution)/shard_map/chunk/pallas_call | solution.py:171
  26.9 0.0 collective-permute-done.2.refs_0_
  26.9 0.0 collective-permute-done.3.refs_1_
  26.9 0.9 %collective-permute-start.6 = (bf16[128,1024]{1,0:T(8,128)(2,1)S(1)}, bf16[128,1024]{1,0:T(8,128)(2,1)S(1)}, u32[]{:S(2)}, u32[]{:S(2)}) collective-permute-start(bf16[128,1024]{1,0:T(8,128)(2,1)S(1)} %collective-permute-done.2.refs_0_), channel_id=1, source_target_pairs={{0,4},{4,12},{12,8},{8,0},{1,5},{5,13},{13,9},{9,1},{2,6},{6,14},{... | collective-permute-start | bytes 786440 | tf_op jit(solution)/shard_map/ppermute | solution.py:309
  27.8 1.0 %collective-permute-start.7 = (bf16[128,1024]{1,0:T(8,128)(2,1)S(1)}, bf16[128,1024]{1,0:T(8,128)(2,1)S(1)}, u32[]{:S(2)}, u32[]{:S(2)}) collective-permute-start(bf16[128,1024]{1,0:T(8,128)(2,1)S(1)} %collective-permute-done.2.refs_0_), channel_id=1, source_target_pairs={{0,2},{2,0},{1,3},{3,1},{4,6},{6,4},{5,7},{7,5},{8,10},{10,8},{9,1... | collective-permute-start | bytes 786440 | tf_op jit(solution)/shard_map/ppermute | solution.py:281
  28.8 0.9 %collective-permute-done.8.refs_2_ = bf16[136,1024]{1,0:T(8,128)(2,1)S(1)} collective-permute-done((bf16[136,1024]{1,0:T(8,128)(2,1)S(1)}, bf16[136,1024]{1,0:T(8,128)(2,1)S(1)}, u32[]{:S(2)}, u32[]{:S(2)}) %collective-permute-start.8) | collective-permute-done | bytes 278560 | tf_op jit(solution)/shard_map/ppermute | solution.py:309
  29.7 1.3 %collective-permute-done.9.refs_3_ = bf16[136,1024]{1,0:T(8,128)(2,1)S(1)} collective-permute-done((bf16[136,1024]{1,0:T(8,128)(2,1)S(1)}, bf16[136,1024]{1,0:T(8,128)(2,1)S(1)}, u32[]{:S(2)}, u32[]{:S(2)}) %collective-permute-start.9) | collective-permute-done | bytes 278560 | tf_op jit(solution)/shard_map/ppermute | solution.py:281
  31.0 2.3 %collective-permute-start.11 = (bf16[136,1024]{1,0:T(8,128)(2,1)S(1)}, bf16[136,1024]{1,0:T(8,128)(2,1)S(1)}, u32[]{:S(2)}, u32[]{:S(2)}) collective-permute-start(bf16[136,1024]{1,0:T(8,128)(2,1)S(1)} %collective-permute-done.8.refs_2_), channel_id=1, source_target_pairs={{0,4},{4,12},{12,8},{8,0},{1,5},{5,13},{13,9},{9,1},{2,6},{6,14},{... | collective-permute-start | bytes 835592 | tf_op jit(solution)/shard_map/ppermute | solution.py:309
  33.3 1.5 %collective-permute-start.12 = (bf16[136,1024]{1,0:T(8,128)(2,1)S(1)}, bf16[136,1024]{1,0:T(8,128)(2,1)S(1)}, u32[]{:S(2)}, u32[]{:S(2)}) collective-permute-start(bf16[136,1024]{1,0:T(8,128)(2,1)S(1)} %collective-permute-done.8.refs_2_), channel_id=1, source_target_pairs={{0,2},{2,0},{1,3},{3,1},{4,6},{6,4},{5,7},{7,5},{8,10},{10,8},{9,1... | collective-permute-start | bytes 835592 | tf_op jit(solution)/shard_map/ppermute | solution.py:281
  34.8 3.7 %chunk.5 = (bf16[256,1024]{1,0:T(8,128)(2,1)S(1)}, bf16[4,96,1024]{2,1,0:T(8,128)(2,1)S(1)}, bf16[4,96,1024]{2,1,0:T(8,128)(2,1)S(1)}, bf16[4,96,768]{2,1,0:T(8,128)(2,1)S(1)}) custom-call(s32[1]{0:T(128)} %bitcast.first_ref, bf16[128,1024]{1,0:T(8,128)(2,1)S(1)} %collective-permute-done.refs_0_, bf16[128,1024]{1,0:T(8,128)(2,1)S(1)} %collective-permute-done.3.refs_1_, ...), custom_call_target="tpu_custom_call" | custom-call | flops 1610612736 | bytes 8388608 | tf_op jit(solution)/shard_map/chunk/pallas_call | solution.py:171
  38.5 0.0 collective-permute-done.6.refs_0_
  38.5 0.0 collective-permute-done.7.refs_1_
  38.5 0.6 collective-permute-start.10
  39.1 1.3 %collective-permute-done.11.refs_2_ = bf16[136,1024]{1,0:T(8,128)(2,1)S(1)} collective-permute-done((bf16[136,1024]{1,0:T(8,128)(2,1)S(1)}, bf16[136,1024]{1,0:T(8,128)(2,1)S(1)}, u32[]{:S(2)}, u32[]{:S(2)}) %collective-permute-start.11) | collective-permute-done | bytes 278560 | tf_op jit(solution)/shard_map/ppermute | solution.py:309
  40.4 2.5 %collective-permute-done.12.refs_3_ = bf16[136,1024]{1,0:T(8,128)(2,1)S(1)} collective-permute-done((bf16[136,1024]{1,0:T(8,128)(2,1)S(1)}, bf16[136,1024]{1,0:T(8,128)(2,1)S(1)}, u32[]{:S(2)}, u32[]{:S(2)}) %collective-permute-start.12) | collective-permute-done | bytes 278560 | tf_op jit(solution)/shard_map/ppermute | solution.py:281
  42.8 1.5 %collective-permute-start.13 = (bf16[136,1024]{1,0:T(8,128)(2,1)S(1)}, bf16[136,1024]{1,0:T(8,128)(2,1)S(1)}, u32[]{:S(2)}, u32[]{:S(2)}) collective-permute-start(bf16[136,1024]{1,0:T(8,128)(2,1)S(1)} %collective-permute-done.11.refs_2_), channel_id=1, source_target_pairs={{0,2},{2,0},{1,3},{3,1},{4,6},{6,4},{5,7},{7,5},{8,10},{10,8},{9,1... | collective-permute-start | bytes 835592 | tf_op jit(solution)/shard_map/ppermute | solution.py:281
  44.4 3.7 %chunk.6 = (bf16[128,1024]{1,0:T(8,128)(2,1)S(1)}, bf16[128,1024]{1,0:T(8,128)(2,1)S(1)}, bf16[4,96,1024]{2,1,0:T(8,128)(2,1)S(1)}, bf16[4,96,1024]{2,1,0:T(8,128)(2,1)S(1)}, bf16[4,96,768]{2,1,0:T(8,128)(2,1)S(1)}) custom-call(s32[1]{0:T(128)} %bitcast.first_ref, bf16[128,1024]{1,0:T(8,128)(2,1)S(1)} %collective-permute-done.2.refs_0_, ...), custom_call_target="tpu_custom_call" | custom-call | flops 1610612736 | bytes 8388608 | tf_op jit(solution)/shard_map/chunk/pallas_call | solution.py:171
  48.1 0.4 collective-permute-done.10.refs_1_
  48.5 2.2 %collective-permute-start.15 = (bf16[256,1024]{1,0:T(8,128)(2,1)S(1)}, bf16[256,1024]{1,0:T(8,128)(2,1)S(1)}, u32[]{:S(2)}, u32[]{:S(2)}) collective-permute-start(bf16[256,1024]{1,0:T(8,128)(2,1)S(1)} %get-tuple-element.215), channel_id=1, source_target_pairs={{0,8},{4,0},{12,4},{8,12},{1,9},{5,1},{13,5},{9,13},{2,10},{6,2},{... | collective-permute-start | bytes 1572872 | tf_op jit(solution)/shard_map/ppermute | solution.py:318
  50.7 1.7 %collective-permute-done.13.refs_3_ = bf16[136,1024]{1,0:T(8,128)(2,1)S(1)} collective-permute-done((bf16[136,1024]{1,0:T(8,128)(2,1)S(1)}, bf16[136,1024]{1,0:T(8,128)(2,1)S(1)}, u32[]{:S(2)}, u32[]{:S(2)}) %collective-permute-start.13) | collective-permute-done | bytes 278560 | tf_op jit(solution)/shard_map/ppermute | solution.py:281
  52.4 1.5 %collective-permute-start.14 = (bf16[128,1024]{1,0:T(8,128)(2,1)S(1)}, bf16[128,1024]{1,0:T(8,128)(2,1)S(1)}, u32[]{:S(2)}, u32[]{:S(2)}) collective-permute-start(bf16[128,1024]{1,0:T(8,128)(2,1)S(1)} %get-tuple-element.233), channel_id=1, source_target_pairs={{0,2},{2,0},{1,3},{3,1},{4,6},{6,4},{5,7},{7,5},{8,10},{10,8},{9,1... | collective-permute-start | bytes 786440 | tf_op jit(solution)/shard_map/ppermute | solution.py:288
  53.9 3.7 %chunk.7 = (bf16[128,1024]{1,0:T(8,128)(2,1)S(1)}, bf16[128,1024]{1,0:T(8,128)(2,1)S(1)}, bf16[4,96,1024]{2,1,0:T(8,128)(2,1)S(1)}, bf16[4,96,1024]{2,1,0:T(8,128)(2,1)S(1)}, bf16[4,96,768]{2,1,0:T(8,128)(2,1)S(1)}) custom-call(s32[1]{0:T(128)} %bitcast.first_ref, bf16[128,1024]{1,0:T(8,128)(2,1)S(1)} %collective-permute-done.6.refs_0_, ...), custom_call_target="tpu_custom_call" | custom-call | flops 1610612736 | bytes 8388608 | tf_op jit(solution)/shard_map/chunk/pallas_call | solution.py:171
  57.6 0.6 collective-permute-start.16
  58.2 1.3 %collective-permute-done.14 = bf16[128,1024]{1,0:T(8,128)(2,1)S(1)} collective-permute-done((bf16[128,1024]{1,0:T(8,128)(2,1)S(1)}, bf16[128,1024]{1,0:T(8,128)(2,1)S(1)}, u32[]{:S(2)}, u32[]{:S(2)}) %collective-permute-start.14) | collective-permute-done | bytes 262176 | tf_op jit(solution)/shard_map/ppermute | solution.py:288
  59.5 0.3 collective-permute-done.15
  59.8 1.9 %weight_grads.2 = bf16[4,768,512]{2,1,0:T(8,128)(2,1)S(1)} custom-call(s32[1]{0:T(128)S(6)} %sub.3.side_ref, bf16[4,96,1024]{2,1,0:T(8,128)(2,1)S(1)} %get-tuple-element.252.refs_0_, bf16[4,96,1024]{2,1,0:T(8,128)(2,1)S(1)} %get-tuple-element.253.refs_1_, bf16[4,96,1024]{2,1,0:T(8,128)(2,1)S(1)} %get-tuple-element.254.refs_2_, ...), custom_call_target="tpu_custom_call" | custom-call | flops 1207959552 | bytes 8650752 | tf_op jit(solution)/shard_map/weight_grads/pallas_call | solution.py:244
  61.7 0.1 add_convert_fusion.3
  61.7 2.7 %collective-permute-done.16 = bf16[128,1024]{1,0:T(8,128)(2,1)S(1)} collective-permute-done((bf16[128,1024]{1,0:T(8,128)(2,1)S(1)}, bf16[128,1024]{1,0:T(8,128)(2,1)S(1)}, u32[]{:S(2)}, u32[]{:S(2)}) %collective-permute-start.16) | collective-permute-done | bytes 262176 | tf_op jit(solution)/shard_map/ppermute | solution.py:288
  64.4 0.0 collective-permute-start.17
  64.4 3.1 %collective-permute-start.18 = (bf16[128,1024]{1,0:T(8,128)(2,1)S(1)}, bf16[128,1024]{1,0:T(8,128)(2,1)S(1)}, u32[]{:S(2)}, u32[]{:S(2)}) collective-permute-start(bf16[128,1024]{1,0:T(8,128)(2,1)S(1)} %add_convert_fusion.3), channel_id=1, source_target_pairs={{0,4},{4,12},{12,8},{8,0},{1,5},{5,13},{13,9},{9,1},{2,6},{6,14},{... | collective-permute-start | bytes 786440 | tf_op jit(solution)/shard_map/ppermute | solution.py:298
  67.5 6.5 %collective-permute-done.18 = bf16[128,1024]{1,0:T(8,128)(2,1)S(1)} collective-permute-done((bf16[128,1024]{1,0:T(8,128)(2,1)S(1)}, bf16[128,1024]{1,0:T(8,128)(2,1)S(1)}, u32[]{:S(2)}, u32[]{:S(2)}) %collective-permute-start.18) | collective-permute-done | bytes 262176 | tf_op jit(solution)/shard_map/ppermute | solution.py:298
  74.0 0.1 add_convert_fusion.2
  74.2 2.2 %collective-permute-start.19 = (bf16[128,1024]{1,0:T(8,128)(2,1)S(1)}, bf16[128,1024]{1,0:T(8,128)(2,1)S(1)}, u32[]{:S(2)}, u32[]{:S(2)}) collective-permute-start(bf16[128,1024]{1,0:T(8,128)(2,1)S(1)} %add_convert_fusion.2), channel_id=1, source_target_pairs={{0,4},{4,12},{12,8},{8,0},{1,5},{5,13},{13,9},{9,1},{2,6},{6,14},{... | collective-permute-start | bytes 786440 | tf_op jit(solution)/shard_map/ppermute | solution.py:298
  76.4 0.1 add_convert_fusion.1
  76.5 1.6 %collective-permute-start.20 = (bf16[128,1024]{1,0:T(8,128)(2,1)S(1)}, bf16[128,1024]{1,0:T(8,128)(2,1)S(1)}, u32[]{:S(2)}, u32[]{:S(2)}) collective-permute-start(bf16[128,1024]{1,0:T(8,128)(2,1)S(1)} %add_convert_fusion.1), channel_id=1, source_target_pairs={{0,2},{2,0},{1,3},{3,1},{4,6},{6,4},{5,7},{7,5},{8,10},{10,8},{9,1... | collective-permute-start | bytes 786440 | tf_op jit(solution)/shard_map/ppermute | solution.py:288
  78.0 0.0 collective-permute-done.17.refs_12_
  78.0 2.7 %weight_grads.3 = (bf16[4,512,256]{2,1,0:T(8,128)(2,1)}, bf16[4,512,256]{2,1,0:T(8,128)(2,1)}, bf16[4,256,512]{2,1,0:T(8,128)(2,1)}) custom-call(s32[1]{0:T(128)} %bitcast.1.side_ref, bf16[4,96,1024]{2,1,0:T(8,128)(2,1)S(1)} %get-tuple-element.252.refs_0_, bf16[4,96,1024]{2,1,0:T(8,128)(2,1)S(1)} %get-tuple-element.253.refs_1_, ...), custom_call_target="tpu_custom_call" | custom-call | flops 1207959552 | bytes 8650752 | tf_op jit(solution)/shard_map/weight_grads/pallas_call | solution.py:244
  80.7 2.3 %collective-permute-done.19 = bf16[128,1024]{1,0:T(8,128)(2,1)S(1)} collective-permute-done((bf16[128,1024]{1,0:T(8,128)(2,1)S(1)}, bf16[128,1024]{1,0:T(8,128)(2,1)S(1)}, u32[]{:S(2)}, u32[]{:S(2)}) %collective-permute-start.19) | collective-permute-done | bytes 262176 | tf_op jit(solution)/shard_map/ppermute | solution.py:298
  83.1 1.1 %collective-permute-done.20 = bf16[128,1024]{1,0:T(8,128)(2,1)S(1)} collective-permute-done((bf16[128,1024]{1,0:T(8,128)(2,1)S(1)}, bf16[128,1024]{1,0:T(8,128)(2,1)S(1)}, u32[]{:S(2)}, u32[]{:S(2)}) %collective-permute-start.20) | collective-permute-done | bytes 262176 | tf_op jit(solution)/shard_map/ppermute | solution.py:288
  84.2 0.9 %add_convert_fusion = bf16[128,1024]{1,0:T(8,128)(2,1)} fusion(bf16[128,1024]{1,0:T(8,128)(2,1)S(1)} %collective-permute-done.19, bf16[128,1024]{1,0:T(8,128)(2,1)S(1)} %collective-permute-done.20, bf16[128,1024]{1,0:T(8,128)(2,1)S(1)} %get-tuple-element.249, bf16[256,1024]{1,0:T(8,128)(2,1)S(1)} %collective-permute-done.15), kind=kLoop, calls=%fused_computation | loop fusion | flops 1048576 | bytes 1310720 | tf_op jit(solution)/shard_map/convert_element_type | solution.py:343
Async XLA Ops:
  0.6 12.4 %collective-permute-start = (bf16[128,1024]{1,0:T(8,128)(2,1)}, bf16[128,1024]{1,0:T(8,128)(2,1)S(1)}, u32[]{:S(2)}, u32[]{:S(2)}) collective-permute-start(bf16[128,1024]{1,0:T(8,128)(2,1)} %tokens), channel_id=1, source_target_pairs={{0,4},{4,12},{12,8},{8,0},{1,5},{5,13},{13,9},{9,1},{2,6},{6,14},{... | collective-permute-start | bytes 786440 | tf_op jit(solution)/shard_map/ppermute | solution.py:309
  3.7 9.3 %collective-permute-start.1 = (bf16[128,1024]{1,0:T(8,128)(2,1)}, bf16[128,1024]{1,0:T(8,128)(2,1)S(1)}, u32[]{:S(2)}, u32[]{:S(2)}) collective-permute-start(bf16[128,1024]{1,0:T(8,128)(2,1)} %tokens), channel_id=1, source_target_pairs={{0,2},{2,0},{1,3},{3,1},{4,6},{6,4},{5,7},{7,5},{8,10},{10,8},{9,1... | collective-permute-start | bytes 786440 | tf_op jit(solution)/shard_map/ppermute | solution.py:281
  7.0 11.1 %collective-permute-start.4 = (bf16[136,1024]{1,0:T(8,128)(2,1)S(1)}, bf16[136,1024]{1,0:T(8,128)(2,1)S(1)}, u32[]{:S(2)}, u32[]{:S(2)}) collective-permute-start(bf16[136,1024]{1,0:T(8,128)(2,1)S(1)} %get-tuple-element.154.refs_2_), channel_id=1, source_target_pairs={{0,4},{4,12},{12,8},{8,0},{1,5},{5,13},{13,9},{9,1},{2,6},{6,14},{... | collective-permute-start | bytes 835592 | tf_op jit(solution)/shard_map/ppermute | solution.py:309
  9.6 9.6 %collective-permute-start.5 = (bf16[136,1024]{1,0:T(8,128)(2,1)S(1)}, bf16[136,1024]{1,0:T(8,128)(2,1)S(1)}, u32[]{:S(2)}, u32[]{:S(2)}) collective-permute-start(bf16[136,1024]{1,0:T(8,128)(2,1)S(1)} %get-tuple-element.154.refs_2_), channel_id=1, source_target_pairs={{0,2},{2,0},{1,3},{3,1},{4,6},{6,4},{5,7},{7,5},{8,10},{10,8},{9,1... | collective-permute-start | bytes 835592 | tf_op jit(solution)/shard_map/ppermute | solution.py:281
  13.1 13.8 %collective-permute-start.2 = (bf16[128,1024]{1,0:T(8,128)(2,1)S(1)}, bf16[128,1024]{1,0:T(8,128)(2,1)S(1)}, u32[]{:S(2)}, u32[]{:S(2)}) collective-permute-start(bf16[128,1024]{1,0:T(8,128)(2,1)S(1)} %collective-permute-done.refs_0_), channel_id=1, source_target_pairs={{0,4},{4,12},{12,8},{8,0},{1,5},{5,13},{13,9},{9,1},{2,6},{6,14},{... | collective-permute-start | bytes 786440 | tf_op jit(solution)/shard_map/ppermute | solution.py:309
  15.7 11.1 %collective-permute-start.3 = (bf16[128,1024]{1,0:T(8,128)(2,1)S(1)}, bf16[128,1024]{1,0:T(8,128)(2,1)S(1)}, u32[]{:S(2)}, u32[]{:S(2)}) collective-permute-start(bf16[128,1024]{1,0:T(8,128)(2,1)S(1)} %collective-permute-done.refs_0_), channel_id=1, source_target_pairs={{0,2},{2,0},{1,3},{3,1},{4,6},{6,4},{5,7},{7,5},{8,10},{10,8},{9,1... | collective-permute-start | bytes 786440 | tf_op jit(solution)/shard_map/ppermute | solution.py:281
  19.2 10.5 %collective-permute-start.8 = (bf16[136,1024]{1,0:T(8,128)(2,1)S(1)}, bf16[136,1024]{1,0:T(8,128)(2,1)S(1)}, u32[]{:S(2)}, u32[]{:S(2)}) collective-permute-start(bf16[136,1024]{1,0:T(8,128)(2,1)S(1)} %collective-permute-done.4.refs_2_), channel_id=1, source_target_pairs={{0,4},{4,12},{12,8},{8,0},{1,5},{5,13},{13,9},{9,1},{2,6},{6,14},{... | collective-permute-start | bytes 835592 | tf_op jit(solution)/shard_map/ppermute | solution.py:309
  21.7 9.3 %collective-permute-start.9 = (bf16[136,1024]{1,0:T(8,128)(2,1)S(1)}, bf16[136,1024]{1,0:T(8,128)(2,1)S(1)}, u32[]{:S(2)}, u32[]{:S(2)}) collective-permute-start(bf16[136,1024]{1,0:T(8,128)(2,1)S(1)} %collective-permute-done.4.refs_2_), channel_id=1, source_target_pairs={{0,2},{2,0},{1,3},{3,1},{4,6},{6,4},{5,7},{7,5},{8,10},{10,8},{9,1... | collective-permute-start | bytes 835592 | tf_op jit(solution)/shard_map/ppermute | solution.py:281
  26.9 11.6 %collective-permute-start.6 = (bf16[128,1024]{1,0:T(8,128)(2,1)S(1)}, bf16[128,1024]{1,0:T(8,128)(2,1)S(1)}, u32[]{:S(2)}, u32[]{:S(2)}) collective-permute-start(bf16[128,1024]{1,0:T(8,128)(2,1)S(1)} %collective-permute-done.2.refs_0_), channel_id=1, source_target_pairs={{0,4},{4,12},{12,8},{8,0},{1,5},{5,13},{13,9},{9,1},{2,6},{6,14},{... | collective-permute-start | bytes 786440 | tf_op jit(solution)/shard_map/ppermute | solution.py:309
  27.8 10.7 %collective-permute-start.7 = (bf16[128,1024]{1,0:T(8,128)(2,1)S(1)}, bf16[128,1024]{1,0:T(8,128)(2,1)S(1)}, u32[]{:S(2)}, u32[]{:S(2)}) collective-permute-start(bf16[128,1024]{1,0:T(8,128)(2,1)S(1)} %collective-permute-done.2.refs_0_), channel_id=1, source_target_pairs={{0,2},{2,0},{1,3},{3,1},{4,6},{6,4},{5,7},{7,5},{8,10},{10,8},{9,1... | collective-permute-start | bytes 786440 | tf_op jit(solution)/shard_map/ppermute | solution.py:281
  31.0 9.3 %collective-permute-start.11 = (bf16[136,1024]{1,0:T(8,128)(2,1)S(1)}, bf16[136,1024]{1,0:T(8,128)(2,1)S(1)}, u32[]{:S(2)}, u32[]{:S(2)}) collective-permute-start(bf16[136,1024]{1,0:T(8,128)(2,1)S(1)} %collective-permute-done.8.refs_2_), channel_id=1, source_target_pairs={{0,4},{4,12},{12,8},{8,0},{1,5},{5,13},{13,9},{9,1},{2,6},{6,14},{... | collective-permute-start | bytes 835592 | tf_op jit(solution)/shard_map/ppermute | solution.py:309
  33.3 9.5 %collective-permute-start.12 = (bf16[136,1024]{1,0:T(8,128)(2,1)S(1)}, bf16[136,1024]{1,0:T(8,128)(2,1)S(1)}, u32[]{:S(2)}, u32[]{:S(2)}) collective-permute-start(bf16[136,1024]{1,0:T(8,128)(2,1)S(1)} %collective-permute-done.8.refs_2_), channel_id=1, source_target_pairs={{0,2},{2,0},{1,3},{3,1},{4,6},{6,4},{5,7},{7,5},{8,10},{10,8},{9,1... | collective-permute-start | bytes 835592 | tf_op jit(solution)/shard_map/ppermute | solution.py:281
  38.5 10.0 %collective-permute-start.10 = (bf16[128,1024]{1,0:T(8,128)(2,1)S(1)}, bf16[128,1024]{1,0:T(8,128)(2,1)S(1)}, u32[]{:S(2)}, u32[]{:S(2)}) collective-permute-start(bf16[128,1024]{1,0:T(8,128)(2,1)S(1)} %collective-permute-done.6.refs_0_), channel_id=1, source_target_pairs={{0,2},{2,0},{1,3},{3,1},{4,6},{6,4},{5,7},{7,5},{8,10},{10,8},{9,1... | collective-permute-start | bytes 786440 | tf_op jit(solution)/shard_map/ppermute | solution.py:281
  42.8 9.6 %collective-permute-start.13 = (bf16[136,1024]{1,0:T(8,128)(2,1)S(1)}, bf16[136,1024]{1,0:T(8,128)(2,1)S(1)}, u32[]{:S(2)}, u32[]{:S(2)}) collective-permute-start(bf16[136,1024]{1,0:T(8,128)(2,1)S(1)} %collective-permute-done.11.refs_2_), channel_id=1, source_target_pairs={{0,2},{2,0},{1,3},{3,1},{4,6},{6,4},{5,7},{7,5},{8,10},{10,8},{9,1... | collective-permute-start | bytes 835592 | tf_op jit(solution)/shard_map/ppermute | solution.py:281
  48.5 11.3 %collective-permute-start.15 = (bf16[256,1024]{1,0:T(8,128)(2,1)S(1)}, bf16[256,1024]{1,0:T(8,128)(2,1)S(1)}, u32[]{:S(2)}, u32[]{:S(2)}) collective-permute-start(bf16[256,1024]{1,0:T(8,128)(2,1)S(1)} %get-tuple-element.215), channel_id=1, source_target_pairs={{0,8},{4,0},{12,4},{8,12},{1,9},{5,1},{13,5},{9,13},{2,10},{6,2},{... | collective-permute-start | bytes 1572872 | tf_op jit(solution)/shard_map/ppermute | solution.py:318
  52.4 7.1 %collective-permute-start.14 = (bf16[128,1024]{1,0:T(8,128)(2,1)S(1)}, bf16[128,1024]{1,0:T(8,128)(2,1)S(1)}, u32[]{:S(2)}, u32[]{:S(2)}) collective-permute-start(bf16[128,1024]{1,0:T(8,128)(2,1)S(1)} %get-tuple-element.233), channel_id=1, source_target_pairs={{0,2},{2,0},{1,3},{3,1},{4,6},{6,4},{5,7},{7,5},{8,10},{10,8},{9,1... | collective-permute-start | bytes 786440 | tf_op jit(solution)/shard_map/ppermute | solution.py:288
  57.6 6.8 %collective-permute-start.16 = (bf16[128,1024]{1,0:T(8,128)(2,1)S(1)}, bf16[128,1024]{1,0:T(8,128)(2,1)S(1)}, u32[]{:S(2)}, u32[]{:S(2)}) collective-permute-start(bf16[128,1024]{1,0:T(8,128)(2,1)S(1)} %get-tuple-element.245), channel_id=1, source_target_pairs={{0,2},{2,0},{1,3},{3,1},{4,6},{6,4},{5,7},{7,5},{8,10},{10,8},{9,1... | collective-permute-start | bytes 786440 | tf_op jit(solution)/shard_map/ppermute | solution.py:288
  64.4 13.6 %collective-permute-start.17 = (bf16[4,768,512]{2,1,0:T(8,128)(2,1)S(1)}, bf16[4,768,512]{2,1,0:T(8,128)(2,1)S(1)}, u32[]{:S(2)}, u32[]{:S(2)}) collective-permute-start(bf16[4,768,512]{2,1,0:T(8,128)(2,1)S(1)} %weight_grads.2), channel_id=1, source_target_pairs={{0,1},{1,0},{2,3},{3,2},{4,5},{5,4},{6,7},{7,6},{8,9},{9,8},{10,11... | collective-permute-start | bytes 9437192 | tf_op jit(solution)/shard_map/ppermute | solution.py:332
  64.4 9.6 %collective-permute-start.18 = (bf16[128,1024]{1,0:T(8,128)(2,1)S(1)}, bf16[128,1024]{1,0:T(8,128)(2,1)S(1)}, u32[]{:S(2)}, u32[]{:S(2)}) collective-permute-start(bf16[128,1024]{1,0:T(8,128)(2,1)S(1)} %add_convert_fusion.3), channel_id=1, source_target_pairs={{0,4},{4,12},{12,8},{8,0},{1,5},{5,13},{13,9},{9,1},{2,6},{6,14},{... | collective-permute-start | bytes 786440 | tf_op jit(solution)/shard_map/ppermute | solution.py:298
  74.2 8.9 %collective-permute-start.19 = (bf16[128,1024]{1,0:T(8,128)(2,1)S(1)}, bf16[128,1024]{1,0:T(8,128)(2,1)S(1)}, u32[]{:S(2)}, u32[]{:S(2)}) collective-permute-start(bf16[128,1024]{1,0:T(8,128)(2,1)S(1)} %add_convert_fusion.2), channel_id=1, source_target_pairs={{0,4},{4,12},{12,8},{8,0},{1,5},{5,13},{13,9},{9,1},{2,6},{6,14},{... | collective-permute-start | bytes 786440 | tf_op jit(solution)/shard_map/ppermute | solution.py:298
  76.5 7.7 %collective-permute-start.20 = (bf16[128,1024]{1,0:T(8,128)(2,1)S(1)}, bf16[128,1024]{1,0:T(8,128)(2,1)S(1)}, u32[]{:S(2)}, u32[]{:S(2)}) collective-permute-start(bf16[128,1024]{1,0:T(8,128)(2,1)S(1)} %add_convert_fusion.1), channel_id=1, source_target_pairs={{0,2},{2,0},{1,3},{3,1},{4,6},{6,4},{5,7},{7,5},{8,10},{10,8},{9,1... | collective-permute-start | bytes 786440 | tf_op jit(solution)/shard_map/ppermute | solution.py:288
